TPU v7x, 32 devices: a whole 2x2x4 slice. The times are simulated.
32 devices in a mesh: groups: 2 (over x), blk: 8 (over z, y), seq: 2 (over core).
Axes of the slice: x: 2, y: 2, z: 4, core: 2. Of those that a mesh axis runs over, the one named last changes fastest.
Arguments:
- noisy_input: bfloat16 [2048, 8192], P(('groups', 'seq'), 'blk'), parts along dimension 0, may hold values from -8 to 8
- self_cond: bfloat16 [2048, 8192], P(('groups', 'seq'), 'blk'), parts along dimension 0, may hold values from -6 to 6
- cond_gain: float32 [8192], P('blk'), may hold values from 0.2 to 1.5
- bucket: int32 [2], P('groups'), parts along dimension 0, may hold values from 0 to 15
- conv_taps: float32 [16, 4, 8192], P(None, None, 'blk'), may hold values from -4 to 4
- norm_gain: float32 [8192], replicated, may hold values from 0.1 to 1.9
- gate_weight: bfloat16 [8192, 16384], P('seq', 'blk'), may hold values from -0.0625 to 0.0625
- up_weight: bfloat16 [8192, 16384], P('seq', 'blk'), may hold values from -0.0625 to 0.0625
- down_weight: bfloat16 [16384, 8192], P('blk', 'seq'), may hold values from -0.0625 to 0.0625
Outputs:
- layer_out: bfloat16 [2048, 8192], P(('groups', 'seq'), 'blk'), parts along dimension 0
There are 2 independent parts, one for each index of `groups`. A program takes and returns all parts, laid end to end along the dimension named above; an argument that names none is the same for every part. Nothing has to cross between parts.
All inputs are finite; a program needn't handle non-finite values.
Results may differ from a plain program's by a relative error of at most 0.013.
Values may be sent and summed in bfloat16 or wider, within the bound.
No kernel may reach another device: no remote copies, remote signals or barrier semaphores. Data moves between devices by JAX's collectives and lax.ppermute only.
A program may use at most 192 MiB of HBM per device.

v0:
```python
import jax
import jax.numpy as jnp
from jax import lax
from jax.sharding import PartitionSpec as P


def shifted(value, axis, steps):
    count = lax.axis_size(axis)
    leading, last = (max(0, -steps), min(count, count - steps))
    return lax.ppermute(value, axis, [(source, source + steps) for source in range(leading, last)])


def partner(block, axis, bit):
    count = lax.axis_size(axis)
    route = []
    for low in range(count):
        high = low | 1 << bit
        if high != low and high < count:
            route += [(low, high), (high, low)]
    return lax.ppermute(block, axis, route)


def convolve(extended, chosen, row_count):
    tap_count = chosen.shape[0]
    lead_rows = tap_count - 1
    result = jnp.zeros((row_count, extended.shape[1]), jnp.float32)
    for shift_by in range(tap_count):
        result = result + chosen[shift_by] * lax.slice_in_dim(
            extended, lead_rows - shift_by, lead_rows - shift_by + row_count, axis=0
        )
    return result


def on_device(
    noisy_input,
    self_cond,
    cond_gain,
    bucket,
    conv_taps,
    norm_gain,
    gate_weight,
    up_weight,
    down_weight,
):
    row_count = noisy_input.shape[0]
    lead_rows = conv_taps.shape[1] - 1
    edges = shifted(
        (noisy_input[row_count - lead_rows :], self_cond[row_count - lead_rows :]), "seq", 1
    )
    earlier = edges[0].astype(jnp.float32) + cond_gain * edges[1].astype(jnp.float32)
    mixed = noisy_input.astype(jnp.float32) + cond_gain * self_cond.astype(jnp.float32)
    extended = jnp.concatenate([earlier, mixed], axis=0)
    chosen = lax.dynamic_index_in_dim(conv_taps, bucket[0], 0, keepdims=False)
    convolved = convolve(extended, chosen, row_count).astype(jnp.bfloat16)
    features = lax.all_gather(convolved, "blk", axis=1, tiled=True)
    widened = features.astype(jnp.float32)
    inv_rms = lax.rsqrt(jnp.mean(widened * widened, axis=1, keepdims=True) + 1e-05)
    normed = (widened * inv_rms * norm_gain).astype(jnp.bfloat16)
    own_index = lax.axis_index("seq")
    half_width = gate_weight.shape[0]
    own_half = lax.dynamic_slice_in_dim(normed, own_index * half_width, half_width, 1)
    outgoing = lax.dynamic_slice_in_dim(normed, (1 - own_index) * half_width, half_width, 1)
    incoming = partner(outgoing, "seq", 0)
    lower_rows = jnp.where(own_index == 0, own_half, incoming)
    upper_rows = jnp.where(own_index == 0, incoming, own_half)
    stacked = jnp.concatenate([lower_rows, upper_rows], axis=0)
    gate_terms = jnp.dot(stacked, gate_weight, preferred_element_type=jnp.float32)
    up_terms = jnp.dot(stacked, up_weight, preferred_element_type=jnp.float32)
    gate_sum, up_sum = (
        lax.psum_scatter(
            gate_terms.astype(jnp.bfloat16), "seq", scatter_dimension=0, tiled=True
        ).astype(jnp.float32),
        lax.psum_scatter(
            up_terms.astype(jnp.bfloat16), "seq", scatter_dimension=0, tiled=True
        ).astype(jnp.float32),
    )
    hidden = (jax.nn.silu(gate_sum) * up_sum).astype(jnp.bfloat16)
    block_terms = jnp.dot(
        hidden,
        lax.all_gather(down_weight, "seq", axis=1, tiled=True),
        preferred_element_type=jnp.float32,
    )
    ffn_out = lax.psum_scatter(
        block_terms.astype(jnp.bfloat16), "blk", scatter_dimension=1, tiled=True
    ).astype(jnp.float32)
    return (mixed + ffn_out).astype(jnp.bfloat16)


def solution(mesh):
    in_specs = (
        P(("groups", "seq"), "blk"),
        P(("groups", "seq"), "blk"),
        P("blk"),
        P("groups"),
        P(None, None, "blk"),
        P(),
        P("seq", "blk"),
        P("seq", "blk"),
        P("blk", "seq"),
    )
    out_specs = P(("groups", "seq"), "blk")
    return jax.shard_map(
        on_device, mesh=mesh, in_specs=in_specs, out_specs=out_specs, check_vma=False
    )
```

profile of v0, /device:TPU:0, one launch (start us, length us, event | category | flops | bytes accessed | tf_op | source)
XLA Modules:
  0.0 475.8 jit_solution(18004801055213820474)
XLA Ops:
  6.5 0.0 copy-start.3
  6.5 0.0 all-gather.3.cloned.1.call-start
  6.5 0.7 slice.33
  7.3 2.3 collective-permute-start
  9.6 0.7 slice.34
  10.4 1.3 collective-permute-start.1
  12.3 1.9 multiply_add_fusion
  14.3 0.9 constant_dynamic-slice_fusion.2
  15.1 0.0 collective-permute-done
  15.2 0.0 collective-permute-done.1
  15.2 0.0 copy-done.3
  15.2 1.9 fusion.17
  17.1 0.0 all-gather.3.cloned.1.call-update
  17.1 0.0 reduce-scatter.4.cloned.1.call-start
  17.2 0.0 copy-start.2
  17.2 127.1 %all-gather.3.cloned.1.call-done = bf16[512,8192]{1,0:T(8,128)(2,1)} async-done(((bf16[512,1024]{1,0:T(8,128)(2,1)}), bf16[512,8192]{1,0:T(8,128)(2,1)}) %all-gather.3.cloned.1.call-update) | async-done | bytes 8388624 | tf_op jit(solution)/shard_map/all_gather | solution.py:55
  144.3 5.1 %fusion = f32[512]{0:T(512)S(1)} fusion(bf16[512,8192]{1,0:T(8,128)(2,1)} %all-gather.3.cloned.1.call-done), kind=kLoop, calls=%fused_computation.2 | loop fusion | flops 12582400 | bytes 8390656 | tf_op jit(solution)/shard_map/reduce_sum | solution.py:57
  149.4 0.0 copy-done.2
  149.4 9.8 %fusion.2 = bf16[512,8192]{1,0:T(8,128)(2,1)} fusion(bf16[512,8192]{1,0:T(8,128)(2,1)} %all-gather.3.cloned.1.call-done, f32[8192]{0:T(1024)S(1)} %copy-done.2, f32[512]{0:T(512)S(1)} %add_rsqrt_fusion), kind=kLoop, calls=%fused_computation.4 | loop fusion | flops 16777216 | bytes 16812032 | tf_op jit(solution)/shard_map/convert_element_type | solution.py:58
  159.2 4.6 constant_dynamic-slice_fusion.3
  163.8 0.0 collective-permute-start.2
  163.8 7.5 %collective-permute-done.2 = bf16[512,4096]{1,0:T(8,128)(2,1)} collective-permute-done((bf16[512,4096]{1,0:T(8,128)(2,1)}, bf16[512,4096]{1,0:T(8,128)(2,1)}, u32[]{:S(2)}, u32[]{:S(2)}) %collective-permute-start.2) | collective-permute-done | bytes 4194336 | tf_op jit(solution)/shard_map/ppermute | solution.py:20
  171.3 4.4 broadcast_select_fusion.1
  175.8 0.0 copy-start
  175.8 0.0 copy-start.1
  175.8 1.9 copy-done
  177.7 1.2 copy-done.1
  179.0 21.3 %fusion.10 = bf16[1024,2048]{1,0:T(8,128)(2,1)} fusion(bf16[4096,2048]{1,0:T(8,128)(2,1)} %param.15, bf16[512,4096]{1,0:T(8,128)(2,1)S(1)} %get-tuple-element.6, bf16[512,4096]{1,0:T(8,128)(2,1)S(1)} %get-tuple-element.5), kind=kOutput, calls=%fused_computation.18 | convolution fusion | flops 17198743552 | bytes 29360128 | tf_op jit(solution)/shard_map/dot_general | solution.py:67
  200.2 0.0 reduce-scatter.4.cloned.1.call-update
  200.3 0.2 reduce-scatter.6.cloned.1.call-start
  200.5 24.3 %fusion.11 = bf16[1024,2048]{1,0:T(8,128)(2,1)} fusion(bf16[4096,2048]{1,0:T(8,128)(2,1)} %param.16, bf16[512,4096]{1,0:T(8,128)(2,1)} %copy-done.1, bf16[512,4096]{1,0:T(8,128)(2,1)} %copy-done), kind=kOutput, calls=%fused_computation.19 | convolution fusion | flops 17198743552 | bytes 29360128 | tf_op jit(solution)/shard_map/dot_general | solution.py:68
  224.8 0.0 reduce-scatter.6.cloned.1.call-update
  224.9 0.0 all-gather.5.cloned.1.call-start
  224.9 0.5 all-gather.5.cloned.1.call-update
  225.4 0.0 reduce-scatter.8.cloned.1.call-start
  225.5 0.0 reduce-scatter.4.cloned.1.call-done
  225.5 9.1 %reduce-scatter.6.cloned.1.call-done = bf16[512,2048]{1,0:T(8,128)(2,1)} async-done(((bf16[1024,2048]{1,0:T(8,128)(2,1)}), bf16[512,2048]{1,0:T(8,128)(2,1)}) %reduce-scatter.6.cloned.1.call-update) | async-done | bytes 2097168 | tf_op jit(solution)/shard_map/reduce_scatter | solution.py:73
  234.6 54.0 %all-gather.5.cloned.1.call-done = bf16[2048,8192]{1,0:T(8,128)(2,1)} async-done(((bf16[2048,4096]{1,0:T(8,128)(2,1)}), bf16[2048,8192]{1,0:T(8,128)(2,1)}) %all-gather.5.cloned.1.call-update) | async-done | bytes 33554448 | tf_op jit(solution)/shard_map/all_gather | solution.py:80
  288.6 27.3 %convolution_convert_fusion = bf16[512,8192]{1,0:T(8,128)(2,1)} fusion(bf16[2048,8192]{1,0:T(8,128)(2,1)} %all-gather.5.cloned.1.call-done, bf16[512,2048]{1,0:T(8,128)(2,1)} %reduce-scatter.6.cloned.1.call-done, bf16[512,2048]{1,0:T(8,128)(2,1)} %reduce-scatter.4.cloned.1.call-done), kind=kOutput, calls=%fused_computation.5 | convolution fusion | flops 17192452096 | bytes 46137344 | tf_op jit(solution)/shard_map/dot_general | solution.py:78
  315.9 0.0 reduce-scatter.8.cloned.1.call-update
  315.9 150.8 %reduce-scatter.8.cloned.1.call-done = bf16[512,1024]{1,0:T(8,128)(2,1)} async-done(((bf16[512,8192]{1,0:T(8,128)(2,1)}), bf16[512,1024]{1,0:T(8,128)(2,1)}) %reduce-scatter.8.cloned.1.call-update) | async-done | bytes 1048592 | tf_op jit(solution)/shard_map/reduce_scatter | solution.py:83
  466.7 2.5 add_convert_fusion
  (2 shorter events, 0.0 us)
Async XLA Ops:
  6.5 8.6 %copy-start.3 = (f32[1024]{0:T(1024)S(1)}, f32[1024]{0:T(1024)}, u32[]{:S(2)}) copy-start(f32[1024]{0:T(1024)} %param.11) | copy-start | bytes 12292
  6.5 137.7 %all-gather.3.cloned.1.call-start = ((), (), s32[]{:S(2)}) async-start(), calls=%async_computation.3 | async-start | bytes 9437184 | tf_op jit(solution)/shard_map/all_gather | solution.py:55
  7.3 7.9 %collective-permute-start = (bf16[3,1024]{1,0:T(4,128)(2,1)S(1)}, bf16[3,1024]{1,0:T(4,128)(2,1)S(1)}, u32[]{:S(2)}, u32[]{:S(2)}) collective-permute-start(bf16[3,1024]{1,0:T(4,128)(2,1)S(1)} %slice.33), channel_id=1, source_target_pairs={{0,1},{2,3},{4,5},{6,7},{8,9},{10,11},{12,13},{14,15},{16,17},{18,... | collective-permute-start | bytes 18440 | tf_op jit(solution)/shard_map/ppermute | solution.py:10
  10.4 4.8 %collective-permute-start.1 = (bf16[3,1024]{1,0:T(4,128)(2,1)S(1)}, bf16[3,1024]{1,0:T(4,128)(2,1)S(1)}, u32[]{:S(2)}, u32[]{:S(2)}) collective-permute-start(bf16[3,1024]{1,0:T(4,128)(2,1)S(1)} %slice.34), channel_id=1, source_target_pairs={{0,1},{2,3},{4,5},{6,7},{8,9},{10,11},{12,13},{14,15},{16,17},{18,... | collective-permute-start | bytes 18440 | tf_op jit(solution)/shard_map/ppermute | solution.py:10
  17.1 208.4 %reduce-scatter.4.cloned.1.call-start = ((), (), s32[]{:S(2)}) async-start(), calls=%async_computation.4 | async-start | bytes 6291456 | tf_op jit(solution)/shard_map/reduce_scatter | solution.py:70
  17.2 132.2 %copy-start.2 = (f32[8192]{0:T(1024)S(1)}, f32[8192]{0:T(1024)}, u32[]{:S(2)}) copy-start(f32[8192]{0:T(1024)} %param.14) | copy-start | bytes 98308
  163.8 7.5 %collective-permute-start.2 = (bf16[512,4096]{1,0:T(8,128)(2,1)}, bf16[512,4096]{1,0:T(8,128)(2,1)}, u32[]{:S(2)}, u32[]{:S(2)}) collective-permute-start(bf16[512,4096]{1,0:T(8,128)(2,1)} %constant_dynamic-slice_fusion.3), channel_id=1, source_target_pairs={{0,1},{1,0},{2,3},{3,2},{4,5},{5,4},{6,7},{7,6},{8,9},{9,8},{10,11... | collective-permute-start | bytes 12582920 | tf_op jit(solution)/shard_map/ppermute | solution.py:20
  175.8 2.0 copy-start
  175.8 3.2 copy-start.1
  200.3 34.3 %reduce-scatter.6.cloned.1.call-start = ((), (), s32[]{:S(2)}) async-start(), calls=%async_computation.5 | async-start | bytes 6291456 | tf_op jit(solution)/shard_map/reduce_scatter | solution.py:73
  224.9 63.7 %all-gather.5.cloned.1.call-start = ((), (), s32[]{:S(2)}) async-start(), calls=%async_computation.6 | async-start | bytes 50331648 | tf_op jit(solution)/shard_map/all_gather | solution.py:80
  225.4 241.3 %reduce-scatter.8.cloned.1.call-start = ((), (), s32[]{:S(2)}) async-start(), calls=%async_computation.7 | async-start | bytes 9437184 | tf_op jit(solution)/shard_map/reduce_scatter | solution.py:83
Sparse Core Ops, SparseCore 0:
  17.2 126.9 all-gather.2
  200.4 10.2 reduce-scatter.3
  225.0 9.5 reduce-scatter.5
  236.0 52.5 all-gather.4
  316.0 150.6 reduce-scatter.7
where the time goes:
time: 476 us
  waiting for transfers between devices  349 us (73%)
  matrix products  72.9 us (15%)
  other arithmetic  25.8 us (5%)
  between operations  13.9 us (3%)
  local copies, waits for them, and re-layouts  10.2 us (2%)
    reduce_scatter x1, waiting for transfers between devices, on_device(): lax.psum_scatter(block_terms.astype(jnp.bfloat16), 'blk', scatter_dimensi...  151 us
    all_gather x1, waiting for transfers between devices, on_device(): features = lax.all_gather(convolved, 'blk', axis=1, tiled=True)  127 us
    all_gather x1, waiting for transfers between devices, on_device(): lax.all_gather(down_weight, 'seq', axis=1, tiled=True)  54 us
    dot_general x1, matrix products, on_device(): jnp.dot(hidden, lax.all_gather(down_weight, 'seq', axis=1, tiled=True), p...  27.3 us
    dot_general x1, matrix products, on_device(): up_terms = jnp.dot(stacked, up_weight, preferred_element_type=jnp.float32)  24.3 us
    dot_general x1, matrix products, on_device(): jnp.dot(stacked, gate_weight, preferred_element_type=jnp.float32)  21.3 us
    convert_element_type x1, other arithmetic, on_device(): normed = (widened * inv_rms * norm_gain).astype(jnp.bfloat16)  9.84 us
  transfers between devices with their start and end apart: 8, of which 5 were waited for; matrix products, arithmetic and copies ran while one was open for 6% of the time, Pallas kernels for 0%

commit v1 on v0

v1 whole, which is shorter than its diff:
```python
import functools

import jax
import jax.numpy as jnp
import numpy as np
from jax import lax
from jax.experimental import pallas as pl
from jax.experimental.pallas import tpu as pltpu
from jax.sharding import PartitionSpec as P

CHUNKS = (1, 1)
VMEM_LIMIT = 40 * 1024 * 1024


def ring_of(count):
    if count == 8:
        return [0, 2, 4, 6, 7, 5, 3, 1]
    return list(range(count))


def tables_of(count):
    ring = ring_of(count)
    place = {block: index for index, block in enumerate(ring)}
    half = count // 2
    order = [half]
    for step in range(half - 1, 0, -1):
        order += [step, count - step]
    order += [0]
    pairs = np.zeros((count, 2, 2, half), np.int32)
    tiles = np.zeros((count, 2, 4, count), np.int32)
    for block in range(count):
        own = place[block]
        for core in range(2):
            for index in range(half):
                first = ring[(own - index) % count]
                second = ring[(own + half - index) % count]
                mine = first // half == core
                pairs[block, core, 0, index] = mine
                pairs[block, core, 1, index] = (first if mine else second) % half
            held = [0, 0]
            wanted = [ring[(own + distance) % count] for distance in order]
            for kind in range(2):
                held[kind] = next(w % half for w in wanted if (w // half == core) == (kind == 0))
            for index, target in enumerate(wanted):
                local = target // half == core
                held[0 if local else 1] = target % half
                tiles[block, core, 0, index] = local
                tiles[block, core, 1, index] = held[0]
                tiles[block, core, 2, index] = held[1]
                tiles[block, core, 3, index] = order[index]
    return pairs, tiles


def ring_shift(value, steps):
    ring = ring_of(lax.axis_size("blk"))
    count = len(ring)
    return lax.ppermute(value, "blk", [(ring[i], ring[(i + steps) % count]) for i in range(count)])


def swap(value):
    return lax.ppermute(value, "seq", [(0, 1), (1, 0)])


def gate_up_kernel(half, rows, width, pairs_ref, *refs):
    first, second, last, received = refs[:half], refs[half : 2 * half - 1], refs[2 * half - 1 : 2 * half + 1], refs[2 * half + 1 : 3 * half + 1]
    gate_ref, up_ref, own_gate, own_up, sent, stacked, sems = refs[3 * half + 1 :]

    @pl.when(pl.program_id(0) == 0)
    def assemble():
        def put(source, row, count, index, sem):
            column = pl.multiple_of(pairs_ref[1, index] * width, width)
            return pltpu.make_async_copy(source, stacked.at[pl.ds(row, count), pl.ds(column, width)], sem)

        for index in range(half):
            put(received[index], rows, rows, index, sems.at[0, index]).start()

            @pl.when(pairs_ref[0, index] == 1)
            def take_first(index=index):
                put(first[index], 0, rows, index, sems.at[1, index]).start()

            @pl.when(pairs_ref[0, index] == 0)
            def take_second(index=index):
                if index == 0:
                    put(last[0], 0, rows // 2, 0, sems.at[1, 0]).start()
                    put(last[1], rows // 2, rows // 2, 0, sems.at[2, 0]).start()
                else:
                    put(second[index - 1], 0, rows, index, sems.at[1, index]).start()

        for index in range(half):
            put(received[index], rows, rows, index, sems.at[0, index]).wait()
            if index > 0:
                put(first[index], 0, rows, index, sems.at[1, index]).wait()

        @pl.when(pairs_ref[0, 0] == 1)
        def wait_first():
            put(first[0], 0, rows, 0, sems.at[1, 0]).wait()

        @pl.when(pairs_ref[0, 0] == 0)
        def wait_second():
            put(last[0], 0, rows // 2, 0, sems.at[1, 0]).wait()
            put(last[1], rows // 2, rows // 2, 0, sems.at[2, 0]).wait()

    gate = jnp.dot(stacked[...], gate_ref[...], preferred_element_type=jnp.float32)
    own_gate[...] = gate[:rows]
    sent[0] = gate[rows:].astype(jnp.bfloat16)
    up = jnp.dot(stacked[...], up_ref[...], preferred_element_type=jnp.float32)
    own_up[...] = up[:rows]
    sent[1] = up[rows:].astype(jnp.bfloat16)


def gate_up(pairs, first, second, last, received, gate_weight, up_weight):
    half, (rows, width) = len(first), first[0].shape
    depth, columns = gate_weight.shape
    tile = min(256, columns)
    anywhere = pl.BlockSpec(memory_space=pl.ANY)
    weight_spec = pl.BlockSpec((depth, tile), lambda n, pairs: (0, n))
    out_spec = pl.BlockSpec((rows, tile), lambda n, pairs: (0, n))
    return pl.pallas_call(
        functools.partial(gate_up_kernel, half, rows, width),
        out_shape=(
            jax.ShapeDtypeStruct((rows, columns), jnp.float32),
            jax.ShapeDtypeStruct((rows, columns), jnp.float32),
            jax.ShapeDtypeStruct((2, rows, columns), jnp.bfloat16),
        ),
        grid_spec=pltpu.PrefetchScalarGridSpec(
            num_scalar_prefetch=1,
            grid=(columns // tile,),
            in_specs=[anywhere] * (3 * half + 1) + [weight_spec] * 2,
            out_specs=(out_spec, out_spec, pl.BlockSpec((2, rows, tile), lambda n, pairs: (0, 0, n))),
            scratch_shapes=[
                pltpu.VMEM((2 * rows, depth), jnp.bfloat16),
                pltpu.SemaphoreType.DMA((3, half)),
            ],
        ),
        compiler_params=pltpu.CompilerParams(vmem_limit_bytes=VMEM_LIMIT),
        cost_estimate=pl.CostEstimate(
            flops=8 * rows * depth * columns, bytes_accessed=4 * depth * columns, transcendentals=0
        ),
        name="gate_up",
    )(pairs, *first, *second, *last, *received, gate_weight, up_weight)


def down_kernel(tiles_ref, inv_ref, gate_ref, up_ref, received_ref, local_ref, other_ref, out_ref, hidden):
    @pl.when((pl.program_id(0) == 0) & (pl.program_id(1) == 0))
    def activate():
        inv = inv_ref[...]
        gate = (gate_ref[...] + received_ref[0].astype(jnp.float32)) * inv
        up = (up_ref[...] + received_ref[1].astype(jnp.float32)) * inv
        hidden[...] = (gate / (1.0 + jnp.exp(-gate)) * up).astype(jnp.bfloat16)

    def product(weight_ref):
        out_ref[0] = jnp.dot(hidden[...], weight_ref[...], preferred_element_type=jnp.float32).astype(jnp.bfloat16)

    local = tiles_ref[0, pl.program_id(0)] == 1
    pl.when(local)(functools.partial(product, local_ref))
    pl.when(jnp.logical_not(local))(functools.partial(product, other_ref))


def down(tiles, inv_rms, own_gate, own_up, received, local, other, width):
    rows, depth = own_gate.shape
    count = tiles.shape[1]
    whole = pl.BlockSpec((rows, depth), lambda j, t, tiles: (0, 0))

    def weight_spec(row):
        return pl.BlockSpec((depth, width), lambda j, t, tiles: (0, tiles[row, j]))

    return pl.pallas_call(
        down_kernel,
        out_shape=jax.ShapeDtypeStruct((count, rows, width), jnp.bfloat16),
        grid_spec=pltpu.PrefetchScalarGridSpec(
            num_scalar_prefetch=1,
            grid=(count, 1),
            in_specs=[
                pl.BlockSpec((rows, 1), lambda j, t, tiles: (0, 0)),
                whole,
                whole,
                pl.BlockSpec((2, rows, depth), lambda j, t, tiles: (0, 0, 0)),
                weight_spec(1),
                weight_spec(2),
            ],
            out_specs=pl.BlockSpec((1, rows, width), lambda j, t, tiles: (tiles[3, j], 0, 0)),
            scratch_shapes=[pltpu.VMEM((rows, depth), jnp.bfloat16)],
        ),
        compiler_params=pltpu.CompilerParams(vmem_limit_bytes=VMEM_LIMIT),
        cost_estimate=pl.CostEstimate(
            flops=2 * rows * depth * width * count,
            bytes_accessed=2 * depth * width * count,
            transcendentals=rows * depth,
        ),
        name="down",
    )(tiles, inv_rms, own_gate, own_up, received, local, other)


def gather(block, half, mine_first):
    rows = block.shape[0]
    before, after = [block], []
    ahead = block
    for step in range(1, half):
        before.append(ring_shift(before[-1], 1))
        ahead = ring_shift(ahead, -1)
        after.append(ahead)
    last = (ring_shift(before[-1][: rows // 2], 1), ring_shift(after[-1][rows // 2 :], -1))
    second = after[::-1]
    received = []
    for index in range(half):
        other = jnp.concatenate(last, axis=0) if index == 0 else second[index - 1]
        received.append(swap(jnp.where(mine_first[index], other, before[index])))
    return before, second, last, received


def scatter(terms):
    count, rows, _ = terms.shape
    half = count // 2
    cut = rows // 2

    def joined(one, two):
        return (one.astype(jnp.float32) + two.astype(jnp.float32)).astype(jnp.bfloat16)

    forth = ring_shift(terms[half, :cut], 1)
    back = ring_shift(terms[half, cut:], -1)
    for distance in range(half - 1, 0, -1):
        ahead, behind = terms[distance], terms[count - distance]
        if distance == half - 1:
            forth = jnp.concatenate([joined(ahead[:cut], forth), ahead[cut:]], axis=0)
            back = jnp.concatenate([behind[:cut], joined(behind[cut:], back)], axis=0)
        else:
            forth, back = joined(ahead, forth), joined(behind, back)
        forth, back = ring_shift(forth, 1), ring_shift(back, -1)
    return terms[0].astype(jnp.float32) + forth.astype(jnp.float32) + back.astype(jnp.float32)


def on_device(
    noisy_input,
    self_cond,
    cond_gain,
    bucket,
    conv_taps,
    norm_gain,
    gate_weight,
    up_weight,
    down_weight,
):
    row_count, width = noisy_input.shape
    count = lax.axis_size("blk")
    half = count // 2
    core, own = lax.axis_index("seq"), lax.axis_index("blk")
    pair_table, tile_table = tables_of(count)
    pairs = jnp.asarray(pair_table)[own, core]
    tiles = jnp.asarray(tile_table)[own, core]
    mine_first = pairs[0] == 1

    lead_rows = conv_taps.shape[1] - 1
    edges = lax.ppermute(
        (noisy_input[row_count - lead_rows :], self_cond[row_count - lead_rows :]), "seq", [(0, 1)]
    )
    other_down = swap(down_weight)
    chosen = lax.dynamic_index_in_dim(conv_taps, bucket[0], 0, keepdims=False)
    own_gain = lax.dynamic_slice_in_dim(norm_gain, own * width, width, 0)

    def mix(noisy, cond):
        return noisy.astype(jnp.float32) + cond_gain * cond.astype(jnp.float32)

    def convolve(start, size):
        if start == 0:
            extended = jnp.concatenate([mix(*edges), mix(noisy_input[:size], self_cond[:size])], axis=0)
        else:
            where = slice(start - lead_rows, start + size)
            extended = mix(noisy_input[where], self_cond[where])
        result = jnp.zeros((size, width), jnp.float32)
        for shift_by in range(lead_rows + 1):
            result = result + chosen[shift_by] * lax.slice_in_dim(
                extended, lead_rows - shift_by, lead_rows - shift_by + size, axis=0
            )
        return result.astype(jnp.bfloat16).astype(jnp.float32)

    unit = row_count // sum(CHUNKS)
    chunks, end = [], row_count
    for part in CHUNKS:
        chunks.append((end - part * unit, part * unit))
        end -= part * unit
    blocks, squares = [], []
    for start, size in chunks:
        convolved = convolve(start, size)
        blocks.append((convolved * own_gain).astype(jnp.bfloat16))
        squares.append(jnp.sum(convolved * convolved, axis=1))
    total = lax.psum(jnp.concatenate(squares), "blk")
    inv_rms = lax.rsqrt(total / (width * count) + 1e-05)[:, None]

    outs, done = [], 0
    for (start, size), block in zip(chunks, blocks):
        before, second, last, received = gather(block, half, mine_first)
        own_gate, own_up, sent = gate_up(pairs, before, second, last, received, gate_weight, up_weight)
        terms = down(
            tiles, inv_rms[done : done + size], own_gate, own_up, swap(sent), down_weight, other_down, width
        )
        done += size
        mixed = mix(noisy_input[start : start + size], self_cond[start : start + size])
        outs.append((mixed + scatter(terms)).astype(jnp.bfloat16))
    return jnp.concatenate(outs[::-1], axis=0)


def solution(mesh):
    in_specs = (
        P(("groups", "seq"), "blk"),
        P(("groups", "seq"), "blk"),
        P("blk"),
        P("groups"),
        P(None, None, "blk"),
        P(),
        P("seq", "blk"),
        P("seq", "blk"),
        P("blk", "seq"),
    )
    out_specs = P(("groups", "seq"), "blk")
    return jax.shard_map(
        on_device, mesh=mesh, in_specs=in_specs, out_specs=out_specs, check_vma=False
    )
```

time: 476 us -> 322 us (0.68)
  waiting for transfers between devices: 349 us -> 148 us
  Pallas kernels: 0 us -> 87 us
  matrix products: 72.9 us -> 0 us
  starting transfers between devices: 3.97 us -> 36.6 us
  blocking collectives: 0 us -> 20.6 us
  between operations: 13.9 us -> 1.23 us
  other arithmetic: 25.8 us -> 15.8 us
    all_gather x2 -> x0, waiting for transfers between devices: 181 us -> none  [the longest x1 127 us: on_device(): features = lax.all_gather(convolved, 'blk', axis=1, tiled=True)]
    reduce_scatter x3 -> x0, waiting for transfers between devices: 160 us -> none  [the longest x1 151 us: on_device(): lax.psum_scatter(block_terms.astype(jnp.bfloat16), 'blk', scatter_dimensi...]
    ppermute x3 -> x45, waiting for transfers between devices: 7.5 us -> 148 us  [the longest x32 132 us: ring_shift(): lax.ppermute(value, 'blk', [(ring[i], ring[(i + steps) % count]) for i in...]
    pallas_call x0 -> x4, Pallas kernels: none -> 87 us  [the longest x2 47.6 us: gate_up(): pl.pallas_call(functools.partial(gate_up_kernel, half, rows, width), out_...]
    dot_general x3 -> x0, matrix products: 72.9 us -> none  [the longest x1 27.3 us: on_device(): jnp.dot(hidden, lax.all_gather(down_weight, 'seq', axis=1, tiled=True), p...]
    ppermute x3 -> x45, starting transfers between devices: 3.63 us -> 36.6 us  [the longest x32 30 us: ring_shift(): lax.ppermute(value, 'blk', [(ring[i], ring[(i + steps) % count]) for i in...]
    psum x0 -> x1, blocking collectives: none -> 20.6 us  [on_device(): total = lax.psum(jnp.concatenate(squares), 'blk')]
    convert_element_type x3 -> x11, other arithmetic: 14.3 us -> 4.8 us  [the longest x1 2.04 us: on_device(): blocks.append((convolved * own_gain).astype(jnp.bfloat16))]
  transfers between devices with their start and end apart: 8 -> 45, of which waited for: 5 -> 22; matrix products, arithmetic and copies ran while one was open for 6% -> 6% of each run, Pallas kernels for 0% -> 27%
where the time goes in v1:
time: 322 us; the launch traced here: 321 us
  waiting for transfers between devices  148 us (46%)
  Pallas kernels  87 us (27%)
  starting transfers between devices  36.6 us (11%)
  blocking collectives  20.6 us (6%)
  other arithmetic  15.8 us (5%)
  local copies, waits for them, and re-layouts  11.2 us (3%)
    ppermute x32, waiting for transfers between devices, ring_shift(): lax.ppermute(value, 'blk', [(ring[i], ring[(i + steps) % count]) for i in...  132 us
    pallas_call x2, Pallas kernels, gate_up(): pl.pallas_call(functools.partial(gate_up_kernel, half, rows, width), out_...  47.6 us
    pallas_call x2, Pallas kernels, down(): pl.pallas_call(down_kernel, out_shape=jax.ShapeDtypeStruct((count, rows,...  39.4 us
    ppermute x32, starting transfers between devices, ring_shift(): lax.ppermute(value, 'blk', [(ring[i], ring[(i + steps) % count]) for i in...  30 us
    psum x1, blocking collectives, on_device(): total = lax.psum(jnp.concatenate(squares), 'blk')  20.6 us
    ppermute x2, waiting for transfers between devices, on_device(): lax.ppermute((noisy_input[row_count - lead_rows:], self_cond[row_count -...  15.9 us
    select_n x8, other arithmetic, gather(): received.append(swap(jnp.where(mine_first[index], other, before[index])))  7.76 us
  transfers between devices with their start and end apart: 45, of which 22 were waited for; matrix products, arithmetic and copies ran while one was open for 6% of the time, Pallas kernels for 27%

profile of v1, /device:TPU:0, one launch (start us, length us, event | category | flops | bytes accessed | tf_op | source)
XLA Modules:
  0.0 320.9 jit_solution(10142165688619368030)
XLA Ops:
  0.5 0.7 slice.221
  1.2 2.0 collective-permute-start
  3.2 0.7 slice.222
  3.9 1.3 collective-permute-start.1
  5.9 1.5 multiply_add_fusion.1
  7.7 0.9 constant_dynamic-slice_fusion.2
  8.6 0.7 dynamic_slice.16
  9.3 15.9 %collective-permute-done = bf16[3,1024]{1,0:T(4,128)(2,1)S(1)} collective-permute-done((bf16[3,1024]{1,0:T(4,128)(2,1)S(1)}, bf16[3,1024]{1,0:T(4,128)(2,1)S(1)}, u32[]{:S(2)}, u32[]{:S(2)}) %collective-permute-start) | collective-permute-done | bytes 6176 | tf_op jit(solution)/shard_map/ppermute | solution.py:253
  25.3 2.0 fusion.1
  27.3 2.6 collective-permute-start.2
  29.9 2.0 collective-permute-start.24
  31.9 10.7 %collective-permute-done.2.refs_1_ = bf16[256,1024]{1,0:T(8,128)(2,1)S(1)} collective-permute-done((bf16[256,1024]{1,0:T(8,128)(2,1)S(1)}, bf16[256,1024]{1,0:T(8,128)(2,1)S(1)}, u32[]{:S(2)}, u32[]{:S(2)}) %collective-permute-start.2) | collective-permute-done | bytes 524320 | tf_op jit(solution)/shard_map/ppermute | solution.py:57
  42.6 2.0 collective-permute-start.3
  44.8 9.0 %collective-permute-done.24.refs_1_ = bf16[256,1024]{1,0:T(8,128)(2,1)S(1)} collective-permute-done((bf16[256,1024]{1,0:T(8,128)(2,1)S(1)}, bf16[256,1024]{1,0:T(8,128)(2,1)S(1)}, u32[]{:S(2)}, u32[]{:S(2)}) %collective-permute-start.24) | collective-permute-done | bytes 524320 | tf_op jit(solution)/shard_map/ppermute | solution.py:57
  53.9 2.0 collective-permute-start.25
  55.9 0.7 constant_dynamic-slice_fusion.3
  56.6 0.7 fusion.39
  57.3 7.9 %collective-permute-done.3.refs_2_ = bf16[256,1024]{1,0:T(8,128)(2,1)} collective-permute-done((bf16[256,1024]{1,0:T(8,128)(2,1)S(1)}, bf16[256,1024]{1,0:T(8,128)(2,1)}, u32[]{:S(2)}, u32[]{:S(2)}) %collective-permute-start.3) | collective-permute-done | bytes 524320 | tf_op jit(solution)/shard_map/ppermute | solution.py:57
  65.2 2.0 collective-permute-start.4
  67.3 9.0 %collective-permute-done.25.refs_2_ = bf16[256,1024]{1,0:T(8,128)(2,1)S(1)} collective-permute-done((bf16[256,1024]{1,0:T(8,128)(2,1)S(1)}, bf16[256,1024]{1,0:T(8,128)(2,1)S(1)}, u32[]{:S(2)}, u32[]{:S(2)}) %collective-permute-start.25) | collective-permute-done | bytes 524320 | tf_op jit(solution)/shard_map/ppermute | solution.py:57
  76.3 2.0 collective-permute-start.26
  78.5 1.8 broadcast_select_fusion.3
  80.3 1.8 broadcast_select_fusion.2
  82.1 5.5 %collective-permute-done.4.refs_3_ = bf16[256,1024]{1,0:T(8,128)(2,1)S(1)} collective-permute-done((bf16[256,1024]{1,0:T(8,128)(2,1)}, bf16[256,1024]{1,0:T(8,128)(2,1)S(1)}, u32[]{:S(2)}, u32[]{:S(2)}) %collective-permute-start.4) | collective-permute-done | bytes 524320 | tf_op jit(solution)/shard_map/ppermute | solution.py:57
  87.6 2.1 collective-permute-start.8
  89.8 9.0 %collective-permute-done.26.refs_3_ = bf16[256,1024]{1,0:T(8,128)(2,1)S(1)} collective-permute-done((bf16[256,1024]{1,0:T(8,128)(2,1)S(1)}, bf16[256,1024]{1,0:T(8,128)(2,1)S(1)}, u32[]{:S(2)}, u32[]{:S(2)}) %collective-permute-start.26) | collective-permute-done | bytes 524320 | tf_op jit(solution)/shard_map/ppermute | solution.py:57
  98.8 2.1 collective-permute-start.30
  101.0 0.7 broadcast_select_fusion.5
  101.7 0.6 broadcast_select_fusion.1
  102.3 2.1 collective-permute-done.8.refs_7_
  104.4 2.1 collective-permute-done.9.refs_8_
  106.5 0.8 maximum_select_fusion
  107.3 2.4 collective-permute-done.30.refs_7_
  109.7 1.5 collective-permute-done.31.refs_8_
  111.2 0.6 broadcast_select_fusion
  111.9 0.7 broadcast_select_fusion.4
  112.5 0.8 maximum_select_fusion.1
  114.6 24.4 %gate_up.2 = (f32[256,2048]{1,0:T(8,128)S(1)}, f32[256,2048]{1,0:T(8,128)S(1)}, bf16[2,256,2048]{2,1,0:T(8,128)(2,1)}) custom-call(s32[2,4]{1,0:T(2,128)S(1)} %get-tuple-element.44.pairs_ref, bf16[256,1024]{1,0:T(8,128)(2,1)S(1)} %get-tuple-element.41.refs_0_, bf16[256,1024]{1,0:T(8,128)(2,1)S(1)} %copy-done.13, ...), custom_call_target="tpu_custom_call" | custom-call | flops 17179869184 | bytes 33554432 | tf_op jit(solution)/shard_map/gate_up/pallas_call | solution.py:118
  139.0 1.3 copy-done
  140.7 23.1 %gate_up.3 = (f32[256,2048]{1,0:T(8,128)S(1)}, f32[256,2048]{1,0:T(8,128)S(1)}, bf16[2,256,2048]{2,1,0:T(8,128)(2,1)}) custom-call(s32[2,4]{1,0:T(2,128)S(1)} %get-tuple-element.44.pairs_ref, bf16[256,1024]{1,0:T(8,128)(2,1)S(1)} %get-tuple-element.19.refs_0_, bf16[256,1024]{1,0:T(8,128)(2,1)S(1)} %copy-done.7, bf16[256,1024]{1,0:T(8,128)(2,1)S(1)} %copy-done.11, ...), custom_call_target="tpu_custom_call" | custom-call | flops 17179869184 | bytes 33554432 | tf_op jit(solution)/shard_map/gate_up/pallas_call | solution.py:118
  163.8 1.3 copy-done.2
  165.1 1.3 copy-done.4
  166.4 1.4 collective-permute-start.36
  167.8 0.7 dynamic-slice_bitcast_fusion.tiles_ref
  168.8 20.6 %psum.7 = f32[512]{0:T(512)S(1)} all-reduce(f32[512]{0:T(512)S(1)} %pad_maximum_fusion.6), channel_id=1, replica_groups=mesh['groups'=2,'blk'=8,'seq'=2] {'blk'}, use_global_device_ids=true, to_apply=%region_2.3 | all-reduce | flops 512 | bytes 4096 | tf_op jit(solution)/shard_map/psum | solution.py:286
  189.8 1.6 copy-done.1
  191.4 19.7 %down.2 = bf16[8,256,1024]{2,1,0:T(8,128)(2,1)S(1)} custom-call(s32[4,8]{1,0:T(4,128)S(1)} %dynamic-slice_bitcast_fusion.tiles_ref, f32[256,1]{1,0:T(8,128)S(1)} %copy.12.inv_ref, f32[256,2048]{1,0:T(8,128)S(1)} %get-tuple-element.11.gate_ref, f32[256,2048]{1,0:T(8,128)S(1)} %copy-done.1, bf16[2,256,2048]{2,1,0:T(8,128)(2,1)} %collective-permute-done.14.received_ref, ...), custom_call_target="tpu_custom_call" | custom-call | flops 8589934592 | bytes 33554432 | tf_op jit(solution)/shard_map/down/pallas_call | solution.py:167
  211.2 2.0 collective-permute-start.20
  213.3 19.7 %down.3 = bf16[8,256,1024]{2,1,0:T(8,128)(2,1)S(1)} custom-call(s32[4,8]{1,0:T(4,128)S(1)} %dynamic-slice_bitcast_fusion.tiles_ref, f32[256,1]{1,0:T(8,128)S(1)} %copy.13.inv_ref, f32[256,2048]{1,0:T(8,128)S(1)} %copy-done.3, f32[256,2048]{1,0:T(8,128)S(1)} %copy-done.5, bf16[2,256,2048]{2,1,0:T(8,128)(2,1)} %collective-permute-done.36.received_ref, ...), custom_call_target="tpu_custom_call" | custom-call | flops 8589934592 | bytes 33554432 | tf_op jit(solution)/shard_map/down/pallas_call | solution.py:167
  233.1 2.0 collective-permute-start.41
  235.5 6.9 %collective-permute-done.37 = bf16[128,1024]{1,0:T(8,128)(2,1)S(1)} collective-permute-done((bf16[128,1024]{1,0:T(8,128)(2,1)S(1)}, bf16[128,1024]{1,0:T(8,128)(2,1)S(1)}, u32[]{:S(2)}, u32[]{:S(2)}) %collective-permute-start.37) | collective-permute-done | bytes 262176 | tf_op jit(solution)/shard_map/ppermute | solution.py:57
  242.7 2.1 collective-permute-start.21
  244.7 8.8 %collective-permute-done.17 = bf16[256,1024]{1,0:T(8,128)(2,1)S(1)} collective-permute-done((bf16[256,1024]{1,0:T(8,128)(2,1)S(1)}, bf16[256,1024]{1,0:T(8,128)(2,1)S(1)}, u32[]{:S(2)}, u32[]{:S(2)}) %collective-permute-start.17) | collective-permute-done | bytes 524320 | tf_op jit(solution)/shard_map/ppermute | solution.py:57
  253.9 2.1 collective-permute-start.42
  255.9 8.9 %collective-permute-done.38 = bf16[256,1024]{1,0:T(8,128)(2,1)S(1)} collective-permute-done((bf16[256,1024]{1,0:T(8,128)(2,1)S(1)}, bf16[256,1024]{1,0:T(8,128)(2,1)S(1)}, u32[]{:S(2)}, u32[]{:S(2)}) %collective-permute-start.38) | collective-permute-done | bytes 524320 | tf_op jit(solution)/shard_map/ppermute | solution.py:57
  265.1 11.0 %collective-permute-done.18 = bf16[256,1024]{1,0:T(8,128)(2,1)S(1)} collective-permute-done((bf16[256,1024]{1,0:T(8,128)(2,1)S(1)}, bf16[256,1024]{1,0:T(8,128)(2,1)S(1)}, u32[]{:S(2)}, u32[]{:S(2)}) %collective-permute-start.18) | collective-permute-done | bytes 524320 | tf_op jit(solution)/shard_map/ppermute | solution.py:57
  276.6 7.0 %collective-permute-done.39 = bf16[256,1024]{1,0:T(8,128)(2,1)S(1)} collective-permute-done((bf16[256,1024]{1,0:T(8,128)(2,1)S(1)}, bf16[256,1024]{1,0:T(8,128)(2,1)S(1)}, u32[]{:S(2)}, u32[]{:S(2)}) %collective-permute-start.39) | collective-permute-done | bytes 524320 | tf_op jit(solution)/shard_map/ppermute | solution.py:57
  284.6 1.6 collective-permute-start.19
  286.1 4.5 %collective-permute-done.22 = bf16[256,1024]{1,0:T(8,128)(2,1)S(1)} collective-permute-done((bf16[256,1024]{1,0:T(8,128)(2,1)S(1)}, bf16[256,1024]{1,0:T(8,128)(2,1)S(1)}, u32[]{:S(2)}, u32[]{:S(2)}) %collective-permute-start.22) | collective-permute-done | bytes 524320 | tf_op jit(solution)/shard_map/ppermute | solution.py:57
  290.9 2.0 collective-permute-start.40
  292.9 9.0 %collective-permute-done.43 = bf16[256,1024]{1,0:T(8,128)(2,1)S(1)} collective-permute-done((bf16[256,1024]{1,0:T(8,128)(2,1)S(1)}, bf16[256,1024]{1,0:T(8,128)(2,1)S(1)}, u32[]{:S(2)}, u32[]{:S(2)}) %collective-permute-start.43) | collective-permute-done | bytes 524320 | tf_op jit(solution)/shard_map/ppermute | solution.py:57
  302.1 11.0 %collective-permute-done.23 = bf16[256,1024]{1,0:T(8,128)(2,1)S(1)} collective-permute-done((bf16[256,1024]{1,0:T(8,128)(2,1)S(1)}, bf16[256,1024]{1,0:T(8,128)(2,1)S(1)}, u32[]{:S(2)}, u32[]{:S(2)}) %collective-permute-start.23) | collective-permute-done | bytes 524320 | tf_op jit(solution)/shard_map/ppermute | solution.py:57
  313.4 5.9 %collective-permute-done.44 = bf16[256,1024]{1,0:T(8,128)(2,1)S(1)} collective-permute-done((bf16[256,1024]{1,0:T(8,128)(2,1)S(1)}, bf16[256,1024]{1,0:T(8,128)(2,1)S(1)}, u32[]{:S(2)}, u32[]{:S(2)}) %collective-permute-start.44) | collective-permute-done | bytes 524320 | tf_op jit(solution)/shard_map/ppermute | solution.py:57
  319.9 1.0 pad_maximum_fusion.1
  (124 shorter events, 7.8 us)
Async XLA Ops:
  0.0 7.4 %copy-start.16 = (bf16[512,1024]{1,0:T(8,128)(2,1)S(1)}, bf16[512,1024]{1,0:T(8,128)(2,1)}, u32[]{:S(2)}) copy-start(bf16[512,1024]{1,0:T(8,128)(2,1)} %param.12) | copy-start | bytes 3145732
  0.0 7.4 %copy-start.22 = (f32[1024]{0:T(1024)S(1)}, f32[1024]{0:T(1024)}, u32[]{:S(2)}) copy-start(f32[1024]{0:T(1024)} %param.13) | copy-start | bytes 12292
  0.0 189.7 %collective-permute-start.15 = (bf16[2048,4096]{1,0:T(8,128)(2,1)}, bf16[2048,4096]{1,0:T(8,128)(2,1)}, u32[]{:S(2)}, u32[]{:S(2)}) collective-permute-start(bf16[2048,4096]{1,0:T(8,128)(2,1)} %local_ref.3), channel_id=1, source_target_pairs={{0,1},{1,0},{2,3},{3,2},{4,5},{5,4},{6,7},{7,6},{8,9},{9,8},{10,11... | collective-permute-start | bytes 50331656 | tf_op jit(solution)/shard_map/ppermute | solution.py:61
  1.2 24.1 %collective-permute-start = (bf16[3,1024]{1,0:T(4,128)(2,1)S(1)}, bf16[3,1024]{1,0:T(4,128)(2,1)S(1)}, u32[]{:S(2)}, u32[]{:S(2)}) collective-permute-start(bf16[3,1024]{1,0:T(4,128)(2,1)S(1)} %slice.221), channel_id=1, source_target_pairs={{0,1},{2,3},{4,5},{6,7},{8,9},{10,11},{12,13},{14,15},{16,17},{18,... | collective-permute-start | bytes 18440 | tf_op jit(solution)/shard_map/ppermute | solution.py:253
  3.9 21.3 %collective-permute-start.1 = (bf16[3,1024]{1,0:T(4,128)(2,1)S(1)}, bf16[3,1024]{1,0:T(4,128)(2,1)S(1)}, u32[]{:S(2)}, u32[]{:S(2)}) collective-permute-start(bf16[3,1024]{1,0:T(4,128)(2,1)S(1)} %slice.222), channel_id=1, source_target_pairs={{0,1},{2,3},{4,5},{6,7},{8,9},{10,11},{12,13},{14,15},{16,17},{18,... | collective-permute-start | bytes 18440 | tf_op jit(solution)/shard_map/ppermute | solution.py:253
  7.4 19.9 %copy-start.14 = (f32[256,1024]{1,0:T(8,128)}, f32[256,1024]{1,0:T(8,128)S(1)}, u32[]{:S(2)}) copy-start(f32[256,1024]{1,0:T(8,128)S(1)} %multiply_add_fusion.1) | copy-start | bytes 3145732
  27.3 15.3 %collective-permute-start.2 = (bf16[256,1024]{1,0:T(8,128)(2,1)S(1)}, bf16[256,1024]{1,0:T(8,128)(2,1)S(1)}, u32[]{:S(2)}, u32[]{:S(2)}) collective-permute-start(bf16[256,1024]{1,0:T(8,128)(2,1)S(1)} %get-tuple-element.41.refs_0_), channel_id=1, source_target_pairs={{0,4},{4,8},{8,12},{12,14},{14,10},{10,6},{6,2},{2,0},{1,5},{5,9},... | collective-permute-start | bytes 1572872 | tf_op jit(solution)/shard_map/ppermute | solution.py:57
  29.9 14.9 %collective-permute-start.5 = (bf16[256,1024]{1,0:T(8,128)(2,1)S(1)}, bf16[256,1024]{1,0:T(8,128)(2,1)}, u32[]{:S(2)}, u32[]{:S(2)}) collective-permute-start(bf16[256,1024]{1,0:T(8,128)(2,1)S(1)} %get-tuple-element.41.refs_0_), channel_id=1, source_target_pairs={{0,2},{4,0},{8,4},{12,8},{14,12},{10,14},{6,10},{2,6},{1,3},{5,1},... | collective-permute-start | bytes 1572872 | tf_op jit(solution)/shard_map/ppermute | solution.py:57
  29.9 23.9 %collective-permute-start.24 = (bf16[256,1024]{1,0:T(8,128)(2,1)S(1)}, bf16[256,1024]{1,0:T(8,128)(2,1)S(1)}, u32[]{:S(2)}, u32[]{:S(2)}) collective-permute-start(bf16[256,1024]{1,0:T(8,128)(2,1)S(1)} %get-tuple-element.19.refs_0_), channel_id=1, source_target_pairs={{0,4},{4,8},{8,12},{12,14},{14,10},{10,6},{6,2},{2,0},{1,5},{5,9},... | collective-permute-start | bytes 1572872 | tf_op jit(solution)/shard_map/ppermute | solution.py:57
  31.9 24.0 %collective-permute-start.27 = (bf16[256,1024]{1,0:T(8,128)(2,1)S(1)}, bf16[256,1024]{1,0:T(8,128)(2,1)S(1)}, u32[]{:S(2)}, u32[]{:S(2)}) collective-permute-start(bf16[256,1024]{1,0:T(8,128)(2,1)S(1)} %get-tuple-element.19.refs_0_), channel_id=1, source_target_pairs={{0,2},{4,0},{8,4},{12,8},{14,12},{10,14},{6,10},{2,6},{1,3},{5,1},... | collective-permute-start | bytes 1572872 | tf_op jit(solution)/shard_map/ppermute | solution.py:57
  42.6 58.4 %copy-start.12 = (bf16[256,1024]{1,0:T(8,128)(2,1)}, bf16[256,1024]{1,0:T(8,128)(2,1)S(1)}, u32[]{:S(2)}) copy-start(bf16[256,1024]{1,0:T(8,128)(2,1)S(1)} %collective-permute-done.2.refs_1_) | copy-start | bytes 1572868
  42.6 22.6 %collective-permute-start.3 = (bf16[256,1024]{1,0:T(8,128)(2,1)S(1)}, bf16[256,1024]{1,0:T(8,128)(2,1)}, u32[]{:S(2)}, u32[]{:S(2)}) collective-permute-start(bf16[256,1024]{1,0:T(8,128)(2,1)S(1)} %collective-permute-done.2.refs_1_), channel_id=1, source_target_pairs={{0,4},{4,8},{8,12},{12,14},{14,10},{10,6},{6,2},{2,0},{1,5},{5,9},... | collective-permute-start | bytes 1572872 | tf_op jit(solution)/shard_map/ppermute | solution.py:57
  44.8 22.5 %collective-permute-start.6 = (bf16[256,1024]{1,0:T(8,128)(2,1)}, bf16[256,1024]{1,0:T(8,128)(2,1)}, u32[]{:S(2)}, u32[]{:S(2)}) collective-permute-start(bf16[256,1024]{1,0:T(8,128)(2,1)} %collective-permute-done.5.refs_6_), channel_id=1, source_target_pairs={{0,2},{4,0},{8,4},{12,8},{14,12},{10,14},{6,10},{2,6},{1,3},{5,1},... | collective-permute-start | bytes 1572872 | tf_op jit(solution)/shard_map/ppermute | solution.py:57
  53.9 58.0 %copy-start.6 = (bf16[256,1024]{1,0:T(8,128)(2,1)}, bf16[256,1024]{1,0:T(8,128)(2,1)S(1)}, u32[]{:S(2)}) copy-start(bf16[256,1024]{1,0:T(8,128)(2,1)S(1)} %collective-permute-done.24.refs_1_) | copy-start | bytes 1572868
  53.9 22.5 %collective-permute-start.25 = (bf16[256,1024]{1,0:T(8,128)(2,1)S(1)}, bf16[256,1024]{1,0:T(8,128)(2,1)S(1)}, u32[]{:S(2)}, u32[]{:S(2)}) collective-permute-start(bf16[256,1024]{1,0:T(8,128)(2,1)S(1)} %collective-permute-done.24.refs_1_), channel_id=1, source_target_pairs={{0,4},{4,8},{8,12},{12,14},{14,10},{10,6},{6,2},{2,0},{1,5},{5,9},... | collective-permute-start | bytes 1572872 | tf_op jit(solution)/shard_map/ppermute | solution.py:57
  55.9 55.3 %copy-start.8 = (bf16[256,1024]{1,0:T(8,128)(2,1)}, bf16[256,1024]{1,0:T(8,128)(2,1)S(1)}, u32[]{:S(2)}) copy-start(bf16[256,1024]{1,0:T(8,128)(2,1)S(1)} %collective-permute-done.27.refs_6_) | copy-start | bytes 1572868
  55.9 22.6 %collective-permute-start.28 = (bf16[256,1024]{1,0:T(8,128)(2,1)S(1)}, bf16[256,1024]{1,0:T(8,128)(2,1)}, u32[]{:S(2)}, u32[]{:S(2)}) collective-permute-start(bf16[256,1024]{1,0:T(8,128)(2,1)S(1)} %collective-permute-done.27.refs_6_), channel_id=1, source_target_pairs={{0,2},{4,0},{8,4},{12,8},{14,12},{10,14},{6,10},{2,6},{1,3},{5,1},... | collective-permute-start | bytes 1572872 | tf_op jit(solution)/shard_map/ppermute | solution.py:57
  65.2 22.4 %collective-permute-start.4 = (bf16[256,1024]{1,0:T(8,128)(2,1)}, bf16[256,1024]{1,0:T(8,128)(2,1)S(1)}, u32[]{:S(2)}, u32[]{:S(2)}) collective-permute-start(bf16[256,1024]{1,0:T(8,128)(2,1)} %collective-permute-done.3.refs_2_), channel_id=1, source_target_pairs={{0,4},{4,8},{8,12},{12,14},{14,10},{10,6},{6,2},{2,0},{1,5},{5,9},... | collective-permute-start | bytes 1572872 | tf_op jit(solution)/shard_map/ppermute | solution.py:57
  67.3 22.4 %collective-permute-start.7 = (bf16[256,1024]{1,0:T(8,128)(2,1)}, bf16[256,1024]{1,0:T(8,128)(2,1)S(1)}, u32[]{:S(2)}, u32[]{:S(2)}) collective-permute-start(bf16[256,1024]{1,0:T(8,128)(2,1)} %collective-permute-done.6.refs_5_), channel_id=1, source_target_pairs={{0,2},{4,0},{8,4},{12,8},{14,12},{10,14},{6,10},{2,6},{1,3},{5,1},... | collective-permute-start | bytes 1572872 | tf_op jit(solution)/shard_map/ppermute | solution.py:57
  76.3 13.4 %copy-start.10 = (bf16[256,1024]{1,0:T(8,128)(2,1)}, bf16[256,1024]{1,0:T(8,128)(2,1)S(1)}, u32[]{:S(2)}) copy-start(bf16[256,1024]{1,0:T(8,128)(2,1)S(1)} %collective-permute-done.25.refs_2_) | copy-start | bytes 1572868
  76.3 22.5 %collective-permute-start.26 = (bf16[256,1024]{1,0:T(8,128)(2,1)S(1)}, bf16[256,1024]{1,0:T(8,128)(2,1)S(1)}, u32[]{:S(2)}, u32[]{:S(2)}) collective-permute-start(bf16[256,1024]{1,0:T(8,128)(2,1)S(1)} %collective-permute-done.25.refs_2_), channel_id=1, source_target_pairs={{0,4},{4,8},{8,12},{12,14},{14,10},{10,6},{6,2},{2,0},{1,5},{5,9},... | collective-permute-start | bytes 1572872 | tf_op jit(solution)/shard_map/ppermute | solution.py:57
  78.5 22.4 %collective-permute-start.29 = (bf16[256,1024]{1,0:T(8,128)(2,1)}, bf16[256,1024]{1,0:T(8,128)(2,1)S(1)}, u32[]{:S(2)}, u32[]{:S(2)}) collective-permute-start(bf16[256,1024]{1,0:T(8,128)(2,1)} %collective-permute-done.28.refs_5_), channel_id=1, source_target_pairs={{0,2},{4,0},{8,4},{12,8},{14,12},{10,14},{6,10},{2,6},{1,3},{5,1},... | collective-permute-start | bytes 1572872 | tf_op jit(solution)/shard_map/ppermute | solution.py:57
  87.6 16.8 %collective-permute-start.8 = (bf16[128,1024]{1,0:T(8,128)(2,1)S(1)}, bf16[128,1024]{1,0:T(8,128)(2,1)S(1)}, u32[]{:S(2)}, u32[]{:S(2)}) collective-permute-start(bf16[128,1024]{1,0:T(8,128)(2,1)S(1)} %slice.275), channel_id=1, source_target_pairs={{0,4},{4,8},{8,12},{12,14},{14,10},{10,6},{6,2},{2,0},{1,5},{5,9},... | collective-permute-start | bytes 786440 | tf_op jit(solution)/shard_map/ppermute | solution.py:57
  89.7 16.8 %collective-permute-start.9 = (bf16[128,1024]{1,0:T(8,128)(2,1)S(1)}, bf16[128,1024]{1,0:T(8,128)(2,1)S(1)}, u32[]{:S(2)}, u32[]{:S(2)}) collective-permute-start(bf16[128,1024]{1,0:T(8,128)(2,1)S(1)} %slice.276), channel_id=1, source_target_pairs={{0,2},{4,0},{8,4},{12,8},{14,12},{10,14},{6,10},{2,6},{1,3},{5,1},... | collective-permute-start | bytes 786440 | tf_op jit(solution)/shard_map/ppermute | solution.py:57
  98.8 10.9 %collective-permute-start.30 = (bf16[128,1024]{1,0:T(8,128)(2,1)S(1)}, bf16[128,1024]{1,0:T(8,128)(2,1)S(1)}, u32[]{:S(2)}, u32[]{:S(2)}) collective-permute-start(bf16[128,1024]{1,0:T(8,128)(2,1)S(1)} %slice.288), channel_id=1, source_target_pairs={{0,4},{4,8},{8,12},{12,14},{14,10},{10,6},{6,2},{2,0},{1,5},{5,9},... | collective-permute-start | bytes 786440 | tf_op jit(solution)/shard_map/ppermute | solution.py:57
  100.9 10.3 %collective-permute-start.31 = (bf16[128,1024]{1,0:T(8,128)(2,1)S(1)}, bf16[128,1024]{1,0:T(8,128)(2,1)S(1)}, u32[]{:S(2)}, u32[]{:S(2)}) collective-permute-start(bf16[128,1024]{1,0:T(8,128)(2,1)S(1)} %slice.289), channel_id=1, source_target_pairs={{0,2},{4,0},{8,4},{12,8},{14,12},{10,14},{6,10},{2,6},{1,3},{5,1},... | collective-permute-start | bytes 786440 | tf_op jit(solution)/shard_map/ppermute | solution.py:57
  104.4 8.9 %collective-permute-start.12 = (bf16[256,1024]{1,0:T(8,128)(2,1)S(1)}, bf16[256,1024]{1,0:T(8,128)(2,1)S(1)}, u32[]{:S(2)}, u32[]{:S(2)}) collective-permute-start(bf16[256,1024]{1,0:T(8,128)(2,1)S(1)} %broadcast_select_fusion.3), channel_id=1, source_target_pairs={{0,1},{1,0},{2,3},{3,2},{4,5},{5,4},{6,7},{7,6},{8,9},{9,8},{10,11... | collective-permute-start | bytes 1572872 | tf_op jit(solution)/shard_map/ppermute | solution.py:61
  106.5 7.4 %collective-permute-start.11 = (bf16[256,1024]{1,0:T(8,128)(2,1)S(1)}, bf16[256,1024]{1,0:T(8,128)(2,1)S(1)}, u32[]{:S(2)}, u32[]{:S(2)}) collective-permute-start(bf16[256,1024]{1,0:T(8,128)(2,1)S(1)} %broadcast_select_fusion.5), channel_id=1, source_target_pairs={{0,1},{1,0},{2,3},{3,2},{4,5},{5,4},{6,7},{7,6},{8,9},{9,8},{10,11... | collective-permute-start | bytes 1572872 | tf_op jit(solution)/shard_map/ppermute | solution.py:61
  107.3 7.2 %copy-start.13 = (bf16[256,1024]{1,0:T(8,128)(2,1)S(1)}, bf16[256,1024]{1,0:T(8,128)(2,1)}, u32[]{:S(2)}) copy-start(bf16[256,1024]{1,0:T(8,128)(2,1)} %copy-done.12) | copy-start | bytes 1572868
  109.7 4.3 %collective-permute-start.13 = (bf16[256,1024]{1,0:T(8,128)(2,1)S(1)}, bf16[256,1024]{1,0:T(8,128)(2,1)S(1)}, u32[]{:S(2)}, u32[]{:S(2)}) collective-permute-start(bf16[256,1024]{1,0:T(8,128)(2,1)S(1)} %broadcast_select_fusion.1), channel_id=1, source_target_pairs={{0,1},{1,0},{2,3},{3,2},{4,5},{5,4},{6,7},{7,6},{8,9},{9,8},{10,11... | collective-permute-start | bytes 1572872 | tf_op jit(solution)/shard_map/ppermute | solution.py:61
  111.2 3.2 %collective-permute-start.10 = (bf16[256,1024]{1,0:T(8,128)(2,1)S(1)}, bf16[256,1024]{1,0:T(8,128)(2,1)S(1)}, u32[]{:S(2)}, u32[]{:S(2)}) collective-permute-start(bf16[256,1024]{1,0:T(8,128)(2,1)S(1)} %maximum_select_fusion), channel_id=1, source_target_pairs={{0,1},{1,0},{2,3},{3,2},{4,5},{5,4},{6,7},{7,6},{8,9},{9,8},{10,11... | collective-permute-start | bytes 1572872 | tf_op jit(solution)/shard_map/ppermute | solution.py:61
  113.4 27.0 %collective-permute-start.34 = (bf16[256,1024]{1,0:T(8,128)(2,1)S(1)}, bf16[256,1024]{1,0:T(8,128)(2,1)S(1)}, u32[]{:S(2)}, u32[]{:S(2)}) collective-permute-start(bf16[256,1024]{1,0:T(8,128)(2,1)S(1)} %broadcast_select_fusion.2), channel_id=1, source_target_pairs={{0,1},{1,0},{2,3},{3,2},{4,5},{5,4},{6,7},{7,6},{8,9},{9,8},{10,11... | collective-permute-start | bytes 1572872 | tf_op jit(solution)/shard_map/ppermute | solution.py:61
  113.9 26.7 %collective-permute-start.35 = (bf16[256,1024]{1,0:T(8,128)(2,1)S(1)}, bf16[256,1024]{1,0:T(8,128)(2,1)S(1)}, u32[]{:S(2)}, u32[]{:S(2)}) collective-permute-start(bf16[256,1024]{1,0:T(8,128)(2,1)S(1)} %broadcast_select_fusion), channel_id=1, source_target_pairs={{0,1},{1,0},{2,3},{3,2},{4,5},{5,4},{6,7},{7,6},{8,9},{9,8},{10,11... | collective-permute-start | bytes 1572872 | tf_op jit(solution)/shard_map/ppermute | solution.py:61
  114.0 26.6 %collective-permute-start.33 = (bf16[256,1024]{1,0:T(8,128)(2,1)S(1)}, bf16[256,1024]{1,0:T(8,128)(2,1)S(1)}, u32[]{:S(2)}, u32[]{:S(2)}) collective-permute-start(bf16[256,1024]{1,0:T(8,128)(2,1)S(1)} %broadcast_select_fusion.4), channel_id=1, source_target_pairs={{0,1},{1,0},{2,3},{3,2},{4,5},{5,4},{6,7},{7,6},{8,9},{9,8},{10,11... | collective-permute-start | bytes 1572872 | tf_op jit(solution)/shard_map/ppermute | solution.py:61
  114.5 26.2 %collective-permute-start.32 = (bf16[256,1024]{1,0:T(8,128)(2,1)S(1)}, bf16[256,1024]{1,0:T(8,128)(2,1)S(1)}, u32[]{:S(2)}, u32[]{:S(2)}) collective-permute-start(bf16[256,1024]{1,0:T(8,128)(2,1)S(1)} %maximum_select_fusion.1), channel_id=1, source_target_pairs={{0,1},{1,0},{2,3},{3,2},{4,5},{5,4},{6,7},{7,6},{8,9},{9,8},{10,11... | collective-permute-start | bytes 1572872 | tf_op jit(solution)/shard_map/ppermute | solution.py:61
  114.5 26.1 %copy-start.7 = (bf16[256,1024]{1,0:T(8,128)(2,1)S(1)}, bf16[256,1024]{1,0:T(8,128)(2,1)}, u32[]{:S(2)}) copy-start(bf16[256,1024]{1,0:T(8,128)(2,1)} %copy-done.6) | copy-start | bytes 1572868
  114.5 26.1 %copy-start.9 = (bf16[256,1024]{1,0:T(8,128)(2,1)S(1)}, bf16[256,1024]{1,0:T(8,128)(2,1)}, u32[]{:S(2)}) copy-start(bf16[256,1024]{1,0:T(8,128)(2,1)} %copy-done.8) | copy-start | bytes 1572868
  114.5 26.1 %copy-start.11 = (bf16[256,1024]{1,0:T(8,128)(2,1)S(1)}, bf16[256,1024]{1,0:T(8,128)(2,1)}, u32[]{:S(2)}) copy-start(bf16[256,1024]{1,0:T(8,128)(2,1)} %copy-done.10) | copy-start | bytes 1572868
  140.4 28.1 %copy-start.20 = (bf16[256,1024]{1,0:T(8,128)(2,1)S(1)}, bf16[256,1024]{1,0:T(8,128)(2,1)}, u32[]{:S(2)}) copy-start(bf16[256,1024]{1,0:T(8,128)(2,1)} %get-tuple-element.20) | copy-start | bytes 1572868
  140.4 28.1 %copy-start.21 = (bf16[256,1024]{1,0:T(8,128)(2,1)S(1)}, bf16[256,1024]{1,0:T(8,128)(2,1)}, u32[]{:S(2)}) copy-start(bf16[256,1024]{1,0:T(8,128)(2,1)} %get-tuple-element.42) | copy-start | bytes 1572868
  140.4 49.4 %collective-permute-start.14 = (bf16[2,256,2048]{2,1,0:T(8,128)(2,1)}, bf16[2,256,2048]{2,1,0:T(8,128)(2,1)}, u32[]{:S(2)}, u32[]{:S(2)}) collective-permute-start(bf16[2,256,2048]{2,1,0:T(8,128)(2,1)} %get-tuple-element.13), channel_id=1, source_target_pairs={{0,1},{1,0},{2,3},{3,2},{4,5},{5,4},{6,7},{7,6},{8,9},{9,8},{10,11... | collective-permute-start | bytes 6291464 | tf_op jit(solution)/shard_map/ppermute | solution.py:61
  166.4 46.8 %collective-permute-start.36 = (bf16[2,256,2048]{2,1,0:T(8,128)(2,1)}, bf16[2,256,2048]{2,1,0:T(8,128)(2,1)}, u32[]{:S(2)}, u32[]{:S(2)}) collective-permute-start(bf16[2,256,2048]{2,1,0:T(8,128)(2,1)} %get-tuple-element.16), channel_id=1, source_target_pairs={{0,1},{1,0},{2,3},{3,2},{4,5},{5,4},{6,7},{7,6},{8,9},{9,8},{10,11... | collective-permute-start | bytes 6291464 | tf_op jit(solution)/shard_map/ppermute | solution.py:61
  189.8 1.6 copy-start.1
  191.3 21.9 %copy-start.5 = (f32[256,2048]{1,0:T(8,128)S(1)}, f32[256,2048]{1,0:T(8,128)}, u32[]{:S(2)}) copy-start(f32[256,2048]{1,0:T(8,128)} %copy-done.4) | copy-start | bytes 6291460
  211.1 2.2 copy-start.3
  211.2 23.9 %collective-permute-start.16 = (bf16[128,1024]{1,0:T(8,128)(2,1)S(1)}, bf16[128,1024]{1,0:T(8,128)(2,1)S(1)}, u32[]{:S(2)}, u32[]{:S(2)}) collective-permute-start(bf16[128,1024]{1,0:T(8,128)(2,1)S(1)} %get-tuple-element.25), channel_id=1, source_target_pairs={{0,4},{4,8},{8,12},{12,14},{14,10},{10,6},{6,2},{2,0},{1,5},{5,9},... | collective-permute-start | bytes 786440 | tf_op jit(solution)/shard_map/ppermute | solution.py:57
  211.2 23.9 %collective-permute-start.20 = (bf16[128,1024]{1,0:T(8,128)(2,1)S(1)}, bf16[128,1024]{1,0:T(8,128)(2,1)S(1)}, u32[]{:S(2)}, u32[]{:S(2)}) collective-permute-start(bf16[128,1024]{1,0:T(8,128)(2,1)S(1)} %get-tuple-element.26), channel_id=1, source_target_pairs={{0,2},{4,0},{8,4},{12,8},{14,12},{10,14},{6,10},{2,6},{1,3},{5,1},... | collective-permute-start | bytes 786440 | tf_op jit(solution)/shard_map/ppermute | solution.py:57
  233.0 9.3 %collective-permute-start.37 = (bf16[128,1024]{1,0:T(8,128)(2,1)S(1)}, bf16[128,1024]{1,0:T(8,128)(2,1)S(1)}, u32[]{:S(2)}, u32[]{:S(2)}) collective-permute-start(bf16[128,1024]{1,0:T(8,128)(2,1)S(1)} %get-tuple-element.33), channel_id=1, source_target_pairs={{0,4},{4,8},{8,12},{12,14},{14,10},{10,6},{6,2},{2,0},{1,5},{5,9},... | collective-permute-start | bytes 786440 | tf_op jit(solution)/shard_map/ppermute | solution.py:57
  233.1 9.2 %collective-permute-start.41 = (bf16[128,1024]{1,0:T(8,128)(2,1)S(1)}, bf16[128,1024]{1,0:T(8,128)(2,1)S(1)}, u32[]{:S(2)}, u32[]{:S(2)}) collective-permute-start(bf16[128,1024]{1,0:T(8,128)(2,1)S(1)} %get-tuple-element.34), channel_id=1, source_target_pairs={{0,2},{4,0},{8,4},{12,8},{14,12},{10,14},{6,10},{2,6},{1,3},{5,1},... | collective-permute-start | bytes 786440 | tf_op jit(solution)/shard_map/ppermute | solution.py:57
  235.4 18.2 %collective-permute-start.17 = (bf16[256,1024]{1,0:T(8,128)(2,1)S(1)}, bf16[256,1024]{1,0:T(8,128)(2,1)S(1)}, u32[]{:S(2)}, u32[]{:S(2)}) collective-permute-start(bf16[256,1024]{1,0:T(8,128)(2,1)S(1)} %pad_maximum_fusion.2), channel_id=1, source_target_pairs={{0,4},{4,8},{8,12},{12,14},{14,10},{10,6},{6,2},{2,0},{1,5},{5,9},... | collective-permute-start | bytes 1572872 | tf_op jit(solution)/shard_map/ppermute | solution.py:57
  242.6 22.2 %collective-permute-start.38 = (bf16[256,1024]{1,0:T(8,128)(2,1)S(1)}, bf16[256,1024]{1,0:T(8,128)(2,1)S(1)}, u32[]{:S(2)}, u32[]{:S(2)}) collective-permute-start(bf16[256,1024]{1,0:T(8,128)(2,1)S(1)} %pad_maximum_fusion.4), channel_id=1, source_target_pairs={{0,4},{4,8},{8,12},{12,14},{14,10},{10,6},{6,2},{2,0},{1,5},{5,9},... | collective-permute-start | bytes 1572872 | tf_op jit(solution)/shard_map/ppermute | solution.py:57
  242.7 22.4 %collective-permute-start.21 = (bf16[256,1024]{1,0:T(8,128)(2,1)S(1)}, bf16[256,1024]{1,0:T(8,128)(2,1)S(1)}, u32[]{:S(2)}, u32[]{:S(2)}) collective-permute-start(bf16[256,1024]{1,0:T(8,128)(2,1)S(1)} %pad_maximum_fusion.3), channel_id=1, source_target_pairs={{0,2},{4,0},{8,4},{12,8},{14,12},{10,14},{6,10},{2,6},{1,3},{5,1},... | collective-permute-start | bytes 1572872 | tf_op jit(solution)/shard_map/ppermute | solution.py:57
  253.8 22.3 %collective-permute-start.18 = (bf16[256,1024]{1,0:T(8,128)(2,1)S(1)}, bf16[256,1024]{1,0:T(8,128)(2,1)S(1)}, u32[]{:S(2)}, u32[]{:S(2)}) collective-permute-start(bf16[256,1024]{1,0:T(8,128)(2,1)S(1)} %fusion.26), channel_id=1, source_target_pairs={{0,4},{4,8},{8,12},{12,14},{14,10},{10,6},{6,2},{2,0},{1,5},{5,9},... | collective-permute-start | bytes 1572872 | tf_op jit(solution)/shard_map/ppermute | solution.py:57
  253.9 22.8 %collective-permute-start.42 = (bf16[256,1024]{1,0:T(8,128)(2,1)S(1)}, bf16[256,1024]{1,0:T(8,128)(2,1)S(1)}, u32[]{:S(2)}, u32[]{:S(2)}) collective-permute-start(bf16[256,1024]{1,0:T(8,128)(2,1)S(1)} %pad_maximum_fusion.5), channel_id=1, source_target_pairs={{0,2},{4,0},{8,4},{12,8},{14,12},{10,14},{6,10},{2,6},{1,3},{5,1},... | collective-permute-start | bytes 1572872 | tf_op jit(solution)/shard_map/ppermute | solution.py:57
  265.0 18.6 %collective-permute-start.39 = (bf16[256,1024]{1,0:T(8,128)(2,1)S(1)}, bf16[256,1024]{1,0:T(8,128)(2,1)S(1)}, u32[]{:S(2)}, u32[]{:S(2)}) collective-permute-start(bf16[256,1024]{1,0:T(8,128)(2,1)S(1)} %fusion.19), channel_id=1, source_target_pairs={{0,4},{4,8},{8,12},{12,14},{14,10},{10,6},{6,2},{2,0},{1,5},{5,9},... | collective-permute-start | bytes 1572872 | tf_op jit(solution)/shard_map/ppermute | solution.py:57
  276.4 14.2 %collective-permute-start.22 = (bf16[256,1024]{1,0:T(8,128)(2,1)S(1)}, bf16[256,1024]{1,0:T(8,128)(2,1)S(1)}, u32[]{:S(2)}, u32[]{:S(2)}) collective-permute-start(bf16[256,1024]{1,0:T(8,128)(2,1)S(1)} %get-tuple-element.22), channel_id=1, source_target_pairs={{0,2},{4,0},{8,4},{12,8},{14,12},{10,14},{6,10},{2,6},{1,3},{5,1},... | collective-permute-start | bytes 1572872 | tf_op jit(solution)/shard_map/ppermute | solution.py:57
  284.0 29.1 %copy-start.15 = (f32[256,1024]{1,0:T(8,128)S(1)}, f32[256,1024]{1,0:T(8,128)}, u32[]{:S(2)}) copy-start(f32[256,1024]{1,0:T(8,128)} %copy-done.14) | copy-start | bytes 3145732
  284.0 17.8 %collective-permute-start.43 = (bf16[256,1024]{1,0:T(8,128)(2,1)S(1)}, bf16[256,1024]{1,0:T(8,128)(2,1)S(1)}, u32[]{:S(2)}, u32[]{:S(2)}) collective-permute-start(bf16[256,1024]{1,0:T(8,128)(2,1)S(1)} %get-tuple-element.30), channel_id=1, source_target_pairs={{0,2},{4,0},{8,4},{12,8},{14,12},{10,14},{6,10},{2,6},{1,3},{5,1},... | collective-permute-start | bytes 1572872 | tf_op jit(solution)/shard_map/ppermute | solution.py:57
  284.6 17.6 %collective-permute-start.19 = (bf16[256,1024]{1,0:T(8,128)(2,1)S(1)}, bf16[256,1024]{1,0:T(8,128)(2,1)S(1)}, u32[]{:S(2)}, u32[]{:S(2)}) collective-permute-start(bf16[256,1024]{1,0:T(8,128)(2,1)S(1)} %get-tuple-element.21), channel_id=1, source_target_pairs={{0,4},{4,8},{8,12},{12,14},{14,10},{10,6},{6,2},{2,0},{1,5},{5,9},... | collective-permute-start | bytes 1572872 | tf_op jit(solution)/shard_map/ppermute | solution.py:57
  290.8 22.3 %collective-permute-start.23 = (bf16[256,1024]{1,0:T(8,128)(2,1)S(1)}, bf16[256,1024]{1,0:T(8,128)(2,1)S(1)}, u32[]{:S(2)}, u32[]{:S(2)}) collective-permute-start(bf16[256,1024]{1,0:T(8,128)(2,1)S(1)} %fusion.25), channel_id=1, source_target_pairs={{0,2},{4,0},{8,4},{12,8},{14,12},{10,14},{6,10},{2,6},{1,3},{5,1},... | collective-permute-start | bytes 1572872 | tf_op jit(solution)/shard_map/ppermute | solution.py:57
  290.9 28.5 %copy-start.17 = (bf16[512,1024]{1,0:T(8,128)(2,1)S(1)}, bf16[512,1024]{1,0:T(8,128)(2,1)}, u32[]{:S(2)}) copy-start(bf16[512,1024]{1,0:T(8,128)(2,1)} %param.12) | copy-start | bytes 3145732
  290.9 28.5 %copy-start.19 = (bf16[512,1024]{1,0:T(8,128)(2,1)S(1)}, bf16[512,1024]{1,0:T(8,128)(2,1)}, u32[]{:S(2)}) copy-start(bf16[512,1024]{1,0:T(8,128)(2,1)} %param.11) | copy-start | bytes 3145732
  290.9 22.5 %collective-permute-start.40 = (bf16[256,1024]{1,0:T(8,128)(2,1)S(1)}, bf16[256,1024]{1,0:T(8,128)(2,1)S(1)}, u32[]{:S(2)}, u32[]{:S(2)}) collective-permute-start(bf16[256,1024]{1,0:T(8,128)(2,1)S(1)} %get-tuple-element.29), channel_id=1, source_target_pairs={{0,4},{4,8},{8,12},{12,14},{14,10},{10,6},{6,2},{2,0},{1,5},{5,9},... | collective-permute-start | bytes 1572872 | tf_op jit(solution)/shard_map/ppermute | solution.py:57
  302.1 17.3 %collective-permute-start.44 = (bf16[256,1024]{1,0:T(8,128)(2,1)S(1)}, bf16[256,1024]{1,0:T(8,128)(2,1)S(1)}, u32[]{:S(2)}, u32[]{:S(2)}) collective-permute-start(bf16[256,1024]{1,0:T(8,128)(2,1)S(1)} %fusion.18), channel_id=1, source_target_pairs={{0,2},{4,0},{8,4},{12,8},{14,12},{10,14},{6,10},{2,6},{1,3},{5,1},... | collective-permute-start | bytes 1572872 | tf_op jit(solution)/shard_map/ppermute | solution.py:57
  (4 other events, 5.5 us)

commit v2 on v1

v2 whole, which is shorter than its diff:
```python
import functools

import jax
import jax.numpy as jnp
import numpy as np
from jax import lax
from jax.experimental import pallas as pl
from jax.experimental.pallas import tpu as pltpu
from jax.sharding import PartitionSpec as P

VMEM_LIMIT = 40 * 1024 * 1024
LANES = 128


def ring_of(count):
    if count == 8:
        return [0, 2, 4, 6, 7, 5, 3, 1]
    return list(range(count))


def send_order(count):
    half = count // 2
    order = [half]
    for step in range(half - 1, 0, -1):
        order += [step, count - step]
    return order + [0]


def pair_groups(half):
    if half == 4:
        return [[2], [1, 3], [0]]
    return [list(range(1, half)), [0]]


def tables_of(count):
    ring = ring_of(count)
    place = {block: index for index, block in enumerate(ring)}
    half = count // 2
    order = send_order(count)
    pairs = np.zeros((count, 2, 3, half), np.int32)
    tiles = np.zeros((count, 2, 3, count), np.int32)
    for block in range(count):
        own = place[block]
        for core in range(2):
            for index in range(half):
                first = ring[(own - index) % count]
                second = ring[(own + half - index) % count]
                mine = first // half == core
                kept = first if mine else second
                pairs[block, core, :, index] = mine, kept % half, kept
            wanted = [ring[(own + distance) % count] for distance in order]
            held = [next(w % half for w in wanted if (w // half == core) == (kind == 0)) for kind in range(2)]
            for index, target in enumerate(wanted):
                local = target // half == core
                held[0 if local else 1] = target % half
                tiles[block, core, :, index] = local, held[0], held[1]
    return pairs, tiles


def ring_shift(value, steps):
    ring = ring_of(lax.axis_size("blk"))
    count = len(ring)
    return lax.ppermute(value, "blk", [(ring[i], ring[(i + steps) % count]) for i in range(count)])


def swap(value):
    return lax.ppermute(value, "seq", [(0, 1), (1, 0)])


def after(value, *earlier):
    return lax.optimization_barrier((value, earlier))[0]


def gate_up_kernel(group, final, rows, width, pairs_ref, *refs):
    refs = list(refs)
    first, second, received = {}, {}, {}
    for index in group:
        first[index] = refs.pop(0)
        second[index] = [refs.pop(0)] if index else [refs.pop(0), refs.pop(0)]
        received[index] = refs.pop(0)
    gains_ref = refs.pop(0)
    gate_refs = [refs.pop(0) for _ in group]
    up_refs = [refs.pop(0) for _ in group]
    sofar_ref, sofar_stat = (refs.pop(0), refs.pop(0)) if len(refs) > (6 if final else 4) else (None, None)
    stacked, sems = refs[-2:]
    outs = refs[:-2]

    @pl.when(pl.program_id(0) == 0)
    def assemble():
        def put(source, row, count, slot, sem):
            return pltpu.make_async_copy(source, stacked.at[slot, pl.ds(row, count)], sem)

        def own_copies(slot, index, from_first):
            if from_first:
                return [put(first[index], 0, rows, slot, sems.at[1, slot])]
            parts = second[index]
            size = rows // len(parts)
            return [put(part, number * size, size, slot, sems.at[1 + number, slot]) for number, part in enumerate(parts)]

        def each(slot, index, act):
            for wanted in (True, False):
                @pl.when((pairs_ref[0, index] == 1) == wanted)
                def chosen(wanted=wanted):
                    for copy in own_copies(slot, index, wanted):
                        act(copy)

        for slot, index in enumerate(group):
            put(received[index], rows, rows, slot, sems.at[0, slot]).start()
            each(slot, index, lambda copy: copy.start())
        for slot, index in enumerate(group):
            put(received[index], rows, rows, slot, sems.at[0, slot]).wait()
            each(slot, index, lambda copy: copy.wait())

        stat = jnp.zeros((2 * rows, LANES), jnp.float32) if sofar_stat is None else sofar_stat[...]
        for slot, index in enumerate(group):
            gain = gains_ref[pairs_ref[2, index]]
            weight = 1.0 / (gain * gain)
            for column in range(0, width, LANES):
                value = stacked[slot, :, column : column + LANES].astype(jnp.float32)
                stat = stat + value * value * weight[:, column : column + LANES]
        if final:
            outs[1][...] = stat[:rows]
            outs[3][...] = stat[rows:]
        else:
            outs[1][...] = stat

    for which, weights in enumerate((gate_refs, up_refs)):
        total = None if sofar_ref is None else sofar_ref[which]
        for slot, weight_ref in enumerate(weights):
            term = jnp.dot(stacked[slot], weight_ref[...], preferred_element_type=jnp.float32)
            total = term if total is None else total + term
        if final:
            outs[0][which] = total[:rows]
            outs[2][which] = total[rows:].astype(jnp.bfloat16)
        else:
            outs[0][which] = total


def gate_up(group, final, pairs, before, second, last, received, gains, gate_weight, up_weight, sofar):
    rows, width = before[0].shape
    columns = gate_weight.shape[1]
    tile = min(512, columns)
    anywhere = pl.BlockSpec(memory_space=pl.ANY)
    operands, in_specs = [], []
    for index in group:
        pieces = [before[index], *(second[index - 1 : index] if index else last), received[index]]
        operands += pieces
        in_specs += [anywhere] * len(pieces)
    operands.append(gains)
    in_specs.append(pl.BlockSpec(gains.shape, lambda n, pairs: (0, 0, 0)))
    for weight in (gate_weight, up_weight):
        for index in group:
            operands.append(weight)
            in_specs.append(pl.BlockSpec((width, tile), lambda n, pairs, index=index: (pairs[1, index], n)))

    def tiled(*lead):
        return pl.BlockSpec((*lead, tile), lambda n, pairs: (0,) * len(lead) + (n,))

    def whole(height):
        return pl.BlockSpec((height, LANES), lambda n, pairs: (0, 0))

    if sofar is not None:
        operands += sofar
        in_specs += [tiled(2, 2 * rows), whole(2 * rows)]
    if final:
        out_shape = (
            jax.ShapeDtypeStruct((2, rows, columns), jnp.float32),
            jax.ShapeDtypeStruct((rows, LANES), jnp.float32),
            jax.ShapeDtypeStruct((2, rows, columns), jnp.bfloat16),
            jax.ShapeDtypeStruct((rows, LANES), jnp.float32),
        )
        out_specs = (tiled(2, rows), whole(rows), tiled(2, rows), whole(rows))
    else:
        out_shape = (
            jax.ShapeDtypeStruct((2, 2 * rows, columns), jnp.float32),
            jax.ShapeDtypeStruct((2 * rows, LANES), jnp.float32),
        )
        out_specs = (tiled(2, 2 * rows), whole(2 * rows))
    return pl.pallas_call(
        functools.partial(gate_up_kernel, group, final, rows, width),
        out_shape=out_shape,
        grid_spec=pltpu.PrefetchScalarGridSpec(
            num_scalar_prefetch=1,
            grid=(columns // tile,),
            in_specs=in_specs,
            out_specs=out_specs,
            scratch_shapes=[
                pltpu.VMEM((len(group), 2 * rows, width), jnp.bfloat16),
                pltpu.SemaphoreType.DMA((3, len(group))),
            ],
        ),
        compiler_params=pltpu.CompilerParams(vmem_limit_bytes=VMEM_LIMIT),
        cost_estimate=pl.CostEstimate(
            flops=12 * rows * width * columns * len(group),
            bytes_accessed=4 * width * columns * len(group),
            transcendentals=0,
        ),
        name="gate_up",
    )(pairs, *operands)


def down_kernel(start, mean_of, tiles_ref, *refs):
    if start == 0:
        own_ref, own_stat, received_ref, received_stat, local_ref, other_ref, out_ref, hidden = refs

        @pl.when(pl.program_id(0) == 0)
        def activate():
            total = jnp.sum(own_stat[...] + received_stat[...], axis=1, keepdims=True)
            inv = lax.rsqrt(total / mean_of + 1e-05)
            gate = (own_ref[0] + received_ref[0].astype(jnp.float32)) * inv
            up = (own_ref[1] + received_ref[1].astype(jnp.float32)) * inv
            hidden[...] = (gate / (1.0 + jnp.exp(-gate)) * up).astype(jnp.bfloat16)
    else:
        hidden, local_ref, other_ref, out_ref = refs

    def product(weight_ref):
        out_ref[0] = jnp.dot(hidden[...], weight_ref[...], preferred_element_type=jnp.float32).astype(jnp.bfloat16)

    local = tiles_ref[0, pl.program_id(0) + start] == 1
    pl.when(local)(functools.partial(product, local_ref))
    pl.when(jnp.logical_not(local))(functools.partial(product, other_ref))


def down(start, stop, tiles, operands, local, other, width):
    count = tiles.shape[1]
    rows, depth = operands[0].shape[-2:]

    def whole(value):
        return pl.BlockSpec(value.shape, lambda j, tiles: (0,) * value.ndim)

    def weight_spec(row):
        return pl.BlockSpec((depth, width), lambda j, tiles: (0, tiles[row, j + start]))

    out_shape = [jax.ShapeDtypeStruct((stop - start, rows, width), jnp.bfloat16)]
    out_specs = [pl.BlockSpec((1, rows, width), lambda j, tiles: (j, 0, 0))]
    if start == 0:
        out_shape.append(jax.ShapeDtypeStruct((rows, depth), jnp.bfloat16))
        out_specs.append(pl.BlockSpec((rows, depth), lambda j, tiles: (0, 0)))
    return pl.pallas_call(
        functools.partial(down_kernel, start, width * count),
        out_shape=out_shape,
        grid_spec=pltpu.PrefetchScalarGridSpec(
            num_scalar_prefetch=1,
            grid=(stop - start,),
            in_specs=[*map(whole, operands), weight_spec(1), weight_spec(2)],
            out_specs=out_specs,
        ),
        compiler_params=pltpu.CompilerParams(vmem_limit_bytes=VMEM_LIMIT),
        cost_estimate=pl.CostEstimate(
            flops=4 * rows * depth * width * (stop - start),
            bytes_accessed=2 * depth * width * (stop - start),
            transcendentals=rows * depth,
        ),
        name="down",
    )(tiles, *operands, local, other)


def gather(block, half, mine_first):
    rows = block.shape[0]
    before, behind = [block], []
    ahead = block
    for step in range(1, half):
        before.append(ring_shift(before[-1], 1))
        ahead = ring_shift(ahead, -1)
        behind.append(ahead)
    last = (ring_shift(before[-1][: rows // 2], 1), ring_shift(behind[-1][rows // 2 :], -1))
    second = behind[::-1]
    received = []
    for index in range(half):
        other = jnp.concatenate(last, axis=0) if index == 0 else second[index - 1]
        received.append(swap(jnp.where(mine_first[index], other, before[index])))
    return before, second, last, received


def scatter(term, count):
    half = count // 2
    cut = term(0).shape[0] // 2

    def joined(one, two):
        return (one.astype(jnp.float32) + two.astype(jnp.float32)).astype(jnp.bfloat16)

    forth = ring_shift(term(half)[:cut], 1)
    back = ring_shift(term(half)[cut:], -1)
    for distance in range(half - 1, 0, -1):
        ahead, behind = term(distance), term(count - distance)
        if distance == half - 1:
            forth = jnp.concatenate([joined(ahead[:cut], forth), ahead[cut:]], axis=0)
            back = jnp.concatenate([behind[:cut], joined(behind[cut:], back)], axis=0)
        else:
            forth, back = joined(ahead, forth), joined(behind, back)
        forth, back = ring_shift(forth, 1), ring_shift(back, -1)
    return term(0).astype(jnp.float32) + forth.astype(jnp.float32) + back.astype(jnp.float32)


def on_device(
    noisy_input,
    self_cond,
    cond_gain,
    bucket,
    conv_taps,
    norm_gain,
    gate_weight,
    up_weight,
    down_weight,
):
    row_count, width = noisy_input.shape
    count = lax.axis_size("blk")
    half = count // 2
    core, own = lax.axis_index("seq"), lax.axis_index("blk")
    pair_table, tile_table = tables_of(count)
    pairs = jnp.asarray(pair_table)[own, core]
    tiles = jnp.asarray(tile_table)[own, core]
    mine_first = pairs[0] == 1
    order = send_order(count)
    gains = norm_gain.reshape(count, 1, width)

    lead_rows = conv_taps.shape[1] - 1
    edges = lax.ppermute(
        (noisy_input[row_count - lead_rows :], self_cond[row_count - lead_rows :]), "seq", [(0, 1)]
    )
    other_down = swap(down_weight)
    chosen = lax.dynamic_index_in_dim(conv_taps, bucket[0], 0, keepdims=False)
    own_gain = lax.dynamic_slice_in_dim(norm_gain, own * width, width, 0)

    def mix(noisy, cond):
        return noisy.astype(jnp.float32) + cond_gain * cond.astype(jnp.float32)

    def convolve(noisy, cond, edge, start, size):
        if start == 0:
            extended = jnp.concatenate([mix(*edge), mix(noisy[:size], cond[:size])], axis=0)
        else:
            where = slice(start - lead_rows, start + size)
            extended = mix(noisy[where], cond[where])
        result = jnp.zeros((size, width), jnp.float32)
        for shift_by in range(lead_rows + 1):
            result = result + chosen[shift_by] * lax.slice_in_dim(
                extended, lead_rows - shift_by, lead_rows - shift_by + size, axis=0
            )
        return (result.astype(jnp.bfloat16).astype(jnp.float32) * own_gain).astype(jnp.bfloat16)

    size = row_count // 2
    gathered = {}
    gathered[size] = gather(convolve(noisy_input, self_cond, edges, size, size), half, mine_first)
    near = min(2, half - 1)
    lead = (gathered[size][0][near], gathered[size][1][half - 1 - near])
    later_noisy, later_cond, later_edges = after((noisy_input, self_cond, edges), *lead)
    gathered[0] = gather(convolve(later_noisy, later_cond, later_edges, 0, size), half, mine_first)

    groups = pair_groups(half)
    outs = {}
    for start in (size, 0):
        before, second, last, received = gathered[start]
        sofar = None
        used = groups if start else [sum(groups[:-1], []), groups[-1]]
        for number, group in enumerate(used):
            final = number == len(used) - 1
            sofar = gate_up(
                group, final, pairs, before, second, last, received, gains, gate_weight, up_weight, sofar
            )
        own_sum, own_stat, sent, sent_stat = sofar
        received_sum, received_stat = swap((sent, sent_stat))
        early = min(3, count - 1)
        terms, hidden = down(
            0, early, tiles, [own_sum, own_stat, received_sum, received_stat], down_weight, other_down, width
        )
        (more,) = down(early, count, tiles, [hidden], down_weight, other_down, width)

        def term(distance, terms=terms, more=more):
            index = order.index(distance)
            return terms[index] if index < early else more[index - early]

        mixed = mix(noisy_input[start : start + size], self_cond[start : start + size])
        outs[start] = (mixed + scatter(term, count)).astype(jnp.bfloat16)
    return jnp.concatenate([outs[0], outs[size]], axis=0)


def solution(mesh):
    in_specs = (
        P(("groups", "seq"), "blk"),
        P(("groups", "seq"), "blk"),
        P("blk"),
        P("groups"),
        P(None, None, "blk"),
        P(),
        P("seq", "blk"),
        P("seq", "blk"),
        P("blk", "seq"),
    )
    out_specs = P(("groups", "seq"), "blk")
    return jax.shard_map(
        on_device, mesh=mesh, in_specs=in_specs, out_specs=out_specs, check_vma=False
    )
```

time: 322 us -> 285 us (0.89)
  waiting for transfers between devices: 148 us -> 105 us
  Pallas kernels: 87 us -> 110 us
  blocking collectives: 20.6 us -> 0 us
  local copies, waits for them, and re-layouts: 11.2 us -> 15.7 us
    ppermute x32, waiting for transfers between devices: 132 us -> 102 us  [ring_shift(): lax.ppermute(value, 'blk', [(ring[i], ring[(i + steps) % count]) for i in...]
    pallas_call x4 -> x9, Pallas kernels: 87 us -> 110 us  [the longest x5 63.6 us: gate_up(): pl.pallas_call(functools.partial(gate_up_kernel, group, final, rows, widt...]
    psum x1 -> x0, blocking collectives: 20.6 us -> none  [on_device(): total = lax.psum(jnp.concatenate(squares), 'blk')]
    ppermute x2, waiting for transfers between devices: 15.9 us -> 0.01 us  [on_device(): lax.ppermute((noisy_input[row_count - lead_rows:], self_cond[row_count -...]
    unnamed x46 -> x18, local copies, waits for them, and re-layouts: 5.65 us -> 10.4 us
  transfers between devices with their start and end apart: 45 -> 47, of which waited for: 22 -> 20; matrix products, arithmetic and copies ran while one was open for 6% -> 6% of each run, Pallas kernels for 27% -> 39%
where the time goes in v2:
time: 285 us
  Pallas kernels  110 us (39%)
  waiting for transfers between devices  105 us (37%)
  starting transfers between devices  38.5 us (14%)
  local copies, waits for them, and re-layouts  15.7 us (6%)
  other arithmetic  14.4 us (5%)
    ppermute x32, waiting for transfers between devices, ring_shift(): lax.ppermute(value, 'blk', [(ring[i], ring[(i + steps) % count]) for i in...  102 us
    pallas_call x5, Pallas kernels, gate_up(): pl.pallas_call(functools.partial(gate_up_kernel, group, final, rows, widt...  63.6 us
    pallas_call x4, Pallas kernels, down(): pl.pallas_call(functools.partial(down_kernel, start, width * count), out_...  46 us
    ppermute x32, starting transfers between devices, ring_shift(): lax.ppermute(value, 'blk', [(ring[i], ring[(i + steps) % count]) for i in...  32.6 us
    unnamed x18, local copies, waits for them, and re-layouts  10.4 us
    select_n x8, other arithmetic, gather(): received.append(swap(jnp.where(mine_first[index], other, before[index])))  6.08 us
  transfers between devices with their start and end apart: 47, of which 20 were waited for; matrix products, arithmetic and copies ran while one was open for 6% of the time, Pallas kernels for 39%

profile of v2, /device:TPU:0, one launch (start us, length us, event | category | flops | bytes accessed | tf_op | source)
XLA Modules:
  0.0 284.6 jit_solution(9949275977757724376)
XLA Ops:
  1.1 0.7 dynamic_slice.16
  1.8 0.9 constant_dynamic-slice_fusion.2
  2.7 1.5 multiply_add_fusion
  5.2 2.5 collective-permute-start.4
  7.7 12.6 %collective-permute-done.4.refs_4_ = bf16[256,1024]{1,0:T(8,128)(2,1)S(1)} collective-permute-done((bf16[256,1024]{1,0:T(8,128)(2,1)S(1)}, bf16[256,1024]{1,0:T(8,128)(2,1)S(1)}, u32[]{:S(2)}, u32[]{:S(2)}) %collective-permute-start.4) | collective-permute-done | bytes 524320 | tf_op jit(solution)/shard_map/ppermute | solution.py:63
  20.3 1.7 collective-permute-start.5
  22.4 0.7 slice.225
  23.1 1.3 collective-permute-start.1
  24.4 0.7 slice.224
  25.1 1.3 collective-permute-start
  26.4 0.7 constant_dynamic-slice_fusion.4
  27.7 6.4 %collective-permute-done.5.refs_1_ = bf16[256,1024]{1,0:T(8,128)(2,1)S(1)} collective-permute-done((bf16[256,1024]{1,0:T(8,128)(2,1)S(1)}, bf16[256,1024]{1,0:T(8,128)(2,1)S(1)}, u32[]{:S(2)}, u32[]{:S(2)}) %collective-permute-start.5) | collective-permute-done | bytes 524320 | tf_op jit(solution)/shard_map/ppermute | solution.py:63
  34.1 1.2 collective-permute-done.3.refs_0_
  35.3 0.7 broadcast_select_fusion.4
  36.1 1.6 collective-permute-start.31
  38.2 1.4 multiply_add_fusion.1
  40.1 1.6 collective-permute-start.10
  41.7 9.1 %collective-permute-done.31.refs_1_ = bf16[256,1024]{1,0:T(8,128)(2,1)S(1)} collective-permute-done((bf16[256,1024]{1,0:T(8,128)(2,1)S(1)}, bf16[256,1024]{1,0:T(8,128)(2,1)S(1)}, u32[]{:S(2)}, u32[]{:S(2)}) %collective-permute-start.31) | collective-permute-done | bytes 524320 | tf_op jit(solution)/shard_map/ppermute | solution.py:63
  51.7 1.6 collective-permute-start.32
  54.5 7.6 %collective-permute-done.10.refs_7_ = bf16[256,1024]{1,0:T(8,128)(2,1)S(1)} collective-permute-done((bf16[256,1024]{1,0:T(8,128)(2,1)S(1)}, bf16[256,1024]{1,0:T(8,128)(2,1)S(1)}, u32[]{:S(2)}, u32[]{:S(2)}) %collective-permute-start.10) | collective-permute-done | bytes 524320 | tf_op jit(solution)/shard_map/ppermute | solution.py:63
  62.1 1.6 collective-permute-start.11
  63.7 2.0 collective-permute-done.6.refs_3_
  66.3 8.3 %gate_up.7 = (f32[2,512,2048]{2,1,0:T(8,128)S(1)}, f32[512,128]{1,0:T(8,128)S(1)}) custom-call(s32[3,4]{1,0:T(4,128)S(1)} %get-tuple-element.72.pairs_ref, bf16[256,1024]{1,0:T(8,128)(2,1)S(1)} %collective-permute-done.3.refs_0_, bf16[256,1024]{1,0:T(8,128)(2,1)S(1)} %collective-permute-done.5.refs_1_, ...), custom_call_target="tpu_custom_call" | custom-call | flops 6442450944 | bytes 8388608 | tf_op jit(solution)/shard_map/gate_up/pallas_call | solution.py:179
  74.6 3.3 %copy-done.2 = f32[2,512,2048]{2,1,0:T(8,128)} copy-done((f32[2,512,2048]{2,1,0:T(8,128)}, f32[2,512,2048]{2,1,0:T(8,128)S(1)}, u32[]{:S(2)}) %copy-start.2) | copy-done | bytes 8388632
  77.9 0.7 broadcast_select_fusion
  79.2 1.2 maximum_select_fusion.1
  80.8 0.7 broadcast_select_fusion.5
  81.8 1.5 collective-permute-start.12
  83.8 14.8 %gate_up.8 = (f32[2,512,2048]{2,1,0:T(8,128)S(1)}, f32[512,128]{1,0:T(8,128)S(1)}) custom-call(s32[3,4]{1,0:T(4,128)S(1)} %get-tuple-element.72.pairs_ref, bf16[256,1024]{1,0:T(8,128)(2,1)S(1)} %collective-permute-done.2.refs_0_, bf16[256,1024]{1,0:T(8,128)(2,1)S(1)} %collective-permute-done.31.refs_1_, ...), custom_call_target="tpu_custom_call" | custom-call | flops 12884901888 | bytes 16777216 | tf_op jit(solution)/shard_map/gate_up/pallas_call | solution.py:179
  98.6 3.3 %copy-done = f32[2,512,2048]{2,1,0:T(8,128)} copy-done((f32[2,512,2048]{2,1,0:T(8,128)}, f32[2,512,2048]{2,1,0:T(8,128)S(1)}, u32[]{:S(2)}) %copy-start) | copy-done | bytes 8388632
  101.9 1.6 collective-permute-start.13
  104.9 0.7 collective-permute-start.9
  105.6 4.2 %collective-permute-done.13.refs_2_ = bf16[128,1024]{1,0:T(8,128)(2,1)S(1)} collective-permute-done((bf16[128,1024]{1,0:T(8,128)(2,1)S(1)}, bf16[128,1024]{1,0:T(8,128)(2,1)S(1)}, u32[]{:S(2)}, u32[]{:S(2)}) %collective-permute-start.13) | collective-permute-done | bytes 262176 | tf_op jit(solution)/shard_map/ppermute | solution.py:63
  109.9 10.8 %gate_up.9 = (f32[2,256,2048]{2,1,0:T(8,128)S(1)}, f32[256,128]{1,0:T(8,128)S(1)}, bf16[2,256,2048]{2,1,0:T(8,128)(2,1)}, f32[256,128]{1,0:T(8,128)S(1)}) custom-call(s32[3,4]{1,0:T(4,128)S(1)} %get-tuple-element.72.pairs_ref, bf16[256,1024]{1,0:T(8,128)(2,1)S(1)} %multiply_convert_fusion.1.refs_0_, bf16[128,1024]{1,0:T(8,128)(2,1)S(1)} %collective-permute-done.30.refs_1_, ...), custom_call_target="tpu_custom_call" | custom-call | flops 6442450944 | bytes 8388608 | tf_op jit(solution)/shard_map/gate_up/pallas_call | solution.py:179
  121.3 0.8 maximum_select_fusion
  122.2 19.0 %gate_up.5 = (f32[2,512,2048]{2,1,0:T(8,128)S(1)}, f32[512,128]{1,0:T(8,128)S(1)}) custom-call(s32[3,4]{1,0:T(4,128)S(1)} %get-tuple-element.72.pairs_ref, bf16[256,1024]{1,0:T(8,128)(2,1)S(1)} %collective-permute-done.7.refs_0_, bf16[256,1024]{1,0:T(8,128)(2,1)S(1)} %collective-permute-done.11.refs_1_, ...), custom_call_target="tpu_custom_call" | custom-call | flops 19327352832 | bytes 25165824 | tf_op jit(solution)/shard_map/gate_up/pallas_call | solution.py:179
  141.2 3.3 %copy-done.1 = f32[2,512,2048]{2,1,0:T(8,128)} copy-done((f32[2,512,2048]{2,1,0:T(8,128)}, f32[2,512,2048]{2,1,0:T(8,128)S(1)}, u32[]{:S(2)}) %copy-start.1) | copy-done | bytes 8388632
  144.6 10.8 %gate_up.6 = (f32[2,256,2048]{2,1,0:T(8,128)S(1)}, f32[256,128]{1,0:T(8,128)S(1)}, bf16[2,256,2048]{2,1,0:T(8,128)(2,1)}, f32[256,128]{1,0:T(8,128)S(1)}) custom-call(s32[3,4]{1,0:T(4,128)S(1)} %get-tuple-element.72.pairs_ref, bf16[256,1024]{1,0:T(8,128)(2,1)S(1)} %multiply_convert_fusion.refs_0_, bf16[128,1024]{1,0:T(8,128)(2,1)S(1)} %collective-permute-done.9.refs_1_, ...), custom_call_target="tpu_custom_call" | custom-call | flops 6442450944 | bytes 8388608 | tf_op jit(solution)/shard_map/gate_up/pallas_call | solution.py:179
  157.1 2.7 collective-permute-done.38.refs_3_
  159.8 10.7 %down.6 = (bf16[3,256,1024]{2,1,0:T(8,128)(2,1)S(1)}, bf16[256,2048]{1,0:T(8,128)(2,1)S(1)}) custom-call(s32[3,8]{1,0:T(4,128)S(1)} %dynamic-slice_bitcast_fusion.tiles_ref, f32[2,256,2048]{2,1,0:T(8,128)S(1)} %get-tuple-element.43.refs_0_, f32[256,128]{1,0:T(8,128)S(1)} %get-tuple-element.44.refs_1_, ...), custom_call_target="tpu_custom_call" | custom-call | flops 6442450944 | bytes 12582912 | tf_op jit(solution)/shard_map/down/pallas_call | solution.py:239
  171.1 1.5 collective-permute-start.43
  172.7 10.7 %down.4 = (bf16[3,256,1024]{2,1,0:T(8,128)(2,1)S(1)}, bf16[256,2048]{1,0:T(8,128)(2,1)S(1)}) custom-call(s32[3,8]{1,0:T(4,128)S(1)} %dynamic-slice_bitcast_fusion.tiles_ref, f32[2,256,2048]{2,1,0:T(8,128)S(1)} %get-tuple-element.33.refs_0_, f32[256,128]{1,0:T(8,128)S(1)} %get-tuple-element.34.refs_1_, ...), custom_call_target="tpu_custom_call" | custom-call | flops 6442450944 | bytes 12582912 | tf_op jit(solution)/shard_map/down/pallas_call | solution.py:239
  183.5 2.0 collective-permute-start.25
  185.5 12.3 %down.7 = bf16[5,256,1024]{2,1,0:T(8,128)(2,1)S(1)} custom-call(s32[3,8]{1,0:T(4,128)S(1)} %dynamic-slice_bitcast_fusion.tiles_ref, bf16[256,2048]{1,0:T(8,128)(2,1)S(1)} %get-tuple-element.47.refs_0_, bf16[2048,4096]{1,0:T(8,128)(2,1)} %refs_1_.3, bf16[2048,4096]{1,0:T(8,128)(2,1)} %collective-permute-done.20.refs_5_.refs_2_), custom_call_target="tpu_custom_call" | custom-call | flops 10737418240 | bytes 20971520 | tf_op jit(solution)/shard_map/down/pallas_call | solution.py:239
  198.1 0.9 collective-permute-start.40
  199.3 2.1 collective-permute-start.22
  201.4 12.3 %down.5 = bf16[5,256,1024]{2,1,0:T(8,128)(2,1)S(1)} custom-call(s32[3,8]{1,0:T(4,128)S(1)} %dynamic-slice_bitcast_fusion.tiles_ref, bf16[256,2048]{1,0:T(8,128)(2,1)S(1)} %get-tuple-element.37.refs_0_, bf16[2048,4096]{1,0:T(8,128)(2,1)} %refs_1_.3, bf16[2048,4096]{1,0:T(8,128)(2,1)} %collective-permute-done.20.refs_5_.refs_2_), custom_call_target="tpu_custom_call" | custom-call | flops 10737418240 | bytes 20971520 | tf_op jit(solution)/shard_map/down/pallas_call | solution.py:239
  214.1 2.1 collective-permute-start.41
  216.2 8.0 %collective-permute-done.22 = bf16[256,1024]{1,0:T(8,128)(2,1)S(1)} collective-permute-done((bf16[256,1024]{1,0:T(8,128)(2,1)S(1)}, bf16[256,1024]{1,0:T(8,128)(2,1)S(1)}, u32[]{:S(2)}, u32[]{:S(2)}) %collective-permute-start.22) | collective-permute-done | bytes 524320 | tf_op jit(solution)/shard_map/ppermute | solution.py:63
  224.5 1.0 collective-permute-start.23
  225.4 3.3 %collective-permute-done.44 = bf16[256,1024]{1,0:T(8,128)(2,1)S(1)} collective-permute-done((bf16[256,1024]{1,0:T(8,128)(2,1)S(1)}, bf16[256,1024]{1,0:T(8,128)(2,1)S(1)}, u32[]{:S(2)}, u32[]{:S(2)}) %collective-permute-start.44) | collective-permute-done | bytes 524320 | tf_op jit(solution)/shard_map/ppermute | solution.py:63
  228.7 6.8 %collective-permute-done.41 = bf16[256,1024]{1,0:T(8,128)(2,1)S(1)} collective-permute-done((bf16[256,1024]{1,0:T(8,128)(2,1)S(1)}, bf16[256,1024]{1,0:T(8,128)(2,1)S(1)}, u32[]{:S(2)}, u32[]{:S(2)}) %collective-permute-start.41) | collective-permute-done | bytes 524320 | tf_op jit(solution)/shard_map/ppermute | solution.py:63
  235.9 1.6 collective-permute-start.45
  237.6 2.2 collective-permute-done.26
  239.8 5.1 %collective-permute-done.23 = bf16[256,1024]{1,0:T(8,128)(2,1)S(1)} collective-permute-done((bf16[256,1024]{1,0:T(8,128)(2,1)S(1)}, bf16[256,1024]{1,0:T(8,128)(2,1)S(1)}, u32[]{:S(2)}, u32[]{:S(2)}) %collective-permute-start.23) | collective-permute-done | bytes 524320 | tf_op jit(solution)/shard_map/ppermute | solution.py:63
  245.3 1.6 collective-permute-start.27
  247.4 1.1 collective-permute-start.24
  248.4 2.6 collective-permute-done.45
  251.3 11.0 %collective-permute-done.27 = bf16[256,1024]{1,0:T(8,128)(2,1)S(1)} collective-permute-done((bf16[256,1024]{1,0:T(8,128)(2,1)S(1)}, bf16[256,1024]{1,0:T(8,128)(2,1)S(1)}, u32[]{:S(2)}, u32[]{:S(2)}) %collective-permute-start.27) | collective-permute-done | bytes 524320 | tf_op jit(solution)/shard_map/ppermute | solution.py:63
  262.5 7.4 %collective-permute-done.24 = bf16[256,1024]{1,0:T(8,128)(2,1)S(1)} collective-permute-done((bf16[256,1024]{1,0:T(8,128)(2,1)S(1)}, bf16[256,1024]{1,0:T(8,128)(2,1)S(1)}, u32[]{:S(2)}, u32[]{:S(2)}) %collective-permute-start.24) | collective-permute-done | bytes 524320 | tf_op jit(solution)/shard_map/ppermute | solution.py:63
  269.9 3.6 %collective-permute-done.46 = bf16[256,1024]{1,0:T(8,128)(2,1)S(1)} collective-permute-done((bf16[256,1024]{1,0:T(8,128)(2,1)S(1)}, bf16[256,1024]{1,0:T(8,128)(2,1)S(1)}, u32[]{:S(2)}, u32[]{:S(2)}) %collective-permute-start.46) | collective-permute-done | bytes 524320 | tf_op jit(solution)/shard_map/ppermute | solution.py:63
  273.5 8.8 %collective-permute-done.28 = bf16[256,1024]{1,0:T(8,128)(2,1)S(1)} collective-permute-done((bf16[256,1024]{1,0:T(8,128)(2,1)S(1)}, bf16[256,1024]{1,0:T(8,128)(2,1)S(1)}, u32[]{:S(2)}, u32[]{:S(2)}) %collective-permute-start.28) | collective-permute-done | bytes 524320 | tf_op jit(solution)/shard_map/ppermute | solution.py:63
  282.3 1.2 fusion.26
  283.5 1.0 pad_maximum_fusion.1
  (98 shorter events, 15.2 us)
Async XLA Ops:
  0.0 159.8 %collective-permute-start.20 = (bf16[2048,4096]{1,0:T(8,128)(2,1)}, bf16[2048,4096]{1,0:T(8,128)(2,1)}, u32[]{:S(2)}, u32[]{:S(2)}) collective-permute-start(bf16[2048,4096]{1,0:T(8,128)(2,1)} %refs_1_.3), channel_id=1, source_target_pairs={{0,1},{1,0},{2,3},{3,2},{4,5},{5,4},{6,7},{7,6},{8,9},{9,8},{10,11... | collective-permute-start | bytes 50331656 | tf_op jit(solution)/shard_map/ppermute | solution.py:67
  4.2 1.0 copy-start.4
  4.2 34.0 %copy-start.8 = (f32[1024]{0:T(1024)S(1)}, f32[1024]{0:T(1024)}, u32[]{:S(2)}) copy-start(f32[1024]{0:T(1024)} %param.13) | copy-start | bytes 12292
  5.2 15.2 %collective-permute-start.4 = (bf16[256,1024]{1,0:T(8,128)(2,1)S(1)}, bf16[256,1024]{1,0:T(8,128)(2,1)S(1)}, u32[]{:S(2)}, u32[]{:S(2)}) collective-permute-start(bf16[256,1024]{1,0:T(8,128)(2,1)S(1)} %multiply_convert_fusion.1.refs_0_), channel_id=1, source_target_pairs={{0,2},{4,0},{8,4},{12,8},{14,12},{10,14},{6,10},{2,6},{1,3},{5,1},... | collective-permute-start | bytes 1572872 | tf_op jit(solution)/shard_map/ppermute | solution.py:63
  7.7 14.3 %collective-permute-start.2 = (bf16[256,1024]{1,0:T(8,128)(2,1)S(1)}, bf16[256,1024]{1,0:T(8,128)(2,1)S(1)}, u32[]{:S(2)}, u32[]{:S(2)}) collective-permute-start(bf16[256,1024]{1,0:T(8,128)(2,1)S(1)} %multiply_convert_fusion.1.refs_0_), channel_id=1, source_target_pairs={{0,4},{4,8},{8,12},{12,14},{14,10},{10,6},{6,2},{2,0},{1,5},{5,9},... | collective-permute-start | bytes 1572872 | tf_op jit(solution)/shard_map/ppermute | solution.py:63
  20.3 13.8 %collective-permute-start.5 = (bf16[256,1024]{1,0:T(8,128)(2,1)S(1)}, bf16[256,1024]{1,0:T(8,128)(2,1)S(1)}, u32[]{:S(2)}, u32[]{:S(2)}) collective-permute-start(bf16[256,1024]{1,0:T(8,128)(2,1)S(1)} %collective-permute-done.4.refs_4_), channel_id=1, source_target_pairs={{0,2},{4,0},{8,4},{12,8},{14,12},{10,14},{6,10},{2,6},{1,3},{5,1},... | collective-permute-start | bytes 1572872 | tf_op jit(solution)/shard_map/ppermute | solution.py:63
  22.0 13.3 %collective-permute-start.3 = (bf16[256,1024]{1,0:T(8,128)(2,1)S(1)}, bf16[256,1024]{1,0:T(8,128)(2,1)S(1)}, u32[]{:S(2)}, u32[]{:S(2)}) collective-permute-start(bf16[256,1024]{1,0:T(8,128)(2,1)S(1)} %collective-permute-done.2.refs_0_), channel_id=1, source_target_pairs={{0,4},{4,8},{8,12},{12,14},{14,10},{10,6},{6,2},{2,0},{1,5},{5,9},... | collective-permute-start | bytes 1572872 | tf_op jit(solution)/shard_map/ppermute | solution.py:63
  23.1 4.6 %collective-permute-start.1 = (bf16[3,1024]{1,0:T(4,128)(2,1)S(1)}, bf16[3,1024]{1,0:T(4,128)(2,1)S(1)}, u32[]{:S(2)}, u32[]{:S(2)}) collective-permute-start(bf16[3,1024]{1,0:T(4,128)(2,1)S(1)} %slice.225), channel_id=1, source_target_pairs={{0,1},{2,3},{4,5},{6,7},{8,9},{10,11},{12,13},{14,15},{16,17},{18,... | collective-permute-start | bytes 18440 | tf_op jit(solution)/shard_map/ppermute | solution.py:318
  25.1 2.6 collective-permute-start
  36.0 18.0 %collective-permute-start.36 = (bf16[256,1024]{1,0:T(8,128)(2,1)S(1)}, bf16[256,1024]{1,0:T(8,128)(2,1)S(1)}, u32[]{:S(2)}, u32[]{:S(2)}) collective-permute-start(bf16[256,1024]{1,0:T(8,128)(2,1)S(1)} %broadcast_select_fusion.4), channel_id=1, source_target_pairs={{0,1},{1,0},{2,3},{3,2},{4,5},{5,4},{6,7},{7,6},{8,9},{9,8},{10,11... | collective-permute-start | bytes 1572872 | tf_op jit(solution)/shard_map/ppermute | solution.py:67
  36.1 14.8 %collective-permute-start.31 = (bf16[256,1024]{1,0:T(8,128)(2,1)S(1)}, bf16[256,1024]{1,0:T(8,128)(2,1)S(1)}, u32[]{:S(2)}, u32[]{:S(2)}) collective-permute-start(bf16[256,1024]{1,0:T(8,128)(2,1)S(1)} %collective-permute-done.5.refs_1_), channel_id=1, source_target_pairs={{0,2},{4,0},{8,4},{12,8},{14,12},{10,14},{6,10},{2,6},{1,3},{5,1},... | collective-permute-start | bytes 1572872 | tf_op jit(solution)/shard_map/ppermute | solution.py:63
  37.7 14.0 %collective-permute-start.29 = (bf16[256,1024]{1,0:T(8,128)(2,1)S(1)}, bf16[256,1024]{1,0:T(8,128)(2,1)S(1)}, u32[]{:S(2)}, u32[]{:S(2)}) collective-permute-start(bf16[256,1024]{1,0:T(8,128)(2,1)S(1)} %collective-permute-done.3.refs_0_), channel_id=1, source_target_pairs={{0,4},{4,8},{8,12},{12,14},{14,10},{10,6},{6,2},{2,0},{1,5},{5,9},... | collective-permute-start | bytes 1572872 | tf_op jit(solution)/shard_map/ppermute | solution.py:63
  39.6 26.7 %copy-start.3 = (f32[8192]{0:T(1024)S(1)}, f32[8192]{0:T(1024)}, u32[]{:S(2)}) copy-start(f32[8192]{0:T(1024)} %param.16) | copy-start | bytes 98308
  40.1 22.0 %collective-permute-start.10 = (bf16[256,1024]{1,0:T(8,128)(2,1)S(1)}, bf16[256,1024]{1,0:T(8,128)(2,1)S(1)}, u32[]{:S(2)}, u32[]{:S(2)}) collective-permute-start(bf16[256,1024]{1,0:T(8,128)(2,1)S(1)} %multiply_convert_fusion.refs_0_), channel_id=1, source_target_pairs={{0,2},{4,0},{8,4},{12,8},{14,12},{10,14},{6,10},{2,6},{1,3},{5,1},... | collective-permute-start | bytes 1572872 | tf_op jit(solution)/shard_map/ppermute | solution.py:63
  50.9 14.9 %collective-permute-start.6 = (bf16[256,1024]{1,0:T(8,128)(2,1)S(1)}, bf16[256,1024]{1,0:T(8,128)(2,1)S(1)}, u32[]{:S(2)}, u32[]{:S(2)}) collective-permute-start(bf16[256,1024]{1,0:T(8,128)(2,1)S(1)} %multiply_convert_fusion.refs_0_), channel_id=1, source_target_pairs={{0,4},{4,8},{8,12},{12,14},{14,10},{10,6},{6,2},{2,0},{1,5},{5,9},... | collective-permute-start | bytes 1572872 | tf_op jit(solution)/shard_map/ppermute | solution.py:63
  51.7 26.9 %collective-permute-start.32 = (bf16[128,1024]{1,0:T(8,128)(2,1)S(1)}, bf16[128,1024]{1,0:T(8,128)(2,1)S(1)}, u32[]{:S(2)}, u32[]{:S(2)}) collective-permute-start(bf16[128,1024]{1,0:T(8,128)(2,1)S(1)} %slice.297), channel_id=1, source_target_pairs={{0,2},{4,0},{8,4},{12,8},{14,12},{10,14},{6,10},{2,6},{1,3},{5,1},... | collective-permute-start | bytes 786440 | tf_op jit(solution)/shard_map/ppermute | solution.py:63
  54.0 24.7 %collective-permute-start.30 = (bf16[128,1024]{1,0:T(8,128)(2,1)S(1)}, bf16[128,1024]{1,0:T(8,128)(2,1)S(1)}, u32[]{:S(2)}, u32[]{:S(2)}) collective-permute-start(bf16[128,1024]{1,0:T(8,128)(2,1)S(1)} %slice.296), channel_id=1, source_target_pairs={{0,4},{4,8},{8,12},{12,14},{14,10},{10,6},{6,2},{2,0},{1,5},{5,9},... | collective-permute-start | bytes 786440 | tf_op jit(solution)/shard_map/ppermute | solution.py:63
  62.1 18.3 %collective-permute-start.11 = (bf16[256,1024]{1,0:T(8,128)(2,1)S(1)}, bf16[256,1024]{1,0:T(8,128)(2,1)S(1)}, u32[]{:S(2)}, u32[]{:S(2)}) collective-permute-start(bf16[256,1024]{1,0:T(8,128)(2,1)S(1)} %collective-permute-done.10.refs_7_), channel_id=1, source_target_pairs={{0,2},{4,0},{8,4},{12,8},{14,12},{10,14},{6,10},{2,6},{1,3},{5,1},... | collective-permute-start | bytes 1572872 | tf_op jit(solution)/shard_map/ppermute | solution.py:63
  65.7 15.0 %collective-permute-start.7 = (bf16[256,1024]{1,0:T(8,128)(2,1)S(1)}, bf16[256,1024]{1,0:T(8,128)(2,1)S(1)}, u32[]{:S(2)}, u32[]{:S(2)}) collective-permute-start(bf16[256,1024]{1,0:T(8,128)(2,1)S(1)} %collective-permute-done.6.refs_3_), channel_id=1, source_target_pairs={{0,4},{4,8},{8,12},{12,14},{14,10},{10,6},{6,2},{2,0},{1,5},{5,9},... | collective-permute-start | bytes 1572872 | tf_op jit(solution)/shard_map/ppermute | solution.py:63
  74.6 3.3 %copy-start.2 = (f32[2,512,2048]{2,1,0:T(8,128)}, f32[2,512,2048]{2,1,0:T(8,128)S(1)}, u32[]{:S(2)}) copy-start(f32[2,512,2048]{2,1,0:T(8,128)S(1)} %get-tuple-element.39.refs_11_) | copy-start | bytes 25165828
  77.9 1.3 copy-start.5
  78.6 3.1 %collective-permute-start.34 = (bf16[256,1024]{1,0:T(8,128)(2,1)S(1)}, bf16[256,1024]{1,0:T(8,128)(2,1)S(1)}, u32[]{:S(2)}, u32[]{:S(2)}) collective-permute-start(bf16[256,1024]{1,0:T(8,128)(2,1)S(1)} %broadcast_select_fusion.2), channel_id=1, source_target_pairs={{0,1},{1,0},{2,3},{3,2},{4,5},{5,4},{6,7},{7,6},{8,9},{9,8},{10,11... | collective-permute-start | bytes 1572872 | tf_op jit(solution)/shard_map/ppermute | solution.py:67
  78.7 4.6 %collective-permute-start.35 = (bf16[256,1024]{1,0:T(8,128)(2,1)S(1)}, bf16[256,1024]{1,0:T(8,128)(2,1)S(1)}, u32[]{:S(2)}, u32[]{:S(2)}) collective-permute-start(bf16[256,1024]{1,0:T(8,128)(2,1)S(1)} %broadcast_select_fusion), channel_id=1, source_target_pairs={{0,1},{1,0},{2,3},{3,2},{4,5},{5,4},{6,7},{7,6},{8,9},{9,8},{10,11... | collective-permute-start | bytes 1572872 | tf_op jit(solution)/shard_map/ppermute | solution.py:67
  80.4 24.5 %collective-permute-start.33 = (bf16[256,1024]{1,0:T(8,128)(2,1)S(1)}, bf16[256,1024]{1,0:T(8,128)(2,1)S(1)}, u32[]{:S(2)}, u32[]{:S(2)}) collective-permute-start(bf16[256,1024]{1,0:T(8,128)(2,1)S(1)} %maximum_select_fusion.1), channel_id=1, source_target_pairs={{0,1},{1,0},{2,3},{3,2},{4,5},{5,4},{6,7},{7,6},{8,9},{9,8},{10,11... | collective-permute-start | bytes 1572872 | tf_op jit(solution)/shard_map/ppermute | solution.py:67
  81.5 40.6 %collective-permute-start.15 = (bf16[256,1024]{1,0:T(8,128)(2,1)S(1)}, bf16[256,1024]{1,0:T(8,128)(2,1)S(1)}, u32[]{:S(2)}, u32[]{:S(2)}) collective-permute-start(bf16[256,1024]{1,0:T(8,128)(2,1)S(1)} %broadcast_select_fusion.5), channel_id=1, source_target_pairs={{0,1},{1,0},{2,3},{3,2},{4,5},{5,4},{6,7},{7,6},{8,9},{9,8},{10,11... | collective-permute-start | bytes 1572872 | tf_op jit(solution)/shard_map/ppermute | solution.py:67
  81.8 20.1 %collective-permute-start.12 = (bf16[256,1024]{1,0:T(8,128)(2,1)S(1)}, bf16[256,1024]{1,0:T(8,128)(2,1)S(1)}, u32[]{:S(2)}, u32[]{:S(2)}) collective-permute-start(bf16[256,1024]{1,0:T(8,128)(2,1)S(1)} %collective-permute-done.11.refs_1_), channel_id=1, source_target_pairs={{0,2},{4,0},{8,4},{12,8},{14,12},{10,14},{6,10},{2,6},{1,3},{5,1},... | collective-permute-start | bytes 1572872 | tf_op jit(solution)/shard_map/ppermute | solution.py:63
  83.3 20.9 %collective-permute-start.8 = (bf16[256,1024]{1,0:T(8,128)(2,1)S(1)}, bf16[256,1024]{1,0:T(8,128)(2,1)S(1)}, u32[]{:S(2)}, u32[]{:S(2)}) collective-permute-start(bf16[256,1024]{1,0:T(8,128)(2,1)S(1)} %collective-permute-done.7.refs_0_), channel_id=1, source_target_pairs={{0,4},{4,8},{8,12},{12,14},{14,10},{10,6},{6,2},{2,0},{1,5},{5,9},... | collective-permute-start | bytes 1572872 | tf_op jit(solution)/shard_map/ppermute | solution.py:63
  98.6 3.3 %copy-start = (f32[2,512,2048]{2,1,0:T(8,128)}, f32[2,512,2048]{2,1,0:T(8,128)S(1)}, u32[]{:S(2)}) copy-start(f32[2,512,2048]{2,1,0:T(8,128)S(1)} %get-tuple-element.41.refs_7_) | copy-start | bytes 25165828
  101.9 8.0 %collective-permute-start.13 = (bf16[128,1024]{1,0:T(8,128)(2,1)S(1)}, bf16[128,1024]{1,0:T(8,128)(2,1)S(1)}, u32[]{:S(2)}, u32[]{:S(2)}) collective-permute-start(bf16[128,1024]{1,0:T(8,128)(2,1)S(1)} %slice.290), channel_id=1, source_target_pairs={{0,2},{4,0},{8,4},{12,8},{14,12},{10,14},{6,10},{2,6},{1,3},{5,1},... | collective-permute-start | bytes 786440 | tf_op jit(solution)/shard_map/ppermute | solution.py:63
  104.2 18.0 %collective-permute-start.16 = (bf16[256,1024]{1,0:T(8,128)(2,1)S(1)}, bf16[256,1024]{1,0:T(8,128)(2,1)S(1)}, u32[]{:S(2)}, u32[]{:S(2)}) collective-permute-start(bf16[256,1024]{1,0:T(8,128)(2,1)S(1)} %broadcast_select_fusion.3), channel_id=1, source_target_pairs={{0,1},{1,0},{2,3},{3,2},{4,5},{5,4},{6,7},{7,6},{8,9},{9,8},{10,11... | collective-permute-start | bytes 1572872 | tf_op jit(solution)/shard_map/ppermute | solution.py:67
  104.9 15.8 %collective-permute-start.9 = (bf16[128,1024]{1,0:T(8,128)(2,1)S(1)}, bf16[128,1024]{1,0:T(8,128)(2,1)S(1)}, u32[]{:S(2)}, u32[]{:S(2)}) collective-permute-start(bf16[128,1024]{1,0:T(8,128)(2,1)S(1)} %slice.289), channel_id=1, source_target_pairs={{0,4},{4,8},{8,12},{12,14},{14,10},{10,6},{6,2},{2,0},{1,5},{5,9},... | collective-permute-start | bytes 786440 | tf_op jit(solution)/shard_map/ppermute | solution.py:63
  109.9 12.3 %collective-permute-start.17 = (bf16[256,1024]{1,0:T(8,128)(2,1)S(1)}, bf16[256,1024]{1,0:T(8,128)(2,1)S(1)}, u32[]{:S(2)}, u32[]{:S(2)}) collective-permute-start(bf16[256,1024]{1,0:T(8,128)(2,1)S(1)} %broadcast_select_fusion.1), channel_id=1, source_target_pairs={{0,1},{1,0},{2,3},{3,2},{4,5},{5,4},{6,7},{7,6},{8,9},{9,8},{10,11... | collective-permute-start | bytes 1572872 | tf_op jit(solution)/shard_map/ppermute | solution.py:67
  120.7 39.1 %collective-permute-start.37 = (bf16[2,256,2048]{2,1,0:T(8,128)(2,1)}, bf16[2,256,2048]{2,1,0:T(8,128)(2,1)S(1)}, u32[]{:S(2)}, u32[]{:S(2)}) collective-permute-start(bf16[2,256,2048]{2,1,0:T(8,128)(2,1)} %get-tuple-element.45), channel_id=1, source_target_pairs={{0,1},{1,0},{2,3},{3,2},{4,5},{5,4},{6,7},{7,6},{8,9},{9,8},{10,11... | collective-permute-start | bytes 6291464 | tf_op jit(solution)/shard_map/ppermute | solution.py:67
  122.1 22.5 %collective-permute-start.14 = (bf16[256,1024]{1,0:T(8,128)(2,1)S(1)}, bf16[256,1024]{1,0:T(8,128)(2,1)S(1)}, u32[]{:S(2)}, u32[]{:S(2)}) collective-permute-start(bf16[256,1024]{1,0:T(8,128)(2,1)S(1)} %maximum_select_fusion), channel_id=1, source_target_pairs={{0,1},{1,0},{2,3},{3,2},{4,5},{5,4},{6,7},{7,6},{8,9},{9,8},{10,11... | collective-permute-start | bytes 1572872 | tf_op jit(solution)/shard_map/ppermute | solution.py:67
  141.2 3.3 %copy-start.1 = (f32[2,512,2048]{2,1,0:T(8,128)}, f32[2,512,2048]{2,1,0:T(8,128)S(1)}, u32[]{:S(2)}) copy-start(f32[2,512,2048]{2,1,0:T(8,128)S(1)} %get-tuple-element.31.refs_7_) | copy-start | bytes 25165828
  155.4 17.3 %collective-permute-start.18 = (bf16[2,256,2048]{2,1,0:T(8,128)(2,1)}, bf16[2,256,2048]{2,1,0:T(8,128)(2,1)S(1)}, u32[]{:S(2)}, u32[]{:S(2)}) collective-permute-start(bf16[2,256,2048]{2,1,0:T(8,128)(2,1)} %get-tuple-element.35), channel_id=1, source_target_pairs={{0,1},{1,0},{2,3},{3,2},{4,5},{5,4},{6,7},{7,6},{8,9},{9,8},{10,11... | collective-permute-start | bytes 6291464 | tf_op jit(solution)/shard_map/ppermute | solution.py:67
  155.9 3.9 %collective-permute-start.38 = (f32[256,128]{1,0:T(8,128)S(1)}, f32[256,128]{1,0:T(8,128)S(1)}, u32[]{:S(2)}, u32[]{:S(2)}) collective-permute-start(f32[256,128]{1,0:T(8,128)S(1)} %get-tuple-element.46), channel_id=1, source_target_pairs={{0,1},{1,0},{2,3},{3,2},{4,5},{5,4},{6,7},{7,6},{8,9},{9,8},{10,11... | collective-permute-start | bytes 393224 | tf_op jit(solution)/shard_map/ppermute | solution.py:67
  156.7 16.0 %collective-permute-start.19 = (f32[256,128]{1,0:T(8,128)S(1)}, f32[256,128]{1,0:T(8,128)S(1)}, u32[]{:S(2)}, u32[]{:S(2)}) collective-permute-start(f32[256,128]{1,0:T(8,128)S(1)} %get-tuple-element.36), channel_id=1, source_target_pairs={{0,1},{1,0},{2,3},{3,2},{4,5},{5,4},{6,7},{7,6},{8,9},{9,8},{10,11... | collective-permute-start | bytes 393224 | tf_op jit(solution)/shard_map/ppermute | solution.py:67
  170.6 27.3 %collective-permute-start.39 = (bf16[128,1024]{1,0:T(8,128)(2,1)S(1)}, bf16[128,1024]{1,0:T(8,128)(2,1)S(1)}, u32[]{:S(2)}, u32[]{:S(2)}) collective-permute-start(bf16[128,1024]{1,0:T(8,128)(2,1)S(1)} %get-tuple-element.63), channel_id=1, source_target_pairs={{0,4},{4,8},{8,12},{12,14},{14,10},{10,6},{6,2},{2,0},{1,5},{5,9},... | collective-permute-start | bytes 786440 | tf_op jit(solution)/shard_map/ppermute | solution.py:63
  171.1 26.8 %collective-permute-start.43 = (bf16[128,1024]{1,0:T(8,128)(2,1)S(1)}, bf16[128,1024]{1,0:T(8,128)(2,1)S(1)}, u32[]{:S(2)}, u32[]{:S(2)}) collective-permute-start(bf16[128,1024]{1,0:T(8,128)(2,1)S(1)} %get-tuple-element.64), channel_id=1, source_target_pairs={{0,2},{4,0},{8,4},{12,8},{14,12},{10,14},{6,10},{2,6},{1,3},{5,1},... | collective-permute-start | bytes 786440 | tf_op jit(solution)/shard_map/ppermute | solution.py:63
  183.4 15.6 %collective-permute-start.21 = (bf16[128,1024]{1,0:T(8,128)(2,1)S(1)}, bf16[128,1024]{1,0:T(8,128)(2,1)S(1)}, u32[]{:S(2)}, u32[]{:S(2)}) collective-permute-start(bf16[128,1024]{1,0:T(8,128)(2,1)S(1)} %get-tuple-element.57), channel_id=1, source_target_pairs={{0,4},{4,8},{8,12},{12,14},{14,10},{10,6},{6,2},{2,0},{1,5},{5,9},... | collective-permute-start | bytes 786440 | tf_op jit(solution)/shard_map/ppermute | solution.py:63
  183.5 15.6 %collective-permute-start.25 = (bf16[128,1024]{1,0:T(8,128)(2,1)S(1)}, bf16[128,1024]{1,0:T(8,128)(2,1)S(1)}, u32[]{:S(2)}, u32[]{:S(2)}) collective-permute-start(bf16[128,1024]{1,0:T(8,128)(2,1)S(1)} %get-tuple-element.58), channel_id=1, source_target_pairs={{0,2},{4,0},{8,4},{12,8},{14,12},{10,14},{6,10},{2,6},{1,3},{5,1},... | collective-permute-start | bytes 786440 | tf_op jit(solution)/shard_map/ppermute | solution.py:63
  198.1 15.7 %collective-permute-start.40 = (bf16[256,1024]{1,0:T(8,128)(2,1)S(1)}, bf16[256,1024]{1,0:T(8,128)(2,1)S(1)}, u32[]{:S(2)}, u32[]{:S(2)}) collective-permute-start(bf16[256,1024]{1,0:T(8,128)(2,1)S(1)} %pad_maximum_fusion.4), channel_id=1, source_target_pairs={{0,4},{4,8},{8,12},{12,14},{14,10},{10,6},{6,2},{2,0},{1,5},{5,9},... | collective-permute-start | bytes 1572872 | tf_op jit(solution)/shard_map/ppermute | solution.py:63
  199.3 24.9 %collective-permute-start.22 = (bf16[256,1024]{1,0:T(8,128)(2,1)S(1)}, bf16[256,1024]{1,0:T(8,128)(2,1)S(1)}, u32[]{:S(2)}, u32[]{:S(2)}) collective-permute-start(bf16[256,1024]{1,0:T(8,128)(2,1)S(1)} %pad_maximum_fusion.2), channel_id=1, source_target_pairs={{0,4},{4,8},{8,12},{12,14},{14,10},{10,6},{6,2},{2,0},{1,5},{5,9},... | collective-permute-start | bytes 1572872 | tf_op jit(solution)/shard_map/ppermute | solution.py:63
  213.8 14.9 %collective-permute-start.44 = (bf16[256,1024]{1,0:T(8,128)(2,1)S(1)}, bf16[256,1024]{1,0:T(8,128)(2,1)S(1)}, u32[]{:S(2)}, u32[]{:S(2)}) collective-permute-start(bf16[256,1024]{1,0:T(8,128)(2,1)S(1)} %pad_maximum_fusion.5), channel_id=1, source_target_pairs={{0,2},{4,0},{8,4},{12,8},{14,12},{10,14},{6,10},{2,6},{1,3},{5,1},... | collective-permute-start | bytes 1572872 | tf_op jit(solution)/shard_map/ppermute | solution.py:63
  214.1 21.4 %collective-permute-start.41 = (bf16[256,1024]{1,0:T(8,128)(2,1)S(1)}, bf16[256,1024]{1,0:T(8,128)(2,1)S(1)}, u32[]{:S(2)}, u32[]{:S(2)}) collective-permute-start(bf16[256,1024]{1,0:T(8,128)(2,1)S(1)} %fusion.15), channel_id=1, source_target_pairs={{0,4},{4,8},{8,12},{12,14},{14,10},{10,6},{6,2},{2,0},{1,5},{5,9},... | collective-permute-start | bytes 1572872 | tf_op jit(solution)/shard_map/ppermute | solution.py:63
  216.2 23.6 %collective-permute-start.26 = (bf16[256,1024]{1,0:T(8,128)(2,1)S(1)}, bf16[256,1024]{1,0:T(8,128)(2,1)S(1)}, u32[]{:S(2)}, u32[]{:S(2)}) collective-permute-start(bf16[256,1024]{1,0:T(8,128)(2,1)S(1)} %pad_maximum_fusion.3), channel_id=1, source_target_pairs={{0,2},{4,0},{8,4},{12,8},{14,12},{10,14},{6,10},{2,6},{1,3},{5,1},... | collective-permute-start | bytes 1572872 | tf_op jit(solution)/shard_map/ppermute | solution.py:63
  224.5 20.4 %collective-permute-start.23 = (bf16[256,1024]{1,0:T(8,128)(2,1)S(1)}, bf16[256,1024]{1,0:T(8,128)(2,1)S(1)}, u32[]{:S(2)}, u32[]{:S(2)}) collective-permute-start(bf16[256,1024]{1,0:T(8,128)(2,1)S(1)} %fusion.22), channel_id=1, source_target_pairs={{0,4},{4,8},{8,12},{12,14},{14,10},{10,6},{6,2},{2,0},{1,5},{5,9},... | collective-permute-start | bytes 1572872 | tf_op jit(solution)/shard_map/ppermute | solution.py:63
  235.9 15.1 %collective-permute-start.45 = (bf16[256,1024]{1,0:T(8,128)(2,1)S(1)}, bf16[256,1024]{1,0:T(8,128)(2,1)S(1)}, u32[]{:S(2)}, u32[]{:S(2)}) collective-permute-start(bf16[256,1024]{1,0:T(8,128)(2,1)S(1)} %get-tuple-element.52), channel_id=1, source_target_pairs={{0,2},{4,0},{8,4},{12,8},{14,12},{10,14},{6,10},{2,6},{1,3},{5,1},... | collective-permute-start | bytes 1572872 | tf_op jit(solution)/shard_map/ppermute | solution.py:63
  245.3 37.1 %copy-start.6 = (bf16[512,1024]{1,0:T(8,128)(2,1)S(1)}, bf16[512,1024]{1,0:T(8,128)(2,1)}, u32[]{:S(2)}) copy-start(bf16[512,1024]{1,0:T(8,128)(2,1)} %param.12) | copy-start | bytes 3145732
  245.3 37.0 %copy-start.7 = (bf16[512,1024]{1,0:T(8,128)(2,1)S(1)}, bf16[512,1024]{1,0:T(8,128)(2,1)}, u32[]{:S(2)}) copy-start(bf16[512,1024]{1,0:T(8,128)(2,1)} %param.11) | copy-start | bytes 3145732
  245.3 17.0 %collective-permute-start.27 = (bf16[256,1024]{1,0:T(8,128)(2,1)S(1)}, bf16[256,1024]{1,0:T(8,128)(2,1)S(1)}, u32[]{:S(2)}, u32[]{:S(2)}) collective-permute-start(bf16[256,1024]{1,0:T(8,128)(2,1)S(1)} %get-tuple-element.50), channel_id=1, source_target_pairs={{0,2},{4,0},{8,4},{12,8},{14,12},{10,14},{6,10},{2,6},{1,3},{5,1},... | collective-permute-start | bytes 1572872 | tf_op jit(solution)/shard_map/ppermute | solution.py:63
  246.9 15.6 %collective-permute-start.42 = (bf16[256,1024]{1,0:T(8,128)(2,1)S(1)}, bf16[256,1024]{1,0:T(8,128)(2,1)S(1)}, u32[]{:S(2)}, u32[]{:S(2)}) collective-permute-start(bf16[256,1024]{1,0:T(8,128)(2,1)S(1)} %get-tuple-element.51), channel_id=1, source_target_pairs={{0,4},{4,8},{8,12},{12,14},{14,10},{10,6},{6,2},{2,0},{1,5},{5,9},... | collective-permute-start | bytes 1572872 | tf_op jit(solution)/shard_map/ppermute | solution.py:63
  247.4 22.5 %collective-permute-start.24 = (bf16[256,1024]{1,0:T(8,128)(2,1)S(1)}, bf16[256,1024]{1,0:T(8,128)(2,1)S(1)}, u32[]{:S(2)}, u32[]{:S(2)}) collective-permute-start(bf16[256,1024]{1,0:T(8,128)(2,1)S(1)} %get-tuple-element.49), channel_id=1, source_target_pairs={{0,4},{4,8},{8,12},{12,14},{14,10},{10,6},{6,2},{2,0},{1,5},{5,9},... | collective-permute-start | bytes 1572872 | tf_op jit(solution)/shard_map/ppermute | solution.py:63
  251.2 22.3 %collective-permute-start.46 = (bf16[256,1024]{1,0:T(8,128)(2,1)S(1)}, bf16[256,1024]{1,0:T(8,128)(2,1)S(1)}, u32[]{:S(2)}, u32[]{:S(2)}) collective-permute-start(bf16[256,1024]{1,0:T(8,128)(2,1)S(1)} %fusion.14), channel_id=1, source_target_pairs={{0,2},{4,0},{8,4},{12,8},{14,12},{10,14},{6,10},{2,6},{1,3},{5,1},... | collective-permute-start | bytes 1572872 | tf_op jit(solution)/shard_map/ppermute | solution.py:63
  262.4 19.9 %collective-permute-start.28 = (bf16[256,1024]{1,0:T(8,128)(2,1)S(1)}, bf16[256,1024]{1,0:T(8,128)(2,1)S(1)}, u32[]{:S(2)}, u32[]{:S(2)}) collective-permute-start(bf16[256,1024]{1,0:T(8,128)(2,1)S(1)} %fusion.21), channel_id=1, source_target_pairs={{0,2},{4,0},{8,4},{12,8},{14,12},{10,14},{6,10},{2,6},{1,3},{5,1},... | collective-permute-start | bytes 1572872 | tf_op jit(solution)/shard_map/ppermute | solution.py:63

commit v3 on v2

--- a/solution.py
+++ b/solution.py
@@ -8,7 +8,9 @@
 from jax.experimental.pallas import tpu as pltpu
 from jax.sharding import PartitionSpec as P
 
-VMEM_LIMIT = 40 * 1024 * 1024
+GATE_UP_VMEM = 56 * 1024 * 1024
+DOWN_VMEM = 40 * 1024 * 1024
+DEEP, PARTS = 3, 4
 LANES = 128
 
 
@@ -38,7 +40,7 @@
     half = count // 2
     order = send_order(count)
     pairs = np.zeros((count, 2, 3, half), np.int32)
-    tiles = np.zeros((count, 2, 3, count), np.int32)
+    tiles = np.zeros((count, 2, 2, count), np.int32)
     for block in range(count):
         own = place[block]
         for core in range(2):
@@ -48,12 +50,9 @@
                 mine = first // half == core
                 kept = first if mine else second
                 pairs[block, core, :, index] = mine, kept % half, kept
-            wanted = [ring[(own + distance) % count] for distance in order]
-            held = [next(w % half for w in wanted if (w // half == core) == (kind == 0)) for kind in range(2)]
-            for index, target in enumerate(wanted):
-                local = target // half == core
-                held[0 if local else 1] = target % half
-                tiles[block, core, :, index] = local, held[0], held[1]
+            for index, distance in enumerate(order):
+                target = ring[(own + distance) % count]
+                tiles[block, core, :, index] = target // half == core, target % half
     return pairs, tiles
 
 
@@ -136,16 +135,15 @@
             outs[0][which] = total
 
 
-def gate_up(group, final, pairs, before, second, last, received, gains, gate_weight, up_weight, sofar):
-    rows, width = before[0].shape
+def gate_up(group, final, pairs, pieces, gains, gate_weight, up_weight, sofar):
+    rows, width = pieces[0][0].shape
     columns = gate_weight.shape[1]
     tile = min(512, columns)
     anywhere = pl.BlockSpec(memory_space=pl.ANY)
     operands, in_specs = [], []
-    for index in group:
-        pieces = [before[index], *(second[index - 1 : index] if index else last), received[index]]
-        operands += pieces
-        in_specs += [anywhere] * len(pieces)
+    for piece in pieces:
+        operands += piece
+        in_specs += [anywhere] * len(piece)
     operands.append(gains)
     in_specs.append(pl.BlockSpec(gains.shape, lambda n, pairs: (0, 0, 0)))
     for weight in (gate_weight, up_weight):
@@ -189,7 +187,7 @@
                 pltpu.SemaphoreType.DMA((3, len(group))),
             ],
         ),
-        compiler_params=pltpu.CompilerParams(vmem_limit_bytes=VMEM_LIMIT),
+        compiler_params=pltpu.CompilerParams(vmem_limit_bytes=GATE_UP_VMEM),
         cost_estimate=pl.CostEstimate(
             flops=12 * rows * width * columns * len(group),
             bytes_accessed=4 * width * columns * len(group),
@@ -199,53 +197,77 @@
     )(pairs, *operands)
 
 
-def down_kernel(start, mean_of, tiles_ref, *refs):
+def down_kernel(start, steps, mean_of, tiles_ref, *refs):
+    refs = list(refs)
+    buffer, sems = refs.pop(), refs.pop()
+    step = pl.program_id(0)
     if start == 0:
         own_ref, own_stat, received_ref, received_stat, local_ref, other_ref, out_ref, hidden = refs
-
-        @pl.when(pl.program_id(0) == 0)
-        def activate():
+    else:
+        hidden, local_ref, other_ref, out_ref = refs
+    depth, width = buffer.shape[1:]
+
+    def fetch(tile, act):
+        slot = lax.rem(tile, DEEP)
+        for kind, source in ((1, local_ref), (0, other_ref)):
+
+            @pl.when(tiles_ref[0, tile + start] == kind)
+            def chosen(source=source):
+                column = pl.multiple_of(tiles_ref[1, tile + start] * width, width)
+                for part in range(PARTS):
+                    row = pl.ds(part * (depth // PARTS), depth // PARTS)
+                    act(
+                        pltpu.make_async_copy(
+                            source.at[row, pl.ds(column, width)], buffer.at[slot, row], sems.at[slot, part]
+                        )
+                    )
+
+    @pl.when(step == 0)
+    def first():
+        for tile in range(min(DEEP - 1, steps)):
+            fetch(tile, lambda copy: copy.start())
+        if start == 0:
             total = jnp.sum(own_stat[...] + received_stat[...], axis=1, keepdims=True)
             inv = lax.rsqrt(total / mean_of + 1e-05)
             gate = (own_ref[0] + received_ref[0].astype(jnp.float32)) * inv
             up = (own_ref[1] + received_ref[1].astype(jnp.float32)) * inv
             hidden[...] = (gate / (1.0 + jnp.exp(-gate)) * up).astype(jnp.bfloat16)
-    else:
-        hidden, local_ref, other_ref, out_ref = refs
-
-    def product(weight_ref):
-        out_ref[0] = jnp.dot(hidden[...], weight_ref[...], preferred_element_type=jnp.float32).astype(jnp.bfloat16)
-
-    local = tiles_ref[0, pl.program_id(0) + start] == 1
-    pl.when(local)(functools.partial(product, local_ref))
-    pl.when(jnp.logical_not(local))(functools.partial(product, other_ref))
+
+    @pl.when(step + DEEP - 1 < steps)
+    def ahead():
+        fetch(step + DEEP - 1, lambda copy: copy.start())
+
+    fetch(step, lambda copy: copy.wait())
+    weight = buffer[lax.rem(step, DEEP)]
+    out_ref[0] = jnp.dot(hidden[...], weight, preferred_element_type=jnp.float32).astype(jnp.bfloat16)
 
 
 def down(start, stop, tiles, operands, local, other, width):
-    count = tiles.shape[1]
     rows, depth = operands[0].shape[-2:]
 
     def whole(value):
         return pl.BlockSpec(value.shape, lambda j, tiles: (0,) * value.ndim)
 
-    def weight_spec(row):
-        return pl.BlockSpec((depth, width), lambda j, tiles: (0, tiles[row, j + start]))
-
+    anywhere = pl.BlockSpec(memory_space=pl.ANY)
     out_shape = [jax.ShapeDtypeStruct((stop - start, rows, width), jnp.bfloat16)]
     out_specs = [pl.BlockSpec((1, rows, width), lambda j, tiles: (j, 0, 0))]
     if start == 0:
         out_shape.append(jax.ShapeDtypeStruct((rows, depth), jnp.bfloat16))
         out_specs.append(pl.BlockSpec((rows, depth), lambda j, tiles: (0, 0)))
     return pl.pallas_call(
-        functools.partial(down_kernel, start, width * count),
+        functools.partial(down_kernel, start, stop - start, width * tiles.shape[1]),
         out_shape=out_shape,
         grid_spec=pltpu.PrefetchScalarGridSpec(
             num_scalar_prefetch=1,
             grid=(stop - start,),
-            in_specs=[*map(whole, operands), weight_spec(1), weight_spec(2)],
+            in_specs=[*map(whole, operands), anywhere, anywhere],
             out_specs=out_specs,
+            scratch_shapes=[
+                pltpu.SemaphoreType.DMA((DEEP, PARTS)),
+                pltpu.VMEM((DEEP, depth, width), jnp.bfloat16),
+            ],
         ),
-        compiler_params=pltpu.CompilerParams(vmem_limit_bytes=VMEM_LIMIT),
+        compiler_params=pltpu.CompilerParams(vmem_limit_bytes=DOWN_VMEM),
         cost_estimate=pl.CostEstimate(
             flops=4 * rows * depth * width * (stop - start),
             bytes_accessed=2 * depth * width * (stop - start),
@@ -255,41 +277,42 @@
     )(tiles, *operands, local, other)
 
 
-def gather(block, half, mine_first):
-    rows = block.shape[0]
-    before, behind = [block], []
-    ahead = block
-    for step in range(1, half):
-        before.append(ring_shift(before[-1], 1))
-        ahead = ring_shift(ahead, -1)
-        behind.append(ahead)
-    last = (ring_shift(before[-1][: rows // 2], 1), ring_shift(behind[-1][rows // 2 :], -1))
-    second = behind[::-1]
-    received = []
-    for index in range(half):
-        other = jnp.concatenate(last, axis=0) if index == 0 else second[index - 1]
-        received.append(swap(jnp.where(mine_first[index], other, before[index])))
-    return before, second, last, received
-
-
-def scatter(term, count):
+def exchange(index, block, steps, mine_first):
+    half = len(steps)
+    if index:
+        first, second = steps[index - 1][0], (steps[half - index - 1][1],)
+    else:
+        first, second = block, steps[half - 1]
+    other = second[0] if index else jnp.concatenate(second, axis=0)
+    return (first, *second, swap(jnp.where(mine_first[index], other, first)))
+
+
+def gather_step(block, steps, half, *earlier):
+    before, behind = after(steps[-1] if steps else (block, block), *earlier)
+    if len(steps) == half - 1:
+        cut = block.shape[0] // 2
+        before, behind = before[:cut], behind[cut:]
+    return [*steps, (ring_shift(before, 1), ring_shift(behind, -1))]
+
+
+def joined(one, two):
+    return (one.astype(jnp.float32) + two.astype(jnp.float32)).astype(jnp.bfloat16)
+
+
+def scatter_step(moved, term, count, distance, *earlier):
     half = count // 2
-    cut = term(0).shape[0] // 2
-
-    def joined(one, two):
-        return (one.astype(jnp.float32) + two.astype(jnp.float32)).astype(jnp.bfloat16)
-
-    forth = ring_shift(term(half)[:cut], 1)
-    back = ring_shift(term(half)[cut:], -1)
-    for distance in range(half - 1, 0, -1):
-        ahead, behind = term(distance), term(count - distance)
-        if distance == half - 1:
-            forth = jnp.concatenate([joined(ahead[:cut], forth), ahead[cut:]], axis=0)
-            back = jnp.concatenate([behind[:cut], joined(behind[cut:], back)], axis=0)
-        else:
-            forth, back = joined(ahead, forth), joined(behind, back)
-        forth, back = ring_shift(forth, 1), ring_shift(back, -1)
-    return term(0).astype(jnp.float32) + forth.astype(jnp.float32) + back.astype(jnp.float32)
+    ahead, behind = term(distance), term(count - distance)
+    cut = ahead.shape[0] // 2
+    if distance == half:
+        forth, back = ahead[:cut], behind[cut:]
+    elif distance == half - 1:
+        forth, back = after(moved, *earlier)
+        forth = jnp.concatenate([joined(ahead[:cut], forth), ahead[cut:]], axis=0)
+        back = jnp.concatenate([behind[:cut], joined(behind[cut:], back)], axis=0)
+    else:
+        forth, back = after(moved, *earlier)
+        forth, back = joined(ahead, forth), joined(behind, back)
+    return ring_shift(forth, 1), ring_shift(back, -1)
 
 
 def on_device(
@@ -339,39 +362,76 @@
         return (result.astype(jnp.bfloat16).astype(jnp.float32) * own_gain).astype(jnp.bfloat16)
 
     size = row_count // 2
-    gathered = {}
-    gathered[size] = gather(convolve(noisy_input, self_cond, edges, size, size), half, mine_first)
-    near = min(2, half - 1)
-    lead = (gathered[size][0][near], gathered[size][1][half - 1 - near])
-    later_noisy, later_cond, later_edges = after((noisy_input, self_cond, edges), *lead)
-    gathered[0] = gather(convolve(later_noisy, later_cond, later_edges, 0, size), half, mine_first)
-
+    early = min(3, count - 1)
     groups = pair_groups(half)
-    outs = {}
-    for start in (size, 0):
-        before, second, last, received = gathered[start]
-        sofar = None
-        used = groups if start else [sum(groups[:-1], []), groups[-1]]
-        for number, group in enumerate(used):
-            final = number == len(used) - 1
-            sofar = gate_up(
-                group, final, pairs, before, second, last, received, gains, gate_weight, up_weight, sofar
-            )
-        own_sum, own_stat, sent, sent_stat = sofar
+
+    def matmul(group, final, block, steps, sofar, *earlier):
+        pieces = [exchange(index, block, steps, mine_first) for index in group]
+        pieces = after(pieces, *earlier)
+        return gate_up(group, final, pairs, pieces, gains, gate_weight, up_weight, sofar)
+
+    def open_down(sums, *earlier):
+        own_sum, own_stat, sent, sent_stat = sums
         received_sum, received_stat = swap((sent, sent_stat))
-        early = min(3, count - 1)
-        terms, hidden = down(
-            0, early, tiles, [own_sum, own_stat, received_sum, received_stat], down_weight, other_down, width
-        )
-        (more,) = down(early, count, tiles, [hidden], down_weight, other_down, width)
-
-        def term(distance, terms=terms, more=more):
+        operands = after([own_sum, own_stat, received_sum, received_stat], *earlier)
+        return down(0, early, tiles, operands, down_weight, other_down, width)
+
+    def close_down(hidden, *earlier):
+        return down(early, count, tiles, [after(hidden, *earlier)], down_weight, other_down, width)[0]
+
+    def term_of(opened, closed):
+        def term(distance):
             index = order.index(distance)
-            return terms[index] if index < early else more[index - early]
-
+            return opened[index] if index < early else closed[index - early]
+
+        return term
+
+    block_a = convolve(noisy_input, self_cond, edges, size, size)
+    steps_a = []
+    for _ in range(half - 1):
+        steps_a = gather_step(block_a, steps_a, half)
+        if len(steps_a) == min(2, half - 1):
+            later = after((noisy_input, self_cond, edges), *steps_a[-1])
+    block_b = convolve(*later, 0, size)
+    sums_a = matmul(groups[0], False, block_a, steps_a + [None], None)
+    third_a = steps_a[-1]
+    steps_a = gather_step(block_a, steps_a, half, sums_a[1])
+    steps_b = gather_step(block_b, [], half, sums_a[1], *third_a)
+    for group in groups[1:-1]:
+        sums_a = matmul(group, False, block_a, steps_a, sums_a)
+    first_b = steps_b[-1]
+    steps_b = gather_step(block_b, steps_b, half, sums_a[1])
+    sums_a = matmul(groups[-1], True, block_a, steps_a, sums_a, *first_b)
+    second_b = steps_b[-1]
+    steps_b = gather_step(block_b, steps_b, half, sums_a[1])
+    opened_a, hidden_a = open_down(sums_a, *second_b)
+    while len(steps_b) < half - 1:
+        steps_b = gather_step(block_b, steps_b, half)
+    third_b = steps_b[-1]
+    steps_b = gather_step(block_b, steps_b, half, opened_a)
+    closed_a = close_down(hidden_a, *third_b)
+    term_a = term_of(opened_a, closed_a)
+    moved_a = scatter_step(None, term_a, count, half)
+    sums_b = matmul(sum(groups[:-1], []), False, block_b, steps_b, None, closed_a, *moved_a)
+    distances = list(range(half - 1, 0, -1))
+    moved_a = scatter_step(moved_a, term_a, count, distances.pop(0))
+    sums_b = matmul(groups[-1], True, block_b, steps_b, sums_b, *moved_a)
+    moved_a = scatter_step(moved_a, term_a, count, distances.pop(0), sums_b[1])
+    opened_b, hidden_b = open_down(sums_b, *moved_a)
+    for distance in distances:
+        moved_a = scatter_step(moved_a, term_a, count, distance)
+    closed_b = close_down(hidden_b)
+    term_b = term_of(opened_b, closed_b)
+    moved_b = scatter_step(None, term_b, count, half)
+    for distance in range(half - 1, 0, -1):
+        moved_b = scatter_step(moved_b, term_b, count, distance)
+
+    def finish(start, term, moved):
         mixed = mix(noisy_input[start : start + size], self_cond[start : start + size])
-        outs[start] = (mixed + scatter(term, count)).astype(jnp.bfloat16)
-    return jnp.concatenate([outs[0], outs[size]], axis=0)
+        ffn = term(0).astype(jnp.float32) + moved[0].astype(jnp.float32) + moved[1].astype(jnp.float32)
+        return (mixed + ffn).astype(jnp.bfloat16)
+
+    return jnp.concatenate([finish(0, term_b, moved_b), finish(size, term_a, moved_a)], axis=0)
 
 
 def solution(mesh):

time: 285 us -> 300 us (1.053)
  waiting for transfers between devices: 105 us -> 114 us
  local copies, waits for them, and re-layouts: 15.7 us -> 10.9 us
  other arithmetic: 14.4 us -> 18.7 us
  Pallas kernels: 110 us -> 113 us
    pallas_call x5, Pallas kernels: 63.6 us -> 80.6 us  [gate_up(): pl.pallas_call(functools.partial(gate_up_kernel, group, final, rows, widt...]
    pallas_call x4, Pallas kernels: 46 us -> 32.5 us  [down(): pl.pallas_call(functools.partial(down_kernel, start, stop - start, width...]
    ppermute x32, waiting for transfers between devices: 102 us -> 112 us  [ring_shift(): lax.ppermute(value, 'blk', [(ring[i], ring[(i + steps) % count]) for i in...]
    unnamed x18 -> x58, local copies, waits for them, and re-layouts: 10.4 us -> 6.52 us
    select_n x8, other arithmetic: 6.08 us -> 9.77 us  [exchange(): return (first, *second, swap(jnp.where(mine_first[index], other, first)))]
  transfers between devices with their start and end apart: 47 -> 47, of which waited for: 20 -> 23; matrix products, arithmetic and copies ran while one was open for 6% -> 7% of each run, Pallas kernels for 39% -> 31%
where the time goes in v3:
time: 300 us; the launch traced here: 299 us
  waiting for transfers between devices  114 us (38%)
  Pallas kernels  113 us (38%)
  starting transfers between devices  40.9 us (14%)
  other arithmetic  18.7 us (6%)
  local copies, waits for them, and re-layouts  10.9 us (4%)
    ppermute x32, waiting for transfers between devices, ring_shift(): lax.ppermute(value, 'blk', [(ring[i], ring[(i + steps) % count]) for i in...  112 us
    pallas_call x5, Pallas kernels, gate_up(): pl.pallas_call(functools.partial(gate_up_kernel, group, final, rows, widt...  80.6 us
    ppermute x32, starting transfers between devices, ring_shift(): lax.ppermute(value, 'blk', [(ring[i], ring[(i + steps) % count]) for i in...  34.5 us
    pallas_call x4, Pallas kernels, down(): pl.pallas_call(functools.partial(down_kernel, start, stop - start, width...  32.5 us
    select_n x8, other arithmetic, exchange(): return (first, *second, swap(jnp.where(mine_first[index], other, first)))  9.77 us
    unnamed x58, local copies, waits for them, and re-layouts  6.52 us
  transfers between devices with their start and end apart: 47, of which 23 were waited for; matrix products, arithmetic and copies ran while one was open for 7% of the time, Pallas kernels for 31%

profile of v3, /device:TPU:0, one launch (start us, length us, event | category | flops | bytes accessed | tf_op | source)
XLA Modules:
  0.0 299.2 jit_solution(17849931928098379834)
XLA Ops:
  1.8 0.9 constant_dynamic-slice_fusion.2
  2.7 1.5 multiply_add_fusion
  4.8 2.6 collective-permute-start.2
  8.1 11.9 %collective-permute-done.2.refs_0_ = bf16[256,1024]{1,0:T(8,128)(2,1)} collective-permute-done((bf16[256,1024]{1,0:T(8,128)(2,1)S(1)}, bf16[256,1024]{1,0:T(8,128)(2,1)}, u32[]{:S(2)}, u32[]{:S(2)}) %collective-permute-start.2) | collective-permute-done | bytes 524320 | tf_op jit(solution)/shard_map/ppermute | solution.py:62
  20.0 1.5 collective-permute-done.3.refs_4_
  21.5 1.6 collective-permute-start.4
  23.6 1.3 constant_dynamic-slice_fusion.4
  25.5 9.6 %collective-permute-done.4.refs_0_ = bf16[256,1024]{1,0:T(8,128)(2,1)} collective-permute-done((bf16[256,1024]{1,0:T(8,128)(2,1)}, bf16[256,1024]{1,0:T(8,128)(2,1)}, u32[]{:S(2)}, u32[]{:S(2)}) %collective-permute-start.4) | collective-permute-done | bytes 524320 | tf_op jit(solution)/shard_map/ppermute | solution.py:62
  35.1 1.3 collective-permute-done.5.refs_1_
  36.4 1.6 broadcast_select_fusion.5
  38.1 1.6 collective-permute-start.7
  39.8 2.1 collective-permute-start.1
  41.9 1.3 collective-permute-start
  43.2 0.8 collective-permute-done
  44.7 8.0 %collective-permute-done.7.refs_3_ = bf16[256,1024]{1,0:T(8,128)(2,1)S(1)} collective-permute-done((bf16[256,1024]{1,0:T(8,128)(2,1)}, bf16[256,1024]{1,0:T(8,128)(2,1)S(1)}, u32[]{:S(2)}, u32[]{:S(2)}) %collective-permute-start.7) | collective-permute-done | bytes 524320 | tf_op jit(solution)/shard_map/ppermute | solution.py:62
  52.7 1.6 broadcast_select_fusion.1
  54.9 3.4 %collective-permute-done.8.refs_1_ = bf16[256,1024]{1,0:T(8,128)(2,1)S(1)} collective-permute-done((bf16[256,1024]{1,0:T(8,128)(2,1)}, bf16[256,1024]{1,0:T(8,128)(2,1)S(1)}, u32[]{:S(2)}, u32[]{:S(2)}) %collective-permute-start.8) | collective-permute-done | bytes 524320 | tf_op jit(solution)/shard_map/ppermute | solution.py:62
  58.4 1.4 broadcast_select_fusion.3
  60.4 11.6 %gate_up.5 = (f32[2,512,2048]{2,1,0:T(8,128)}, f32[512,128]{1,0:T(8,128)}) custom-call(s32[3,4]{1,0:T(4,128)} %get-tuple-element.202.pairs_ref, bf16[256,1024]{1,0:T(8,128)(2,1)} %collective-permute-done.4.refs_0_, bf16[256,1024]{1,0:T(8,128)(2,1)} %collective-permute-done.5.refs_1_, bf16[256,1024]{1,0:T(8,128)(2,1)} %copy-done.25, f32[8,1,1024]{2,1,0:T(1,128)} %bitcast.95, ...), custom_call_target="tpu_custom_call" | custom-call | flops 6442450944 | bytes 8388608 | tf_op jit(solution)/shard_map/gate_up/pallas_call | solution.py:177
  72.6 1.6 collective-permute-start.15
  74.7 5.7 %collective-permute-done.16.refs_2_ = bf16[128,1024]{1,0:T(8,128)(2,1)S(1)} collective-permute-done((bf16[128,1024]{1,0:T(8,128)(2,1)S(1)}, bf16[128,1024]{1,0:T(8,128)(2,1)S(1)}, u32[]{:S(2)}, u32[]{:S(2)}) %collective-permute-start.16) | collective-permute-done | bytes 262176 | tf_op jit(solution)/shard_map/ppermute | solution.py:62
  80.4 1.5 collective-permute-start.9
  82.4 1.2 maximum_select_fusion
  84.6 19.6 %gate_up.6 = (f32[2,512,2048]{2,1,0:T(8,128)}, f32[512,128]{1,0:T(8,128)}) custom-call(s32[3,4]{1,0:T(4,128)} %get-tuple-element.202.pairs_ref, bf16[256,1024]{1,0:T(8,128)(2,1)} %collective-permute-done.2.refs_0_, bf16[256,1024]{1,0:T(8,128)(2,1)} %copy-done.10, bf16[256,1024]{1,0:T(8,128)(2,1)} %copy-done.23, bf16[256,1024]{1,0:T(8,128)(2,1)} %copy-done.9, ...), custom_call_target="tpu_custom_call" | custom-call | flops 12884901888 | bytes 16777216 | tf_op jit(solution)/shard_map/gate_up/pallas_call | solution.py:177
  104.3 1.0 copy-done.26
  105.3 13.3 %gate_up.7 = (f32[2,256,2048]{2,1,0:T(8,128)}, f32[256,128]{1,0:T(8,128)}, bf16[2,256,2048]{2,1,0:T(8,128)(2,1)}, f32[256,128]{1,0:T(8,128)}) custom-call(s32[3,4]{1,0:T(4,128)} %get-tuple-element.202.pairs_ref, bf16[256,1024]{1,0:T(8,128)(2,1)} %copy-done.15, bf16[128,1024]{1,0:T(8,128)(2,1)} %copy-done.17, bf16[128,1024]{1,0:T(8,128)(2,1)} %copy-done.16, ...), custom_call_target="tpu_custom_call" | custom-call | flops 6442450944 | bytes 8388608 | tf_op jit(solution)/shard_map/gate_up/pallas_call | solution.py:177
  119.1 1.5 collective-permute-start.13
  121.1 11.9 %collective-permute-done.13.refs_0_ = bf16[256,1024]{1,0:T(8,128)(2,1)S(1)} collective-permute-done((bf16[256,1024]{1,0:T(8,128)(2,1)S(1)}, bf16[256,1024]{1,0:T(8,128)(2,1)S(1)}, u32[]{:S(2)}, u32[]{:S(2)}) %collective-permute-start.13) | collective-permute-done | bytes 524320 | tf_op jit(solution)/shard_map/ppermute | solution.py:62
  133.0 1.2 collective-permute-done.14.refs_1_
  134.3 1.3 collective-permute-start.18
  136.3 0.9 collective-permute-start.19
  137.2 1.0 broadcast_select_fusion.4
  138.2 8.9 %collective-permute-done.18.refs_6_ = bf16[256,1024]{1,0:T(8,128)(2,1)S(1)} collective-permute-done((bf16[256,1024]{1,0:T(8,128)(2,1)S(1)}, bf16[256,1024]{1,0:T(8,128)(2,1)S(1)}, u32[]{:S(2)}, u32[]{:S(2)}) %collective-permute-start.18) | collective-permute-done | bytes 524320 | tf_op jit(solution)/shard_map/ppermute | solution.py:62
  147.8 2.8 collective-permute-done.19.refs_4_
  151.3 6.8 %down.4 = (bf16[3,256,1024]{2,1,0:T(8,128)(2,1)S(1)}, bf16[256,2048]{1,0:T(8,128)(2,1)S(1)}) custom-call(s32[2,8]{1,0:T(2,128)S(1)} %fusion.31.tiles_ref, f32[2,256,2048]{2,1,0:T(8,128)S(1)} %copy-done, f32[256,128]{1,0:T(8,128)S(1)} %copy-done.2, bf16[2,256,2048]{2,1,0:T(8,128)(2,1)S(1)} %collective-permute-done.20.refs_2_, ...), custom_call_target="tpu_custom_call" | custom-call | flops 6442450944 | bytes 12582912 | tf_op jit(solution)/shard_map/down/pallas_call | solution.py:257
  159.0 1.3 collective-permute-start.23
  161.1 1.3 collective-permute-start.26
  162.4 9.4 %down.5 = bf16[5,256,1024]{2,1,0:T(8,128)(2,1)S(1)} custom-call(s32[2,8]{1,0:T(2,128)S(1)} %fusion.31.tiles_ref, bf16[256,2048]{1,0:T(8,128)(2,1)S(1)} %get-tuple-element.143.refs_0_, bf16[2048,4096]{1,0:T(8,128)(2,1)} %refs_1_.3, bf16[2048,4096]{1,0:T(8,128)(2,1)} %collective-permute-done.22.refs_5_.refs_2_), custom_call_target="tpu_custom_call" | custom-call | flops 10737418240 | bytes 20971520 | tf_op jit(solution)/shard_map/down/pallas_call | solution.py:257
  172.5 1.6 maximum_select_fusion.1
  174.4 0.9 pad_maximum_fusion.2
  175.3 1.4 collective-permute-start.28
  177.4 0.8 copy-done.22
  178.2 0.8 copy-done.24
  179.0 22.7 %gate_up.8 = (f32[2,512,2048]{2,1,0:T(8,128)}, f32[512,128]{1,0:T(8,128)}) custom-call(s32[3,4]{1,0:T(4,128)} %get-tuple-element.202.pairs_ref, bf16[256,1024]{1,0:T(8,128)(2,1)} %copy-done.13, bf16[256,1024]{1,0:T(8,128)(2,1)} %copy-done.14, bf16[256,1024]{1,0:T(8,128)(2,1)} %collective-permute-done.30.refs_2_, bf16[256,1024]{1,0:T(8,128)(2,1)} %copy-done.11, ...), custom_call_target="tpu_custom_call" | custom-call | flops 19327352832 | bytes 25165824 | tf_op jit(solution)/shard_map/gate_up/pallas_call | solution.py:177
  202.5 13.3 %gate_up.9 = (f32[2,256,2048]{2,1,0:T(8,128)}, f32[256,128]{1,0:T(8,128)}, bf16[2,256,2048]{2,1,0:T(8,128)(2,1)}, f32[256,128]{1,0:T(8,128)}) custom-call(s32[3,4]{1,0:T(4,128)} %get-tuple-element.202.pairs_ref, bf16[256,1024]{1,0:T(8,128)(2,1)} %copy-done.4, bf16[128,1024]{1,0:T(8,128)(2,1)} %copy-done.19, bf16[128,1024]{1,0:T(8,128)(2,1)} %copy-done.18, ...), custom_call_target="tpu_custom_call" | custom-call | flops 6442450944 | bytes 8388608 | tf_op jit(solution)/shard_map/gate_up/pallas_call | solution.py:177
  216.0 1.4 fusion.25
  218.2 1.3 collective-permute-start.35
  219.5 1.3 collective-permute-done.34.refs_3_
  220.8 10.9 %collective-permute-done.36 = bf16[256,1024]{1,0:T(8,128)(2,1)S(1)} collective-permute-done((bf16[256,1024]{1,0:T(8,128)(2,1)S(1)}, bf16[256,1024]{1,0:T(8,128)(2,1)S(1)}, u32[]{:S(2)}, u32[]{:S(2)}) %collective-permute-start.36) | collective-permute-done | bytes 524320 | tf_op jit(solution)/shard_map/ppermute | solution.py:62
  232.2 2.2 copy-done.1
  234.4 6.8 %down.6 = (bf16[3,256,1024]{2,1,0:T(8,128)(2,1)S(1)}, bf16[256,2048]{1,0:T(8,128)(2,1)S(1)}) custom-call(s32[2,8]{1,0:T(2,128)S(1)} %fusion.31.tiles_ref, f32[2,256,2048]{2,1,0:T(8,128)S(1)} %copy-done.1, f32[256,128]{1,0:T(8,128)S(1)} %copy-done.3, bf16[2,256,2048]{2,1,0:T(8,128)(2,1)S(1)} %collective-permute-done.33.refs_2_, ...), custom_call_target="tpu_custom_call" | custom-call | flops 6442450944 | bytes 12582912 | tf_op jit(solution)/shard_map/down/pallas_call | solution.py:257
  241.9 1.5 collective-permute-start.37
  243.3 5.5 %collective-permute-done.38 = bf16[128,1024]{1,0:T(8,128)(2,1)S(1)} collective-permute-done((bf16[128,1024]{1,0:T(8,128)(2,1)S(1)}, bf16[128,1024]{1,0:T(8,128)(2,1)S(1)}, u32[]{:S(2)}, u32[]{:S(2)}) %collective-permute-start.38) | collective-permute-done | bytes 262176 | tf_op jit(solution)/shard_map/ppermute | solution.py:62
  249.5 1.4 collective-permute-start.39
  251.6 9.4 %down.7 = bf16[5,256,1024]{2,1,0:T(8,128)(2,1)S(1)} custom-call(s32[2,8]{1,0:T(2,128)S(1)} %fusion.31.tiles_ref, bf16[256,2048]{1,0:T(8,128)(2,1)S(1)} %get-tuple-element.165.refs_0_, bf16[2048,4096]{1,0:T(8,128)(2,1)} %refs_1_.3, bf16[2048,4096]{1,0:T(8,128)(2,1)} %collective-permute-done.22.refs_5_.refs_2_), custom_call_target="tpu_custom_call" | custom-call | flops 10737418240 | bytes 20971520 | tf_op jit(solution)/shard_map/down/pallas_call | solution.py:257
  261.6 1.1 collective-permute-done.40
  263.9 1.3 collective-permute-start.41
  265.6 1.4 collective-permute-start.45
  267.7 10.3 %collective-permute-done.42 = bf16[256,1024]{1,0:T(8,128)(2,1)S(1)} collective-permute-done((bf16[256,1024]{1,0:T(8,128)(2,1)S(1)}, bf16[256,1024]{1,0:T(8,128)(2,1)S(1)}, u32[]{:S(2)}, u32[]{:S(2)}) %collective-permute-start.42) | collective-permute-done | bytes 524320 | tf_op jit(solution)/shard_map/ppermute | solution.py:62
  279.2 1.4 collective-permute-start.43
  281.2 8.7 %collective-permute-done.45 = bf16[256,1024]{1,0:T(8,128)(2,1)S(1)} collective-permute-done((bf16[256,1024]{1,0:T(8,128)(2,1)S(1)}, bf16[256,1024]{1,0:T(8,128)(2,1)S(1)}, u32[]{:S(2)}, u32[]{:S(2)}) %collective-permute-start.45) | collective-permute-done | bytes 524320 | tf_op jit(solution)/shard_map/ppermute | solution.py:62
  290.0 6.9 %collective-permute-done.43 = bf16[256,1024]{1,0:T(8,128)(2,1)S(1)} collective-permute-done((bf16[256,1024]{1,0:T(8,128)(2,1)S(1)}, bf16[256,1024]{1,0:T(8,128)(2,1)S(1)}, u32[]{:S(2)}, u32[]{:S(2)}) %collective-permute-start.43) | collective-permute-done | bytes 524320 | tf_op jit(solution)/shard_map/ppermute | solution.py:62
  296.9 1.2 fusion.24
  298.1 1.0 pad_maximum_fusion.1
  (136 shorter events, 22.7 us)
Async XLA Ops:
  0.0 151.3 %collective-permute-start.22 = (bf16[2048,4096]{1,0:T(8,128)(2,1)}, bf16[2048,4096]{1,0:T(8,128)(2,1)}, u32[]{:S(2)}, u32[]{:S(2)}) collective-permute-start(bf16[2048,4096]{1,0:T(8,128)(2,1)} %refs_1_.3), channel_id=1, source_target_pairs={{0,1},{1,0},{2,3},{3,2},{4,5},{5,4},{6,7},{7,6},{8,9},{9,8},{10,11... | collective-permute-start | bytes 50331656 | tf_op jit(solution)/shard_map/ppermute | solution.py:66
  4.2 35.6 %copy-start.5 = (bf16[512,1024]{1,0:T(8,128)(2,1)S(1)}, bf16[512,1024]{1,0:T(8,128)(2,1)}, u32[]{:S(2)}) copy-start(bf16[512,1024]{1,0:T(8,128)(2,1)} %param.12) | copy-start | bytes 3145732
  4.2 37.6 %copy-start.6 = (bf16[512,1024]{1,0:T(8,128)(2,1)S(1)}, bf16[512,1024]{1,0:T(8,128)(2,1)}, u32[]{:S(2)}) copy-start(bf16[512,1024]{1,0:T(8,128)(2,1)} %param.11) | copy-start | bytes 3145732
  4.2 40.2 %copy-start.27 = (f32[1024]{0:T(1024)S(1)}, f32[1024]{0:T(1024)}, u32[]{:S(2)}) copy-start(f32[1024]{0:T(1024)} %param.13) | copy-start | bytes 12292
  4.8 15.3 %collective-permute-start.2 = (bf16[256,1024]{1,0:T(8,128)(2,1)S(1)}, bf16[256,1024]{1,0:T(8,128)(2,1)}, u32[]{:S(2)}, u32[]{:S(2)}) collective-permute-start(bf16[256,1024]{1,0:T(8,128)(2,1)S(1)} %multiply_convert_fusion.1.refs_0_), channel_id=1, source_target_pairs={{0,4},{4,8},{8,12},{12,14},{14,10},{10,6},{6,2},{2,0},{1,5},{5,9},... | collective-permute-start | bytes 1572872 | tf_op jit(solution)/shard_map/ppermute | solution.py:62
  7.4 14.2 %collective-permute-start.3 = (bf16[256,1024]{1,0:T(8,128)(2,1)S(1)}, bf16[256,1024]{1,0:T(8,128)(2,1)}, u32[]{:S(2)}, u32[]{:S(2)}) collective-permute-start(bf16[256,1024]{1,0:T(8,128)(2,1)S(1)} %multiply_convert_fusion.1.refs_0_), channel_id=1, source_target_pairs={{0,2},{4,0},{8,4},{12,8},{14,12},{10,14},{6,10},{2,6},{1,3},{5,1},... | collective-permute-start | bytes 1572872 | tf_op jit(solution)/shard_map/ppermute | solution.py:62
  21.5 13.6 %collective-permute-start.4 = (bf16[256,1024]{1,0:T(8,128)(2,1)}, bf16[256,1024]{1,0:T(8,128)(2,1)}, u32[]{:S(2)}, u32[]{:S(2)}) collective-permute-start(bf16[256,1024]{1,0:T(8,128)(2,1)} %collective-permute-done.2.refs_0_), channel_id=1, source_target_pairs={{0,4},{4,8},{8,12},{12,14},{14,10},{10,6},{6,2},{2,0},{1,5},{5,9},... | collective-permute-start | bytes 1572872 | tf_op jit(solution)/shard_map/ppermute | solution.py:62
  23.1 13.3 %collective-permute-start.5 = (bf16[256,1024]{1,0:T(8,128)(2,1)}, bf16[256,1024]{1,0:T(8,128)(2,1)}, u32[]{:S(2)}, u32[]{:S(2)}) collective-permute-start(bf16[256,1024]{1,0:T(8,128)(2,1)} %collective-permute-done.3.refs_4_), channel_id=1, source_target_pairs={{0,2},{4,0},{8,4},{12,8},{14,12},{10,14},{6,10},{2,6},{1,3},{5,1},... | collective-permute-start | bytes 1572872 | tf_op jit(solution)/shard_map/ppermute | solution.py:62
  38.0 6.6 %collective-permute-start.6 = (bf16[256,1024]{1,0:T(8,128)(2,1)S(1)}, bf16[256,1024]{1,0:T(8,128)(2,1)S(1)}, u32[]{:S(2)}, u32[]{:S(2)}) collective-permute-start(bf16[256,1024]{1,0:T(8,128)(2,1)S(1)} %broadcast_select_fusion.5), channel_id=1, source_target_pairs={{0,1},{1,0},{2,3},{3,2},{4,5},{5,4},{6,7},{7,6},{8,9},{9,8},{10,11... | collective-permute-start | bytes 1572872 | tf_op jit(solution)/shard_map/ppermute | solution.py:66
  38.1 14.5 %collective-permute-start.7 = (bf16[256,1024]{1,0:T(8,128)(2,1)}, bf16[256,1024]{1,0:T(8,128)(2,1)S(1)}, u32[]{:S(2)}, u32[]{:S(2)}) collective-permute-start(bf16[256,1024]{1,0:T(8,128)(2,1)} %collective-permute-done.4.refs_0_), channel_id=1, source_target_pairs={{0,4},{4,8},{8,12},{12,14},{14,10},{10,6},{6,2},{2,0},{1,5},{5,9},... | collective-permute-start | bytes 1572872 | tf_op jit(solution)/shard_map/ppermute | solution.py:62
  39.8 3.4 %collective-permute-start.1 = (bf16[3,1024]{1,0:T(4,128)(2,1)S(1)}, bf16[3,1024]{1,0:T(4,128)(2,1)S(1)}, u32[]{:S(2)}, u32[]{:S(2)}) collective-permute-start(bf16[3,1024]{1,0:T(4,128)(2,1)S(1)} %slice.225), channel_id=1, source_target_pairs={{0,1},{2,3},{4,5},{6,7},{8,9},{10,11},{12,13},{14,15},{16,17},{18,... | collective-permute-start | bytes 18440 | tf_op jit(solution)/shard_map/ppermute | solution.py:341
  41.9 2.1 collective-permute-start
  44.0 14.4 %collective-permute-start.8 = (bf16[256,1024]{1,0:T(8,128)(2,1)}, bf16[256,1024]{1,0:T(8,128)(2,1)S(1)}, u32[]{:S(2)}, u32[]{:S(2)}) collective-permute-start(bf16[256,1024]{1,0:T(8,128)(2,1)} %collective-permute-done.5.refs_1_), channel_id=1, source_target_pairs={{0,2},{4,0},{8,4},{12,8},{14,12},{10,14},{6,10},{2,6},{1,3},{5,1},... | collective-permute-start | bytes 1572872 | tf_op jit(solution)/shard_map/ppermute | solution.py:62
  44.7 15.7 %copy-start.25 = (bf16[256,1024]{1,0:T(8,128)(2,1)}, bf16[256,1024]{1,0:T(8,128)(2,1)S(1)}, u32[]{:S(2)}) copy-start(bf16[256,1024]{1,0:T(8,128)(2,1)S(1)} %collective-permute-done.6.refs_2_) | copy-start | bytes 1572868
  52.7 19.4 %copy-start.9 = (bf16[256,1024]{1,0:T(8,128)(2,1)}, bf16[256,1024]{1,0:T(8,128)(2,1)S(1)}, u32[]{:S(2)}) copy-start(bf16[256,1024]{1,0:T(8,128)(2,1)S(1)} %collective-permute-done.7.refs_3_) | copy-start | bytes 1572868
  54.2 29.4 %collective-permute-start.12 = (bf16[256,1024]{1,0:T(8,128)(2,1)}, bf16[256,1024]{1,0:T(8,128)(2,1)S(1)}, u32[]{:S(2)}, u32[]{:S(2)}) collective-permute-start(bf16[256,1024]{1,0:T(8,128)(2,1)} %broadcast_select_fusion.1), channel_id=1, source_target_pairs={{0,1},{1,0},{2,3},{3,2},{4,5},{5,4},{6,7},{7,6},{8,9},{9,8},{10,11... | collective-permute-start | bytes 1572872 | tf_op jit(solution)/shard_map/ppermute | solution.py:66
  58.4 13.7 %copy-start.10 = (bf16[256,1024]{1,0:T(8,128)(2,1)}, bf16[256,1024]{1,0:T(8,128)(2,1)S(1)}, u32[]{:S(2)}) copy-start(bf16[256,1024]{1,0:T(8,128)(2,1)S(1)} %collective-permute-done.8.refs_1_) | copy-start | bytes 1572868
  59.8 23.9 %collective-permute-start.11 = (bf16[256,1024]{1,0:T(8,128)(2,1)}, bf16[256,1024]{1,0:T(8,128)(2,1)S(1)}, u32[]{:S(2)}, u32[]{:S(2)}) collective-permute-start(bf16[256,1024]{1,0:T(8,128)(2,1)} %broadcast_select_fusion.3), channel_id=1, source_target_pairs={{0,1},{1,0},{2,3},{3,2},{4,5},{5,4},{6,7},{7,6},{8,9},{9,8},{10,11... | collective-permute-start | bytes 1572872 | tf_op jit(solution)/shard_map/ppermute | solution.py:66
  72.1 8.3 %collective-permute-start.16 = (bf16[128,1024]{1,0:T(8,128)(2,1)S(1)}, bf16[128,1024]{1,0:T(8,128)(2,1)S(1)}, u32[]{:S(2)}, u32[]{:S(2)}) collective-permute-start(bf16[128,1024]{1,0:T(8,128)(2,1)S(1)} %slice.245), channel_id=1, source_target_pairs={{0,2},{4,0},{8,4},{12,8},{14,12},{10,14},{6,10},{2,6},{1,3},{5,1},... | collective-permute-start | bytes 786440 | tf_op jit(solution)/shard_map/ppermute | solution.py:62
  72.6 9.3 %collective-permute-start.15 = (bf16[128,1024]{1,0:T(8,128)(2,1)S(1)}, bf16[128,1024]{1,0:T(8,128)(2,1)S(1)}, u32[]{:S(2)}, u32[]{:S(2)}) collective-permute-start(bf16[128,1024]{1,0:T(8,128)(2,1)S(1)} %slice.244), channel_id=1, source_target_pairs={{0,4},{4,8},{8,12},{12,14},{14,10},{10,6},{6,2},{2,0},{1,5},{5,9},... | collective-permute-start | bytes 786440 | tf_op jit(solution)/shard_map/ppermute | solution.py:62
  74.7 97.8 %copy-start.4 = (bf16[256,1024]{1,0:T(8,128)(2,1)}, bf16[256,1024]{1,0:T(8,128)(2,1)S(1)}, u32[]{:S(2)}) copy-start(bf16[256,1024]{1,0:T(8,128)(2,1)S(1)} %multiply_convert_fusion.refs_0_) | copy-start | bytes 1572868
  80.4 23.8 %collective-permute-start.9 = (bf16[256,1024]{1,0:T(8,128)(2,1)S(1)}, bf16[256,1024]{1,0:T(8,128)(2,1)S(1)}, u32[]{:S(2)}, u32[]{:S(2)}) collective-permute-start(bf16[256,1024]{1,0:T(8,128)(2,1)S(1)} %multiply_convert_fusion.refs_0_), channel_id=1, source_target_pairs={{0,4},{4,8},{8,12},{12,14},{14,10},{10,6},{6,2},{2,0},{1,5},{5,9},... | collective-permute-start | bytes 1572872 | tf_op jit(solution)/shard_map/ppermute | solution.py:62
  81.9 22.3 %collective-permute-start.10 = (bf16[256,1024]{1,0:T(8,128)(2,1)S(1)}, bf16[256,1024]{1,0:T(8,128)(2,1)S(1)}, u32[]{:S(2)}, u32[]{:S(2)}) collective-permute-start(bf16[256,1024]{1,0:T(8,128)(2,1)S(1)} %multiply_convert_fusion.refs_0_), channel_id=1, source_target_pairs={{0,2},{4,0},{8,4},{12,8},{14,12},{10,14},{6,10},{2,6},{1,3},{5,1},... | collective-permute-start | bytes 1572872 | tf_op jit(solution)/shard_map/ppermute | solution.py:62
  83.6 20.6 %collective-permute-start.17 = (bf16[256,1024]{1,0:T(8,128)(2,1)S(1)}, bf16[256,1024]{1,0:T(8,128)(2,1)S(1)}, u32[]{:S(2)}, u32[]{:S(2)}) collective-permute-start(bf16[256,1024]{1,0:T(8,128)(2,1)S(1)} %maximum_select_fusion), channel_id=1, source_target_pairs={{0,1},{1,0},{2,3},{3,2},{4,5},{5,4},{6,7},{7,6},{8,9},{9,8},{10,11... | collective-permute-start | bytes 1572872 | tf_op jit(solution)/shard_map/ppermute | solution.py:66
  104.2 46.4 %copy-start.11 = (bf16[256,1024]{1,0:T(8,128)(2,1)}, bf16[256,1024]{1,0:T(8,128)(2,1)S(1)}, u32[]{:S(2)}) copy-start(bf16[256,1024]{1,0:T(8,128)(2,1)S(1)} %collective-permute-done.9.refs_3_) | copy-start | bytes 1572868
  104.2 42.8 %copy-start.12 = (bf16[256,1024]{1,0:T(8,128)(2,1)}, bf16[256,1024]{1,0:T(8,128)(2,1)S(1)}, u32[]{:S(2)}) copy-start(bf16[256,1024]{1,0:T(8,128)(2,1)S(1)} %collective-permute-done.10.refs_7_) | copy-start | bytes 1572868
  118.6 32.7 %collective-permute-start.20 = (bf16[2,256,2048]{2,1,0:T(8,128)(2,1)}, bf16[2,256,2048]{2,1,0:T(8,128)(2,1)S(1)}, u32[]{:S(2)}, u32[]{:S(2)}) collective-permute-start(bf16[2,256,2048]{2,1,0:T(8,128)(2,1)} %get-tuple-element.127), channel_id=1, source_target_pairs={{0,1},{1,0},{2,3},{3,2},{4,5},{5,4},{6,7},{7,6},{8,9},{9,8},{10,11... | collective-permute-start | bytes 6291464 | tf_op jit(solution)/shard_map/ppermute | solution.py:66
  119.1 13.9 %collective-permute-start.13 = (bf16[256,1024]{1,0:T(8,128)(2,1)S(1)}, bf16[256,1024]{1,0:T(8,128)(2,1)S(1)}, u32[]{:S(2)}, u32[]{:S(2)}) collective-permute-start(bf16[256,1024]{1,0:T(8,128)(2,1)S(1)} %collective-permute-done.9.refs_3_), channel_id=1, source_target_pairs={{0,4},{4,8},{8,12},{12,14},{14,10},{10,6},{6,2},{2,0},{1,5},{5,9},... | collective-permute-start | bytes 1572872 | tf_op jit(solution)/shard_map/ppermute | solution.py:62
  120.6 13.7 %collective-permute-start.14 = (bf16[256,1024]{1,0:T(8,128)(2,1)S(1)}, bf16[256,1024]{1,0:T(8,128)(2,1)S(1)}, u32[]{:S(2)}, u32[]{:S(2)}) collective-permute-start(bf16[256,1024]{1,0:T(8,128)(2,1)S(1)} %collective-permute-done.10.refs_7_), channel_id=1, source_target_pairs={{0,2},{4,0},{8,4},{12,8},{14,12},{10,14},{6,10},{2,6},{1,3},{5,1},... | collective-permute-start | bytes 1572872 | tf_op jit(solution)/shard_map/ppermute | solution.py:62
  133.0 18.2 %copy-start.13 = (bf16[256,1024]{1,0:T(8,128)(2,1)}, bf16[256,1024]{1,0:T(8,128)(2,1)S(1)}, u32[]{:S(2)}) copy-start(bf16[256,1024]{1,0:T(8,128)(2,1)S(1)} %collective-permute-done.13.refs_0_) | copy-start | bytes 1572868
  134.3 17.0 %copy-start.14 = (bf16[256,1024]{1,0:T(8,128)(2,1)}, bf16[256,1024]{1,0:T(8,128)(2,1)S(1)}, u32[]{:S(2)}) copy-start(bf16[256,1024]{1,0:T(8,128)(2,1)S(1)} %collective-permute-done.14.refs_1_) | copy-start | bytes 1572868
  134.3 12.8 %collective-permute-start.18 = (bf16[256,1024]{1,0:T(8,128)(2,1)S(1)}, bf16[256,1024]{1,0:T(8,128)(2,1)S(1)}, u32[]{:S(2)}, u32[]{:S(2)}) collective-permute-start(bf16[256,1024]{1,0:T(8,128)(2,1)S(1)} %collective-permute-done.13.refs_0_), channel_id=1, source_target_pairs={{0,4},{4,8},{8,12},{12,14},{14,10},{10,6},{6,2},{2,0},{1,5},{5,9},... | collective-permute-start | bytes 1572872 | tf_op jit(solution)/shard_map/ppermute | solution.py:62
  136.3 15.0 %copy-start = (f32[2,256,2048]{2,1,0:T(8,128)S(1)}, f32[2,256,2048]{2,1,0:T(8,128)}, u32[]{:S(2)}) copy-start(f32[2,256,2048]{2,1,0:T(8,128)} %get-tuple-element.129.refs_0_) | copy-start | bytes 12582916
  136.3 15.0 %copy-start.2 = (f32[256,128]{1,0:T(8,128)S(1)}, f32[256,128]{1,0:T(8,128)}, u32[]{:S(2)}) copy-start(f32[256,128]{1,0:T(8,128)} %get-tuple-element.130.refs_1_) | copy-start | bytes 393220
  136.3 15.0 %collective-permute-start.21 = (f32[256,128]{1,0:T(8,128)}, f32[256,128]{1,0:T(8,128)S(1)}, u32[]{:S(2)}, u32[]{:S(2)}) collective-permute-start(f32[256,128]{1,0:T(8,128)} %get-tuple-element.128), channel_id=1, source_target_pairs={{0,1},{1,0},{2,3},{3,2},{4,5},{5,4},{6,7},{7,6},{8,9},{9,8},{10,11... | collective-permute-start | bytes 393224 | tf_op jit(solution)/shard_map/ppermute | solution.py:66
  136.3 14.3 %collective-permute-start.19 = (bf16[256,1024]{1,0:T(8,128)(2,1)S(1)}, bf16[256,1024]{1,0:T(8,128)(2,1)S(1)}, u32[]{:S(2)}, u32[]{:S(2)}) collective-permute-start(bf16[256,1024]{1,0:T(8,128)(2,1)S(1)} %collective-permute-done.14.refs_1_), channel_id=1, source_target_pairs={{0,2},{4,0},{8,4},{12,8},{14,12},{10,14},{6,10},{2,6},{1,3},{5,1},... | collective-permute-start | bytes 1572872 | tf_op jit(solution)/shard_map/ppermute | solution.py:62
  147.1 11.2 %copy-start.7 = (bf16[256,1024]{1,0:T(8,128)(2,1)}, bf16[256,1024]{1,0:T(8,128)(2,1)S(1)}, u32[]{:S(2)}) copy-start(bf16[256,1024]{1,0:T(8,128)(2,1)S(1)} %collective-permute-done.18.refs_6_) | copy-start | bytes 1572868
  147.1 29.7 %collective-permute-start.30 = (bf16[256,1024]{1,0:T(8,128)(2,1)S(1)}, bf16[256,1024]{1,0:T(8,128)(2,1)}, u32[]{:S(2)}, u32[]{:S(2)}) collective-permute-start(bf16[256,1024]{1,0:T(8,128)(2,1)S(1)} %broadcast_select_fusion.4), channel_id=1, source_target_pairs={{0,1},{1,0},{2,3},{3,2},{4,5},{5,4},{6,7},{7,6},{8,9},{9,8},{10,11... | collective-permute-start | bytes 1572872 | tf_op jit(solution)/shard_map/ppermute | solution.py:66
  150.6 7.6 %copy-start.8 = (bf16[256,1024]{1,0:T(8,128)(2,1)}, bf16[256,1024]{1,0:T(8,128)(2,1)S(1)}, u32[]{:S(2)}) copy-start(bf16[256,1024]{1,0:T(8,128)(2,1)S(1)} %collective-permute-done.19.refs_4_) | copy-start | bytes 1572868
  158.3 13.6 %collective-permute-start.24 = (bf16[128,1024]{1,0:T(8,128)(2,1)S(1)}, bf16[128,1024]{1,0:T(8,128)(2,1)S(1)}, u32[]{:S(2)}, u32[]{:S(2)}) collective-permute-start(bf16[128,1024]{1,0:T(8,128)(2,1)S(1)} %slice.248), channel_id=1, source_target_pairs={{0,2},{4,0},{8,4},{12,8},{14,12},{10,14},{6,10},{2,6},{1,3},{5,1},... | collective-permute-start | bytes 786440 | tf_op jit(solution)/shard_map/ppermute | solution.py:62
  159.0 12.9 %collective-permute-start.23 = (bf16[128,1024]{1,0:T(8,128)(2,1)S(1)}, bf16[128,1024]{1,0:T(8,128)(2,1)S(1)}, u32[]{:S(2)}, u32[]{:S(2)}) collective-permute-start(bf16[128,1024]{1,0:T(8,128)(2,1)S(1)} %slice.247), channel_id=1, source_target_pairs={{0,4},{4,8},{8,12},{12,14},{14,10},{10,6},{6,2},{2,0},{1,5},{5,9},... | collective-permute-start | bytes 786440 | tf_op jit(solution)/shard_map/ppermute | solution.py:62
  160.4 13.7 %collective-permute-start.27 = (bf16[128,1024]{1,0:T(8,128)(2,1)S(1)}, bf16[128,1024]{1,0:T(8,128)(2,1)S(1)}, u32[]{:S(2)}, u32[]{:S(2)}) collective-permute-start(bf16[128,1024]{1,0:T(8,128)(2,1)S(1)} %get-tuple-element.193), channel_id=1, source_target_pairs={{0,2},{4,0},{8,4},{12,8},{14,12},{10,14},{6,10},{2,6},{1,3},{5,1},... | collective-permute-start | bytes 786440 | tf_op jit(solution)/shard_map/ppermute | solution.py:62
  161.1 13.1 %collective-permute-start.26 = (bf16[128,1024]{1,0:T(8,128)(2,1)S(1)}, bf16[128,1024]{1,0:T(8,128)(2,1)S(1)}, u32[]{:S(2)}, u32[]{:S(2)}) collective-permute-start(bf16[128,1024]{1,0:T(8,128)(2,1)S(1)} %get-tuple-element.194), channel_id=1, source_target_pairs={{0,4},{4,8},{8,12},{12,14},{14,10},{10,6},{6,2},{2,0},{1,5},{5,9},... | collective-permute-start | bytes 786440 | tf_op jit(solution)/shard_map/ppermute | solution.py:62
  171.9 5.5 %collective-permute-start.32 = (bf16[256,1024]{1,0:T(8,128)(2,1)S(1)}, bf16[256,1024]{1,0:T(8,128)(2,1)S(1)}, u32[]{:S(2)}, u32[]{:S(2)}) collective-permute-start(bf16[256,1024]{1,0:T(8,128)(2,1)S(1)} %broadcast_select_fusion), channel_id=1, source_target_pairs={{0,1},{1,0},{2,3},{3,2},{4,5},{5,4},{6,7},{7,6},{8,9},{9,8},{10,11... | collective-permute-start | bytes 1572872 | tf_op jit(solution)/shard_map/ppermute | solution.py:66
  172.0 5.4 %collective-permute-start.31 = (bf16[256,1024]{1,0:T(8,128)(2,1)S(1)}, bf16[256,1024]{1,0:T(8,128)(2,1)S(1)}, u32[]{:S(2)}, u32[]{:S(2)}) collective-permute-start(bf16[256,1024]{1,0:T(8,128)(2,1)S(1)} %broadcast_select_fusion.2), channel_id=1, source_target_pairs={{0,1},{1,0},{2,3},{3,2},{4,5},{5,4},{6,7},{7,6},{8,9},{9,8},{10,11... | collective-permute-start | bytes 1572872 | tf_op jit(solution)/shard_map/ppermute | solution.py:66
  174.1 27.6 %collective-permute-start.25 = (bf16[256,1024]{1,0:T(8,128)(2,1)}, bf16[256,1024]{1,0:T(8,128)(2,1)S(1)}, u32[]{:S(2)}, u32[]{:S(2)}) collective-permute-start(bf16[256,1024]{1,0:T(8,128)(2,1)} %maximum_select_fusion.1), channel_id=1, source_target_pairs={{0,1},{1,0},{2,3},{3,2},{4,5},{5,4},{6,7},{7,6},{8,9},{9,8},{10,11... | collective-permute-start | bytes 1572872 | tf_op jit(solution)/shard_map/ppermute | solution.py:66
  175.3 26.5 %collective-permute-start.28 = (bf16[256,1024]{1,0:T(8,128)(2,1)}, bf16[256,1024]{1,0:T(8,128)(2,1)}, u32[]{:S(2)}, u32[]{:S(2)}) collective-permute-start(bf16[256,1024]{1,0:T(8,128)(2,1)} %pad_maximum_fusion.2), channel_id=1, source_target_pairs={{0,4},{4,8},{8,12},{12,14},{14,10},{10,6},{6,2},{2,0},{1,5},{5,9},... | collective-permute-start | bytes 1572872 | tf_op jit(solution)/shard_map/ppermute | solution.py:62
  176.7 25.0 %collective-permute-start.29 = (bf16[256,1024]{1,0:T(8,128)(2,1)S(1)}, bf16[256,1024]{1,0:T(8,128)(2,1)S(1)}, u32[]{:S(2)}, u32[]{:S(2)}) collective-permute-start(bf16[256,1024]{1,0:T(8,128)(2,1)S(1)} %pad_maximum_fusion.3), channel_id=1, source_target_pairs={{0,2},{4,0},{8,4},{12,8},{14,12},{10,14},{6,10},{2,6},{1,3},{5,1},... | collective-permute-start | bytes 1572872 | tf_op jit(solution)/shard_map/ppermute | solution.py:62
  215.9 3.6 %copy-start.28 = (f32[256,128]{1,0:T(8,128)S(1)}, f32[256,128]{1,0:T(8,128)}, u32[]{:S(2)}) copy-start(f32[256,128]{1,0:T(8,128)} %get-tuple-element.158) | copy-start | bytes 393220
  215.9 16.3 %copy-start.3 = (f32[256,128]{1,0:T(8,128)S(1)}, f32[256,128]{1,0:T(8,128)}, u32[]{:S(2)}) copy-start(f32[256,128]{1,0:T(8,128)} %get-tuple-element.162.refs_1_) | copy-start | bytes 393220
  215.9 16.3 %collective-permute-start.33 = (bf16[2,256,2048]{2,1,0:T(8,128)(2,1)}, bf16[2,256,2048]{2,1,0:T(8,128)(2,1)S(1)}, u32[]{:S(2)}, u32[]{:S(2)}) collective-permute-start(bf16[2,256,2048]{2,1,0:T(8,128)(2,1)} %get-tuple-element.157), channel_id=1, source_target_pairs={{0,1},{1,0},{2,3},{3,2},{4,5},{5,4},{6,7},{7,6},{8,9},{9,8},{10,11... | collective-permute-start | bytes 6291464 | tf_op jit(solution)/shard_map/ppermute | solution.py:66
  217.4 14.3 %collective-permute-start.36 = (bf16[256,1024]{1,0:T(8,128)(2,1)S(1)}, bf16[256,1024]{1,0:T(8,128)(2,1)S(1)}, u32[]{:S(2)}, u32[]{:S(2)}) collective-permute-start(bf16[256,1024]{1,0:T(8,128)(2,1)S(1)} %get-tuple-element.181), channel_id=1, source_target_pairs={{0,2},{4,0},{8,4},{12,8},{14,12},{10,14},{6,10},{2,6},{1,3},{5,1},... | collective-permute-start | bytes 1572872 | tf_op jit(solution)/shard_map/ppermute | solution.py:62
  218.2 14.0 %collective-permute-start.35 = (bf16[256,1024]{1,0:T(8,128)(2,1)S(1)}, bf16[256,1024]{1,0:T(8,128)(2,1)S(1)}, u32[]{:S(2)}, u32[]{:S(2)}) collective-permute-start(bf16[256,1024]{1,0:T(8,128)(2,1)S(1)} %get-tuple-element.182), channel_id=1, source_target_pairs={{0,4},{4,8},{8,12},{12,14},{14,10},{10,6},{6,2},{2,0},{1,5},{5,9},... | collective-permute-start | bytes 1572872 | tf_op jit(solution)/shard_map/ppermute | solution.py:62
  219.5 1.3 collective-permute-start.34
  241.3 7.6 %collective-permute-start.38 = (bf16[128,1024]{1,0:T(8,128)(2,1)S(1)}, bf16[128,1024]{1,0:T(8,128)(2,1)S(1)}, u32[]{:S(2)}, u32[]{:S(2)}) collective-permute-start(bf16[128,1024]{1,0:T(8,128)(2,1)S(1)} %get-tuple-element.187), channel_id=1, source_target_pairs={{0,2},{4,0},{8,4},{12,8},{14,12},{10,14},{6,10},{2,6},{1,3},{5,1},... | collective-permute-start | bytes 786440 | tf_op jit(solution)/shard_map/ppermute | solution.py:62
  241.9 7.4 %collective-permute-start.37 = (bf16[128,1024]{1,0:T(8,128)(2,1)S(1)}, bf16[128,1024]{1,0:T(8,128)(2,1)S(1)}, u32[]{:S(2)}, u32[]{:S(2)}) collective-permute-start(bf16[128,1024]{1,0:T(8,128)(2,1)S(1)} %get-tuple-element.188), channel_id=1, source_target_pairs={{0,4},{4,8},{8,12},{12,14},{14,10},{10,6},{6,2},{2,0},{1,5},{5,9},... | collective-permute-start | bytes 786440 | tf_op jit(solution)/shard_map/ppermute | solution.py:62
  249.5 12.1 %collective-permute-start.39 = (bf16[256,1024]{1,0:T(8,128)(2,1)S(1)}, bf16[256,1024]{1,0:T(8,128)(2,1)S(1)}, u32[]{:S(2)}, u32[]{:S(2)}) collective-permute-start(bf16[256,1024]{1,0:T(8,128)(2,1)S(1)} %pad_maximum_fusion.4), channel_id=1, source_target_pairs={{0,4},{4,8},{8,12},{12,14},{14,10},{10,6},{6,2},{2,0},{1,5},{5,9},... | collective-permute-start | bytes 1572872 | tf_op jit(solution)/shard_map/ppermute | solution.py:62
  250.9 11.7 %collective-permute-start.40 = (bf16[256,1024]{1,0:T(8,128)(2,1)S(1)}, bf16[256,1024]{1,0:T(8,128)(2,1)S(1)}, u32[]{:S(2)}, u32[]{:S(2)}) collective-permute-start(bf16[256,1024]{1,0:T(8,128)(2,1)S(1)} %pad_maximum_fusion.5), channel_id=1, source_target_pairs={{0,2},{4,0},{8,4},{12,8},{14,12},{10,14},{6,10},{2,6},{1,3},{5,1},... | collective-permute-start | bytes 1572872 | tf_op jit(solution)/shard_map/ppermute | solution.py:62
  263.1 14.9 %collective-permute-start.42 = (bf16[256,1024]{1,0:T(8,128)(2,1)S(1)}, bf16[256,1024]{1,0:T(8,128)(2,1)S(1)}, u32[]{:S(2)}, u32[]{:S(2)}) collective-permute-start(bf16[256,1024]{1,0:T(8,128)(2,1)S(1)} %get-tuple-element.177), channel_id=1, source_target_pairs={{0,2},{4,0},{8,4},{12,8},{14,12},{10,14},{6,10},{2,6},{1,3},{5,1},... | collective-permute-start | bytes 1572872 | tf_op jit(solution)/shard_map/ppermute | solution.py:62
  263.9 14.9 %collective-permute-start.41 = (bf16[256,1024]{1,0:T(8,128)(2,1)S(1)}, bf16[256,1024]{1,0:T(8,128)(2,1)S(1)}, u32[]{:S(2)}, u32[]{:S(2)}) collective-permute-start(bf16[256,1024]{1,0:T(8,128)(2,1)S(1)} %get-tuple-element.178), channel_id=1, source_target_pairs={{0,4},{4,8},{8,12},{12,14},{14,10},{10,6},{6,2},{2,0},{1,5},{5,9},... | collective-permute-start | bytes 1572872 | tf_op jit(solution)/shard_map/ppermute | solution.py:62
  265.6 24.4 %collective-permute-start.45 = (bf16[256,1024]{1,0:T(8,128)(2,1)S(1)}, bf16[256,1024]{1,0:T(8,128)(2,1)S(1)}, u32[]{:S(2)}, u32[]{:S(2)}) collective-permute-start(bf16[256,1024]{1,0:T(8,128)(2,1)S(1)} %get-tuple-element.179), channel_id=1, source_target_pairs={{0,4},{4,8},{8,12},{12,14},{14,10},{10,6},{6,2},{2,0},{1,5},{5,9},... | collective-permute-start | bytes 1572872 | tf_op jit(solution)/shard_map/ppermute | solution.py:62
  267.0 23.0 %collective-permute-start.46 = (bf16[256,1024]{1,0:T(8,128)(2,1)S(1)}, bf16[256,1024]{1,0:T(8,128)(2,1)S(1)}, u32[]{:S(2)}, u32[]{:S(2)}) collective-permute-start(bf16[256,1024]{1,0:T(8,128)(2,1)S(1)} %get-tuple-element.180), channel_id=1, source_target_pairs={{0,2},{4,0},{8,4},{12,8},{14,12},{10,14},{6,10},{2,6},{1,3},{5,1},... | collective-permute-start | bytes 1572872 | tf_op jit(solution)/shard_map/ppermute | solution.py:62
  279.2 17.8 %collective-permute-start.43 = (bf16[256,1024]{1,0:T(8,128)(2,1)S(1)}, bf16[256,1024]{1,0:T(8,128)(2,1)S(1)}, u32[]{:S(2)}, u32[]{:S(2)}) collective-permute-start(bf16[256,1024]{1,0:T(8,128)(2,1)S(1)} %get-tuple-element.175), channel_id=1, source_target_pairs={{0,4},{4,8},{8,12},{12,14},{14,10},{10,6},{6,2},{2,0},{1,5},{5,9},... | collective-permute-start | bytes 1572872 | tf_op jit(solution)/shard_map/ppermute | solution.py:62
  280.5 16.4 %collective-permute-start.44 = (bf16[256,1024]{1,0:T(8,128)(2,1)S(1)}, bf16[256,1024]{1,0:T(8,128)(2,1)S(1)}, u32[]{:S(2)}, u32[]{:S(2)}) collective-permute-start(bf16[256,1024]{1,0:T(8,128)(2,1)S(1)} %get-tuple-element.176), channel_id=1, source_target_pairs={{0,2},{4,0},{8,4},{12,8},{14,12},{10,14},{6,10},{2,6},{1,3},{5,1},... | collective-permute-start | bytes 1572872 | tf_op jit(solution)/shard_map/ppermute | solution.py:62
  (12 other events, 21.5 us)

commit v4 on v3

v4 whole, which is shorter than its diff:
```python
import functools

import jax
import jax.numpy as jnp
import numpy as np
from jax import lax
from jax.experimental import pallas as pl
from jax.experimental.pallas import tpu as pltpu
from jax.sharding import PartitionSpec as P

VMEM_LIMIT = 26 * 1024 * 1024
DEEP, PARTS = 3, 4
LANES = 128


def ring_of(count):
    if count == 8:
        return [0, 2, 4, 6, 7, 5, 3, 1]
    return list(range(count))


def send_order(count):
    half = count // 2
    order = [half]
    for step in range(half - 1, 0, -1):
        order += [step, count - step]
    return order + [0]


def tables_of(count):
    ring = ring_of(count)
    place = {block: index for index, block in enumerate(ring)}
    half = count // 2
    order = send_order(count)
    pairs = np.zeros((count, 2, 3, half), np.int32)
    tiles = np.zeros((count, 2, 2, count), np.int32)
    for block in range(count):
        own = place[block]
        for core in range(2):
            for index in range(half):
                first = ring[(own - index) % count]
                second = ring[(own + half - index) % count]
                mine = first // half == core
                kept = first if mine else second
                pairs[block, core, :, index] = mine, kept % half, kept
            for index, distance in enumerate(order):
                target = ring[(own + distance) % count]
                tiles[block, core, :, index] = target // half == core, target % half
    return pairs, tiles


def ring_shift(value, steps):
    ring = ring_of(lax.axis_size("blk"))
    count = len(ring)
    return lax.ppermute(value, "blk", [(ring[i], ring[(i + steps) % count]) for i in range(count)])


def swap(value):
    return lax.ppermute(value, "seq", [(0, 1), (1, 0)])


def after(value, *earlier):
    return lax.optimization_barrier((value, earlier))[0]


def gate_up_kernel(group, shape_of, final, rows, width, steps, pairs_ref, *refs):
    refs = list(refs)
    stacked, weights, sems, weight_sems = refs[-4:]
    pieces = [[[refs.pop(0) for _ in side] for side in sides] for sides in shape_of]
    gains_ref, gate_ref, up_ref = refs.pop(0), refs.pop(0), refs.pop(0)
    sofar_ref, sofar_stat = (None, None) if len(refs) == (8 if final else 6) else (refs.pop(0), refs.pop(0))
    outs = refs[:-4]
    step = pl.program_id(0)
    tile = weights.shape[-1]

    def fetch(number, act):
        slot = lax.rem(number, DEEP)
        column = pl.multiple_of(number * tile, tile)
        for which, source in enumerate((gate_ref, up_ref)):
            for place, index in enumerate(group):
                row = pl.multiple_of(pairs_ref[1, index] * width, width)
                act(
                    pltpu.make_async_copy(
                        source.at[pl.ds(row, width), pl.ds(column, tile)],
                        weights.at[slot, which, pl.ds(place * width, width)],
                        weight_sems.at[slot, which, place],
                    )
                )

    def gather_pieces(act):
        for place, index in enumerate(group):
            for side, wanted in ((0, 1), (1, 0)):

                @pl.when(pairs_ref[0, index] == wanted)
                def chosen(place=place, side=side):
                    row = 0
                    for number, source in enumerate(pieces[place][side]):
                        size = source.shape[0]
                        target = stacked.at[pl.ds(row, size), pl.ds(place * width, width)]
                        act(pltpu.make_async_copy(source, target, sems.at[place, number]))
                        row += size

    @pl.when(step == 0)
    def first():
        gather_pieces(lambda copy: copy.start())
        for number in range(min(DEEP - 1, steps)):
            fetch(number, lambda copy: copy.start())
        gather_pieces(lambda copy: copy.wait())
        stat = jnp.zeros((2 * rows, LANES), jnp.float32) if sofar_stat is None else sofar_stat[...]
        for place, index in enumerate(group):
            gain = gains_ref[pairs_ref[2, index]]
            weight = 1.0 / (gain * gain)
            for column in range(0, width, LANES):
                value = stacked[:, place * width + column : place * width + column + LANES].astype(jnp.float32)
                stat = stat + value * value * weight[:, column : column + LANES]
        if final:
            outs[1][...] = stat[:rows]
            outs[3][...] = stat[rows:]
        else:
            outs[1][...] = stat

    @pl.when(step + DEEP - 1 < steps)
    def ahead():
        fetch(step + DEEP - 1, lambda copy: copy.start())

    fetch(step, lambda copy: copy.wait())
    slot = lax.rem(step, DEEP)
    for which in range(2):
        total = jnp.dot(stacked[...], weights[slot, which], preferred_element_type=jnp.float32)
        if sofar_ref is not None:
            total = total + sofar_ref[which]
        if final:
            outs[0][which] = total[:rows]
            outs[2][which] = total[rows:].astype(jnp.bfloat16)
        else:
            outs[0][which] = total


def gate_up(group, final, pairs, pieces, gains, gate_weight, up_weight, sofar):
    rows, width = sum(part.shape[0] for part in pieces[0][0]) // 2, pieces[0][0][0].shape[1]
    columns = gate_weight.shape[1]
    tile = min(256, columns)
    anywhere = pl.BlockSpec(memory_space=pl.ANY)
    operands = [part for sides in pieces for side in sides for part in side]
    in_specs = [anywhere] * len(operands) + [pl.BlockSpec(gains.shape, lambda n, pairs: (0, 0, 0)), anywhere, anywhere]
    operands += [gains, gate_weight, up_weight]

    def tiled(*lead):
        return pl.BlockSpec((*lead, tile), lambda n, pairs: (0,) * len(lead) + (n,))

    def whole(height):
        return pl.BlockSpec((height, LANES), lambda n, pairs: (0, 0))

    if sofar is not None:
        operands += sofar
        in_specs += [tiled(2, 2 * rows), whole(2 * rows)]
    if final:
        out_shape = (
            jax.ShapeDtypeStruct((2, rows, columns), jnp.float32),
            jax.ShapeDtypeStruct((rows, LANES), jnp.float32),
            jax.ShapeDtypeStruct((2, rows, columns), jnp.bfloat16),
            jax.ShapeDtypeStruct((rows, LANES), jnp.float32),
        )
        out_specs = (tiled(2, rows), whole(rows), tiled(2, rows), whole(rows))
    else:
        out_shape = (
            jax.ShapeDtypeStruct((2, 2 * rows, columns), jnp.float32),
            jax.ShapeDtypeStruct((2 * rows, LANES), jnp.float32),
        )
        out_specs = (tiled(2, 2 * rows), whole(2 * rows))
    shape_of = [[[None] * len(side) for side in sides] for sides in pieces]
    most = max(len(side) for sides in pieces for side in sides)
    return pl.pallas_call(
        functools.partial(gate_up_kernel, group, shape_of, final, rows, width, columns // tile),
        out_shape=out_shape,
        grid_spec=pltpu.PrefetchScalarGridSpec(
            num_scalar_prefetch=1,
            grid=(columns // tile,),
            in_specs=in_specs,
            out_specs=out_specs,
            scratch_shapes=[
                pltpu.VMEM((2 * rows, len(group) * width), jnp.bfloat16),
                pltpu.VMEM((DEEP, 2, len(group) * width, tile), jnp.bfloat16),
                pltpu.SemaphoreType.DMA((len(group), most)),
                pltpu.SemaphoreType.DMA((DEEP, 2, len(group))),
            ],
        ),
        compiler_params=pltpu.CompilerParams(vmem_limit_bytes=VMEM_LIMIT),
        cost_estimate=pl.CostEstimate(
            flops=12 * rows * width * columns * len(group),
            bytes_accessed=4 * width * columns * len(group),
            transcendentals=0,
        ),
        name="gate_up",
    )(pairs, *operands)


def down_kernel(start, stop, split, mean_of, tiles_ref, *refs):
    refs = list(refs)
    buffer, sems = refs.pop(), refs.pop()
    if start == 0:
        own_ref, own_stat, received_ref, received_stat, local_ref, other_ref, out_ref, hidden = refs
    else:
        hidden, local_ref, other_ref, out_ref = refs
    step, steps = pl.program_id(0) * split + pl.program_id(1), (stop - start) * split
    depth, tile = buffer.shape[1:]

    def fetch(number, act):
        slot = lax.rem(number, DEEP)
        block = start + lax.div(number, split)
        for kind, source in ((1, local_ref), (0, other_ref)):

            @pl.when(tiles_ref[0, block] == kind)
            def chosen(source=source):
                column = pl.multiple_of((tiles_ref[1, block] * split + lax.rem(number, split)) * tile, tile)
                for part in range(PARTS):
                    row = pl.ds(part * (depth // PARTS), depth // PARTS)
                    act(
                        pltpu.make_async_copy(
                            source.at[row, pl.ds(column, tile)], buffer.at[slot, row], sems.at[slot, part]
                        )
                    )

    @pl.when(step == 0)
    def first():
        for number in range(min(DEEP - 1, steps)):
            fetch(jnp.int32(number), lambda copy: copy.start())
        if start == 0:
            total = jnp.sum(own_stat[...] + received_stat[...], axis=1, keepdims=True)
            inv = lax.rsqrt(total / mean_of + 1e-05)
            gate = (own_ref[0] + received_ref[0].astype(jnp.float32)) * inv
            up = (own_ref[1] + received_ref[1].astype(jnp.float32)) * inv
            hidden[...] = (gate / (1.0 + jnp.exp(-gate)) * up).astype(jnp.bfloat16)

    @pl.when(step + DEEP - 1 < steps)
    def ahead():
        fetch(step + DEEP - 1, lambda copy: copy.start())

    fetch(step, lambda copy: copy.wait())
    weight = buffer[lax.rem(step, DEEP)]
    out_ref[0] = jnp.dot(hidden[...], weight, preferred_element_type=jnp.float32).astype(jnp.bfloat16)


def down(start, stop, tiles, operands, local, other, width):
    rows, depth = operands[0].shape[-2:]
    tile = min(512, width)
    split = width // tile

    def whole(value):
        return pl.BlockSpec(value.shape, lambda j, t, tiles: (0,) * value.ndim)

    anywhere = pl.BlockSpec(memory_space=pl.ANY)
    out_shape = [jax.ShapeDtypeStruct((stop - start, rows, width), jnp.bfloat16)]
    out_specs = [pl.BlockSpec((1, rows, tile), lambda j, t, tiles: (j, 0, t))]
    if start == 0:
        out_shape.append(jax.ShapeDtypeStruct((rows, depth), jnp.bfloat16))
        out_specs.append(pl.BlockSpec((rows, depth), lambda j, t, tiles: (0, 0)))
    return pl.pallas_call(
        functools.partial(down_kernel, start, stop, split, width * tiles.shape[1]),
        out_shape=out_shape,
        grid_spec=pltpu.PrefetchScalarGridSpec(
            num_scalar_prefetch=1,
            grid=(stop - start, split),
            in_specs=[*map(whole, operands), anywhere, anywhere],
            out_specs=out_specs,
            scratch_shapes=[
                pltpu.SemaphoreType.DMA((DEEP, PARTS)),
                pltpu.VMEM((DEEP, depth, tile), jnp.bfloat16),
            ],
        ),
        compiler_params=pltpu.CompilerParams(vmem_limit_bytes=VMEM_LIMIT),
        cost_estimate=pl.CostEstimate(
            flops=4 * rows * depth * width * (stop - start),
            bytes_accessed=2 * depth * width * (stop - start),
            transcendentals=rows * depth,
        ),
        name="down",
    )(tiles, *operands, local, other)


def carry(value, step, way, crossing=False):
    ring = ring_of(lax.axis_size("blk"))
    count = len(ring)
    route = []
    for q in range(count):
        core = ring[(q - way * (step - 1)) % count] // (count // 2)
        source = 1 - core if crossing else core
        route.append((2 * ring[q] + source, 2 * ring[(q + way) % count] + core))
    return lax.ppermute(value, ("blk", "seq"), route)


def gather_step(block, steps, half, crossing, *earlier):
    before, behind = after(steps[-1] if steps else (block, block), *earlier)
    if len(steps) == half - 1:
        cut = block.shape[0] // 2
        before, behind = before[:cut], behind[cut:]
    step = len(steps) + 1
    crossing = crossing and step == 1
    return [*steps, (carry(before, step, 1, crossing), carry(behind, step, -1, crossing))]


def pair_pieces(index, half, own, streams):
    if index:
        return [[steps[index - 1][0] for steps in streams], [steps[half - index - 1][1] for steps in streams]]
    return [list(own), [part for steps in streams for part in steps[half - 1]]]


def joined(one, two):
    return (one.astype(jnp.float32) + two.astype(jnp.float32)).astype(jnp.bfloat16)


def scatter_sums(moved, term, count, distance, *earlier):
    half = count // 2
    ahead, behind = term(distance), term(count - distance)
    cut = ahead.shape[0] // 2
    if distance == half:
        return after((ahead[:cut], behind[cut:]), *earlier)
    forth, back = after(moved, *earlier)
    if distance == half - 1:
        forth = jnp.concatenate([joined(ahead[:cut], forth), ahead[cut:]], axis=0)
        back = jnp.concatenate([behind[:cut], joined(behind[cut:], back)], axis=0)
        return forth, back
    return joined(ahead, forth), joined(behind, back)


def scatter_send(sums):
    return ring_shift(sums[0], 1), ring_shift(sums[1], -1)


def on_device(
    noisy_input,
    self_cond,
    cond_gain,
    bucket,
    conv_taps,
    norm_gain,
    gate_weight,
    up_weight,
    down_weight,
):
    row_count, width = noisy_input.shape
    count = lax.axis_size("blk")
    half = count // 2
    core, own = lax.axis_index("seq"), lax.axis_index("blk")
    pair_table, tile_table = tables_of(count)
    pairs = jnp.asarray(pair_table)[own, core]
    tiles = jnp.asarray(tile_table)[own, core]
    order = send_order(count)
    gains = norm_gain.reshape(count, 1, width)

    lead_rows = conv_taps.shape[1] - 1
    edges = lax.ppermute(
        (noisy_input[row_count - lead_rows :], self_cond[row_count - lead_rows :]), "seq", [(0, 1)]
    )
    other_down = swap(down_weight)
    chosen = lax.dynamic_index_in_dim(conv_taps, bucket[0], 0, keepdims=False)
    own_gain = lax.dynamic_slice_in_dim(norm_gain, own * width, width, 0)

    def mix(noisy, cond):
        return noisy.astype(jnp.float32) + cond_gain * cond.astype(jnp.float32)

    def convolve(noisy, cond, edge, start, size):
        if start == 0:
            extended = jnp.concatenate([mix(*edge), mix(noisy[:size], cond[:size])], axis=0)
        else:
            where = slice(start - lead_rows, start + size)
            extended = mix(noisy[where], cond[where])
        result = jnp.zeros((size, width), jnp.float32)
        for shift_by in range(lead_rows + 1):
            result = result + chosen[shift_by] * lax.slice_in_dim(
                extended, lead_rows - shift_by, lead_rows - shift_by + size, axis=0
            )
        return (result.astype(jnp.bfloat16).astype(jnp.float32) * own_gain).astype(jnp.bfloat16)

    size = row_count // 2
    early = min(3, count - 1)
    near = [2, 1, 3] if half == 4 else list(range(1, half))

    def matmul(group, own, streams, sofar, *earlier):
        pieces = after([pair_pieces(index, half, own, streams) for index in group], *earlier)
        return gate_up(group, sofar is not None, pairs, pieces, gains, gate_weight, up_weight, sofar)

    def open_down(sums, *earlier):
        own_sum, own_stat, sent, sent_stat = sums
        received_sum, received_stat = swap(after((sent, sent_stat), *earlier))
        operands = [own_sum, own_stat, received_sum, received_stat]
        return down(0, early, tiles, operands, down_weight, other_down, width)

    def close_down(hidden, *earlier):
        return down(early, count, tiles, [after(hidden, *earlier)], down_weight, other_down, width)[0]

    def term_of(opened, closed, rows=slice(None)):
        def term(distance):
            index = order.index(distance)
            return (opened[index] if index < early else closed[index - early])[rows]

        return term

    block_a = convolve(noisy_input, self_cond, edges, size, size)
    streams_a = [[], []]
    for step in range(half - 1):
        streams_a = [gather_step(block_a, steps, half, bool(number)) for number, steps in enumerate(streams_a)]
        if step == 0:
            own_a = (block_a, swap(block_a))
            later = after((noisy_input, self_cond, edges), [steps[0] for steps in streams_a])
            block_b = convolve(*later, 0, size)
            own_b = (block_b, swap(block_b))
            stack_b = jnp.concatenate(own_b, axis=0)
    thirds = [steps[-1] for steps in streams_a]
    streams_a = [gather_step(block_a, steps, half, False) for steps in streams_a]
    steps_b = gather_step(stack_b, [], half, False, thirds)
    sums_a = matmul(near, own_a, streams_a, None)
    first_b = steps_b[-1]
    steps_b = gather_step(stack_b, steps_b, half, False, sums_a[1], [steps[-1] for steps in streams_a])
    sums_a = matmul([0], own_a, streams_a, sums_a, first_b)
    second_b = steps_b[-1]
    steps_b = gather_step(stack_b, steps_b, half, False, sums_a[1])
    opened_a, hidden_a = open_down(sums_a, second_b)
    while len(steps_b) < half - 1:
        steps_b = gather_step(stack_b, steps_b, half, False)
    third_b = steps_b[-1]
    steps_b = gather_step(stack_b, steps_b, half, False, opened_a)
    closed_a = close_down(hidden_a, third_b)
    term_a = term_of(opened_a, closed_a)
    distances = list(range(half - 1, 0, -1))
    moved_a = scatter_send(scatter_sums(None, term_a, count, half))
    sums_a = scatter_sums(moved_a, term_a, count, distances.pop(0))
    sums_b = matmul(near, own_b, [steps_b], None, closed_a, sums_a)
    sums_a = scatter_sums(scatter_send(sums_a), term_a, count, distances.pop(0), sums_b[1])
    sums_b = matmul([0], own_b, [steps_b], sums_b, sums_a)
    for distance in distances:
        sums_a = scatter_sums(scatter_send(sums_a), term_a, count, distance)
    opened_b, hidden_b = open_down(sums_b, sums_a)
    moved_a = scatter_send(sums_a)
    spans = [slice(0, size // 2), slice(size // 2, size)]
    distances = list(range(half, 0, -1))
    parts_b = [None, None]
    closed_b = None
    for number, distance in enumerate(distances):
        earlier = []
        for which, span in enumerate(spans):
            moved = scatter_send(parts_b[which]) if number else None
            parts_b[which] = scatter_sums(moved, term_of(opened_b, closed_b, span), count, distance, earlier)
            earlier = parts_b[which]
        if number == 1:
            closed_b = close_down(hidden_b, parts_b, moved_a)
    moved_b = [scatter_send(part) for part in parts_b]
    terms_b = [term_of(opened_b, closed_b, span) for span in spans]

    def finish(start, term, moved):
        ffn = term(0).astype(jnp.float32) + moved[0].astype(jnp.float32) + moved[1].astype(jnp.float32)
        rows = slice(start, start + ffn.shape[0])
        return (mix(noisy_input[rows], self_cond[rows]) + ffn).astype(jnp.bfloat16)

    outs = [finish(span.start, term, moved) for span, term, moved in zip(spans, terms_b, moved_b)]
    return jnp.concatenate([*outs, finish(size, term_a, moved_a)], axis=0)


def solution(mesh):
    in_specs = (
        P(("groups", "seq"), "blk"),
        P(("groups", "seq"), "blk"),
        P("blk"),
        P("groups"),
        P(None, None, "blk"),
        P(),
        P("seq", "blk"),
        P("seq", "blk"),
        P("blk", "seq"),
    )
    out_specs = P(("groups", "seq"), "blk")
    return jax.shard_map(
        on_device, mesh=mesh, in_specs=in_specs, out_specs=out_specs, check_vma=False
    )
```

time: 300 us -> 276 us (0.920)
  waiting for transfers between devices: 114 us -> 53 us
  starting transfers between devices: 40.9 us -> 89.6 us
  Pallas kernels: 113 us -> 93.3 us
  local copies, waits for them, and re-layouts: 10.9 us -> 30.4 us
  other arithmetic: 18.7 us -> 6.87 us
    ppermute x32 -> x24, waiting for transfers between devices: 112 us -> 33.4 us  [ring_shift(): lax.ppermute(value, 'blk', [(ring[i], ring[(i + steps) % count]) for i in...]
    ppermute x0 -> x24, starting transfers between devices: none -> 48.4 us  [carry(): return lax.ppermute(value, ('blk', 'seq'), route)]
    pallas_call x9 -> x8, Pallas kernels: 113 us -> 93.3 us  [the longest x4 54.4 us: gate_up(): pl.pallas_call(functools.partial(gate_up_kernel, group, shape_of, final,...]
    unnamed x58 -> x66, local copies, waits for them, and re-layouts: 6.52 us -> 24 us
    ppermute x0 -> x24, waiting for transfers between devices: none -> 15.4 us  [carry(): return lax.ppermute(value, ('blk', 'seq'), route)]
    select_n x8 -> x0, other arithmetic: 9.77 us -> none  [exchange(): return (first, *second, swap(jnp.where(mine_first[index], other, first)))]
    ppermute x13 -> x7, starting transfers between devices: 3.07 us -> 10.1 us  [swap(): return lax.ppermute(value, 'seq', [(0, 1), (1, 0)])]
    ppermute x32 -> x24, starting transfers between devices: 34.5 us -> 28.6 us  [ring_shift(): lax.ppermute(value, 'blk', [(ring[i], ring[(i + steps) % count]) for i in...]
  transfers between devices with their start and end apart: 47 -> 57, of which waited for: 23 -> 21; matrix products, arithmetic and copies ran while one was open for 7% -> 4% of each run, Pallas kernels for 31% -> 31%
where the time goes in v4:
time: 276 us; the launch traced here: 275 us
  Pallas kernels  93.3 us (34%)
  starting transfers between devices  89.6 us (32%)
  waiting for transfers between devices  53 us (19%)
  local copies, waits for them, and re-layouts  30.4 us (11%)
  other arithmetic  6.87 us (2%)
    pallas_call x4, Pallas kernels, gate_up(): pl.pallas_call(functools.partial(gate_up_kernel, group, shape_of, final,...  54.4 us
    ppermute x24, starting transfers between devices, carry(): return lax.ppermute(value, ('blk', 'seq'), route)  48.4 us
    pallas_call x4, Pallas kernels, down(): pl.pallas_call(functools.partial(down_kernel, start, stop, split, width *...  38.8 us
    ppermute x24, waiting for transfers between devices, ring_shift(): lax.ppermute(value, 'blk', [(ring[i], ring[(i + steps) % count]) for i in...  33.4 us
    ppermute x24, starting transfers between devices, ring_shift(): lax.ppermute(value, 'blk', [(ring[i], ring[(i + steps) % count]) for i in...  28.6 us
    unnamed x66, local copies, waits for them, and re-layouts  24 us
    ppermute x24, waiting for transfers between devices, carry(): return lax.ppermute(value, ('blk', 'seq'), route)  15.4 us
    ppermute x7, starting transfers between devices, swap(): return lax.ppermute(value, 'seq', [(0, 1), (1, 0)])  10.1 us
  transfers between devices with their start and end apart: 57, of which 21 were waited for; matrix products, arithmetic and copies ran while one was open for 4% of the time, Pallas kernels for 31%

profile of v4, /device:TPU:0, one launch (start us, length us, event | category | flops | bytes accessed | tf_op | source)
XLA Modules:
  0.0 274.9 jit_solution(16249889685572824353)
XLA Ops:
  2.7 1.5 multiply_add_fusion
  4.7 1.4 collective-permute-start.4
  6.2 1.3 collective-permute-start.5
  7.5 3.9 %collective-permute-start.2 = (bf16[256,1024]{1,0:T(8,128)(2,1)S(1)}, bf16[256,1024]{1,0:T(8,128)(2,1)S(1)}, u32[]{:S(2)}, u32[]{:S(2)}) collective-permute-start(bf16[256,1024]{1,0:T(8,128)(2,1)S(1)} %multiply_convert_fusion.1.refs_0_), channel_id=1, source_target_pairs={{0,4},{4,8},{9,13},{13,15},{15,11},{11,7},{6,2},{2,0},{16,20},{20,... | collective-permute-start | bytes 1572872 | tf_op jit(solution)/shard_map/ppermute | solution.py:289
  11.4 2.5 collective-permute-start.3
  13.8 3.9 %collective-permute-done.4.refs_5_ = bf16[256,1024]{1,0:T(8,128)(2,1)S(1)} collective-permute-done((bf16[256,1024]{1,0:T(8,128)(2,1)S(1)}, bf16[256,1024]{1,0:T(8,128)(2,1)S(1)}, u32[]{:S(2)}, u32[]{:S(2)}) %collective-permute-start.4) | collective-permute-done | bytes 524320 | tf_op jit(solution)/shard_map/ppermute | solution.py:289
  17.8 1.7 collective-permute-done.5.refs_11_
  19.5 3.4 %collective-permute-start.11 = (bf16[256,1024]{1,0:T(8,128)(2,1)S(1)}, bf16[256,1024]{1,0:T(8,128)(2,1)S(1)}, u32[]{:S(2)}, u32[]{:S(2)}) collective-permute-start(bf16[256,1024]{1,0:T(8,128)(2,1)S(1)} %collective-permute-done.4.refs_5_), channel_id=1, source_target_pairs={{0,4},{4,8},{8,12},{13,15},{15,11},{11,7},{7,3},{2,0},{16,20},{20,... | collective-permute-start | bytes 1572872 | tf_op jit(solution)/shard_map/ppermute | solution.py:289
  23.6 2.5 collective-permute-start.12
  27.0 1.3 collective-permute-start.1
  28.4 1.3 collective-permute-start
  29.7 4.9 %collective-permute-start.7 = (bf16[256,1024]{1,0:T(8,128)(2,1)S(1)}, bf16[256,1024]{1,0:T(8,128)(2,1)S(1)}, u32[]{:S(2)}, u32[]{:S(2)}) collective-permute-start(bf16[256,1024]{1,0:T(8,128)(2,1)S(1)} %collective-permute-done.2.refs_4_), channel_id=1, source_target_pairs={{0,4},{4,8},{8,12},{13,15},{15,11},{11,7},{7,3},{2,0},{16,20},{20,... | collective-permute-start | bytes 1572872 | tf_op jit(solution)/shard_map/ppermute | solution.py:289
  34.5 1.3 collective-permute-start.8
  35.9 3.0 %collective-permute-start.13 = (bf16[256,1024]{1,0:T(8,128)(2,1)S(1)}, bf16[256,1024]{1,0:T(8,128)(2,1)S(1)}, u32[]{:S(2)}, u32[]{:S(2)}) collective-permute-start(bf16[256,1024]{1,0:T(8,128)(2,1)S(1)} %collective-permute-done.11.refs_1_), channel_id=1, source_target_pairs={{0,4},{4,8},{8,12},{12,14},{15,11},{11,7},{7,3},{3,1},{16,20},{20,... | collective-permute-start | bytes 1572872 | tf_op jit(solution)/shard_map/ppermute | solution.py:289
  39.9 2.3 collective-permute-done.7.refs_0_
  42.2 2.2 collective-permute-done.8.refs_2_
  44.4 2.1 collective-permute-start.9
  50.3 2.2 collective-permute-done.9.refs_8_
  56.2 5.3 %collective-permute-start.23 = (bf16[256,1024]{1,0:T(8,128)(2,1)S(1)}, bf16[256,1024]{1,0:T(8,128)(2,1)S(1)}, u32[]{:S(2)}, u32[]{:S(2)}) collective-permute-start(bf16[256,1024]{1,0:T(8,128)(2,1)S(1)} %multiply_convert_fusion.1.refs_0_), channel_id=1, source_target_pairs={{0,1},{1,0},{2,3},{3,2},{4,5},{5,4},{6,7},{7,6},{8,9},{9,8},{10,11... | collective-permute-start | bytes 1572872 | tf_op jit(solution)/shard_map/ppermute | solution.py:59
  63.3 5.3 %collective-permute-start.15 = (bf16[512,1024]{1,0:T(8,128)(2,1)S(1)}, bf16[512,1024]{1,0:T(8,128)(2,1)S(1)}, u32[]{:S(2)}, u32[]{:S(2)}) collective-permute-start(bf16[512,1024]{1,0:T(8,128)(2,1)S(1)} %pad_maximum_fusion.1), channel_id=1, source_target_pairs={{0,4},{4,8},{9,13},{13,15},{15,11},{11,7},{6,2},{2,0},{16,20},{20,... | collective-permute-start | bytes 3145736 | tf_op jit(solution)/shard_map/ppermute | solution.py:289
  68.6 1.9 collective-permute-start.16
  71.6 1.0 copy-done.23
  72.7 1.0 copy-done.25
  73.7 1.0 copy-done.27
  74.7 18.1 %gate_up.4 = (f32[2,512,2048]{2,1,0:T(8,128)S(1)}, f32[512,128]{1,0:T(8,128)S(1)}) custom-call(s32[3,4]{1,0:T(4,128)S(1)} %dynamic-slice_bitcast_fusion.pairs_ref, bf16[256,1024]{1,0:T(8,128)(2,1)S(1)} %copy-done.25, bf16[256,1024]{1,0:T(8,128)(2,1)S(1)} %copy-done.21, bf16[256,1024]{1,0:T(8,128)(2,1)S(1)} %copy-done.27, bf16[256,1024]{1,0:T(8,128)(2,1)S(1)} %copy-done.23, ...), custom_call_target="tpu_custom_call" | custom-call | flops 19327352832 | bytes 25165824 | tf_op jit(solution)/shard_map/gate_up/pallas_call | solution.py:173
  92.9 4.1 %collective-permute-start.21 = (bf16[512,1024]{1,0:T(8,128)(2,1)S(1)}, bf16[512,1024]{1,0:T(8,128)(2,1)S(1)}, u32[]{:S(2)}, u32[]{:S(2)}) collective-permute-start(bf16[512,1024]{1,0:T(8,128)(2,1)S(1)} %collective-permute-done.15.refs_2_), channel_id=1, source_target_pairs={{0,4},{4,8},{8,12},{13,15},{15,11},{11,7},{7,3},{2,0},{16,20},{20,... | collective-permute-start | bytes 3145736 | tf_op jit(solution)/shard_map/ppermute | solution.py:289
  97.0 1.9 collective-permute-start.22
  98.9 9.1 %gate_up.5 = (f32[2,256,2048]{2,1,0:T(8,128)S(1)}, f32[256,128]{1,0:T(8,128)S(1)}, bf16[2,256,2048]{2,1,0:T(8,128)(2,1)S(1)}, f32[256,128]{1,0:T(8,128)S(1)}) custom-call(s32[3,4]{1,0:T(4,128)S(1)} %dynamic-slice_bitcast_fusion.pairs_ref, bf16[256,1024]{1,0:T(8,128)(2,1)S(1)} %multiply_convert_fusion.1.refs_0_, ...), custom_call_target="tpu_custom_call" | custom-call | flops 6442450944 | bytes 8388608 | tf_op jit(solution)/shard_map/gate_up/pallas_call | solution.py:173
  108.0 1.6 collective-permute-done.21.refs_0_
  109.6 1.5 collective-permute-done.22.refs_1_
  111.1 2.6 collective-permute-start.24
  114.6 3.2 %collective-permute-start.27 = (f32[256,128]{1,0:T(8,128)S(1)}, f32[256,128]{1,0:T(8,128)S(1)}, u32[]{:S(2)}, u32[]{:S(2)}) collective-permute-start(f32[256,128]{1,0:T(8,128)S(1)} %get-tuple-element.154), channel_id=1, source_target_pairs={{0,1},{1,0},{2,3},{3,2},{4,5},{5,4},{6,7},{7,6},{8,9},{9,8},{10,11... | collective-permute-start | bytes 393224 | tf_op jit(solution)/shard_map/ppermute | solution.py:59
  118.9 5.8 %copy-done = bf16[2048,4096]{1,0:T(8,128)(2,1)S(1)} copy-done((bf16[2048,4096]{1,0:T(8,128)(2,1)S(1)}, bf16[2048,4096]{1,0:T(8,128)(2,1)}, u32[]{:S(2)}) %copy-start) | copy-done | bytes 16777240
  124.7 7.4 %down.4 = (bf16[3,256,1024]{2,1,0:T(8,128)(2,1)S(1)}, bf16[256,2048]{1,0:T(8,128)(2,1)S(1)}) custom-call(s32[2,8]{1,0:T(2,128)S(1)} %fusion.40.tiles_ref, f32[2,256,2048]{2,1,0:T(8,128)S(1)} %get-tuple-element.150.refs_0_, f32[256,128]{1,0:T(8,128)S(1)} %get-tuple-element.147.refs_1_, bf16[2,256,2048]{2,1,0:T(8,128)(2,1)S(1)} %collective-permute-done.26.refs_2_, ...), custom_call_target="tpu_custom_call" | custom-call | flops 6442450944 | bytes 12582912 | tf_op jit(solution)/shard_map/down/pallas_call | solution.py:258
  133.7 3.6 %collective-permute-start.31 = (bf16[128,1024]{1,0:T(8,128)(2,1)S(1)}, bf16[128,1024]{1,0:T(8,128)(2,1)S(1)}, u32[]{:S(2)}, u32[]{:S(2)}) collective-permute-start(bf16[128,1024]{1,0:T(8,128)(2,1)S(1)} %get-tuple-element.160), channel_id=1, source_target_pairs={{0,4},{4,8},{8,12},{12,14},{14,10},{10,6},{6,2},{2,0},{1,5},{5,9},... | collective-permute-start | bytes 786440 | tf_op jit(solution)/shard_map/ppermute | solution.py:55
  137.3 5.8 %copy-done.1 = bf16[2048,4096]{1,0:T(8,128)(2,1)S(1)} copy-done((bf16[2048,4096]{1,0:T(8,128)(2,1)S(1)}, bf16[2048,4096]{1,0:T(8,128)(2,1)}, u32[]{:S(2)}) %copy-start.1) | copy-done | bytes 16777240
  143.1 12.0 %down.5 = bf16[5,256,1024]{2,1,0:T(8,128)(2,1)S(1)} custom-call(s32[2,8]{1,0:T(2,128)S(1)} %fusion.40.tiles_ref, bf16[256,2048]{1,0:T(8,128)(2,1)S(1)} %get-tuple-element.159.refs_0_, bf16[2048,4096]{1,0:T(8,128)(2,1)S(1)} %copy-done.1, bf16[2048,4096]{1,0:T(8,128)(2,1)} %collective-permute-done.28.refs_5_.refs_2_), custom_call_target="tpu_custom_call" | custom-call | flops 10737418240 | bytes 20971520 | tf_op jit(solution)/shard_map/down/pallas_call | solution.py:258
  155.4 2.1 collective-permute-start.33
  157.7 18.3 %gate_up.6 = (f32[2,512,2048]{2,1,0:T(8,128)S(1)}, f32[512,128]{1,0:T(8,128)S(1)}) custom-call(s32[3,4]{1,0:T(4,128)S(1)} %dynamic-slice_bitcast_fusion.pairs_ref, bf16[512,1024]{1,0:T(8,128)(2,1)S(1)} %collective-permute-done.21.refs_0_, bf16[512,1024]{1,0:T(8,128)(2,1)S(1)} %copy-done.11, bf16[512,1024]{1,0:T(8,128)(2,1)S(1)} %copy-done.7, ...), custom_call_target="tpu_custom_call" | custom-call | flops 19327352832 | bytes 25165824 | tf_op jit(solution)/shard_map/gate_up/pallas_call | solution.py:173
  176.4 2.3 collective-permute-start.35
  178.7 9.0 %gate_up.7 = (f32[2,256,2048]{2,1,0:T(8,128)S(1)}, f32[256,128]{1,0:T(8,128)S(1)}, bf16[2,256,2048]{2,1,0:T(8,128)(2,1)S(1)}, f32[256,128]{1,0:T(8,128)S(1)}) custom-call(s32[3,4]{1,0:T(4,128)S(1)} %dynamic-slice_bitcast_fusion.pairs_ref, bf16[256,1024]{1,0:T(8,128)(2,1)S(1)} %multiply_convert_fusion.refs_0_, ...), custom_call_target="tpu_custom_call" | custom-call | flops 6442450944 | bytes 8388608 | tf_op jit(solution)/shard_map/gate_up/pallas_call | solution.py:173
  187.7 3.0 %collective-permute-done.36 = bf16[256,1024]{1,0:T(8,128)(2,1)S(1)} collective-permute-done((bf16[256,1024]{1,0:T(8,128)(2,1)S(1)}, bf16[256,1024]{1,0:T(8,128)(2,1)S(1)}, u32[]{:S(2)}, u32[]{:S(2)}) %collective-permute-start.36) | collective-permute-done | bytes 524320 | tf_op jit(solution)/shard_map/ppermute | solution.py:55
  192.1 3.8 %collective-permute-done.38.refs_3_ = f32[256,128]{1,0:T(8,128)S(1)} collective-permute-done((f32[256,128]{1,0:T(8,128)S(1)}, f32[256,128]{1,0:T(8,128)S(1)}, u32[]{:S(2)}, u32[]{:S(2)}) %collective-permute-start.38) | collective-permute-done | bytes 131104 | tf_op jit(solution)/shard_map/ppermute | solution.py:59
  196.0 5.8 %copy-done.2 = bf16[2048,4096]{1,0:T(8,128)(2,1)S(1)} copy-done((bf16[2048,4096]{1,0:T(8,128)(2,1)S(1)}, bf16[2048,4096]{1,0:T(8,128)(2,1)}, u32[]{:S(2)}) %copy-start.2) | copy-done | bytes 16777240
  201.7 7.4 %down.6 = (bf16[3,256,1024]{2,1,0:T(8,128)(2,1)S(1)}, bf16[256,2048]{1,0:T(8,128)(2,1)S(1)}) custom-call(s32[2,8]{1,0:T(2,128)S(1)} %fusion.40.tiles_ref, f32[2,256,2048]{2,1,0:T(8,128)S(1)} %get-tuple-element.178.refs_0_, f32[256,128]{1,0:T(8,128)S(1)} %get-tuple-element.179.refs_1_, bf16[2,256,2048]{2,1,0:T(8,128)(2,1)S(1)} %collective-permute-done.37.refs_2_, ...), custom_call_target="tpu_custom_call" | custom-call | flops 6442450944 | bytes 12582912 | tf_op jit(solution)/shard_map/down/pallas_call | solution.py:258
  209.2 1.8 collective-permute-start.39
  211.3 1.7 collective-permute-start.43
  213.3 1.7 collective-permute-start.41
  215.1 1.4 collective-permute-start.42
  217.4 1.4 collective-permute-start.45
  218.8 10.2 %collective-permute-done.41 = bf16[64,1024]{1,0:T(8,128)(2,1)S(1)} collective-permute-done((bf16[64,1024]{1,0:T(8,128)(2,1)S(1)}, bf16[64,1024]{1,0:T(8,128)(2,1)S(1)}, u32[]{:S(2)}, u32[]{:S(2)}) %collective-permute-start.41) | collective-permute-done | bytes 131104 | tf_op jit(solution)/shard_map/ppermute | solution.py:55
  229.0 1.5 collective-permute-start.46
  231.6 1.6 collective-permute-start.52
  233.2 12.0 %down.7 = bf16[5,256,1024]{2,1,0:T(8,128)(2,1)S(1)} custom-call(s32[2,8]{1,0:T(2,128)S(1)} %fusion.40.tiles_ref, bf16[256,2048]{1,0:T(8,128)(2,1)S(1)} %get-tuple-element.196.refs_0_, bf16[2048,4096]{1,0:T(8,128)(2,1)S(1)} %copy-done.2, bf16[2048,4096]{1,0:T(8,128)(2,1)} %collective-permute-done.28.refs_5_.refs_2_), custom_call_target="tpu_custom_call" | custom-call | flops 10737418240 | bytes 20971520 | tf_op jit(solution)/shard_map/down/pallas_call | solution.py:258
  245.6 2.0 collective-permute-start.47
  247.6 4.3 %collective-permute-done.48 = bf16[128,1024]{1,0:T(8,128)(2,1)S(1)} collective-permute-done((bf16[128,1024]{1,0:T(8,128)(2,1)S(1)}, bf16[128,1024]{1,0:T(8,128)(2,1)S(1)}, u32[]{:S(2)}, u32[]{:S(2)}) %collective-permute-start.48) | collective-permute-done | bytes 262176 | tf_op jit(solution)/shard_map/ppermute | solution.py:55
  252.9 1.8 collective-permute-start.54
  255.0 1.7 collective-permute-start.50
  257.1 5.0 %collective-permute-done.54 = bf16[128,1024]{1,0:T(8,128)(2,1)S(1)} collective-permute-done((bf16[128,1024]{1,0:T(8,128)(2,1)S(1)}, bf16[128,1024]{1,0:T(8,128)(2,1)S(1)}, u32[]{:S(2)}, u32[]{:S(2)}) %collective-permute-start.54) | collective-permute-done | bytes 262176 | tf_op jit(solution)/shard_map/ppermute | solution.py:55
  262.1 1.9 collective-permute-done.53
  264.5 1.7 collective-permute-start.56
  267.1 2.5 collective-permute-done.49
  269.6 3.7 %collective-permute-done.55 = bf16[128,1024]{1,0:T(8,128)(2,1)S(1)} collective-permute-done((bf16[128,1024]{1,0:T(8,128)(2,1)S(1)}, bf16[128,1024]{1,0:T(8,128)(2,1)S(1)}, u32[]{:S(2)}, u32[]{:S(2)}) %collective-permute-start.55) | collective-permute-done | bytes 262176 | tf_op jit(solution)/shard_map/ppermute | solution.py:55
  273.8 1.0 pad_maximum_fusion.2
  (161 shorter events, 27.6 us)
Async XLA Ops:
  0.0 118.9 %collective-permute-start.28 = (bf16[2048,4096]{1,0:T(8,128)(2,1)}, bf16[2048,4096]{1,0:T(8,128)(2,1)}, u32[]{:S(2)}, u32[]{:S(2)}) collective-permute-start(bf16[2048,4096]{1,0:T(8,128)(2,1)} %refs_1_.3), channel_id=1, source_target_pairs={{0,1},{1,0},{2,3},{3,2},{4,5},{5,4},{6,7},{7,6},{8,9},{9,8},{10,11... | collective-permute-start | bytes 50331656 | tf_op jit(solution)/shard_map/ppermute | solution.py:59
  4.2 22.8 %copy-start.28 = (bf16[512,1024]{1,0:T(8,128)(2,1)S(1)}, bf16[512,1024]{1,0:T(8,128)(2,1)}, u32[]{:S(2)}) copy-start(bf16[512,1024]{1,0:T(8,128)(2,1)} %param.12) | copy-start | bytes 3145732
  4.2 24.1 %copy-start.30 = (bf16[512,1024]{1,0:T(8,128)(2,1)S(1)}, bf16[512,1024]{1,0:T(8,128)(2,1)}, u32[]{:S(2)}) copy-start(bf16[512,1024]{1,0:T(8,128)(2,1)} %param.11) | copy-start | bytes 3145732
  4.2 31.7 %copy-start.32 = (f32[1024]{0:T(1024)S(1)}, f32[1024]{0:T(1024)}, u32[]{:S(2)}) copy-start(f32[1024]{0:T(1024)} %param.13) | copy-start | bytes 12292
  4.7 13.0 %collective-permute-start.4 = (bf16[256,1024]{1,0:T(8,128)(2,1)S(1)}, bf16[256,1024]{1,0:T(8,128)(2,1)S(1)}, u32[]{:S(2)}, u32[]{:S(2)}) collective-permute-start(bf16[256,1024]{1,0:T(8,128)(2,1)S(1)} %multiply_convert_fusion.1.refs_0_), channel_id=1, source_target_pairs={{1,4},{5,8},{8,13},{12,15},{14,11},{10,7},{7,2},{3,0},{17,20},{21,... | collective-permute-start | bytes 1572872 | tf_op jit(solution)/shard_map/ppermute | solution.py:289
  6.2 13.3 %collective-permute-start.5 = (bf16[256,1024]{1,0:T(8,128)(2,1)S(1)}, bf16[256,1024]{1,0:T(8,128)(2,1)S(1)}, u32[]{:S(2)}, u32[]{:S(2)}) collective-permute-start(bf16[256,1024]{1,0:T(8,128)(2,1)S(1)} %multiply_convert_fusion.1.refs_0_), channel_id=1, source_target_pairs={{1,2},{5,0},{8,5},{12,9},{14,13},{10,15},{7,10},{3,6},{17,18},{21,... | collective-permute-start | bytes 1572872 | tf_op jit(solution)/shard_map/ppermute | solution.py:289
  7.5 19.5 %collective-permute-start.2 = (bf16[256,1024]{1,0:T(8,128)(2,1)S(1)}, bf16[256,1024]{1,0:T(8,128)(2,1)S(1)}, u32[]{:S(2)}, u32[]{:S(2)}) collective-permute-start(bf16[256,1024]{1,0:T(8,128)(2,1)S(1)} %multiply_convert_fusion.1.refs_0_), channel_id=1, source_target_pairs={{0,4},{4,8},{9,13},{13,15},{15,11},{11,7},{6,2},{2,0},{16,20},{20,... | collective-permute-start | bytes 1572872 | tf_op jit(solution)/shard_map/ppermute | solution.py:289
  11.4 17.0 %collective-permute-start.3 = (bf16[256,1024]{1,0:T(8,128)(2,1)S(1)}, bf16[256,1024]{1,0:T(8,128)(2,1)S(1)}, u32[]{:S(2)}, u32[]{:S(2)}) collective-permute-start(bf16[256,1024]{1,0:T(8,128)(2,1)S(1)} %multiply_convert_fusion.1.refs_0_), channel_id=1, source_target_pairs={{0,2},{4,0},{9,5},{13,9},{15,13},{11,15},{6,10},{2,6},{16,18},{20,... | collective-permute-start | bytes 1572872 | tf_op jit(solution)/shard_map/ppermute | solution.py:289
  19.5 16.5 %collective-permute-start.11 = (bf16[256,1024]{1,0:T(8,128)(2,1)S(1)}, bf16[256,1024]{1,0:T(8,128)(2,1)S(1)}, u32[]{:S(2)}, u32[]{:S(2)}) collective-permute-start(bf16[256,1024]{1,0:T(8,128)(2,1)S(1)} %collective-permute-done.4.refs_5_), channel_id=1, source_target_pairs={{0,4},{4,8},{8,12},{13,15},{15,11},{11,7},{7,3},{2,0},{16,20},{20,... | collective-permute-start | bytes 1572872 | tf_op jit(solution)/shard_map/ppermute | solution.py:289
  23.6 12.3 %collective-permute-start.12 = (bf16[256,1024]{1,0:T(8,128)(2,1)S(1)}, bf16[256,1024]{1,0:T(8,128)(2,1)S(1)}, u32[]{:S(2)}, u32[]{:S(2)}) collective-permute-start(bf16[256,1024]{1,0:T(8,128)(2,1)S(1)} %collective-permute-done.5.refs_11_), channel_id=1, source_target_pairs={{0,2},{5,1},{9,5},{13,9},{15,13},{10,14},{6,10},{2,6},{16,18},{21,... | collective-permute-start | bytes 1572872 | tf_op jit(solution)/shard_map/ppermute | solution.py:289
  27.0 21.9 %copy-start.16 = (bf16[256,1024]{1,0:T(8,128)(2,1)}, bf16[256,1024]{1,0:T(8,128)(2,1)S(1)}, u32[]{:S(2)}) copy-start(bf16[256,1024]{1,0:T(8,128)(2,1)S(1)} %collective-permute-done.2.refs_4_) | copy-start | bytes 1572868
  27.0 2.6 collective-permute-start.1
  28.4 6.2 %collective-permute-start = (bf16[3,1024]{1,0:T(4,128)(2,1)S(1)}, bf16[3,1024]{1,0:T(4,128)(2,1)S(1)}, u32[]{:S(2)}, u32[]{:S(2)}) collective-permute-start(bf16[3,1024]{1,0:T(4,128)(2,1)S(1)} %slice.319), channel_id=1, source_target_pairs={{0,1},{2,3},{4,5},{6,7},{8,9},{10,11},{12,13},{14,15},{16,17},{18,... | collective-permute-start | bytes 18440 | tf_op jit(solution)/shard_map/ppermute | solution.py:352
  29.7 12.5 %collective-permute-start.7 = (bf16[256,1024]{1,0:T(8,128)(2,1)S(1)}, bf16[256,1024]{1,0:T(8,128)(2,1)S(1)}, u32[]{:S(2)}, u32[]{:S(2)}) collective-permute-start(bf16[256,1024]{1,0:T(8,128)(2,1)S(1)} %collective-permute-done.2.refs_4_), channel_id=1, source_target_pairs={{0,4},{4,8},{8,12},{13,15},{15,11},{11,7},{7,3},{2,0},{16,20},{20,... | collective-permute-start | bytes 1572872 | tf_op jit(solution)/shard_map/ppermute | solution.py:289
  34.5 9.8 %collective-permute-start.8 = (bf16[256,1024]{1,0:T(8,128)(2,1)S(1)}, bf16[256,1024]{1,0:T(8,128)(2,1)S(1)}, u32[]{:S(2)}, u32[]{:S(2)}) collective-permute-start(bf16[256,1024]{1,0:T(8,128)(2,1)S(1)} %collective-permute-done.3.refs_10_), channel_id=1, source_target_pairs={{0,2},{5,1},{9,5},{13,9},{15,13},{10,14},{6,10},{2,6},{16,18},{21,... | collective-permute-start | bytes 1572872 | tf_op jit(solution)/shard_map/ppermute | solution.py:289
  35.9 11.7 %collective-permute-start.13 = (bf16[256,1024]{1,0:T(8,128)(2,1)S(1)}, bf16[256,1024]{1,0:T(8,128)(2,1)S(1)}, u32[]{:S(2)}, u32[]{:S(2)}) collective-permute-start(bf16[256,1024]{1,0:T(8,128)(2,1)S(1)} %collective-permute-done.11.refs_1_), channel_id=1, source_target_pairs={{0,4},{4,8},{8,12},{12,14},{15,11},{11,7},{7,3},{3,1},{16,20},{20,... | collective-permute-start | bytes 1572872 | tf_op jit(solution)/shard_map/ppermute | solution.py:289
  39.2 9.0 %collective-permute-start.14 = (bf16[256,1024]{1,0:T(8,128)(2,1)S(1)}, bf16[256,1024]{1,0:T(8,128)(2,1)S(1)}, u32[]{:S(2)}, u32[]{:S(2)}) collective-permute-start(bf16[256,1024]{1,0:T(8,128)(2,1)S(1)} %collective-permute-done.12.refs_3_), channel_id=1, source_target_pairs={{1,3},{5,1},{9,5},{13,9},{14,12},{10,14},{6,10},{2,6},{17,19},{21,... | collective-permute-start | bytes 1572872 | tf_op jit(solution)/shard_map/ppermute | solution.py:289
  44.4 8.1 %collective-permute-start.9 = (bf16[256,1024]{1,0:T(8,128)(2,1)S(1)}, bf16[256,1024]{1,0:T(8,128)(2,1)}, u32[]{:S(2)}, u32[]{:S(2)}) collective-permute-start(bf16[256,1024]{1,0:T(8,128)(2,1)S(1)} %collective-permute-done.7.refs_0_), channel_id=1, source_target_pairs={{0,4},{4,8},{8,12},{12,14},{15,11},{11,7},{7,3},{3,1},{16,20},{20,... | collective-permute-start | bytes 1572872 | tf_op jit(solution)/shard_map/ppermute | solution.py:289
  46.5 6.7 %collective-permute-start.10 = (bf16[256,1024]{1,0:T(8,128)(2,1)S(1)}, bf16[256,1024]{1,0:T(8,128)(2,1)S(1)}, u32[]{:S(2)}, u32[]{:S(2)}) collective-permute-start(bf16[256,1024]{1,0:T(8,128)(2,1)S(1)} %collective-permute-done.8.refs_2_), channel_id=1, source_target_pairs={{1,3},{5,1},{9,5},{13,9},{14,12},{10,14},{6,10},{2,6},{17,19},{21,... | collective-permute-start | bytes 1572872 | tf_op jit(solution)/shard_map/ppermute | solution.py:289
  47.7 22.8 %copy-start.3 = (f32[8192]{0:T(1024)S(1)}, f32[8192]{0:T(1024)}, u32[]{:S(2)}) copy-start(f32[8192]{0:T(1024)} %param.16) | copy-start | bytes 98308
  47.7 8.5 %collective-permute-start.6 = (bf16[256,1024]{1,0:T(8,128)(2,1)S(1)}, bf16[256,1024]{1,0:T(8,128)(2,1)S(1)}, u32[]{:S(2)}, u32[]{:S(2)}) collective-permute-start(bf16[256,1024]{1,0:T(8,128)(2,1)S(1)} %multiply_convert_fusion.refs_0_), channel_id=1, source_target_pairs={{0,1},{1,0},{2,3},{3,2},{4,5},{5,4},{6,7},{7,6},{8,9},{9,8},{10,11... | collective-permute-start | bytes 1572872 | tf_op jit(solution)/shard_map/ppermute | solution.py:59
  49.6 13.0 %collective-permute-start.20 = (bf16[128,1024]{1,0:T(8,128)(2,1)}, bf16[128,1024]{1,0:T(8,128)(2,1)S(1)}, u32[]{:S(2)}, u32[]{:S(2)}) collective-permute-start(bf16[128,1024]{1,0:T(8,128)(2,1)} %slice.338), channel_id=1, source_target_pairs={{1,3},{5,1},{9,5},{12,8},{14,12},{10,14},{6,10},{3,7},{17,19},{21,... | collective-permute-start | bytes 786440 | tf_op jit(solution)/shard_map/ppermute | solution.py:289
  52.5 10.8 %collective-permute-start.19 = (bf16[128,1024]{1,0:T(8,128)(2,1)}, bf16[128,1024]{1,0:T(8,128)(2,1)S(1)}, u32[]{:S(2)}, u32[]{:S(2)}) collective-permute-start(bf16[128,1024]{1,0:T(8,128)(2,1)} %slice.337), channel_id=1, source_target_pairs={{1,5},{4,8},{8,12},{12,14},{14,10},{11,7},{7,3},{3,1},{17,21},{20,... | collective-permute-start | bytes 786440 | tf_op jit(solution)/shard_map/ppermute | solution.py:289
  54.6 13.9 %collective-permute-start.18 = (bf16[128,1024]{1,0:T(8,128)(2,1)}, bf16[128,1024]{1,0:T(8,128)(2,1)S(1)}, u32[]{:S(2)}, u32[]{:S(2)}) collective-permute-start(bf16[128,1024]{1,0:T(8,128)(2,1)} %slice.336), channel_id=1, source_target_pairs={{1,3},{5,1},{9,5},{12,8},{14,12},{10,14},{6,10},{3,7},{17,19},{21,... | collective-permute-start | bytes 786440 | tf_op jit(solution)/shard_map/ppermute | solution.py:289
  56.2 42.7 %collective-permute-start.23 = (bf16[256,1024]{1,0:T(8,128)(2,1)S(1)}, bf16[256,1024]{1,0:T(8,128)(2,1)S(1)}, u32[]{:S(2)}, u32[]{:S(2)}) collective-permute-start(bf16[256,1024]{1,0:T(8,128)(2,1)S(1)} %multiply_convert_fusion.1.refs_0_), channel_id=1, source_target_pairs={{0,1},{1,0},{2,3},{3,2},{4,5},{5,4},{6,7},{7,6},{8,9},{9,8},{10,11... | collective-permute-start | bytes 1572872 | tf_op jit(solution)/shard_map/ppermute | solution.py:59
  62.6 30.2 %collective-permute-start.17 = (bf16[128,1024]{1,0:T(8,128)(2,1)S(1)}, bf16[128,1024]{1,0:T(8,128)(2,1)S(1)}, u32[]{:S(2)}, u32[]{:S(2)}) collective-permute-start(bf16[128,1024]{1,0:T(8,128)(2,1)S(1)} %slice.335), channel_id=1, source_target_pairs={{1,5},{4,8},{8,12},{12,14},{14,10},{11,7},{7,3},{3,1},{17,21},{20,... | collective-permute-start | bytes 786440 | tf_op jit(solution)/shard_map/ppermute | solution.py:289
  63.3 29.6 %collective-permute-start.15 = (bf16[512,1024]{1,0:T(8,128)(2,1)S(1)}, bf16[512,1024]{1,0:T(8,128)(2,1)S(1)}, u32[]{:S(2)}, u32[]{:S(2)}) collective-permute-start(bf16[512,1024]{1,0:T(8,128)(2,1)S(1)} %pad_maximum_fusion.1), channel_id=1, source_target_pairs={{0,4},{4,8},{9,13},{13,15},{15,11},{11,7},{6,2},{2,0},{16,20},{20,... | collective-permute-start | bytes 3145736 | tf_op jit(solution)/shard_map/ppermute | solution.py:289
  68.6 24.3 %collective-permute-start.16 = (bf16[512,1024]{1,0:T(8,128)(2,1)S(1)}, bf16[512,1024]{1,0:T(8,128)(2,1)S(1)}, u32[]{:S(2)}, u32[]{:S(2)}) collective-permute-start(bf16[512,1024]{1,0:T(8,128)(2,1)S(1)} %pad_maximum_fusion.1), channel_id=1, source_target_pairs={{0,2},{4,0},{9,5},{13,9},{15,13},{11,15},{6,10},{2,6},{16,18},{20,... | collective-permute-start | bytes 3145736 | tf_op jit(solution)/shard_map/ppermute | solution.py:289
  92.9 16.7 %collective-permute-start.21 = (bf16[512,1024]{1,0:T(8,128)(2,1)S(1)}, bf16[512,1024]{1,0:T(8,128)(2,1)S(1)}, u32[]{:S(2)}, u32[]{:S(2)}) collective-permute-start(bf16[512,1024]{1,0:T(8,128)(2,1)S(1)} %collective-permute-done.15.refs_2_), channel_id=1, source_target_pairs={{0,4},{4,8},{8,12},{13,15},{15,11},{11,7},{7,3},{2,0},{16,20},{20,... | collective-permute-start | bytes 3145736 | tf_op jit(solution)/shard_map/ppermute | solution.py:289
  97.0 14.1 %collective-permute-start.22 = (bf16[512,1024]{1,0:T(8,128)(2,1)S(1)}, bf16[512,1024]{1,0:T(8,128)(2,1)S(1)}, u32[]{:S(2)}, u32[]{:S(2)}) collective-permute-start(bf16[512,1024]{1,0:T(8,128)(2,1)S(1)} %collective-permute-done.16.refs_5_), channel_id=1, source_target_pairs={{0,2},{5,1},{9,5},{13,9},{15,13},{10,14},{6,10},{2,6},{16,18},{21,... | collective-permute-start | bytes 3145736 | tf_op jit(solution)/shard_map/ppermute | solution.py:289
  111.1 21.0 %copy-start.10 = (bf16[512,1024]{1,0:T(8,128)(2,1)}, bf16[512,1024]{1,0:T(8,128)(2,1)S(1)}, u32[]{:S(2)}) copy-start(bf16[512,1024]{1,0:T(8,128)(2,1)S(1)} %collective-permute-done.22.refs_1_) | copy-start | bytes 3145732
  111.1 7.8 %collective-permute-start.26 = (bf16[2,256,2048]{2,1,0:T(8,128)(2,1)S(1)}, bf16[2,256,2048]{2,1,0:T(8,128)(2,1)S(1)}, u32[]{:S(2)}, u32[]{:S(2)}) collective-permute-start(bf16[2,256,2048]{2,1,0:T(8,128)(2,1)S(1)} %get-tuple-element.153), channel_id=1, source_target_pairs={{0,1},{1,0},{2,3},{3,2},{4,5},{5,4},{6,7},{7,6},{8,9},{9,8},{10,11... | collective-permute-start | bytes 6291464 | tf_op jit(solution)/shard_map/ppermute | solution.py:59
  111.1 21.0 %collective-permute-start.24 = (bf16[512,1024]{1,0:T(8,128)(2,1)S(1)}, bf16[512,1024]{1,0:T(8,128)(2,1)S(1)}, u32[]{:S(2)}, u32[]{:S(2)}) collective-permute-start(bf16[512,1024]{1,0:T(8,128)(2,1)S(1)} %collective-permute-done.21.refs_0_), channel_id=1, source_target_pairs={{0,4},{4,8},{8,12},{12,14},{15,11},{11,7},{7,3},{3,1},{16,20},{20,... | collective-permute-start | bytes 3145736 | tf_op jit(solution)/shard_map/ppermute | solution.py:289
  113.7 18.4 %collective-permute-start.25 = (bf16[512,1024]{1,0:T(8,128)(2,1)S(1)}, bf16[512,1024]{1,0:T(8,128)(2,1)S(1)}, u32[]{:S(2)}, u32[]{:S(2)}) collective-permute-start(bf16[512,1024]{1,0:T(8,128)(2,1)S(1)} %collective-permute-done.22.refs_1_), channel_id=1, source_target_pairs={{1,3},{5,1},{9,5},{13,9},{14,12},{10,14},{6,10},{2,6},{17,19},{21,... | collective-permute-start | bytes 3145736 | tf_op jit(solution)/shard_map/ppermute | solution.py:289
  114.6 4.2 %collective-permute-start.27 = (f32[256,128]{1,0:T(8,128)S(1)}, f32[256,128]{1,0:T(8,128)S(1)}, u32[]{:S(2)}, u32[]{:S(2)}) collective-permute-start(f32[256,128]{1,0:T(8,128)S(1)} %get-tuple-element.154), channel_id=1, source_target_pairs={{0,1},{1,0},{2,3},{3,2},{4,5},{5,4},{6,7},{7,6},{8,9},{9,8},{10,11... | collective-permute-start | bytes 393224 | tf_op jit(solution)/shard_map/ppermute | solution.py:59
  132.3 46.4 %collective-permute-start.30 = (bf16[256,1024]{1,0:T(8,128)(2,1)S(1)}, bf16[256,1024]{1,0:T(8,128)(2,1)S(1)}, u32[]{:S(2)}, u32[]{:S(2)}) collective-permute-start(bf16[256,1024]{1,0:T(8,128)(2,1)S(1)} %slice.340), channel_id=1, source_target_pairs={{1,3},{5,1},{9,5},{12,8},{14,12},{10,14},{6,10},{3,7},{17,19},{21,... | collective-permute-start | bytes 1572872 | tf_op jit(solution)/shard_map/ppermute | solution.py:289
  133.0 45.7 %collective-permute-start.29 = (bf16[256,1024]{1,0:T(8,128)(2,1)S(1)}, bf16[256,1024]{1,0:T(8,128)(2,1)S(1)}, u32[]{:S(2)}, u32[]{:S(2)}) collective-permute-start(bf16[256,1024]{1,0:T(8,128)(2,1)S(1)} %slice.339), channel_id=1, source_target_pairs={{1,5},{4,8},{8,12},{12,14},{14,10},{11,7},{7,3},{3,1},{17,21},{20,... | collective-permute-start | bytes 1572872 | tf_op jit(solution)/shard_map/ppermute | solution.py:289
  133.7 21.5 %collective-permute-start.31 = (bf16[128,1024]{1,0:T(8,128)(2,1)S(1)}, bf16[128,1024]{1,0:T(8,128)(2,1)S(1)}, u32[]{:S(2)}, u32[]{:S(2)}) collective-permute-start(bf16[128,1024]{1,0:T(8,128)(2,1)S(1)} %get-tuple-element.160), channel_id=1, source_target_pairs={{0,4},{4,8},{8,12},{12,14},{14,10},{10,6},{6,2},{2,0},{1,5},{5,9},... | collective-permute-start | bytes 786440 | tf_op jit(solution)/shard_map/ppermute | solution.py:55
  137.3 17.8 %collective-permute-start.32 = (bf16[128,1024]{1,0:T(8,128)(2,1)S(1)}, bf16[128,1024]{1,0:T(8,128)(2,1)S(1)}, u32[]{:S(2)}, u32[]{:S(2)}) collective-permute-start(bf16[128,1024]{1,0:T(8,128)(2,1)S(1)} %get-tuple-element.161), channel_id=1, source_target_pairs={{0,2},{4,0},{8,4},{12,8},{14,12},{10,14},{6,10},{2,6},{1,3},{5,1},... | collective-permute-start | bytes 786440 | tf_op jit(solution)/shard_map/ppermute | solution.py:55
  155.4 20.5 %collective-permute-start.33 = (bf16[256,1024]{1,0:T(8,128)(2,1)S(1)}, bf16[256,1024]{1,0:T(8,128)(2,1)S(1)}, u32[]{:S(2)}, u32[]{:S(2)}) collective-permute-start(bf16[256,1024]{1,0:T(8,128)(2,1)S(1)} %pad_maximum_fusion.3), channel_id=1, source_target_pairs={{0,4},{4,8},{8,12},{12,14},{14,10},{10,6},{6,2},{2,0},{1,5},{5,9},... | collective-permute-start | bytes 1572872 | tf_op jit(solution)/shard_map/ppermute | solution.py:55
  157.6 18.4 %collective-permute-start.34 = (bf16[256,1024]{1,0:T(8,128)(2,1)S(1)}, bf16[256,1024]{1,0:T(8,128)(2,1)S(1)}, u32[]{:S(2)}, u32[]{:S(2)}) collective-permute-start(bf16[256,1024]{1,0:T(8,128)(2,1)S(1)} %pad_maximum_fusion.4), channel_id=1, source_target_pairs={{0,2},{4,0},{8,4},{12,8},{14,12},{10,14},{6,10},{2,6},{1,3},{5,1},... | collective-permute-start | bytes 1572872 | tf_op jit(solution)/shard_map/ppermute | solution.py:55
  176.4 14.3 %collective-permute-start.36 = (bf16[256,1024]{1,0:T(8,128)(2,1)S(1)}, bf16[256,1024]{1,0:T(8,128)(2,1)S(1)}, u32[]{:S(2)}, u32[]{:S(2)}) collective-permute-start(bf16[256,1024]{1,0:T(8,128)(2,1)S(1)} %get-tuple-element.217), channel_id=1, source_target_pairs={{0,2},{4,0},{8,4},{12,8},{14,12},{10,14},{6,10},{2,6},{1,3},{5,1},... | collective-permute-start | bytes 1572872 | tf_op jit(solution)/shard_map/ppermute | solution.py:55
  176.4 14.8 %collective-permute-start.35 = (bf16[256,1024]{1,0:T(8,128)(2,1)S(1)}, bf16[256,1024]{1,0:T(8,128)(2,1)S(1)}, u32[]{:S(2)}, u32[]{:S(2)}) collective-permute-start(bf16[256,1024]{1,0:T(8,128)(2,1)S(1)} %get-tuple-element.218), channel_id=1, source_target_pairs={{0,4},{4,8},{8,12},{12,14},{14,10},{10,6},{6,2},{2,0},{1,5},{5,9},... | collective-permute-start | bytes 1572872 | tf_op jit(solution)/shard_map/ppermute | solution.py:55
  191.6 4.4 %collective-permute-start.37 = (bf16[2,256,2048]{2,1,0:T(8,128)(2,1)S(1)}, bf16[2,256,2048]{2,1,0:T(8,128)(2,1)S(1)}, u32[]{:S(2)}, u32[]{:S(2)}) collective-permute-start(bf16[2,256,2048]{2,1,0:T(8,128)(2,1)S(1)} %get-tuple-element.184), channel_id=1, source_target_pairs={{0,1},{1,0},{2,3},{3,2},{4,5},{5,4},{6,7},{7,6},{8,9},{9,8},{10,11... | collective-permute-start | bytes 6291464 | tf_op jit(solution)/shard_map/ppermute | solution.py:59
  191.8 4.2 %collective-permute-start.38 = (f32[256,128]{1,0:T(8,128)S(1)}, f32[256,128]{1,0:T(8,128)S(1)}, u32[]{:S(2)}, u32[]{:S(2)}) collective-permute-start(f32[256,128]{1,0:T(8,128)S(1)} %get-tuple-element.185), channel_id=1, source_target_pairs={{0,1},{1,0},{2,3},{3,2},{4,5},{5,4},{6,7},{7,6},{8,9},{9,8},{10,11... | collective-permute-start | bytes 393224 | tf_op jit(solution)/shard_map/ppermute | solution.py:59
  209.2 5.8 %collective-permute-start.39 = (bf16[64,1024]{1,0:T(8,128)(2,1)S(1)}, bf16[64,1024]{1,0:T(8,128)(2,1)S(1)}, u32[]{:S(2)}, u32[]{:S(2)}) collective-permute-start(bf16[64,1024]{1,0:T(8,128)(2,1)S(1)} %get-tuple-element.188), channel_id=1, source_target_pairs={{0,4},{4,8},{8,12},{12,14},{14,10},{10,6},{6,2},{2,0},{1,5},{5,9},... | collective-permute-start | bytes 393224 | tf_op jit(solution)/shard_map/ppermute | solution.py:55
  211.0 6.3 %collective-permute-start.40 = (bf16[64,1024]{1,0:T(8,128)(2,1)S(1)}, bf16[64,1024]{1,0:T(8,128)(2,1)S(1)}, u32[]{:S(2)}, u32[]{:S(2)}) collective-permute-start(bf16[64,1024]{1,0:T(8,128)(2,1)S(1)} %get-tuple-element.189), channel_id=1, source_target_pairs={{0,2},{4,0},{8,4},{12,8},{14,12},{10,14},{6,10},{2,6},{1,3},{5,1},... | collective-permute-start | bytes 393224 | tf_op jit(solution)/shard_map/ppermute | solution.py:55
  211.3 20.3 %collective-permute-start.43 = (bf16[256,1024]{1,0:T(8,128)(2,1)S(1)}, bf16[256,1024]{1,0:T(8,128)(2,1)S(1)}, u32[]{:S(2)}, u32[]{:S(2)}) collective-permute-start(bf16[256,1024]{1,0:T(8,128)(2,1)S(1)} %get-tuple-element.215), channel_id=1, source_target_pairs={{0,4},{4,8},{8,12},{12,14},{14,10},{10,6},{6,2},{2,0},{1,5},{5,9},... | collective-permute-start | bytes 1572872 | tf_op jit(solution)/shard_map/ppermute | solution.py:55
  213.0 20.2 %collective-permute-start.44 = (bf16[256,1024]{1,0:T(8,128)(2,1)S(1)}, bf16[256,1024]{1,0:T(8,128)(2,1)S(1)}, u32[]{:S(2)}, u32[]{:S(2)}) collective-permute-start(bf16[256,1024]{1,0:T(8,128)(2,1)S(1)} %get-tuple-element.216), channel_id=1, source_target_pairs={{0,2},{4,0},{8,4},{12,8},{14,12},{10,14},{6,10},{2,6},{1,3},{5,1},... | collective-permute-start | bytes 1572872 | tf_op jit(solution)/shard_map/ppermute | solution.py:55
  213.3 15.7 %collective-permute-start.41 = (bf16[64,1024]{1,0:T(8,128)(2,1)S(1)}, bf16[64,1024]{1,0:T(8,128)(2,1)S(1)}, u32[]{:S(2)}, u32[]{:S(2)}) collective-permute-start(bf16[64,1024]{1,0:T(8,128)(2,1)S(1)} %get-tuple-element.192), channel_id=1, source_target_pairs={{0,4},{4,8},{8,12},{12,14},{14,10},{10,6},{6,2},{2,0},{1,5},{5,9},... | collective-permute-start | bytes 393224 | tf_op jit(solution)/shard_map/ppermute | solution.py:55
  215.1 15.9 %collective-permute-start.42 = (bf16[64,1024]{1,0:T(8,128)(2,1)S(1)}, bf16[64,1024]{1,0:T(8,128)(2,1)S(1)}, u32[]{:S(2)}, u32[]{:S(2)}) collective-permute-start(bf16[64,1024]{1,0:T(8,128)(2,1)S(1)} %get-tuple-element.193), channel_id=1, source_target_pairs={{0,2},{4,0},{8,4},{12,8},{14,12},{10,14},{6,10},{2,6},{1,3},{5,1},... | collective-permute-start | bytes 393224 | tf_op jit(solution)/shard_map/ppermute | solution.py:55
  217.4 27.9 %collective-permute-start.45 = (bf16[128,1024]{1,0:T(8,128)(2,1)S(1)}, bf16[128,1024]{1,0:T(8,128)(2,1)S(1)}, u32[]{:S(2)}, u32[]{:S(2)}) collective-permute-start(bf16[128,1024]{1,0:T(8,128)(2,1)S(1)} %pad_maximum_fusion.5), channel_id=1, source_target_pairs={{0,4},{4,8},{8,12},{12,14},{14,10},{10,6},{6,2},{2,0},{1,5},{5,9},... | collective-permute-start | bytes 786440 | tf_op jit(solution)/shard_map/ppermute | solution.py:55
  229.0 16.2 %collective-permute-start.46 = (bf16[128,1024]{1,0:T(8,128)(2,1)S(1)}, bf16[128,1024]{1,0:T(8,128)(2,1)S(1)}, u32[]{:S(2)}, u32[]{:S(2)}) collective-permute-start(bf16[128,1024]{1,0:T(8,128)(2,1)S(1)} %pad_maximum_fusion.6), channel_id=1, source_target_pairs={{0,2},{4,0},{8,4},{12,8},{14,12},{10,14},{6,10},{2,6},{1,3},{5,1},... | collective-permute-start | bytes 786440 | tf_op jit(solution)/shard_map/ppermute | solution.py:55
  231.1 16.5 %collective-permute-start.51 = (bf16[128,1024]{1,0:T(8,128)(2,1)S(1)}, bf16[128,1024]{1,0:T(8,128)(2,1)S(1)}, u32[]{:S(2)}, u32[]{:S(2)}) collective-permute-start(bf16[128,1024]{1,0:T(8,128)(2,1)S(1)} %pad_maximum_fusion.7), channel_id=1, source_target_pairs={{0,4},{4,8},{8,12},{12,14},{14,10},{10,6},{6,2},{2,0},{1,5},{5,9},... | collective-permute-start | bytes 786440 | tf_op jit(solution)/shard_map/ppermute | solution.py:55
  231.6 16.0 %collective-permute-start.52 = (bf16[128,1024]{1,0:T(8,128)(2,1)S(1)}, bf16[128,1024]{1,0:T(8,128)(2,1)S(1)}, u32[]{:S(2)}, u32[]{:S(2)}) collective-permute-start(bf16[128,1024]{1,0:T(8,128)(2,1)S(1)} %pad_maximum_fusion.8), channel_id=1, source_target_pairs={{0,2},{4,0},{8,4},{12,8},{14,12},{10,14},{6,10},{2,6},{1,3},{5,1},... | collective-permute-start | bytes 786440 | tf_op jit(solution)/shard_map/ppermute | solution.py:55
  245.5 6.4 %collective-permute-start.48 = (bf16[128,1024]{1,0:T(8,128)(2,1)S(1)}, bf16[128,1024]{1,0:T(8,128)(2,1)S(1)}, u32[]{:S(2)}, u32[]{:S(2)}) collective-permute-start(bf16[128,1024]{1,0:T(8,128)(2,1)S(1)} %get-tuple-element.213), channel_id=1, source_target_pairs={{0,2},{4,0},{8,4},{12,8},{14,12},{10,14},{6,10},{2,6},{1,3},{5,1},... | collective-permute-start | bytes 786440 | tf_op jit(solution)/shard_map/ppermute | solution.py:55
  245.6 20.7 %copy-start.31 = (bf16[512,1024]{1,0:T(8,128)(2,1)S(1)}, bf16[512,1024]{1,0:T(8,128)(2,1)}, u32[]{:S(2)}) copy-start(bf16[512,1024]{1,0:T(8,128)(2,1)} %param.11) | copy-start | bytes 3145732
  245.6 7.0 %collective-permute-start.47 = (bf16[128,1024]{1,0:T(8,128)(2,1)S(1)}, bf16[128,1024]{1,0:T(8,128)(2,1)S(1)}, u32[]{:S(2)}, u32[]{:S(2)}) collective-permute-start(bf16[128,1024]{1,0:T(8,128)(2,1)S(1)} %get-tuple-element.214), channel_id=1, source_target_pairs={{0,4},{4,8},{8,12},{12,14},{14,10},{10,6},{6,2},{2,0},{1,5},{5,9},... | collective-permute-start | bytes 786440 | tf_op jit(solution)/shard_map/ppermute | solution.py:55
  252.9 9.1 %collective-permute-start.54 = (bf16[128,1024]{1,0:T(8,128)(2,1)S(1)}, bf16[128,1024]{1,0:T(8,128)(2,1)S(1)}, u32[]{:S(2)}, u32[]{:S(2)}) collective-permute-start(bf16[128,1024]{1,0:T(8,128)(2,1)S(1)} %get-tuple-element.210), channel_id=1, source_target_pairs={{0,2},{4,0},{8,4},{12,8},{14,12},{10,14},{6,10},{2,6},{1,3},{5,1},... | collective-permute-start | bytes 786440 | tf_op jit(solution)/shard_map/ppermute | solution.py:55
  254.7 9.2 %collective-permute-start.53 = (bf16[128,1024]{1,0:T(8,128)(2,1)S(1)}, bf16[128,1024]{1,0:T(8,128)(2,1)S(1)}, u32[]{:S(2)}, u32[]{:S(2)}) collective-permute-start(bf16[128,1024]{1,0:T(8,128)(2,1)S(1)} %get-tuple-element.211), channel_id=1, source_target_pairs={{0,4},{4,8},{8,12},{12,14},{14,10},{10,6},{6,2},{2,0},{1,5},{5,9},... | collective-permute-start | bytes 786440 | tf_op jit(solution)/shard_map/ppermute | solution.py:55
  255.0 12.1 %collective-permute-start.50 = (bf16[128,1024]{1,0:T(8,128)(2,1)S(1)}, bf16[128,1024]{1,0:T(8,128)(2,1)S(1)}, u32[]{:S(2)}, u32[]{:S(2)}) collective-permute-start(bf16[128,1024]{1,0:T(8,128)(2,1)S(1)} %get-tuple-element.209), channel_id=1, source_target_pairs={{0,2},{4,0},{8,4},{12,8},{14,12},{10,14},{6,10},{2,6},{1,3},{5,1},... | collective-permute-start | bytes 786440 | tf_op jit(solution)/shard_map/ppermute | solution.py:55
  256.8 12.8 %collective-permute-start.49 = (bf16[128,1024]{1,0:T(8,128)(2,1)S(1)}, bf16[128,1024]{1,0:T(8,128)(2,1)S(1)}, u32[]{:S(2)}, u32[]{:S(2)}) collective-permute-start(bf16[128,1024]{1,0:T(8,128)(2,1)S(1)} %get-tuple-element.212), channel_id=1, source_target_pairs={{0,4},{4,8},{8,12},{12,14},{14,10},{10,6},{6,2},{2,0},{1,5},{5,9},... | collective-permute-start | bytes 786440 | tf_op jit(solution)/shard_map/ppermute | solution.py:55
  264.2 9.1 %collective-permute-start.55 = (bf16[128,1024]{1,0:T(8,128)(2,1)S(1)}, bf16[128,1024]{1,0:T(8,128)(2,1)S(1)}, u32[]{:S(2)}, u32[]{:S(2)}) collective-permute-start(bf16[128,1024]{1,0:T(8,128)(2,1)S(1)} %get-tuple-element.207), channel_id=1, source_target_pairs={{0,4},{4,8},{8,12},{12,14},{14,10},{10,6},{6,2},{2,0},{1,5},{5,9},... | collective-permute-start | bytes 786440 | tf_op jit(solution)/shard_map/ppermute | solution.py:55
  264.5 8.8 %collective-permute-start.56 = (bf16[128,1024]{1,0:T(8,128)(2,1)S(1)}, bf16[128,1024]{1,0:T(8,128)(2,1)S(1)}, u32[]{:S(2)}, u32[]{:S(2)}) collective-permute-start(bf16[128,1024]{1,0:T(8,128)(2,1)S(1)} %get-tuple-element.208), channel_id=1, source_target_pairs={{0,2},{4,0},{8,4},{12,8},{14,12},{10,14},{6,10},{2,6},{1,3},{5,1},... | collective-permute-start | bytes 786440 | tf_op jit(solution)/shard_map/ppermute | solution.py:55
  (26 other events, 222.3 us)

commit v5 on v4

v5 whole, which is shorter than its diff:
```python
import functools

import jax
import jax.numpy as jnp
import numpy as np
from jax import lax
from jax.experimental import pallas as pl
from jax.experimental.pallas import tpu as pltpu
from jax.sharding import PartitionSpec as P

VMEM_LIMIT = 50 * 1024 * 1024
DEEP, PARTS = 3, 4
LANES = 128


def ring_of(count):
    if count == 8:
        return [0, 2, 4, 6, 7, 5, 3, 1]
    return list(range(count))


def send_order(count):
    half = count // 2
    order = [half]
    for step in range(half - 1, 0, -1):
        order += [step, count - step]
    return order + [0]


def arrival_order(count):
    half = count // 2
    order = [0]
    for step in range(1, half):
        order += [-step, step]
    return order + [half]


def tables_of(count):
    ring = ring_of(count)
    place = {block: index for index, block in enumerate(ring)}
    half = count // 2
    table = np.zeros((2, count, 2, 3, count), np.int32)
    for which, order in enumerate((arrival_order(count), send_order(count))):
        for block in range(count):
            for core in range(2):
                for index, distance in enumerate(order):
                    target = ring[(place[block] + distance) % count]
                    table[which, block, core, :, index] = target // half == core, target % half, target
    return table


def ring_shift(value, steps):
    ring = ring_of(lax.axis_size("blk"))
    count = len(ring)
    return lax.ppermute(value, "blk", [(ring[i], ring[(i + steps) % count]) for i in range(count)])


def swap(value):
    return lax.ppermute(value, "seq", [(0, 1), (1, 0)])


def after(value, *earlier):
    return lax.optimization_barrier((value, earlier))[0]


def gate_up_kernel(columns, steps, mean_of, blocks_ref, *refs):
    refs = list(refs)
    stacked, gate, inv, weights, sems, weight_sems = refs[-6:]
    out_ref = refs[-7]
    gains_ref = refs[-12]
    sources = [refs[-11:-9], refs[-9:-7]]
    pieces = refs[:-12]
    count, width = gains_ref.shape[0], gains_ref.shape[2]
    step = pl.program_id(0) * 2 + pl.program_id(1)
    tile = weights.shape[-1]

    def fetch(number, act):
        slot, which = lax.rem(number, DEEP), lax.rem(number, 2)
        column = pl.multiple_of(columns + lax.div(number, 2) * tile, tile)
        for index in range(count):
            row = pl.multiple_of(blocks_ref[1, index] * width, width)
            for gate_or_up in range(2):
                for other in range(2):

                    @pl.when((which == gate_or_up) & (blocks_ref[0, index] == 1 - other))
                    def chosen(index=index, row=row, source=sources[gate_or_up][other]):
                        act(
                            pltpu.make_async_copy(
                                source.at[pl.ds(row, width), pl.ds(column, tile)],
                                weights.at[slot, pl.ds(index * width, width)],
                                weight_sems.at[slot, index],
                            )
                        )

    def gather_pieces(act):
        start = 0
        for number, source in enumerate(pieces):
            size = source.shape[0]
            row = start % stacked.shape[0]
            target = stacked.at[pl.ds(row, size), pl.ds((start // stacked.shape[0]) * width, width)]
            act(pltpu.make_async_copy(source, target, sems.at[number]))
            start += size

    @pl.when(step == 0)
    def first():
        gather_pieces(lambda copy: copy.start())
        for number in range(min(DEEP - 1, steps)):
            fetch(jnp.int32(number), lambda copy: copy.start())
        gather_pieces(lambda copy: copy.wait())
        stat = jnp.zeros((stacked.shape[0], LANES), jnp.float32)
        for index in range(count):
            gain = gains_ref[blocks_ref[2, index]]
            weight = 1.0 / (gain * gain)
            for column in range(0, width, LANES):
                value = stacked[:, index * width + column : index * width + column + LANES].astype(jnp.float32)
                stat = stat + value * value * weight[:, column : column + LANES]
        total = jnp.sum(stat, axis=1, keepdims=True)
        inv[...] = jnp.broadcast_to(lax.rsqrt(total / mean_of + 1e-05), inv.shape)

    @pl.when(step + DEEP - 1 < steps)
    def ahead():
        fetch(step + DEEP - 1, lambda copy: copy.start())

    fetch(step, lambda copy: copy.wait())
    total = jnp.dot(stacked[...], weights[lax.rem(step, DEEP)], preferred_element_type=jnp.float32) * inv[:, :1]

    @pl.when(pl.program_id(1) == 0)
    def keep():
        gate[...] = total

    @pl.when(pl.program_id(1) == 1)
    def activate():
        value = gate[...]
        out_ref[...] = (value / (1.0 + jnp.exp(-value)) * total).astype(jnp.bfloat16)


def gate_up(part, blocks, pieces, gains, weights):
    rows, width = pieces[0].shape
    count = blocks.shape[1]
    columns = weights[0].shape[1] // 2
    tile = min(256, columns)
    steps = 2 * (columns // tile)
    anywhere = pl.BlockSpec(memory_space=pl.ANY)
    return pl.pallas_call(
        functools.partial(gate_up_kernel, part * columns, steps, width * count),
        out_shape=jax.ShapeDtypeStruct((rows, columns), jnp.bfloat16),
        grid_spec=pltpu.PrefetchScalarGridSpec(
            num_scalar_prefetch=1,
            grid=(columns // tile, 2),
            in_specs=[
                *[anywhere] * len(pieces),
                pl.BlockSpec(gains.shape, lambda n, w, blocks: (0, 0, 0)),
                *[anywhere] * 4,
            ],
            out_specs=pl.BlockSpec((rows, tile), lambda n, w, blocks: (0, n)),
            scratch_shapes=[
                pltpu.VMEM((rows, count * width), jnp.bfloat16),
                pltpu.VMEM((rows, tile), jnp.float32),
                pltpu.VMEM((rows, LANES), jnp.float32),
                pltpu.VMEM((DEEP, count * width, tile), jnp.bfloat16),
                pltpu.SemaphoreType.DMA((len(pieces),)),
                pltpu.SemaphoreType.DMA((DEEP, count)),
            ],
        ),
        compiler_params=pltpu.CompilerParams(vmem_limit_bytes=VMEM_LIMIT),
        cost_estimate=pl.CostEstimate(
            flops=8 * rows * count * width * columns,
            bytes_accessed=4 * count * width * columns,
            transcendentals=rows * columns,
        ),
        name="gate_up",
    )(blocks, *pieces, gains, *weights)


def down_kernel(start, steps, tiles_ref, first_ref, second_ref, local_ref, other_ref, out_ref, hidden, buffer, sems):
    step = pl.program_id(0)
    depth, width = buffer.shape[1:]

    def fetch(number, act):
        slot = lax.rem(number, DEEP)
        for kind, source in ((1, local_ref), (0, other_ref)):

            @pl.when(tiles_ref[0, number + start] == kind)
            def chosen(source=source):
                column = pl.multiple_of(tiles_ref[1, number + start] * width, width)
                for part in range(PARTS):
                    row = pl.ds(part * (depth // PARTS), depth // PARTS)
                    act(
                        pltpu.make_async_copy(
                            source.at[row, pl.ds(column, width)], buffer.at[slot, row], sems.at[slot, part]
                        )
                    )

    @pl.when(step == 0)
    def first():
        for number in range(min(DEEP - 1, steps)):
            fetch(jnp.int32(number), lambda copy: copy.start())
        hidden[:, : depth // 2] = first_ref[...]
        hidden[:, depth // 2 :] = second_ref[...]

    @pl.when(step + DEEP - 1 < steps)
    def ahead():
        fetch(step + DEEP - 1, lambda copy: copy.start())

    fetch(step, lambda copy: copy.wait())
    weight = buffer[lax.rem(step, DEEP)]
    out_ref[0] = jnp.dot(hidden[...], weight, preferred_element_type=jnp.float32).astype(jnp.bfloat16)


def down(start, stop, tiles, hidden, local, other, width):
    rows = hidden[0].shape[0]
    depth = local.shape[0]
    half_spec = pl.BlockSpec((rows, depth // 2), lambda j, tiles: (0, 0))
    anywhere = pl.BlockSpec(memory_space=pl.ANY)
    return pl.pallas_call(
        functools.partial(down_kernel, start, stop - start),
        out_shape=jax.ShapeDtypeStruct((stop - start, rows, width), jnp.bfloat16),
        grid_spec=pltpu.PrefetchScalarGridSpec(
            num_scalar_prefetch=1,
            grid=(stop - start,),
            in_specs=[half_spec, half_spec, anywhere, anywhere],
            out_specs=pl.BlockSpec((1, rows, width), lambda j, tiles: (j, 0, 0)),
            scratch_shapes=[
                pltpu.VMEM((rows, depth), jnp.bfloat16),
                pltpu.VMEM((DEEP, depth, width), jnp.bfloat16),
                pltpu.SemaphoreType.DMA((DEEP, PARTS)),
            ],
        ),
        compiler_params=pltpu.CompilerParams(vmem_limit_bytes=VMEM_LIMIT),
        cost_estimate=pl.CostEstimate(
            flops=4 * rows * depth * width * (stop - start),
            bytes_accessed=2 * depth * width * (stop - start),
            transcendentals=0,
        ),
        name="down",
    )(tiles, *hidden, local, other)


def gather_step(block, steps, half, *earlier):
    before, behind = after(steps[-1] if steps else (block, block), *earlier)
    if len(steps) == half - 1:
        cut = block.shape[0] // 2
        before, behind = before[:cut], behind[cut:]
    return [*steps, (ring_shift(before, 1), ring_shift(behind, -1))]


def joined(one, two):
    return (one.astype(jnp.float32) + two.astype(jnp.float32)).astype(jnp.bfloat16)


def scatter_sums(moved, term, count, distance, *earlier):
    half = count // 2
    ahead, behind = term(distance), term(count - distance)
    cut = ahead.shape[0] // 2
    if distance == half:
        return after((ahead[:cut], behind[cut:]), *earlier)
    forth, back = after(moved, *earlier)
    if distance == half - 1:
        forth = jnp.concatenate([joined(ahead[:cut], forth), ahead[cut:]], axis=0)
        back = jnp.concatenate([behind[:cut], joined(behind[cut:], back)], axis=0)
        return forth, back
    return joined(ahead, forth), joined(behind, back)


def scatter_send(sums):
    return ring_shift(sums[0], 1), ring_shift(sums[1], -1)


def on_device(
    noisy_input,
    self_cond,
    cond_gain,
    bucket,
    conv_taps,
    norm_gain,
    gate_weight,
    up_weight,
    down_weight,
):
    row_count, width = noisy_input.shape
    count = lax.axis_size("blk")
    half = count // 2
    core, own = lax.axis_index("seq"), lax.axis_index("blk")
    blocks, tiles = jnp.asarray(tables_of(count))[:, own, core]
    order = send_order(count)
    gains = norm_gain.reshape(count, 1, width)

    lead_rows = conv_taps.shape[1] - 1
    edges = lax.ppermute(
        (noisy_input[row_count - lead_rows :], self_cond[row_count - lead_rows :]), "seq", [(0, 1)]
    )
    other_gate, other_up, other_down = (swap(weight) for weight in (gate_weight, up_weight, down_weight))
    weights = (gate_weight, other_gate, up_weight, other_up)
    chosen = lax.dynamic_index_in_dim(conv_taps, bucket[0], 0, keepdims=False)
    own_gain = lax.dynamic_slice_in_dim(norm_gain, own * width, width, 0)

    def mix(noisy, cond):
        return noisy.astype(jnp.float32) + cond_gain * cond.astype(jnp.float32)

    def convolve(noisy, cond, edge, start, size):
        if start == 0:
            extended = jnp.concatenate([mix(*edge), mix(noisy[:size], cond[:size])], axis=0)
        else:
            where = slice(start - lead_rows, start + size)
            extended = mix(noisy[where], cond[where])
        result = jnp.zeros((size, width), jnp.float32)
        for shift_by in range(lead_rows + 1):
            result = result + chosen[shift_by] * lax.slice_in_dim(
                extended, lead_rows - shift_by, lead_rows - shift_by + size, axis=0
            )
        return (result.astype(jnp.bfloat16).astype(jnp.float32) * own_gain).astype(jnp.bfloat16)

    size = row_count // 2
    early = min(3, count - 1)

    def matmul(part, block, steps, *earlier):
        pieces = after([block, *(piece for step in steps for piece in step)], *earlier)
        return gate_up(part, blocks, pieces, gains, weights)

    def open_down(hidden, *earlier):
        return down(0, early, tiles, after(hidden, *earlier), down_weight, other_down, width)

    def close_down(hidden, *earlier):
        return down(early, count, tiles, after(hidden, *earlier), down_weight, other_down, width)

    def term_of(opened, closed, rows=slice(None)):
        def term(distance):
            index = order.index(distance)
            return (opened[index] if index < early else closed[index - early])[rows]

        return term

    block_a = convolve(noisy_input, self_cond, edges, size, size)
    steps_a = gather_step(block_a, [], half)
    later = after((noisy_input, self_cond, edges), steps_a[0])
    block_b = convolve(*later, 0, size)
    while len(steps_a) < half - 1:
        steps_a = gather_step(block_a, steps_a, half)
    steps_b = gather_step(block_b, [], half, steps_a[min(1, half - 2)])
    steps_a = gather_step(block_a, steps_a, half)
    hidden_a = [matmul(0, block_a, steps_a)]
    first_b = steps_b[-1]
    steps_b = gather_step(block_b, steps_b, half, hidden_a)
    hidden_a += [matmul(1, block_a, steps_a, hidden_a, first_b)]
    second_b = steps_b[-1]
    steps_b = gather_step(block_b, steps_b, half, hidden_a)
    opened_a = open_down(hidden_a, second_b)
    while len(steps_b) < half - 1:
        steps_b = gather_step(block_b, steps_b, half)
    third_b = steps_b[-1]
    closed_a = close_down(hidden_a, opened_a, third_b)
    steps_b = gather_step(block_b, steps_b, half, opened_a)
    term_a = term_of(opened_a, closed_a)
    distances = list(range(half - 1, 0, -1))
    moved_a = scatter_send(scatter_sums(None, term_a, count, half, third_b))
    sums_a = scatter_sums(moved_a, term_a, count, distances.pop(0))
    hidden_b = [matmul(0, block_b, steps_b, closed_a, sums_a)]
    sums_a = scatter_sums(scatter_send(sums_a), term_a, count, distances.pop(0))
    hidden_b += [matmul(1, block_b, steps_b, hidden_b, sums_a)]
    for distance in distances:
        sums_a = scatter_sums(scatter_send(sums_a), term_a, count, distance)
    opened_b = open_down(hidden_b, sums_a)
    moved_a = scatter_send(sums_a)
    spans = [slice(0, size // 2), slice(size // 2, size)]
    distances = list(range(half, 0, -1))
    parts_b = [None, None]
    closed_b = None
    for number, distance in enumerate(distances):
        earlier = []
        for which, span in enumerate(spans):
            moved = scatter_send(parts_b[which]) if number else None
            parts_b[which] = scatter_sums(moved, term_of(opened_b, closed_b, span), count, distance, earlier)
            earlier = parts_b[which]
        if number == 1:
            closed_b = close_down(hidden_b, parts_b, moved_a)
    moved_b = [scatter_send(part) for part in parts_b]
    terms_b = [term_of(opened_b, closed_b, span) for span in spans]

    def finish(start, term, moved):
        ffn = term(0).astype(jnp.float32) + moved[0].astype(jnp.float32) + moved[1].astype(jnp.float32)
        rows = slice(start, start + ffn.shape[0])
        return (mix(noisy_input[rows], self_cond[rows]) + ffn).astype(jnp.bfloat16)

    outs = [finish(span.start, term, moved) for span, term, moved in zip(spans, terms_b, moved_b)]
    return jnp.concatenate([*outs, finish(size, term_a, moved_a)], axis=0)


def solution(mesh):
    in_specs = (
        P(("groups", "seq"), "blk"),
        P(("groups", "seq"), "blk"),
        P("blk"),
        P("groups"),
        P(None, None, "blk"),
        P(),
        P("seq", "blk"),
        P("seq", "blk"),
        P("blk", "seq"),
    )
    out_specs = P(("groups", "seq"), "blk")
    return jax.shard_map(
        on_device, mesh=mesh, in_specs=in_specs, out_specs=out_specs, check_vma=False
    )
```

time: 276 us -> 241 us (0.87)
  starting transfers between devices: 89.6 us -> 46 us
  waiting for transfers between devices: 53 us -> 86.4 us
  local copies, waits for them, and re-layouts: 30.4 us -> 3.98 us
    ppermute x24 -> x0, starting transfers between devices: 48.4 us -> none  [carry(): return lax.ppermute(value, ('blk', 'seq'), route)]
    ppermute x24 -> x40, waiting for transfers between devices: 33.4 us -> 75.6 us  [ring_shift(): lax.ppermute(value, 'blk', [(ring[i], ring[(i + steps) % count]) for i in...]
    unnamed x66 -> x16, local copies, waits for them, and re-layouts: 24 us -> 0.03 us
    ppermute x24 -> x0, waiting for transfers between devices: 15.4 us -> none  [carry(): return lax.ppermute(value, ('blk', 'seq'), route)]
    ppermute x24 -> x40, starting transfers between devices: 28.6 us -> 42.5 us  [ring_shift(): lax.ppermute(value, 'blk', [(ring[i], ring[(i + steps) % count]) for i in...]
    ppermute x2, waiting for transfers between devices: 0.01 us -> 10.8 us  [on_device(): lax.ppermute((noisy_input[row_count - lead_rows:], self_cond[row_count -...]
    ppermute x7 -> x3, starting transfers between devices: 10.1 us -> 0.96 us  [swap(): return lax.ppermute(value, 'seq', [(0, 1), (1, 0)])]
    ppermute x7 -> x3, waiting for transfers between devices: 4.16 us -> 0.01 us  [swap(): return lax.ppermute(value, 'seq', [(0, 1), (1, 0)])]
  transfers between devices with their start and end apart: 57 -> 45, of which waited for: 21 -> 20; matrix products, arithmetic and copies ran while one was open for 4% -> 4% of each run, Pallas kernels for 31% -> 37%
where the time goes in v5:
time: 241 us
  Pallas kernels  95.2 us (40%)
  waiting for transfers between devices  86.4 us (36%)
  starting transfers between devices  46 us (19%)
  other arithmetic  8.03 us (3%)
  local copies, waits for them, and re-layouts  3.98 us (2%)
    ppermute x40, waiting for transfers between devices, ring_shift(): lax.ppermute(value, 'blk', [(ring[i], ring[(i + steps) % count]) for i in...  75.6 us
    pallas_call x4, Pallas kernels, gate_up(): pl.pallas_call(functools.partial(gate_up_kernel, part * columns, steps, w...  63 us
    ppermute x40, starting transfers between devices, ring_shift(): lax.ppermute(value, 'blk', [(ring[i], ring[(i + steps) % count]) for i in...  42.5 us
    pallas_call x4, Pallas kernels, down(): pl.pallas_call(functools.partial(down_kernel, start, stop - start), out_s...  32.2 us
    ppermute x2, waiting for transfers between devices, on_device(): lax.ppermute((noisy_input[row_count - lead_rows:], self_cond[row_count -...  10.8 us
  transfers between devices with their start and end apart: 45, of which 20 were waited for; matrix products, arithmetic and copies ran while one was open for 4% of the time, Pallas kernels for 37%

profile of v5, /device:TPU:0, one launch (start us, length us, event | category | flops | bytes accessed | tf_op | source)
XLA Modules:
  0.0 240.6 jit_solution(11482785409956741946)
XLA Ops:
  1.6 0.7 dynamic_slice.12
  2.3 0.9 constant_dynamic-slice_fusion.2
  3.2 1.5 multiply_add_fusion
  5.2 2.6 %collective-permute-start.2 = (bf16[256,1024]{1,0:T(8,128)(2,1)S(1)}, bf16[256,1024]{1,0:T(8,128)(2,1)S(1)}, u32[]{:S(2)}, u32[]{:S(2)}) collective-permute-start(bf16[256,1024]{1,0:T(8,128)(2,1)S(1)} %multiply_convert_fusion.1.refs_0_), channel_id=1, source_target_pairs={{0,4},{4,8},{8,12},{12,14},{14,10},{10,6},{6,2},{2,0},{1,5},{5,9},... | collective-permute-start | bytes 1572872 | tf_op jit(solution)/shard_map/ppermute | solution.py:55
  7.9 12.5 %collective-permute-done.2.refs_1_ = bf16[256,1024]{1,0:T(8,128)(2,1)S(1)} collective-permute-done((bf16[256,1024]{1,0:T(8,128)(2,1)S(1)}, bf16[256,1024]{1,0:T(8,128)(2,1)S(1)}, u32[]{:S(2)}, u32[]{:S(2)}) %collective-permute-start.2) | collective-permute-done | bytes 524320 | tf_op jit(solution)/shard_map/ppermute | solution.py:55
  20.4 1.5 collective-permute-done.3.refs_2_
  21.9 1.6 collective-permute-start.4
  23.9 0.7 slice.316
  24.7 10.5 %collective-permute-done.4.refs_3_ = bf16[256,1024]{1,0:T(8,128)(2,1)S(1)} collective-permute-done((bf16[256,1024]{1,0:T(8,128)(2,1)S(1)}, bf16[256,1024]{1,0:T(8,128)(2,1)S(1)}, u32[]{:S(2)}, u32[]{:S(2)}) %collective-permute-start.4) | collective-permute-done | bytes 524320 | tf_op jit(solution)/shard_map/ppermute | solution.py:55
  35.1 1.3 collective-permute-start.1
  36.4 0.7 slice.315
  37.2 1.3 collective-permute-start
  38.5 10.8 %collective-permute-done.1 = bf16[3,1024]{1,0:T(4,128)(2,1)S(1)} collective-permute-done((bf16[3,1024]{1,0:T(4,128)(2,1)S(1)}, bf16[3,1024]{1,0:T(4,128)(2,1)S(1)}, u32[]{:S(2)}, u32[]{:S(2)}) %collective-permute-start.1) | collective-permute-done | bytes 6176 | tf_op jit(solution)/shard_map/ppermute | solution.py:289
  49.3 2.6 %collective-permute-start.8 = (bf16[256,1024]{1,0:T(8,128)(2,1)S(1)}, bf16[256,1024]{1,0:T(8,128)(2,1)S(1)}, u32[]{:S(2)}, u32[]{:S(2)}) collective-permute-start(bf16[256,1024]{1,0:T(8,128)(2,1)S(1)} %collective-permute-done.4.refs_3_), channel_id=1, source_target_pairs={{0,4},{4,8},{8,12},{12,14},{14,10},{10,6},{6,2},{2,0},{1,5},{5,9},... | collective-permute-start | bytes 1572872 | tf_op jit(solution)/shard_map/ppermute | solution.py:55
  51.8 0.7 dynamic-slice_bitcast_fusion
  52.6 1.4 multiply_add_fusion.1
  54.0 10.3 %collective-permute-done.8.refs_5_ = bf16[256,1024]{1,0:T(8,128)(2,1)S(1)} collective-permute-done((bf16[256,1024]{1,0:T(8,128)(2,1)S(1)}, bf16[256,1024]{1,0:T(8,128)(2,1)S(1)}, u32[]{:S(2)}, u32[]{:S(2)}) %collective-permute-start.8) | collective-permute-done | bytes 524320 | tf_op jit(solution)/shard_map/ppermute | solution.py:55
  64.2 1.5 collective-permute-done.9.refs_6_
  66.1 1.7 collective-permute-start.10
  68.4 4.9 %collective-permute-done.11.refs_8_ = bf16[128,1024]{1,0:T(8,128)(2,1)S(1)} collective-permute-done((bf16[128,1024]{1,0:T(8,128)(2,1)S(1)}, bf16[128,1024]{1,0:T(8,128)(2,1)S(1)}, u32[]{:S(2)}, u32[]{:S(2)}) %collective-permute-start.11) | collective-permute-done | bytes 262176 | tf_op jit(solution)/shard_map/ppermute | solution.py:55
  73.3 1.6 collective-permute-start.6
  75.4 15.8 %gate_up.4.first_ref = bf16[256,1024]{1,0:T(8,128)(2,1)S(1)} custom-call(s32[3,8]{1,0:T(4,128)S(1)} %get-tuple-element.217.blocks_ref, bf16[256,1024]{1,0:T(8,128)(2,1)S(1)} %multiply_convert_fusion.1.refs_0_, bf16[256,1024]{1,0:T(8,128)(2,1)S(1)} %collective-permute-done.2.refs_1_, bf16[256,1024]{1,0:T(8,128)(2,1)S(1)} %collective-permute-done.3.refs_2_, ...), custom_call_target="tpu_custom_call" | custom-call | flops 17179869184 | bytes 33554432 | tf_op jit(solution)/shard_map/gate_up/pallas_call | solution.py:144
  91.2 1.6 collective-permute-start.14
  93.3 15.8 %gate_up.5.second_ref = bf16[256,1024]{1,0:T(8,128)(2,1)S(1)} custom-call(s32[3,8]{1,0:T(4,128)S(1)} %get-tuple-element.217.blocks_ref, bf16[256,1024]{1,0:T(8,128)(2,1)S(1)} %multiply_convert_fusion.1.refs_0_, bf16[256,1024]{1,0:T(8,128)(2,1)S(1)} %collective-permute-done.2.refs_1_, bf16[256,1024]{1,0:T(8,128)(2,1)S(1)} %collective-permute-done.3.refs_2_, ...), custom_call_target="tpu_custom_call" | custom-call | flops 17179869184 | bytes 33554432 | tf_op jit(solution)/shard_map/gate_up/pallas_call | solution.py:144
  109.0 1.6 collective-permute-start.16
  111.1 6.7 %down.4 = bf16[3,256,1024]{2,1,0:T(8,128)(2,1)S(1)} custom-call(s32[3,8]{1,0:T(4,128)S(1)} %get-tuple-element.218.tiles_ref, bf16[256,1024]{1,0:T(8,128)(2,1)S(1)} %gate_up.4.first_ref, bf16[256,1024]{1,0:T(8,128)(2,1)S(1)} %gate_up.5.second_ref, bf16[2048,4096]{1,0:T(8,128)(2,1)} %local_ref.7, bf16[2048,4096]{1,0:T(8,128)(2,1)} %collective-permute-done.18.other_ref), custom_call_target="tpu_custom_call" | custom-call | flops 6442450944 | bytes 12582912 | tf_op jit(solution)/shard_map/down/pallas_call | solution.py:215
  118.0 2.2 collective-permute-done.16.refs_5_
  120.1 2.5 %collective-permute-done.17.refs_6_ = bf16[256,1024]{1,0:T(8,128)(2,1)S(1)} collective-permute-done((bf16[256,1024]{1,0:T(8,128)(2,1)S(1)}, bf16[256,1024]{1,0:T(8,128)(2,1)S(1)}, u32[]{:S(2)}, u32[]{:S(2)}) %collective-permute-start.17) | collective-permute-done | bytes 524320 | tf_op jit(solution)/shard_map/ppermute | solution.py:55
  123.2 1.6 collective-permute-start.19
  124.8 1.6 collective-permute-start.21
  126.8 9.3 %down.5 = bf16[5,256,1024]{2,1,0:T(8,128)(2,1)S(1)} custom-call(s32[3,8]{1,0:T(4,128)S(1)} %get-tuple-element.218.tiles_ref, bf16[256,1024]{1,0:T(8,128)(2,1)S(1)} %gate_up.4.first_ref, bf16[256,1024]{1,0:T(8,128)(2,1)S(1)} %gate_up.5.second_ref, bf16[2048,4096]{1,0:T(8,128)(2,1)} %local_ref.7, bf16[2048,4096]{1,0:T(8,128)(2,1)} %collective-permute-done.18.other_ref), custom_call_target="tpu_custom_call" | custom-call | flops 10737418240 | bytes 20971520 | tf_op jit(solution)/shard_map/down/pallas_call | solution.py:215
  136.5 1.8 collective-permute-start.23
  138.8 15.7 %gate_up.6.first_ref = bf16[256,1024]{1,0:T(8,128)(2,1)S(1)} custom-call(s32[3,8]{1,0:T(4,128)S(1)} %get-tuple-element.217.blocks_ref, bf16[256,1024]{1,0:T(8,128)(2,1)S(1)} %multiply_convert_fusion.refs_0_, bf16[256,1024]{1,0:T(8,128)(2,1)S(1)} %collective-permute-done.6.refs_1_, bf16[256,1024]{1,0:T(8,128)(2,1)S(1)} %collective-permute-done.7.refs_2_, ...), custom_call_target="tpu_custom_call" | custom-call | flops 17179869184 | bytes 33554432 | tf_op jit(solution)/shard_map/gate_up/pallas_call | solution.py:144
  155.4 1.6 collective-permute-start.25
  157.1 15.7 %gate_up.7.second_ref = bf16[256,1024]{1,0:T(8,128)(2,1)S(1)} custom-call(s32[3,8]{1,0:T(4,128)S(1)} %get-tuple-element.217.blocks_ref, bf16[256,1024]{1,0:T(8,128)(2,1)S(1)} %multiply_convert_fusion.refs_0_, bf16[256,1024]{1,0:T(8,128)(2,1)S(1)} %collective-permute-done.6.refs_1_, bf16[256,1024]{1,0:T(8,128)(2,1)S(1)} %collective-permute-done.7.refs_2_, ...), custom_call_target="tpu_custom_call" | custom-call | flops 17179869184 | bytes 33554432 | tf_op jit(solution)/shard_map/gate_up/pallas_call | solution.py:144
  173.2 6.7 %down.6 = bf16[3,256,1024]{2,1,0:T(8,128)(2,1)S(1)} custom-call(s32[3,8]{1,0:T(4,128)S(1)} %get-tuple-element.218.tiles_ref, bf16[256,1024]{1,0:T(8,128)(2,1)S(1)} %gate_up.6.first_ref, bf16[256,1024]{1,0:T(8,128)(2,1)S(1)} %gate_up.7.second_ref, bf16[2048,4096]{1,0:T(8,128)(2,1)} %local_ref.7, bf16[2048,4096]{1,0:T(8,128)(2,1)} %collective-permute-done.18.other_ref), custom_call_target="tpu_custom_call" | custom-call | flops 6442450944 | bytes 12582912 | tf_op jit(solution)/shard_map/down/pallas_call | solution.py:215
  180.1 1.6 collective-permute-start.27
  182.2 1.6 collective-permute-start.31
  184.2 1.6 collective-permute-start.29
  185.8 0.8 collective-permute-done.27
  187.4 1.5 collective-permute-start.33
  188.9 8.9 %collective-permute-done.29 = bf16[64,1024]{1,0:T(8,128)(2,1)S(1)} collective-permute-done((bf16[64,1024]{1,0:T(8,128)(2,1)S(1)}, bf16[64,1024]{1,0:T(8,128)(2,1)S(1)}, u32[]{:S(2)}, u32[]{:S(2)}) %collective-permute-start.29) | collective-permute-done | bytes 131104 | tf_op jit(solution)/shard_map/ppermute | solution.py:55
  197.8 0.5 collective-permute-start.34
  198.3 1.1 collective-permute-done.30
  199.4 1.6 collective-permute-start.39
  201.0 0.6 collective-permute-start.40
  201.6 2.6 %collective-permute-done.34 = bf16[128,1024]{1,0:T(8,128)(2,1)S(1)} collective-permute-done((bf16[128,1024]{1,0:T(8,128)(2,1)S(1)}, bf16[128,1024]{1,0:T(8,128)(2,1)S(1)}, u32[]{:S(2)}, u32[]{:S(2)}) %collective-permute-start.34) | collective-permute-done | bytes 262176 | tf_op jit(solution)/shard_map/ppermute | solution.py:55
  204.2 9.3 %down.7 = bf16[5,256,1024]{2,1,0:T(8,128)(2,1)S(1)} custom-call(s32[3,8]{1,0:T(4,128)S(1)} %get-tuple-element.218.tiles_ref, bf16[256,1024]{1,0:T(8,128)(2,1)S(1)} %gate_up.6.first_ref, bf16[256,1024]{1,0:T(8,128)(2,1)S(1)} %gate_up.7.second_ref, bf16[2048,4096]{1,0:T(8,128)(2,1)} %local_ref.7, bf16[2048,4096]{1,0:T(8,128)(2,1)} %collective-permute-done.18.other_ref), custom_call_target="tpu_custom_call" | custom-call | flops 10737418240 | bytes 20971520 | tf_op jit(solution)/shard_map/down/pallas_call | solution.py:215
  213.8 0.6 collective-permute-start.36
  214.3 1.5 collective-permute-start.35
  215.9 6.5 %collective-permute-done.36 = bf16[128,1024]{1,0:T(8,128)(2,1)S(1)} collective-permute-done((bf16[128,1024]{1,0:T(8,128)(2,1)S(1)}, bf16[128,1024]{1,0:T(8,128)(2,1)S(1)}, u32[]{:S(2)}, u32[]{:S(2)}) %collective-permute-start.36) | collective-permute-done | bytes 262176 | tf_op jit(solution)/shard_map/ppermute | solution.py:55
  222.4 1.2 collective-permute-done.35
  224.0 1.5 collective-permute-start.42
  225.5 0.5 collective-permute-start.41
  226.1 1.5 collective-permute-start.38
  227.5 0.5 collective-permute-start.37
  228.1 2.3 collective-permute-done.42
  230.4 1.5 collective-permute-done.41
  232.1 0.6 collective-permute-start.43
  232.7 1.5 collective-permute-start.44
  234.7 3.8 %collective-permute-done.43 = bf16[128,1024]{1,0:T(8,128)(2,1)S(1)} collective-permute-done((bf16[128,1024]{1,0:T(8,128)(2,1)S(1)}, bf16[128,1024]{1,0:T(8,128)(2,1)S(1)}, u32[]{:S(2)}, u32[]{:S(2)}) %collective-permute-start.43) | collective-permute-done | bytes 262176 | tf_op jit(solution)/shard_map/ppermute | solution.py:55
  238.5 0.5 collective-permute-done.44
  239.1 0.5 fusion.33
  239.6 1.0 pad_maximum_fusion.1
  (83 shorter events, 10.4 us)
Async XLA Ops:
  0.0 75.3 %collective-permute-start.12 = (bf16[4096,2048]{1,0:T(8,128)(2,1)}, bf16[4096,2048]{1,0:T(8,128)(2,1)}, u32[]{:S(2)}, u32[]{:S(2)}) collective-permute-start(bf16[4096,2048]{1,0:T(8,128)(2,1)} %refs_10_.7), channel_id=1, source_target_pairs={{0,1},{1,0},{2,3},{3,2},{4,5},{5,4},{6,7},{7,6},{8,9},{9,8},{10,11... | collective-permute-start | bytes 50331656 | tf_op jit(solution)/shard_map/ppermute | solution.py:59
  0.5 74.9 %collective-permute-start.13 = (bf16[4096,2048]{1,0:T(8,128)(2,1)}, bf16[4096,2048]{1,0:T(8,128)(2,1)}, u32[]{:S(2)}, u32[]{:S(2)}) collective-permute-start(bf16[4096,2048]{1,0:T(8,128)(2,1)} %refs_12_.7), channel_id=1, source_target_pairs={{0,1},{1,0},{2,3},{3,2},{4,5},{5,4},{6,7},{7,6},{8,9},{9,8},{10,11... | collective-permute-start | bytes 50331656 | tf_op jit(solution)/shard_map/ppermute | solution.py:59
  0.5 110.6 %collective-permute-start.18 = (bf16[2048,4096]{1,0:T(8,128)(2,1)}, bf16[2048,4096]{1,0:T(8,128)(2,1)}, u32[]{:S(2)}, u32[]{:S(2)}) collective-permute-start(bf16[2048,4096]{1,0:T(8,128)(2,1)} %local_ref.7), channel_id=1, source_target_pairs={{0,1},{1,0},{2,3},{3,2},{4,5},{5,4},{6,7},{7,6},{8,9},{9,8},{10,11... | collective-permute-start | bytes 50331656 | tf_op jit(solution)/shard_map/ppermute | solution.py:59
  4.7 47.8 %copy-start.7 = (f32[1024]{0:T(1024)S(1)}, f32[1024]{0:T(1024)}, u32[]{:S(2)}) copy-start(f32[1024]{0:T(1024)} %param.12) | copy-start | bytes 12292
  5.2 15.2 %collective-permute-start.2 = (bf16[256,1024]{1,0:T(8,128)(2,1)S(1)}, bf16[256,1024]{1,0:T(8,128)(2,1)S(1)}, u32[]{:S(2)}, u32[]{:S(2)}) collective-permute-start(bf16[256,1024]{1,0:T(8,128)(2,1)S(1)} %multiply_convert_fusion.1.refs_0_), channel_id=1, source_target_pairs={{0,4},{4,8},{8,12},{12,14},{14,10},{10,6},{6,2},{2,0},{1,5},{5,9},... | collective-permute-start | bytes 1572872 | tf_op jit(solution)/shard_map/ppermute | solution.py:55
  7.9 14.1 %collective-permute-start.3 = (bf16[256,1024]{1,0:T(8,128)(2,1)S(1)}, bf16[256,1024]{1,0:T(8,128)(2,1)S(1)}, u32[]{:S(2)}, u32[]{:S(2)}) collective-permute-start(bf16[256,1024]{1,0:T(8,128)(2,1)S(1)} %multiply_convert_fusion.1.refs_0_), channel_id=1, source_target_pairs={{0,2},{4,0},{8,4},{12,8},{14,12},{10,14},{6,10},{2,6},{1,3},{5,1},... | collective-permute-start | bytes 1572872 | tf_op jit(solution)/shard_map/ppermute | solution.py:55
  21.9 13.2 %collective-permute-start.4 = (bf16[256,1024]{1,0:T(8,128)(2,1)S(1)}, bf16[256,1024]{1,0:T(8,128)(2,1)S(1)}, u32[]{:S(2)}, u32[]{:S(2)}) collective-permute-start(bf16[256,1024]{1,0:T(8,128)(2,1)S(1)} %collective-permute-done.2.refs_1_), channel_id=1, source_target_pairs={{0,4},{4,8},{8,12},{12,14},{14,10},{10,6},{6,2},{2,0},{1,5},{5,9},... | collective-permute-start | bytes 1572872 | tf_op jit(solution)/shard_map/ppermute | solution.py:55
  23.5 13.7 %collective-permute-start.5 = (bf16[256,1024]{1,0:T(8,128)(2,1)S(1)}, bf16[256,1024]{1,0:T(8,128)(2,1)S(1)}, u32[]{:S(2)}, u32[]{:S(2)}) collective-permute-start(bf16[256,1024]{1,0:T(8,128)(2,1)S(1)} %collective-permute-done.3.refs_2_), channel_id=1, source_target_pairs={{0,2},{4,0},{8,4},{12,8},{14,12},{10,14},{6,10},{2,6},{1,3},{5,1},... | collective-permute-start | bytes 1572872 | tf_op jit(solution)/shard_map/ppermute | solution.py:55
  35.1 14.1 %collective-permute-start.1 = (bf16[3,1024]{1,0:T(4,128)(2,1)S(1)}, bf16[3,1024]{1,0:T(4,128)(2,1)S(1)}, u32[]{:S(2)}, u32[]{:S(2)}) collective-permute-start(bf16[3,1024]{1,0:T(4,128)(2,1)S(1)} %slice.316), channel_id=1, source_target_pairs={{0,1},{2,3},{4,5},{6,7},{8,9},{10,11},{12,13},{14,15},{16,17},{18,... | collective-permute-start | bytes 18440 | tf_op jit(solution)/shard_map/ppermute | solution.py:289
  37.2 14.7 %collective-permute-start = (bf16[3,1024]{1,0:T(4,128)(2,1)S(1)}, bf16[3,1024]{1,0:T(4,128)(2,1)S(1)}, u32[]{:S(2)}, u32[]{:S(2)}) collective-permute-start(bf16[3,1024]{1,0:T(4,128)(2,1)S(1)} %slice.315), channel_id=1, source_target_pairs={{0,1},{2,3},{4,5},{6,7},{8,9},{10,11},{12,13},{14,15},{16,17},{18,... | collective-permute-start | bytes 18440 | tf_op jit(solution)/shard_map/ppermute | solution.py:289
  49.3 15.0 %collective-permute-start.8 = (bf16[256,1024]{1,0:T(8,128)(2,1)S(1)}, bf16[256,1024]{1,0:T(8,128)(2,1)S(1)}, u32[]{:S(2)}, u32[]{:S(2)}) collective-permute-start(bf16[256,1024]{1,0:T(8,128)(2,1)S(1)} %collective-permute-done.4.refs_3_), channel_id=1, source_target_pairs={{0,4},{4,8},{8,12},{12,14},{14,10},{10,6},{6,2},{2,0},{1,5},{5,9},... | collective-permute-start | bytes 1572872 | tf_op jit(solution)/shard_map/ppermute | solution.py:55
  51.8 13.9 %collective-permute-start.9 = (bf16[256,1024]{1,0:T(8,128)(2,1)S(1)}, bf16[256,1024]{1,0:T(8,128)(2,1)S(1)}, u32[]{:S(2)}, u32[]{:S(2)}) collective-permute-start(bf16[256,1024]{1,0:T(8,128)(2,1)S(1)} %collective-permute-done.5.refs_4_), channel_id=1, source_target_pairs={{0,2},{4,0},{8,4},{12,8},{14,12},{10,14},{6,10},{2,6},{1,3},{5,1},... | collective-permute-start | bytes 1572872 | tf_op jit(solution)/shard_map/ppermute | solution.py:55
  52.6 22.8 %copy-start = (f32[8192]{0:T(1024)S(1)}, f32[8192]{0:T(1024)}, u32[]{:S(2)}) copy-start(f32[8192]{0:T(1024)} %param.15) | copy-start | bytes 98308
  64.2 11.1 %copy-start.5 = (bf16[256,1024]{1,0:T(8,128)(2,1)}, bf16[256,1024]{1,0:T(8,128)(2,1)S(1)}, u32[]{:S(2)}) copy-start(bf16[256,1024]{1,0:T(8,128)(2,1)S(1)} %collective-permute-done.8.refs_5_) | copy-start | bytes 1572868
  65.8 9.6 %copy-start.6 = (bf16[256,1024]{1,0:T(8,128)(2,1)}, bf16[256,1024]{1,0:T(8,128)(2,1)S(1)}, u32[]{:S(2)}) copy-start(bf16[256,1024]{1,0:T(8,128)(2,1)S(1)} %collective-permute-done.9.refs_6_) | copy-start | bytes 1572868
  65.8 7.5 %collective-permute-start.11 = (bf16[128,1024]{1,0:T(8,128)(2,1)S(1)}, bf16[128,1024]{1,0:T(8,128)(2,1)S(1)}, u32[]{:S(2)}, u32[]{:S(2)}) collective-permute-start(bf16[128,1024]{1,0:T(8,128)(2,1)S(1)} %slice.332), channel_id=1, source_target_pairs={{0,2},{4,0},{8,4},{12,8},{14,12},{10,14},{6,10},{2,6},{1,3},{5,1},... | collective-permute-start | bytes 786440 | tf_op jit(solution)/shard_map/ppermute | solution.py:55
  66.1 8.7 %collective-permute-start.10 = (bf16[128,1024]{1,0:T(8,128)(2,1)S(1)}, bf16[128,1024]{1,0:T(8,128)(2,1)S(1)}, u32[]{:S(2)}, u32[]{:S(2)}) collective-permute-start(bf16[128,1024]{1,0:T(8,128)(2,1)S(1)} %slice.331), channel_id=1, source_target_pairs={{0,4},{4,8},{8,12},{12,14},{14,10},{10,6},{6,2},{2,0},{1,5},{5,9},... | collective-permute-start | bytes 786440 | tf_op jit(solution)/shard_map/ppermute | solution.py:55
  73.3 17.9 %collective-permute-start.6 = (bf16[256,1024]{1,0:T(8,128)(2,1)S(1)}, bf16[256,1024]{1,0:T(8,128)(2,1)S(1)}, u32[]{:S(2)}, u32[]{:S(2)}) collective-permute-start(bf16[256,1024]{1,0:T(8,128)(2,1)S(1)} %multiply_convert_fusion.refs_0_), channel_id=1, source_target_pairs={{0,4},{4,8},{8,12},{12,14},{14,10},{10,6},{6,2},{2,0},{1,5},{5,9},... | collective-permute-start | bytes 1572872 | tf_op jit(solution)/shard_map/ppermute | solution.py:55
  74.9 16.3 %collective-permute-start.7 = (bf16[256,1024]{1,0:T(8,128)(2,1)S(1)}, bf16[256,1024]{1,0:T(8,128)(2,1)S(1)}, u32[]{:S(2)}, u32[]{:S(2)}) collective-permute-start(bf16[256,1024]{1,0:T(8,128)(2,1)S(1)} %multiply_convert_fusion.refs_0_), channel_id=1, source_target_pairs={{0,2},{4,0},{8,4},{12,8},{14,12},{10,14},{6,10},{2,6},{1,3},{5,1},... | collective-permute-start | bytes 1572872 | tf_op jit(solution)/shard_map/ppermute | solution.py:55
  91.2 17.8 %collective-permute-start.14 = (bf16[256,1024]{1,0:T(8,128)(2,1)S(1)}, bf16[256,1024]{1,0:T(8,128)(2,1)S(1)}, u32[]{:S(2)}, u32[]{:S(2)}) collective-permute-start(bf16[256,1024]{1,0:T(8,128)(2,1)S(1)} %collective-permute-done.6.refs_1_), channel_id=1, source_target_pairs={{0,4},{4,8},{8,12},{12,14},{14,10},{10,6},{6,2},{2,0},{1,5},{5,9},... | collective-permute-start | bytes 1572872 | tf_op jit(solution)/shard_map/ppermute | solution.py:55
  92.8 16.2 %collective-permute-start.15 = (bf16[256,1024]{1,0:T(8,128)(2,1)S(1)}, bf16[256,1024]{1,0:T(8,128)(2,1)S(1)}, u32[]{:S(2)}, u32[]{:S(2)}) collective-permute-start(bf16[256,1024]{1,0:T(8,128)(2,1)S(1)} %collective-permute-done.7.refs_2_), channel_id=1, source_target_pairs={{0,2},{4,0},{8,4},{12,8},{14,12},{10,14},{6,10},{2,6},{1,3},{5,1},... | collective-permute-start | bytes 1572872 | tf_op jit(solution)/shard_map/ppermute | solution.py:55
  109.0 11.1 %collective-permute-start.16 = (bf16[256,1024]{1,0:T(8,128)(2,1)S(1)}, bf16[256,1024]{1,0:T(8,128)(2,1)S(1)}, u32[]{:S(2)}, u32[]{:S(2)}) collective-permute-start(bf16[256,1024]{1,0:T(8,128)(2,1)S(1)} %collective-permute-done.14.refs_3_), channel_id=1, source_target_pairs={{0,4},{4,8},{8,12},{12,14},{14,10},{10,6},{6,2},{2,0},{1,5},{5,9},... | collective-permute-start | bytes 1572872 | tf_op jit(solution)/shard_map/ppermute | solution.py:55
  110.7 12.0 %collective-permute-start.17 = (bf16[256,1024]{1,0:T(8,128)(2,1)S(1)}, bf16[256,1024]{1,0:T(8,128)(2,1)S(1)}, u32[]{:S(2)}, u32[]{:S(2)}) collective-permute-start(bf16[256,1024]{1,0:T(8,128)(2,1)S(1)} %collective-permute-done.15.refs_4_), channel_id=1, source_target_pairs={{0,2},{4,0},{8,4},{12,8},{14,12},{10,14},{6,10},{2,6},{1,3},{5,1},... | collective-permute-start | bytes 1572872 | tf_op jit(solution)/shard_map/ppermute | solution.py:55
  120.1 16.0 %copy-start.3 = (bf16[256,1024]{1,0:T(8,128)(2,1)}, bf16[256,1024]{1,0:T(8,128)(2,1)S(1)}, u32[]{:S(2)}) copy-start(bf16[256,1024]{1,0:T(8,128)(2,1)S(1)} %collective-permute-done.16.refs_5_) | copy-start | bytes 1572868
  122.7 13.5 %copy-start.4 = (bf16[256,1024]{1,0:T(8,128)(2,1)}, bf16[256,1024]{1,0:T(8,128)(2,1)S(1)}, u32[]{:S(2)}) copy-start(bf16[256,1024]{1,0:T(8,128)(2,1)S(1)} %collective-permute-done.17.refs_6_) | copy-start | bytes 1572868
  122.7 16.1 %collective-permute-start.20 = (bf16[128,1024]{1,0:T(8,128)(2,1)S(1)}, bf16[128,1024]{1,0:T(8,128)(2,1)S(1)}, u32[]{:S(2)}, u32[]{:S(2)}) collective-permute-start(bf16[128,1024]{1,0:T(8,128)(2,1)S(1)} %slice.334), channel_id=1, source_target_pairs={{0,2},{4,0},{8,4},{12,8},{14,12},{10,14},{6,10},{2,6},{1,3},{5,1},... | collective-permute-start | bytes 786440 | tf_op jit(solution)/shard_map/ppermute | solution.py:55
  123.2 15.6 %collective-permute-start.19 = (bf16[128,1024]{1,0:T(8,128)(2,1)S(1)}, bf16[128,1024]{1,0:T(8,128)(2,1)S(1)}, u32[]{:S(2)}, u32[]{:S(2)}) collective-permute-start(bf16[128,1024]{1,0:T(8,128)(2,1)S(1)} %slice.333), channel_id=1, source_target_pairs={{0,4},{4,8},{8,12},{12,14},{14,10},{10,6},{6,2},{2,0},{1,5},{5,9},... | collective-permute-start | bytes 786440 | tf_op jit(solution)/shard_map/ppermute | solution.py:55
  124.8 11.4 %collective-permute-start.21 = (bf16[128,1024]{1,0:T(8,128)(2,1)S(1)}, bf16[128,1024]{1,0:T(8,128)(2,1)S(1)}, u32[]{:S(2)}, u32[]{:S(2)}) collective-permute-start(bf16[128,1024]{1,0:T(8,128)(2,1)S(1)} %get-tuple-element.135), channel_id=1, source_target_pairs={{0,4},{4,8},{8,12},{12,14},{14,10},{10,6},{6,2},{2,0},{1,5},{5,9},... | collective-permute-start | bytes 786440 | tf_op jit(solution)/shard_map/ppermute | solution.py:55
  126.4 9.8 %collective-permute-start.22 = (bf16[128,1024]{1,0:T(8,128)(2,1)S(1)}, bf16[128,1024]{1,0:T(8,128)(2,1)S(1)}, u32[]{:S(2)}, u32[]{:S(2)}) collective-permute-start(bf16[128,1024]{1,0:T(8,128)(2,1)S(1)} %get-tuple-element.136), channel_id=1, source_target_pairs={{0,2},{4,0},{8,4},{12,8},{14,12},{10,14},{6,10},{2,6},{1,3},{5,1},... | collective-permute-start | bytes 786440 | tf_op jit(solution)/shard_map/ppermute | solution.py:55
  136.5 18.1 %collective-permute-start.23 = (bf16[256,1024]{1,0:T(8,128)(2,1)S(1)}, bf16[256,1024]{1,0:T(8,128)(2,1)S(1)}, u32[]{:S(2)}, u32[]{:S(2)}) collective-permute-start(bf16[256,1024]{1,0:T(8,128)(2,1)S(1)} %pad_maximum_fusion.2), channel_id=1, source_target_pairs={{0,4},{4,8},{8,12},{12,14},{14,10},{10,6},{6,2},{2,0},{1,5},{5,9},... | collective-permute-start | bytes 1572872 | tf_op jit(solution)/shard_map/ppermute | solution.py:55
  138.3 16.3 %collective-permute-start.24 = (bf16[256,1024]{1,0:T(8,128)(2,1)S(1)}, bf16[256,1024]{1,0:T(8,128)(2,1)S(1)}, u32[]{:S(2)}, u32[]{:S(2)}) collective-permute-start(bf16[256,1024]{1,0:T(8,128)(2,1)S(1)} %pad_maximum_fusion.3), channel_id=1, source_target_pairs={{0,2},{4,0},{8,4},{12,8},{14,12},{10,14},{6,10},{2,6},{1,3},{5,1},... | collective-permute-start | bytes 1572872 | tf_op jit(solution)/shard_map/ppermute | solution.py:55
  155.0 17.8 %collective-permute-start.26 = (bf16[256,1024]{1,0:T(8,128)(2,1)S(1)}, bf16[256,1024]{1,0:T(8,128)(2,1)S(1)}, u32[]{:S(2)}, u32[]{:S(2)}) collective-permute-start(bf16[256,1024]{1,0:T(8,128)(2,1)S(1)} %get-tuple-element.193), channel_id=1, source_target_pairs={{0,2},{4,0},{8,4},{12,8},{14,12},{10,14},{6,10},{2,6},{1,3},{5,1},... | collective-permute-start | bytes 1572872 | tf_op jit(solution)/shard_map/ppermute | solution.py:55
  155.4 17.4 %collective-permute-start.25 = (bf16[256,1024]{1,0:T(8,128)(2,1)S(1)}, bf16[256,1024]{1,0:T(8,128)(2,1)S(1)}, u32[]{:S(2)}, u32[]{:S(2)}) collective-permute-start(bf16[256,1024]{1,0:T(8,128)(2,1)S(1)} %get-tuple-element.194), channel_id=1, source_target_pairs={{0,4},{4,8},{8,12},{12,14},{14,10},{10,6},{6,2},{2,0},{1,5},{5,9},... | collective-permute-start | bytes 1572872 | tf_op jit(solution)/shard_map/ppermute | solution.py:55
  180.1 6.5 %collective-permute-start.27 = (bf16[64,1024]{1,0:T(8,128)(2,1)S(1)}, bf16[64,1024]{1,0:T(8,128)(2,1)S(1)}, u32[]{:S(2)}, u32[]{:S(2)}) collective-permute-start(bf16[64,1024]{1,0:T(8,128)(2,1)S(1)} %get-tuple-element.163), channel_id=1, source_target_pairs={{0,4},{4,8},{8,12},{12,14},{14,10},{10,6},{6,2},{2,0},{1,5},{5,9},... | collective-permute-start | bytes 393224 | tf_op jit(solution)/shard_map/ppermute | solution.py:55
  181.7 5.5 %collective-permute-start.28 = (bf16[64,1024]{1,0:T(8,128)(2,1)S(1)}, bf16[64,1024]{1,0:T(8,128)(2,1)S(1)}, u32[]{:S(2)}, u32[]{:S(2)}) collective-permute-start(bf16[64,1024]{1,0:T(8,128)(2,1)S(1)} %get-tuple-element.164), channel_id=1, source_target_pairs={{0,2},{4,0},{8,4},{12,8},{14,12},{10,14},{6,10},{2,6},{1,3},{5,1},... | collective-permute-start | bytes 393224 | tf_op jit(solution)/shard_map/ppermute | solution.py:55
  182.2 22.1 %collective-permute-start.31 = (bf16[256,1024]{1,0:T(8,128)(2,1)S(1)}, bf16[256,1024]{1,0:T(8,128)(2,1)S(1)}, u32[]{:S(2)}, u32[]{:S(2)}) collective-permute-start(bf16[256,1024]{1,0:T(8,128)(2,1)S(1)} %get-tuple-element.191), channel_id=1, source_target_pairs={{0,4},{4,8},{8,12},{12,14},{14,10},{10,6},{6,2},{2,0},{1,5},{5,9},... | collective-permute-start | bytes 1572872 | tf_op jit(solution)/shard_map/ppermute | solution.py:55
  183.7 20.5 %collective-permute-start.32 = (bf16[256,1024]{1,0:T(8,128)(2,1)S(1)}, bf16[256,1024]{1,0:T(8,128)(2,1)S(1)}, u32[]{:S(2)}, u32[]{:S(2)}) collective-permute-start(bf16[256,1024]{1,0:T(8,128)(2,1)S(1)} %get-tuple-element.192), channel_id=1, source_target_pairs={{0,2},{4,0},{8,4},{12,8},{14,12},{10,14},{6,10},{2,6},{1,3},{5,1},... | collective-permute-start | bytes 1572872 | tf_op jit(solution)/shard_map/ppermute | solution.py:55
  184.2 13.6 %collective-permute-start.29 = (bf16[64,1024]{1,0:T(8,128)(2,1)S(1)}, bf16[64,1024]{1,0:T(8,128)(2,1)S(1)}, u32[]{:S(2)}, u32[]{:S(2)}) collective-permute-start(bf16[64,1024]{1,0:T(8,128)(2,1)S(1)} %get-tuple-element.167), channel_id=1, source_target_pairs={{0,4},{4,8},{8,12},{12,14},{14,10},{10,6},{6,2},{2,0},{1,5},{5,9},... | collective-permute-start | bytes 393224 | tf_op jit(solution)/shard_map/ppermute | solution.py:55
  186.6 12.7 %collective-permute-start.30 = (bf16[64,1024]{1,0:T(8,128)(2,1)S(1)}, bf16[64,1024]{1,0:T(8,128)(2,1)S(1)}, u32[]{:S(2)}, u32[]{:S(2)}) collective-permute-start(bf16[64,1024]{1,0:T(8,128)(2,1)S(1)} %get-tuple-element.168), channel_id=1, source_target_pairs={{0,2},{4,0},{8,4},{12,8},{14,12},{10,14},{6,10},{2,6},{1,3},{5,1},... | collective-permute-start | bytes 393224 | tf_op jit(solution)/shard_map/ppermute | solution.py:55
  187.4 13.7 %collective-permute-start.33 = (bf16[128,1024]{1,0:T(8,128)(2,1)S(1)}, bf16[128,1024]{1,0:T(8,128)(2,1)S(1)}, u32[]{:S(2)}, u32[]{:S(2)}) collective-permute-start(bf16[128,1024]{1,0:T(8,128)(2,1)S(1)} %pad_maximum_fusion.4), channel_id=1, source_target_pairs={{0,4},{4,8},{8,12},{12,14},{14,10},{10,6},{6,2},{2,0},{1,5},{5,9},... | collective-permute-start | bytes 786440 | tf_op jit(solution)/shard_map/ppermute | solution.py:55
  197.8 6.5 %collective-permute-start.34 = (bf16[128,1024]{1,0:T(8,128)(2,1)S(1)}, bf16[128,1024]{1,0:T(8,128)(2,1)S(1)}, u32[]{:S(2)}, u32[]{:S(2)}) collective-permute-start(bf16[128,1024]{1,0:T(8,128)(2,1)S(1)} %pad_maximum_fusion.5), channel_id=1, source_target_pairs={{0,2},{4,0},{8,4},{12,8},{14,12},{10,14},{6,10},{2,6},{1,3},{5,1},... | collective-permute-start | bytes 786440 | tf_op jit(solution)/shard_map/ppermute | solution.py:55
  199.4 16.4 %collective-permute-start.39 = (bf16[128,1024]{1,0:T(8,128)(2,1)S(1)}, bf16[128,1024]{1,0:T(8,128)(2,1)S(1)}, u32[]{:S(2)}, u32[]{:S(2)}) collective-permute-start(bf16[128,1024]{1,0:T(8,128)(2,1)S(1)} %pad_maximum_fusion.6), channel_id=1, source_target_pairs={{0,4},{4,8},{8,12},{12,14},{14,10},{10,6},{6,2},{2,0},{1,5},{5,9},... | collective-permute-start | bytes 786440 | tf_op jit(solution)/shard_map/ppermute | solution.py:55
  201.0 14.8 %collective-permute-start.40 = (bf16[128,1024]{1,0:T(8,128)(2,1)S(1)}, bf16[128,1024]{1,0:T(8,128)(2,1)S(1)}, u32[]{:S(2)}, u32[]{:S(2)}) collective-permute-start(bf16[128,1024]{1,0:T(8,128)(2,1)S(1)} %pad_maximum_fusion.7), channel_id=1, source_target_pairs={{0,2},{4,0},{8,4},{12,8},{14,12},{10,14},{6,10},{2,6},{1,3},{5,1},... | collective-permute-start | bytes 786440 | tf_op jit(solution)/shard_map/ppermute | solution.py:55
  213.8 8.6 %collective-permute-start.36 = (bf16[128,1024]{1,0:T(8,128)(2,1)S(1)}, bf16[128,1024]{1,0:T(8,128)(2,1)S(1)}, u32[]{:S(2)}, u32[]{:S(2)}) collective-permute-start(bf16[128,1024]{1,0:T(8,128)(2,1)S(1)} %get-tuple-element.189), channel_id=1, source_target_pairs={{0,2},{4,0},{8,4},{12,8},{14,12},{10,14},{6,10},{2,6},{1,3},{5,1},... | collective-permute-start | bytes 786440 | tf_op jit(solution)/shard_map/ppermute | solution.py:55
  214.3 19.8 %copy-start.1 = (bf16[512,1024]{1,0:T(8,128)(2,1)S(1)}, bf16[512,1024]{1,0:T(8,128)(2,1)}, u32[]{:S(2)}) copy-start(bf16[512,1024]{1,0:T(8,128)(2,1)} %param.11) | copy-start | bytes 3145732
  214.3 19.8 %copy-start.2 = (bf16[512,1024]{1,0:T(8,128)(2,1)S(1)}, bf16[512,1024]{1,0:T(8,128)(2,1)}, u32[]{:S(2)}) copy-start(bf16[512,1024]{1,0:T(8,128)(2,1)} %param.10) | copy-start | bytes 3145732
  214.3 9.2 %collective-permute-start.35 = (bf16[128,1024]{1,0:T(8,128)(2,1)S(1)}, bf16[128,1024]{1,0:T(8,128)(2,1)S(1)}, u32[]{:S(2)}, u32[]{:S(2)}) collective-permute-start(bf16[128,1024]{1,0:T(8,128)(2,1)S(1)} %get-tuple-element.190), channel_id=1, source_target_pairs={{0,4},{4,8},{8,12},{12,14},{14,10},{10,6},{6,2},{2,0},{1,5},{5,9},... | collective-permute-start | bytes 786440 | tf_op jit(solution)/shard_map/ppermute | solution.py:55
  224.0 6.4 %collective-permute-start.42 = (bf16[128,1024]{1,0:T(8,128)(2,1)S(1)}, bf16[128,1024]{1,0:T(8,128)(2,1)S(1)}, u32[]{:S(2)}, u32[]{:S(2)}) collective-permute-start(bf16[128,1024]{1,0:T(8,128)(2,1)S(1)} %get-tuple-element.186), channel_id=1, source_target_pairs={{0,2},{4,0},{8,4},{12,8},{14,12},{10,14},{6,10},{2,6},{1,3},{5,1},... | collective-permute-start | bytes 786440 | tf_op jit(solution)/shard_map/ppermute | solution.py:55
  225.5 6.4 %collective-permute-start.41 = (bf16[128,1024]{1,0:T(8,128)(2,1)S(1)}, bf16[128,1024]{1,0:T(8,128)(2,1)S(1)}, u32[]{:S(2)}, u32[]{:S(2)}) collective-permute-start(bf16[128,1024]{1,0:T(8,128)(2,1)S(1)} %get-tuple-element.187), channel_id=1, source_target_pairs={{0,4},{4,8},{8,12},{12,14},{14,10},{10,6},{6,2},{2,0},{1,5},{5,9},... | collective-permute-start | bytes 786440 | tf_op jit(solution)/shard_map/ppermute | solution.py:55
  226.1 8.6 %collective-permute-start.38 = (bf16[128,1024]{1,0:T(8,128)(2,1)S(1)}, bf16[128,1024]{1,0:T(8,128)(2,1)S(1)}, u32[]{:S(2)}, u32[]{:S(2)}) collective-permute-start(bf16[128,1024]{1,0:T(8,128)(2,1)S(1)} %get-tuple-element.185), channel_id=1, source_target_pairs={{0,2},{4,0},{8,4},{12,8},{14,12},{10,14},{6,10},{2,6},{1,3},{5,1},... | collective-permute-start | bytes 786440 | tf_op jit(solution)/shard_map/ppermute | solution.py:55
  227.5 7.2 %collective-permute-start.37 = (bf16[128,1024]{1,0:T(8,128)(2,1)S(1)}, bf16[128,1024]{1,0:T(8,128)(2,1)S(1)}, u32[]{:S(2)}, u32[]{:S(2)}) collective-permute-start(bf16[128,1024]{1,0:T(8,128)(2,1)S(1)} %get-tuple-element.188), channel_id=1, source_target_pairs={{0,4},{4,8},{8,12},{12,14},{14,10},{10,6},{6,2},{2,0},{1,5},{5,9},... | collective-permute-start | bytes 786440 | tf_op jit(solution)/shard_map/ppermute | solution.py:55
  232.1 6.4 %collective-permute-start.43 = (bf16[128,1024]{1,0:T(8,128)(2,1)S(1)}, bf16[128,1024]{1,0:T(8,128)(2,1)S(1)}, u32[]{:S(2)}, u32[]{:S(2)}) collective-permute-start(bf16[128,1024]{1,0:T(8,128)(2,1)S(1)} %get-tuple-element.183), channel_id=1, source_target_pairs={{0,4},{4,8},{8,12},{12,14},{14,10},{10,6},{6,2},{2,0},{1,5},{5,9},... | collective-permute-start | bytes 786440 | tf_op jit(solution)/shard_map/ppermute | solution.py:55
  232.7 6.4 %collective-permute-start.44 = (bf16[128,1024]{1,0:T(8,128)(2,1)S(1)}, bf16[128,1024]{1,0:T(8,128)(2,1)S(1)}, u32[]{:S(2)}, u32[]{:S(2)}) collective-permute-start(bf16[128,1024]{1,0:T(8,128)(2,1)S(1)} %get-tuple-element.184), channel_id=1, source_target_pairs={{0,2},{4,0},{8,4},{12,8},{14,12},{10,14},{6,10},{2,6},{1,3},{5,1},... | collective-permute-start | bytes 786440 | tf_op jit(solution)/shard_map/ppermute | solution.py:55

commit v6 on v5

--- a/solution.py
+++ b/solution.py
@@ -63,103 +63,116 @@
     return lax.optimization_barrier((value, earlier))[0]
 
 
-def gate_up_kernel(columns, steps, mean_of, blocks_ref, *refs):
+def gate_up_kernel(columns, groups, mean_of, blocks_ref, *refs):
     refs = list(refs)
-    stacked, gate, inv, weights, sems, weight_sems = refs[-6:]
+    stacked, sums, stat, weights, sems, weight_sems = refs[-6:]
     out_ref = refs[-7]
     gains_ref = refs[-12]
     sources = [refs[-11:-9], refs[-9:-7]]
     pieces = refs[:-12]
+    rows = stacked.shape[0]
     count, width = gains_ref.shape[0], gains_ref.shape[2]
-    step = pl.program_id(0) * 2 + pl.program_id(1)
-    tile = weights.shape[-1]
+    size, tile = count // groups, weights.shape[-1]
+    group, which = pl.program_id(0), pl.program_id(1)
+    step, steps = group * 2 + which, 2 * groups
+    parts = 2 if size < 4 else 1
 
     def fetch(number, act):
-        slot, which = lax.rem(number, DEEP), lax.rem(number, 2)
-        column = pl.multiple_of(columns + lax.div(number, 2) * tile, tile)
-        for index in range(count):
-            row = pl.multiple_of(blocks_ref[1, index] * width, width)
+        slot, kind, first = lax.rem(number, DEEP), lax.rem(number, 2), lax.div(number, 2) * size
+        for index in range(size):
             for gate_or_up in range(2):
                 for other in range(2):
 
-                    @pl.when((which == gate_or_up) & (blocks_ref[0, index] == 1 - other))
-                    def chosen(index=index, row=row, source=sources[gate_or_up][other]):
-                        act(
-                            pltpu.make_async_copy(
-                                source.at[pl.ds(row, width), pl.ds(column, tile)],
-                                weights.at[slot, pl.ds(index * width, width)],
-                                weight_sems.at[slot, index],
+                    @pl.when((kind == gate_or_up) & (blocks_ref[0, first + index] == 1 - other))
+                    def chosen(index=index, source=sources[gate_or_up][other]):
+                        begin = pl.multiple_of(blocks_ref[1, first + index] * width, width)
+                        height = width // parts
+                        for part in range(parts):
+                            act(
+                                pltpu.make_async_copy(
+                                    source.at[pl.ds(begin + part * height, height), pl.ds(columns, tile)],
+                                    weights.at[slot, pl.ds(index * width + part * height, height)],
+                                    weight_sems.at[slot, index, part],
+                                )
                             )
-                        )
-
-    def gather_pieces(act):
+
+    def gather_pieces(wanted, act):
         start = 0
         for number, source in enumerate(pieces):
-            size = source.shape[0]
-            row = start % stacked.shape[0]
-            target = stacked.at[pl.ds(row, size), pl.ds((start // stacked.shape[0]) * width, width)]
-            act(pltpu.make_async_copy(source, target, sems.at[number]))
-            start += size
+            height = source.shape[0]
+            if start // rows // size == wanted:
+                target = stacked.at[pl.ds(start % rows, height), pl.ds((start // rows) * width, width)]
+                act(pltpu.make_async_copy(source, target, sems.at[number]))
+            start += height
 
     @pl.when(step == 0)
     def first():
-        gather_pieces(lambda copy: copy.start())
+        gather_pieces(0, lambda copy: copy.start())
         for number in range(min(DEEP - 1, steps)):
             fetch(jnp.int32(number), lambda copy: copy.start())
-        gather_pieces(lambda copy: copy.wait())
-        stat = jnp.zeros((stacked.shape[0], LANES), jnp.float32)
-        for index in range(count):
-            gain = gains_ref[blocks_ref[2, index]]
-            weight = 1.0 / (gain * gain)
-            for column in range(0, width, LANES):
-                value = stacked[:, index * width + column : index * width + column + LANES].astype(jnp.float32)
-                stat = stat + value * value * weight[:, column : column + LANES]
-        total = jnp.sum(stat, axis=1, keepdims=True)
-        inv[...] = jnp.broadcast_to(lax.rsqrt(total / mean_of + 1e-05), inv.shape)
+        for wanted in range(1, groups):
+            gather_pieces(wanted, lambda copy: copy.start())
+        sums[...] = jnp.zeros_like(sums)
+        stat[...] = jnp.zeros_like(stat)
 
     @pl.when(step + DEEP - 1 < steps)
     def ahead():
         fetch(step + DEEP - 1, lambda copy: copy.start())
 
+    for wanted in range(groups):
+
+        @pl.when((group == wanted) & (which == 0))
+        def arrived(wanted=wanted):
+            gather_pieces(wanted, lambda copy: copy.wait())
+
     fetch(step, lambda copy: copy.wait())
-    total = jnp.dot(stacked[...], weights[lax.rem(step, DEEP)], preferred_element_type=jnp.float32) * inv[:, :1]
-
-    @pl.when(pl.program_id(1) == 0)
-    def keep():
-        gate[...] = total
-
-    @pl.when(pl.program_id(1) == 1)
+    begin = pl.multiple_of(group * (size * width), size * width)
+    values = stacked[:, pl.ds(begin, size * width)]
+    sums[which] += jnp.dot(values, weights[lax.rem(step, DEEP)], preferred_element_type=jnp.float32)
+    squares = stat[...]
+    for index in range(size // 2):
+        place = group * size + which * (size // 2) + index
+        gain = gains_ref[blocks_ref[2, place]]
+        weight = 1.0 / (gain * gain)
+        block = stacked[:, pl.ds(pl.multiple_of(place * width, width), width)].astype(jnp.float32)
+        for column in range(0, width, LANES):
+            value = block[:, column : column + LANES]
+            squares = squares + value * value * weight[:, column : column + LANES]
+    stat[...] = squares
+
+    @pl.when(step == steps - 1)
     def activate():
-        value = gate[...]
-        out_ref[...] = (value / (1.0 + jnp.exp(-value)) * total).astype(jnp.bfloat16)
+        inv = lax.rsqrt(jnp.sum(stat[...], axis=1, keepdims=True) / mean_of + 1e-05)
+        gate = sums[0] * inv
+        out_ref[...] = (gate / (1.0 + jnp.exp(-gate)) * (sums[1] * inv)).astype(jnp.bfloat16)
 
 
 def gate_up(part, blocks, pieces, gains, weights):
     rows, width = pieces[0].shape
     count = blocks.shape[1]
     columns = weights[0].shape[1] // 2
-    tile = min(256, columns)
-    steps = 2 * (columns // tile)
+    size = max(2, 2048 // width)
+    groups = count // size
     anywhere = pl.BlockSpec(memory_space=pl.ANY)
     return pl.pallas_call(
-        functools.partial(gate_up_kernel, part * columns, steps, width * count),
+        functools.partial(gate_up_kernel, part * columns, groups, width * count),
         out_shape=jax.ShapeDtypeStruct((rows, columns), jnp.bfloat16),
         grid_spec=pltpu.PrefetchScalarGridSpec(
             num_scalar_prefetch=1,
-            grid=(columns // tile, 2),
+            grid=(groups, 2),
             in_specs=[
                 *[anywhere] * len(pieces),
                 pl.BlockSpec(gains.shape, lambda n, w, blocks: (0, 0, 0)),
                 *[anywhere] * 4,
             ],
-            out_specs=pl.BlockSpec((rows, tile), lambda n, w, blocks: (0, n)),
+            out_specs=pl.BlockSpec((rows, columns), lambda n, w, blocks: (0, 0)),
             scratch_shapes=[
                 pltpu.VMEM((rows, count * width), jnp.bfloat16),
-                pltpu.VMEM((rows, tile), jnp.float32),
+                pltpu.VMEM((2, rows, columns), jnp.float32),
                 pltpu.VMEM((rows, LANES), jnp.float32),
-                pltpu.VMEM((DEEP, count * width, tile), jnp.bfloat16),
+                pltpu.VMEM((DEEP, size * width, columns), jnp.bfloat16),
                 pltpu.SemaphoreType.DMA((len(pieces),)),
-                pltpu.SemaphoreType.DMA((DEEP, count)),
+                pltpu.SemaphoreType.DMA((DEEP, size, 2)),
             ],
         ),
         compiler_params=pltpu.CompilerParams(vmem_limit_bytes=VMEM_LIMIT),
@@ -286,20 +299,19 @@
     gains = norm_gain.reshape(count, 1, width)
 
     lead_rows = conv_taps.shape[1] - 1
-    edges = lax.ppermute(
-        (noisy_input[row_count - lead_rows :], self_cond[row_count - lead_rows :]), "seq", [(0, 1)]
-    )
-    other_gate, other_up, other_down = (swap(weight) for weight in (gate_weight, up_weight, down_weight))
-    weights = (gate_weight, other_gate, up_weight, other_up)
     chosen = lax.dynamic_index_in_dim(conv_taps, bucket[0], 0, keepdims=False)
     own_gain = lax.dynamic_slice_in_dim(norm_gain, own * width, width, 0)
 
     def mix(noisy, cond):
         return noisy.astype(jnp.float32) + cond_gain * cond.astype(jnp.float32)
 
+    edges = lax.ppermute(
+        mix(noisy_input[row_count - lead_rows :], self_cond[row_count - lead_rows :]), "seq", [(0, 1)]
+    )
+
     def convolve(noisy, cond, edge, start, size):
         if start == 0:
-            extended = jnp.concatenate([mix(*edge), mix(noisy[:size], cond[:size])], axis=0)
+            extended = jnp.concatenate([edge, mix(noisy[:size], cond[:size])], axis=0)
         else:
             where = slice(start - lead_rows, start + size)
             extended = mix(noisy[where], cond[where])
@@ -330,7 +342,10 @@
 
         return term
 
-    block_a = convolve(noisy_input, self_cond, edges, size, size)
+    block_a = convolve(noisy_input, self_cond, None, size, size)
+    later = after((gate_weight, up_weight, down_weight), edges, block_a)
+    other_gate, other_up, other_down = (swap(weight) for weight in later)
+    weights = (gate_weight, other_gate, up_weight, other_up)
     steps_a = gather_step(block_a, [], half)
     later = after((noisy_input, self_cond, edges), steps_a[0])
     block_b = convolve(*later, 0, size)
@@ -369,10 +384,11 @@
         earlier = []
         for which, span in enumerate(spans):
             moved = scatter_send(parts_b[which]) if number else None
-            parts_b[which] = scatter_sums(moved, term_of(opened_b, closed_b, span), count, distance, earlier)
+            tied = (earlier, moved_a)
+            parts_b[which] = scatter_sums(moved, term_of(opened_b, closed_b, span), count, distance, tied)
             earlier = parts_b[which]
         if number == 1:
-            closed_b = close_down(hidden_b, parts_b, moved_a)
+            closed_b = close_down(hidden_b, parts_b)
     moved_b = [scatter_send(part) for part in parts_b]
     terms_b = [term_of(opened_b, closed_b, span) for span in spans]
 

time: 241 us -> 229 us (0.950)
  waiting for transfers between devices: 86.4 us -> 73.4 us
    ppermute x2 -> x1, waiting for transfers between devices: 10.8 us -> 0.01 us  [on_device(): lax.ppermute(mix(noisy_input[row_count - lead_rows:], self_cond[row_count...]
  transfers between devices with their start and end apart: 45 -> 44, of which waited for: 20 -> 24; matrix products, arithmetic and copies ran while one was open for 4% -> 3% of each run, Pallas kernels for 37% -> 42%
where the time goes in v6:
time: 229 us; the launch traced here: 228 us
  Pallas kernels  95.9 us (42%)
  waiting for transfers between devices  73.4 us (32%)
  starting transfers between devices  46.5 us (20%)
  other arithmetic  8.8 us (4%)
  local copies, waits for them, and re-layouts  2.79 us (1%)
    ppermute x40, waiting for transfers between devices, ring_shift(): lax.ppermute(value, 'blk', [(ring[i], ring[(i + steps) % count]) for i in...  73.4 us
    pallas_call x4, Pallas kernels, gate_up(): pl.pallas_call(functools.partial(gate_up_kernel, part * columns, groups,...  63.7 us
    ppermute x40, starting transfers between devices, ring_shift(): lax.ppermute(value, 'blk', [(ring[i], ring[(i + steps) % count]) for i in...  43.5 us
    pallas_call x4, Pallas kernels, down(): pl.pallas_call(functools.partial(down_kernel, start, stop - start), out_s...  32.2 us
  transfers between devices with their start and end apart: 44, of which 24 were waited for; matrix products, arithmetic and copies ran while one was open for 3% of the time, Pallas kernels for 42%

profile of v6, /device:TPU:0, one launch (start us, length us, event | category | flops | bytes accessed | tf_op | source)
XLA Modules:
  0.0 228.4 jit_solution(12783586774716363880)
XLA Ops:
  0.0 0.8 multiply_add_fusion.2
  0.8 2.4 %collective-permute-start = (f32[3,1024]{1,0:T(4,128)S(1)}, f32[3,1024]{1,0:T(4,128)S(1)}, u32[]{:S(2)}, u32[]{:S(2)}) collective-permute-start(f32[3,1024]{1,0:T(4,128)S(1)} %multiply_add_fusion.2), channel_id=1, source_target_pairs={{0,1},{2,3},{4,5},{6,7},{8,9},{10,11},{12,13},{14,15},{16,17},{18,... | collective-permute-start | bytes 36872 | tf_op jit(solution)/shard_map/ppermute | solution.py:308
  3.1 1.5 multiply_add_fusion
  5.3 0.9 constant_dynamic-slice_fusion.2
  6.2 0.5 multiply_convert_fusion.1.refs_0_
  7.4 2.4 %collective-permute-start.1 = (bf16[256,1024]{1,0:T(8,128)(2,1)S(1)}, bf16[256,1024]{1,0:T(8,128)(2,1)S(1)}, u32[]{:S(2)}, u32[]{:S(2)}) collective-permute-start(bf16[256,1024]{1,0:T(8,128)(2,1)S(1)} %multiply_convert_fusion.1.refs_0_), channel_id=1, source_target_pairs={{0,4},{4,8},{8,12},{12,14},{14,10},{10,6},{6,2},{2,0},{1,5},{5,9},... | collective-permute-start | bytes 1572872 | tf_op jit(solution)/shard_map/ppermute | solution.py:55
  9.8 12.5 %collective-permute-done.1.refs_1_ = bf16[256,1024]{1,0:T(8,128)(2,1)S(1)} collective-permute-done((bf16[256,1024]{1,0:T(8,128)(2,1)S(1)}, bf16[256,1024]{1,0:T(8,128)(2,1)S(1)}, u32[]{:S(2)}, u32[]{:S(2)}) %collective-permute-start.1) | collective-permute-done | bytes 524320 | tf_op jit(solution)/shard_map/ppermute | solution.py:55
  22.3 1.5 collective-permute-done.2.refs_2_
  23.8 1.6 collective-permute-start.3
  25.8 11.1 %collective-permute-done.3.refs_3_ = bf16[256,1024]{1,0:T(8,128)(2,1)S(1)} collective-permute-done((bf16[256,1024]{1,0:T(8,128)(2,1)S(1)}, bf16[256,1024]{1,0:T(8,128)(2,1)S(1)}, u32[]{:S(2)}, u32[]{:S(2)}) %collective-permute-start.3) | collective-permute-done | bytes 524320 | tf_op jit(solution)/shard_map/ppermute | solution.py:55
  37.0 1.3 collective-permute-done.4.refs_4_
  38.3 1.6 collective-permute-start.7
  40.3 0.7 dynamic-slice_bitcast_fusion
  41.0 1.4 multiply_add_fusion.1
  42.4 7.8 %collective-permute-done.7.refs_5_ = bf16[256,1024]{1,0:T(8,128)(2,1)S(1)} collective-permute-done((bf16[256,1024]{1,0:T(8,128)(2,1)S(1)}, bf16[256,1024]{1,0:T(8,128)(2,1)S(1)}, u32[]{:S(2)}, u32[]{:S(2)}) %collective-permute-start.7) | collective-permute-done | bytes 524320 | tf_op jit(solution)/shard_map/ppermute | solution.py:55
  50.2 1.4 collective-permute-done.8.refs_6_
  51.7 1.0 slice.332
  52.6 0.5 collective-permute-start.10
  53.1 1.6 collective-permute-start.9
  54.7 0.5 multiply_convert_fusion.refs_0_
  55.2 4.2 %collective-permute-done.10.refs_8_ = bf16[128,1024]{1,0:T(8,128)(2,1)S(1)} collective-permute-done((bf16[128,1024]{1,0:T(8,128)(2,1)S(1)}, bf16[128,1024]{1,0:T(8,128)(2,1)S(1)}, u32[]{:S(2)}, u32[]{:S(2)}) %collective-permute-start.10) | collective-permute-done | bytes 262176 | tf_op jit(solution)/shard_map/ppermute | solution.py:55
  59.4 2.1 collective-permute-start.5
  62.1 15.9 %gate_up.4.first_ref = bf16[256,1024]{1,0:T(8,128)(2,1)S(1)} custom-call(s32[3,8]{1,0:T(4,128)S(1)} %get-tuple-element.221.blocks_ref, bf16[256,1024]{1,0:T(8,128)(2,1)S(1)} %multiply_convert_fusion.1.refs_0_, bf16[256,1024]{1,0:T(8,128)(2,1)S(1)} %collective-permute-done.1.refs_1_, bf16[256,1024]{1,0:T(8,128)(2,1)S(1)} %collective-permute-done.2.refs_2_, ...), custom_call_target="tpu_custom_call" | custom-call | flops 17179869184 | bytes 33554432 | tf_op jit(solution)/shard_map/gate_up/pallas_call | solution.py:157
  78.1 1.6 collective-permute-start.13
  80.1 15.9 %gate_up.5.second_ref = bf16[256,1024]{1,0:T(8,128)(2,1)S(1)} custom-call(s32[3,8]{1,0:T(4,128)S(1)} %get-tuple-element.221.blocks_ref, bf16[256,1024]{1,0:T(8,128)(2,1)S(1)} %multiply_convert_fusion.1.refs_0_, bf16[256,1024]{1,0:T(8,128)(2,1)S(1)} %collective-permute-done.1.refs_1_, bf16[256,1024]{1,0:T(8,128)(2,1)S(1)} %collective-permute-done.2.refs_2_, ...), custom_call_target="tpu_custom_call" | custom-call | flops 17179869184 | bytes 33554432 | tf_op jit(solution)/shard_map/gate_up/pallas_call | solution.py:157
  96.1 1.6 collective-permute-start.15
  98.2 6.7 %down.4 = bf16[3,256,1024]{2,1,0:T(8,128)(2,1)S(1)} custom-call(s32[3,8]{1,0:T(4,128)S(1)} %get-tuple-element.222.tiles_ref, bf16[256,1024]{1,0:T(8,128)(2,1)S(1)} %gate_up.4.first_ref, bf16[256,1024]{1,0:T(8,128)(2,1)S(1)} %gate_up.5.second_ref, bf16[2048,4096]{1,0:T(8,128)(2,1)} %local_ref.7, bf16[2048,4096]{1,0:T(8,128)(2,1)} %collective-permute-done.17.other_ref), custom_call_target="tpu_custom_call" | custom-call | flops 6442450944 | bytes 12582912 | tf_op jit(solution)/shard_map/down/pallas_call | solution.py:228
  105.0 2.4 %collective-permute-done.15.refs_5_ = bf16[256,1024]{1,0:T(8,128)(2,1)S(1)} collective-permute-done((bf16[256,1024]{1,0:T(8,128)(2,1)S(1)}, bf16[256,1024]{1,0:T(8,128)(2,1)S(1)}, u32[]{:S(2)}, u32[]{:S(2)}) %collective-permute-start.15) | collective-permute-done | bytes 524320 | tf_op jit(solution)/shard_map/ppermute | solution.py:55
  107.4 3.2 %collective-permute-done.16.refs_6_ = bf16[256,1024]{1,0:T(8,128)(2,1)S(1)} collective-permute-done((bf16[256,1024]{1,0:T(8,128)(2,1)S(1)}, bf16[256,1024]{1,0:T(8,128)(2,1)S(1)}, u32[]{:S(2)}, u32[]{:S(2)}) %collective-permute-start.16) | collective-permute-done | bytes 524320 | tf_op jit(solution)/shard_map/ppermute | solution.py:55
  110.7 0.7 collective-permute-start.19
  111.4 1.4 collective-permute-start.18
  112.8 2.4 %collective-permute-start.20 = (bf16[128,1024]{1,0:T(8,128)(2,1)S(1)}, bf16[128,1024]{1,0:T(8,128)(2,1)S(1)}, u32[]{:S(2)}, u32[]{:S(2)}) collective-permute-start(bf16[128,1024]{1,0:T(8,128)(2,1)S(1)} %get-tuple-element.139), channel_id=1, source_target_pairs={{0,4},{4,8},{8,12},{12,14},{14,10},{10,6},{6,2},{2,0},{1,5},{5,9},... | collective-permute-start | bytes 786440 | tf_op jit(solution)/shard_map/ppermute | solution.py:55
  115.1 9.3 %down.5 = bf16[5,256,1024]{2,1,0:T(8,128)(2,1)S(1)} custom-call(s32[3,8]{1,0:T(4,128)S(1)} %get-tuple-element.222.tiles_ref, bf16[256,1024]{1,0:T(8,128)(2,1)S(1)} %gate_up.4.first_ref, bf16[256,1024]{1,0:T(8,128)(2,1)S(1)} %gate_up.5.second_ref, bf16[2048,4096]{1,0:T(8,128)(2,1)} %local_ref.7, bf16[2048,4096]{1,0:T(8,128)(2,1)} %collective-permute-done.17.other_ref), custom_call_target="tpu_custom_call" | custom-call | flops 10737418240 | bytes 20971520 | tf_op jit(solution)/shard_map/down/pallas_call | solution.py:228
  124.5 0.9 collective-permute-done.20
  125.7 1.8 collective-permute-start.22
  127.5 0.5 collective-permute-start.23
  128.0 15.9 %gate_up.6.first_ref = bf16[256,1024]{1,0:T(8,128)(2,1)S(1)} custom-call(s32[3,8]{1,0:T(4,128)S(1)} %get-tuple-element.221.blocks_ref, bf16[256,1024]{1,0:T(8,128)(2,1)S(1)} %multiply_convert_fusion.refs_0_, bf16[256,1024]{1,0:T(8,128)(2,1)S(1)} %collective-permute-done.5.refs_1_, bf16[256,1024]{1,0:T(8,128)(2,1)S(1)} %collective-permute-done.6.refs_2_, ...), custom_call_target="tpu_custom_call" | custom-call | flops 17179869184 | bytes 33554432 | tf_op jit(solution)/shard_map/gate_up/pallas_call | solution.py:157
  144.4 1.9 collective-permute-start.25
  146.8 15.9 %gate_up.7.second_ref = bf16[256,1024]{1,0:T(8,128)(2,1)S(1)} custom-call(s32[3,8]{1,0:T(4,128)S(1)} %get-tuple-element.221.blocks_ref, bf16[256,1024]{1,0:T(8,128)(2,1)S(1)} %multiply_convert_fusion.refs_0_, bf16[256,1024]{1,0:T(8,128)(2,1)S(1)} %collective-permute-done.5.refs_1_, bf16[256,1024]{1,0:T(8,128)(2,1)S(1)} %collective-permute-done.6.refs_2_, ...), custom_call_target="tpu_custom_call" | custom-call | flops 17179869184 | bytes 33554432 | tf_op jit(solution)/shard_map/gate_up/pallas_call | solution.py:157
  163.2 2.0 collective-permute-start.26
  165.2 6.7 %down.6 = bf16[3,256,1024]{2,1,0:T(8,128)(2,1)S(1)} custom-call(s32[3,8]{1,0:T(4,128)S(1)} %get-tuple-element.222.tiles_ref, bf16[256,1024]{1,0:T(8,128)(2,1)S(1)} %gate_up.6.first_ref, bf16[256,1024]{1,0:T(8,128)(2,1)S(1)} %gate_up.7.second_ref, bf16[2048,4096]{1,0:T(8,128)(2,1)} %local_ref.7, bf16[2048,4096]{1,0:T(8,128)(2,1)} %collective-permute-done.17.other_ref), custom_call_target="tpu_custom_call" | custom-call | flops 6442450944 | bytes 12582912 | tf_op jit(solution)/shard_map/down/pallas_call | solution.py:228
  172.1 2.8 %collective-permute-done.26 = bf16[256,1024]{1,0:T(8,128)(2,1)S(1)} collective-permute-done((bf16[256,1024]{1,0:T(8,128)(2,1)S(1)}, bf16[256,1024]{1,0:T(8,128)(2,1)S(1)}, u32[]{:S(2)}, u32[]{:S(2)}) %collective-permute-start.26) | collective-permute-done | bytes 524320 | tf_op jit(solution)/shard_map/ppermute | solution.py:55
  174.8 2.4 %collective-permute-done.27 = bf16[256,1024]{1,0:T(8,128)(2,1)S(1)} collective-permute-done((bf16[256,1024]{1,0:T(8,128)(2,1)S(1)}, bf16[256,1024]{1,0:T(8,128)(2,1)S(1)}, u32[]{:S(2)}, u32[]{:S(2)}) %collective-permute-start.27) | collective-permute-done | bytes 524320 | tf_op jit(solution)/shard_map/ppermute | solution.py:55
  177.2 2.5 %collective-permute-start.28 = (bf16[64,1024]{1,0:T(8,128)(2,1)S(1)}, bf16[64,1024]{1,0:T(8,128)(2,1)S(1)}, u32[]{:S(2)}, u32[]{:S(2)}) collective-permute-start(bf16[64,1024]{1,0:T(8,128)(2,1)S(1)} %get-tuple-element.167), channel_id=1, source_target_pairs={{0,4},{4,8},{8,12},{12,14},{14,10},{10,6},{6,2},{2,0},{1,5},{5,9},... | collective-permute-start | bytes 393224 | tf_op jit(solution)/shard_map/ppermute | solution.py:55
  179.7 2.0 collective-permute-start.30
  182.2 3.8 %collective-permute-done.29 = bf16[64,1024]{1,0:T(8,128)(2,1)S(1)} collective-permute-done((bf16[64,1024]{1,0:T(8,128)(2,1)S(1)}, bf16[64,1024]{1,0:T(8,128)(2,1)S(1)}, u32[]{:S(2)}, u32[]{:S(2)}) %collective-permute-start.29) | collective-permute-done | bytes 131104 | tf_op jit(solution)/shard_map/ppermute | solution.py:55
  186.1 2.4 %collective-permute-done.31 = bf16[64,1024]{1,0:T(8,128)(2,1)S(1)} collective-permute-done((bf16[64,1024]{1,0:T(8,128)(2,1)S(1)}, bf16[64,1024]{1,0:T(8,128)(2,1)S(1)}, u32[]{:S(2)}, u32[]{:S(2)}) %collective-permute-start.31) | collective-permute-done | bytes 131104 | tf_op jit(solution)/shard_map/ppermute | solution.py:55
  188.6 1.8 collective-permute-start.38
  190.7 1.7 collective-permute-start.32
  192.8 9.3 %down.7 = bf16[5,256,1024]{2,1,0:T(8,128)(2,1)S(1)} custom-call(s32[3,8]{1,0:T(4,128)S(1)} %get-tuple-element.222.tiles_ref, bf16[256,1024]{1,0:T(8,128)(2,1)S(1)} %gate_up.6.first_ref, bf16[256,1024]{1,0:T(8,128)(2,1)S(1)} %gate_up.7.second_ref, bf16[2048,4096]{1,0:T(8,128)(2,1)} %local_ref.7, bf16[2048,4096]{1,0:T(8,128)(2,1)} %collective-permute-done.17.other_ref), custom_call_target="tpu_custom_call" | custom-call | flops 10737418240 | bytes 20971520 | tf_op jit(solution)/shard_map/down/pallas_call | solution.py:228
  202.1 1.2 collective-permute-done.32
  204.0 1.0 collective-permute-start.35
  205.0 1.0 collective-permute-start.34
  206.1 4.3 %collective-permute-done.35 = bf16[128,1024]{1,0:T(8,128)(2,1)S(1)} collective-permute-done((bf16[128,1024]{1,0:T(8,128)(2,1)S(1)}, bf16[128,1024]{1,0:T(8,128)(2,1)S(1)}, u32[]{:S(2)}, u32[]{:S(2)}) %collective-permute-start.35) | collective-permute-done | bytes 262176 | tf_op jit(solution)/shard_map/ppermute | solution.py:55
  210.4 1.0 collective-permute-done.34
  212.1 1.8 collective-permute-start.40
  214.1 1.8 collective-permute-start.36
  215.9 2.3 %collective-permute-done.41 = bf16[128,1024]{1,0:T(8,128)(2,1)S(1)} collective-permute-done((bf16[128,1024]{1,0:T(8,128)(2,1)S(1)}, bf16[128,1024]{1,0:T(8,128)(2,1)S(1)}, u32[]{:S(2)}, u32[]{:S(2)}) %collective-permute-start.41) | collective-permute-done | bytes 262176 | tf_op jit(solution)/shard_map/ppermute | solution.py:55
  218.7 1.9 collective-permute-start.42
  220.7 0.5 fusion.15
  221.3 3.8 %collective-permute-done.42 = bf16[128,1024]{1,0:T(8,128)(2,1)S(1)} collective-permute-done((bf16[128,1024]{1,0:T(8,128)(2,1)S(1)}, bf16[128,1024]{1,0:T(8,128)(2,1)S(1)}, u32[]{:S(2)}, u32[]{:S(2)}) %collective-permute-start.42) | collective-permute-done | bytes 262176 | tf_op jit(solution)/shard_map/ppermute | solution.py:55
  225.1 1.8 collective-permute-done.43
  226.9 0.5 fusion.33
  227.4 1.0 pad_maximum_fusion.1
  (77 shorter events, 8.4 us)
Async XLA Ops:
  0.0 5.3 %copy-start = (f32[8192]{0:T(1024)S(1)}, f32[8192]{0:T(1024)}, u32[]{:S(2)}) copy-start(f32[8192]{0:T(1024)} %param.15) | copy-start | bytes 98308
  0.8 6.0 %collective-permute-start = (f32[3,1024]{1,0:T(4,128)S(1)}, f32[3,1024]{1,0:T(4,128)S(1)}, u32[]{:S(2)}, u32[]{:S(2)}) collective-permute-start(f32[3,1024]{1,0:T(4,128)S(1)} %multiply_add_fusion.2), channel_id=1, source_target_pairs={{0,1},{2,3},{4,5},{6,7},{8,9},{10,11},{12,13},{14,15},{16,17},{18,... | collective-permute-start | bytes 36872 | tf_op jit(solution)/shard_map/ppermute | solution.py:308
  6.2 34.8 %copy-start.6 = (f32[1024]{0:T(1024)S(1)}, f32[1024]{0:T(1024)}, u32[]{:S(2)}) copy-start(f32[1024]{0:T(1024)} %param.12) | copy-start | bytes 12292
  6.8 55.3 %collective-permute-start.11 = (bf16[4096,2048]{1,0:T(8,128)(2,1)}, bf16[4096,2048]{1,0:T(8,128)(2,1)}, u32[]{:S(2)}, u32[]{:S(2)}) collective-permute-start(bf16[4096,2048]{1,0:T(8,128)(2,1)} %refs_10_.7), channel_id=1, source_target_pairs={{0,1},{1,0},{2,3},{3,2},{4,5},{5,4},{6,7},{7,6},{8,9},{9,8},{10,11... | collective-permute-start | bytes 50331656 | tf_op jit(solution)/shard_map/ppermute | solution.py:59
  6.8 55.2 %collective-permute-start.12 = (bf16[4096,2048]{1,0:T(8,128)(2,1)}, bf16[4096,2048]{1,0:T(8,128)(2,1)}, u32[]{:S(2)}, u32[]{:S(2)}) collective-permute-start(bf16[4096,2048]{1,0:T(8,128)(2,1)} %refs_12_.7), channel_id=1, source_target_pairs={{0,1},{1,0},{2,3},{3,2},{4,5},{5,4},{6,7},{7,6},{8,9},{9,8},{10,11... | collective-permute-start | bytes 50331656 | tf_op jit(solution)/shard_map/ppermute | solution.py:59
  7.3 90.8 %collective-permute-start.17 = (bf16[2048,4096]{1,0:T(8,128)(2,1)}, bf16[2048,4096]{1,0:T(8,128)(2,1)}, u32[]{:S(2)}, u32[]{:S(2)}) collective-permute-start(bf16[2048,4096]{1,0:T(8,128)(2,1)} %local_ref.7), channel_id=1, source_target_pairs={{0,1},{1,0},{2,3},{3,2},{4,5},{5,4},{6,7},{7,6},{8,9},{9,8},{10,11... | collective-permute-start | bytes 50331656 | tf_op jit(solution)/shard_map/ppermute | solution.py:59
  7.4 14.9 %collective-permute-start.1 = (bf16[256,1024]{1,0:T(8,128)(2,1)S(1)}, bf16[256,1024]{1,0:T(8,128)(2,1)S(1)}, u32[]{:S(2)}, u32[]{:S(2)}) collective-permute-start(bf16[256,1024]{1,0:T(8,128)(2,1)S(1)} %multiply_convert_fusion.1.refs_0_), channel_id=1, source_target_pairs={{0,4},{4,8},{8,12},{12,14},{14,10},{10,6},{6,2},{2,0},{1,5},{5,9},... | collective-permute-start | bytes 1572872 | tf_op jit(solution)/shard_map/ppermute | solution.py:55
  9.8 14.0 %collective-permute-start.2 = (bf16[256,1024]{1,0:T(8,128)(2,1)S(1)}, bf16[256,1024]{1,0:T(8,128)(2,1)S(1)}, u32[]{:S(2)}, u32[]{:S(2)}) collective-permute-start(bf16[256,1024]{1,0:T(8,128)(2,1)S(1)} %multiply_convert_fusion.1.refs_0_), channel_id=1, source_target_pairs={{0,2},{4,0},{8,4},{12,8},{14,12},{10,14},{6,10},{2,6},{1,3},{5,1},... | collective-permute-start | bytes 1572872 | tf_op jit(solution)/shard_map/ppermute | solution.py:55
  23.8 13.2 %collective-permute-start.3 = (bf16[256,1024]{1,0:T(8,128)(2,1)S(1)}, bf16[256,1024]{1,0:T(8,128)(2,1)S(1)}, u32[]{:S(2)}, u32[]{:S(2)}) collective-permute-start(bf16[256,1024]{1,0:T(8,128)(2,1)S(1)} %collective-permute-done.1.refs_1_), channel_id=1, source_target_pairs={{0,4},{4,8},{8,12},{12,14},{14,10},{10,6},{6,2},{2,0},{1,5},{5,9},... | collective-permute-start | bytes 1572872 | tf_op jit(solution)/shard_map/ppermute | solution.py:55
  25.4 12.9 %collective-permute-start.4 = (bf16[256,1024]{1,0:T(8,128)(2,1)S(1)}, bf16[256,1024]{1,0:T(8,128)(2,1)S(1)}, u32[]{:S(2)}, u32[]{:S(2)}) collective-permute-start(bf16[256,1024]{1,0:T(8,128)(2,1)S(1)} %collective-permute-done.2.refs_2_), channel_id=1, source_target_pairs={{0,2},{4,0},{8,4},{12,8},{14,12},{10,14},{6,10},{2,6},{1,3},{5,1},... | collective-permute-start | bytes 1572872 | tf_op jit(solution)/shard_map/ppermute | solution.py:55
  38.3 12.0 %collective-permute-start.7 = (bf16[256,1024]{1,0:T(8,128)(2,1)S(1)}, bf16[256,1024]{1,0:T(8,128)(2,1)S(1)}, u32[]{:S(2)}, u32[]{:S(2)}) collective-permute-start(bf16[256,1024]{1,0:T(8,128)(2,1)S(1)} %collective-permute-done.3.refs_3_), channel_id=1, source_target_pairs={{0,4},{4,8},{8,12},{12,14},{14,10},{10,6},{6,2},{2,0},{1,5},{5,9},... | collective-permute-start | bytes 1572872 | tf_op jit(solution)/shard_map/ppermute | solution.py:55
  39.9 11.8 %collective-permute-start.8 = (bf16[256,1024]{1,0:T(8,128)(2,1)S(1)}, bf16[256,1024]{1,0:T(8,128)(2,1)}, u32[]{:S(2)}, u32[]{:S(2)}) collective-permute-start(bf16[256,1024]{1,0:T(8,128)(2,1)S(1)} %collective-permute-done.4.refs_4_), channel_id=1, source_target_pairs={{0,2},{4,0},{8,4},{12,8},{14,12},{10,14},{6,10},{2,6},{1,3},{5,1},... | collective-permute-start | bytes 1572872 | tf_op jit(solution)/shard_map/ppermute | solution.py:55
  50.2 11.8 %copy-start.5 = (bf16[256,1024]{1,0:T(8,128)(2,1)}, bf16[256,1024]{1,0:T(8,128)(2,1)S(1)}, u32[]{:S(2)}) copy-start(bf16[256,1024]{1,0:T(8,128)(2,1)S(1)} %collective-permute-done.7.refs_5_) | copy-start | bytes 1572868
  52.6 6.7 %collective-permute-start.10 = (bf16[128,1024]{1,0:T(8,128)(2,1)S(1)}, bf16[128,1024]{1,0:T(8,128)(2,1)S(1)}, u32[]{:S(2)}, u32[]{:S(2)}) collective-permute-start(bf16[128,1024]{1,0:T(8,128)(2,1)S(1)} %slice.332), channel_id=1, source_target_pairs={{0,2},{4,0},{8,4},{12,8},{14,12},{10,14},{6,10},{2,6},{1,3},{5,1},... | collective-permute-start | bytes 786440 | tf_op jit(solution)/shard_map/ppermute | solution.py:55
  53.1 8.5 %collective-permute-start.9 = (bf16[128,1024]{1,0:T(8,128)(2,1)S(1)}, bf16[128,1024]{1,0:T(8,128)(2,1)S(1)}, u32[]{:S(2)}, u32[]{:S(2)}) collective-permute-start(bf16[128,1024]{1,0:T(8,128)(2,1)S(1)} %slice.331), channel_id=1, source_target_pairs={{0,4},{4,8},{8,12},{12,14},{14,10},{10,6},{6,2},{2,0},{1,5},{5,9},... | collective-permute-start | bytes 786440 | tf_op jit(solution)/shard_map/ppermute | solution.py:55
  59.4 18.7 %collective-permute-start.5 = (bf16[256,1024]{1,0:T(8,128)(2,1)S(1)}, bf16[256,1024]{1,0:T(8,128)(2,1)S(1)}, u32[]{:S(2)}, u32[]{:S(2)}) collective-permute-start(bf16[256,1024]{1,0:T(8,128)(2,1)S(1)} %multiply_convert_fusion.refs_0_), channel_id=1, source_target_pairs={{0,4},{4,8},{8,12},{12,14},{14,10},{10,6},{6,2},{2,0},{1,5},{5,9},... | collective-permute-start | bytes 1572872 | tf_op jit(solution)/shard_map/ppermute | solution.py:55
  61.6 16.4 %collective-permute-start.6 = (bf16[256,1024]{1,0:T(8,128)(2,1)S(1)}, bf16[256,1024]{1,0:T(8,128)(2,1)S(1)}, u32[]{:S(2)}, u32[]{:S(2)}) collective-permute-start(bf16[256,1024]{1,0:T(8,128)(2,1)S(1)} %multiply_convert_fusion.refs_0_), channel_id=1, source_target_pairs={{0,2},{4,0},{8,4},{12,8},{14,12},{10,14},{6,10},{2,6},{1,3},{5,1},... | collective-permute-start | bytes 1572872 | tf_op jit(solution)/shard_map/ppermute | solution.py:55
  78.1 18.0 %collective-permute-start.13 = (bf16[256,1024]{1,0:T(8,128)(2,1)S(1)}, bf16[256,1024]{1,0:T(8,128)(2,1)S(1)}, u32[]{:S(2)}, u32[]{:S(2)}) collective-permute-start(bf16[256,1024]{1,0:T(8,128)(2,1)S(1)} %collective-permute-done.5.refs_1_), channel_id=1, source_target_pairs={{0,4},{4,8},{8,12},{12,14},{14,10},{10,6},{6,2},{2,0},{1,5},{5,9},... | collective-permute-start | bytes 1572872 | tf_op jit(solution)/shard_map/ppermute | solution.py:55
  79.7 16.4 %collective-permute-start.14 = (bf16[256,1024]{1,0:T(8,128)(2,1)S(1)}, bf16[256,1024]{1,0:T(8,128)(2,1)S(1)}, u32[]{:S(2)}, u32[]{:S(2)}) collective-permute-start(bf16[256,1024]{1,0:T(8,128)(2,1)S(1)} %collective-permute-done.6.refs_2_), channel_id=1, source_target_pairs={{0,2},{4,0},{8,4},{12,8},{14,12},{10,14},{6,10},{2,6},{1,3},{5,1},... | collective-permute-start | bytes 1572872 | tf_op jit(solution)/shard_map/ppermute | solution.py:55
  96.1 11.3 %collective-permute-start.15 = (bf16[256,1024]{1,0:T(8,128)(2,1)S(1)}, bf16[256,1024]{1,0:T(8,128)(2,1)S(1)}, u32[]{:S(2)}, u32[]{:S(2)}) collective-permute-start(bf16[256,1024]{1,0:T(8,128)(2,1)S(1)} %collective-permute-done.13.refs_3_), channel_id=1, source_target_pairs={{0,4},{4,8},{8,12},{12,14},{14,10},{10,6},{6,2},{2,0},{1,5},{5,9},... | collective-permute-start | bytes 1572872 | tf_op jit(solution)/shard_map/ppermute | solution.py:55
  97.7 12.9 %collective-permute-start.16 = (bf16[256,1024]{1,0:T(8,128)(2,1)S(1)}, bf16[256,1024]{1,0:T(8,128)(2,1)S(1)}, u32[]{:S(2)}, u32[]{:S(2)}) collective-permute-start(bf16[256,1024]{1,0:T(8,128)(2,1)S(1)} %collective-permute-done.14.refs_4_), channel_id=1, source_target_pairs={{0,2},{4,0},{8,4},{12,8},{14,12},{10,14},{6,10},{2,6},{1,3},{5,1},... | collective-permute-start | bytes 1572872 | tf_op jit(solution)/shard_map/ppermute | solution.py:55
  107.4 17.1 %copy-start.3 = (bf16[256,1024]{1,0:T(8,128)(2,1)}, bf16[256,1024]{1,0:T(8,128)(2,1)S(1)}, u32[]{:S(2)}) copy-start(bf16[256,1024]{1,0:T(8,128)(2,1)S(1)} %collective-permute-done.15.refs_5_) | copy-start | bytes 1572868
  110.6 13.9 %copy-start.4 = (bf16[256,1024]{1,0:T(8,128)(2,1)}, bf16[256,1024]{1,0:T(8,128)(2,1)S(1)}, u32[]{:S(2)}) copy-start(bf16[256,1024]{1,0:T(8,128)(2,1)S(1)} %collective-permute-done.16.refs_6_) | copy-start | bytes 1572868
  110.7 17.4 %collective-permute-start.19 = (bf16[128,1024]{1,0:T(8,128)(2,1)S(1)}, bf16[128,1024]{1,0:T(8,128)(2,1)S(1)}, u32[]{:S(2)}, u32[]{:S(2)}) collective-permute-start(bf16[128,1024]{1,0:T(8,128)(2,1)S(1)} %slice.334), channel_id=1, source_target_pairs={{0,2},{4,0},{8,4},{12,8},{14,12},{10,14},{6,10},{2,6},{1,3},{5,1},... | collective-permute-start | bytes 786440 | tf_op jit(solution)/shard_map/ppermute | solution.py:55
  111.4 16.7 %collective-permute-start.18 = (bf16[128,1024]{1,0:T(8,128)(2,1)S(1)}, bf16[128,1024]{1,0:T(8,128)(2,1)S(1)}, u32[]{:S(2)}, u32[]{:S(2)}) collective-permute-start(bf16[128,1024]{1,0:T(8,128)(2,1)S(1)} %slice.333), channel_id=1, source_target_pairs={{0,4},{4,8},{8,12},{12,14},{14,10},{10,6},{6,2},{2,0},{1,5},{5,9},... | collective-permute-start | bytes 786440 | tf_op jit(solution)/shard_map/ppermute | solution.py:55
  112.8 12.7 %collective-permute-start.20 = (bf16[128,1024]{1,0:T(8,128)(2,1)S(1)}, bf16[128,1024]{1,0:T(8,128)(2,1)S(1)}, u32[]{:S(2)}, u32[]{:S(2)}) collective-permute-start(bf16[128,1024]{1,0:T(8,128)(2,1)S(1)} %get-tuple-element.139), channel_id=1, source_target_pairs={{0,4},{4,8},{8,12},{12,14},{14,10},{10,6},{6,2},{2,0},{1,5},{5,9},... | collective-permute-start | bytes 786440 | tf_op jit(solution)/shard_map/ppermute | solution.py:55
  115.1 10.3 %collective-permute-start.21 = (bf16[128,1024]{1,0:T(8,128)(2,1)S(1)}, bf16[128,1024]{1,0:T(8,128)(2,1)S(1)}, u32[]{:S(2)}, u32[]{:S(2)}) collective-permute-start(bf16[128,1024]{1,0:T(8,128)(2,1)S(1)} %get-tuple-element.140), channel_id=1, source_target_pairs={{0,2},{4,0},{8,4},{12,8},{14,12},{10,14},{6,10},{2,6},{1,3},{5,1},... | collective-permute-start | bytes 786440 | tf_op jit(solution)/shard_map/ppermute | solution.py:55
  125.7 18.3 %collective-permute-start.22 = (bf16[256,1024]{1,0:T(8,128)(2,1)S(1)}, bf16[256,1024]{1,0:T(8,128)(2,1)S(1)}, u32[]{:S(2)}, u32[]{:S(2)}) collective-permute-start(bf16[256,1024]{1,0:T(8,128)(2,1)S(1)} %pad_maximum_fusion.2), channel_id=1, source_target_pairs={{0,4},{4,8},{8,12},{12,14},{14,10},{10,6},{6,2},{2,0},{1,5},{5,9},... | collective-permute-start | bytes 1572872 | tf_op jit(solution)/shard_map/ppermute | solution.py:55
  127.5 16.4 %collective-permute-start.23 = (bf16[256,1024]{1,0:T(8,128)(2,1)S(1)}, bf16[256,1024]{1,0:T(8,128)(2,1)S(1)}, u32[]{:S(2)}, u32[]{:S(2)}) collective-permute-start(bf16[256,1024]{1,0:T(8,128)(2,1)S(1)} %pad_maximum_fusion.3), channel_id=1, source_target_pairs={{0,2},{4,0},{8,4},{12,8},{14,12},{10,14},{6,10},{2,6},{1,3},{5,1},... | collective-permute-start | bytes 1572872 | tf_op jit(solution)/shard_map/ppermute | solution.py:55
  144.4 18.3 %collective-permute-start.25 = (bf16[256,1024]{1,0:T(8,128)(2,1)S(1)}, bf16[256,1024]{1,0:T(8,128)(2,1)S(1)}, u32[]{:S(2)}, u32[]{:S(2)}) collective-permute-start(bf16[256,1024]{1,0:T(8,128)(2,1)S(1)} %get-tuple-element.197), channel_id=1, source_target_pairs={{0,2},{4,0},{8,4},{12,8},{14,12},{10,14},{6,10},{2,6},{1,3},{5,1},... | collective-permute-start | bytes 1572872 | tf_op jit(solution)/shard_map/ppermute | solution.py:55
  146.3 16.4 %collective-permute-start.24 = (bf16[256,1024]{1,0:T(8,128)(2,1)S(1)}, bf16[256,1024]{1,0:T(8,128)(2,1)S(1)}, u32[]{:S(2)}, u32[]{:S(2)}) collective-permute-start(bf16[256,1024]{1,0:T(8,128)(2,1)S(1)} %get-tuple-element.198), channel_id=1, source_target_pairs={{0,4},{4,8},{8,12},{12,14},{14,10},{10,6},{6,2},{2,0},{1,5},{5,9},... | collective-permute-start | bytes 1572872 | tf_op jit(solution)/shard_map/ppermute | solution.py:55
  163.2 11.7 %collective-permute-start.26 = (bf16[256,1024]{1,0:T(8,128)(2,1)S(1)}, bf16[256,1024]{1,0:T(8,128)(2,1)S(1)}, u32[]{:S(2)}, u32[]{:S(2)}) collective-permute-start(bf16[256,1024]{1,0:T(8,128)(2,1)S(1)} %get-tuple-element.195), channel_id=1, source_target_pairs={{0,4},{4,8},{8,12},{12,14},{14,10},{10,6},{6,2},{2,0},{1,5},{5,9},... | collective-permute-start | bytes 1572872 | tf_op jit(solution)/shard_map/ppermute | solution.py:55
  165.2 12.0 %collective-permute-start.27 = (bf16[256,1024]{1,0:T(8,128)(2,1)S(1)}, bf16[256,1024]{1,0:T(8,128)(2,1)S(1)}, u32[]{:S(2)}, u32[]{:S(2)}) collective-permute-start(bf16[256,1024]{1,0:T(8,128)(2,1)S(1)} %get-tuple-element.196), channel_id=1, source_target_pairs={{0,2},{4,0},{8,4},{12,8},{14,12},{10,14},{6,10},{2,6},{1,3},{5,1},... | collective-permute-start | bytes 1572872 | tf_op jit(solution)/shard_map/ppermute | solution.py:55
  177.2 5.0 %collective-permute-start.28 = (bf16[64,1024]{1,0:T(8,128)(2,1)S(1)}, bf16[64,1024]{1,0:T(8,128)(2,1)S(1)}, u32[]{:S(2)}, u32[]{:S(2)}) collective-permute-start(bf16[64,1024]{1,0:T(8,128)(2,1)S(1)} %get-tuple-element.167), channel_id=1, source_target_pairs={{0,4},{4,8},{8,12},{12,14},{14,10},{10,6},{6,2},{2,0},{1,5},{5,9},... | collective-permute-start | bytes 393224 | tf_op jit(solution)/shard_map/ppermute | solution.py:55
  179.7 6.3 %collective-permute-start.29 = (bf16[64,1024]{1,0:T(8,128)(2,1)S(1)}, bf16[64,1024]{1,0:T(8,128)(2,1)S(1)}, u32[]{:S(2)}, u32[]{:S(2)}) collective-permute-start(bf16[64,1024]{1,0:T(8,128)(2,1)S(1)} %get-tuple-element.168), channel_id=1, source_target_pairs={{0,2},{4,0},{8,4},{12,8},{14,12},{10,14},{6,10},{2,6},{1,3},{5,1},... | collective-permute-start | bytes 393224 | tf_op jit(solution)/shard_map/ppermute | solution.py:55
  179.7 6.4 %collective-permute-start.30 = (bf16[64,1024]{1,0:T(8,128)(2,1)S(1)}, bf16[64,1024]{1,0:T(8,128)(2,1)S(1)}, u32[]{:S(2)}, u32[]{:S(2)}) collective-permute-start(bf16[64,1024]{1,0:T(8,128)(2,1)S(1)} %get-tuple-element.171), channel_id=1, source_target_pairs={{0,4},{4,8},{8,12},{12,14},{14,10},{10,6},{6,2},{2,0},{1,5},{5,9},... | collective-permute-start | bytes 393224 | tf_op jit(solution)/shard_map/ppermute | solution.py:55
  181.8 6.7 %collective-permute-start.31 = (bf16[64,1024]{1,0:T(8,128)(2,1)S(1)}, bf16[64,1024]{1,0:T(8,128)(2,1)S(1)}, u32[]{:S(2)}, u32[]{:S(2)}) collective-permute-start(bf16[64,1024]{1,0:T(8,128)(2,1)S(1)} %get-tuple-element.172), channel_id=1, source_target_pairs={{0,2},{4,0},{8,4},{12,8},{14,12},{10,14},{6,10},{2,6},{1,3},{5,1},... | collective-permute-start | bytes 393224 | tf_op jit(solution)/shard_map/ppermute | solution.py:55
  188.6 17.5 %collective-permute-start.38 = (bf16[128,1024]{1,0:T(8,128)(2,1)S(1)}, bf16[128,1024]{1,0:T(8,128)(2,1)S(1)}, u32[]{:S(2)}, u32[]{:S(2)}) collective-permute-start(bf16[128,1024]{1,0:T(8,128)(2,1)S(1)} %pad_maximum_fusion.6), channel_id=1, source_target_pairs={{0,4},{4,8},{8,12},{12,14},{14,10},{10,6},{6,2},{2,0},{1,5},{5,9},... | collective-permute-start | bytes 786440 | tf_op jit(solution)/shard_map/ppermute | solution.py:55
  190.4 15.7 %collective-permute-start.39 = (bf16[128,1024]{1,0:T(8,128)(2,1)S(1)}, bf16[128,1024]{1,0:T(8,128)(2,1)S(1)}, u32[]{:S(2)}, u32[]{:S(2)}) collective-permute-start(bf16[128,1024]{1,0:T(8,128)(2,1)S(1)} %pad_maximum_fusion.7), channel_id=1, source_target_pairs={{0,2},{4,0},{8,4},{12,8},{14,12},{10,14},{6,10},{2,6},{1,3},{5,1},... | collective-permute-start | bytes 786440 | tf_op jit(solution)/shard_map/ppermute | solution.py:55
  190.7 12.6 %collective-permute-start.32 = (bf16[128,1024]{1,0:T(8,128)(2,1)S(1)}, bf16[128,1024]{1,0:T(8,128)(2,1)S(1)}, u32[]{:S(2)}, u32[]{:S(2)}) collective-permute-start(bf16[128,1024]{1,0:T(8,128)(2,1)S(1)} %pad_maximum_fusion.4), channel_id=1, source_target_pairs={{0,4},{4,8},{8,12},{12,14},{14,10},{10,6},{6,2},{2,0},{1,5},{5,9},... | collective-permute-start | bytes 786440 | tf_op jit(solution)/shard_map/ppermute | solution.py:55
  192.5 11.3 %collective-permute-start.33 = (bf16[128,1024]{1,0:T(8,128)(2,1)S(1)}, bf16[128,1024]{1,0:T(8,128)(2,1)S(1)}, u32[]{:S(2)}, u32[]{:S(2)}) collective-permute-start(bf16[128,1024]{1,0:T(8,128)(2,1)S(1)} %pad_maximum_fusion.5), channel_id=1, source_target_pairs={{0,2},{4,0},{8,4},{12,8},{14,12},{10,14},{6,10},{2,6},{1,3},{5,1},... | collective-permute-start | bytes 786440 | tf_op jit(solution)/shard_map/ppermute | solution.py:55
  204.0 6.4 %collective-permute-start.35 = (bf16[128,1024]{1,0:T(8,128)(2,1)S(1)}, bf16[128,1024]{1,0:T(8,128)(2,1)S(1)}, u32[]{:S(2)}, u32[]{:S(2)}) collective-permute-start(bf16[128,1024]{1,0:T(8,128)(2,1)S(1)} %get-tuple-element.193), channel_id=1, source_target_pairs={{0,2},{4,0},{8,4},{12,8},{14,12},{10,14},{6,10},{2,6},{1,3},{5,1},... | collective-permute-start | bytes 786440 | tf_op jit(solution)/shard_map/ppermute | solution.py:55
  205.0 15.7 %copy-start.1 = (bf16[512,1024]{1,0:T(8,128)(2,1)S(1)}, bf16[512,1024]{1,0:T(8,128)(2,1)}, u32[]{:S(2)}) copy-start(bf16[512,1024]{1,0:T(8,128)(2,1)} %param.11) | copy-start | bytes 3145732
  205.0 15.7 %copy-start.2 = (bf16[512,1024]{1,0:T(8,128)(2,1)S(1)}, bf16[512,1024]{1,0:T(8,128)(2,1)}, u32[]{:S(2)}) copy-start(bf16[512,1024]{1,0:T(8,128)(2,1)} %param.10) | copy-start | bytes 3145732
  205.0 6.4 %collective-permute-start.34 = (bf16[128,1024]{1,0:T(8,128)(2,1)S(1)}, bf16[128,1024]{1,0:T(8,128)(2,1)S(1)}, u32[]{:S(2)}, u32[]{:S(2)}) collective-permute-start(bf16[128,1024]{1,0:T(8,128)(2,1)S(1)} %get-tuple-element.194), channel_id=1, source_target_pairs={{0,4},{4,8},{8,12},{12,14},{14,10},{10,6},{6,2},{2,0},{1,5},{5,9},... | collective-permute-start | bytes 786440 | tf_op jit(solution)/shard_map/ppermute | solution.py:55
  211.8 6.4 %collective-permute-start.41 = (bf16[128,1024]{1,0:T(8,128)(2,1)S(1)}, bf16[128,1024]{1,0:T(8,128)(2,1)S(1)}, u32[]{:S(2)}, u32[]{:S(2)}) collective-permute-start(bf16[128,1024]{1,0:T(8,128)(2,1)S(1)} %get-tuple-element.190), channel_id=1, source_target_pairs={{0,2},{4,0},{8,4},{12,8},{14,12},{10,14},{6,10},{2,6},{1,3},{5,1},... | collective-permute-start | bytes 786440 | tf_op jit(solution)/shard_map/ppermute | solution.py:55
  212.1 6.4 %collective-permute-start.40 = (bf16[128,1024]{1,0:T(8,128)(2,1)S(1)}, bf16[128,1024]{1,0:T(8,128)(2,1)S(1)}, u32[]{:S(2)}, u32[]{:S(2)}) collective-permute-start(bf16[128,1024]{1,0:T(8,128)(2,1)S(1)} %get-tuple-element.191), channel_id=1, source_target_pairs={{0,4},{4,8},{8,12},{12,14},{14,10},{10,6},{6,2},{2,0},{1,5},{5,9},... | collective-permute-start | bytes 786440 | tf_op jit(solution)/shard_map/ppermute | solution.py:55
  213.9 7.3 %collective-permute-start.37 = (bf16[128,1024]{1,0:T(8,128)(2,1)S(1)}, bf16[128,1024]{1,0:T(8,128)(2,1)S(1)}, u32[]{:S(2)}, u32[]{:S(2)}) collective-permute-start(bf16[128,1024]{1,0:T(8,128)(2,1)S(1)} %get-tuple-element.189), channel_id=1, source_target_pairs={{0,2},{4,0},{8,4},{12,8},{14,12},{10,14},{6,10},{2,6},{1,3},{5,1},... | collective-permute-start | bytes 786440 | tf_op jit(solution)/shard_map/ppermute | solution.py:55
  214.1 7.2 %collective-permute-start.36 = (bf16[128,1024]{1,0:T(8,128)(2,1)S(1)}, bf16[128,1024]{1,0:T(8,128)(2,1)S(1)}, u32[]{:S(2)}, u32[]{:S(2)}) collective-permute-start(bf16[128,1024]{1,0:T(8,128)(2,1)S(1)} %get-tuple-element.192), channel_id=1, source_target_pairs={{0,4},{4,8},{8,12},{12,14},{14,10},{10,6},{6,2},{2,0},{1,5},{5,9},... | collective-permute-start | bytes 786440 | tf_op jit(solution)/shard_map/ppermute | solution.py:55
  218.7 6.4 %collective-permute-start.42 = (bf16[128,1024]{1,0:T(8,128)(2,1)S(1)}, bf16[128,1024]{1,0:T(8,128)(2,1)S(1)}, u32[]{:S(2)}, u32[]{:S(2)}) collective-permute-start(bf16[128,1024]{1,0:T(8,128)(2,1)S(1)} %get-tuple-element.187), channel_id=1, source_target_pairs={{0,4},{4,8},{8,12},{12,14},{14,10},{10,6},{6,2},{2,0},{1,5},{5,9},... | collective-permute-start | bytes 786440 | tf_op jit(solution)/shard_map/ppermute | solution.py:55
  220.5 6.4 %collective-permute-start.43 = (bf16[128,1024]{1,0:T(8,128)(2,1)S(1)}, bf16[128,1024]{1,0:T(8,128)(2,1)S(1)}, u32[]{:S(2)}, u32[]{:S(2)}) collective-permute-start(bf16[128,1024]{1,0:T(8,128)(2,1)S(1)} %get-tuple-element.188), channel_id=1, source_target_pairs={{0,2},{4,0},{8,4},{12,8},{14,12},{10,14},{6,10},{2,6},{1,3},{5,1},... | collective-permute-start | bytes 786440 | tf_op jit(solution)/shard_map/ppermute | solution.py:55

commit v7 on v6

--- a/solution.py
+++ b/solution.py
@@ -63,84 +63,78 @@
     return lax.optimization_barrier((value, earlier))[0]
 
 
-def gate_up_kernel(columns, groups, mean_of, blocks_ref, *refs):
+def gate_up_kernel(columns, mean_of, blocks_ref, *refs):
     refs = list(refs)
     stacked, sums, stat, weights, sems, weight_sems = refs[-6:]
     out_ref = refs[-7]
     gains_ref = refs[-12]
-    sources = [refs[-11:-9], refs[-9:-7]]
+    own_and_other = refs[-11:-7:2], refs[-10:-7:2]
     pieces = refs[:-12]
     rows = stacked.shape[0]
     count, width = gains_ref.shape[0], gains_ref.shape[2]
-    size, tile = count // groups, weights.shape[-1]
-    group, which = pl.program_id(0), pl.program_id(1)
-    step, steps = group * 2 + which, 2 * groups
-    parts = 2 if size < 4 else 1
-
-    def fetch(number, act):
-        slot, kind, first = lax.rem(number, DEEP), lax.rem(number, 2), lax.div(number, 2) * size
-        for index in range(size):
-            for gate_or_up in range(2):
-                for other in range(2):
-
-                    @pl.when((kind == gate_or_up) & (blocks_ref[0, first + index] == 1 - other))
-                    def chosen(index=index, source=sources[gate_or_up][other]):
-                        begin = pl.multiple_of(blocks_ref[1, first + index] * width, width)
-                        height = width // parts
-                        for part in range(parts):
-                            act(
-                                pltpu.make_async_copy(
-                                    source.at[pl.ds(begin + part * height, height), pl.ds(columns, tile)],
-                                    weights.at[slot, pl.ds(index * width + part * height, height)],
-                                    weight_sems.at[slot, index, part],
-                                )
-                            )
+    tile = weights.shape[-1]
+    step = pl.program_id(0)
+    height = width // 2
+
+    def fetch(number):
+        slot = lax.rem(number, DEEP)
+        begin = pl.multiple_of(blocks_ref[1, number] * width, width)
+        for other in range(2):
+
+            @pl.when(blocks_ref[0, number] == 1 - other)
+            def chosen(sources=own_and_other[other]):
+                for which, source in enumerate(sources):
+                    for part in range(2):
+                        pltpu.make_async_copy(
+                            source.at[pl.ds(begin + part * height, height), pl.ds(columns, tile)],
+                            weights.at[slot, which, pl.ds(part * height, height)],
+                            weight_sems.at[slot, which],
+                        ).start()
 
     def gather_pieces(wanted, act):
         start = 0
         for number, source in enumerate(pieces):
-            height = source.shape[0]
-            if start // rows // size == wanted:
-                target = stacked.at[pl.ds(start % rows, height), pl.ds((start // rows) * width, width)]
+            size = source.shape[0]
+            if start // rows == wanted:
+                target = stacked.at[pl.ds(start % rows, size), pl.ds((start // rows) * width, width)]
                 act(pltpu.make_async_copy(source, target, sems.at[number]))
-            start += height
+            start += size
 
     @pl.when(step == 0)
     def first():
         gather_pieces(0, lambda copy: copy.start())
-        for number in range(min(DEEP - 1, steps)):
-            fetch(jnp.int32(number), lambda copy: copy.start())
-        for wanted in range(1, groups):
+        for number in range(min(DEEP - 1, count)):
+            fetch(jnp.int32(number))
+        for wanted in range(1, count):
             gather_pieces(wanted, lambda copy: copy.start())
         sums[...] = jnp.zeros_like(sums)
         stat[...] = jnp.zeros_like(stat)
 
-    @pl.when(step + DEEP - 1 < steps)
+    @pl.when(step + DEEP - 1 < count)
     def ahead():
-        fetch(step + DEEP - 1, lambda copy: copy.start())
-
-    for wanted in range(groups):
-
-        @pl.when((group == wanted) & (which == 0))
+        fetch(step + DEEP - 1)
+
+    for wanted in range(count):
+
+        @pl.when(step == wanted)
         def arrived(wanted=wanted):
             gather_pieces(wanted, lambda copy: copy.wait())
 
-    fetch(step, lambda copy: copy.wait())
-    begin = pl.multiple_of(group * (size * width), size * width)
-    values = stacked[:, pl.ds(begin, size * width)]
-    sums[which] += jnp.dot(values, weights[lax.rem(step, DEEP)], preferred_element_type=jnp.float32)
+    slot = lax.rem(step, DEEP)
+    block = stacked[:, pl.ds(pl.multiple_of(step * width, width), width)]
+    gain = gains_ref[blocks_ref[2, step]]
+    weight = 1.0 / (gain * gain)
     squares = stat[...]
-    for index in range(size // 2):
-        place = group * size + which * (size // 2) + index
-        gain = gains_ref[blocks_ref[2, place]]
-        weight = 1.0 / (gain * gain)
-        block = stacked[:, pl.ds(pl.multiple_of(place * width, width), width)].astype(jnp.float32)
-        for column in range(0, width, LANES):
-            value = block[:, column : column + LANES]
-            squares = squares + value * value * weight[:, column : column + LANES]
+    for column in range(0, width, LANES):
+        value = block[:, column : column + LANES].astype(jnp.float32)
+        squares = squares + value * value * weight[:, column : column + LANES]
     stat[...] = squares
-
-    @pl.when(step == steps - 1)
+    for which in range(2):
+        sample = own_and_other[0][which].at[pl.ds(0, width), pl.ds(columns, tile)]
+        pltpu.make_async_copy(sample, weights.at[slot, which], weight_sems.at[slot, which]).wait()
+        sums[which] += jnp.dot(block, weights[slot, which], preferred_element_type=jnp.float32)
+
+    @pl.when(step == count - 1)
     def activate():
         inv = lax.rsqrt(jnp.sum(stat[...], axis=1, keepdims=True) / mean_of + 1e-05)
         gate = sums[0] * inv
@@ -151,28 +145,26 @@
     rows, width = pieces[0].shape
     count = blocks.shape[1]
     columns = weights[0].shape[1] // 2
-    size = max(2, 2048 // width)
-    groups = count // size
     anywhere = pl.BlockSpec(memory_space=pl.ANY)
     return pl.pallas_call(
-        functools.partial(gate_up_kernel, part * columns, groups, width * count),
+        functools.partial(gate_up_kernel, part * columns, width * count),
         out_shape=jax.ShapeDtypeStruct((rows, columns), jnp.bfloat16),
         grid_spec=pltpu.PrefetchScalarGridSpec(
             num_scalar_prefetch=1,
-            grid=(groups, 2),
+            grid=(count,),
             in_specs=[
                 *[anywhere] * len(pieces),
-                pl.BlockSpec(gains.shape, lambda n, w, blocks: (0, 0, 0)),
+                pl.BlockSpec(gains.shape, lambda n, blocks: (0, 0, 0)),
                 *[anywhere] * 4,
             ],
-            out_specs=pl.BlockSpec((rows, columns), lambda n, w, blocks: (0, 0)),
+            out_specs=pl.BlockSpec((rows, columns), lambda n, blocks: (0, 0)),
             scratch_shapes=[
                 pltpu.VMEM((rows, count * width), jnp.bfloat16),
                 pltpu.VMEM((2, rows, columns), jnp.float32),
                 pltpu.VMEM((rows, LANES), jnp.float32),
-                pltpu.VMEM((DEEP, size * width, columns), jnp.bfloat16),
+                pltpu.VMEM((DEEP, 2, width, columns), jnp.bfloat16),
                 pltpu.SemaphoreType.DMA((len(pieces),)),
-                pltpu.SemaphoreType.DMA((DEEP, size, 2)),
+                pltpu.SemaphoreType.DMA((DEEP, 2)),
             ],
         ),
         compiler_params=pltpu.CompilerParams(vmem_limit_bytes=VMEM_LIMIT),
@@ -189,7 +181,7 @@
     step = pl.program_id(0)
     depth, width = buffer.shape[1:]
 
-    def fetch(number, act):
+    def fetch(number):
         slot = lax.rem(number, DEEP)
         for kind, source in ((1, local_ref), (0, other_ref)):
 
@@ -198,25 +190,24 @@
                 column = pl.multiple_of(tiles_ref[1, number + start] * width, width)
                 for part in range(PARTS):
                     row = pl.ds(part * (depth // PARTS), depth // PARTS)
-                    act(
-                        pltpu.make_async_copy(
-                            source.at[row, pl.ds(column, width)], buffer.at[slot, row], sems.at[slot, part]
-                        )
-                    )
+                    pltpu.make_async_copy(
+                        source.at[row, pl.ds(column, width)], buffer.at[slot, row], sems.at[slot]
+                    ).start()
 
     @pl.when(step == 0)
     def first():
         for number in range(min(DEEP - 1, steps)):
-            fetch(jnp.int32(number), lambda copy: copy.start())
+            fetch(jnp.int32(number))
         hidden[:, : depth // 2] = first_ref[...]
         hidden[:, depth // 2 :] = second_ref[...]
 
     @pl.when(step + DEEP - 1 < steps)
     def ahead():
-        fetch(step + DEEP - 1, lambda copy: copy.start())
-
-    fetch(step, lambda copy: copy.wait())
-    weight = buffer[lax.rem(step, DEEP)]
+        fetch(step + DEEP - 1)
+
+    slot = lax.rem(step, DEEP)
+    pltpu.make_async_copy(local_ref.at[:, pl.ds(0, width)], buffer.at[slot], sems.at[slot]).wait()
+    weight = buffer[slot]
     out_ref[0] = jnp.dot(hidden[...], weight, preferred_element_type=jnp.float32).astype(jnp.bfloat16)
 
 
@@ -236,7 +227,7 @@
             scratch_shapes=[
                 pltpu.VMEM((rows, depth), jnp.bfloat16),
                 pltpu.VMEM((DEEP, depth, width), jnp.bfloat16),
-                pltpu.SemaphoreType.DMA((DEEP, PARTS)),
+                pltpu.SemaphoreType.DMA((DEEP,)),
             ],
         ),
         compiler_params=pltpu.CompilerParams(vmem_limit_bytes=VMEM_LIMIT),
@@ -325,9 +316,12 @@
     size = row_count // 2
     early = min(3, count - 1)
 
-    def matmul(part, block, steps, *earlier):
-        pieces = after([block, *(piece for step in steps for piece in step)], *earlier)
-        return gate_up(part, blocks, pieces, gains, weights)
+    def matmul(part, block, streams, *earlier):
+        pieces = [block]
+        for step in range(half - 1):
+            pieces += [steps[step][way] for way in range(2) for steps in streams]
+        pieces += [piece for steps in streams for piece in steps[half - 1]]
+        return gate_up(part, blocks, after(pieces, *earlier), gains, weights)
 
     def open_down(hidden, *earlier):
         return down(0, early, tiles, after(hidden, *earlier), down_weight, other_down, width)
@@ -353,10 +347,10 @@
         steps_a = gather_step(block_a, steps_a, half)
     steps_b = gather_step(block_b, [], half, steps_a[min(1, half - 2)])
     steps_a = gather_step(block_a, steps_a, half)
-    hidden_a = [matmul(0, block_a, steps_a)]
+    hidden_a = [matmul(0, block_a, [steps_a])]
     first_b = steps_b[-1]
     steps_b = gather_step(block_b, steps_b, half, hidden_a)
-    hidden_a += [matmul(1, block_a, steps_a, hidden_a, first_b)]
+    hidden_a += [matmul(1, block_a, [steps_a], hidden_a, first_b)]
     second_b = steps_b[-1]
     steps_b = gather_step(block_b, steps_b, half, hidden_a)
     opened_a = open_down(hidden_a, second_b)
@@ -369,9 +363,9 @@
     distances = list(range(half - 1, 0, -1))
     moved_a = scatter_send(scatter_sums(None, term_a, count, half, third_b))
     sums_a = scatter_sums(moved_a, term_a, count, distances.pop(0))
-    hidden_b = [matmul(0, block_b, steps_b, closed_a, sums_a)]
+    hidden_b = [matmul(0, block_b, [steps_b], closed_a, sums_a)]
     sums_a = scatter_sums(scatter_send(sums_a), term_a, count, distances.pop(0))
-    hidden_b += [matmul(1, block_b, steps_b, hidden_b, sums_a)]
+    hidden_b += [matmul(1, block_b, [steps_b], hidden_b, sums_a)]
     for distance in distances:
         sums_a = scatter_sums(scatter_send(sums_a), term_a, count, distance)
     opened_b = open_down(hidden_b, sums_a)
@@ -380,8 +374,8 @@
     distances = list(range(half, 0, -1))
     parts_b = [None, None]
     closed_b = None
+    earlier = []
     for number, distance in enumerate(distances):
-        earlier = []
         for which, span in enumerate(spans):
             moved = scatter_send(parts_b[which]) if number else None
             tied = (earlier, moved_a)

time: 229 us -> 221 us (0.965)
  waiting for transfers between devices: 73.4 us -> 67.6 us
    ppermute x40, waiting for transfers between devices: 73.4 us -> 67.5 us  [ring_shift(): lax.ppermute(value, 'blk', [(ring[i], ring[(i + steps) % count]) for i in...]
  transfers between devices with their start and end apart: 44 -> 44, of which waited for: 24 -> 24; matrix products, arithmetic and copies ran while one was open for 3% -> 4% of each run, Pallas kernels for 42% -> 43%
where the time goes in v7:
time: 221 us; the launch traced here: 220 us
  Pallas kernels  93.9 us (42%)
  waiting for transfers between devices  67.6 us (31%)
  starting transfers between devices  46.2 us (21%)
  other arithmetic  8.78 us (4%)
  local copies, waits for them, and re-layouts  2.79 us (1%)
    ppermute x40, waiting for transfers between devices, ring_shift(): lax.ppermute(value, 'blk', [(ring[i], ring[(i + steps) % count]) for i in...  67.5 us
    pallas_call x4, Pallas kernels, gate_up(): pl.pallas_call(functools.partial(gate_up_kernel, part * columns, width *...  62.1 us
    ppermute x40, starting transfers between devices, ring_shift(): lax.ppermute(value, 'blk', [(ring[i], ring[(i + steps) % count]) for i in...  43.2 us
    pallas_call x4, Pallas kernels, down(): pl.pallas_call(functools.partial(down_kernel, start, stop - start), out_s...  31.8 us
  transfers between devices with their start and end apart: 44, of which 24 were waited for; matrix products, arithmetic and copies ran while one was open for 4% of the time, Pallas kernels for 43%

profile of v7, /device:TPU:0, one launch (start us, length us, event | category | flops | bytes accessed | tf_op | source)
XLA Modules:
  0.0 220.3 jit_solution(8057298863968165170)
XLA Ops:
  0.0 0.8 multiply_add_fusion.2
  0.8 2.4 %collective-permute-start = (f32[3,1024]{1,0:T(4,128)S(1)}, f32[3,1024]{1,0:T(4,128)S(1)}, u32[]{:S(2)}, u32[]{:S(2)}) collective-permute-start(f32[3,1024]{1,0:T(4,128)S(1)} %multiply_add_fusion.2), channel_id=1, source_target_pairs={{0,1},{2,3},{4,5},{6,7},{8,9},{10,11},{12,13},{14,15},{16,17},{18,... | collective-permute-start | bytes 36872 | tf_op jit(solution)/shard_map/ppermute | solution.py:299
  3.1 1.5 multiply_add_fusion
  5.3 0.9 constant_dynamic-slice_fusion.2
  6.2 0.5 multiply_convert_fusion.1.refs_0_
  7.4 2.4 %collective-permute-start.1 = (bf16[256,1024]{1,0:T(8,128)(2,1)S(1)}, bf16[256,1024]{1,0:T(8,128)(2,1)S(1)}, u32[]{:S(2)}, u32[]{:S(2)}) collective-permute-start(bf16[256,1024]{1,0:T(8,128)(2,1)S(1)} %multiply_convert_fusion.1.refs_0_), channel_id=1, source_target_pairs={{0,4},{4,8},{8,12},{12,14},{14,10},{10,6},{6,2},{2,0},{1,5},{5,9},... | collective-permute-start | bytes 1572872 | tf_op jit(solution)/shard_map/ppermute | solution.py:55
  9.8 12.5 %collective-permute-done.1.refs_1_ = bf16[256,1024]{1,0:T(8,128)(2,1)S(1)} collective-permute-done((bf16[256,1024]{1,0:T(8,128)(2,1)S(1)}, bf16[256,1024]{1,0:T(8,128)(2,1)S(1)}, u32[]{:S(2)}, u32[]{:S(2)}) %collective-permute-start.1) | collective-permute-done | bytes 524320 | tf_op jit(solution)/shard_map/ppermute | solution.py:55
  22.3 1.5 collective-permute-done.2.refs_2_
  23.8 1.6 collective-permute-start.3
  25.8 11.1 %collective-permute-done.3.refs_3_ = bf16[256,1024]{1,0:T(8,128)(2,1)S(1)} collective-permute-done((bf16[256,1024]{1,0:T(8,128)(2,1)S(1)}, bf16[256,1024]{1,0:T(8,128)(2,1)S(1)}, u32[]{:S(2)}, u32[]{:S(2)}) %collective-permute-start.3) | collective-permute-done | bytes 524320 | tf_op jit(solution)/shard_map/ppermute | solution.py:55
  37.0 1.3 collective-permute-done.4.refs_4_
  38.3 1.6 collective-permute-start.7
  40.3 0.7 dynamic-slice_bitcast_fusion
  41.0 1.4 multiply_add_fusion.1
  42.4 7.8 %collective-permute-done.7.refs_5_ = bf16[256,1024]{1,0:T(8,128)(2,1)S(1)} collective-permute-done((bf16[256,1024]{1,0:T(8,128)(2,1)S(1)}, bf16[256,1024]{1,0:T(8,128)(2,1)S(1)}, u32[]{:S(2)}, u32[]{:S(2)}) %collective-permute-start.7) | collective-permute-done | bytes 524320 | tf_op jit(solution)/shard_map/ppermute | solution.py:55
  50.2 1.4 collective-permute-done.8.refs_6_
  51.7 1.0 slice.332
  52.6 0.5 collective-permute-start.10
  53.1 1.6 collective-permute-start.9
  54.7 0.5 multiply_convert_fusion.refs_0_
  55.2 4.2 %collective-permute-done.10.refs_8_ = bf16[128,1024]{1,0:T(8,128)(2,1)S(1)} collective-permute-done((bf16[128,1024]{1,0:T(8,128)(2,1)S(1)}, bf16[128,1024]{1,0:T(8,128)(2,1)S(1)}, u32[]{:S(2)}, u32[]{:S(2)}) %collective-permute-start.10) | collective-permute-done | bytes 262176 | tf_op jit(solution)/shard_map/ppermute | solution.py:55
  59.4 2.1 collective-permute-start.5
  62.1 15.5 %gate_up.4.first_ref = bf16[256,1024]{1,0:T(8,128)(2,1)S(1)} custom-call(s32[3,8]{1,0:T(4,128)S(1)} %get-tuple-element.221.blocks_ref, bf16[256,1024]{1,0:T(8,128)(2,1)S(1)} %multiply_convert_fusion.1.refs_0_, bf16[256,1024]{1,0:T(8,128)(2,1)S(1)} %collective-permute-done.1.refs_1_, bf16[256,1024]{1,0:T(8,128)(2,1)S(1)} %collective-permute-done.2.refs_2_, ...), custom_call_target="tpu_custom_call" | custom-call | flops 17179869184 | bytes 33554432 | tf_op jit(solution)/shard_map/gate_up/pallas_call | solution.py:149
  77.6 1.6 collective-permute-start.13
  79.7 15.5 %gate_up.5.second_ref = bf16[256,1024]{1,0:T(8,128)(2,1)S(1)} custom-call(s32[3,8]{1,0:T(4,128)S(1)} %get-tuple-element.221.blocks_ref, bf16[256,1024]{1,0:T(8,128)(2,1)S(1)} %multiply_convert_fusion.1.refs_0_, bf16[256,1024]{1,0:T(8,128)(2,1)S(1)} %collective-permute-done.1.refs_1_, bf16[256,1024]{1,0:T(8,128)(2,1)S(1)} %collective-permute-done.2.refs_2_, ...), custom_call_target="tpu_custom_call" | custom-call | flops 17179869184 | bytes 33554432 | tf_op jit(solution)/shard_map/gate_up/pallas_call | solution.py:149
  95.3 1.6 collective-permute-start.15
  97.3 6.6 %down.4 = bf16[3,256,1024]{2,1,0:T(8,128)(2,1)S(1)} custom-call(s32[3,8]{1,0:T(4,128)S(1)} %get-tuple-element.222.tiles_ref, bf16[256,1024]{1,0:T(8,128)(2,1)S(1)} %gate_up.4.first_ref, bf16[256,1024]{1,0:T(8,128)(2,1)S(1)} %gate_up.5.second_ref, bf16[2048,4096]{1,0:T(8,128)(2,1)} %local_ref.7, bf16[2048,4096]{1,0:T(8,128)(2,1)} %collective-permute-done.17.other_ref), custom_call_target="tpu_custom_call" | custom-call | flops 6442450944 | bytes 12582912 | tf_op jit(solution)/shard_map/down/pallas_call | solution.py:219
  104.1 2.5 %collective-permute-done.15.refs_5_ = bf16[256,1024]{1,0:T(8,128)(2,1)S(1)} collective-permute-done((bf16[256,1024]{1,0:T(8,128)(2,1)S(1)}, bf16[256,1024]{1,0:T(8,128)(2,1)S(1)}, u32[]{:S(2)}, u32[]{:S(2)}) %collective-permute-start.15) | collective-permute-done | bytes 524320 | tf_op jit(solution)/shard_map/ppermute | solution.py:55
  106.6 3.2 %collective-permute-done.16.refs_6_ = bf16[256,1024]{1,0:T(8,128)(2,1)S(1)} collective-permute-done((bf16[256,1024]{1,0:T(8,128)(2,1)S(1)}, bf16[256,1024]{1,0:T(8,128)(2,1)S(1)}, u32[]{:S(2)}, u32[]{:S(2)}) %collective-permute-start.16) | collective-permute-done | bytes 524320 | tf_op jit(solution)/shard_map/ppermute | solution.py:55
  109.8 0.7 collective-permute-start.19
  110.5 1.4 collective-permute-start.18
  111.9 2.4 %collective-permute-start.20 = (bf16[128,1024]{1,0:T(8,128)(2,1)S(1)}, bf16[128,1024]{1,0:T(8,128)(2,1)S(1)}, u32[]{:S(2)}, u32[]{:S(2)}) collective-permute-start(bf16[128,1024]{1,0:T(8,128)(2,1)S(1)} %get-tuple-element.139), channel_id=1, source_target_pairs={{0,4},{4,8},{8,12},{12,14},{14,10},{10,6},{6,2},{2,0},{1,5},{5,9},... | collective-permute-start | bytes 786440 | tf_op jit(solution)/shard_map/ppermute | solution.py:55
  114.3 9.2 %down.5 = bf16[5,256,1024]{2,1,0:T(8,128)(2,1)S(1)} custom-call(s32[3,8]{1,0:T(4,128)S(1)} %get-tuple-element.222.tiles_ref, bf16[256,1024]{1,0:T(8,128)(2,1)S(1)} %gate_up.4.first_ref, bf16[256,1024]{1,0:T(8,128)(2,1)S(1)} %gate_up.5.second_ref, bf16[2048,4096]{1,0:T(8,128)(2,1)} %local_ref.7, bf16[2048,4096]{1,0:T(8,128)(2,1)} %collective-permute-done.17.other_ref), custom_call_target="tpu_custom_call" | custom-call | flops 10737418240 | bytes 20971520 | tf_op jit(solution)/shard_map/down/pallas_call | solution.py:219
  123.6 1.0 collective-permute-done.20
  124.9 1.8 collective-permute-start.22
  127.2 15.5 %gate_up.6.first_ref = bf16[256,1024]{1,0:T(8,128)(2,1)S(1)} custom-call(s32[3,8]{1,0:T(4,128)S(1)} %get-tuple-element.221.blocks_ref, bf16[256,1024]{1,0:T(8,128)(2,1)S(1)} %multiply_convert_fusion.refs_0_, bf16[256,1024]{1,0:T(8,128)(2,1)S(1)} %collective-permute-done.5.refs_1_, bf16[256,1024]{1,0:T(8,128)(2,1)S(1)} %collective-permute-done.6.refs_2_, ...), custom_call_target="tpu_custom_call" | custom-call | flops 17179869184 | bytes 33554432 | tf_op jit(solution)/shard_map/gate_up/pallas_call | solution.py:149
  143.2 1.8 collective-permute-start.25
  145.0 0.6 collective-permute-start.24
  145.6 15.5 %gate_up.7.second_ref = bf16[256,1024]{1,0:T(8,128)(2,1)S(1)} custom-call(s32[3,8]{1,0:T(4,128)S(1)} %get-tuple-element.221.blocks_ref, bf16[256,1024]{1,0:T(8,128)(2,1)S(1)} %multiply_convert_fusion.refs_0_, bf16[256,1024]{1,0:T(8,128)(2,1)S(1)} %collective-permute-done.5.refs_1_, bf16[256,1024]{1,0:T(8,128)(2,1)S(1)} %collective-permute-done.6.refs_2_, ...), custom_call_target="tpu_custom_call" | custom-call | flops 17179869184 | bytes 33554432 | tf_op jit(solution)/shard_map/gate_up/pallas_call | solution.py:149
  161.5 2.0 collective-permute-start.26
  163.6 6.6 %down.6 = bf16[3,256,1024]{2,1,0:T(8,128)(2,1)S(1)} custom-call(s32[3,8]{1,0:T(4,128)S(1)} %get-tuple-element.222.tiles_ref, bf16[256,1024]{1,0:T(8,128)(2,1)S(1)} %gate_up.6.first_ref, bf16[256,1024]{1,0:T(8,128)(2,1)S(1)} %gate_up.7.second_ref, bf16[2048,4096]{1,0:T(8,128)(2,1)} %local_ref.7, bf16[2048,4096]{1,0:T(8,128)(2,1)} %collective-permute-done.17.other_ref), custom_call_target="tpu_custom_call" | custom-call | flops 6442450944 | bytes 12582912 | tf_op jit(solution)/shard_map/down/pallas_call | solution.py:219
  170.3 2.4 %collective-permute-done.26 = bf16[256,1024]{1,0:T(8,128)(2,1)S(1)} collective-permute-done((bf16[256,1024]{1,0:T(8,128)(2,1)S(1)}, bf16[256,1024]{1,0:T(8,128)(2,1)S(1)}, u32[]{:S(2)}, u32[]{:S(2)}) %collective-permute-start.26) | collective-permute-done | bytes 524320 | tf_op jit(solution)/shard_map/ppermute | solution.py:55
  172.8 2.4 %collective-permute-done.27 = bf16[256,1024]{1,0:T(8,128)(2,1)S(1)} collective-permute-done((bf16[256,1024]{1,0:T(8,128)(2,1)S(1)}, bf16[256,1024]{1,0:T(8,128)(2,1)S(1)}, u32[]{:S(2)}, u32[]{:S(2)}) %collective-permute-start.27) | collective-permute-done | bytes 524320 | tf_op jit(solution)/shard_map/ppermute | solution.py:55
  175.2 2.2 collective-permute-start.28
  177.4 2.0 collective-permute-start.30
  179.4 0.7 collective-permute-done.28
  180.2 3.3 %collective-permute-done.29 = bf16[64,1024]{1,0:T(8,128)(2,1)S(1)} collective-permute-done((bf16[64,1024]{1,0:T(8,128)(2,1)S(1)}, bf16[64,1024]{1,0:T(8,128)(2,1)S(1)}, u32[]{:S(2)}, u32[]{:S(2)}) %collective-permute-start.29) | collective-permute-done | bytes 131104 | tf_op jit(solution)/shard_map/ppermute | solution.py:55
  183.6 2.7 %collective-permute-done.31 = bf16[64,1024]{1,0:T(8,128)(2,1)S(1)} collective-permute-done((bf16[64,1024]{1,0:T(8,128)(2,1)S(1)}, bf16[64,1024]{1,0:T(8,128)(2,1)S(1)}, u32[]{:S(2)}, u32[]{:S(2)}) %collective-permute-start.31) | collective-permute-done | bytes 131104 | tf_op jit(solution)/shard_map/ppermute | solution.py:55
  186.4 1.4 collective-permute-start.36
  187.8 0.7 collective-permute-start.37
  188.5 1.3 collective-permute-start.32
  189.9 0.7 collective-permute-start.33
  190.5 9.2 %down.7 = bf16[5,256,1024]{2,1,0:T(8,128)(2,1)S(1)} custom-call(s32[3,8]{1,0:T(4,128)S(1)} %get-tuple-element.222.tiles_ref, bf16[256,1024]{1,0:T(8,128)(2,1)S(1)} %gate_up.6.first_ref, bf16[256,1024]{1,0:T(8,128)(2,1)S(1)} %gate_up.7.second_ref, bf16[2048,4096]{1,0:T(8,128)(2,1)} %local_ref.7, bf16[2048,4096]{1,0:T(8,128)(2,1)} %collective-permute-done.17.other_ref), custom_call_target="tpu_custom_call" | custom-call | flops 10737418240 | bytes 20971520 | tf_op jit(solution)/shard_map/down/pallas_call | solution.py:219
  199.8 0.8 collective-permute-done.32
  201.0 1.9 collective-permute-start.34
  203.3 1.9 collective-permute-start.40
  205.2 2.1 collective-permute-done.35
  207.6 0.9 collective-permute-start.39
  208.5 1.2 collective-permute-start.38
  210.4 1.9 collective-permute-start.42
  213.0 4.7 %collective-permute-done.42 = bf16[128,1024]{1,0:T(8,128)(2,1)S(1)} collective-permute-done((bf16[128,1024]{1,0:T(8,128)(2,1)S(1)}, bf16[128,1024]{1,0:T(8,128)(2,1)S(1)}, u32[]{:S(2)}, u32[]{:S(2)}) %collective-permute-start.42) | collective-permute-done | bytes 262176 | tf_op jit(solution)/shard_map/ppermute | solution.py:55
  217.7 1.0 collective-permute-done.43
  218.7 0.5 fusion.33
  219.2 1.0 pad_maximum_fusion.1
  (78 shorter events, 7.7 us)
Async XLA Ops:
  0.0 5.3 %copy-start = (f32[8192]{0:T(1024)S(1)}, f32[8192]{0:T(1024)}, u32[]{:S(2)}) copy-start(f32[8192]{0:T(1024)} %param.15) | copy-start | bytes 98308
  0.8 6.0 %collective-permute-start = (f32[3,1024]{1,0:T(4,128)S(1)}, f32[3,1024]{1,0:T(4,128)S(1)}, u32[]{:S(2)}, u32[]{:S(2)}) collective-permute-start(f32[3,1024]{1,0:T(4,128)S(1)} %multiply_add_fusion.2), channel_id=1, source_target_pairs={{0,1},{2,3},{4,5},{6,7},{8,9},{10,11},{12,13},{14,15},{16,17},{18,... | collective-permute-start | bytes 36872 | tf_op jit(solution)/shard_map/ppermute | solution.py:299
  6.2 34.8 %copy-start.6 = (f32[1024]{0:T(1024)S(1)}, f32[1024]{0:T(1024)}, u32[]{:S(2)}) copy-start(f32[1024]{0:T(1024)} %param.12) | copy-start | bytes 12292
  6.8 55.3 %collective-permute-start.11 = (bf16[4096,2048]{1,0:T(8,128)(2,1)}, bf16[4096,2048]{1,0:T(8,128)(2,1)}, u32[]{:S(2)}, u32[]{:S(2)}) collective-permute-start(bf16[4096,2048]{1,0:T(8,128)(2,1)} %refs_10_.7), channel_id=1, source_target_pairs={{0,1},{1,0},{2,3},{3,2},{4,5},{5,4},{6,7},{7,6},{8,9},{9,8},{10,11... | collective-permute-start | bytes 50331656 | tf_op jit(solution)/shard_map/ppermute | solution.py:59
  6.8 55.2 %collective-permute-start.12 = (bf16[4096,2048]{1,0:T(8,128)(2,1)}, bf16[4096,2048]{1,0:T(8,128)(2,1)}, u32[]{:S(2)}, u32[]{:S(2)}) collective-permute-start(bf16[4096,2048]{1,0:T(8,128)(2,1)} %refs_12_.7), channel_id=1, source_target_pairs={{0,1},{1,0},{2,3},{3,2},{4,5},{5,4},{6,7},{7,6},{8,9},{9,8},{10,11... | collective-permute-start | bytes 50331656 | tf_op jit(solution)/shard_map/ppermute | solution.py:59
  7.3 90.0 %collective-permute-start.17 = (bf16[2048,4096]{1,0:T(8,128)(2,1)}, bf16[2048,4096]{1,0:T(8,128)(2,1)}, u32[]{:S(2)}, u32[]{:S(2)}) collective-permute-start(bf16[2048,4096]{1,0:T(8,128)(2,1)} %local_ref.7), channel_id=1, source_target_pairs={{0,1},{1,0},{2,3},{3,2},{4,5},{5,4},{6,7},{7,6},{8,9},{9,8},{10,11... | collective-permute-start | bytes 50331656 | tf_op jit(solution)/shard_map/ppermute | solution.py:59
  7.4 14.9 %collective-permute-start.1 = (bf16[256,1024]{1,0:T(8,128)(2,1)S(1)}, bf16[256,1024]{1,0:T(8,128)(2,1)S(1)}, u32[]{:S(2)}, u32[]{:S(2)}) collective-permute-start(bf16[256,1024]{1,0:T(8,128)(2,1)S(1)} %multiply_convert_fusion.1.refs_0_), channel_id=1, source_target_pairs={{0,4},{4,8},{8,12},{12,14},{14,10},{10,6},{6,2},{2,0},{1,5},{5,9},... | collective-permute-start | bytes 1572872 | tf_op jit(solution)/shard_map/ppermute | solution.py:55
  9.8 14.0 %collective-permute-start.2 = (bf16[256,1024]{1,0:T(8,128)(2,1)S(1)}, bf16[256,1024]{1,0:T(8,128)(2,1)S(1)}, u32[]{:S(2)}, u32[]{:S(2)}) collective-permute-start(bf16[256,1024]{1,0:T(8,128)(2,1)S(1)} %multiply_convert_fusion.1.refs_0_), channel_id=1, source_target_pairs={{0,2},{4,0},{8,4},{12,8},{14,12},{10,14},{6,10},{2,6},{1,3},{5,1},... | collective-permute-start | bytes 1572872 | tf_op jit(solution)/shard_map/ppermute | solution.py:55
  23.8 13.2 %collective-permute-start.3 = (bf16[256,1024]{1,0:T(8,128)(2,1)S(1)}, bf16[256,1024]{1,0:T(8,128)(2,1)S(1)}, u32[]{:S(2)}, u32[]{:S(2)}) collective-permute-start(bf16[256,1024]{1,0:T(8,128)(2,1)S(1)} %collective-permute-done.1.refs_1_), channel_id=1, source_target_pairs={{0,4},{4,8},{8,12},{12,14},{14,10},{10,6},{6,2},{2,0},{1,5},{5,9},... | collective-permute-start | bytes 1572872 | tf_op jit(solution)/shard_map/ppermute | solution.py:55
  25.4 12.9 %collective-permute-start.4 = (bf16[256,1024]{1,0:T(8,128)(2,1)S(1)}, bf16[256,1024]{1,0:T(8,128)(2,1)S(1)}, u32[]{:S(2)}, u32[]{:S(2)}) collective-permute-start(bf16[256,1024]{1,0:T(8,128)(2,1)S(1)} %collective-permute-done.2.refs_2_), channel_id=1, source_target_pairs={{0,2},{4,0},{8,4},{12,8},{14,12},{10,14},{6,10},{2,6},{1,3},{5,1},... | collective-permute-start | bytes 1572872 | tf_op jit(solution)/shard_map/ppermute | solution.py:55
  38.3 12.0 %collective-permute-start.7 = (bf16[256,1024]{1,0:T(8,128)(2,1)S(1)}, bf16[256,1024]{1,0:T(8,128)(2,1)S(1)}, u32[]{:S(2)}, u32[]{:S(2)}) collective-permute-start(bf16[256,1024]{1,0:T(8,128)(2,1)S(1)} %collective-permute-done.3.refs_3_), channel_id=1, source_target_pairs={{0,4},{4,8},{8,12},{12,14},{14,10},{10,6},{6,2},{2,0},{1,5},{5,9},... | collective-permute-start | bytes 1572872 | tf_op jit(solution)/shard_map/ppermute | solution.py:55
  39.9 11.8 %collective-permute-start.8 = (bf16[256,1024]{1,0:T(8,128)(2,1)S(1)}, bf16[256,1024]{1,0:T(8,128)(2,1)}, u32[]{:S(2)}, u32[]{:S(2)}) collective-permute-start(bf16[256,1024]{1,0:T(8,128)(2,1)S(1)} %collective-permute-done.4.refs_4_), channel_id=1, source_target_pairs={{0,2},{4,0},{8,4},{12,8},{14,12},{10,14},{6,10},{2,6},{1,3},{5,1},... | collective-permute-start | bytes 1572872 | tf_op jit(solution)/shard_map/ppermute | solution.py:55
  50.2 11.8 %copy-start.5 = (bf16[256,1024]{1,0:T(8,128)(2,1)}, bf16[256,1024]{1,0:T(8,128)(2,1)S(1)}, u32[]{:S(2)}) copy-start(bf16[256,1024]{1,0:T(8,128)(2,1)S(1)} %collective-permute-done.7.refs_5_) | copy-start | bytes 1572868
  52.6 6.7 %collective-permute-start.10 = (bf16[128,1024]{1,0:T(8,128)(2,1)S(1)}, bf16[128,1024]{1,0:T(8,128)(2,1)S(1)}, u32[]{:S(2)}, u32[]{:S(2)}) collective-permute-start(bf16[128,1024]{1,0:T(8,128)(2,1)S(1)} %slice.332), channel_id=1, source_target_pairs={{0,2},{4,0},{8,4},{12,8},{14,12},{10,14},{6,10},{2,6},{1,3},{5,1},... | collective-permute-start | bytes 786440 | tf_op jit(solution)/shard_map/ppermute | solution.py:55
  53.1 8.5 %collective-permute-start.9 = (bf16[128,1024]{1,0:T(8,128)(2,1)S(1)}, bf16[128,1024]{1,0:T(8,128)(2,1)S(1)}, u32[]{:S(2)}, u32[]{:S(2)}) collective-permute-start(bf16[128,1024]{1,0:T(8,128)(2,1)S(1)} %slice.331), channel_id=1, source_target_pairs={{0,4},{4,8},{8,12},{12,14},{14,10},{10,6},{6,2},{2,0},{1,5},{5,9},... | collective-permute-start | bytes 786440 | tf_op jit(solution)/shard_map/ppermute | solution.py:55
  59.4 18.2 %collective-permute-start.5 = (bf16[256,1024]{1,0:T(8,128)(2,1)S(1)}, bf16[256,1024]{1,0:T(8,128)(2,1)S(1)}, u32[]{:S(2)}, u32[]{:S(2)}) collective-permute-start(bf16[256,1024]{1,0:T(8,128)(2,1)S(1)} %multiply_convert_fusion.refs_0_), channel_id=1, source_target_pairs={{0,4},{4,8},{8,12},{12,14},{14,10},{10,6},{6,2},{2,0},{1,5},{5,9},... | collective-permute-start | bytes 1572872 | tf_op jit(solution)/shard_map/ppermute | solution.py:55
  61.6 16.0 %collective-permute-start.6 = (bf16[256,1024]{1,0:T(8,128)(2,1)S(1)}, bf16[256,1024]{1,0:T(8,128)(2,1)S(1)}, u32[]{:S(2)}, u32[]{:S(2)}) collective-permute-start(bf16[256,1024]{1,0:T(8,128)(2,1)S(1)} %multiply_convert_fusion.refs_0_), channel_id=1, source_target_pairs={{0,2},{4,0},{8,4},{12,8},{14,12},{10,14},{6,10},{2,6},{1,3},{5,1},... | collective-permute-start | bytes 1572872 | tf_op jit(solution)/shard_map/ppermute | solution.py:55
  77.6 17.6 %collective-permute-start.13 = (bf16[256,1024]{1,0:T(8,128)(2,1)S(1)}, bf16[256,1024]{1,0:T(8,128)(2,1)S(1)}, u32[]{:S(2)}, u32[]{:S(2)}) collective-permute-start(bf16[256,1024]{1,0:T(8,128)(2,1)S(1)} %collective-permute-done.5.refs_1_), channel_id=1, source_target_pairs={{0,4},{4,8},{8,12},{12,14},{14,10},{10,6},{6,2},{2,0},{1,5},{5,9},... | collective-permute-start | bytes 1572872 | tf_op jit(solution)/shard_map/ppermute | solution.py:55
  79.3 16.0 %collective-permute-start.14 = (bf16[256,1024]{1,0:T(8,128)(2,1)S(1)}, bf16[256,1024]{1,0:T(8,128)(2,1)S(1)}, u32[]{:S(2)}, u32[]{:S(2)}) collective-permute-start(bf16[256,1024]{1,0:T(8,128)(2,1)S(1)} %collective-permute-done.6.refs_2_), channel_id=1, source_target_pairs={{0,2},{4,0},{8,4},{12,8},{14,12},{10,14},{6,10},{2,6},{1,3},{5,1},... | collective-permute-start | bytes 1572872 | tf_op jit(solution)/shard_map/ppermute | solution.py:55
  95.3 11.3 %collective-permute-start.15 = (bf16[256,1024]{1,0:T(8,128)(2,1)S(1)}, bf16[256,1024]{1,0:T(8,128)(2,1)S(1)}, u32[]{:S(2)}, u32[]{:S(2)}) collective-permute-start(bf16[256,1024]{1,0:T(8,128)(2,1)S(1)} %collective-permute-done.13.refs_3_), channel_id=1, source_target_pairs={{0,4},{4,8},{8,12},{12,14},{14,10},{10,6},{6,2},{2,0},{1,5},{5,9},... | collective-permute-start | bytes 1572872 | tf_op jit(solution)/shard_map/ppermute | solution.py:55
  96.9 12.9 %collective-permute-start.16 = (bf16[256,1024]{1,0:T(8,128)(2,1)S(1)}, bf16[256,1024]{1,0:T(8,128)(2,1)S(1)}, u32[]{:S(2)}, u32[]{:S(2)}) collective-permute-start(bf16[256,1024]{1,0:T(8,128)(2,1)S(1)} %collective-permute-done.14.refs_4_), channel_id=1, source_target_pairs={{0,2},{4,0},{8,4},{12,8},{14,12},{10,14},{6,10},{2,6},{1,3},{5,1},... | collective-permute-start | bytes 1572872 | tf_op jit(solution)/shard_map/ppermute | solution.py:55
  106.6 17.0 %copy-start.3 = (bf16[256,1024]{1,0:T(8,128)(2,1)}, bf16[256,1024]{1,0:T(8,128)(2,1)S(1)}, u32[]{:S(2)}) copy-start(bf16[256,1024]{1,0:T(8,128)(2,1)S(1)} %collective-permute-done.15.refs_5_) | copy-start | bytes 1572868
  109.8 13.8 %copy-start.4 = (bf16[256,1024]{1,0:T(8,128)(2,1)}, bf16[256,1024]{1,0:T(8,128)(2,1)S(1)}, u32[]{:S(2)}) copy-start(bf16[256,1024]{1,0:T(8,128)(2,1)S(1)} %collective-permute-done.16.refs_6_) | copy-start | bytes 1572868
  109.8 17.4 %collective-permute-start.19 = (bf16[128,1024]{1,0:T(8,128)(2,1)S(1)}, bf16[128,1024]{1,0:T(8,128)(2,1)S(1)}, u32[]{:S(2)}, u32[]{:S(2)}) collective-permute-start(bf16[128,1024]{1,0:T(8,128)(2,1)S(1)} %slice.334), channel_id=1, source_target_pairs={{0,2},{4,0},{8,4},{12,8},{14,12},{10,14},{6,10},{2,6},{1,3},{5,1},... | collective-permute-start | bytes 786440 | tf_op jit(solution)/shard_map/ppermute | solution.py:55
  110.5 16.7 %collective-permute-start.18 = (bf16[128,1024]{1,0:T(8,128)(2,1)S(1)}, bf16[128,1024]{1,0:T(8,128)(2,1)S(1)}, u32[]{:S(2)}, u32[]{:S(2)}) collective-permute-start(bf16[128,1024]{1,0:T(8,128)(2,1)S(1)} %slice.333), channel_id=1, source_target_pairs={{0,4},{4,8},{8,12},{12,14},{14,10},{10,6},{6,2},{2,0},{1,5},{5,9},... | collective-permute-start | bytes 786440 | tf_op jit(solution)/shard_map/ppermute | solution.py:55
  111.9 12.7 %collective-permute-start.20 = (bf16[128,1024]{1,0:T(8,128)(2,1)S(1)}, bf16[128,1024]{1,0:T(8,128)(2,1)S(1)}, u32[]{:S(2)}, u32[]{:S(2)}) collective-permute-start(bf16[128,1024]{1,0:T(8,128)(2,1)S(1)} %get-tuple-element.139), channel_id=1, source_target_pairs={{0,4},{4,8},{8,12},{12,14},{14,10},{10,6},{6,2},{2,0},{1,5},{5,9},... | collective-permute-start | bytes 786440 | tf_op jit(solution)/shard_map/ppermute | solution.py:55
  114.3 10.3 %collective-permute-start.21 = (bf16[128,1024]{1,0:T(8,128)(2,1)S(1)}, bf16[128,1024]{1,0:T(8,128)(2,1)S(1)}, u32[]{:S(2)}, u32[]{:S(2)}) collective-permute-start(bf16[128,1024]{1,0:T(8,128)(2,1)S(1)} %get-tuple-element.140), channel_id=1, source_target_pairs={{0,2},{4,0},{8,4},{12,8},{14,12},{10,14},{6,10},{2,6},{1,3},{5,1},... | collective-permute-start | bytes 786440 | tf_op jit(solution)/shard_map/ppermute | solution.py:55
  124.9 17.9 %collective-permute-start.22 = (bf16[256,1024]{1,0:T(8,128)(2,1)S(1)}, bf16[256,1024]{1,0:T(8,128)(2,1)S(1)}, u32[]{:S(2)}, u32[]{:S(2)}) collective-permute-start(bf16[256,1024]{1,0:T(8,128)(2,1)S(1)} %pad_maximum_fusion.2), channel_id=1, source_target_pairs={{0,4},{4,8},{8,12},{12,14},{14,10},{10,6},{6,2},{2,0},{1,5},{5,9},... | collective-permute-start | bytes 1572872 | tf_op jit(solution)/shard_map/ppermute | solution.py:55
  126.7 16.0 %collective-permute-start.23 = (bf16[256,1024]{1,0:T(8,128)(2,1)S(1)}, bf16[256,1024]{1,0:T(8,128)(2,1)S(1)}, u32[]{:S(2)}, u32[]{:S(2)}) collective-permute-start(bf16[256,1024]{1,0:T(8,128)(2,1)S(1)} %pad_maximum_fusion.3), channel_id=1, source_target_pairs={{0,2},{4,0},{8,4},{12,8},{14,12},{10,14},{6,10},{2,6},{1,3},{5,1},... | collective-permute-start | bytes 1572872 | tf_op jit(solution)/shard_map/ppermute | solution.py:55
  143.2 17.9 %collective-permute-start.25 = (bf16[256,1024]{1,0:T(8,128)(2,1)S(1)}, bf16[256,1024]{1,0:T(8,128)(2,1)S(1)}, u32[]{:S(2)}, u32[]{:S(2)}) collective-permute-start(bf16[256,1024]{1,0:T(8,128)(2,1)S(1)} %get-tuple-element.197), channel_id=1, source_target_pairs={{0,2},{4,0},{8,4},{12,8},{14,12},{10,14},{6,10},{2,6},{1,3},{5,1},... | collective-permute-start | bytes 1572872 | tf_op jit(solution)/shard_map/ppermute | solution.py:55
  145.0 16.1 %collective-permute-start.24 = (bf16[256,1024]{1,0:T(8,128)(2,1)S(1)}, bf16[256,1024]{1,0:T(8,128)(2,1)S(1)}, u32[]{:S(2)}, u32[]{:S(2)}) collective-permute-start(bf16[256,1024]{1,0:T(8,128)(2,1)S(1)} %get-tuple-element.198), channel_id=1, source_target_pairs={{0,4},{4,8},{8,12},{12,14},{14,10},{10,6},{6,2},{2,0},{1,5},{5,9},... | collective-permute-start | bytes 1572872 | tf_op jit(solution)/shard_map/ppermute | solution.py:55
  161.5 11.2 %collective-permute-start.26 = (bf16[256,1024]{1,0:T(8,128)(2,1)S(1)}, bf16[256,1024]{1,0:T(8,128)(2,1)S(1)}, u32[]{:S(2)}, u32[]{:S(2)}) collective-permute-start(bf16[256,1024]{1,0:T(8,128)(2,1)S(1)} %get-tuple-element.195), channel_id=1, source_target_pairs={{0,4},{4,8},{8,12},{12,14},{14,10},{10,6},{6,2},{2,0},{1,5},{5,9},... | collective-permute-start | bytes 1572872 | tf_op jit(solution)/shard_map/ppermute | solution.py:55
  163.6 11.6 %collective-permute-start.27 = (bf16[256,1024]{1,0:T(8,128)(2,1)S(1)}, bf16[256,1024]{1,0:T(8,128)(2,1)S(1)}, u32[]{:S(2)}, u32[]{:S(2)}) collective-permute-start(bf16[256,1024]{1,0:T(8,128)(2,1)S(1)} %get-tuple-element.196), channel_id=1, source_target_pairs={{0,2},{4,0},{8,4},{12,8},{14,12},{10,14},{6,10},{2,6},{1,3},{5,1},... | collective-permute-start | bytes 1572872 | tf_op jit(solution)/shard_map/ppermute | solution.py:55
  175.2 5.0 %collective-permute-start.28 = (bf16[64,1024]{1,0:T(8,128)(2,1)S(1)}, bf16[64,1024]{1,0:T(8,128)(2,1)S(1)}, u32[]{:S(2)}, u32[]{:S(2)}) collective-permute-start(bf16[64,1024]{1,0:T(8,128)(2,1)S(1)} %get-tuple-element.167), channel_id=1, source_target_pairs={{0,4},{4,8},{8,12},{12,14},{14,10},{10,6},{6,2},{2,0},{1,5},{5,9},... | collective-permute-start | bytes 393224 | tf_op jit(solution)/shard_map/ppermute | solution.py:55
  177.4 6.0 %collective-permute-start.29 = (bf16[64,1024]{1,0:T(8,128)(2,1)S(1)}, bf16[64,1024]{1,0:T(8,128)(2,1)S(1)}, u32[]{:S(2)}, u32[]{:S(2)}) collective-permute-start(bf16[64,1024]{1,0:T(8,128)(2,1)S(1)} %get-tuple-element.168), channel_id=1, source_target_pairs={{0,2},{4,0},{8,4},{12,8},{14,12},{10,14},{6,10},{2,6},{1,3},{5,1},... | collective-permute-start | bytes 393224 | tf_op jit(solution)/shard_map/ppermute | solution.py:55
  177.4 6.2 %collective-permute-start.30 = (bf16[64,1024]{1,0:T(8,128)(2,1)S(1)}, bf16[64,1024]{1,0:T(8,128)(2,1)S(1)}, u32[]{:S(2)}, u32[]{:S(2)}) collective-permute-start(bf16[64,1024]{1,0:T(8,128)(2,1)S(1)} %get-tuple-element.169), channel_id=1, source_target_pairs={{0,4},{4,8},{8,12},{12,14},{14,10},{10,6},{6,2},{2,0},{1,5},{5,9},... | collective-permute-start | bytes 393224 | tf_op jit(solution)/shard_map/ppermute | solution.py:55
  179.4 6.8 %collective-permute-start.31 = (bf16[64,1024]{1,0:T(8,128)(2,1)S(1)}, bf16[64,1024]{1,0:T(8,128)(2,1)S(1)}, u32[]{:S(2)}, u32[]{:S(2)}) collective-permute-start(bf16[64,1024]{1,0:T(8,128)(2,1)S(1)} %get-tuple-element.170), channel_id=1, source_target_pairs={{0,2},{4,0},{8,4},{12,8},{14,12},{10,14},{6,10},{2,6},{1,3},{5,1},... | collective-permute-start | bytes 393224 | tf_op jit(solution)/shard_map/ppermute | solution.py:55
  186.4 16.6 %collective-permute-start.36 = (bf16[128,1024]{1,0:T(8,128)(2,1)S(1)}, bf16[128,1024]{1,0:T(8,128)(2,1)S(1)}, u32[]{:S(2)}, u32[]{:S(2)}) collective-permute-start(bf16[128,1024]{1,0:T(8,128)(2,1)S(1)} %pad_maximum_fusion.6), channel_id=1, source_target_pairs={{0,4},{4,8},{8,12},{12,14},{14,10},{10,6},{6,2},{2,0},{1,5},{5,9},... | collective-permute-start | bytes 786440 | tf_op jit(solution)/shard_map/ppermute | solution.py:55
  187.8 15.1 %collective-permute-start.37 = (bf16[128,1024]{1,0:T(8,128)(2,1)S(1)}, bf16[128,1024]{1,0:T(8,128)(2,1)S(1)}, u32[]{:S(2)}, u32[]{:S(2)}) collective-permute-start(bf16[128,1024]{1,0:T(8,128)(2,1)S(1)} %pad_maximum_fusion.7), channel_id=1, source_target_pairs={{0,2},{4,0},{8,4},{12,8},{14,12},{10,14},{6,10},{2,6},{1,3},{5,1},... | collective-permute-start | bytes 786440 | tf_op jit(solution)/shard_map/ppermute | solution.py:55
  188.5 12.1 %collective-permute-start.32 = (bf16[128,1024]{1,0:T(8,128)(2,1)S(1)}, bf16[128,1024]{1,0:T(8,128)(2,1)S(1)}, u32[]{:S(2)}, u32[]{:S(2)}) collective-permute-start(bf16[128,1024]{1,0:T(8,128)(2,1)S(1)} %pad_maximum_fusion.4), channel_id=1, source_target_pairs={{0,4},{4,8},{8,12},{12,14},{14,10},{10,6},{6,2},{2,0},{1,5},{5,9},... | collective-permute-start | bytes 786440 | tf_op jit(solution)/shard_map/ppermute | solution.py:55
  189.9 10.8 %collective-permute-start.33 = (bf16[128,1024]{1,0:T(8,128)(2,1)S(1)}, bf16[128,1024]{1,0:T(8,128)(2,1)S(1)}, u32[]{:S(2)}, u32[]{:S(2)}) collective-permute-start(bf16[128,1024]{1,0:T(8,128)(2,1)S(1)} %pad_maximum_fusion.5), channel_id=1, source_target_pairs={{0,2},{4,0},{8,4},{12,8},{14,12},{10,14},{6,10},{2,6},{1,3},{5,1},... | collective-permute-start | bytes 786440 | tf_op jit(solution)/shard_map/ppermute | solution.py:55
  200.8 6.4 %collective-permute-start.35 = (bf16[128,1024]{1,0:T(8,128)(2,1)S(1)}, bf16[128,1024]{1,0:T(8,128)(2,1)S(1)}, u32[]{:S(2)}, u32[]{:S(2)}) collective-permute-start(bf16[128,1024]{1,0:T(8,128)(2,1)S(1)} %get-tuple-element.193), channel_id=1, source_target_pairs={{0,2},{4,0},{8,4},{12,8},{14,12},{10,14},{6,10},{2,6},{1,3},{5,1},... | collective-permute-start | bytes 786440 | tf_op jit(solution)/shard_map/ppermute | solution.py:55
  201.0 11.5 %copy-start.1 = (bf16[512,1024]{1,0:T(8,128)(2,1)S(1)}, bf16[512,1024]{1,0:T(8,128)(2,1)}, u32[]{:S(2)}) copy-start(bf16[512,1024]{1,0:T(8,128)(2,1)} %param.11) | copy-start | bytes 3145732
  201.0 11.5 %copy-start.2 = (bf16[512,1024]{1,0:T(8,128)(2,1)S(1)}, bf16[512,1024]{1,0:T(8,128)(2,1)}, u32[]{:S(2)}) copy-start(bf16[512,1024]{1,0:T(8,128)(2,1)} %param.10) | copy-start | bytes 3145732
  201.0 6.4 %collective-permute-start.34 = (bf16[128,1024]{1,0:T(8,128)(2,1)S(1)}, bf16[128,1024]{1,0:T(8,128)(2,1)S(1)}, u32[]{:S(2)}, u32[]{:S(2)}) collective-permute-start(bf16[128,1024]{1,0:T(8,128)(2,1)S(1)} %get-tuple-element.194), channel_id=1, source_target_pairs={{0,4},{4,8},{8,12},{12,14},{14,10},{10,6},{6,2},{2,0},{1,5},{5,9},... | collective-permute-start | bytes 786440 | tf_op jit(solution)/shard_map/ppermute | solution.py:55
  203.1 6.9 %collective-permute-start.41 = (bf16[128,1024]{1,0:T(8,128)(2,1)S(1)}, bf16[128,1024]{1,0:T(8,128)(2,1)S(1)}, u32[]{:S(2)}, u32[]{:S(2)}) collective-permute-start(bf16[128,1024]{1,0:T(8,128)(2,1)S(1)} %get-tuple-element.191), channel_id=1, source_target_pairs={{0,2},{4,0},{8,4},{12,8},{14,12},{10,14},{6,10},{2,6},{1,3},{5,1},... | collective-permute-start | bytes 786440 | tf_op jit(solution)/shard_map/ppermute | solution.py:55
  203.3 6.9 %collective-permute-start.40 = (bf16[128,1024]{1,0:T(8,128)(2,1)S(1)}, bf16[128,1024]{1,0:T(8,128)(2,1)S(1)}, u32[]{:S(2)}, u32[]{:S(2)}) collective-permute-start(bf16[128,1024]{1,0:T(8,128)(2,1)S(1)} %get-tuple-element.192), channel_id=1, source_target_pairs={{0,4},{4,8},{8,12},{12,14},{14,10},{10,6},{6,2},{2,0},{1,5},{5,9},... | collective-permute-start | bytes 786440 | tf_op jit(solution)/shard_map/ppermute | solution.py:55
  207.6 11.1 %collective-permute-start.39 = (bf16[128,1024]{1,0:T(8,128)(2,1)S(1)}, bf16[128,1024]{1,0:T(8,128)(2,1)S(1)}, u32[]{:S(2)}, u32[]{:S(2)}) collective-permute-start(bf16[128,1024]{1,0:T(8,128)(2,1)S(1)} %get-tuple-element.189), channel_id=1, source_target_pairs={{0,2},{4,0},{8,4},{12,8},{14,12},{10,14},{6,10},{2,6},{1,3},{5,1},... | collective-permute-start | bytes 786440 | tf_op jit(solution)/shard_map/ppermute | solution.py:55
  208.5 10.2 %collective-permute-start.38 = (bf16[128,1024]{1,0:T(8,128)(2,1)S(1)}, bf16[128,1024]{1,0:T(8,128)(2,1)S(1)}, u32[]{:S(2)}, u32[]{:S(2)}) collective-permute-start(bf16[128,1024]{1,0:T(8,128)(2,1)S(1)} %get-tuple-element.190), channel_id=1, source_target_pairs={{0,4},{4,8},{8,12},{12,14},{14,10},{10,6},{6,2},{2,0},{1,5},{5,9},... | collective-permute-start | bytes 786440 | tf_op jit(solution)/shard_map/ppermute | solution.py:55
  210.4 7.3 %collective-permute-start.42 = (bf16[128,1024]{1,0:T(8,128)(2,1)S(1)}, bf16[128,1024]{1,0:T(8,128)(2,1)S(1)}, u32[]{:S(2)}, u32[]{:S(2)}) collective-permute-start(bf16[128,1024]{1,0:T(8,128)(2,1)S(1)} %get-tuple-element.187), channel_id=1, source_target_pairs={{0,4},{4,8},{8,12},{12,14},{14,10},{10,6},{6,2},{2,0},{1,5},{5,9},... | collective-permute-start | bytes 786440 | tf_op jit(solution)/shard_map/ppermute | solution.py:55
  212.3 6.4 %collective-permute-start.43 = (bf16[128,1024]{1,0:T(8,128)(2,1)S(1)}, bf16[128,1024]{1,0:T(8,128)(2,1)S(1)}, u32[]{:S(2)}, u32[]{:S(2)}) collective-permute-start(bf16[128,1024]{1,0:T(8,128)(2,1)S(1)} %get-tuple-element.188), channel_id=1, source_target_pairs={{0,2},{4,0},{8,4},{12,8},{14,12},{10,14},{6,10},{2,6},{1,3},{5,1},... | collective-permute-start | bytes 786440 | tf_op jit(solution)/shard_map/ppermute | solution.py:55

commit v8 on v7

--- a/solution.py
+++ b/solution.py
@@ -63,121 +63,154 @@
     return lax.optimization_barrier((value, earlier))[0]
 
 
-def gate_up_kernel(columns, mean_of, blocks_ref, *refs):
+def gate_up_kernel(fixed, blocks_ref, units_ref, *refs):
+    needed, final, taken, mean_of, length = fixed
     refs = list(refs)
-    stacked, sums, stat, weights, sems, weight_sems = refs[-6:]
-    out_ref = refs[-7]
-    gains_ref = refs[-12]
-    own_and_other = refs[-11:-7:2], refs[-10:-7:2]
-    pieces = refs[:-12]
+    pieces = [[refs.pop(0) for _ in range(parts)] for parts in needed]
+    partial_refs = [refs.pop(0) for _ in taken]
+    gains_ref = refs.pop(0)
+    own_and_other = (refs[0], refs[2]), (refs[1], refs[3])
+    before_ref = refs[4]
+    out_ref, stat_ref, stacked, sums, partial, weights, sems, partial_sems, weight_sems = refs[5:]
     rows = stacked.shape[0]
-    count, width = gains_ref.shape[0], gains_ref.shape[2]
-    tile = weights.shape[-1]
+    width = gains_ref.shape[2]
     step = pl.program_id(0)
-    height = width // 2
+    height = width // PARTS if width % (16 * PARTS) == 0 else width
 
     def fetch(number):
         slot = lax.rem(number, DEEP)
-        begin = pl.multiple_of(blocks_ref[1, number] * width, width)
-        for other in range(2):
-
-            @pl.when(blocks_ref[0, number] == 1 - other)
-            def chosen(sources=own_and_other[other]):
-                for which, source in enumerate(sources):
-                    for part in range(2):
+        block = units_ref[1, number]
+        begin = pl.multiple_of(blocks_ref[1, block] * width, width)
+        for which in range(2):
+            for other in range(2):
+
+                @pl.when((units_ref[0, number] == which) & (blocks_ref[0, block] == 1 - other))
+                def chosen(source=own_and_other[other][which]):
+                    for part in range(width // height):
                         pltpu.make_async_copy(
-                            source.at[pl.ds(begin + part * height, height), pl.ds(columns, tile)],
-                            weights.at[slot, which, pl.ds(part * height, height)],
-                            weight_sems.at[slot, which],
+                            source.at[pl.ds(begin + part * height, height)],
+                            weights.at[slot, pl.ds(part * height, height)],
+                            weight_sems.at[slot],
                         ).start()
 
-    def gather_pieces(wanted, act):
-        start = 0
-        for number, source in enumerate(pieces):
+    def gather_pieces(place, act):
+        row = 0
+        for number, source in enumerate(pieces[place]):
             size = source.shape[0]
-            if start // rows == wanted:
-                target = stacked.at[pl.ds(start % rows, size), pl.ds((start // rows) * width, width)]
-                act(pltpu.make_async_copy(source, target, sems.at[number]))
-            start += size
+            target = stacked.at[pl.ds(row, size), pl.ds(place * width, width)]
+            act(pltpu.make_async_copy(source, target, sems.at[place, number]))
+            row += size
+
+    def partials(act):
+        for number, which in enumerate(taken):
+            act(pltpu.make_async_copy(partial_refs[number], partial.at[which], partial_sems.at[number]))
 
     @pl.when(step == 0)
     def first():
         gather_pieces(0, lambda copy: copy.start())
-        for number in range(min(DEEP - 1, count)):
+        for number in range(min(DEEP - 1, length)):
             fetch(jnp.int32(number))
-        for wanted in range(1, count):
-            gather_pieces(wanted, lambda copy: copy.start())
+        for place in range(1, len(pieces)):
+            gather_pieces(place, lambda copy: copy.start())
+        partials(lambda copy: copy.start())
         sums[...] = jnp.zeros_like(sums)
-        stat[...] = jnp.zeros_like(stat)
-
-    @pl.when(step + DEEP - 1 < count)
+        stat_ref[...] = before_ref[...]
+
+    @pl.when(step + DEEP - 1 < length)
     def ahead():
         fetch(step + DEEP - 1)
 
-    for wanted in range(count):
-
-        @pl.when(step == wanted)
+    place = units_ref[2, step]
+    for wanted in range(len(pieces)):
+
+        @pl.when((place == wanted) & (units_ref[3, step] == 1))
         def arrived(wanted=wanted):
             gather_pieces(wanted, lambda copy: copy.wait())
 
+    block = stacked[:, pl.ds(pl.multiple_of(place * width, width), width)]
+
+    @pl.when(units_ref[4, step] == 1)
+    def square():
+        gain = gains_ref[blocks_ref[2, units_ref[1, step]]]
+        weight = 1.0 / (gain * gain)
+        squares = stat_ref[...]
+        for column in range(0, width, LANES):
+            value = stacked[:, pl.ds(pl.multiple_of(place * width + column, LANES), LANES)].astype(jnp.float32)
+            squares = squares + value * value * weight[:, column : column + LANES]
+        stat_ref[...] = squares
+
     slot = lax.rem(step, DEEP)
-    block = stacked[:, pl.ds(pl.multiple_of(step * width, width), width)]
-    gain = gains_ref[blocks_ref[2, step]]
-    weight = 1.0 / (gain * gain)
-    squares = stat[...]
-    for column in range(0, width, LANES):
-        value = block[:, column : column + LANES].astype(jnp.float32)
-        squares = squares + value * value * weight[:, column : column + LANES]
-    stat[...] = squares
-    for which in range(2):
-        sample = own_and_other[0][which].at[pl.ds(0, width), pl.ds(columns, tile)]
-        pltpu.make_async_copy(sample, weights.at[slot, which], weight_sems.at[slot, which]).wait()
-        sums[which] += jnp.dot(block, weights[slot, which], preferred_element_type=jnp.float32)
-
-    @pl.when(step == count - 1)
-    def activate():
-        inv = lax.rsqrt(jnp.sum(stat[...], axis=1, keepdims=True) / mean_of + 1e-05)
-        gate = sums[0] * inv
-        out_ref[...] = (gate / (1.0 + jnp.exp(-gate)) * (sums[1] * inv)).astype(jnp.bfloat16)
-
-
-def gate_up(part, blocks, pieces, gains, weights):
-    rows, width = pieces[0].shape
+    pltpu.make_async_copy(own_and_other[0][0].at[pl.ds(0, width)], weights.at[slot], weight_sems.at[slot]).wait()
+    which = units_ref[0, step]
+    place_of_sum = which if final else 0
+    sums[place_of_sum] += jnp.dot(block, weights[slot], preferred_element_type=jnp.float32)
+
+    @pl.when(step == length - 1)
+    def finish():
+        if final:
+            partials(lambda copy: copy.wait())
+            inv = lax.rsqrt(jnp.sum(stat_ref[...], axis=1, keepdims=True) / mean_of + 1e-05)
+            gate, up = (sums[kind] + partial[kind] if kind in taken else sums[kind] for kind in range(2))
+            gate = gate * inv
+            out_ref[...] = (gate / (1.0 + jnp.exp(-gate)) * (up * inv)).astype(jnp.bfloat16)
+        else:
+            out_ref[...] = sums[0]
+
+
+def gate_up(units, final, partial, squares, blocks, pieces, gains, weights):
+    sofar, counted = squares
+    rows, width = sofar.shape[0], pieces[0][0].shape[1]
     count = blocks.shape[1]
-    columns = weights[0].shape[1] // 2
+    columns = weights[0].shape[1]
+    used = sorted({block for _, block in units})
+    table = np.zeros((5, len(units)), np.int32)
+    seen = set()
+    for number, (which, block) in enumerate(units):
+        fresh = block not in seen
+        seen.add(block)
+        table[:, number] = which, block, used.index(block), fresh, fresh and block not in counted
+    taken = sorted(partial)
+    operands = [part for block in used for part in pieces[block]] + [partial[which] for which in taken]
+    kinds = sorted({which for which, _ in units})
+    weights = [pair for which in range(2) for pair in weights[2 * kinds[which % len(kinds)] :][:2]]
     anywhere = pl.BlockSpec(memory_space=pl.ANY)
-    return pl.pallas_call(
-        functools.partial(gate_up_kernel, part * columns, width * count),
-        out_shape=jax.ShapeDtypeStruct((rows, columns), jnp.bfloat16),
+    needed = [len(pieces[block]) for block in used]
+    fixed = (needed, final, taken, width * count, len(units))
+    whole = lambda *shape: pl.BlockSpec(shape, lambda n, blocks, units: (0,) * len(shape))
+    sums_shape = (2 if final else 1, rows, columns)
+    out, squares = pl.pallas_call(
+        functools.partial(gate_up_kernel, fixed),
+        out_shape=(
+            jax.ShapeDtypeStruct((rows, columns), jnp.bfloat16 if final else jnp.float32),
+            jax.ShapeDtypeStruct((rows, LANES), jnp.float32),
+        ),
         grid_spec=pltpu.PrefetchScalarGridSpec(
-            num_scalar_prefetch=1,
-            grid=(count,),
-            in_specs=[
-                *[anywhere] * len(pieces),
-                pl.BlockSpec(gains.shape, lambda n, blocks: (0, 0, 0)),
-                *[anywhere] * 4,
-            ],
-            out_specs=pl.BlockSpec((rows, columns), lambda n, blocks: (0, 0)),
+            num_scalar_prefetch=2,
+            grid=(len(units),),
+            in_specs=[*[anywhere] * len(operands), whole(*gains.shape), *[anywhere] * 4, whole(rows, LANES)],
+            out_specs=(whole(rows, columns), whole(rows, LANES)),
             scratch_shapes=[
-                pltpu.VMEM((rows, count * width), jnp.bfloat16),
-                pltpu.VMEM((2, rows, columns), jnp.float32),
-                pltpu.VMEM((rows, LANES), jnp.float32),
-                pltpu.VMEM((DEEP, 2, width, columns), jnp.bfloat16),
-                pltpu.SemaphoreType.DMA((len(pieces),)),
-                pltpu.SemaphoreType.DMA((DEEP, 2)),
+                pltpu.VMEM((rows, len(used) * width), jnp.bfloat16),
+                pltpu.VMEM(sums_shape, jnp.float32),
+                pltpu.VMEM((2 if taken else 1, rows if taken else 8, columns), jnp.float32),
+                pltpu.VMEM((DEEP, width, columns), jnp.bfloat16),
+                pltpu.SemaphoreType.DMA((len(used), max(needed))),
+                pltpu.SemaphoreType.DMA((2,)),
+                pltpu.SemaphoreType.DMA((DEEP,)),
             ],
         ),
         compiler_params=pltpu.CompilerParams(vmem_limit_bytes=VMEM_LIMIT),
         cost_estimate=pl.CostEstimate(
-            flops=8 * rows * count * width * columns,
-            bytes_accessed=4 * count * width * columns,
-            transcendentals=rows * columns,
+            flops=4 * rows * width * columns * len(units),
+            bytes_accessed=2 * width * columns * len(units),
+            transcendentals=rows * columns if final else 0,
         ),
         name="gate_up",
-    )(blocks, *pieces, gains, *weights)
-
-
-def down_kernel(start, steps, tiles_ref, first_ref, second_ref, local_ref, other_ref, out_ref, hidden, buffer, sems):
+    )(blocks, jnp.asarray(table), *operands, gains, *weights, sofar)
+    return out, (squares, counted | set(used))
+
+
+def down_kernel(start, steps, tiles_ref, hidden, local_ref, other_ref, out_ref, buffer, sems):
     step = pl.program_id(0)
     depth, width = buffer.shape[1:]
 
@@ -198,8 +231,6 @@
     def first():
         for number in range(min(DEEP - 1, steps)):
             fetch(jnp.int32(number))
-        hidden[:, : depth // 2] = first_ref[...]
-        hidden[:, depth // 2 :] = second_ref[...]
 
     @pl.when(step + DEEP - 1 < steps)
     def ahead():
@@ -212,9 +243,7 @@
 
 
 def down(start, stop, tiles, hidden, local, other, width):
-    rows = hidden[0].shape[0]
-    depth = local.shape[0]
-    half_spec = pl.BlockSpec((rows, depth // 2), lambda j, tiles: (0, 0))
+    rows, depth = hidden.shape
     anywhere = pl.BlockSpec(memory_space=pl.ANY)
     return pl.pallas_call(
         functools.partial(down_kernel, start, stop - start),
@@ -222,10 +251,9 @@
         grid_spec=pltpu.PrefetchScalarGridSpec(
             num_scalar_prefetch=1,
             grid=(stop - start,),
-            in_specs=[half_spec, half_spec, anywhere, anywhere],
+            in_specs=[pl.BlockSpec((rows, depth), lambda j, tiles: (0, 0)), anywhere, anywhere],
             out_specs=pl.BlockSpec((1, rows, width), lambda j, tiles: (j, 0, 0)),
             scratch_shapes=[
-                pltpu.VMEM((rows, depth), jnp.bfloat16),
                 pltpu.VMEM((DEEP, depth, width), jnp.bfloat16),
                 pltpu.SemaphoreType.DMA((DEEP,)),
             ],
@@ -237,7 +265,7 @@
             transcendentals=0,
         ),
         name="down",
-    )(tiles, *hidden, local, other)
+    )(tiles, hidden, local, other)
 
 
 def gather_step(block, steps, half, *earlier):
@@ -316,12 +344,14 @@
     size = row_count // 2
     early = min(3, count - 1)
 
-    def matmul(part, block, streams, *earlier):
-        pieces = [block]
-        for step in range(half - 1):
-            pieces += [steps[step][way] for way in range(2) for steps in streams]
-        pieces += [piece for steps in streams for piece in steps[half - 1]]
-        return gate_up(part, blocks, after(pieces, *earlier), gains, weights)
+    def matmul(units, final, partial, squares, block, steps, *earlier):
+        pieces = [[block]]
+        for number, step in enumerate(steps):
+            pieces += [[step[0]], [step[1]]] if number < half - 1 else [list(step)]
+        return gate_up(units, final, partial, squares, blocks, after(pieces, *earlier), gains, weights)
+
+    def units(which, start, stop):
+        return [(which, block) for block in range(start, stop)]
 
     def open_down(hidden, *earlier):
         return down(0, early, tiles, after(hidden, *earlier), down_weight, other_down, width)
@@ -340,17 +370,22 @@
     later = after((gate_weight, up_weight, down_weight), edges, block_a)
     other_gate, other_up, other_down = (swap(weight) for weight in later)
     weights = (gate_weight, other_gate, up_weight, other_up)
+    nothing = (jnp.zeros((size, LANES), jnp.float32), frozenset())
     steps_a = gather_step(block_a, [], half)
     later = after((noisy_input, self_cond, edges), steps_a[0])
     block_b = convolve(*later, 0, size)
     while len(steps_a) < half - 1:
+        if len(steps_a) == half - 2:
+            near = 2 * len(steps_a) + 1
+            gate_a, squares_a = matmul(units(0, 0, near), False, {}, nothing, block_a, steps_a)
         steps_a = gather_step(block_a, steps_a, half)
-    steps_b = gather_step(block_b, [], half, steps_a[min(1, half - 2)])
-    steps_a = gather_step(block_a, steps_a, half)
-    hidden_a = [matmul(0, block_a, [steps_a])]
+    steps_b = gather_step(block_b, [], half, gate_a)
+    up_a, squares_a = matmul(units(1, 0, count - 1), False, {}, squares_a, block_a, steps_a, gate_a)
+    steps_a = gather_step(block_a, steps_a, half, gate_a)
     first_b = steps_b[-1]
-    steps_b = gather_step(block_b, steps_b, half, hidden_a)
-    hidden_a += [matmul(1, block_a, [steps_a], hidden_a, first_b)]
+    steps_b = gather_step(block_b, steps_b, half, up_a, steps_a[-1])
+    rest = units(0, near, count) + units(1, count - 1, count)
+    hidden_a, _ = matmul(rest, True, {0: gate_a, 1: up_a}, squares_a, block_a, steps_a, first_b)
     second_b = steps_b[-1]
     steps_b = gather_step(block_b, steps_b, half, hidden_a)
     opened_a = open_down(hidden_a, second_b)
@@ -363,9 +398,9 @@
     distances = list(range(half - 1, 0, -1))
     moved_a = scatter_send(scatter_sums(None, term_a, count, half, third_b))
     sums_a = scatter_sums(moved_a, term_a, count, distances.pop(0))
-    hidden_b = [matmul(0, block_b, [steps_b], closed_a, sums_a)]
+    gate_b, squares_b = matmul(units(0, 0, count), False, {}, nothing, block_b, steps_b, closed_a, sums_a)
     sums_a = scatter_sums(scatter_send(sums_a), term_a, count, distances.pop(0))
-    hidden_b += [matmul(1, block_b, [steps_b], hidden_b, sums_a)]
+    hidden_b, _ = matmul(units(1, 0, count), True, {0: gate_b}, squares_b, block_b, steps_b, sums_a)
     for distance in distances:
         sums_a = scatter_sums(scatter_send(sums_a), term_a, count, distance)
     opened_b = open_down(hidden_b, sums_a)

time: 221 us -> 216 us (0.977)
  waiting for transfers between devices: 67.6 us -> 52.7 us
  Pallas kernels: 93.9 us -> 105 us
    ppermute x40, waiting for transfers between devices: 67.5 us -> 52.5 us  [ring_shift(): lax.ppermute(value, 'blk', [(ring[i], ring[(i + steps) % count]) for i in...]
    pallas_call x4 -> x5, Pallas kernels: 62.1 us -> 72.5 us  [gate_up(): pl.pallas_call(functools.partial(gate_up_kernel, fixed), out_shape=(jax.S...]
  transfers between devices with their start and end apart: 44 -> 44, of which waited for: 24 -> 20; matrix products, arithmetic and copies ran while one was open for 4% -> 3% of each run, Pallas kernels for 43% -> 49%
where the time goes in v8:
time: 216 us; the launch traced here: 215 us
  Pallas kernels  105 us (49%)
  waiting for transfers between devices  52.7 us (24%)
  starting transfers between devices  46.5 us (22%)
  other arithmetic  8.59 us (4%)
    pallas_call x5, Pallas kernels, gate_up(): pl.pallas_call(functools.partial(gate_up_kernel, fixed), out_shape=(jax.S...  72.5 us
    ppermute x40, waiting for transfers between devices, ring_shift(): lax.ppermute(value, 'blk', [(ring[i], ring[(i + steps) % count]) for i in...  52.5 us
    ppermute x40, starting transfers between devices, ring_shift(): lax.ppermute(value, 'blk', [(ring[i], ring[(i + steps) % count]) for i in...  43.5 us
    pallas_call x4, Pallas kernels, down(): pl.pallas_call(functools.partial(down_kernel, start, stop - start), out_s...  32.1 us
  transfers between devices with their start and end apart: 44, of which 20 were waited for; matrix products, arithmetic and copies ran while one was open for 3% of the time, Pallas kernels for 49%

profile of v8, /device:TPU:0, one launch (start us, length us, event | category | flops | bytes accessed | tf_op | source)
XLA Modules:
  0.0 215.4 jit_solution(9221843318519658108)
XLA Ops:
  0.0 0.8 multiply_add_fusion.2
  0.8 2.4 %collective-permute-start = (f32[3,1024]{1,0:T(4,128)S(1)}, f32[3,1024]{1,0:T(4,128)S(1)}, u32[]{:S(2)}, u32[]{:S(2)}) collective-permute-start(f32[3,1024]{1,0:T(4,128)S(1)} %multiply_add_fusion.2), channel_id=1, source_target_pairs={{0,1},{2,3},{4,5},{6,7},{8,9},{10,11},{12,13},{14,15},{16,17},{18,... | collective-permute-start | bytes 36872 | tf_op jit(solution)/shard_map/ppermute | solution.py:327
  3.1 1.5 multiply_add_fusion
  5.3 0.9 constant_dynamic-slice_fusion.2
  6.3 0.5 multiply_convert_fusion.1.refs_0_
  6.9 0.5 collective-permute-start.10
  7.4 2.4 %collective-permute-start.1 = (bf16[256,1024]{1,0:T(8,128)(2,1)S(1)}, bf16[256,1024]{1,0:T(8,128)(2,1)S(1)}, u32[]{:S(2)}, u32[]{:S(2)}) collective-permute-start(bf16[256,1024]{1,0:T(8,128)(2,1)S(1)} %multiply_convert_fusion.1.refs_0_), channel_id=1, source_target_pairs={{0,4},{4,8},{8,12},{12,14},{14,10},{10,6},{6,2},{2,0},{1,5},{5,9},... | collective-permute-start | bytes 1572872 | tf_op jit(solution)/shard_map/ppermute | solution.py:55
  9.9 0.7 dynamic-slice_bitcast_fusion
  10.6 11.8 %collective-permute-done.1.refs_1_ = bf16[256,1024]{1,0:T(8,128)(2,1)S(1)} collective-permute-done((bf16[256,1024]{1,0:T(8,128)(2,1)S(1)}, bf16[256,1024]{1,0:T(8,128)(2,1)S(1)}, u32[]{:S(2)}, u32[]{:S(2)}) %collective-permute-start.1) | collective-permute-done | bytes 524320 | tf_op jit(solution)/shard_map/ppermute | solution.py:55
  22.3 1.5 collective-permute-done.2.refs_2_
  23.8 1.6 collective-permute-start.3
  25.9 1.2 multiply_add_fusion.1
  27.1 0.5 multiply_convert_fusion.refs_0_
  27.6 9.4 %collective-permute-done.3.refs_3_ = bf16[256,1024]{1,0:T(8,128)(2,1)S(1)} collective-permute-done((bf16[256,1024]{1,0:T(8,128)(2,1)S(1)}, bf16[256,1024]{1,0:T(8,128)(2,1)S(1)}, u32[]{:S(2)}, u32[]{:S(2)}) %collective-permute-start.3) | collective-permute-done | bytes 524320 | tf_op jit(solution)/shard_map/ppermute | solution.py:55
  37.0 1.3 collective-permute-done.4.refs_4_
  38.3 1.6 collective-permute-start.8
  40.4 12.0 %gate_up.5 = (f32[256,2048]{1,0:T(8,128)}, f32[256,128]{1,0:T(8,128)S(1)}) custom-call(s32[3,8]{1,0:T(4,128)S(1)} %get-tuple-element.225.blocks_ref, s32[5,5]{1,0:T(8,128)S(1)} %copy-done.6, bf16[256,1024]{1,0:T(8,128)(2,1)S(1)} %multiply_convert_fusion.1.refs_0_, bf16[256,1024]{1,0:T(8,128)(2,1)S(1)} %collective-permute-done.1.refs_1_, ...), custom_call_target="tpu_custom_call" | custom-call | flops 10737418240 | bytes 20971520 | tf_op jit(solution)/shard_map/gate_up/pallas_call | solution.py:181
  52.5 0.5 collective-permute-start.12
  53.0 1.6 collective-permute-start.11
  54.6 1.6 collective-permute-start.6
  56.3 2.3 %collective-permute-start.7 = (bf16[256,1024]{1,0:T(8,128)(2,1)S(1)}, bf16[256,1024]{1,0:T(8,128)(2,1)S(1)}, u32[]{:S(2)}, u32[]{:S(2)}) collective-permute-start(bf16[256,1024]{1,0:T(8,128)(2,1)S(1)} %multiply_convert_fusion.refs_0_), channel_id=1, source_target_pairs={{0,2},{4,0},{8,4},{12,8},{14,12},{10,14},{6,10},{2,6},{1,3},{5,1},... | collective-permute-start | bytes 1572872 | tf_op jit(solution)/shard_map/ppermute | solution.py:55
  58.7 14.7 %gate_up.6 = (f32[256,2048]{1,0:T(8,128)}, f32[256,128]{1,0:T(8,128)S(1)}) custom-call(s32[3,8]{1,0:T(4,128)S(1)} %get-tuple-element.225.blocks_ref, s32[5,7]{1,0:T(8,128)S(1)} %copy-done.5, bf16[256,1024]{1,0:T(8,128)(2,1)S(1)} %multiply_convert_fusion.1.refs_0_, bf16[256,1024]{1,0:T(8,128)(2,1)S(1)} %collective-permute-done.1.refs_1_, ...), custom_call_target="tpu_custom_call" | custom-call | flops 15032385536 | bytes 29360128 | tf_op jit(solution)/shard_map/gate_up/pallas_call | solution.py:181
  73.6 1.9 collective-permute-start.14
  75.5 11.6 %gate_up.7 = (bf16[256,2048]{1,0:T(8,128)(2,1)S(1)}, f32[256,128]{1,0:T(8,128)}) custom-call(s32[3,8]{1,0:T(4,128)S(1)} %get-tuple-element.225.blocks_ref, s32[5,4]{1,0:T(8,128)S(1)} %copy-done.4, bf16[256,1024]{1,0:T(8,128)(2,1)S(1)} %collective-permute-done.8.refs_5_.refs_0_, bf16[256,1024]{1,0:T(8,128)(2,1)S(1)} %collective-permute-done.9.refs_6_.refs_1_, ...), custom_call_target="tpu_custom_call" | custom-call | flops 8589934592 | bytes 16777216 | tf_op jit(solution)/shard_map/gate_up/pallas_call | solution.py:181
  87.3 1.7 collective-permute-start.15
  89.3 6.7 %down.4 = bf16[3,256,1024]{2,1,0:T(8,128)(2,1)S(1)} custom-call(s32[3,8]{1,0:T(4,128)S(1)} %get-tuple-element.226.tiles_ref, bf16[256,2048]{1,0:T(8,128)(2,1)S(1)} %get-tuple-element.141.hidden, bf16[2048,4096]{1,0:T(8,128)(2,1)} %local_ref.7, bf16[2048,4096]{1,0:T(8,128)(2,1)} %collective-permute-done.17.other_ref), custom_call_target="tpu_custom_call" | custom-call | flops 6442450944 | bytes 12582912 | tf_op jit(solution)/shard_map/down/pallas_call | solution.py:248
  96.1 4.2 %collective-permute-done.15.refs_5_ = bf16[256,1024]{1,0:T(8,128)(2,1)S(1)} collective-permute-done((bf16[256,1024]{1,0:T(8,128)(2,1)S(1)}, bf16[256,1024]{1,0:T(8,128)(2,1)S(1)}, u32[]{:S(2)}, u32[]{:S(2)}) %collective-permute-start.15) | collective-permute-done | bytes 524320 | tf_op jit(solution)/shard_map/ppermute | solution.py:55
  100.3 0.9 collective-permute-done.16.refs_6_
  101.3 0.9 collective-permute-start.19
  102.2 1.2 collective-permute-start.18
  103.3 1.6 collective-permute-start.20
  104.9 0.5 collective-permute-start.21
  105.4 9.4 %down.5 = bf16[5,256,1024]{2,1,0:T(8,128)(2,1)S(1)} custom-call(s32[3,8]{1,0:T(4,128)S(1)} %get-tuple-element.226.tiles_ref, bf16[256,2048]{1,0:T(8,128)(2,1)S(1)} %get-tuple-element.141.hidden, bf16[2048,4096]{1,0:T(8,128)(2,1)} %local_ref.7, bf16[2048,4096]{1,0:T(8,128)(2,1)} %collective-permute-done.17.other_ref), custom_call_target="tpu_custom_call" | custom-call | flops 10737418240 | bytes 20971520 | tf_op jit(solution)/shard_map/down/pallas_call | solution.py:248
  115.0 1.6 collective-permute-start.22
  116.7 0.5 collective-permute-start.23
  117.2 17.0 %gate_up.8 = (f32[256,2048]{1,0:T(8,128)}, f32[256,128]{1,0:T(8,128)S(1)}) custom-call(s32[3,8]{1,0:T(4,128)S(1)} %get-tuple-element.225.blocks_ref, s32[5,8]{1,0:T(8,128)S(1)} %copy-done.3, bf16[256,1024]{1,0:T(8,128)(2,1)S(1)} %multiply_convert_fusion.refs_0_, bf16[256,1024]{1,0:T(8,128)(2,1)S(1)} %collective-permute-done.6.refs_1_, ...), custom_call_target="tpu_custom_call" | custom-call | flops 17179869184 | bytes 33554432 | tf_op jit(solution)/shard_map/gate_up/pallas_call | solution.py:181
  134.7 0.9 collective-permute-start.25
  135.6 1.2 collective-permute-start.24
  136.8 17.1 %gate_up.9 = (bf16[256,2048]{1,0:T(8,128)(2,1)}, f32[256,128]{1,0:T(8,128)}) custom-call(s32[3,8]{1,0:T(4,128)S(1)} %get-tuple-element.225.blocks_ref, s32[5,8]{1,0:T(8,128)S(1)} %copy-done.2, bf16[256,1024]{1,0:T(8,128)(2,1)S(1)} %multiply_convert_fusion.refs_0_, bf16[256,1024]{1,0:T(8,128)(2,1)S(1)} %collective-permute-done.6.refs_1_, ...), custom_call_target="tpu_custom_call" | custom-call | flops 17179869184 | bytes 33554432 | tf_op jit(solution)/shard_map/gate_up/pallas_call | solution.py:181
  154.4 1.6 collective-permute-start.26
  156.5 6.7 %down.6 = bf16[3,256,1024]{2,1,0:T(8,128)(2,1)S(1)} custom-call(s32[3,8]{1,0:T(4,128)S(1)} %get-tuple-element.226.tiles_ref, bf16[256,2048]{1,0:T(8,128)(2,1)S(1)} %copy-done, bf16[2048,4096]{1,0:T(8,128)(2,1)} %local_ref.7, bf16[2048,4096]{1,0:T(8,128)(2,1)} %collective-permute-done.17.other_ref), custom_call_target="tpu_custom_call" | custom-call | flops 6442450944 | bytes 12582912 | tf_op jit(solution)/shard_map/down/pallas_call | solution.py:248
  163.2 2.0 collective-permute-done.26
  165.3 1.9 collective-permute-done.27
  167.2 1.6 collective-permute-start.28
  169.2 1.6 collective-permute-start.30
  171.2 2.3 %collective-permute-done.28 = bf16[64,1024]{1,0:T(8,128)(2,1)S(1)} collective-permute-done((bf16[64,1024]{1,0:T(8,128)(2,1)S(1)}, bf16[64,1024]{1,0:T(8,128)(2,1)S(1)}, u32[]{:S(2)}, u32[]{:S(2)}) %collective-permute-start.28) | collective-permute-done | bytes 131104 | tf_op jit(solution)/shard_map/ppermute | solution.py:55
  173.5 1.5 collective-permute-done.29
  175.2 1.1 collective-permute-done.30
  176.3 1.5 collective-permute-done.31
  178.0 1.8 collective-permute-start.36
  180.1 1.8 collective-permute-start.32
  182.2 9.3 %down.7 = bf16[5,256,1024]{2,1,0:T(8,128)(2,1)S(1)} custom-call(s32[3,8]{1,0:T(4,128)S(1)} %get-tuple-element.226.tiles_ref, bf16[256,2048]{1,0:T(8,128)(2,1)S(1)} %copy-done, bf16[2048,4096]{1,0:T(8,128)(2,1)} %local_ref.7, bf16[2048,4096]{1,0:T(8,128)(2,1)} %collective-permute-done.17.other_ref), custom_call_target="tpu_custom_call" | custom-call | flops 10737418240 | bytes 20971520 | tf_op jit(solution)/shard_map/down/pallas_call | solution.py:248
  191.5 3.2 %collective-permute-done.33 = bf16[128,1024]{1,0:T(8,128)(2,1)S(1)} collective-permute-done((bf16[128,1024]{1,0:T(8,128)(2,1)S(1)}, bf16[128,1024]{1,0:T(8,128)(2,1)S(1)}, u32[]{:S(2)}, u32[]{:S(2)}) %collective-permute-start.33) | collective-permute-done | bytes 262176 | tf_op jit(solution)/shard_map/ppermute | solution.py:55
  195.2 1.8 collective-permute-start.34
  197.5 1.8 collective-permute-start.40
  199.2 4.8 %collective-permute-done.35 = bf16[128,1024]{1,0:T(8,128)(2,1)S(1)} collective-permute-done((bf16[128,1024]{1,0:T(8,128)(2,1)S(1)}, bf16[128,1024]{1,0:T(8,128)(2,1)S(1)}, u32[]{:S(2)}, u32[]{:S(2)}) %collective-permute-start.35) | collective-permute-done | bytes 262176 | tf_op jit(solution)/shard_map/ppermute | solution.py:55
  204.5 1.8 collective-permute-start.38
  206.3 0.5 collective-permute-done.41
  207.0 0.5 collective-permute-start.42
  207.5 1.6 collective-permute-start.43
  209.1 0.5 fusion.15
  209.6 4.1 %collective-permute-done.42 = bf16[128,1024]{1,0:T(8,128)(2,1)S(1)} collective-permute-done((bf16[128,1024]{1,0:T(8,128)(2,1)S(1)}, bf16[128,1024]{1,0:T(8,128)(2,1)S(1)}, u32[]{:S(2)}, u32[]{:S(2)}) %collective-permute-start.42) | collective-permute-done | bytes 262176 | tf_op jit(solution)/shard_map/ppermute | solution.py:55
  213.9 0.5 fusion.33
  214.4 1.0 pad_maximum_fusion.1
  (92 shorter events, 7.2 us)
Async XLA Ops:
  0.0 5.3 %copy-start.1 = (f32[8192]{0:T(1024)S(1)}, f32[8192]{0:T(1024)}, u32[]{:S(2)}) copy-start(f32[8192]{0:T(1024)} %param.20) | copy-start | bytes 98308
  0.8 6.0 %collective-permute-start = (f32[3,1024]{1,0:T(4,128)S(1)}, f32[3,1024]{1,0:T(4,128)S(1)}, u32[]{:S(2)}, u32[]{:S(2)}) collective-permute-start(f32[3,1024]{1,0:T(4,128)S(1)} %multiply_add_fusion.2), channel_id=1, source_target_pairs={{0,1},{2,3},{4,5},{6,7},{8,9},{10,11},{12,13},{14,15},{16,17},{18,... | collective-permute-start | bytes 36872 | tf_op jit(solution)/shard_map/ppermute | solution.py:327
  6.2 19.6 %copy-start.7 = (bf16[512,1024]{1,0:T(8,128)(2,1)S(1)}, bf16[512,1024]{1,0:T(8,128)(2,1)}, u32[]{:S(2)}) copy-start(bf16[512,1024]{1,0:T(8,128)(2,1)} %param.16) | copy-start | bytes 3145732
  6.2 19.6 %copy-start.11 = (f32[1024]{0:T(1024)S(1)}, f32[1024]{0:T(1024)}, u32[]{:S(2)}) copy-start(f32[1024]{0:T(1024)} %param.17) | copy-start | bytes 12292
  6.8 33.6 %copy-start.6 = (s32[5,5]{1,0:T(8,128)S(1)}, s32[5,5]{1,0:T(8,128)}, u32[]{:S(2)}) copy-start(s32[5,5]{1,0:T(8,128)} %constant.38.clone.units_ref) | copy-start | bytes 304
  6.8 33.5 %collective-permute-start.5 = (bf16[4096,2048]{1,0:T(8,128)(2,1)}, bf16[4096,2048]{1,0:T(8,128)(2,1)}, u32[]{:S(2)}, u32[]{:S(2)}) collective-permute-start(bf16[4096,2048]{1,0:T(8,128)(2,1)} %refs_12_.1), channel_id=1, source_target_pairs={{0,1},{1,0},{2,3},{3,2},{4,5},{5,4},{6,7},{7,6},{8,9},{9,8},{10,11... | collective-permute-start | bytes 50331656 | tf_op jit(solution)/shard_map/ppermute | solution.py:59
  6.9 49.5 %collective-permute-start.10 = (bf16[4096,2048]{1,0:T(8,128)(2,1)}, bf16[4096,2048]{1,0:T(8,128)(2,1)}, u32[]{:S(2)}, u32[]{:S(2)}) collective-permute-start(bf16[4096,2048]{1,0:T(8,128)(2,1)} %refs_13_.1), channel_id=1, source_target_pairs={{0,1},{1,0},{2,3},{3,2},{4,5},{5,4},{6,7},{7,6},{8,9},{9,8},{10,11... | collective-permute-start | bytes 50331656 | tf_op jit(solution)/shard_map/ppermute | solution.py:59
  7.4 81.9 %collective-permute-start.17 = (bf16[2048,4096]{1,0:T(8,128)(2,1)}, bf16[2048,4096]{1,0:T(8,128)(2,1)}, u32[]{:S(2)}, u32[]{:S(2)}) collective-permute-start(bf16[2048,4096]{1,0:T(8,128)(2,1)} %local_ref.7), channel_id=1, source_target_pairs={{0,1},{1,0},{2,3},{3,2},{4,5},{5,4},{6,7},{7,6},{8,9},{9,8},{10,11... | collective-permute-start | bytes 50331656 | tf_op jit(solution)/shard_map/ppermute | solution.py:59
  7.4 14.9 %collective-permute-start.1 = (bf16[256,1024]{1,0:T(8,128)(2,1)S(1)}, bf16[256,1024]{1,0:T(8,128)(2,1)S(1)}, u32[]{:S(2)}, u32[]{:S(2)}) collective-permute-start(bf16[256,1024]{1,0:T(8,128)(2,1)S(1)} %multiply_convert_fusion.1.refs_0_), channel_id=1, source_target_pairs={{0,4},{4,8},{8,12},{12,14},{14,10},{10,6},{6,2},{2,0},{1,5},{5,9},... | collective-permute-start | bytes 1572872 | tf_op jit(solution)/shard_map/ppermute | solution.py:55
  9.9 14.0 %collective-permute-start.2 = (bf16[256,1024]{1,0:T(8,128)(2,1)S(1)}, bf16[256,1024]{1,0:T(8,128)(2,1)S(1)}, u32[]{:S(2)}, u32[]{:S(2)}) collective-permute-start(bf16[256,1024]{1,0:T(8,128)(2,1)S(1)} %multiply_convert_fusion.1.refs_0_), channel_id=1, source_target_pairs={{0,2},{4,0},{8,4},{12,8},{14,12},{10,14},{6,10},{2,6},{1,3},{5,1},... | collective-permute-start | bytes 1572872 | tf_op jit(solution)/shard_map/ppermute | solution.py:55
  23.8 13.2 %collective-permute-start.3 = (bf16[256,1024]{1,0:T(8,128)(2,1)S(1)}, bf16[256,1024]{1,0:T(8,128)(2,1)S(1)}, u32[]{:S(2)}, u32[]{:S(2)}) collective-permute-start(bf16[256,1024]{1,0:T(8,128)(2,1)S(1)} %collective-permute-done.1.refs_1_), channel_id=1, source_target_pairs={{0,4},{4,8},{8,12},{12,14},{14,10},{10,6},{6,2},{2,0},{1,5},{5,9},... | collective-permute-start | bytes 1572872 | tf_op jit(solution)/shard_map/ppermute | solution.py:55
  25.4 12.9 %collective-permute-start.4 = (bf16[256,1024]{1,0:T(8,128)(2,1)S(1)}, bf16[256,1024]{1,0:T(8,128)(2,1)S(1)}, u32[]{:S(2)}, u32[]{:S(2)}) collective-permute-start(bf16[256,1024]{1,0:T(8,128)(2,1)S(1)} %collective-permute-done.2.refs_2_), channel_id=1, source_target_pairs={{0,2},{4,0},{8,4},{12,8},{14,12},{10,14},{6,10},{2,6},{1,3},{5,1},... | collective-permute-start | bytes 1572872 | tf_op jit(solution)/shard_map/ppermute | solution.py:55
  38.3 14.1 %collective-permute-start.8 = (bf16[256,1024]{1,0:T(8,128)(2,1)S(1)}, bf16[256,1024]{1,0:T(8,128)(2,1)S(1)}, u32[]{:S(2)}, u32[]{:S(2)}) collective-permute-start(bf16[256,1024]{1,0:T(8,128)(2,1)S(1)} %collective-permute-done.3.refs_3_), channel_id=1, source_target_pairs={{0,4},{4,8},{8,12},{12,14},{14,10},{10,6},{6,2},{2,0},{1,5},{5,9},... | collective-permute-start | bytes 1572872 | tf_op jit(solution)/shard_map/ppermute | solution.py:55
  39.9 12.5 %collective-permute-start.9 = (bf16[256,1024]{1,0:T(8,128)(2,1)S(1)}, bf16[256,1024]{1,0:T(8,128)(2,1)S(1)}, u32[]{:S(2)}, u32[]{:S(2)}) collective-permute-start(bf16[256,1024]{1,0:T(8,128)(2,1)S(1)} %collective-permute-done.4.refs_4_), channel_id=1, source_target_pairs={{0,2},{4,0},{8,4},{12,8},{14,12},{10,14},{6,10},{2,6},{1,3},{5,1},... | collective-permute-start | bytes 1572872 | tf_op jit(solution)/shard_map/ppermute | solution.py:55
  40.4 18.3 %copy-start.5 = (s32[5,7]{1,0:T(8,128)S(1)}, s32[5,7]{1,0:T(8,128)}, u32[]{:S(2)}) copy-start(s32[5,7]{1,0:T(8,128)} %constant.39.clone.units_ref) | copy-start | bytes 424
  52.5 20.9 %collective-permute-start.12 = (bf16[128,1024]{1,0:T(8,128)(2,1)S(1)}, bf16[128,1024]{1,0:T(8,128)(2,1)S(1)}, u32[]{:S(2)}, u32[]{:S(2)}) collective-permute-start(bf16[128,1024]{1,0:T(8,128)(2,1)S(1)} %slice.332), channel_id=1, source_target_pairs={{0,2},{4,0},{8,4},{12,8},{14,12},{10,14},{6,10},{2,6},{1,3},{5,1},... | collective-permute-start | bytes 786440 | tf_op jit(solution)/shard_map/ppermute | solution.py:55
  53.0 20.4 %collective-permute-start.11 = (bf16[128,1024]{1,0:T(8,128)(2,1)S(1)}, bf16[128,1024]{1,0:T(8,128)(2,1)S(1)}, u32[]{:S(2)}, u32[]{:S(2)}) collective-permute-start(bf16[128,1024]{1,0:T(8,128)(2,1)S(1)} %slice.331), channel_id=1, source_target_pairs={{0,4},{4,8},{8,12},{12,14},{14,10},{10,6},{6,2},{2,0},{1,5},{5,9},... | collective-permute-start | bytes 786440 | tf_op jit(solution)/shard_map/ppermute | solution.py:55
  54.6 18.9 %collective-permute-start.6 = (bf16[256,1024]{1,0:T(8,128)(2,1)S(1)}, bf16[256,1024]{1,0:T(8,128)(2,1)S(1)}, u32[]{:S(2)}, u32[]{:S(2)}) collective-permute-start(bf16[256,1024]{1,0:T(8,128)(2,1)S(1)} %multiply_convert_fusion.refs_0_), channel_id=1, source_target_pairs={{0,4},{4,8},{8,12},{12,14},{14,10},{10,6},{6,2},{2,0},{1,5},{5,9},... | collective-permute-start | bytes 1572872 | tf_op jit(solution)/shard_map/ppermute | solution.py:55
  56.3 17.1 %collective-permute-start.7 = (bf16[256,1024]{1,0:T(8,128)(2,1)S(1)}, bf16[256,1024]{1,0:T(8,128)(2,1)S(1)}, u32[]{:S(2)}, u32[]{:S(2)}) collective-permute-start(bf16[256,1024]{1,0:T(8,128)(2,1)S(1)} %multiply_convert_fusion.refs_0_), channel_id=1, source_target_pairs={{0,2},{4,0},{8,4},{12,8},{14,12},{10,14},{6,10},{2,6},{1,3},{5,1},... | collective-permute-start | bytes 1572872 | tf_op jit(solution)/shard_map/ppermute | solution.py:55
  58.7 16.8 %copy-start.4 = (s32[5,4]{1,0:T(8,128)S(1)}, s32[5,4]{1,0:T(8,128)}, u32[]{:S(2)}) copy-start(s32[5,4]{1,0:T(8,128)} %constant.40.clone.units_ref) | copy-start | bytes 244
  73.5 13.7 %collective-permute-start.13 = (bf16[256,1024]{1,0:T(8,128)(2,1)S(1)}, bf16[256,1024]{1,0:T(8,128)(2,1)S(1)}, u32[]{:S(2)}, u32[]{:S(2)}) collective-permute-start(bf16[256,1024]{1,0:T(8,128)(2,1)S(1)} %collective-permute-done.6.refs_1_), channel_id=1, source_target_pairs={{0,4},{4,8},{8,12},{12,14},{14,10},{10,6},{6,2},{2,0},{1,5},{5,9},... | collective-permute-start | bytes 1572872 | tf_op jit(solution)/shard_map/ppermute | solution.py:55
  73.6 13.7 %collective-permute-start.14 = (bf16[256,1024]{1,0:T(8,128)(2,1)S(1)}, bf16[256,1024]{1,0:T(8,128)(2,1)S(1)}, u32[]{:S(2)}, u32[]{:S(2)}) collective-permute-start(bf16[256,1024]{1,0:T(8,128)(2,1)S(1)} %collective-permute-done.7.refs_2_), channel_id=1, source_target_pairs={{0,2},{4,0},{8,4},{12,8},{14,12},{10,14},{6,10},{2,6},{1,3},{5,1},... | collective-permute-start | bytes 1572872 | tf_op jit(solution)/shard_map/ppermute | solution.py:55
  87.3 13.0 %collective-permute-start.15 = (bf16[256,1024]{1,0:T(8,128)(2,1)S(1)}, bf16[256,1024]{1,0:T(8,128)(2,1)S(1)}, u32[]{:S(2)}, u32[]{:S(2)}) collective-permute-start(bf16[256,1024]{1,0:T(8,128)(2,1)S(1)} %collective-permute-done.13.refs_3_), channel_id=1, source_target_pairs={{0,4},{4,8},{8,12},{12,14},{14,10},{10,6},{6,2},{2,0},{1,5},{5,9},... | collective-permute-start | bytes 1572872 | tf_op jit(solution)/shard_map/ppermute | solution.py:55
  89.0 12.2 %collective-permute-start.16 = (bf16[256,1024]{1,0:T(8,128)(2,1)S(1)}, bf16[256,1024]{1,0:T(8,128)(2,1)S(1)}, u32[]{:S(2)}, u32[]{:S(2)}) collective-permute-start(bf16[256,1024]{1,0:T(8,128)(2,1)S(1)} %collective-permute-done.14.refs_4_), channel_id=1, source_target_pairs={{0,2},{4,0},{8,4},{12,8},{14,12},{10,14},{6,10},{2,6},{1,3},{5,1},... | collective-permute-start | bytes 1572872 | tf_op jit(solution)/shard_map/ppermute | solution.py:55
  101.2 13.5 %copy-start.10 = (bf16[256,1024]{1,0:T(8,128)(2,1)}, bf16[256,1024]{1,0:T(8,128)(2,1)S(1)}, u32[]{:S(2)}) copy-start(bf16[256,1024]{1,0:T(8,128)(2,1)S(1)} %collective-permute-done.16.refs_6_) | copy-start | bytes 1572868
  101.3 15.9 %collective-permute-start.19 = (bf16[128,1024]{1,0:T(8,128)(2,1)S(1)}, bf16[128,1024]{1,0:T(8,128)(2,1)S(1)}, u32[]{:S(2)}, u32[]{:S(2)}) collective-permute-start(bf16[128,1024]{1,0:T(8,128)(2,1)S(1)} %slice.334), channel_id=1, source_target_pairs={{0,2},{4,0},{8,4},{12,8},{14,12},{10,14},{6,10},{2,6},{1,3},{5,1},... | collective-permute-start | bytes 786440 | tf_op jit(solution)/shard_map/ppermute | solution.py:55
  102.2 15.1 %collective-permute-start.18 = (bf16[128,1024]{1,0:T(8,128)(2,1)S(1)}, bf16[128,1024]{1,0:T(8,128)(2,1)S(1)}, u32[]{:S(2)}, u32[]{:S(2)}) collective-permute-start(bf16[128,1024]{1,0:T(8,128)(2,1)S(1)} %slice.333), channel_id=1, source_target_pairs={{0,4},{4,8},{8,12},{12,14},{14,10},{10,6},{6,2},{2,0},{1,5},{5,9},... | collective-permute-start | bytes 786440 | tf_op jit(solution)/shard_map/ppermute | solution.py:55
  103.3 11.4 %collective-permute-start.20 = (bf16[128,1024]{1,0:T(8,128)(2,1)S(1)}, bf16[128,1024]{1,0:T(8,128)(2,1)S(1)}, u32[]{:S(2)}, u32[]{:S(2)}) collective-permute-start(bf16[128,1024]{1,0:T(8,128)(2,1)S(1)} %get-tuple-element.142), channel_id=1, source_target_pairs={{0,4},{4,8},{8,12},{12,14},{14,10},{10,6},{6,2},{2,0},{1,5},{5,9},... | collective-permute-start | bytes 786440 | tf_op jit(solution)/shard_map/ppermute | solution.py:55
  104.9 9.9 %collective-permute-start.21 = (bf16[128,1024]{1,0:T(8,128)(2,1)S(1)}, bf16[128,1024]{1,0:T(8,128)(2,1)S(1)}, u32[]{:S(2)}, u32[]{:S(2)}) collective-permute-start(bf16[128,1024]{1,0:T(8,128)(2,1)S(1)} %get-tuple-element.143), channel_id=1, source_target_pairs={{0,2},{4,0},{8,4},{12,8},{14,12},{10,14},{6,10},{2,6},{1,3},{5,1},... | collective-permute-start | bytes 786440 | tf_op jit(solution)/shard_map/ppermute | solution.py:55
  114.8 2.5 %copy-start.3 = (s32[5,8]{1,0:T(8,128)S(1)}, s32[5,8]{1,0:T(8,128)}, u32[]{:S(2)}) copy-start(s32[5,8]{1,0:T(8,128)} %constant.41.clone.units_ref) | copy-start | bytes 484
  115.0 19.2 %collective-permute-start.22 = (bf16[256,1024]{1,0:T(8,128)(2,1)S(1)}, bf16[256,1024]{1,0:T(8,128)(2,1)S(1)}, u32[]{:S(2)}, u32[]{:S(2)}) collective-permute-start(bf16[256,1024]{1,0:T(8,128)(2,1)S(1)} %pad_maximum_fusion.2), channel_id=1, source_target_pairs={{0,4},{4,8},{8,12},{12,14},{14,10},{10,6},{6,2},{2,0},{1,5},{5,9},... | collective-permute-start | bytes 1572872 | tf_op jit(solution)/shard_map/ppermute | solution.py:55
  116.7 17.6 %collective-permute-start.23 = (bf16[256,1024]{1,0:T(8,128)(2,1)S(1)}, bf16[256,1024]{1,0:T(8,128)(2,1)S(1)}, u32[]{:S(2)}, u32[]{:S(2)}) collective-permute-start(bf16[256,1024]{1,0:T(8,128)(2,1)S(1)} %pad_maximum_fusion.3), channel_id=1, source_target_pairs={{0,2},{4,0},{8,4},{12,8},{14,12},{10,14},{6,10},{2,6},{1,3},{5,1},... | collective-permute-start | bytes 1572872 | tf_op jit(solution)/shard_map/ppermute | solution.py:55
  134.3 2.5 %copy-start.2 = (s32[5,8]{1,0:T(8,128)S(1)}, s32[5,8]{1,0:T(8,128)}, u32[]{:S(2)}) copy-start(s32[5,8]{1,0:T(8,128)} %constant.42.clone.units_ref) | copy-start | bytes 484
  134.7 19.2 %collective-permute-start.25 = (bf16[256,1024]{1,0:T(8,128)(2,1)S(1)}, bf16[256,1024]{1,0:T(8,128)(2,1)S(1)}, u32[]{:S(2)}, u32[]{:S(2)}) collective-permute-start(bf16[256,1024]{1,0:T(8,128)(2,1)S(1)} %get-tuple-element.201), channel_id=1, source_target_pairs={{0,2},{4,0},{8,4},{12,8},{14,12},{10,14},{6,10},{2,6},{1,3},{5,1},... | collective-permute-start | bytes 1572872 | tf_op jit(solution)/shard_map/ppermute | solution.py:55
  135.6 18.4 %collective-permute-start.24 = (bf16[256,1024]{1,0:T(8,128)(2,1)S(1)}, bf16[256,1024]{1,0:T(8,128)(2,1)S(1)}, u32[]{:S(2)}, u32[]{:S(2)}) collective-permute-start(bf16[256,1024]{1,0:T(8,128)(2,1)S(1)} %get-tuple-element.202), channel_id=1, source_target_pairs={{0,4},{4,8},{8,12},{12,14},{14,10},{10,6},{6,2},{2,0},{1,5},{5,9},... | collective-permute-start | bytes 1572872 | tf_op jit(solution)/shard_map/ppermute | solution.py:55
  153.9 2.5 %copy-start = (bf16[256,2048]{1,0:T(8,128)(2,1)S(1)}, bf16[256,2048]{1,0:T(8,128)(2,1)}, u32[]{:S(2)}) copy-start(bf16[256,2048]{1,0:T(8,128)(2,1)} %get-tuple-element.180.hidden) | copy-start | bytes 3145732
  154.4 10.9 %collective-permute-start.26 = (bf16[256,1024]{1,0:T(8,128)(2,1)S(1)}, bf16[256,1024]{1,0:T(8,128)(2,1)S(1)}, u32[]{:S(2)}, u32[]{:S(2)}) collective-permute-start(bf16[256,1024]{1,0:T(8,128)(2,1)S(1)} %get-tuple-element.199), channel_id=1, source_target_pairs={{0,4},{4,8},{8,12},{12,14},{14,10},{10,6},{6,2},{2,0},{1,5},{5,9},... | collective-permute-start | bytes 1572872 | tf_op jit(solution)/shard_map/ppermute | solution.py:55
  156.0 11.2 %collective-permute-start.27 = (bf16[256,1024]{1,0:T(8,128)(2,1)S(1)}, bf16[256,1024]{1,0:T(8,128)(2,1)S(1)}, u32[]{:S(2)}, u32[]{:S(2)}) collective-permute-start(bf16[256,1024]{1,0:T(8,128)(2,1)S(1)} %get-tuple-element.200), channel_id=1, source_target_pairs={{0,2},{4,0},{8,4},{12,8},{14,12},{10,14},{6,10},{2,6},{1,3},{5,1},... | collective-permute-start | bytes 1572872 | tf_op jit(solution)/shard_map/ppermute | solution.py:55
  167.2 6.4 %collective-permute-start.28 = (bf16[64,1024]{1,0:T(8,128)(2,1)S(1)}, bf16[64,1024]{1,0:T(8,128)(2,1)S(1)}, u32[]{:S(2)}, u32[]{:S(2)}) collective-permute-start(bf16[64,1024]{1,0:T(8,128)(2,1)S(1)} %get-tuple-element.172), channel_id=1, source_target_pairs={{0,4},{4,8},{8,12},{12,14},{14,10},{10,6},{6,2},{2,0},{1,5},{5,9},... | collective-permute-start | bytes 393224 | tf_op jit(solution)/shard_map/ppermute | solution.py:55
  168.8 6.3 %collective-permute-start.29 = (bf16[64,1024]{1,0:T(8,128)(2,1)S(1)}, bf16[64,1024]{1,0:T(8,128)(2,1)S(1)}, u32[]{:S(2)}, u32[]{:S(2)}) collective-permute-start(bf16[64,1024]{1,0:T(8,128)(2,1)S(1)} %get-tuple-element.173), channel_id=1, source_target_pairs={{0,2},{4,0},{8,4},{12,8},{14,12},{10,14},{6,10},{2,6},{1,3},{5,1},... | collective-permute-start | bytes 393224 | tf_op jit(solution)/shard_map/ppermute | solution.py:55
  169.2 7.2 %collective-permute-start.30 = (bf16[64,1024]{1,0:T(8,128)(2,1)S(1)}, bf16[64,1024]{1,0:T(8,128)(2,1)S(1)}, u32[]{:S(2)}, u32[]{:S(2)}) collective-permute-start(bf16[64,1024]{1,0:T(8,128)(2,1)S(1)} %get-tuple-element.174), channel_id=1, source_target_pairs={{0,4},{4,8},{8,12},{12,14},{14,10},{10,6},{6,2},{2,0},{1,5},{5,9},... | collective-permute-start | bytes 393224 | tf_op jit(solution)/shard_map/ppermute | solution.py:55
  170.8 7.1 %collective-permute-start.31 = (bf16[64,1024]{1,0:T(8,128)(2,1)S(1)}, bf16[64,1024]{1,0:T(8,128)(2,1)S(1)}, u32[]{:S(2)}, u32[]{:S(2)}) collective-permute-start(bf16[64,1024]{1,0:T(8,128)(2,1)S(1)} %get-tuple-element.175), channel_id=1, source_target_pairs={{0,2},{4,0},{8,4},{12,8},{14,12},{10,14},{6,10},{2,6},{1,3},{5,1},... | collective-permute-start | bytes 393224 | tf_op jit(solution)/shard_map/ppermute | solution.py:55
  178.0 19.0 %collective-permute-start.36 = (bf16[128,1024]{1,0:T(8,128)(2,1)S(1)}, bf16[128,1024]{1,0:T(8,128)(2,1)S(1)}, u32[]{:S(2)}, u32[]{:S(2)}) collective-permute-start(bf16[128,1024]{1,0:T(8,128)(2,1)S(1)} %pad_maximum_fusion.6), channel_id=1, source_target_pairs={{0,4},{4,8},{8,12},{12,14},{14,10},{10,6},{6,2},{2,0},{1,5},{5,9},... | collective-permute-start | bytes 786440 | tf_op jit(solution)/shard_map/ppermute | solution.py:55
  179.8 17.1 %collective-permute-start.37 = (bf16[128,1024]{1,0:T(8,128)(2,1)S(1)}, bf16[128,1024]{1,0:T(8,128)(2,1)S(1)}, u32[]{:S(2)}, u32[]{:S(2)}) collective-permute-start(bf16[128,1024]{1,0:T(8,128)(2,1)S(1)} %pad_maximum_fusion.7), channel_id=1, source_target_pairs={{0,2},{4,0},{8,4},{12,8},{14,12},{10,14},{6,10},{2,6},{1,3},{5,1},... | collective-permute-start | bytes 786440 | tf_op jit(solution)/shard_map/ppermute | solution.py:55
  180.1 11.4 %collective-permute-start.32 = (bf16[128,1024]{1,0:T(8,128)(2,1)S(1)}, bf16[128,1024]{1,0:T(8,128)(2,1)S(1)}, u32[]{:S(2)}, u32[]{:S(2)}) collective-permute-start(bf16[128,1024]{1,0:T(8,128)(2,1)S(1)} %pad_maximum_fusion.4), channel_id=1, source_target_pairs={{0,4},{4,8},{8,12},{12,14},{14,10},{10,6},{6,2},{2,0},{1,5},{5,9},... | collective-permute-start | bytes 786440 | tf_op jit(solution)/shard_map/ppermute | solution.py:55
  181.9 12.8 %collective-permute-start.33 = (bf16[128,1024]{1,0:T(8,128)(2,1)S(1)}, bf16[128,1024]{1,0:T(8,128)(2,1)S(1)}, u32[]{:S(2)}, u32[]{:S(2)}) collective-permute-start(bf16[128,1024]{1,0:T(8,128)(2,1)S(1)} %pad_maximum_fusion.5), channel_id=1, source_target_pairs={{0,2},{4,0},{8,4},{12,8},{14,12},{10,14},{6,10},{2,6},{1,3},{5,1},... | collective-permute-start | bytes 786440 | tf_op jit(solution)/shard_map/ppermute | solution.py:55
  194.9 9.1 %collective-permute-start.35 = (bf16[128,1024]{1,0:T(8,128)(2,1)S(1)}, bf16[128,1024]{1,0:T(8,128)(2,1)S(1)}, u32[]{:S(2)}, u32[]{:S(2)}) collective-permute-start(bf16[128,1024]{1,0:T(8,128)(2,1)S(1)} %get-tuple-element.197), channel_id=1, source_target_pairs={{0,2},{4,0},{8,4},{12,8},{14,12},{10,14},{6,10},{2,6},{1,3},{5,1},... | collective-permute-start | bytes 786440 | tf_op jit(solution)/shard_map/ppermute | solution.py:55
  195.2 13.9 %copy-start.8 = (bf16[512,1024]{1,0:T(8,128)(2,1)S(1)}, bf16[512,1024]{1,0:T(8,128)(2,1)}, u32[]{:S(2)}) copy-start(bf16[512,1024]{1,0:T(8,128)(2,1)} %param.16) | copy-start | bytes 3145732
  195.2 13.9 %copy-start.9 = (bf16[512,1024]{1,0:T(8,128)(2,1)S(1)}, bf16[512,1024]{1,0:T(8,128)(2,1)}, u32[]{:S(2)}) copy-start(bf16[512,1024]{1,0:T(8,128)(2,1)} %param.15) | copy-start | bytes 3145732
  195.2 13.9 %copy-start.12 = (f32[1024]{0:T(1024)S(1)}, f32[1024]{0:T(1024)}, u32[]{:S(2)}) copy-start(f32[1024]{0:T(1024)} %param.17) | copy-start | bytes 12292
  195.2 8.8 %collective-permute-start.34 = (bf16[128,1024]{1,0:T(8,128)(2,1)S(1)}, bf16[128,1024]{1,0:T(8,128)(2,1)S(1)}, u32[]{:S(2)}, u32[]{:S(2)}) collective-permute-start(bf16[128,1024]{1,0:T(8,128)(2,1)S(1)} %get-tuple-element.198), channel_id=1, source_target_pairs={{0,4},{4,8},{8,12},{12,14},{14,10},{10,6},{6,2},{2,0},{1,5},{5,9},... | collective-permute-start | bytes 786440 | tf_op jit(solution)/shard_map/ppermute | solution.py:55
  197.1 9.7 %collective-permute-start.41 = (bf16[128,1024]{1,0:T(8,128)(2,1)S(1)}, bf16[128,1024]{1,0:T(8,128)(2,1)S(1)}, u32[]{:S(2)}, u32[]{:S(2)}) collective-permute-start(bf16[128,1024]{1,0:T(8,128)(2,1)S(1)} %get-tuple-element.195), channel_id=1, source_target_pairs={{0,2},{4,0},{8,4},{12,8},{14,12},{10,14},{6,10},{2,6},{1,3},{5,1},... | collective-permute-start | bytes 786440 | tf_op jit(solution)/shard_map/ppermute | solution.py:55
  197.5 9.3 %collective-permute-start.40 = (bf16[128,1024]{1,0:T(8,128)(2,1)S(1)}, bf16[128,1024]{1,0:T(8,128)(2,1)S(1)}, u32[]{:S(2)}, u32[]{:S(2)}) collective-permute-start(bf16[128,1024]{1,0:T(8,128)(2,1)S(1)} %get-tuple-element.196), channel_id=1, source_target_pairs={{0,4},{4,8},{8,12},{12,14},{14,10},{10,6},{6,2},{2,0},{1,5},{5,9},... | collective-permute-start | bytes 786440 | tf_op jit(solution)/shard_map/ppermute | solution.py:55
  204.2 9.7 %collective-permute-start.39 = (bf16[128,1024]{1,0:T(8,128)(2,1)S(1)}, bf16[128,1024]{1,0:T(8,128)(2,1)S(1)}, u32[]{:S(2)}, u32[]{:S(2)}) collective-permute-start(bf16[128,1024]{1,0:T(8,128)(2,1)S(1)} %get-tuple-element.193), channel_id=1, source_target_pairs={{0,2},{4,0},{8,4},{12,8},{14,12},{10,14},{6,10},{2,6},{1,3},{5,1},... | collective-permute-start | bytes 786440 | tf_op jit(solution)/shard_map/ppermute | solution.py:55
  204.5 9.4 %collective-permute-start.38 = (bf16[128,1024]{1,0:T(8,128)(2,1)S(1)}, bf16[128,1024]{1,0:T(8,128)(2,1)S(1)}, u32[]{:S(2)}, u32[]{:S(2)}) collective-permute-start(bf16[128,1024]{1,0:T(8,128)(2,1)S(1)} %get-tuple-element.194), channel_id=1, source_target_pairs={{0,4},{4,8},{8,12},{12,14},{14,10},{10,6},{6,2},{2,0},{1,5},{5,9},... | collective-permute-start | bytes 786440 | tf_op jit(solution)/shard_map/ppermute | solution.py:55
  207.0 6.7 %collective-permute-start.42 = (bf16[128,1024]{1,0:T(8,128)(2,1)S(1)}, bf16[128,1024]{1,0:T(8,128)(2,1)S(1)}, u32[]{:S(2)}, u32[]{:S(2)}) collective-permute-start(bf16[128,1024]{1,0:T(8,128)(2,1)S(1)} %get-tuple-element.191), channel_id=1, source_target_pairs={{0,4},{4,8},{8,12},{12,14},{14,10},{10,6},{6,2},{2,0},{1,5},{5,9},... | collective-permute-start | bytes 786440 | tf_op jit(solution)/shard_map/ppermute | solution.py:55
  207.5 6.4 %collective-permute-start.43 = (bf16[128,1024]{1,0:T(8,128)(2,1)S(1)}, bf16[128,1024]{1,0:T(8,128)(2,1)S(1)}, u32[]{:S(2)}, u32[]{:S(2)}) collective-permute-start(bf16[128,1024]{1,0:T(8,128)(2,1)S(1)} %get-tuple-element.192), channel_id=1, source_target_pairs={{0,2},{4,0},{8,4},{12,8},{14,12},{10,14},{6,10},{2,6},{1,3},{5,1},... | collective-permute-start | bytes 786440 | tf_op jit(solution)/shard_map/ppermute | solution.py:55

commit v9 on v8

--- a/solution.py
+++ b/solution.py
@@ -63,151 +63,160 @@
     return lax.optimization_barrier((value, earlier))[0]
 
 
-def gate_up_kernel(fixed, blocks_ref, units_ref, *refs):
-    needed, final, taken, mean_of, length = fixed
+def gate_up_kernel(fixed, blocks_ref, *refs):
+    ranges, counted, needed, final, taken, mean_of, chunks = fixed
     refs = list(refs)
+    start = min(low for low, _ in ranges.values())
     pieces = [[refs.pop(0) for _ in range(parts)] for parts in needed]
-    partial_refs = [refs.pop(0) for _ in taken]
-    gains_ref = refs.pop(0)
+    partial_refs = {which: refs.pop(0) for which in taken}
+    gains_ref, before_ref = refs.pop(0), refs.pop(0)
     own_and_other = (refs[0], refs[2]), (refs[1], refs[3])
-    before_ref = refs[4]
-    out_ref, stat_ref, stacked, sums, partial, weights, sems, partial_sems, weight_sems = refs[5:]
-    rows = stacked.shape[0]
+    out_ref, stat_ref, stacked, inv, weights, sems, weight_sems = refs[4:]
     width = gains_ref.shape[2]
-    step = pl.program_id(0)
-    height = width // PARTS if width % (16 * PARTS) == 0 else width
+    tile = weights.shape[-1]
+    step, steps = pl.program_id(0), pl.num_programs(0)
+
+    def slot_of(number):
+        return lax.rem(step * len(chunks) + number, DEEP)
 
     def fetch(number):
-        slot = lax.rem(number, DEEP)
-        block = units_ref[1, number]
-        begin = pl.multiple_of(blocks_ref[1, block] * width, width)
-        for which in range(2):
+        which, low, high = chunks[number % len(chunks)]
+        column = pl.multiple_of((step + number // len(chunks)) * tile, tile)
+        for block in range(low, high):
+            begin = pl.multiple_of(blocks_ref[1, block] * width, width)
             for other in range(2):
 
-                @pl.when((units_ref[0, number] == which) & (blocks_ref[0, block] == 1 - other))
-                def chosen(source=own_and_other[other][which]):
-                    for part in range(width // height):
-                        pltpu.make_async_copy(
-                            source.at[pl.ds(begin + part * height, height)],
-                            weights.at[slot, pl.ds(part * height, height)],
-                            weight_sems.at[slot],
-                        ).start()
-
-    def gather_pieces(place, act):
-        row = 0
-        for number, source in enumerate(pieces[place]):
-            size = source.shape[0]
-            target = stacked.at[pl.ds(row, size), pl.ds(place * width, width)]
-            act(pltpu.make_async_copy(source, target, sems.at[place, number]))
-            row += size
-
-    def partials(act):
-        for number, which in enumerate(taken):
-            act(pltpu.make_async_copy(partial_refs[number], partial.at[which], partial_sems.at[number]))
+                @pl.when(blocks_ref[0, block] == 1 - other)
+                def chosen(block=block, begin=begin, source=own_and_other[other][which]):
+                    pltpu.make_async_copy(
+                        source.at[pl.ds(begin, width), pl.ds(column, tile)],
+                        weights.at[slot_of(number), pl.ds((block - low) * width, width)],
+                        weight_sems.at[slot_of(number)],
+                    ).start()
+
+    def fetch_if_any(number):
+        pl.when(step + number // len(chunks) < steps)(functools.partial(fetch, number))
+
+    def arrive(number):
+        which, low, high = chunks[number]
+        size = (high - low) * width
+        sample = own_and_other[0][which].at[pl.ds(0, size), pl.ds(0, tile)]
+        pltpu.make_async_copy(
+            sample, weights.at[slot_of(number), pl.ds(0, size)], weight_sems.at[slot_of(number)]
+        ).wait()
+
+    def gather_pieces(act):
+        for place, parts in enumerate(pieces):
+            row = 0
+            for number, source in enumerate(parts):
+                size = source.shape[0]
+                target = stacked.at[pl.ds(row, size), pl.ds(place * width, width)]
+                act(pltpu.make_async_copy(source, target, sems.at[place, number]))
+                row += size
 
     @pl.when(step == 0)
     def first():
-        gather_pieces(0, lambda copy: copy.start())
-        for number in range(min(DEEP - 1, length)):
-            fetch(jnp.int32(number))
-        for place in range(1, len(pieces)):
-            gather_pieces(place, lambda copy: copy.start())
-        partials(lambda copy: copy.start())
-        sums[...] = jnp.zeros_like(sums)
-        stat_ref[...] = before_ref[...]
-
-    @pl.when(step + DEEP - 1 < length)
-    def ahead():
-        fetch(step + DEEP - 1)
-
-    place = units_ref[2, step]
-    for wanted in range(len(pieces)):
-
-        @pl.when((place == wanted) & (units_ref[3, step] == 1))
-        def arrived(wanted=wanted):
-            gather_pieces(wanted, lambda copy: copy.wait())
-
-    block = stacked[:, pl.ds(pl.multiple_of(place * width, width), width)]
-
-    @pl.when(units_ref[4, step] == 1)
-    def square():
-        gain = gains_ref[blocks_ref[2, units_ref[1, step]]]
-        weight = 1.0 / (gain * gain)
-        squares = stat_ref[...]
-        for column in range(0, width, LANES):
-            value = stacked[:, pl.ds(pl.multiple_of(place * width + column, LANES), LANES)].astype(jnp.float32)
-            squares = squares + value * value * weight[:, column : column + LANES]
+        fetch(0)
+        gather_pieces(lambda copy: copy.start())
+        gather_pieces(lambda copy: copy.wait())
+        squares = before_ref[...]
+        for place in range(len(pieces)):
+            if place + start in counted:
+                continue
+            gain = gains_ref[blocks_ref[2, place + start]]
+            weight = 1.0 / (gain * gain)
+            for column in range(0, width, LANES):
+                value = stacked[:, place * width + column : place * width + column + LANES].astype(jnp.float32)
+                squares = squares + value * value * weight[:, column : column + LANES]
         stat_ref[...] = squares
-
-    slot = lax.rem(step, DEEP)
-    pltpu.make_async_copy(own_and_other[0][0].at[pl.ds(0, width)], weights.at[slot], weight_sems.at[slot]).wait()
-    which = units_ref[0, step]
-    place_of_sum = which if final else 0
-    sums[place_of_sum] += jnp.dot(block, weights[slot], preferred_element_type=jnp.float32)
-
-    @pl.when(step == length - 1)
-    def finish():
         if final:
-            partials(lambda copy: copy.wait())
-            inv = lax.rsqrt(jnp.sum(stat_ref[...], axis=1, keepdims=True) / mean_of + 1e-05)
-            gate, up = (sums[kind] + partial[kind] if kind in taken else sums[kind] for kind in range(2))
-            gate = gate * inv
-            out_ref[...] = (gate / (1.0 + jnp.exp(-gate)) * (up * inv)).astype(jnp.bfloat16)
-        else:
-            out_ref[...] = sums[0]
-
-
-def gate_up(units, final, partial, squares, blocks, pieces, gains, weights):
+            total = jnp.sum(squares, axis=1, keepdims=True)
+            inv[...] = jnp.broadcast_to(lax.rsqrt(total / mean_of + 1e-05), inv.shape)
+
+    sums = {which: partial_refs[which][...] for which in taken}
+    for number, (which, low, high) in enumerate(chunks):
+        arrive(number)
+        if number == 0:
+
+            @pl.when(step == 0)
+            def follow():
+                for later in range(1, DEEP - 1):
+                    fetch_if_any(later)
+
+        fetch_if_any(number + DEEP - 1)
+        term = jnp.dot(
+            stacked[:, (low - start) * width : (high - start) * width],
+            weights[slot_of(number), : (high - low) * width],
+            preferred_element_type=jnp.float32,
+        )
+        sums[which] = sums[which] + term if which in sums else term
+    if final:
+        gate, up = sums[0] * inv[:, :1], sums[1] * inv[:, :1]
+        out_ref[...] = (gate / (1.0 + jnp.exp(-gate)) * up).astype(jnp.bfloat16)
+    else:
+        out_ref[...] = sums[min(ranges)]
+
+
+def gate_up(ranges, final, partial, squares, blocks, pieces, gains, weights):
     sofar, counted = squares
     rows, width = sofar.shape[0], pieces[0][0].shape[1]
     count = blocks.shape[1]
     columns = weights[0].shape[1]
-    used = sorted({block for _, block in units})
-    table = np.zeros((5, len(units)), np.int32)
-    seen = set()
-    for number, (which, block) in enumerate(units):
-        fresh = block not in seen
-        seen.add(block)
-        table[:, number] = which, block, used.index(block), fresh, fresh and block not in counted
+    tile = min(512, columns)
+    used = range(min(low for low, _ in ranges.values()), max(high for _, high in ranges.values()))
+    most = max(1, 4096 // width)
+    chunks = []
+    for which, (low, high) in ranges.items():
+        parts = -(-(high - low) // most)
+        cuts = [low + (high - low) * part // parts for part in range(parts + 1)]
+        chunks += [(which, *cut) for cut in zip(cuts, cuts[1:])]
     taken = sorted(partial)
-    operands = [part for block in used for part in pieces[block]] + [partial[which] for which in taken]
-    kinds = sorted({which for which, _ in units})
+    operands = [part for block in used for part in pieces[block]]
+    kinds = sorted(ranges)
     weights = [pair for which in range(2) for pair in weights[2 * kinds[which % len(kinds)] :][:2]]
     anywhere = pl.BlockSpec(memory_space=pl.ANY)
     needed = [len(pieces[block]) for block in used]
-    fixed = (needed, final, taken, width * count, len(units))
-    whole = lambda *shape: pl.BlockSpec(shape, lambda n, blocks, units: (0,) * len(shape))
-    sums_shape = (2 if final else 1, rows, columns)
-    out, squares = pl.pallas_call(
+    fixed = (ranges, counted, needed, final, taken, width * count, chunks)
+
+    def whole(*shape):
+        return pl.BlockSpec(shape, lambda n, blocks: (0,) * len(shape))
+
+    tiled = pl.BlockSpec((rows, tile), lambda n, blocks: (0, n))
+    longest = max(high - low for _, low, high in chunks)
+    out, stat = pl.pallas_call(
         functools.partial(gate_up_kernel, fixed),
         out_shape=(
             jax.ShapeDtypeStruct((rows, columns), jnp.bfloat16 if final else jnp.float32),
             jax.ShapeDtypeStruct((rows, LANES), jnp.float32),
         ),
         grid_spec=pltpu.PrefetchScalarGridSpec(
-            num_scalar_prefetch=2,
-            grid=(len(units),),
-            in_specs=[*[anywhere] * len(operands), whole(*gains.shape), *[anywhere] * 4, whole(rows, LANES)],
-            out_specs=(whole(rows, columns), whole(rows, LANES)),
+            num_scalar_prefetch=1,
+            grid=(columns // tile,),
+            in_specs=[
+                *[anywhere] * len(operands),
+                *[tiled] * len(taken),
+                whole(*gains.shape),
+                whole(rows, LANES),
+                *[anywhere] * 4,
+            ],
+            out_specs=(tiled, whole(rows, LANES)),
             scratch_shapes=[
                 pltpu.VMEM((rows, len(used) * width), jnp.bfloat16),
-                pltpu.VMEM(sums_shape, jnp.float32),
-                pltpu.VMEM((2 if taken else 1, rows if taken else 8, columns), jnp.float32),
-                pltpu.VMEM((DEEP, width, columns), jnp.bfloat16),
+                pltpu.VMEM((rows, LANES), jnp.float32),
+                pltpu.VMEM((DEEP, longest * width, tile), jnp.bfloat16),
                 pltpu.SemaphoreType.DMA((len(used), max(needed))),
-                pltpu.SemaphoreType.DMA((2,)),
                 pltpu.SemaphoreType.DMA((DEEP,)),
             ],
         ),
         compiler_params=pltpu.CompilerParams(vmem_limit_bytes=VMEM_LIMIT),
         cost_estimate=pl.CostEstimate(
-            flops=4 * rows * width * columns * len(units),
-            bytes_accessed=2 * width * columns * len(units),
+            flops=4 * rows * width * columns * sum(high - low for low, high in ranges.values()),
+            bytes_accessed=2 * width * columns * sum(high - low for low, high in ranges.values()),
             transcendentals=rows * columns if final else 0,
         ),
         name="gate_up",
-    )(blocks, jnp.asarray(table), *operands, gains, *weights, sofar)
-    return out, (squares, counted | set(used))
+    )(blocks, *operands, *[partial[which] for which in taken], gains, sofar, *weights)
+    return out, (stat, counted | set(used))
 
 
 def down_kernel(start, steps, tiles_ref, hidden, local_ref, other_ref, out_ref, buffer, sems):
@@ -229,15 +238,20 @@
 
     @pl.when(step == 0)
     def first():
-        for number in range(min(DEEP - 1, steps)):
+        fetch(jnp.int32(0))
+
+    slot = lax.rem(step, DEEP)
+    pltpu.make_async_copy(local_ref.at[:, pl.ds(0, width)], buffer.at[slot], sems.at[slot]).wait()
+
+    @pl.when(step == 0)
+    def follow():
+        for number in range(1, min(DEEP - 1, steps)):
             fetch(jnp.int32(number))
 
     @pl.when(step + DEEP - 1 < steps)
     def ahead():
         fetch(step + DEEP - 1)
 
-    slot = lax.rem(step, DEEP)
-    pltpu.make_async_copy(local_ref.at[:, pl.ds(0, width)], buffer.at[slot], sems.at[slot]).wait()
     weight = buffer[slot]
     out_ref[0] = jnp.dot(hidden[...], weight, preferred_element_type=jnp.float32).astype(jnp.bfloat16)
 
@@ -344,14 +358,11 @@
     size = row_count // 2
     early = min(3, count - 1)
 
-    def matmul(units, final, partial, squares, block, steps, *earlier):
+    def matmul(ranges, final, partial, squares, block, steps, *earlier):
         pieces = [[block]]
         for number, step in enumerate(steps):
             pieces += [[step[0]], [step[1]]] if number < half - 1 else [list(step)]
-        return gate_up(units, final, partial, squares, blocks, after(pieces, *earlier), gains, weights)
-
-    def units(which, start, stop):
-        return [(which, block) for block in range(start, stop)]
+        return gate_up(ranges, final, partial, squares, blocks, after(pieces, *earlier), gains, weights)
 
     def open_down(hidden, *earlier):
         return down(0, early, tiles, after(hidden, *earlier), down_weight, other_down, width)
@@ -377,14 +388,14 @@
     while len(steps_a) < half - 1:
         if len(steps_a) == half - 2:
             near = 2 * len(steps_a) + 1
-            gate_a, squares_a = matmul(units(0, 0, near), False, {}, nothing, block_a, steps_a)
+            gate_a, squares_a = matmul({0: (0, near)}, False, {}, nothing, block_a, steps_a)
         steps_a = gather_step(block_a, steps_a, half)
     steps_b = gather_step(block_b, [], half, gate_a)
-    up_a, squares_a = matmul(units(1, 0, count - 1), False, {}, squares_a, block_a, steps_a, gate_a)
+    up_a, squares_a = matmul({1: (0, count - 1)}, False, {}, squares_a, block_a, steps_a, gate_a)
     steps_a = gather_step(block_a, steps_a, half, gate_a)
     first_b = steps_b[-1]
     steps_b = gather_step(block_b, steps_b, half, up_a, steps_a[-1])
-    rest = units(0, near, count) + units(1, count - 1, count)
+    rest = {0: (near, count), 1: (count - 1, count)}
     hidden_a, _ = matmul(rest, True, {0: gate_a, 1: up_a}, squares_a, block_a, steps_a, first_b)
     second_b = steps_b[-1]
     steps_b = gather_step(block_b, steps_b, half, hidden_a)
@@ -398,9 +409,9 @@
     distances = list(range(half - 1, 0, -1))
     moved_a = scatter_send(scatter_sums(None, term_a, count, half, third_b))
     sums_a = scatter_sums(moved_a, term_a, count, distances.pop(0))
-    gate_b, squares_b = matmul(units(0, 0, count), False, {}, nothing, block_b, steps_b, closed_a, sums_a)
+    gate_b, squares_b = matmul({0: (0, count)}, False, {}, nothing, block_b, steps_b, closed_a, sums_a)
     sums_a = scatter_sums(scatter_send(sums_a), term_a, count, distances.pop(0))
-    hidden_b, _ = matmul(units(1, 0, count), True, {0: gate_b}, squares_b, block_b, steps_b, sums_a)
+    hidden_b, _ = matmul({1: (0, count)}, True, {0: gate_b}, squares_b, block_b, steps_b, sums_a)
     for distance in distances:
         sums_a = scatter_sums(scatter_send(sums_a), term_a, count, distance)
     opened_b = open_down(hidden_b, sums_a)

time: 216 us -> 221 us (1.023)
  Pallas kernels: 105 us -> 114 us
  waiting for transfers between devices: 52.7 us -> 48.6 us
    pallas_call x5, Pallas kernels: 72.5 us -> 77.9 us  [gate_up(): pl.pallas_call(functools.partial(gate_up_kernel, fixed), out_shape=(jax.S...]
    ppermute x40, waiting for transfers between devices: 52.5 us -> 48.6 us  [ring_shift(): lax.ppermute(value, 'blk', [(ring[i], ring[(i + steps) % count]) for i in...]
    pallas_call x4, Pallas kernels: 32.1 us -> 35.7 us  [down(): pl.pallas_call(functools.partial(down_kernel, start, stop - start), out_s...]
  transfers between devices with their start and end apart: 44 -> 44, of which waited for: 20 -> 18; matrix products, arithmetic and copies ran while one was open for 3% -> 3% of each run, Pallas kernels for 49% -> 51%
where the time goes in v9:
time: 221 us
  Pallas kernels  114 us (52%)
  waiting for transfers between devices  48.6 us (22%)
  starting transfers between devices  46.9 us (21%)
  other arithmetic  8.59 us (4%)
    pallas_call x5, Pallas kernels, gate_up(): pl.pallas_call(functools.partial(gate_up_kernel, fixed), out_shape=(jax.S...  77.9 us
    ppermute x40, waiting for transfers between devices, ring_shift(): lax.ppermute(value, 'blk', [(ring[i], ring[(i + steps) % count]) for i in...  48.6 us
    ppermute x40, starting transfers between devices, ring_shift(): lax.ppermute(value, 'blk', [(ring[i], ring[(i + steps) % count]) for i in...  43.9 us
    pallas_call x4, Pallas kernels, down(): pl.pallas_call(functools.partial(down_kernel, start, stop - start), out_s...  35.7 us
  transfers between devices with their start and end apart: 44, of which 18 were waited for; matrix products, arithmetic and copies ran while one was open for 3% of the time, Pallas kernels for 51%

profile of v9, /device:TPU:0, one launch (start us, length us, event | category | flops | bytes accessed | tf_op | source)
XLA Modules:
  0.0 220.7 jit_solution(11277232676902245047)
XLA Ops:
  0.0 0.8 multiply_add_fusion.2
  0.8 2.4 %collective-permute-start = (f32[3,1024]{1,0:T(4,128)S(1)}, f32[3,1024]{1,0:T(4,128)S(1)}, u32[]{:S(2)}, u32[]{:S(2)}) collective-permute-start(f32[3,1024]{1,0:T(4,128)S(1)} %multiply_add_fusion.2), channel_id=1, source_target_pairs={{0,1},{2,3},{4,5},{6,7},{8,9},{10,11},{12,13},{14,15},{16,17},{18,... | collective-permute-start | bytes 36872 | tf_op jit(solution)/shard_map/ppermute | solution.py:341
  3.1 1.5 multiply_add_fusion
  5.3 0.9 constant_dynamic-slice_fusion.2
  6.3 0.5 multiply_convert_fusion.1.refs_0_
  7.4 2.4 %collective-permute-start.1 = (bf16[256,1024]{1,0:T(8,128)(2,1)S(1)}, bf16[256,1024]{1,0:T(8,128)(2,1)S(1)}, u32[]{:S(2)}, u32[]{:S(2)}) collective-permute-start(bf16[256,1024]{1,0:T(8,128)(2,1)S(1)} %multiply_convert_fusion.1.refs_0_), channel_id=1, source_target_pairs={{0,4},{4,8},{8,12},{12,14},{14,10},{10,6},{6,2},{2,0},{1,5},{5,9},... | collective-permute-start | bytes 1572872 | tf_op jit(solution)/shard_map/ppermute | solution.py:55
  9.8 0.7 dynamic-slice_bitcast_fusion
  10.5 11.8 %collective-permute-done.1.refs_1_ = bf16[256,1024]{1,0:T(8,128)(2,1)S(1)} collective-permute-done((bf16[256,1024]{1,0:T(8,128)(2,1)S(1)}, bf16[256,1024]{1,0:T(8,128)(2,1)S(1)}, u32[]{:S(2)}, u32[]{:S(2)}) %collective-permute-start.1) | collective-permute-done | bytes 524320 | tf_op jit(solution)/shard_map/ppermute | solution.py:55
  22.3 1.5 collective-permute-done.2.refs_2_
  23.8 1.6 collective-permute-start.3
  25.9 1.2 multiply_add_fusion.1
  27.1 0.5 multiply_convert_fusion.refs_0_
  27.6 9.4 %collective-permute-done.3.refs_3_ = bf16[256,1024]{1,0:T(8,128)(2,1)S(1)} collective-permute-done((bf16[256,1024]{1,0:T(8,128)(2,1)S(1)}, bf16[256,1024]{1,0:T(8,128)(2,1)S(1)}, u32[]{:S(2)}, u32[]{:S(2)}) %collective-permute-start.3) | collective-permute-done | bytes 524320 | tf_op jit(solution)/shard_map/ppermute | solution.py:55
  37.0 1.3 collective-permute-done.4.refs_4_
  38.3 1.6 collective-permute-start.8
  40.3 12.8 %gate_up.5 = (f32[256,2048]{1,0:T(8,128)}, f32[256,128]{1,0:T(8,128)S(1)}) custom-call(s32[3,8]{1,0:T(4,128)S(1)} %get-tuple-element.225.blocks_ref, bf16[256,1024]{1,0:T(8,128)(2,1)S(1)} %multiply_convert_fusion.1.refs_0_, bf16[256,1024]{1,0:T(8,128)(2,1)S(1)} %collective-permute-done.1.refs_1_, bf16[256,1024]{1,0:T(8,128)(2,1)S(1)} %collective-permute-done.2.refs_2_, ...), custom_call_target="tpu_custom_call" | custom-call | flops 10737418240 | bytes 20971520 | tf_op jit(solution)/shard_map/gate_up/pallas_call | solution.py:186
  53.2 0.5 collective-permute-start.12
  53.7 1.6 collective-permute-start.11
  55.3 1.6 collective-permute-start.6
  56.9 1.8 collective-permute-start.7
  58.7 15.6 %gate_up.6 = (f32[256,2048]{1,0:T(8,128)}, f32[256,128]{1,0:T(8,128)S(1)}) custom-call(s32[3,8]{1,0:T(4,128)S(1)} %get-tuple-element.225.blocks_ref, bf16[256,1024]{1,0:T(8,128)(2,1)S(1)} %multiply_convert_fusion.1.refs_0_, bf16[256,1024]{1,0:T(8,128)(2,1)S(1)} %collective-permute-done.1.refs_1_, bf16[256,1024]{1,0:T(8,128)(2,1)S(1)} %collective-permute-done.2.refs_2_, ...), custom_call_target="tpu_custom_call" | custom-call | flops 15032385536 | bytes 29360128 | tf_op jit(solution)/shard_map/gate_up/pallas_call | solution.py:186
  74.6 1.8 collective-permute-start.14
  76.4 12.2 %gate_up.7 = (bf16[256,2048]{1,0:T(8,128)(2,1)S(1)}, f32[256,128]{1,0:T(8,128)}) custom-call(s32[3,8]{1,0:T(4,128)S(1)} %get-tuple-element.225.blocks_ref, bf16[256,1024]{1,0:T(8,128)(2,1)S(1)} %collective-permute-done.8.refs_5_.refs_0_, bf16[256,1024]{1,0:T(8,128)(2,1)S(1)} %collective-permute-done.9.refs_6_.refs_1_, ...), custom_call_target="tpu_custom_call" | custom-call | flops 8589934592 | bytes 16777216 | tf_op jit(solution)/shard_map/gate_up/pallas_call | solution.py:186
  88.7 1.2 collective-permute-start.15
  89.9 0.9 collective-permute-start.16
  90.8 7.6 %down.4 = bf16[3,256,1024]{2,1,0:T(8,128)(2,1)S(1)} custom-call(s32[3,8]{1,0:T(4,128)S(1)} %get-tuple-element.226.tiles_ref, bf16[256,2048]{1,0:T(8,128)(2,1)S(1)} %get-tuple-element.141.hidden, bf16[2048,4096]{1,0:T(8,128)(2,1)} %local_ref.7, bf16[2048,4096]{1,0:T(8,128)(2,1)} %collective-permute-done.17.other_ref), custom_call_target="tpu_custom_call" | custom-call | flops 6442450944 | bytes 12582912 | tf_op jit(solution)/shard_map/down/pallas_call | solution.py:262
  98.4 3.6 %collective-permute-done.15.refs_5_ = bf16[256,1024]{1,0:T(8,128)(2,1)S(1)} collective-permute-done((bf16[256,1024]{1,0:T(8,128)(2,1)S(1)}, bf16[256,1024]{1,0:T(8,128)(2,1)S(1)}, u32[]{:S(2)}, u32[]{:S(2)}) %collective-permute-start.15) | collective-permute-done | bytes 524320 | tf_op jit(solution)/shard_map/ppermute | solution.py:55
  102.2 1.7 collective-permute-start.19
  104.2 1.6 collective-permute-start.20
  106.3 10.3 %down.5 = bf16[5,256,1024]{2,1,0:T(8,128)(2,1)S(1)} custom-call(s32[3,8]{1,0:T(4,128)S(1)} %get-tuple-element.226.tiles_ref, bf16[256,2048]{1,0:T(8,128)(2,1)S(1)} %get-tuple-element.141.hidden, bf16[2048,4096]{1,0:T(8,128)(2,1)} %local_ref.7, bf16[2048,4096]{1,0:T(8,128)(2,1)} %collective-permute-done.17.other_ref), custom_call_target="tpu_custom_call" | custom-call | flops 10737418240 | bytes 20971520 | tf_op jit(solution)/shard_map/down/pallas_call | solution.py:262
  116.8 1.6 collective-permute-start.22
  118.5 0.7 collective-permute-start.23
  119.2 18.6 %gate_up.8 = (f32[256,2048]{1,0:T(8,128)}, f32[256,128]{1,0:T(8,128)S(1)}) custom-call(s32[3,8]{1,0:T(4,128)S(1)} %get-tuple-element.225.blocks_ref, bf16[256,1024]{1,0:T(8,128)(2,1)S(1)} %multiply_convert_fusion.refs_0_, bf16[256,1024]{1,0:T(8,128)(2,1)S(1)} %collective-permute-done.6.refs_1_, bf16[256,1024]{1,0:T(8,128)(2,1)S(1)} %collective-permute-done.7.refs_2_, ...), custom_call_target="tpu_custom_call" | custom-call | flops 17179869184 | bytes 33554432 | tf_op jit(solution)/shard_map/gate_up/pallas_call | solution.py:186
  138.2 1.7 collective-permute-start.25
  140.3 18.7 %gate_up.9 = (bf16[256,2048]{1,0:T(8,128)(2,1)}, f32[256,128]{1,0:T(8,128)}) custom-call(s32[3,8]{1,0:T(4,128)S(1)} %get-tuple-element.225.blocks_ref, bf16[256,1024]{1,0:T(8,128)(2,1)S(1)} %multiply_convert_fusion.refs_0_, bf16[256,1024]{1,0:T(8,128)(2,1)S(1)} %collective-permute-done.6.refs_1_, bf16[256,1024]{1,0:T(8,128)(2,1)S(1)} %collective-permute-done.7.refs_2_, ...), custom_call_target="tpu_custom_call" | custom-call | flops 17179869184 | bytes 33554432 | tf_op jit(solution)/shard_map/gate_up/pallas_call | solution.py:186
  159.4 1.7 collective-permute-start.26
  161.5 7.6 %down.6 = bf16[3,256,1024]{2,1,0:T(8,128)(2,1)S(1)} custom-call(s32[3,8]{1,0:T(4,128)S(1)} %get-tuple-element.226.tiles_ref, bf16[256,2048]{1,0:T(8,128)(2,1)S(1)} %copy-done, bf16[2048,4096]{1,0:T(8,128)(2,1)} %local_ref.7, bf16[2048,4096]{1,0:T(8,128)(2,1)} %collective-permute-done.17.other_ref), custom_call_target="tpu_custom_call" | custom-call | flops 6442450944 | bytes 12582912 | tf_op jit(solution)/shard_map/down/pallas_call | solution.py:262
  169.1 2.2 %collective-permute-done.26 = bf16[256,1024]{1,0:T(8,128)(2,1)S(1)} collective-permute-done((bf16[256,1024]{1,0:T(8,128)(2,1)S(1)}, bf16[256,1024]{1,0:T(8,128)(2,1)S(1)}, u32[]{:S(2)}, u32[]{:S(2)}) %collective-permute-start.26) | collective-permute-done | bytes 524320 | tf_op jit(solution)/shard_map/ppermute | solution.py:55
  171.3 0.6 collective-permute-done.27
  172.0 1.3 collective-permute-start.28
  173.3 0.7 collective-permute-start.29
  174.0 1.3 collective-permute-start.30
  175.3 0.7 collective-permute-start.31
  176.0 2.2 %collective-permute-done.28 = bf16[64,1024]{1,0:T(8,128)(2,1)S(1)} collective-permute-done((bf16[64,1024]{1,0:T(8,128)(2,1)S(1)}, bf16[64,1024]{1,0:T(8,128)(2,1)S(1)}, u32[]{:S(2)}, u32[]{:S(2)}) %collective-permute-start.28) | collective-permute-done | bytes 131104 | tf_op jit(solution)/shard_map/ppermute | solution.py:55
  178.2 1.4 collective-permute-done.29
  179.7 1.3 collective-permute-done.30
  181.0 1.4 collective-permute-done.31
  182.5 1.8 collective-permute-start.36
  184.7 1.7 collective-permute-start.32
  186.7 10.3 %down.7 = bf16[5,256,1024]{2,1,0:T(8,128)(2,1)S(1)} custom-call(s32[3,8]{1,0:T(4,128)S(1)} %get-tuple-element.226.tiles_ref, bf16[256,2048]{1,0:T(8,128)(2,1)S(1)} %copy-done, bf16[2048,4096]{1,0:T(8,128)(2,1)} %local_ref.7, bf16[2048,4096]{1,0:T(8,128)(2,1)} %collective-permute-done.17.other_ref), custom_call_target="tpu_custom_call" | custom-call | flops 10737418240 | bytes 20971520 | tf_op jit(solution)/shard_map/down/pallas_call | solution.py:262
  197.0 0.9 collective-permute-done.33
  198.2 2.4 %collective-permute-start.34 = (bf16[128,1024]{1,0:T(8,128)(2,1)S(1)}, bf16[128,1024]{1,0:T(8,128)(2,1)S(1)}, u32[]{:S(2)}, u32[]{:S(2)}) collective-permute-start(bf16[128,1024]{1,0:T(8,128)(2,1)S(1)} %get-tuple-element.198), channel_id=1, source_target_pairs={{0,4},{4,8},{8,12},{12,14},{14,10},{10,6},{6,2},{2,0},{1,5},{5,9},... | collective-permute-start | bytes 786440 | tf_op jit(solution)/shard_map/ppermute | solution.py:55
  200.9 2.0 collective-permute-start.40
  202.9 3.3 %collective-permute-done.35 = bf16[128,1024]{1,0:T(8,128)(2,1)S(1)} collective-permute-done((bf16[128,1024]{1,0:T(8,128)(2,1)S(1)}, bf16[128,1024]{1,0:T(8,128)(2,1)S(1)}, u32[]{:S(2)}, u32[]{:S(2)}) %collective-permute-start.35) | collective-permute-done | bytes 262176 | tf_op jit(solution)/shard_map/ppermute | solution.py:55
  206.3 1.2 collective-permute-done.34
  207.6 0.9 collective-permute-start.39
  208.5 1.5 collective-permute-start.38
  210.0 0.5 collective-permute-done.41
  210.7 2.1 collective-permute-start.42
  212.8 0.5 fusion.15
  213.3 4.4 %collective-permute-done.42 = bf16[128,1024]{1,0:T(8,128)(2,1)S(1)} collective-permute-done((bf16[128,1024]{1,0:T(8,128)(2,1)S(1)}, bf16[128,1024]{1,0:T(8,128)(2,1)S(1)}, u32[]{:S(2)}, u32[]{:S(2)}) %collective-permute-start.42) | collective-permute-done | bytes 262176 | tf_op jit(solution)/shard_map/ppermute | solution.py:55
  217.7 1.5 collective-permute-done.43
  219.2 0.5 fusion.33
  219.7 1.0 pad_maximum_fusion.1
  (82 shorter events, 6.8 us)
Async XLA Ops:
  0.0 5.3 %copy-start.1 = (f32[8192]{0:T(1024)S(1)}, f32[8192]{0:T(1024)}, u32[]{:S(2)}) copy-start(f32[8192]{0:T(1024)} %param.15) | copy-start | bytes 98308
  0.8 6.0 %collective-permute-start = (f32[3,1024]{1,0:T(4,128)S(1)}, f32[3,1024]{1,0:T(4,128)S(1)}, u32[]{:S(2)}, u32[]{:S(2)}) collective-permute-start(f32[3,1024]{1,0:T(4,128)S(1)} %multiply_add_fusion.2), channel_id=1, source_target_pairs={{0,1},{2,3},{4,5},{6,7},{8,9},{10,11},{12,13},{14,15},{16,17},{18,... | collective-permute-start | bytes 36872 | tf_op jit(solution)/shard_map/ppermute | solution.py:341
  6.2 19.6 %copy-start.2 = (bf16[512,1024]{1,0:T(8,128)(2,1)S(1)}, bf16[512,1024]{1,0:T(8,128)(2,1)}, u32[]{:S(2)}) copy-start(bf16[512,1024]{1,0:T(8,128)(2,1)} %param.11) | copy-start | bytes 3145732
  6.2 19.6 %copy-start.6 = (f32[1024]{0:T(1024)S(1)}, f32[1024]{0:T(1024)}, u32[]{:S(2)}) copy-start(f32[1024]{0:T(1024)} %param.12) | copy-start | bytes 12292
  6.8 33.5 %collective-permute-start.5 = (bf16[4096,2048]{1,0:T(8,128)(2,1)}, bf16[4096,2048]{1,0:T(8,128)(2,1)}, u32[]{:S(2)}, u32[]{:S(2)}) collective-permute-start(bf16[4096,2048]{1,0:T(8,128)(2,1)} %refs_13_.1), channel_id=1, source_target_pairs={{0,1},{1,0},{2,3},{3,2},{4,5},{5,4},{6,7},{7,6},{8,9},{9,8},{10,11... | collective-permute-start | bytes 50331656 | tf_op jit(solution)/shard_map/ppermute | solution.py:59
  6.9 50.0 %collective-permute-start.10 = (bf16[4096,2048]{1,0:T(8,128)(2,1)}, bf16[4096,2048]{1,0:T(8,128)(2,1)}, u32[]{:S(2)}, u32[]{:S(2)}) collective-permute-start(bf16[4096,2048]{1,0:T(8,128)(2,1)} %refs_14_.1), channel_id=1, source_target_pairs={{0,1},{1,0},{2,3},{3,2},{4,5},{5,4},{6,7},{7,6},{8,9},{9,8},{10,11... | collective-permute-start | bytes 50331656 | tf_op jit(solution)/shard_map/ppermute | solution.py:59
  7.4 83.4 %collective-permute-start.17 = (bf16[2048,4096]{1,0:T(8,128)(2,1)}, bf16[2048,4096]{1,0:T(8,128)(2,1)}, u32[]{:S(2)}, u32[]{:S(2)}) collective-permute-start(bf16[2048,4096]{1,0:T(8,128)(2,1)} %local_ref.7), channel_id=1, source_target_pairs={{0,1},{1,0},{2,3},{3,2},{4,5},{5,4},{6,7},{7,6},{8,9},{9,8},{10,11... | collective-permute-start | bytes 50331656 | tf_op jit(solution)/shard_map/ppermute | solution.py:59
  7.4 14.9 %collective-permute-start.1 = (bf16[256,1024]{1,0:T(8,128)(2,1)S(1)}, bf16[256,1024]{1,0:T(8,128)(2,1)S(1)}, u32[]{:S(2)}, u32[]{:S(2)}) collective-permute-start(bf16[256,1024]{1,0:T(8,128)(2,1)S(1)} %multiply_convert_fusion.1.refs_0_), channel_id=1, source_target_pairs={{0,4},{4,8},{8,12},{12,14},{14,10},{10,6},{6,2},{2,0},{1,5},{5,9},... | collective-permute-start | bytes 1572872 | tf_op jit(solution)/shard_map/ppermute | solution.py:55
  9.8 14.0 %collective-permute-start.2 = (bf16[256,1024]{1,0:T(8,128)(2,1)S(1)}, bf16[256,1024]{1,0:T(8,128)(2,1)S(1)}, u32[]{:S(2)}, u32[]{:S(2)}) collective-permute-start(bf16[256,1024]{1,0:T(8,128)(2,1)S(1)} %multiply_convert_fusion.1.refs_0_), channel_id=1, source_target_pairs={{0,2},{4,0},{8,4},{12,8},{14,12},{10,14},{6,10},{2,6},{1,3},{5,1},... | collective-permute-start | bytes 1572872 | tf_op jit(solution)/shard_map/ppermute | solution.py:55
  23.8 13.2 %collective-permute-start.3 = (bf16[256,1024]{1,0:T(8,128)(2,1)S(1)}, bf16[256,1024]{1,0:T(8,128)(2,1)S(1)}, u32[]{:S(2)}, u32[]{:S(2)}) collective-permute-start(bf16[256,1024]{1,0:T(8,128)(2,1)S(1)} %collective-permute-done.1.refs_1_), channel_id=1, source_target_pairs={{0,4},{4,8},{8,12},{12,14},{14,10},{10,6},{6,2},{2,0},{1,5},{5,9},... | collective-permute-start | bytes 1572872 | tf_op jit(solution)/shard_map/ppermute | solution.py:55
  25.4 12.9 %collective-permute-start.4 = (bf16[256,1024]{1,0:T(8,128)(2,1)S(1)}, bf16[256,1024]{1,0:T(8,128)(2,1)S(1)}, u32[]{:S(2)}, u32[]{:S(2)}) collective-permute-start(bf16[256,1024]{1,0:T(8,128)(2,1)S(1)} %collective-permute-done.2.refs_2_), channel_id=1, source_target_pairs={{0,2},{4,0},{8,4},{12,8},{14,12},{10,14},{6,10},{2,6},{1,3},{5,1},... | collective-permute-start | bytes 1572872 | tf_op jit(solution)/shard_map/ppermute | solution.py:55
  38.3 14.9 %collective-permute-start.8 = (bf16[256,1024]{1,0:T(8,128)(2,1)S(1)}, bf16[256,1024]{1,0:T(8,128)(2,1)S(1)}, u32[]{:S(2)}, u32[]{:S(2)}) collective-permute-start(bf16[256,1024]{1,0:T(8,128)(2,1)S(1)} %collective-permute-done.3.refs_3_), channel_id=1, source_target_pairs={{0,4},{4,8},{8,12},{12,14},{14,10},{10,6},{6,2},{2,0},{1,5},{5,9},... | collective-permute-start | bytes 1572872 | tf_op jit(solution)/shard_map/ppermute | solution.py:55
  39.9 13.3 %collective-permute-start.9 = (bf16[256,1024]{1,0:T(8,128)(2,1)S(1)}, bf16[256,1024]{1,0:T(8,128)(2,1)S(1)}, u32[]{:S(2)}, u32[]{:S(2)}) collective-permute-start(bf16[256,1024]{1,0:T(8,128)(2,1)S(1)} %collective-permute-done.4.refs_4_), channel_id=1, source_target_pairs={{0,2},{4,0},{8,4},{12,8},{14,12},{10,14},{6,10},{2,6},{1,3},{5,1},... | collective-permute-start | bytes 1572872 | tf_op jit(solution)/shard_map/ppermute | solution.py:55
  53.2 21.1 %collective-permute-start.12 = (bf16[128,1024]{1,0:T(8,128)(2,1)S(1)}, bf16[128,1024]{1,0:T(8,128)(2,1)S(1)}, u32[]{:S(2)}, u32[]{:S(2)}) collective-permute-start(bf16[128,1024]{1,0:T(8,128)(2,1)S(1)} %slice.332), channel_id=1, source_target_pairs={{0,2},{4,0},{8,4},{12,8},{14,12},{10,14},{6,10},{2,6},{1,3},{5,1},... | collective-permute-start | bytes 786440 | tf_op jit(solution)/shard_map/ppermute | solution.py:55
  53.7 20.6 %collective-permute-start.11 = (bf16[128,1024]{1,0:T(8,128)(2,1)S(1)}, bf16[128,1024]{1,0:T(8,128)(2,1)S(1)}, u32[]{:S(2)}, u32[]{:S(2)}) collective-permute-start(bf16[128,1024]{1,0:T(8,128)(2,1)S(1)} %slice.331), channel_id=1, source_target_pairs={{0,4},{4,8},{8,12},{12,14},{14,10},{10,6},{6,2},{2,0},{1,5},{5,9},... | collective-permute-start | bytes 786440 | tf_op jit(solution)/shard_map/ppermute | solution.py:55
  55.3 19.0 %collective-permute-start.6 = (bf16[256,1024]{1,0:T(8,128)(2,1)S(1)}, bf16[256,1024]{1,0:T(8,128)(2,1)S(1)}, u32[]{:S(2)}, u32[]{:S(2)}) collective-permute-start(bf16[256,1024]{1,0:T(8,128)(2,1)S(1)} %multiply_convert_fusion.refs_0_), channel_id=1, source_target_pairs={{0,4},{4,8},{8,12},{12,14},{14,10},{10,6},{6,2},{2,0},{1,5},{5,9},... | collective-permute-start | bytes 1572872 | tf_op jit(solution)/shard_map/ppermute | solution.py:55
  56.9 17.5 %collective-permute-start.7 = (bf16[256,1024]{1,0:T(8,128)(2,1)S(1)}, bf16[256,1024]{1,0:T(8,128)(2,1)S(1)}, u32[]{:S(2)}, u32[]{:S(2)}) collective-permute-start(bf16[256,1024]{1,0:T(8,128)(2,1)S(1)} %multiply_convert_fusion.refs_0_), channel_id=1, source_target_pairs={{0,2},{4,0},{8,4},{12,8},{14,12},{10,14},{6,10},{2,6},{1,3},{5,1},... | collective-permute-start | bytes 1572872 | tf_op jit(solution)/shard_map/ppermute | solution.py:55
  74.4 14.3 %collective-permute-start.13 = (bf16[256,1024]{1,0:T(8,128)(2,1)S(1)}, bf16[256,1024]{1,0:T(8,128)(2,1)S(1)}, u32[]{:S(2)}, u32[]{:S(2)}) collective-permute-start(bf16[256,1024]{1,0:T(8,128)(2,1)S(1)} %collective-permute-done.6.refs_1_), channel_id=1, source_target_pairs={{0,4},{4,8},{8,12},{12,14},{14,10},{10,6},{6,2},{2,0},{1,5},{5,9},... | collective-permute-start | bytes 1572872 | tf_op jit(solution)/shard_map/ppermute | solution.py:55
  74.6 14.0 %collective-permute-start.14 = (bf16[256,1024]{1,0:T(8,128)(2,1)S(1)}, bf16[256,1024]{1,0:T(8,128)(2,1)S(1)}, u32[]{:S(2)}, u32[]{:S(2)}) collective-permute-start(bf16[256,1024]{1,0:T(8,128)(2,1)S(1)} %collective-permute-done.7.refs_2_), channel_id=1, source_target_pairs={{0,2},{4,0},{8,4},{12,8},{14,12},{10,14},{6,10},{2,6},{1,3},{5,1},... | collective-permute-start | bytes 1572872 | tf_op jit(solution)/shard_map/ppermute | solution.py:55
  88.7 13.3 %collective-permute-start.15 = (bf16[256,1024]{1,0:T(8,128)(2,1)S(1)}, bf16[256,1024]{1,0:T(8,128)(2,1)S(1)}, u32[]{:S(2)}, u32[]{:S(2)}) collective-permute-start(bf16[256,1024]{1,0:T(8,128)(2,1)S(1)} %collective-permute-done.13.refs_3_), channel_id=1, source_target_pairs={{0,4},{4,8},{8,12},{12,14},{14,10},{10,6},{6,2},{2,0},{1,5},{5,9},... | collective-permute-start | bytes 1572872 | tf_op jit(solution)/shard_map/ppermute | solution.py:55
  89.9 12.2 %collective-permute-start.16 = (bf16[256,1024]{1,0:T(8,128)(2,1)S(1)}, bf16[256,1024]{1,0:T(8,128)(2,1)S(1)}, u32[]{:S(2)}, u32[]{:S(2)}) collective-permute-start(bf16[256,1024]{1,0:T(8,128)(2,1)S(1)} %collective-permute-done.14.refs_4_), channel_id=1, source_target_pairs={{0,2},{4,0},{8,4},{12,8},{14,12},{10,14},{6,10},{2,6},{1,3},{5,1},... | collective-permute-start | bytes 1572872 | tf_op jit(solution)/shard_map/ppermute | solution.py:55
  102.1 14.4 %copy-start.5 = (bf16[256,1024]{1,0:T(8,128)(2,1)}, bf16[256,1024]{1,0:T(8,128)(2,1)S(1)}, u32[]{:S(2)}) copy-start(bf16[256,1024]{1,0:T(8,128)(2,1)S(1)} %collective-permute-done.16.refs_6_) | copy-start | bytes 1572868
  102.2 17.0 %collective-permute-start.19 = (bf16[128,1024]{1,0:T(8,128)(2,1)S(1)}, bf16[128,1024]{1,0:T(8,128)(2,1)S(1)}, u32[]{:S(2)}, u32[]{:S(2)}) collective-permute-start(bf16[128,1024]{1,0:T(8,128)(2,1)S(1)} %slice.334), channel_id=1, source_target_pairs={{0,2},{4,0},{8,4},{12,8},{14,12},{10,14},{6,10},{2,6},{1,3},{5,1},... | collective-permute-start | bytes 786440 | tf_op jit(solution)/shard_map/ppermute | solution.py:55
  103.8 15.3 %collective-permute-start.18 = (bf16[128,1024]{1,0:T(8,128)(2,1)S(1)}, bf16[128,1024]{1,0:T(8,128)(2,1)S(1)}, u32[]{:S(2)}, u32[]{:S(2)}) collective-permute-start(bf16[128,1024]{1,0:T(8,128)(2,1)S(1)} %slice.333), channel_id=1, source_target_pairs={{0,4},{4,8},{8,12},{12,14},{14,10},{10,6},{6,2},{2,0},{1,5},{5,9},... | collective-permute-start | bytes 786440 | tf_op jit(solution)/shard_map/ppermute | solution.py:55
  104.2 12.3 %collective-permute-start.20 = (bf16[128,1024]{1,0:T(8,128)(2,1)S(1)}, bf16[128,1024]{1,0:T(8,128)(2,1)S(1)}, u32[]{:S(2)}, u32[]{:S(2)}) collective-permute-start(bf16[128,1024]{1,0:T(8,128)(2,1)S(1)} %get-tuple-element.142), channel_id=1, source_target_pairs={{0,4},{4,8},{8,12},{12,14},{14,10},{10,6},{6,2},{2,0},{1,5},{5,9},... | collective-permute-start | bytes 786440 | tf_op jit(solution)/shard_map/ppermute | solution.py:55
  105.8 10.7 %collective-permute-start.21 = (bf16[128,1024]{1,0:T(8,128)(2,1)S(1)}, bf16[128,1024]{1,0:T(8,128)(2,1)S(1)}, u32[]{:S(2)}, u32[]{:S(2)}) collective-permute-start(bf16[128,1024]{1,0:T(8,128)(2,1)S(1)} %get-tuple-element.143), channel_id=1, source_target_pairs={{0,2},{4,0},{8,4},{12,8},{14,12},{10,14},{6,10},{2,6},{1,3},{5,1},... | collective-permute-start | bytes 786440 | tf_op jit(solution)/shard_map/ppermute | solution.py:55
  116.8 20.9 %collective-permute-start.22 = (bf16[256,1024]{1,0:T(8,128)(2,1)S(1)}, bf16[256,1024]{1,0:T(8,128)(2,1)S(1)}, u32[]{:S(2)}, u32[]{:S(2)}) collective-permute-start(bf16[256,1024]{1,0:T(8,128)(2,1)S(1)} %pad_maximum_fusion.2), channel_id=1, source_target_pairs={{0,4},{4,8},{8,12},{12,14},{14,10},{10,6},{6,2},{2,0},{1,5},{5,9},... | collective-permute-start | bytes 1572872 | tf_op jit(solution)/shard_map/ppermute | solution.py:55
  118.5 19.3 %collective-permute-start.23 = (bf16[256,1024]{1,0:T(8,128)(2,1)S(1)}, bf16[256,1024]{1,0:T(8,128)(2,1)S(1)}, u32[]{:S(2)}, u32[]{:S(2)}) collective-permute-start(bf16[256,1024]{1,0:T(8,128)(2,1)S(1)} %pad_maximum_fusion.3), channel_id=1, source_target_pairs={{0,2},{4,0},{8,4},{12,8},{14,12},{10,14},{6,10},{2,6},{1,3},{5,1},... | collective-permute-start | bytes 1572872 | tf_op jit(solution)/shard_map/ppermute | solution.py:55
  138.2 20.8 %collective-permute-start.25 = (bf16[256,1024]{1,0:T(8,128)(2,1)S(1)}, bf16[256,1024]{1,0:T(8,128)(2,1)S(1)}, u32[]{:S(2)}, u32[]{:S(2)}) collective-permute-start(bf16[256,1024]{1,0:T(8,128)(2,1)S(1)} %get-tuple-element.201), channel_id=1, source_target_pairs={{0,2},{4,0},{8,4},{12,8},{14,12},{10,14},{6,10},{2,6},{1,3},{5,1},... | collective-permute-start | bytes 1572872 | tf_op jit(solution)/shard_map/ppermute | solution.py:55
  139.8 19.1 %collective-permute-start.24 = (bf16[256,1024]{1,0:T(8,128)(2,1)S(1)}, bf16[256,1024]{1,0:T(8,128)(2,1)S(1)}, u32[]{:S(2)}, u32[]{:S(2)}) collective-permute-start(bf16[256,1024]{1,0:T(8,128)(2,1)S(1)} %get-tuple-element.202), channel_id=1, source_target_pairs={{0,4},{4,8},{8,12},{12,14},{14,10},{10,6},{6,2},{2,0},{1,5},{5,9},... | collective-permute-start | bytes 1572872 | tf_op jit(solution)/shard_map/ppermute | solution.py:55
  158.9 2.5 %copy-start = (bf16[256,2048]{1,0:T(8,128)(2,1)S(1)}, bf16[256,2048]{1,0:T(8,128)(2,1)}, u32[]{:S(2)}) copy-start(bf16[256,2048]{1,0:T(8,128)(2,1)} %get-tuple-element.180.hidden) | copy-start | bytes 3145732
  159.4 12.0 %collective-permute-start.26 = (bf16[256,1024]{1,0:T(8,128)(2,1)S(1)}, bf16[256,1024]{1,0:T(8,128)(2,1)S(1)}, u32[]{:S(2)}, u32[]{:S(2)}) collective-permute-start(bf16[256,1024]{1,0:T(8,128)(2,1)S(1)} %get-tuple-element.199), channel_id=1, source_target_pairs={{0,4},{4,8},{8,12},{12,14},{14,10},{10,6},{6,2},{2,0},{1,5},{5,9},... | collective-permute-start | bytes 1572872 | tf_op jit(solution)/shard_map/ppermute | solution.py:55
  161.0 10.9 %collective-permute-start.27 = (bf16[256,1024]{1,0:T(8,128)(2,1)S(1)}, bf16[256,1024]{1,0:T(8,128)(2,1)S(1)}, u32[]{:S(2)}, u32[]{:S(2)}) collective-permute-start(bf16[256,1024]{1,0:T(8,128)(2,1)S(1)} %get-tuple-element.200), channel_id=1, source_target_pairs={{0,2},{4,0},{8,4},{12,8},{14,12},{10,14},{6,10},{2,6},{1,3},{5,1},... | collective-permute-start | bytes 1572872 | tf_op jit(solution)/shard_map/ppermute | solution.py:55
  172.0 6.3 %collective-permute-start.28 = (bf16[64,1024]{1,0:T(8,128)(2,1)S(1)}, bf16[64,1024]{1,0:T(8,128)(2,1)S(1)}, u32[]{:S(2)}, u32[]{:S(2)}) collective-permute-start(bf16[64,1024]{1,0:T(8,128)(2,1)S(1)} %get-tuple-element.172), channel_id=1, source_target_pairs={{0,4},{4,8},{8,12},{12,14},{14,10},{10,6},{6,2},{2,0},{1,5},{5,9},... | collective-permute-start | bytes 393224 | tf_op jit(solution)/shard_map/ppermute | solution.py:55
  173.3 6.3 %collective-permute-start.29 = (bf16[64,1024]{1,0:T(8,128)(2,1)S(1)}, bf16[64,1024]{1,0:T(8,128)(2,1)S(1)}, u32[]{:S(2)}, u32[]{:S(2)}) collective-permute-start(bf16[64,1024]{1,0:T(8,128)(2,1)S(1)} %get-tuple-element.173), channel_id=1, source_target_pairs={{0,2},{4,0},{8,4},{12,8},{14,12},{10,14},{6,10},{2,6},{1,3},{5,1},... | collective-permute-start | bytes 393224 | tf_op jit(solution)/shard_map/ppermute | solution.py:55
  174.0 7.1 %collective-permute-start.30 = (bf16[64,1024]{1,0:T(8,128)(2,1)S(1)}, bf16[64,1024]{1,0:T(8,128)(2,1)S(1)}, u32[]{:S(2)}, u32[]{:S(2)}) collective-permute-start(bf16[64,1024]{1,0:T(8,128)(2,1)S(1)} %get-tuple-element.174), channel_id=1, source_target_pairs={{0,4},{4,8},{8,12},{12,14},{14,10},{10,6},{6,2},{2,0},{1,5},{5,9},... | collective-permute-start | bytes 393224 | tf_op jit(solution)/shard_map/ppermute | solution.py:55
  175.3 7.1 %collective-permute-start.31 = (bf16[64,1024]{1,0:T(8,128)(2,1)S(1)}, bf16[64,1024]{1,0:T(8,128)(2,1)S(1)}, u32[]{:S(2)}, u32[]{:S(2)}) collective-permute-start(bf16[64,1024]{1,0:T(8,128)(2,1)S(1)} %get-tuple-element.175), channel_id=1, source_target_pairs={{0,2},{4,0},{8,4},{12,8},{14,12},{10,14},{6,10},{2,6},{1,3},{5,1},... | collective-permute-start | bytes 393224 | tf_op jit(solution)/shard_map/ppermute | solution.py:55
  182.5 18.1 %collective-permute-start.36 = (bf16[128,1024]{1,0:T(8,128)(2,1)S(1)}, bf16[128,1024]{1,0:T(8,128)(2,1)S(1)}, u32[]{:S(2)}, u32[]{:S(2)}) collective-permute-start(bf16[128,1024]{1,0:T(8,128)(2,1)S(1)} %pad_maximum_fusion.6), channel_id=1, source_target_pairs={{0,4},{4,8},{8,12},{12,14},{14,10},{10,6},{6,2},{2,0},{1,5},{5,9},... | collective-permute-start | bytes 786440 | tf_op jit(solution)/shard_map/ppermute | solution.py:55
  184.3 16.3 %collective-permute-start.37 = (bf16[128,1024]{1,0:T(8,128)(2,1)S(1)}, bf16[128,1024]{1,0:T(8,128)(2,1)S(1)}, u32[]{:S(2)}, u32[]{:S(2)}) collective-permute-start(bf16[128,1024]{1,0:T(8,128)(2,1)S(1)} %pad_maximum_fusion.7), channel_id=1, source_target_pairs={{0,2},{4,0},{8,4},{12,8},{14,12},{10,14},{6,10},{2,6},{1,3},{5,1},... | collective-permute-start | bytes 786440 | tf_op jit(solution)/shard_map/ppermute | solution.py:55
  184.7 12.3 %collective-permute-start.32 = (bf16[128,1024]{1,0:T(8,128)(2,1)S(1)}, bf16[128,1024]{1,0:T(8,128)(2,1)S(1)}, u32[]{:S(2)}, u32[]{:S(2)}) collective-permute-start(bf16[128,1024]{1,0:T(8,128)(2,1)S(1)} %pad_maximum_fusion.4), channel_id=1, source_target_pairs={{0,4},{4,8},{8,12},{12,14},{14,10},{10,6},{6,2},{2,0},{1,5},{5,9},... | collective-permute-start | bytes 786440 | tf_op jit(solution)/shard_map/ppermute | solution.py:55
  186.4 11.5 %collective-permute-start.33 = (bf16[128,1024]{1,0:T(8,128)(2,1)S(1)}, bf16[128,1024]{1,0:T(8,128)(2,1)S(1)}, u32[]{:S(2)}, u32[]{:S(2)}) collective-permute-start(bf16[128,1024]{1,0:T(8,128)(2,1)S(1)} %pad_maximum_fusion.5), channel_id=1, source_target_pairs={{0,2},{4,0},{8,4},{12,8},{14,12},{10,14},{6,10},{2,6},{1,3},{5,1},... | collective-permute-start | bytes 786440 | tf_op jit(solution)/shard_map/ppermute | solution.py:55
  198.1 8.2 %collective-permute-start.35 = (bf16[128,1024]{1,0:T(8,128)(2,1)S(1)}, bf16[128,1024]{1,0:T(8,128)(2,1)S(1)}, u32[]{:S(2)}, u32[]{:S(2)}) collective-permute-start(bf16[128,1024]{1,0:T(8,128)(2,1)S(1)} %get-tuple-element.197), channel_id=1, source_target_pairs={{0,2},{4,0},{8,4},{12,8},{14,12},{10,14},{6,10},{2,6},{1,3},{5,1},... | collective-permute-start | bytes 786440 | tf_op jit(solution)/shard_map/ppermute | solution.py:55
  198.2 14.6 %copy-start.3 = (bf16[512,1024]{1,0:T(8,128)(2,1)S(1)}, bf16[512,1024]{1,0:T(8,128)(2,1)}, u32[]{:S(2)}) copy-start(bf16[512,1024]{1,0:T(8,128)(2,1)} %param.11) | copy-start | bytes 3145732
  198.2 14.6 %copy-start.4 = (bf16[512,1024]{1,0:T(8,128)(2,1)S(1)}, bf16[512,1024]{1,0:T(8,128)(2,1)}, u32[]{:S(2)}) copy-start(bf16[512,1024]{1,0:T(8,128)(2,1)} %param.10) | copy-start | bytes 3145732
  198.2 14.6 %copy-start.7 = (f32[1024]{0:T(1024)S(1)}, f32[1024]{0:T(1024)}, u32[]{:S(2)}) copy-start(f32[1024]{0:T(1024)} %param.12) | copy-start | bytes 12292
  198.2 9.2 %collective-permute-start.34 = (bf16[128,1024]{1,0:T(8,128)(2,1)S(1)}, bf16[128,1024]{1,0:T(8,128)(2,1)S(1)}, u32[]{:S(2)}, u32[]{:S(2)}) collective-permute-start(bf16[128,1024]{1,0:T(8,128)(2,1)S(1)} %get-tuple-element.198), channel_id=1, source_target_pairs={{0,4},{4,8},{8,12},{12,14},{14,10},{10,6},{6,2},{2,0},{1,5},{5,9},... | collective-permute-start | bytes 786440 | tf_op jit(solution)/shard_map/ppermute | solution.py:55
  200.8 9.7 %collective-permute-start.41 = (bf16[128,1024]{1,0:T(8,128)(2,1)S(1)}, bf16[128,1024]{1,0:T(8,128)(2,1)S(1)}, u32[]{:S(2)}, u32[]{:S(2)}) collective-permute-start(bf16[128,1024]{1,0:T(8,128)(2,1)S(1)} %get-tuple-element.195), channel_id=1, source_target_pairs={{0,2},{4,0},{8,4},{12,8},{14,12},{10,14},{6,10},{2,6},{1,3},{5,1},... | collective-permute-start | bytes 786440 | tf_op jit(solution)/shard_map/ppermute | solution.py:55
  200.9 9.6 %collective-permute-start.40 = (bf16[128,1024]{1,0:T(8,128)(2,1)S(1)}, bf16[128,1024]{1,0:T(8,128)(2,1)S(1)}, u32[]{:S(2)}, u32[]{:S(2)}) collective-permute-start(bf16[128,1024]{1,0:T(8,128)(2,1)S(1)} %get-tuple-element.196), channel_id=1, source_target_pairs={{0,4},{4,8},{8,12},{12,14},{14,10},{10,6},{6,2},{2,0},{1,5},{5,9},... | collective-permute-start | bytes 786440 | tf_op jit(solution)/shard_map/ppermute | solution.py:55
  207.6 11.5 %collective-permute-start.39 = (bf16[128,1024]{1,0:T(8,128)(2,1)S(1)}, bf16[128,1024]{1,0:T(8,128)(2,1)S(1)}, u32[]{:S(2)}, u32[]{:S(2)}) collective-permute-start(bf16[128,1024]{1,0:T(8,128)(2,1)S(1)} %get-tuple-element.193), channel_id=1, source_target_pairs={{0,2},{4,0},{8,4},{12,8},{14,12},{10,14},{6,10},{2,6},{1,3},{5,1},... | collective-permute-start | bytes 786440 | tf_op jit(solution)/shard_map/ppermute | solution.py:55
  208.5 10.6 %collective-permute-start.38 = (bf16[128,1024]{1,0:T(8,128)(2,1)S(1)}, bf16[128,1024]{1,0:T(8,128)(2,1)S(1)}, u32[]{:S(2)}, u32[]{:S(2)}) collective-permute-start(bf16[128,1024]{1,0:T(8,128)(2,1)S(1)} %get-tuple-element.194), channel_id=1, source_target_pairs={{0,4},{4,8},{8,12},{12,14},{14,10},{10,6},{6,2},{2,0},{1,5},{5,9},... | collective-permute-start | bytes 786440 | tf_op jit(solution)/shard_map/ppermute | solution.py:55
  210.7 7.0 %collective-permute-start.42 = (bf16[128,1024]{1,0:T(8,128)(2,1)S(1)}, bf16[128,1024]{1,0:T(8,128)(2,1)S(1)}, u32[]{:S(2)}, u32[]{:S(2)}) collective-permute-start(bf16[128,1024]{1,0:T(8,128)(2,1)S(1)} %get-tuple-element.191), channel_id=1, source_target_pairs={{0,4},{4,8},{8,12},{12,14},{14,10},{10,6},{6,2},{2,0},{1,5},{5,9},... | collective-permute-start | bytes 786440 | tf_op jit(solution)/shard_map/ppermute | solution.py:55
  212.8 6.4 %collective-permute-start.43 = (bf16[128,1024]{1,0:T(8,128)(2,1)S(1)}, bf16[128,1024]{1,0:T(8,128)(2,1)S(1)}, u32[]{:S(2)}, u32[]{:S(2)}) collective-permute-start(bf16[128,1024]{1,0:T(8,128)(2,1)S(1)} %get-tuple-element.192), channel_id=1, source_target_pairs={{0,2},{4,0},{8,4},{12,8},{14,12},{10,14},{6,10},{2,6},{1,3},{5,1},... | collective-permute-start | bytes 786440 | tf_op jit(solution)/shard_map/ppermute | solution.py:55

commit v10 on v8

--- a/solution.py
+++ b/solution.py
@@ -210,7 +210,127 @@
     return out, (squares, counted | set(used))
 
 
-def down_kernel(start, steps, tiles_ref, hidden, local_ref, other_ref, out_ref, buffer, sems):
+def columns_kernel(columns, mean_of, fresh, blocks_ref, *refs):
+    refs = list(refs)
+    before_ref, out_ref, stat, stacked, sums, weights, sems, weight_sems = refs[-8:]
+    gains_ref = refs[-13]
+    own_and_other = refs[-12:-8:2], refs[-11:-8:2]
+    pieces = refs[:-13]
+    rows = stacked.shape[0]
+    count, width = gains_ref.shape[0], gains_ref.shape[2]
+    tile = weights.shape[-1]
+    step = pl.program_id(0)
+    height = width // 2
+
+    def fetch(number):
+        slot = lax.rem(number, DEEP)
+        begin = pl.multiple_of(blocks_ref[1, number] * width, width)
+        for other in range(2):
+
+            @pl.when(blocks_ref[0, number] == 1 - other)
+            def chosen(sources=own_and_other[other]):
+                for which, source in enumerate(sources):
+                    for part in range(2):
+                        pltpu.make_async_copy(
+                            source.at[pl.ds(begin + part * height, height), pl.ds(columns, tile)],
+                            weights.at[slot, which, pl.ds(part * height, height)],
+                            weight_sems.at[slot, which],
+                        ).start()
+
+    def gather_pieces(wanted, act):
+        start = 0
+        for number, source in enumerate(pieces):
+            size = source.shape[0]
+            if start // rows == wanted:
+                target = stacked.at[pl.ds(start % rows, size), pl.ds((start // rows) * width, width)]
+                act(pltpu.make_async_copy(source, target, sems.at[number]))
+            start += size
+
+    @pl.when(step == 0)
+    def first():
+        gather_pieces(0, lambda copy: copy.start())
+        for number in range(min(DEEP - 1, count)):
+            fetch(jnp.int32(number))
+        for wanted in range(1, count):
+            gather_pieces(wanted, lambda copy: copy.start())
+        sums[...] = jnp.zeros_like(sums)
+        stat[...] = before_ref[...]
+
+    @pl.when(step + DEEP - 1 < count)
+    def ahead():
+        fetch(step + DEEP - 1)
+
+    for wanted in range(count):
+
+        @pl.when(step == wanted)
+        def arrived(wanted=wanted):
+            gather_pieces(wanted, lambda copy: copy.wait())
+
+    slot = lax.rem(step, DEEP)
+    block = stacked[:, pl.ds(pl.multiple_of(step * width, width), width)]
+    if fresh:
+        gain = gains_ref[blocks_ref[2, step]]
+        weight = 1.0 / (gain * gain)
+        squares = stat[...]
+        for column in range(0, width, LANES):
+            value = block[:, column : column + LANES].astype(jnp.float32)
+            squares = squares + value * value * weight[:, column : column + LANES]
+        stat[...] = squares
+    for which in range(2):
+        sample = own_and_other[0][which].at[pl.ds(0, width), pl.ds(columns, tile)]
+        pltpu.make_async_copy(sample, weights.at[slot, which], weight_sems.at[slot, which]).wait()
+        sums[which] += jnp.dot(block, weights[slot, which], preferred_element_type=jnp.float32)
+
+    @pl.when(step == count - 1)
+    def activate():
+        inv = lax.rsqrt(jnp.sum(stat[...], axis=1, keepdims=True) / mean_of + 1e-05)
+        gate = sums[0] * inv
+        out_ref[...] = (gate / (1.0 + jnp.exp(-gate)) * (sums[1] * inv)).astype(jnp.bfloat16)
+
+
+def gate_up_columns(start, stop, squares, blocks, pieces, gains, weights):
+    sofar, counted = squares
+    rows, width = sofar.shape[0], pieces[0][0].shape[1]
+    count = blocks.shape[1]
+    columns = stop - start
+    pieces = [part for parts in pieces for part in parts]
+    anywhere = pl.BlockSpec(memory_space=pl.ANY)
+
+    def whole(*shape):
+        return pl.BlockSpec(shape, lambda n, blocks: (0,) * len(shape))
+
+    out, stat = pl.pallas_call(
+        functools.partial(columns_kernel, start, width * count, not counted),
+        out_shape=(
+            jax.ShapeDtypeStruct((rows, columns), jnp.bfloat16),
+            jax.ShapeDtypeStruct((rows, LANES), jnp.float32),
+        ),
+        grid_spec=pltpu.PrefetchScalarGridSpec(
+            num_scalar_prefetch=1,
+            grid=(count,),
+            in_specs=[*[anywhere] * len(pieces), whole(*gains.shape), *[anywhere] * 4, whole(rows, LANES)],
+            out_specs=(whole(rows, columns), whole(rows, LANES)),
+            scratch_shapes=[
+                pltpu.VMEM((rows, count * width), jnp.bfloat16),
+                pltpu.VMEM((2, rows, columns), jnp.float32),
+                pltpu.VMEM((DEEP, 2, width, columns), jnp.bfloat16),
+                pltpu.SemaphoreType.DMA((len(pieces),)),
+                pltpu.SemaphoreType.DMA((DEEP, 2)),
+            ],
+        ),
+        compiler_params=pltpu.CompilerParams(vmem_limit_bytes=VMEM_LIMIT),
+        cost_estimate=pl.CostEstimate(
+            flops=8 * rows * count * width * columns,
+            bytes_accessed=4 * count * width * columns,
+            transcendentals=rows * columns,
+        ),
+        name="gate_up",
+    )(blocks, *pieces, gains, *weights, sofar)
+    return out, (stat, frozenset(range(count)))
+
+
+def down_kernel(start, steps, tiles_ref, *refs):
+    local_ref, other_ref, out_ref, hidden, buffer, sems = refs[-6:]
     step = pl.program_id(0)
     depth, width = buffer.shape[1:]
 
@@ -231,6 +351,10 @@
     def first():
         for number in range(min(DEEP - 1, steps)):
             fetch(jnp.int32(number))
+        column = 0
+        for part_ref in refs[:-6]:
+            hidden[:, column : column + part_ref.shape[1]] = part_ref[...]
+            column += part_ref.shape[1]
 
     @pl.when(step + DEEP - 1 < steps)
     def ahead():
@@ -243,7 +367,8 @@
 
 
 def down(start, stop, tiles, hidden, local, other, width):
-    rows, depth = hidden.shape
+    rows, depth = hidden[0].shape[0], local.shape[0]
+    parts = [pl.BlockSpec(part.shape, lambda j, tiles: (0, 0)) for part in hidden]
     anywhere = pl.BlockSpec(memory_space=pl.ANY)
     return pl.pallas_call(
         functools.partial(down_kernel, start, stop - start),
@@ -251,9 +376,10 @@
         grid_spec=pltpu.PrefetchScalarGridSpec(
             num_scalar_prefetch=1,
             grid=(stop - start,),
-            in_specs=[pl.BlockSpec((rows, depth), lambda j, tiles: (0, 0)), anywhere, anywhere],
+            in_specs=[*parts, anywhere, anywhere],
             out_specs=pl.BlockSpec((1, rows, width), lambda j, tiles: (j, 0, 0)),
             scratch_shapes=[
+                pltpu.VMEM((rows, depth), jnp.bfloat16),
                 pltpu.VMEM((DEEP, depth, width), jnp.bfloat16),
                 pltpu.SemaphoreType.DMA((DEEP,)),
             ],
@@ -265,7 +391,7 @@
             transcendentals=0,
         ),
         name="down",
-    )(tiles, hidden, local, other)
+    )(tiles, *hidden, local, other)
 
 
 def gather_step(block, steps, half, *earlier):
@@ -324,10 +450,6 @@
     def mix(noisy, cond):
         return noisy.astype(jnp.float32) + cond_gain * cond.astype(jnp.float32)
 
-    edges = lax.ppermute(
-        mix(noisy_input[row_count - lead_rows :], self_cond[row_count - lead_rows :]), "seq", [(0, 1)]
-    )
-
     def convolve(noisy, cond, edge, start, size):
         if start == 0:
             extended = jnp.concatenate([edge, mix(noisy[:size], cond[:size])], axis=0)
@@ -344,11 +466,15 @@
     size = row_count // 2
     early = min(3, count - 1)
 
-    def matmul(units, final, partial, squares, block, steps, *earlier):
+    def pieces_of(block, steps):
         pieces = [[block]]
         for number, step in enumerate(steps):
             pieces += [[step[0]], [step[1]]] if number < half - 1 else [list(step)]
-        return gate_up(units, final, partial, squares, blocks, after(pieces, *earlier), gains, weights)
+        return pieces
+
+    def matmul(units, final, partial, squares, block, steps, *earlier):
+        pieces = after(pieces_of(block, steps), *earlier)
+        return gate_up(units, final, partial, squares, blocks, pieces, gains, weights)
 
     def units(which, start, stop):
         return [(which, block) for block in range(start, stop)]
@@ -367,11 +493,16 @@
         return term
 
     block_a = convolve(noisy_input, self_cond, None, size, size)
-    later = after((gate_weight, up_weight, down_weight), edges, block_a)
-    other_gate, other_up, other_down = (swap(weight) for weight in later)
-    weights = (gate_weight, other_gate, up_weight, other_up)
+    other_gate = swap(gate_weight)
+    edges = lax.ppermute(
+        mix(*after((noisy_input[row_count - lead_rows :], self_cond[row_count - lead_rows :]), block_a)),
+        "seq",
+        [(0, 1)],
+    )
     nothing = (jnp.zeros((size, LANES), jnp.float32), frozenset())
     steps_a = gather_step(block_a, [], half)
+    other_up, other_down = (swap(weight) for weight in after((up_weight, down_weight), steps_a[0]))
+    weights = (gate_weight, other_gate, up_weight, other_up)
     later = after((noisy_input, self_cond, edges), steps_a[0])
     block_b = convolve(*later, 0, size)
     while len(steps_a) < half - 1:
@@ -385,7 +516,7 @@
     first_b = steps_b[-1]
     steps_b = gather_step(block_b, steps_b, half, up_a, steps_a[-1])
     rest = units(0, near, count) + units(1, count - 1, count)
-    hidden_a, _ = matmul(rest, True, {0: gate_a, 1: up_a}, squares_a, block_a, steps_a, first_b)
+    hidden_a = [matmul(rest, True, {0: gate_a, 1: up_a}, squares_a, block_a, steps_a, first_b)[0]]
     second_b = steps_b[-1]
     steps_b = gather_step(block_b, steps_b, half, hidden_a)
     opened_a = open_down(hidden_a, second_b)
@@ -398,13 +529,19 @@
     distances = list(range(half - 1, 0, -1))
     moved_a = scatter_send(scatter_sums(None, term_a, count, half, third_b))
     sums_a = scatter_sums(moved_a, term_a, count, distances.pop(0))
-    gate_b, squares_b = matmul(units(0, 0, count), False, {}, nothing, block_b, steps_b, closed_a, sums_a)
-    sums_a = scatter_sums(scatter_send(sums_a), term_a, count, distances.pop(0))
-    hidden_b, _ = matmul(units(1, 0, count), True, {0: gate_b}, squares_b, block_b, steps_b, sums_a)
+    columns = gate_weight.shape[1]
+    cuts = [0, 768, 1536, 2048] if columns == 2048 else [0, columns // 2, columns]
+    hidden_b, squares_b = [], nothing
+    for first, last in zip(cuts, cuts[1:]):
+        pieces = after(pieces_of(block_b, steps_b), closed_a, sums_a, hidden_b)
+        part, squares_b = gate_up_columns(first, last, squares_b, blocks, pieces, gains, weights)
+        hidden_b.append(part)
+        if distances:
+            sums_a = scatter_sums(scatter_send(sums_a), term_a, count, distances.pop(0))
     for distance in distances:
         sums_a = scatter_sums(scatter_send(sums_a), term_a, count, distance)
-    opened_b = open_down(hidden_b, sums_a)
     moved_a = scatter_send(sums_a)
+    opened_b = open_down(hidden_b, moved_a)
     spans = [slice(0, size // 2), slice(size // 2, size)]
     distances = list(range(half, 0, -1))
     parts_b = [None, None]
@@ -413,8 +550,7 @@
     for number, distance in enumerate(distances):
         for which, span in enumerate(spans):
             moved = scatter_send(parts_b[which]) if number else None
-            tied = (earlier, moved_a)
-            parts_b[which] = scatter_sums(moved, term_of(opened_b, closed_b, span), count, distance, tied)
+            parts_b[which] = scatter_sums(moved, term_of(opened_b, closed_b, span), count, distance, earlier)
             earlier = parts_b[which]
         if number == 1:
             closed_b = close_down(hidden_b, parts_b)

time: 216 us -> 234 us (1.083)
  waiting for transfers between devices: 52.7 us -> 66 us
  Pallas kernels: 105 us -> 111 us
    pallas_call x0 -> x3, Pallas kernels: none -> 40.3 us  [gate_up_columns(): pl.pallas_call(functools.partial(columns_kernel, start, width * count, no...]
    pallas_call x5 -> x3, Pallas kernels: 72.5 us -> 38.3 us  [gate_up(): pl.pallas_call(functools.partial(gate_up_kernel, fixed), out_shape=(jax.S...]
    ppermute x1, waiting for transfers between devices: 0.01 us -> 22.3 us  [on_device(): lax.ppermute(mix(*after((noisy_input[row_count - lead_rows:], self_cond[r...]
    ppermute x40, waiting for transfers between devices: 52.5 us -> 43.6 us  [ring_shift(): lax.ppermute(value, 'blk', [(ring[i], ring[(i + steps) % count]) for i in...]
  transfers between devices with their start and end apart: 44 -> 44, of which waited for: 20 -> 12; matrix products, arithmetic and copies ran while one was open for 3% -> 4% of each run, Pallas kernels for 49% -> 45%
where the time goes in v10:
time: 234 us
  Pallas kernels  111 us (47%)
  waiting for transfers between devices  66 us (28%)
  starting transfers between devices  44.6 us (19%)
  other arithmetic  7.8 us (3%)
  local copies, waits for them, and re-layouts  3.29 us (1%)
    ppermute x40, waiting for transfers between devices, ring_shift(): lax.ppermute(value, 'blk', [(ring[i], ring[(i + steps) % count]) for i in...  43.6 us
    ppermute x40, starting transfers between devices, ring_shift(): lax.ppermute(value, 'blk', [(ring[i], ring[(i + steps) % count]) for i in...  41.7 us
    pallas_call x3, Pallas kernels, gate_up_columns(): pl.pallas_call(functools.partial(columns_kernel, start, width * count, no...  40.3 us
    pallas_call x3, Pallas kernels, gate_up(): pl.pallas_call(functools.partial(gate_up_kernel, fixed), out_shape=(jax.S...  38.3 us
    pallas_call x4, Pallas kernels, down(): pl.pallas_call(functools.partial(down_kernel, start, stop - start), out_s...  32 us
    ppermute x1, waiting for transfers between devices, on_device(): lax.ppermute(mix(*after((noisy_input[row_count - lead_rows:], self_cond[r...  22.3 us
  transfers between devices with their start and end apart: 44, of which 12 were waited for; matrix products, arithmetic and copies ran while one was open for 4% of the time, Pallas kernels for 45%

profile of v10, /device:TPU:0, one launch (start us, length us, event | category | flops | bytes accessed | tf_op | source)
XLA Modules:
  0.0 233.5 jit_solution(17961576216073677966)
XLA Ops:
  0.0 0.5 collective-permute-start.5
  1.1 0.7 dynamic_slice.12
  1.8 0.9 constant_dynamic-slice_fusion.2
  2.7 1.5 multiply_add_fusion
  4.2 0.5 multiply_convert_fusion.1.refs_0_
  4.8 2.6 %collective-permute-start.1 = (bf16[256,1024]{1,0:T(8,128)(2,1)S(1)}, bf16[256,1024]{1,0:T(8,128)(2,1)S(1)}, u32[]{:S(2)}, u32[]{:S(2)}) collective-permute-start(bf16[256,1024]{1,0:T(8,128)(2,1)S(1)} %multiply_convert_fusion.1.refs_0_), channel_id=1, source_target_pairs={{0,4},{4,8},{8,12},{12,14},{14,10},{10,6},{6,2},{2,0},{1,5},{5,9},... | collective-permute-start | bytes 1572872 | tf_op jit(solution)/shard_map/ppermute | solution.py:55
  7.4 12.5 %collective-permute-done.1.refs_1_ = bf16[256,1024]{1,0:T(8,128)(2,1)S(1)} collective-permute-done((bf16[256,1024]{1,0:T(8,128)(2,1)S(1)}, bf16[256,1024]{1,0:T(8,128)(2,1)S(1)}, u32[]{:S(2)}, u32[]{:S(2)}) %collective-permute-start.1) | collective-permute-done | bytes 524320 | tf_op jit(solution)/shard_map/ppermute | solution.py:55
  19.9 1.5 collective-permute-done.2.refs_2_
  21.4 0.5 collective-permute-start.17
  21.9 0.7 slice.315
  22.7 1.9 collective-permute-start
  24.6 0.7 dynamic-slice_bitcast_fusion
  25.4 1.6 collective-permute-start.3
  26.9 22.3 %collective-permute-done = f32[3,1024]{1,0:T(4,128)S(1)} collective-permute-done((f32[3,1024]{1,0:T(4,128)S(1)}, f32[3,1024]{1,0:T(4,128)S(1)}, u32[]{:S(2)}, u32[]{:S(2)}) %collective-permute-start) | collective-permute-done | bytes 12320 | tf_op jit(solution)/shard_map/ppermute | solution.py:497
  49.3 1.2 multiply_add_fusion.1
  50.5 0.5 multiply_convert_fusion.refs_0_
  51.0 12.5 %collective-permute-done.4.refs_4_ = bf16[256,1024]{1,0:T(8,128)(2,1)S(1)} collective-permute-done((bf16[256,1024]{1,0:T(8,128)(2,1)S(1)}, bf16[256,1024]{1,0:T(8,128)(2,1)S(1)}, u32[]{:S(2)}, u32[]{:S(2)}) %collective-permute-start.4) | collective-permute-done | bytes 524320 | tf_op jit(solution)/shard_map/ppermute | solution.py:55
  63.5 2.0 collective-permute-start.9
  65.6 12.0 %gate_up.6 = (f32[256,2048]{1,0:T(8,128)}, f32[256,128]{1,0:T(8,128)S(1)}) custom-call(s32[3,8]{1,0:T(4,128)S(1)} %get-tuple-element.257.blocks_ref, s32[5,5]{1,0:T(8,128)S(1)} %copy-done.3, bf16[256,1024]{1,0:T(8,128)(2,1)S(1)} %multiply_convert_fusion.1.refs_0_, bf16[256,1024]{1,0:T(8,128)(2,1)S(1)} %collective-permute-done.1.refs_1_, ...), custom_call_target="tpu_custom_call" | custom-call | flops 10737418240 | bytes 20971520 | tf_op jit(solution)/shard_map/gate_up/pallas_call | solution.py:181
  77.7 2.0 collective-permute-start.7
  79.9 2.0 collective-permute-start.12
  81.9 14.7 %gate_up.7 = (f32[256,2048]{1,0:T(8,128)}, f32[256,128]{1,0:T(8,128)S(1)}) custom-call(s32[3,8]{1,0:T(4,128)S(1)} %get-tuple-element.257.blocks_ref, s32[5,7]{1,0:T(8,128)S(1)} %copy-done.2, bf16[256,1024]{1,0:T(8,128)(2,1)S(1)} %multiply_convert_fusion.1.refs_0_, bf16[256,1024]{1,0:T(8,128)(2,1)S(1)} %collective-permute-done.1.refs_1_, ...), custom_call_target="tpu_custom_call" | custom-call | flops 15032385536 | bytes 29360128 | tf_op jit(solution)/shard_map/gate_up/pallas_call | solution.py:181
  96.8 2.0 collective-permute-start.14
  98.7 11.6 %gate_up.8 = (bf16[256,2048]{1,0:T(8,128)(2,1)S(1)}, f32[256,128]{1,0:T(8,128)}) custom-call(s32[3,8]{1,0:T(4,128)S(1)} %get-tuple-element.257.blocks_ref, s32[5,4]{1,0:T(8,128)S(1)} %copy-done.1, bf16[256,1024]{1,0:T(8,128)(2,1)S(1)} %collective-permute-done.8.refs_5_.refs_0_, bf16[256,1024]{1,0:T(8,128)(2,1)S(1)} %collective-permute-done.9.refs_6_.refs_1_, ...), custom_call_target="tpu_custom_call" | custom-call | flops 8589934592 | bytes 16777216 | tf_op jit(solution)/shard_map/gate_up/pallas_call | solution.py:181
  110.5 1.9 collective-permute-start.16
  112.4 6.7 %down.4 = bf16[3,256,1024]{2,1,0:T(8,128)(2,1)S(1)} custom-call(s32[3,8]{1,0:T(4,128)S(1)} %get-tuple-element.258.tiles_ref, bf16[256,2048]{1,0:T(8,128)(2,1)S(1)} %get-tuple-element.158.refs_0_, bf16[2048,4096]{1,0:T(8,128)(2,1)} %refs_3_.3, bf16[2048,4096]{1,0:T(8,128)(2,1)} %collective-permute-done.17.refs_2_.refs_4_), custom_call_target="tpu_custom_call" | custom-call | flops 6442450944 | bytes 12582912 | tf_op jit(solution)/shard_map/down/pallas_call | solution.py:373
  119.2 3.2 %collective-permute-done.15.refs_5_ = bf16[256,1024]{1,0:T(8,128)(2,1)S(1)} collective-permute-done((bf16[256,1024]{1,0:T(8,128)(2,1)S(1)}, bf16[256,1024]{1,0:T(8,128)(2,1)S(1)}, u32[]{:S(2)}, u32[]{:S(2)}) %collective-permute-start.15) | collective-permute-done | bytes 524320 | tf_op jit(solution)/shard_map/ppermute | solution.py:55
  122.5 2.1 collective-permute-start.19
  124.6 2.0 collective-permute-start.21
  126.6 9.3 %down.5 = bf16[5,256,1024]{2,1,0:T(8,128)(2,1)S(1)} custom-call(s32[3,8]{1,0:T(4,128)S(1)} %get-tuple-element.258.tiles_ref, bf16[256,2048]{1,0:T(8,128)(2,1)S(1)} %get-tuple-element.158.refs_0_, bf16[2048,4096]{1,0:T(8,128)(2,1)} %refs_3_.3, bf16[2048,4096]{1,0:T(8,128)(2,1)} %collective-permute-done.17.refs_2_.refs_4_), custom_call_target="tpu_custom_call" | custom-call | flops 10737418240 | bytes 20971520 | tf_op jit(solution)/shard_map/down/pallas_call | solution.py:373
  135.9 0.2 fusion.34
  136.2 1.7 collective-permute-start.23
  137.9 0.4 collective-permute-start.22
  138.4 15.4 %gate_up.9 = (bf16[256,768]{1,0:T(8,128)(2,1)S(1)}, f32[256,128]{1,0:T(8,128)S(1)}) custom-call(s32[3,8]{1,0:T(4,128)S(1)} %get-tuple-element.257.blocks_ref, bf16[256,1024]{1,0:T(8,128)(2,1)S(1)} %multiply_convert_fusion.refs_0_, bf16[256,1024]{1,0:T(8,128)(2,1)S(1)} %collective-permute-done.6.refs_1_, ...), custom_call_target="tpu_custom_call" | custom-call | flops 12884901888 | bytes 25165824 | tf_op jit(solution)/shard_map/gate_up/pallas_call | solution.py:302
  153.7 0.4 fusion.18
  154.2 2.0 collective-permute-start.25
  156.2 14.5 %gate_up.10 = (bf16[256,768]{1,0:T(8,128)(2,1)S(1)}, f32[256,128]{1,0:T(8,128)S(1)}) custom-call(s32[3,8]{1,0:T(4,128)S(1)} %get-tuple-element.257.blocks_ref, bf16[256,1024]{1,0:T(8,128)(2,1)S(1)} %multiply_convert_fusion.refs_0_, bf16[256,1024]{1,0:T(8,128)(2,1)S(1)} %collective-permute-done.6.refs_1_, ...), custom_call_target="tpu_custom_call" | custom-call | flops 12884901888 | bytes 25165824 | tf_op jit(solution)/shard_map/gate_up/pallas_call | solution.py:302
  170.8 0.4 fusion.17
  171.3 2.0 collective-permute-start.27
  173.3 10.4 %gate_up.11 = (bf16[256,512]{1,0:T(8,128)(2,1)S(1)}, f32[256,128]{1,0:T(8,128)}) custom-call(s32[3,8]{1,0:T(4,128)S(1)} %get-tuple-element.257.blocks_ref, bf16[256,1024]{1,0:T(8,128)(2,1)S(1)} %multiply_convert_fusion.refs_0_, bf16[256,1024]{1,0:T(8,128)(2,1)S(1)} %collective-permute-done.6.refs_1_, bf16[256,1024]{1,0:T(8,128)(2,1)S(1)} %collective-permute-done.7.refs_2_, ...), custom_call_target="tpu_custom_call" | custom-call | flops 8589934592 | bytes 16777216 | tf_op jit(solution)/shard_map/gate_up/pallas_call | solution.py:302
  183.7 6.7 %down.6 = bf16[3,256,1024]{2,1,0:T(8,128)(2,1)S(1)} custom-call(s32[3,8]{1,0:T(4,128)S(1)} %get-tuple-element.258.tiles_ref, bf16[256,768]{1,0:T(8,128)(2,1)S(1)} %get-tuple-element.210.refs_0_, bf16[256,768]{1,0:T(8,128)(2,1)S(1)} %get-tuple-element.211.refs_1_, bf16[256,512]{1,0:T(8,128)(2,1)S(1)} %get-tuple-element.212.refs_2_, ...), custom_call_target="tpu_custom_call" | custom-call | flops 6442450944 | bytes 12582912 | tf_op jit(solution)/shard_map/down/pallas_call | solution.py:373
  190.6 2.0 collective-permute-start.29
  192.7 2.0 collective-permute-start.31
  194.6 2.4 %collective-permute-done.28 = bf16[64,1024]{1,0:T(8,128)(2,1)S(1)} collective-permute-done((bf16[64,1024]{1,0:T(8,128)(2,1)S(1)}, bf16[64,1024]{1,0:T(8,128)(2,1)S(1)}, u32[]{:S(2)}, u32[]{:S(2)}) %collective-permute-start.28) | collective-permute-done | bytes 131104 | tf_op jit(solution)/shard_map/ppermute | solution.py:55
  197.2 1.7 collective-permute-start.33
  198.8 0.5 collective-permute-start.32
  199.3 0.5 collective-permute-done.30
  199.9 1.5 collective-permute-start.37
  201.5 0.6 collective-permute-start.36
  202.1 9.3 %down.7 = bf16[5,256,1024]{2,1,0:T(8,128)(2,1)S(1)} custom-call(s32[3,8]{1,0:T(4,128)S(1)} %get-tuple-element.258.tiles_ref, bf16[256,768]{1,0:T(8,128)(2,1)S(1)} %get-tuple-element.210.refs_0_, bf16[256,768]{1,0:T(8,128)(2,1)S(1)} %get-tuple-element.211.refs_1_, bf16[256,512]{1,0:T(8,128)(2,1)S(1)} %get-tuple-element.212.refs_2_, ...), custom_call_target="tpu_custom_call" | custom-call | flops 10737418240 | bytes 20971520 | tf_op jit(solution)/shard_map/down/pallas_call | solution.py:373
  211.4 0.2 fusion.28
  211.7 2.0 collective-permute-start.35
  214.0 1.9 collective-permute-start.41
  216.0 4.9 %collective-permute-done.34 = bf16[128,1024]{1,0:T(8,128)(2,1)S(1)} collective-permute-done((bf16[128,1024]{1,0:T(8,128)(2,1)S(1)}, bf16[128,1024]{1,0:T(8,128)(2,1)S(1)}, u32[]{:S(2)}, u32[]{:S(2)}) %collective-permute-start.34) | collective-permute-done | bytes 262176 | tf_op jit(solution)/shard_map/ppermute | solution.py:55
  221.1 0.4 collective-permute-start.38
  221.5 1.7 collective-permute-start.39
  223.2 1.7 collective-permute-done.40
  225.1 0.5 collective-permute-start.42
  225.6 1.6 collective-permute-start.43
  227.2 0.5 fusion.15
  227.7 3.8 %collective-permute-done.42 = bf16[128,1024]{1,0:T(8,128)(2,1)S(1)} collective-permute-done((bf16[128,1024]{1,0:T(8,128)(2,1)S(1)}, bf16[128,1024]{1,0:T(8,128)(2,1)S(1)}, u32[]{:S(2)}, u32[]{:S(2)}) %collective-permute-start.42) | collective-permute-done | bytes 262176 | tf_op jit(solution)/shard_map/ppermute | solution.py:55
  231.6 0.4 collective-permute-done.43
  232.0 0.5 fusion.33
  232.5 1.0 pad_maximum_fusion.1
  (91 shorter events, 2.5 us)
Async XLA Ops:
  0.0 65.5 %collective-permute-start.5 = (bf16[4096,2048]{1,0:T(8,128)(2,1)}, bf16[4096,2048]{1,0:T(8,128)(2,1)}, u32[]{:S(2)}, u32[]{:S(2)}) collective-permute-start(bf16[4096,2048]{1,0:T(8,128)(2,1)} %refs_10_.7), channel_id=1, source_target_pairs={{0,1},{1,0},{2,3},{3,2},{4,5},{5,4},{6,7},{7,6},{8,9},{9,8},{10,11... | collective-permute-start | bytes 50331656 | tf_op jit(solution)/shard_map/ppermute | solution.py:59
  4.2 18.5 %copy-start.6 = (bf16[512,1024]{1,0:T(8,128)(2,1)S(1)}, bf16[512,1024]{1,0:T(8,128)(2,1)}, u32[]{:S(2)}) copy-start(bf16[512,1024]{1,0:T(8,128)(2,1)} %param.14) | copy-start | bytes 3145732
  4.2 18.5 %copy-start.9 = (f32[1024]{0:T(1024)S(1)}, f32[1024]{0:T(1024)}, u32[]{:S(2)}) copy-start(f32[1024]{0:T(1024)} %param.15) | copy-start | bytes 12292
  4.7 60.8 %copy-start = (f32[8192]{0:T(1024)S(1)}, f32[8192]{0:T(1024)}, u32[]{:S(2)}) copy-start(f32[8192]{0:T(1024)} %param.18) | copy-start | bytes 98308
  4.7 60.8 %copy-start.3 = (s32[5,5]{1,0:T(8,128)S(1)}, s32[5,5]{1,0:T(8,128)}, u32[]{:S(2)}) copy-start(s32[5,5]{1,0:T(8,128)} %constant.34.clone.units_ref) | copy-start | bytes 304
  4.8 15.2 %collective-permute-start.1 = (bf16[256,1024]{1,0:T(8,128)(2,1)S(1)}, bf16[256,1024]{1,0:T(8,128)(2,1)S(1)}, u32[]{:S(2)}, u32[]{:S(2)}) collective-permute-start(bf16[256,1024]{1,0:T(8,128)(2,1)S(1)} %multiply_convert_fusion.1.refs_0_), channel_id=1, source_target_pairs={{0,4},{4,8},{8,12},{12,14},{14,10},{10,6},{6,2},{2,0},{1,5},{5,9},... | collective-permute-start | bytes 1572872 | tf_op jit(solution)/shard_map/ppermute | solution.py:55
  7.4 14.1 %collective-permute-start.2 = (bf16[256,1024]{1,0:T(8,128)(2,1)S(1)}, bf16[256,1024]{1,0:T(8,128)(2,1)S(1)}, u32[]{:S(2)}, u32[]{:S(2)}) collective-permute-start(bf16[256,1024]{1,0:T(8,128)(2,1)S(1)} %multiply_convert_fusion.1.refs_0_), channel_id=1, source_target_pairs={{0,2},{4,0},{8,4},{12,8},{14,12},{10,14},{6,10},{2,6},{1,3},{5,1},... | collective-permute-start | bytes 1572872 | tf_op jit(solution)/shard_map/ppermute | solution.py:55
  21.4 58.4 %collective-permute-start.10 = (bf16[4096,2048]{1,0:T(8,128)(2,1)}, bf16[4096,2048]{1,0:T(8,128)(2,1)}, u32[]{:S(2)}, u32[]{:S(2)}) collective-permute-start(bf16[4096,2048]{1,0:T(8,128)(2,1)} %refs_12_.5), channel_id=1, source_target_pairs={{0,1},{1,0},{2,3},{3,2},{4,5},{5,4},{6,7},{7,6},{8,9},{9,8},{10,11... | collective-permute-start | bytes 50331656 | tf_op jit(solution)/shard_map/ppermute | solution.py:59
  21.4 91.0 %collective-permute-start.17 = (bf16[2048,4096]{1,0:T(8,128)(2,1)}, bf16[2048,4096]{1,0:T(8,128)(2,1)}, u32[]{:S(2)}, u32[]{:S(2)}) collective-permute-start(bf16[2048,4096]{1,0:T(8,128)(2,1)} %refs_3_.3), channel_id=1, source_target_pairs={{0,1},{1,0},{2,3},{3,2},{4,5},{5,4},{6,7},{7,6},{8,9},{9,8},{10,11... | collective-permute-start | bytes 50331656 | tf_op jit(solution)/shard_map/ppermute | solution.py:59
  22.7 26.6 %collective-permute-start = (f32[3,1024]{1,0:T(4,128)S(1)}, f32[3,1024]{1,0:T(4,128)S(1)}, u32[]{:S(2)}, u32[]{:S(2)}) collective-permute-start(f32[3,1024]{1,0:T(4,128)S(1)} %multiply_add_fusion.2), channel_id=1, source_target_pairs={{0,1},{2,3},{4,5},{6,7},{8,9},{10,11},{12,13},{14,15},{16,17},{18,... | collective-permute-start | bytes 36872 | tf_op jit(solution)/shard_map/ppermute | solution.py:497
  25.4 25.6 %collective-permute-start.3 = (bf16[256,1024]{1,0:T(8,128)(2,1)S(1)}, bf16[256,1024]{1,0:T(8,128)(2,1)S(1)}, u32[]{:S(2)}, u32[]{:S(2)}) collective-permute-start(bf16[256,1024]{1,0:T(8,128)(2,1)S(1)} %collective-permute-done.1.refs_1_), channel_id=1, source_target_pairs={{0,4},{4,8},{8,12},{12,14},{14,10},{10,6},{6,2},{2,0},{1,5},{5,9},... | collective-permute-start | bytes 1572872 | tf_op jit(solution)/shard_map/ppermute | solution.py:55
  49.3 14.2 %collective-permute-start.4 = (bf16[256,1024]{1,0:T(8,128)(2,1)S(1)}, bf16[256,1024]{1,0:T(8,128)(2,1)S(1)}, u32[]{:S(2)}, u32[]{:S(2)}) collective-permute-start(bf16[256,1024]{1,0:T(8,128)(2,1)S(1)} %collective-permute-done.2.refs_2_), channel_id=1, source_target_pairs={{0,2},{4,0},{8,4},{12,8},{14,12},{10,14},{6,10},{2,6},{1,3},{5,1},... | collective-permute-start | bytes 1572872 | tf_op jit(solution)/shard_map/ppermute | solution.py:55
  63.5 14.1 %collective-permute-start.8 = (bf16[256,1024]{1,0:T(8,128)(2,1)S(1)}, bf16[256,1024]{1,0:T(8,128)(2,1)S(1)}, u32[]{:S(2)}, u32[]{:S(2)}) collective-permute-start(bf16[256,1024]{1,0:T(8,128)(2,1)S(1)} %collective-permute-done.3.refs_3_), channel_id=1, source_target_pairs={{0,4},{4,8},{8,12},{12,14},{14,10},{10,6},{6,2},{2,0},{1,5},{5,9},... | collective-permute-start | bytes 1572872 | tf_op jit(solution)/shard_map/ppermute | solution.py:55
  63.5 14.1 %collective-permute-start.9 = (bf16[256,1024]{1,0:T(8,128)(2,1)S(1)}, bf16[256,1024]{1,0:T(8,128)(2,1)S(1)}, u32[]{:S(2)}, u32[]{:S(2)}) collective-permute-start(bf16[256,1024]{1,0:T(8,128)(2,1)S(1)} %collective-permute-done.4.refs_4_), channel_id=1, source_target_pairs={{0,2},{4,0},{8,4},{12,8},{14,12},{10,14},{6,10},{2,6},{1,3},{5,1},... | collective-permute-start | bytes 1572872 | tf_op jit(solution)/shard_map/ppermute | solution.py:55
  65.5 16.3 %copy-start.2 = (s32[5,7]{1,0:T(8,128)S(1)}, s32[5,7]{1,0:T(8,128)}, u32[]{:S(2)}) copy-start(s32[5,7]{1,0:T(8,128)} %constant.35.clone.units_ref) | copy-start | bytes 424
  77.6 19.0 %collective-permute-start.6 = (bf16[256,1024]{1,0:T(8,128)(2,1)S(1)}, bf16[256,1024]{1,0:T(8,128)(2,1)S(1)}, u32[]{:S(2)}, u32[]{:S(2)}) collective-permute-start(bf16[256,1024]{1,0:T(8,128)(2,1)S(1)} %multiply_convert_fusion.refs_0_), channel_id=1, source_target_pairs={{0,4},{4,8},{8,12},{12,14},{14,10},{10,6},{6,2},{2,0},{1,5},{5,9},... | collective-permute-start | bytes 1572872 | tf_op jit(solution)/shard_map/ppermute | solution.py:55
  77.7 19.0 %collective-permute-start.7 = (bf16[256,1024]{1,0:T(8,128)(2,1)S(1)}, bf16[256,1024]{1,0:T(8,128)(2,1)S(1)}, u32[]{:S(2)}, u32[]{:S(2)}) collective-permute-start(bf16[256,1024]{1,0:T(8,128)(2,1)S(1)} %multiply_convert_fusion.refs_0_), channel_id=1, source_target_pairs={{0,2},{4,0},{8,4},{12,8},{14,12},{10,14},{6,10},{2,6},{1,3},{5,1},... | collective-permute-start | bytes 1572872 | tf_op jit(solution)/shard_map/ppermute | solution.py:55
  79.7 16.9 %collective-permute-start.11 = (bf16[128,1024]{1,0:T(8,128)(2,1)S(1)}, bf16[128,1024]{1,0:T(8,128)(2,1)S(1)}, u32[]{:S(2)}, u32[]{:S(2)}) collective-permute-start(bf16[128,1024]{1,0:T(8,128)(2,1)S(1)} %slice.331), channel_id=1, source_target_pairs={{0,4},{4,8},{8,12},{12,14},{14,10},{10,6},{6,2},{2,0},{1,5},{5,9},... | collective-permute-start | bytes 786440 | tf_op jit(solution)/shard_map/ppermute | solution.py:55
  79.9 16.8 %collective-permute-start.12 = (bf16[128,1024]{1,0:T(8,128)(2,1)S(1)}, bf16[128,1024]{1,0:T(8,128)(2,1)S(1)}, u32[]{:S(2)}, u32[]{:S(2)}) collective-permute-start(bf16[128,1024]{1,0:T(8,128)(2,1)S(1)} %slice.332), channel_id=1, source_target_pairs={{0,2},{4,0},{8,4},{12,8},{14,12},{10,14},{6,10},{2,6},{1,3},{5,1},... | collective-permute-start | bytes 786440 | tf_op jit(solution)/shard_map/ppermute | solution.py:55
  81.9 16.9 %copy-start.1 = (s32[5,4]{1,0:T(8,128)S(1)}, s32[5,4]{1,0:T(8,128)}, u32[]{:S(2)}) copy-start(s32[5,4]{1,0:T(8,128)} %constant.36.clone.units_ref) | copy-start | bytes 244
  96.7 13.6 %collective-permute-start.13 = (bf16[256,1024]{1,0:T(8,128)(2,1)S(1)}, bf16[256,1024]{1,0:T(8,128)(2,1)S(1)}, u32[]{:S(2)}, u32[]{:S(2)}) collective-permute-start(bf16[256,1024]{1,0:T(8,128)(2,1)S(1)} %collective-permute-done.6.refs_1_), channel_id=1, source_target_pairs={{0,4},{4,8},{8,12},{12,14},{14,10},{10,6},{6,2},{2,0},{1,5},{5,9},... | collective-permute-start | bytes 1572872 | tf_op jit(solution)/shard_map/ppermute | solution.py:55
  96.8 13.5 %collective-permute-start.14 = (bf16[256,1024]{1,0:T(8,128)(2,1)S(1)}, bf16[256,1024]{1,0:T(8,128)(2,1)S(1)}, u32[]{:S(2)}, u32[]{:S(2)}) collective-permute-start(bf16[256,1024]{1,0:T(8,128)(2,1)S(1)} %collective-permute-done.7.refs_2_), channel_id=1, source_target_pairs={{0,2},{4,0},{8,4},{12,8},{14,12},{10,14},{6,10},{2,6},{1,3},{5,1},... | collective-permute-start | bytes 1572872 | tf_op jit(solution)/shard_map/ppermute | solution.py:55
  110.3 12.0 %collective-permute-start.15 = (bf16[256,1024]{1,0:T(8,128)(2,1)S(1)}, bf16[256,1024]{1,0:T(8,128)(2,1)S(1)}, u32[]{:S(2)}, u32[]{:S(2)}) collective-permute-start(bf16[256,1024]{1,0:T(8,128)(2,1)S(1)} %collective-permute-done.13.refs_3_), channel_id=1, source_target_pairs={{0,4},{4,8},{8,12},{12,14},{14,10},{10,6},{6,2},{2,0},{1,5},{5,9},... | collective-permute-start | bytes 1572872 | tf_op jit(solution)/shard_map/ppermute | solution.py:55
  110.5 11.9 %collective-permute-start.16 = (bf16[256,1024]{1,0:T(8,128)(2,1)S(1)}, bf16[256,1024]{1,0:T(8,128)(2,1)S(1)}, u32[]{:S(2)}, u32[]{:S(2)}) collective-permute-start(bf16[256,1024]{1,0:T(8,128)(2,1)S(1)} %collective-permute-done.14.refs_4_), channel_id=1, source_target_pairs={{0,2},{4,0},{8,4},{12,8},{14,12},{10,14},{6,10},{2,6},{1,3},{5,1},... | collective-permute-start | bytes 1572872 | tf_op jit(solution)/shard_map/ppermute | solution.py:55
  122.4 13.5 %copy-start.4 = (bf16[256,1024]{1,0:T(8,128)(2,1)}, bf16[256,1024]{1,0:T(8,128)(2,1)S(1)}, u32[]{:S(2)}) copy-start(bf16[256,1024]{1,0:T(8,128)(2,1)S(1)} %collective-permute-done.15.refs_5_) | copy-start | bytes 1572868
  122.4 13.5 %copy-start.5 = (bf16[256,1024]{1,0:T(8,128)(2,1)}, bf16[256,1024]{1,0:T(8,128)(2,1)S(1)}, u32[]{:S(2)}) copy-start(bf16[256,1024]{1,0:T(8,128)(2,1)S(1)} %collective-permute-done.16.refs_6_) | copy-start | bytes 1572868
  122.4 16.0 %collective-permute-start.18 = (bf16[128,1024]{1,0:T(8,128)(2,1)S(1)}, bf16[128,1024]{1,0:T(8,128)(2,1)S(1)}, u32[]{:S(2)}, u32[]{:S(2)}) collective-permute-start(bf16[128,1024]{1,0:T(8,128)(2,1)S(1)} %slice.333), channel_id=1, source_target_pairs={{0,4},{4,8},{8,12},{12,14},{14,10},{10,6},{6,2},{2,0},{1,5},{5,9},... | collective-permute-start | bytes 786440 | tf_op jit(solution)/shard_map/ppermute | solution.py:55
  122.5 15.9 %collective-permute-start.19 = (bf16[128,1024]{1,0:T(8,128)(2,1)S(1)}, bf16[128,1024]{1,0:T(8,128)(2,1)S(1)}, u32[]{:S(2)}, u32[]{:S(2)}) collective-permute-start(bf16[128,1024]{1,0:T(8,128)(2,1)S(1)} %slice.334), channel_id=1, source_target_pairs={{0,2},{4,0},{8,4},{12,8},{14,12},{10,14},{6,10},{2,6},{1,3},{5,1},... | collective-permute-start | bytes 786440 | tf_op jit(solution)/shard_map/ppermute | solution.py:55
  124.5 11.4 %collective-permute-start.20 = (bf16[128,1024]{1,0:T(8,128)(2,1)S(1)}, bf16[128,1024]{1,0:T(8,128)(2,1)S(1)}, u32[]{:S(2)}, u32[]{:S(2)}) collective-permute-start(bf16[128,1024]{1,0:T(8,128)(2,1)S(1)} %get-tuple-element.159), channel_id=1, source_target_pairs={{0,4},{4,8},{8,12},{12,14},{14,10},{10,6},{6,2},{2,0},{1,5},{5,9},... | collective-permute-start | bytes 786440 | tf_op jit(solution)/shard_map/ppermute | solution.py:55
  124.6 11.4 %collective-permute-start.21 = (bf16[128,1024]{1,0:T(8,128)(2,1)S(1)}, bf16[128,1024]{1,0:T(8,128)(2,1)S(1)}, u32[]{:S(2)}, u32[]{:S(2)}) collective-permute-start(bf16[128,1024]{1,0:T(8,128)(2,1)S(1)} %get-tuple-element.160), channel_id=1, source_target_pairs={{0,2},{4,0},{8,4},{12,8},{14,12},{10,14},{6,10},{2,6},{1,3},{5,1},... | collective-permute-start | bytes 786440 | tf_op jit(solution)/shard_map/ppermute | solution.py:55
  136.2 17.5 %collective-permute-start.23 = (bf16[256,1024]{1,0:T(8,128)(2,1)S(1)}, bf16[256,1024]{1,0:T(8,128)(2,1)S(1)}, u32[]{:S(2)}, u32[]{:S(2)}) collective-permute-start(bf16[256,1024]{1,0:T(8,128)(2,1)S(1)} %pad_maximum_fusion.3), channel_id=1, source_target_pairs={{0,2},{4,0},{8,4},{12,8},{14,12},{10,14},{6,10},{2,6},{1,3},{5,1},... | collective-permute-start | bytes 1572872 | tf_op jit(solution)/shard_map/ppermute | solution.py:55
  137.9 15.8 %collective-permute-start.22 = (bf16[256,1024]{1,0:T(8,128)(2,1)S(1)}, bf16[256,1024]{1,0:T(8,128)(2,1)S(1)}, u32[]{:S(2)}, u32[]{:S(2)}) collective-permute-start(bf16[256,1024]{1,0:T(8,128)(2,1)S(1)} %pad_maximum_fusion.2), channel_id=1, source_target_pairs={{0,4},{4,8},{8,12},{12,14},{14,10},{10,6},{6,2},{2,0},{1,5},{5,9},... | collective-permute-start | bytes 1572872 | tf_op jit(solution)/shard_map/ppermute | solution.py:55
  154.2 16.6 %collective-permute-start.24 = (bf16[256,1024]{1,0:T(8,128)(2,1)S(1)}, bf16[256,1024]{1,0:T(8,128)(2,1)S(1)}, u32[]{:S(2)}, u32[]{:S(2)}) collective-permute-start(bf16[256,1024]{1,0:T(8,128)(2,1)S(1)} %get-tuple-element.234), channel_id=1, source_target_pairs={{0,4},{4,8},{8,12},{12,14},{14,10},{10,6},{6,2},{2,0},{1,5},{5,9},... | collective-permute-start | bytes 1572872 | tf_op jit(solution)/shard_map/ppermute | solution.py:55
  154.2 16.5 %collective-permute-start.25 = (bf16[256,1024]{1,0:T(8,128)(2,1)S(1)}, bf16[256,1024]{1,0:T(8,128)(2,1)S(1)}, u32[]{:S(2)}, u32[]{:S(2)}) collective-permute-start(bf16[256,1024]{1,0:T(8,128)(2,1)S(1)} %get-tuple-element.233), channel_id=1, source_target_pairs={{0,2},{4,0},{8,4},{12,8},{14,12},{10,14},{6,10},{2,6},{1,3},{5,1},... | collective-permute-start | bytes 1572872 | tf_op jit(solution)/shard_map/ppermute | solution.py:55
  171.2 12.5 %collective-permute-start.26 = (bf16[256,1024]{1,0:T(8,128)(2,1)S(1)}, bf16[256,1024]{1,0:T(8,128)(2,1)S(1)}, u32[]{:S(2)}, u32[]{:S(2)}) collective-permute-start(bf16[256,1024]{1,0:T(8,128)(2,1)S(1)} %get-tuple-element.231), channel_id=1, source_target_pairs={{0,4},{4,8},{8,12},{12,14},{14,10},{10,6},{6,2},{2,0},{1,5},{5,9},... | collective-permute-start | bytes 1572872 | tf_op jit(solution)/shard_map/ppermute | solution.py:55
  171.3 12.4 %collective-permute-start.27 = (bf16[256,1024]{1,0:T(8,128)(2,1)S(1)}, bf16[256,1024]{1,0:T(8,128)(2,1)S(1)}, u32[]{:S(2)}, u32[]{:S(2)}) collective-permute-start(bf16[256,1024]{1,0:T(8,128)(2,1)S(1)} %get-tuple-element.232), channel_id=1, source_target_pairs={{0,2},{4,0},{8,4},{12,8},{14,12},{10,14},{6,10},{2,6},{1,3},{5,1},... | collective-permute-start | bytes 1572872 | tf_op jit(solution)/shard_map/ppermute | solution.py:55
  190.5 6.5 %collective-permute-start.28 = (bf16[64,1024]{1,0:T(8,128)(2,1)S(1)}, bf16[64,1024]{1,0:T(8,128)(2,1)S(1)}, u32[]{:S(2)}, u32[]{:S(2)}) collective-permute-start(bf16[64,1024]{1,0:T(8,128)(2,1)S(1)} %get-tuple-element.202), channel_id=1, source_target_pairs={{0,4},{4,8},{8,12},{12,14},{14,10},{10,6},{6,2},{2,0},{1,5},{5,9},... | collective-permute-start | bytes 393224 | tf_op jit(solution)/shard_map/ppermute | solution.py:55
  190.6 6.4 %collective-permute-start.29 = (bf16[64,1024]{1,0:T(8,128)(2,1)S(1)}, bf16[64,1024]{1,0:T(8,128)(2,1)S(1)}, u32[]{:S(2)}, u32[]{:S(2)}) collective-permute-start(bf16[64,1024]{1,0:T(8,128)(2,1)S(1)} %get-tuple-element.203), channel_id=1, source_target_pairs={{0,2},{4,0},{8,4},{12,8},{14,12},{10,14},{6,10},{2,6},{1,3},{5,1},... | collective-permute-start | bytes 393224 | tf_op jit(solution)/shard_map/ppermute | solution.py:55
  192.6 7.2 %collective-permute-start.30 = (bf16[64,1024]{1,0:T(8,128)(2,1)S(1)}, bf16[64,1024]{1,0:T(8,128)(2,1)S(1)}, u32[]{:S(2)}, u32[]{:S(2)}) collective-permute-start(bf16[64,1024]{1,0:T(8,128)(2,1)S(1)} %get-tuple-element.204), channel_id=1, source_target_pairs={{0,4},{4,8},{8,12},{12,14},{14,10},{10,6},{6,2},{2,0},{1,5},{5,9},... | collective-permute-start | bytes 393224 | tf_op jit(solution)/shard_map/ppermute | solution.py:55
  192.7 7.2 %collective-permute-start.31 = (bf16[64,1024]{1,0:T(8,128)(2,1)S(1)}, bf16[64,1024]{1,0:T(8,128)(2,1)S(1)}, u32[]{:S(2)}, u32[]{:S(2)}) collective-permute-start(bf16[64,1024]{1,0:T(8,128)(2,1)S(1)} %get-tuple-element.205), channel_id=1, source_target_pairs={{0,2},{4,0},{8,4},{12,8},{14,12},{10,14},{6,10},{2,6},{1,3},{5,1},... | collective-permute-start | bytes 393224 | tf_op jit(solution)/shard_map/ppermute | solution.py:55
  197.2 14.2 %collective-permute-start.33 = (bf16[128,1024]{1,0:T(8,128)(2,1)S(1)}, bf16[128,1024]{1,0:T(8,128)(2,1)S(1)}, u32[]{:S(2)}, u32[]{:S(2)}) collective-permute-start(bf16[128,1024]{1,0:T(8,128)(2,1)S(1)} %pad_maximum_fusion.5), channel_id=1, source_target_pairs={{0,2},{4,0},{8,4},{12,8},{14,12},{10,14},{6,10},{2,6},{1,3},{5,1},... | collective-permute-start | bytes 786440 | tf_op jit(solution)/shard_map/ppermute | solution.py:55
  198.8 12.6 %collective-permute-start.32 = (bf16[128,1024]{1,0:T(8,128)(2,1)S(1)}, bf16[128,1024]{1,0:T(8,128)(2,1)S(1)}, u32[]{:S(2)}, u32[]{:S(2)}) collective-permute-start(bf16[128,1024]{1,0:T(8,128)(2,1)S(1)} %pad_maximum_fusion.4), channel_id=1, source_target_pairs={{0,4},{4,8},{8,12},{12,14},{14,10},{10,6},{6,2},{2,0},{1,5},{5,9},... | collective-permute-start | bytes 786440 | tf_op jit(solution)/shard_map/ppermute | solution.py:55
  199.9 13.8 %collective-permute-start.37 = (bf16[128,1024]{1,0:T(8,128)(2,1)S(1)}, bf16[128,1024]{1,0:T(8,128)(2,1)S(1)}, u32[]{:S(2)}, u32[]{:S(2)}) collective-permute-start(bf16[128,1024]{1,0:T(8,128)(2,1)S(1)} %pad_maximum_fusion.7), channel_id=1, source_target_pairs={{0,2},{4,0},{8,4},{12,8},{14,12},{10,14},{6,10},{2,6},{1,3},{5,1},... | collective-permute-start | bytes 786440 | tf_op jit(solution)/shard_map/ppermute | solution.py:55
  201.5 12.2 %collective-permute-start.36 = (bf16[128,1024]{1,0:T(8,128)(2,1)S(1)}, bf16[128,1024]{1,0:T(8,128)(2,1)S(1)}, u32[]{:S(2)}, u32[]{:S(2)}) collective-permute-start(bf16[128,1024]{1,0:T(8,128)(2,1)S(1)} %pad_maximum_fusion.6), channel_id=1, source_target_pairs={{0,4},{4,8},{8,12},{12,14},{14,10},{10,6},{6,2},{2,0},{1,5},{5,9},... | collective-permute-start | bytes 786440 | tf_op jit(solution)/shard_map/ppermute | solution.py:55
  211.6 9.3 %collective-permute-start.34 = (bf16[128,1024]{1,0:T(8,128)(2,1)S(1)}, bf16[128,1024]{1,0:T(8,128)(2,1)S(1)}, u32[]{:S(2)}, u32[]{:S(2)}) collective-permute-start(bf16[128,1024]{1,0:T(8,128)(2,1)S(1)} %get-tuple-element.230), channel_id=1, source_target_pairs={{0,4},{4,8},{8,12},{12,14},{14,10},{10,6},{6,2},{2,0},{1,5},{5,9},... | collective-permute-start | bytes 786440 | tf_op jit(solution)/shard_map/ppermute | solution.py:55
  211.7 15.5 %copy-start.7 = (bf16[512,1024]{1,0:T(8,128)(2,1)S(1)}, bf16[512,1024]{1,0:T(8,128)(2,1)}, u32[]{:S(2)}) copy-start(bf16[512,1024]{1,0:T(8,128)(2,1)} %param.14) | copy-start | bytes 3145732
  211.7 15.5 %copy-start.8 = (bf16[512,1024]{1,0:T(8,128)(2,1)S(1)}, bf16[512,1024]{1,0:T(8,128)(2,1)}, u32[]{:S(2)}) copy-start(bf16[512,1024]{1,0:T(8,128)(2,1)} %param.13) | copy-start | bytes 3145732
  211.7 15.5 %copy-start.10 = (f32[1024]{0:T(1024)S(1)}, f32[1024]{0:T(1024)}, u32[]{:S(2)}) copy-start(f32[1024]{0:T(1024)} %param.15) | copy-start | bytes 12292
  211.7 9.2 %collective-permute-start.35 = (bf16[128,1024]{1,0:T(8,128)(2,1)S(1)}, bf16[128,1024]{1,0:T(8,128)(2,1)S(1)}, u32[]{:S(2)}, u32[]{:S(2)}) collective-permute-start(bf16[128,1024]{1,0:T(8,128)(2,1)S(1)} %get-tuple-element.229), channel_id=1, source_target_pairs={{0,2},{4,0},{8,4},{12,8},{14,12},{10,14},{6,10},{2,6},{1,3},{5,1},... | collective-permute-start | bytes 786440 | tf_op jit(solution)/shard_map/ppermute | solution.py:55
  213.9 11.0 %collective-permute-start.40 = (bf16[128,1024]{1,0:T(8,128)(2,1)S(1)}, bf16[128,1024]{1,0:T(8,128)(2,1)S(1)}, u32[]{:S(2)}, u32[]{:S(2)}) collective-permute-start(bf16[128,1024]{1,0:T(8,128)(2,1)S(1)} %get-tuple-element.228), channel_id=1, source_target_pairs={{0,4},{4,8},{8,12},{12,14},{14,10},{10,6},{6,2},{2,0},{1,5},{5,9},... | collective-permute-start | bytes 786440 | tf_op jit(solution)/shard_map/ppermute | solution.py:55
  214.0 10.9 %collective-permute-start.41 = (bf16[128,1024]{1,0:T(8,128)(2,1)S(1)}, bf16[128,1024]{1,0:T(8,128)(2,1)S(1)}, u32[]{:S(2)}, u32[]{:S(2)}) collective-permute-start(bf16[128,1024]{1,0:T(8,128)(2,1)S(1)} %get-tuple-element.227), channel_id=1, source_target_pairs={{0,2},{4,0},{8,4},{12,8},{14,12},{10,14},{6,10},{2,6},{1,3},{5,1},... | collective-permute-start | bytes 786440 | tf_op jit(solution)/shard_map/ppermute | solution.py:55
  221.1 10.9 %collective-permute-start.38 = (bf16[128,1024]{1,0:T(8,128)(2,1)S(1)}, bf16[128,1024]{1,0:T(8,128)(2,1)S(1)}, u32[]{:S(2)}, u32[]{:S(2)}) collective-permute-start(bf16[128,1024]{1,0:T(8,128)(2,1)S(1)} %get-tuple-element.226), channel_id=1, source_target_pairs={{0,4},{4,8},{8,12},{12,14},{14,10},{10,6},{6,2},{2,0},{1,5},{5,9},... | collective-permute-start | bytes 786440 | tf_op jit(solution)/shard_map/ppermute | solution.py:55
  221.5 10.5 %collective-permute-start.39 = (bf16[128,1024]{1,0:T(8,128)(2,1)S(1)}, bf16[128,1024]{1,0:T(8,128)(2,1)S(1)}, u32[]{:S(2)}, u32[]{:S(2)}) collective-permute-start(bf16[128,1024]{1,0:T(8,128)(2,1)S(1)} %get-tuple-element.225), channel_id=1, source_target_pairs={{0,2},{4,0},{8,4},{12,8},{14,12},{10,14},{6,10},{2,6},{1,3},{5,1},... | collective-permute-start | bytes 786440 | tf_op jit(solution)/shard_map/ppermute | solution.py:55
  225.1 6.4 %collective-permute-start.42 = (bf16[128,1024]{1,0:T(8,128)(2,1)S(1)}, bf16[128,1024]{1,0:T(8,128)(2,1)S(1)}, u32[]{:S(2)}, u32[]{:S(2)}) collective-permute-start(bf16[128,1024]{1,0:T(8,128)(2,1)S(1)} %get-tuple-element.223), channel_id=1, source_target_pairs={{0,4},{4,8},{8,12},{12,14},{14,10},{10,6},{6,2},{2,0},{1,5},{5,9},... | collective-permute-start | bytes 786440 | tf_op jit(solution)/shard_map/ppermute | solution.py:55
  225.6 6.4 %collective-permute-start.43 = (bf16[128,1024]{1,0:T(8,128)(2,1)S(1)}, bf16[128,1024]{1,0:T(8,128)(2,1)S(1)}, u32[]{:S(2)}, u32[]{:S(2)}) collective-permute-start(bf16[128,1024]{1,0:T(8,128)(2,1)S(1)} %get-tuple-element.224), channel_id=1, source_target_pairs={{0,2},{4,0},{8,4},{12,8},{14,12},{10,14},{6,10},{2,6},{1,3},{5,1},... | collective-permute-start | bytes 786440 | tf_op jit(solution)/shard_map/ppermute | solution.py:55

commit v11 on v10

--- a/solution.py
+++ b/solution.py
@@ -8,7 +8,8 @@
 from jax.experimental.pallas import tpu as pltpu
 from jax.sharding import PartitionSpec as P
 
-VMEM_LIMIT = 50 * 1024 * 1024
+GATE_UP_VMEM = 62 * 1024 * 1024
+DOWN_VMEM = 50 * 1024 * 1024
 DEEP, PARTS = 3, 4
 LANES = 128
 
@@ -199,7 +200,7 @@
                 pltpu.SemaphoreType.DMA((DEEP,)),
             ],
         ),
-        compiler_params=pltpu.CompilerParams(vmem_limit_bytes=VMEM_LIMIT),
+        compiler_params=pltpu.CompilerParams(vmem_limit_bytes=GATE_UP_VMEM),
         cost_estimate=pl.CostEstimate(
             flops=4 * rows * width * columns * len(units),
             bytes_accessed=2 * width * columns * len(units),
@@ -318,7 +319,7 @@
                 pltpu.SemaphoreType.DMA((DEEP, 2)),
             ],
         ),
-        compiler_params=pltpu.CompilerParams(vmem_limit_bytes=VMEM_LIMIT),
+        compiler_params=pltpu.CompilerParams(vmem_limit_bytes=GATE_UP_VMEM),
         cost_estimate=pl.CostEstimate(
             flops=8 * rows * count * width * columns,
             bytes_accessed=4 * count * width * columns,
@@ -384,7 +385,7 @@
                 pltpu.SemaphoreType.DMA((DEEP,)),
             ],
         ),
-        compiler_params=pltpu.CompilerParams(vmem_limit_bytes=VMEM_LIMIT),
+        compiler_params=pltpu.CompilerParams(vmem_limit_bytes=DOWN_VMEM),
         cost_estimate=pl.CostEstimate(
             flops=4 * rows * depth * width * (stop - start),
             bytes_accessed=2 * depth * width * (stop - start),
@@ -450,6 +451,10 @@
     def mix(noisy, cond):
         return noisy.astype(jnp.float32) + cond_gain * cond.astype(jnp.float32)
 
+    edges = lax.ppermute(
+        mix(noisy_input[row_count - lead_rows :], self_cond[row_count - lead_rows :]), "seq", [(0, 1)]
+    )
+
     def convolve(noisy, cond, edge, start, size):
         if start == 0:
             extended = jnp.concatenate([edge, mix(noisy[:size], cond[:size])], axis=0)
@@ -493,16 +498,11 @@
         return term
 
     block_a = convolve(noisy_input, self_cond, None, size, size)
-    other_gate = swap(gate_weight)
-    edges = lax.ppermute(
-        mix(*after((noisy_input[row_count - lead_rows :], self_cond[row_count - lead_rows :]), block_a)),
-        "seq",
-        [(0, 1)],
-    )
+    later = after((gate_weight, up_weight, down_weight), edges, block_a)
+    other_gate, other_up, other_down = (swap(weight) for weight in later)
+    weights = (gate_weight, other_gate, up_weight, other_up)
     nothing = (jnp.zeros((size, LANES), jnp.float32), frozenset())
     steps_a = gather_step(block_a, [], half)
-    other_up, other_down = (swap(weight) for weight in after((up_weight, down_weight), steps_a[0]))
-    weights = (gate_weight, other_gate, up_weight, other_up)
     later = after((noisy_input, self_cond, edges), steps_a[0])
     block_b = convolve(*later, 0, size)
     while len(steps_a) < half - 1:
@@ -530,18 +530,16 @@
     moved_a = scatter_send(scatter_sums(None, term_a, count, half, third_b))
     sums_a = scatter_sums(moved_a, term_a, count, distances.pop(0))
     columns = gate_weight.shape[1]
-    cuts = [0, 768, 1536, 2048] if columns == 2048 else [0, columns // 2, columns]
     hidden_b, squares_b = [], nothing
-    for first, last in zip(cuts, cuts[1:]):
+    for first in (0, columns // 2):
         pieces = after(pieces_of(block_b, steps_b), closed_a, sums_a, hidden_b)
-        part, squares_b = gate_up_columns(first, last, squares_b, blocks, pieces, gains, weights)
+        part, squares_b = gate_up_columns(first, first + columns // 2, squares_b, blocks, pieces, gains, weights)
         hidden_b.append(part)
-        if distances:
-            sums_a = scatter_sums(scatter_send(sums_a), term_a, count, distances.pop(0))
+        sums_a = scatter_sums(scatter_send(sums_a), term_a, count, distances.pop(0))
     for distance in distances:
         sums_a = scatter_sums(scatter_send(sums_a), term_a, count, distance)
+    opened_b = open_down(hidden_b, sums_a)
     moved_a = scatter_send(sums_a)
-    opened_b = open_down(hidden_b, moved_a)
     spans = [slice(0, size // 2), slice(size // 2, size)]
     distances = list(range(half, 0, -1))
     parts_b = [None, None]
@@ -550,7 +548,8 @@
     for number, distance in enumerate(distances):
         for which, span in enumerate(spans):
             moved = scatter_send(parts_b[which]) if number else None
-            parts_b[which] = scatter_sums(moved, term_of(opened_b, closed_b, span), count, distance, earlier)
+            tied = (earlier, moved_a)
+            parts_b[which] = scatter_sums(moved, term_of(opened_b, closed_b, span), count, distance, tied)
             earlier = parts_b[which]
         if number == 1:
             closed_b = close_down(hidden_b, parts_b)

time: 234 us -> 229 us (0.979)
  waiting for transfers between devices: 66 us -> 46.5 us
  local copies, waits for them, and re-layouts: 3.29 us -> 10.4 us
  other arithmetic: 7.8 us -> 12.5 us
    ppermute x1, waiting for transfers between devices: 22.3 us -> 0.01 us  [on_device(): lax.ppermute(mix(noisy_input[row_count - lead_rows:], self_cond[row_count...]
    pallas_call x3, Pallas kernels: 38.3 us -> 44.6 us  [gate_up(): pl.pallas_call(functools.partial(gate_up_kernel, fixed), out_shape=(jax.S...]
    unnamed x22 -> x46, local copies, waits for them, and re-layouts: 0.05 us -> 4.25 us
    pallas_call x3 -> x2, Pallas kernels: 40.3 us -> 36.5 us  [gate_up_columns(): pl.pallas_call(functools.partial(columns_kernel, start, width * count, no...]
    convert_element_type x9, other arithmetic: 1.9 us -> 4.84 us  [joined(): (one.astype(jnp.float32) + two.astype(jnp.float32)).astype(jnp.bfloat16)]
    ppermute x40, waiting for transfers between devices: 43.6 us -> 46.5 us  [ring_shift(): lax.ppermute(value, 'blk', [(ring[i], ring[(i + steps) % count]) for i in...]
    slice x4, local copies, waits for them, and re-layouts: 0.07 us -> 2.46 us  [gather_step(): before, behind = (before[:cut], behind[cut:])]
  transfers between devices with their start and end apart: 44 -> 44, of which waited for: 12 -> 16; matrix products, arithmetic and copies ran while one was open for 4% -> 5% of each run, Pallas kernels for 45% -> 50%
where the time goes in v11:
time: 229 us; the launch traced here: 228 us
  Pallas kernels  113 us (49%)
  waiting for transfers between devices  46.5 us (20%)
  starting transfers between devices  44.5 us (19%)
  other arithmetic  12.5 us (5%)
  local copies, waits for them, and re-layouts  10.4 us (5%)
    ppermute x40, waiting for transfers between devices, ring_shift(): lax.ppermute(value, 'blk', [(ring[i], ring[(i + steps) % count]) for i in...  46.5 us
    pallas_call x3, Pallas kernels, gate_up(): pl.pallas_call(functools.partial(gate_up_kernel, fixed), out_shape=(jax.S...  44.6 us
    ppermute x40, starting transfers between devices, ring_shift(): lax.ppermute(value, 'blk', [(ring[i], ring[(i + steps) % count]) for i in...  41.5 us
    pallas_call x2, Pallas kernels, gate_up_columns(): pl.pallas_call(functools.partial(columns_kernel, start, width * count, no...  36.5 us
    pallas_call x4, Pallas kernels, down(): pl.pallas_call(functools.partial(down_kernel, start, stop - start), out_s...  32 us
    convert_element_type x9, other arithmetic, joined(): (one.astype(jnp.float32) + two.astype(jnp.float32)).astype(jnp.bfloat16)  4.84 us
  transfers between devices with their start and end apart: 44, of which 16 were waited for; matrix products, arithmetic and copies ran while one was open for 5% of the time, Pallas kernels for 50%

profile of v11, /device:TPU:0, one launch (start us, length us, event | category | flops | bytes accessed | tf_op | source)
XLA Modules:
  0.0 228.3 jit_solution(17816403265895452578)
XLA Ops:
  0.0 0.8 multiply_add_fusion.2
  0.8 2.4 %collective-permute-start = (f32[3,1024]{1,0:T(4,128)S(1)}, f32[3,1024]{1,0:T(4,128)S(1)}, u32[]{:S(2)}, u32[]{:S(2)}) collective-permute-start(f32[3,1024]{1,0:T(4,128)S(1)} %multiply_add_fusion.2), channel_id=1, source_target_pairs={{0,1},{2,3},{4,5},{6,7},{8,9},{10,11},{12,13},{14,15},{16,17},{18,... | collective-permute-start | bytes 36872 | tf_op jit(solution)/shard_map/ppermute | solution.py:454
  3.1 1.5 multiply_add_fusion
  5.3 0.7 dynamic_slice.12
  6.0 0.9 constant_dynamic-slice_fusion.2
  8.1 2.4 %collective-permute-start.1 = (bf16[256,1024]{1,0:T(8,128)(2,1)S(1)}, bf16[256,1024]{1,0:T(8,128)(2,1)S(1)}, u32[]{:S(2)}, u32[]{:S(2)}) collective-permute-start(bf16[256,1024]{1,0:T(8,128)(2,1)S(1)} %multiply_convert_fusion.1.refs_0_), channel_id=1, source_target_pairs={{0,4},{4,8},{8,12},{12,14},{14,10},{10,6},{6,2},{2,0},{1,5},{5,9},... | collective-permute-start | bytes 1572872 | tf_op jit(solution)/shard_map/ppermute | solution.py:56
  10.5 1.3 dynamic-slice_bitcast_fusion
  11.8 11.2 %collective-permute-done.1.refs_1_ = bf16[256,1024]{1,0:T(8,128)(2,1)S(1)} collective-permute-done((bf16[256,1024]{1,0:T(8,128)(2,1)S(1)}, bf16[256,1024]{1,0:T(8,128)(2,1)S(1)}, u32[]{:S(2)}, u32[]{:S(2)}) %collective-permute-start.1) | collective-permute-done | bytes 524320 | tf_op jit(solution)/shard_map/ppermute | solution.py:56
  23.0 1.5 collective-permute-done.2.refs_2_
  24.5 1.6 collective-permute-start.3
  26.5 1.2 multiply_add_fusion.1
  28.3 9.5 %collective-permute-done.3.refs_3_ = bf16[256,1024]{1,0:T(8,128)(2,1)} collective-permute-done((bf16[256,1024]{1,0:T(8,128)(2,1)S(1)}, bf16[256,1024]{1,0:T(8,128)(2,1)}, u32[]{:S(2)}, u32[]{:S(2)}) %collective-permute-start.3) | collective-permute-done | bytes 524320 | tf_op jit(solution)/shard_map/ppermute | solution.py:56
  37.8 1.3 collective-permute-done.4.refs_4_
  39.1 1.6 collective-permute-start.8
  41.1 0.7 broadcast_in_dim.2.refs_10_.refs_14_
  41.8 14.7 %gate_up.5 = (f32[256,2048]{1,0:T(8,128)}, f32[256,128]{1,0:T(8,128)}) custom-call(s32[3,8]{1,0:T(4,128)} %get-tuple-element.229.blocks_ref, s32[5,5]{1,0:T(8,128)} %constant.34.clone.units_ref, bf16[256,1024]{1,0:T(8,128)(2,1)} %copy-done.6, bf16[256,1024]{1,0:T(8,128)(2,1)} %copy-done.16, bf16[256,1024]{1,0:T(8,128)(2,1)} %copy-done.17, ...), custom_call_target="tpu_custom_call" | custom-call | flops 10737418240 | bytes 20971520 | tf_op jit(solution)/shard_map/gate_up/pallas_call | solution.py:182
  56.4 0.8 slice.331
  57.2 1.7 slice.332
  59.4 1.6 collective-permute-start.11
  60.9 1.6 collective-permute-start.6
  62.9 16.4 %gate_up.6 = (f32[256,2048]{1,0:T(8,128)}, f32[256,128]{1,0:T(8,128)}) custom-call(s32[3,8]{1,0:T(4,128)} %get-tuple-element.229.blocks_ref, s32[5,7]{1,0:T(8,128)} %constant.35.clone.units_ref, bf16[256,1024]{1,0:T(8,128)(2,1)} %copy-done.6, bf16[256,1024]{1,0:T(8,128)(2,1)} %copy-done.16, bf16[256,1024]{1,0:T(8,128)(2,1)} %copy-done.17, ...), custom_call_target="tpu_custom_call" | custom-call | flops 15032385536 | bytes 29360128 | tf_op jit(solution)/shard_map/gate_up/pallas_call | solution.py:182
  79.4 1.6 collective-permute-start.13
  81.5 13.6 %gate_up.7 = (bf16[256,2048]{1,0:T(8,128)(2,1)}, f32[256,128]{1,0:T(8,128)}) custom-call(s32[3,8]{1,0:T(4,128)} %get-tuple-element.229.blocks_ref, s32[5,4]{1,0:T(8,128)} %constant.36.clone.units_ref, bf16[256,1024]{1,0:T(8,128)(2,1)} %copy-done.12, bf16[256,1024]{1,0:T(8,128)(2,1)} %collective-permute-done.9.refs_6_.refs_1_, ...), custom_call_target="tpu_custom_call" | custom-call | flops 8589934592 | bytes 16777216 | tf_op jit(solution)/shard_map/gate_up/pallas_call | solution.py:182
  95.1 1.6 collective-permute-start.15
  97.2 1.2 copy-done.1
  98.4 6.7 %down.4 = bf16[3,256,1024]{2,1,0:T(8,128)(2,1)S(1)} custom-call(s32[3,8]{1,0:T(4,128)S(1)} %get-tuple-element.230.tiles_ref, bf16[256,2048]{1,0:T(8,128)(2,1)S(1)} %copy-done.1, bf16[2048,4096]{1,0:T(8,128)(2,1)} %refs_2_.3, bf16[2048,4096]{1,0:T(8,128)(2,1)} %collective-permute-done.17.refs_2_.refs_3_), custom_call_target="tpu_custom_call" | custom-call | flops 6442450944 | bytes 12582912 | tf_op jit(solution)/shard_map/down/pallas_call | solution.py:374
  105.2 3.5 %collective-permute-done.16.refs_6_ = bf16[256,1024]{1,0:T(8,128)(2,1)S(1)} collective-permute-done((bf16[256,1024]{1,0:T(8,128)(2,1)S(1)}, bf16[256,1024]{1,0:T(8,128)(2,1)S(1)}, u32[]{:S(2)}, u32[]{:S(2)}) %collective-permute-start.16) | collective-permute-done | bytes 524320 | tf_op jit(solution)/shard_map/ppermute | solution.py:56
  108.8 2.0 collective-permute-start.18
  110.8 1.5 collective-permute-start.20
  112.9 9.3 %down.5 = bf16[5,256,1024]{2,1,0:T(8,128)(2,1)S(1)} custom-call(s32[3,8]{1,0:T(4,128)S(1)} %get-tuple-element.230.tiles_ref, bf16[256,2048]{1,0:T(8,128)(2,1)S(1)} %copy-done.2, bf16[2048,4096]{1,0:T(8,128)(2,1)} %refs_2_.3, bf16[2048,4096]{1,0:T(8,128)(2,1)} %collective-permute-done.17.refs_2_.refs_3_), custom_call_target="tpu_custom_call" | custom-call | flops 10737418240 | bytes 20971520 | tf_op jit(solution)/shard_map/down/pallas_call | solution.py:374
  122.2 1.5 copy-done
  124.0 1.6 collective-permute-start.22
  126.2 0.7 copy-done.18
  126.9 0.7 copy-done.19
  127.6 18.7 %gate_up.8 = (bf16[256,1024]{1,0:T(8,128)(2,1)}, f32[256,128]{1,0:T(8,128)}) custom-call(s32[3,8]{1,0:T(4,128)} %get-tuple-element.229.blocks_ref, bf16[256,1024]{1,0:T(8,128)(2,1)} %copy-done.5, bf16[256,1024]{1,0:T(8,128)(2,1)} %copy-done.13, bf16[256,1024]{1,0:T(8,128)(2,1)} %collective-permute-done.7.refs_2_, bf16[256,1024]{1,0:T(8,128)(2,1)} %copy-done.14, ...), custom_call_target="tpu_custom_call" | custom-call | flops 17179869184 | bytes 33554432 | tf_op jit(solution)/shard_map/gate_up/pallas_call | solution.py:303
  146.3 1.9 fusion.18
  148.3 2.0 collective-permute-start.24
  150.3 17.7 %gate_up.9 = (bf16[256,1024]{1,0:T(8,128)(2,1)}, f32[256,128]{1,0:T(8,128)}) custom-call(s32[3,8]{1,0:T(4,128)} %get-tuple-element.229.blocks_ref, bf16[256,1024]{1,0:T(8,128)(2,1)} %copy-done.5, bf16[256,1024]{1,0:T(8,128)(2,1)} %copy-done.13, bf16[256,1024]{1,0:T(8,128)(2,1)} %collective-permute-done.7.refs_2_, bf16[256,1024]{1,0:T(8,128)(2,1)} %copy-done.14, ...), custom_call_target="tpu_custom_call" | custom-call | flops 17179869184 | bytes 33554432 | tf_op jit(solution)/shard_map/gate_up/pallas_call | solution.py:303
  168.1 1.8 fusion.17
  170.0 1.6 collective-permute-start.26
  172.1 6.7 %down.6 = bf16[3,256,1024]{2,1,0:T(8,128)(2,1)S(1)} custom-call(s32[3,8]{1,0:T(4,128)S(1)} %get-tuple-element.230.tiles_ref, bf16[256,1024]{1,0:T(8,128)(2,1)S(1)} %copy-done.3, bf16[256,1024]{1,0:T(8,128)(2,1)S(1)} %copy-done.4, bf16[2048,4096]{1,0:T(8,128)(2,1)} %refs_2_.3, bf16[2048,4096]{1,0:T(8,128)(2,1)} %collective-permute-done.17.refs_2_.refs_3_), custom_call_target="tpu_custom_call" | custom-call | flops 6442450944 | bytes 12582912 | tf_op jit(solution)/shard_map/down/pallas_call | solution.py:374
  178.8 1.7 collective-permute-done.26
  180.6 1.5 collective-permute-done.27
  182.1 1.6 collective-permute-start.28
  184.1 1.6 collective-permute-start.30
  186.1 1.6 collective-permute-done.28
  187.7 2.4 %collective-permute-done.29 = bf16[64,1024]{1,0:T(8,128)(2,1)S(1)} collective-permute-done((bf16[64,1024]{1,0:T(8,128)(2,1)S(1)}, bf16[64,1024]{1,0:T(8,128)(2,1)S(1)}, u32[]{:S(2)}, u32[]{:S(2)}) %collective-permute-start.29) | collective-permute-done | bytes 131104 | tf_op jit(solution)/shard_map/ppermute | solution.py:56
  190.2 1.6 collective-permute-done.31
  191.9 1.4 collective-permute-start.36
  193.3 0.7 collective-permute-start.37
  194.0 1.4 collective-permute-start.32
  195.4 0.7 collective-permute-start.33
  196.0 9.3 %down.7 = bf16[5,256,1024]{2,1,0:T(8,128)(2,1)S(1)} custom-call(s32[3,8]{1,0:T(4,128)S(1)} %get-tuple-element.230.tiles_ref, bf16[256,1024]{1,0:T(8,128)(2,1)S(1)} %copy-done.3, bf16[256,1024]{1,0:T(8,128)(2,1)S(1)} %copy-done.4, bf16[2048,4096]{1,0:T(8,128)(2,1)} %refs_2_.3, bf16[2048,4096]{1,0:T(8,128)(2,1)} %collective-permute-done.17.refs_2_.refs_3_), custom_call_target="tpu_custom_call" | custom-call | flops 10737418240 | bytes 20971520 | tf_op jit(solution)/shard_map/down/pallas_call | solution.py:374
  205.4 1.3 collective-permute-done.32
  206.7 1.5 collective-permute-done.33
  208.5 2.0 collective-permute-start.34
  210.8 1.9 collective-permute-start.40
  212.8 2.8 %collective-permute-done.35 = bf16[128,1024]{1,0:T(8,128)(2,1)S(1)} collective-permute-done((bf16[128,1024]{1,0:T(8,128)(2,1)S(1)}, bf16[128,1024]{1,0:T(8,128)(2,1)S(1)}, u32[]{:S(2)}, u32[]{:S(2)}) %collective-permute-start.35) | collective-permute-done | bytes 262176 | tf_op jit(solution)/shard_map/ppermute | solution.py:56
  215.9 1.9 collective-permute-start.38
  218.6 1.8 collective-permute-start.42
  220.7 1.5 fusion.15
  222.2 2.9 %collective-permute-done.42 = bf16[128,1024]{1,0:T(8,128)(2,1)S(1)} collective-permute-done((bf16[128,1024]{1,0:T(8,128)(2,1)S(1)}, bf16[128,1024]{1,0:T(8,128)(2,1)S(1)}, u32[]{:S(2)}, u32[]{:S(2)}) %collective-permute-start.42) | collective-permute-done | bytes 262176 | tf_op jit(solution)/shard_map/ppermute | solution.py:56
  225.1 1.6 collective-permute-done.43
  227.3 1.0 pad_maximum_fusion.1
  (112 shorter events, 10.3 us)
Async XLA Ops:
  0.8 6.7 %collective-permute-start = (f32[3,1024]{1,0:T(4,128)S(1)}, f32[3,1024]{1,0:T(4,128)S(1)}, u32[]{:S(2)}, u32[]{:S(2)}) collective-permute-start(f32[3,1024]{1,0:T(4,128)S(1)} %multiply_add_fusion.2), channel_id=1, source_target_pairs={{0,1},{2,3},{4,5},{6,7},{8,9},{10,11},{12,13},{14,15},{16,17},{18,... | collective-permute-start | bytes 36872 | tf_op jit(solution)/shard_map/ppermute | solution.py:454
  6.9 19.6 %copy-start.7 = (bf16[512,1024]{1,0:T(8,128)(2,1)S(1)}, bf16[512,1024]{1,0:T(8,128)(2,1)}, u32[]{:S(2)}) copy-start(bf16[512,1024]{1,0:T(8,128)(2,1)} %param.14) | copy-start | bytes 3145732
  6.9 19.6 %copy-start.21 = (f32[1024]{0:T(1024)S(1)}, f32[1024]{0:T(1024)}, u32[]{:S(2)}) copy-start(f32[1024]{0:T(1024)} %param.15) | copy-start | bytes 12292
  7.4 34.3 %copy-start.6 = (bf16[256,1024]{1,0:T(8,128)(2,1)}, bf16[256,1024]{1,0:T(8,128)(2,1)S(1)}, u32[]{:S(2)}) copy-start(bf16[256,1024]{1,0:T(8,128)(2,1)S(1)} %multiply_convert_fusion.1.refs_0_) | copy-start | bytes 1572868
  7.4 33.7 %collective-permute-start.5 = (bf16[4096,2048]{1,0:T(8,128)(2,1)}, bf16[4096,2048]{1,0:T(8,128)(2,1)}, u32[]{:S(2)}, u32[]{:S(2)}) collective-permute-start(bf16[4096,2048]{1,0:T(8,128)(2,1)} %refs_10_.5), channel_id=1, source_target_pairs={{0,1},{1,0},{2,3},{3,2},{4,5},{5,4},{6,7},{7,6},{8,9},{9,8},{10,11... | collective-permute-start | bytes 50331656 | tf_op jit(solution)/shard_map/ppermute | solution.py:60
  7.5 55.0 %collective-permute-start.10 = (bf16[4096,2048]{1,0:T(8,128)(2,1)}, bf16[4096,2048]{1,0:T(8,128)(2,1)}, u32[]{:S(2)}, u32[]{:S(2)}) collective-permute-start(bf16[4096,2048]{1,0:T(8,128)(2,1)} %refs_12_.3), channel_id=1, source_target_pairs={{0,1},{1,0},{2,3},{3,2},{4,5},{5,4},{6,7},{7,6},{8,9},{9,8},{10,11... | collective-permute-start | bytes 50331656 | tf_op jit(solution)/shard_map/ppermute | solution.py:60
  8.0 89.1 %collective-permute-start.17 = (bf16[2048,4096]{1,0:T(8,128)(2,1)}, bf16[2048,4096]{1,0:T(8,128)(2,1)}, u32[]{:S(2)}, u32[]{:S(2)}) collective-permute-start(bf16[2048,4096]{1,0:T(8,128)(2,1)} %refs_2_.3), channel_id=1, source_target_pairs={{0,1},{1,0},{2,3},{3,2},{4,5},{5,4},{6,7},{7,6},{8,9},{9,8},{10,11... | collective-permute-start | bytes 50331656 | tf_op jit(solution)/shard_map/ppermute | solution.py:60
  8.1 14.9 %collective-permute-start.1 = (bf16[256,1024]{1,0:T(8,128)(2,1)S(1)}, bf16[256,1024]{1,0:T(8,128)(2,1)S(1)}, u32[]{:S(2)}, u32[]{:S(2)}) collective-permute-start(bf16[256,1024]{1,0:T(8,128)(2,1)S(1)} %multiply_convert_fusion.1.refs_0_), channel_id=1, source_target_pairs={{0,4},{4,8},{8,12},{12,14},{14,10},{10,6},{6,2},{2,0},{1,5},{5,9},... | collective-permute-start | bytes 1572872 | tf_op jit(solution)/shard_map/ppermute | solution.py:56
  10.5 14.0 %collective-permute-start.2 = (bf16[256,1024]{1,0:T(8,128)(2,1)S(1)}, bf16[256,1024]{1,0:T(8,128)(2,1)S(1)}, u32[]{:S(2)}, u32[]{:S(2)}) collective-permute-start(bf16[256,1024]{1,0:T(8,128)(2,1)S(1)} %multiply_convert_fusion.1.refs_0_), channel_id=1, source_target_pairs={{0,2},{4,0},{8,4},{12,8},{14,12},{10,14},{6,10},{2,6},{1,3},{5,1},... | collective-permute-start | bytes 1572872 | tf_op jit(solution)/shard_map/ppermute | solution.py:56
  23.0 14.8 %copy-start.16 = (bf16[256,1024]{1,0:T(8,128)(2,1)}, bf16[256,1024]{1,0:T(8,128)(2,1)S(1)}, u32[]{:S(2)}) copy-start(bf16[256,1024]{1,0:T(8,128)(2,1)S(1)} %collective-permute-done.1.refs_1_) | copy-start | bytes 1572868
  24.5 14.6 %copy-start.17 = (bf16[256,1024]{1,0:T(8,128)(2,1)}, bf16[256,1024]{1,0:T(8,128)(2,1)S(1)}, u32[]{:S(2)}) copy-start(bf16[256,1024]{1,0:T(8,128)(2,1)S(1)} %collective-permute-done.2.refs_2_) | copy-start | bytes 1572868
  24.5 13.3 %collective-permute-start.3 = (bf16[256,1024]{1,0:T(8,128)(2,1)S(1)}, bf16[256,1024]{1,0:T(8,128)(2,1)}, u32[]{:S(2)}, u32[]{:S(2)}) collective-permute-start(bf16[256,1024]{1,0:T(8,128)(2,1)S(1)} %collective-permute-done.1.refs_1_), channel_id=1, source_target_pairs={{0,4},{4,8},{8,12},{12,14},{14,10},{10,6},{6,2},{2,0},{1,5},{5,9},... | collective-permute-start | bytes 1572872 | tf_op jit(solution)/shard_map/ppermute | solution.py:56
  26.1 13.0 %collective-permute-start.4 = (bf16[256,1024]{1,0:T(8,128)(2,1)S(1)}, bf16[256,1024]{1,0:T(8,128)(2,1)}, u32[]{:S(2)}, u32[]{:S(2)}) collective-permute-start(bf16[256,1024]{1,0:T(8,128)(2,1)S(1)} %collective-permute-done.2.refs_2_), channel_id=1, source_target_pairs={{0,2},{4,0},{8,4},{12,8},{14,12},{10,14},{6,10},{2,6},{1,3},{5,1},... | collective-permute-start | bytes 1572872 | tf_op jit(solution)/shard_map/ppermute | solution.py:56
  28.3 34.2 %copy-start.5 = (bf16[256,1024]{1,0:T(8,128)(2,1)}, bf16[256,1024]{1,0:T(8,128)(2,1)S(1)}, u32[]{:S(2)}) copy-start(bf16[256,1024]{1,0:T(8,128)(2,1)S(1)} %multiply_convert_fusion.refs_0_) | copy-start | bytes 1572868
  39.1 17.4 %collective-permute-start.8 = (bf16[256,1024]{1,0:T(8,128)(2,1)}, bf16[256,1024]{1,0:T(8,128)(2,1)S(1)}, u32[]{:S(2)}, u32[]{:S(2)}) collective-permute-start(bf16[256,1024]{1,0:T(8,128)(2,1)} %collective-permute-done.3.refs_3_), channel_id=1, source_target_pairs={{0,4},{4,8},{8,12},{12,14},{14,10},{10,6},{6,2},{2,0},{1,5},{5,9},... | collective-permute-start | bytes 1572872 | tf_op jit(solution)/shard_map/ppermute | solution.py:56
  40.6 15.8 %collective-permute-start.9 = (bf16[256,1024]{1,0:T(8,128)(2,1)}, bf16[256,1024]{1,0:T(8,128)(2,1)}, u32[]{:S(2)}, u32[]{:S(2)}) collective-permute-start(bf16[256,1024]{1,0:T(8,128)(2,1)} %collective-permute-done.4.refs_4_), channel_id=1, source_target_pairs={{0,2},{4,0},{8,4},{12,8},{14,12},{10,14},{6,10},{2,6},{1,3},{5,1},... | collective-permute-start | bytes 1572872 | tf_op jit(solution)/shard_map/ppermute | solution.py:56
  56.4 6.5 %copy-start.12 = (bf16[256,1024]{1,0:T(8,128)(2,1)}, bf16[256,1024]{1,0:T(8,128)(2,1)S(1)}, u32[]{:S(2)}) copy-start(bf16[256,1024]{1,0:T(8,128)(2,1)S(1)} %collective-permute-done.8.refs_5_.refs_0_) | copy-start | bytes 1572868
  58.9 20.4 %collective-permute-start.12 = (bf16[128,1024]{1,0:T(8,128)(2,1)}, bf16[128,1024]{1,0:T(8,128)(2,1)S(1)}, u32[]{:S(2)}, u32[]{:S(2)}) collective-permute-start(bf16[128,1024]{1,0:T(8,128)(2,1)} %slice.332), channel_id=1, source_target_pairs={{0,2},{4,0},{8,4},{12,8},{14,12},{10,14},{6,10},{2,6},{1,3},{5,1},... | collective-permute-start | bytes 786440 | tf_op jit(solution)/shard_map/ppermute | solution.py:56
  59.4 20.0 %collective-permute-start.11 = (bf16[128,1024]{1,0:T(8,128)(2,1)}, bf16[128,1024]{1,0:T(8,128)(2,1)}, u32[]{:S(2)}, u32[]{:S(2)}) collective-permute-start(bf16[128,1024]{1,0:T(8,128)(2,1)} %slice.331), channel_id=1, source_target_pairs={{0,4},{4,8},{8,12},{12,14},{14,10},{10,6},{6,2},{2,0},{1,5},{5,9},... | collective-permute-start | bytes 786440 | tf_op jit(solution)/shard_map/ppermute | solution.py:56
  60.9 18.4 %collective-permute-start.6 = (bf16[256,1024]{1,0:T(8,128)(2,1)S(1)}, bf16[256,1024]{1,0:T(8,128)(2,1)S(1)}, u32[]{:S(2)}, u32[]{:S(2)}) collective-permute-start(bf16[256,1024]{1,0:T(8,128)(2,1)S(1)} %multiply_convert_fusion.refs_0_), channel_id=1, source_target_pairs={{0,4},{4,8},{8,12},{12,14},{14,10},{10,6},{6,2},{2,0},{1,5},{5,9},... | collective-permute-start | bytes 1572872 | tf_op jit(solution)/shard_map/ppermute | solution.py:56
  62.5 16.9 %collective-permute-start.7 = (bf16[256,1024]{1,0:T(8,128)(2,1)S(1)}, bf16[256,1024]{1,0:T(8,128)(2,1)}, u32[]{:S(2)}, u32[]{:S(2)}) collective-permute-start(bf16[256,1024]{1,0:T(8,128)(2,1)S(1)} %multiply_convert_fusion.refs_0_), channel_id=1, source_target_pairs={{0,2},{4,0},{8,4},{12,8},{14,12},{10,14},{6,10},{2,6},{1,3},{5,1},... | collective-permute-start | bytes 1572872 | tf_op jit(solution)/shard_map/ppermute | solution.py:56
  79.3 2.1 copy-start.20
  79.4 15.7 %copy-start.13 = (bf16[256,1024]{1,0:T(8,128)(2,1)}, bf16[256,1024]{1,0:T(8,128)(2,1)S(1)}, u32[]{:S(2)}) copy-start(bf16[256,1024]{1,0:T(8,128)(2,1)S(1)} %collective-permute-done.6.refs_1_) | copy-start | bytes 1572868
  79.4 15.7 %collective-permute-start.13 = (bf16[256,1024]{1,0:T(8,128)(2,1)S(1)}, bf16[256,1024]{1,0:T(8,128)(2,1)S(1)}, u32[]{:S(2)}, u32[]{:S(2)}) collective-permute-start(bf16[256,1024]{1,0:T(8,128)(2,1)S(1)} %collective-permute-done.6.refs_1_), channel_id=1, source_target_pairs={{0,4},{4,8},{8,12},{12,14},{14,10},{10,6},{6,2},{2,0},{1,5},{5,9},... | collective-permute-start | bytes 1572872 | tf_op jit(solution)/shard_map/ppermute | solution.py:56
  81.0 14.0 %collective-permute-start.14 = (bf16[256,1024]{1,0:T(8,128)(2,1)}, bf16[256,1024]{1,0:T(8,128)(2,1)S(1)}, u32[]{:S(2)}, u32[]{:S(2)}) collective-permute-start(bf16[256,1024]{1,0:T(8,128)(2,1)} %collective-permute-done.7.refs_2_), channel_id=1, source_target_pairs={{0,2},{4,0},{8,4},{12,8},{14,12},{10,14},{6,10},{2,6},{1,3},{5,1},... | collective-permute-start | bytes 1572872 | tf_op jit(solution)/shard_map/ppermute | solution.py:56
  95.0 10.0 %copy-start.14 = (bf16[256,1024]{1,0:T(8,128)(2,1)}, bf16[256,1024]{1,0:T(8,128)(2,1)S(1)}, u32[]{:S(2)}) copy-start(bf16[256,1024]{1,0:T(8,128)(2,1)S(1)} %collective-permute-done.13.refs_3_) | copy-start | bytes 1572868
  95.1 10.0 %copy-start.15 = (bf16[256,1024]{1,0:T(8,128)(2,1)}, bf16[256,1024]{1,0:T(8,128)(2,1)S(1)}, u32[]{:S(2)}) copy-start(bf16[256,1024]{1,0:T(8,128)(2,1)S(1)} %collective-permute-done.14.refs_4_) | copy-start | bytes 1572868
  95.1 10.1 %collective-permute-start.15 = (bf16[256,1024]{1,0:T(8,128)(2,1)S(1)}, bf16[256,1024]{1,0:T(8,128)(2,1)S(1)}, u32[]{:S(2)}, u32[]{:S(2)}) collective-permute-start(bf16[256,1024]{1,0:T(8,128)(2,1)S(1)} %collective-permute-done.13.refs_3_), channel_id=1, source_target_pairs={{0,4},{4,8},{8,12},{12,14},{14,10},{10,6},{6,2},{2,0},{1,5},{5,9},... | collective-permute-start | bytes 1572872 | tf_op jit(solution)/shard_map/ppermute | solution.py:56
  96.7 12.0 %collective-permute-start.16 = (bf16[256,1024]{1,0:T(8,128)(2,1)S(1)}, bf16[256,1024]{1,0:T(8,128)(2,1)S(1)}, u32[]{:S(2)}, u32[]{:S(2)}) collective-permute-start(bf16[256,1024]{1,0:T(8,128)(2,1)S(1)} %collective-permute-done.14.refs_4_), channel_id=1, source_target_pairs={{0,2},{4,0},{8,4},{12,8},{14,12},{10,14},{6,10},{2,6},{1,3},{5,1},... | collective-permute-start | bytes 1572872 | tf_op jit(solution)/shard_map/ppermute | solution.py:56
  105.1 7.8 %copy-start.2 = (bf16[256,2048]{1,0:T(8,128)(2,1)S(1)}, bf16[256,2048]{1,0:T(8,128)(2,1)}, u32[]{:S(2)}) copy-start(bf16[256,2048]{1,0:T(8,128)(2,1)} %get-tuple-element.143.refs_0_) | copy-start | bytes 3145732
  105.2 17.0 %copy-start.10 = (bf16[256,1024]{1,0:T(8,128)(2,1)}, bf16[256,1024]{1,0:T(8,128)(2,1)S(1)}, u32[]{:S(2)}) copy-start(bf16[256,1024]{1,0:T(8,128)(2,1)S(1)} %collective-permute-done.15.refs_5_) | copy-start | bytes 1572868
  108.7 13.5 %copy-start.11 = (bf16[256,1024]{1,0:T(8,128)(2,1)}, bf16[256,1024]{1,0:T(8,128)(2,1)S(1)}, u32[]{:S(2)}) copy-start(bf16[256,1024]{1,0:T(8,128)(2,1)S(1)} %collective-permute-done.16.refs_6_) | copy-start | bytes 1572868
  108.8 17.4 %collective-permute-start.19 = (bf16[128,1024]{1,0:T(8,128)(2,1)S(1)}, bf16[128,1024]{1,0:T(8,128)(2,1)S(1)}, u32[]{:S(2)}, u32[]{:S(2)}) collective-permute-start(bf16[128,1024]{1,0:T(8,128)(2,1)S(1)} %slice.334), channel_id=1, source_target_pairs={{0,2},{4,0},{8,4},{12,8},{14,12},{10,14},{6,10},{2,6},{1,3},{5,1},... | collective-permute-start | bytes 786440 | tf_op jit(solution)/shard_map/ppermute | solution.py:56
  108.8 17.3 %collective-permute-start.18 = (bf16[128,1024]{1,0:T(8,128)(2,1)S(1)}, bf16[128,1024]{1,0:T(8,128)(2,1)S(1)}, u32[]{:S(2)}, u32[]{:S(2)}) collective-permute-start(bf16[128,1024]{1,0:T(8,128)(2,1)S(1)} %slice.333), channel_id=1, source_target_pairs={{0,4},{4,8},{8,12},{12,14},{14,10},{10,6},{6,2},{2,0},{1,5},{5,9},... | collective-permute-start | bytes 786440 | tf_op jit(solution)/shard_map/ppermute | solution.py:56
  110.8 12.9 %collective-permute-start.20 = (bf16[128,1024]{1,0:T(8,128)(2,1)S(1)}, bf16[128,1024]{1,0:T(8,128)(2,1)S(1)}, u32[]{:S(2)}, u32[]{:S(2)}) collective-permute-start(bf16[128,1024]{1,0:T(8,128)(2,1)S(1)} %get-tuple-element.144), channel_id=1, source_target_pairs={{0,4},{4,8},{8,12},{12,14},{14,10},{10,6},{6,2},{2,0},{1,5},{5,9},... | collective-permute-start | bytes 786440 | tf_op jit(solution)/shard_map/ppermute | solution.py:56
  112.3 11.4 %collective-permute-start.21 = (bf16[128,1024]{1,0:T(8,128)(2,1)S(1)}, bf16[128,1024]{1,0:T(8,128)(2,1)S(1)}, u32[]{:S(2)}, u32[]{:S(2)}) collective-permute-start(bf16[128,1024]{1,0:T(8,128)(2,1)S(1)} %get-tuple-element.145), channel_id=1, source_target_pairs={{0,2},{4,0},{8,4},{12,8},{14,12},{10,14},{6,10},{2,6},{1,3},{5,1},... | collective-permute-start | bytes 786440 | tf_op jit(solution)/shard_map/ppermute | solution.py:56
  122.2 1.5 copy-start
  124.0 22.3 %collective-permute-start.22 = (bf16[256,1024]{1,0:T(8,128)(2,1)S(1)}, bf16[256,1024]{1,0:T(8,128)(2,1)}, u32[]{:S(2)}, u32[]{:S(2)}) collective-permute-start(bf16[256,1024]{1,0:T(8,128)(2,1)S(1)} %pad_maximum_fusion.2), channel_id=1, source_target_pairs={{0,4},{4,8},{8,12},{12,14},{14,10},{10,6},{6,2},{2,0},{1,5},{5,9},... | collective-permute-start | bytes 1572872 | tf_op jit(solution)/shard_map/ppermute | solution.py:56
  125.6 20.7 %collective-permute-start.23 = (bf16[256,1024]{1,0:T(8,128)(2,1)S(1)}, bf16[256,1024]{1,0:T(8,128)(2,1)}, u32[]{:S(2)}, u32[]{:S(2)}) collective-permute-start(bf16[256,1024]{1,0:T(8,128)(2,1)S(1)} %pad_maximum_fusion.3), channel_id=1, source_target_pairs={{0,2},{4,0},{8,4},{12,8},{14,12},{10,14},{6,10},{2,6},{1,3},{5,1},... | collective-permute-start | bytes 1572872 | tf_op jit(solution)/shard_map/ppermute | solution.py:56
  148.2 19.9 %collective-permute-start.25 = (bf16[256,1024]{1,0:T(8,128)(2,1)S(1)}, bf16[256,1024]{1,0:T(8,128)(2,1)S(1)}, u32[]{:S(2)}, u32[]{:S(2)}) collective-permute-start(bf16[256,1024]{1,0:T(8,128)(2,1)S(1)} %get-tuple-element.205), channel_id=1, source_target_pairs={{0,2},{4,0},{8,4},{12,8},{14,12},{10,14},{6,10},{2,6},{1,3},{5,1},... | collective-permute-start | bytes 1572872 | tf_op jit(solution)/shard_map/ppermute | solution.py:56
  148.3 19.8 %collective-permute-start.24 = (bf16[256,1024]{1,0:T(8,128)(2,1)S(1)}, bf16[256,1024]{1,0:T(8,128)(2,1)}, u32[]{:S(2)}, u32[]{:S(2)}) collective-permute-start(bf16[256,1024]{1,0:T(8,128)(2,1)S(1)} %get-tuple-element.206), channel_id=1, source_target_pairs={{0,4},{4,8},{8,12},{12,14},{14,10},{10,6},{6,2},{2,0},{1,5},{5,9},... | collective-permute-start | bytes 1572872 | tf_op jit(solution)/shard_map/ppermute | solution.py:56
  168.1 4.0 %copy-start.3 = (bf16[256,1024]{1,0:T(8,128)(2,1)S(1)}, bf16[256,1024]{1,0:T(8,128)(2,1)}, u32[]{:S(2)}) copy-start(bf16[256,1024]{1,0:T(8,128)(2,1)} %get-tuple-element.183.refs_0_) | copy-start | bytes 1572868
  168.1 4.0 %copy-start.4 = (bf16[256,1024]{1,0:T(8,128)(2,1)S(1)}, bf16[256,1024]{1,0:T(8,128)(2,1)}, u32[]{:S(2)}) copy-start(bf16[256,1024]{1,0:T(8,128)(2,1)} %get-tuple-element.184.refs_1_) | copy-start | bytes 1572868
  170.0 10.6 %collective-permute-start.26 = (bf16[256,1024]{1,0:T(8,128)(2,1)S(1)}, bf16[256,1024]{1,0:T(8,128)(2,1)S(1)}, u32[]{:S(2)}, u32[]{:S(2)}) collective-permute-start(bf16[256,1024]{1,0:T(8,128)(2,1)S(1)} %get-tuple-element.203), channel_id=1, source_target_pairs={{0,4},{4,8},{8,12},{12,14},{14,10},{10,6},{6,2},{2,0},{1,5},{5,9},... | collective-permute-start | bytes 1572872 | tf_op jit(solution)/shard_map/ppermute | solution.py:56
  171.5 10.5 %collective-permute-start.27 = (bf16[256,1024]{1,0:T(8,128)(2,1)S(1)}, bf16[256,1024]{1,0:T(8,128)(2,1)S(1)}, u32[]{:S(2)}, u32[]{:S(2)}) collective-permute-start(bf16[256,1024]{1,0:T(8,128)(2,1)S(1)} %get-tuple-element.204), channel_id=1, source_target_pairs={{0,2},{4,0},{8,4},{12,8},{14,12},{10,14},{6,10},{2,6},{1,3},{5,1},... | collective-permute-start | bytes 1572872 | tf_op jit(solution)/shard_map/ppermute | solution.py:56
  182.1 5.6 %collective-permute-start.28 = (bf16[64,1024]{1,0:T(8,128)(2,1)S(1)}, bf16[64,1024]{1,0:T(8,128)(2,1)S(1)}, u32[]{:S(2)}, u32[]{:S(2)}) collective-permute-start(bf16[64,1024]{1,0:T(8,128)(2,1)S(1)} %get-tuple-element.175), channel_id=1, source_target_pairs={{0,4},{4,8},{8,12},{12,14},{14,10},{10,6},{6,2},{2,0},{1,5},{5,9},... | collective-permute-start | bytes 393224 | tf_op jit(solution)/shard_map/ppermute | solution.py:56
  183.6 6.4 %collective-permute-start.29 = (bf16[64,1024]{1,0:T(8,128)(2,1)S(1)}, bf16[64,1024]{1,0:T(8,128)(2,1)S(1)}, u32[]{:S(2)}, u32[]{:S(2)}) collective-permute-start(bf16[64,1024]{1,0:T(8,128)(2,1)S(1)} %get-tuple-element.176), channel_id=1, source_target_pairs={{0,2},{4,0},{8,4},{12,8},{14,12},{10,14},{6,10},{2,6},{1,3},{5,1},... | collective-permute-start | bytes 393224 | tf_op jit(solution)/shard_map/ppermute | solution.py:56
  184.1 6.1 %collective-permute-start.30 = (bf16[64,1024]{1,0:T(8,128)(2,1)S(1)}, bf16[64,1024]{1,0:T(8,128)(2,1)S(1)}, u32[]{:S(2)}, u32[]{:S(2)}) collective-permute-start(bf16[64,1024]{1,0:T(8,128)(2,1)S(1)} %get-tuple-element.177), channel_id=1, source_target_pairs={{0,4},{4,8},{8,12},{12,14},{14,10},{10,6},{6,2},{2,0},{1,5},{5,9},... | collective-permute-start | bytes 393224 | tf_op jit(solution)/shard_map/ppermute | solution.py:56
  185.6 6.1 %collective-permute-start.31 = (bf16[64,1024]{1,0:T(8,128)(2,1)S(1)}, bf16[64,1024]{1,0:T(8,128)(2,1)S(1)}, u32[]{:S(2)}, u32[]{:S(2)}) collective-permute-start(bf16[64,1024]{1,0:T(8,128)(2,1)S(1)} %get-tuple-element.178), channel_id=1, source_target_pairs={{0,2},{4,0},{8,4},{12,8},{14,12},{10,14},{6,10},{2,6},{1,3},{5,1},... | collective-permute-start | bytes 393224 | tf_op jit(solution)/shard_map/ppermute | solution.py:56
  191.9 18.6 %collective-permute-start.36 = (bf16[128,1024]{1,0:T(8,128)(2,1)S(1)}, bf16[128,1024]{1,0:T(8,128)(2,1)S(1)}, u32[]{:S(2)}, u32[]{:S(2)}) collective-permute-start(bf16[128,1024]{1,0:T(8,128)(2,1)S(1)} %pad_maximum_fusion.6), channel_id=1, source_target_pairs={{0,4},{4,8},{8,12},{12,14},{14,10},{10,6},{6,2},{2,0},{1,5},{5,9},... | collective-permute-start | bytes 786440 | tf_op jit(solution)/shard_map/ppermute | solution.py:56
  193.3 17.2 %collective-permute-start.37 = (bf16[128,1024]{1,0:T(8,128)(2,1)S(1)}, bf16[128,1024]{1,0:T(8,128)(2,1)S(1)}, u32[]{:S(2)}, u32[]{:S(2)}) collective-permute-start(bf16[128,1024]{1,0:T(8,128)(2,1)S(1)} %pad_maximum_fusion.7), channel_id=1, source_target_pairs={{0,2},{4,0},{8,4},{12,8},{14,12},{10,14},{6,10},{2,6},{1,3},{5,1},... | collective-permute-start | bytes 786440 | tf_op jit(solution)/shard_map/ppermute | solution.py:56
  194.0 12.7 %collective-permute-start.32 = (bf16[128,1024]{1,0:T(8,128)(2,1)S(1)}, bf16[128,1024]{1,0:T(8,128)(2,1)S(1)}, u32[]{:S(2)}, u32[]{:S(2)}) collective-permute-start(bf16[128,1024]{1,0:T(8,128)(2,1)S(1)} %pad_maximum_fusion.4), channel_id=1, source_target_pairs={{0,4},{4,8},{8,12},{12,14},{14,10},{10,6},{6,2},{2,0},{1,5},{5,9},... | collective-permute-start | bytes 786440 | tf_op jit(solution)/shard_map/ppermute | solution.py:56
  195.4 12.8 %collective-permute-start.33 = (bf16[128,1024]{1,0:T(8,128)(2,1)S(1)}, bf16[128,1024]{1,0:T(8,128)(2,1)S(1)}, u32[]{:S(2)}, u32[]{:S(2)}) collective-permute-start(bf16[128,1024]{1,0:T(8,128)(2,1)S(1)} %pad_maximum_fusion.5), channel_id=1, source_target_pairs={{0,2},{4,0},{8,4},{12,8},{14,12},{10,14},{6,10},{2,6},{1,3},{5,1},... | collective-permute-start | bytes 786440 | tf_op jit(solution)/shard_map/ppermute | solution.py:56
  208.4 7.2 %collective-permute-start.35 = (bf16[128,1024]{1,0:T(8,128)(2,1)S(1)}, bf16[128,1024]{1,0:T(8,128)(2,1)S(1)}, u32[]{:S(2)}, u32[]{:S(2)}) collective-permute-start(bf16[128,1024]{1,0:T(8,128)(2,1)S(1)} %get-tuple-element.201), channel_id=1, source_target_pairs={{0,2},{4,0},{8,4},{12,8},{14,12},{10,14},{6,10},{2,6},{1,3},{5,1},... | collective-permute-start | bytes 786440 | tf_op jit(solution)/shard_map/ppermute | solution.py:56
  208.5 12.2 %copy-start.8 = (bf16[512,1024]{1,0:T(8,128)(2,1)S(1)}, bf16[512,1024]{1,0:T(8,128)(2,1)}, u32[]{:S(2)}) copy-start(bf16[512,1024]{1,0:T(8,128)(2,1)} %param.14) | copy-start | bytes 3145732
  208.5 12.2 %copy-start.9 = (bf16[512,1024]{1,0:T(8,128)(2,1)S(1)}, bf16[512,1024]{1,0:T(8,128)(2,1)}, u32[]{:S(2)}) copy-start(bf16[512,1024]{1,0:T(8,128)(2,1)} %param.13) | copy-start | bytes 3145732
  208.5 12.2 %copy-start.22 = (f32[1024]{0:T(1024)S(1)}, f32[1024]{0:T(1024)}, u32[]{:S(2)}) copy-start(f32[1024]{0:T(1024)} %param.15) | copy-start | bytes 12292
  208.5 7.1 %collective-permute-start.34 = (bf16[128,1024]{1,0:T(8,128)(2,1)S(1)}, bf16[128,1024]{1,0:T(8,128)(2,1)S(1)}, u32[]{:S(2)}, u32[]{:S(2)}) collective-permute-start(bf16[128,1024]{1,0:T(8,128)(2,1)S(1)} %get-tuple-element.202), channel_id=1, source_target_pairs={{0,4},{4,8},{8,12},{12,14},{14,10},{10,6},{6,2},{2,0},{1,5},{5,9},... | collective-permute-start | bytes 786440 | tf_op jit(solution)/shard_map/ppermute | solution.py:56
  210.7 7.7 %collective-permute-start.41 = (bf16[128,1024]{1,0:T(8,128)(2,1)S(1)}, bf16[128,1024]{1,0:T(8,128)(2,1)S(1)}, u32[]{:S(2)}, u32[]{:S(2)}) collective-permute-start(bf16[128,1024]{1,0:T(8,128)(2,1)S(1)} %get-tuple-element.199), channel_id=1, source_target_pairs={{0,2},{4,0},{8,4},{12,8},{14,12},{10,14},{6,10},{2,6},{1,3},{5,1},... | collective-permute-start | bytes 786440 | tf_op jit(solution)/shard_map/ppermute | solution.py:56
  210.8 7.6 %collective-permute-start.40 = (bf16[128,1024]{1,0:T(8,128)(2,1)S(1)}, bf16[128,1024]{1,0:T(8,128)(2,1)S(1)}, u32[]{:S(2)}, u32[]{:S(2)}) collective-permute-start(bf16[128,1024]{1,0:T(8,128)(2,1)S(1)} %get-tuple-element.200), channel_id=1, source_target_pairs={{0,4},{4,8},{8,12},{12,14},{14,10},{10,6},{6,2},{2,0},{1,5},{5,9},... | collective-permute-start | bytes 786440 | tf_op jit(solution)/shard_map/ppermute | solution.py:56
  215.8 11.0 %collective-permute-start.39 = (bf16[128,1024]{1,0:T(8,128)(2,1)S(1)}, bf16[128,1024]{1,0:T(8,128)(2,1)S(1)}, u32[]{:S(2)}, u32[]{:S(2)}) collective-permute-start(bf16[128,1024]{1,0:T(8,128)(2,1)S(1)} %get-tuple-element.197), channel_id=1, source_target_pairs={{0,2},{4,0},{8,4},{12,8},{14,12},{10,14},{6,10},{2,6},{1,3},{5,1},... | collective-permute-start | bytes 786440 | tf_op jit(solution)/shard_map/ppermute | solution.py:56
  215.9 10.8 %collective-permute-start.38 = (bf16[128,1024]{1,0:T(8,128)(2,1)S(1)}, bf16[128,1024]{1,0:T(8,128)(2,1)S(1)}, u32[]{:S(2)}, u32[]{:S(2)}) collective-permute-start(bf16[128,1024]{1,0:T(8,128)(2,1)S(1)} %get-tuple-element.198), channel_id=1, source_target_pairs={{0,4},{4,8},{8,12},{12,14},{14,10},{10,6},{6,2},{2,0},{1,5},{5,9},... | collective-permute-start | bytes 786440 | tf_op jit(solution)/shard_map/ppermute | solution.py:56
  218.6 6.5 %collective-permute-start.42 = (bf16[128,1024]{1,0:T(8,128)(2,1)S(1)}, bf16[128,1024]{1,0:T(8,128)(2,1)S(1)}, u32[]{:S(2)}, u32[]{:S(2)}) collective-permute-start(bf16[128,1024]{1,0:T(8,128)(2,1)S(1)} %get-tuple-element.195), channel_id=1, source_target_pairs={{0,4},{4,8},{8,12},{12,14},{14,10},{10,6},{6,2},{2,0},{1,5},{5,9},... | collective-permute-start | bytes 786440 | tf_op jit(solution)/shard_map/ppermute | solution.py:56
  220.4 6.4 %collective-permute-start.43 = (bf16[128,1024]{1,0:T(8,128)(2,1)S(1)}, bf16[128,1024]{1,0:T(8,128)(2,1)S(1)}, u32[]{:S(2)}, u32[]{:S(2)}) collective-permute-start(bf16[128,1024]{1,0:T(8,128)(2,1)S(1)} %get-tuple-element.196), channel_id=1, source_target_pairs={{0,2},{4,0},{8,4},{12,8},{14,12},{10,14},{6,10},{2,6},{1,3},{5,1},... | collective-permute-start | bytes 786440 | tf_op jit(solution)/shard_map/ppermute | solution.py:56
  (3 other events, 2.6 us)

commit v12 on v11

--- a/solution.py
+++ b/solution.py
@@ -8,8 +8,7 @@
 from jax.experimental.pallas import tpu as pltpu
 from jax.sharding import PartitionSpec as P
 
-GATE_UP_VMEM = 62 * 1024 * 1024
-DOWN_VMEM = 50 * 1024 * 1024
+VMEM_LIMIT = 50 * 1024 * 1024
 DEEP, PARTS = 3, 4
 LANES = 128
 
@@ -111,8 +110,6 @@
         gather_pieces(0, lambda copy: copy.start())
         for number in range(min(DEEP - 1, length)):
             fetch(jnp.int32(number))
-        for place in range(1, len(pieces)):
-            gather_pieces(place, lambda copy: copy.start())
         partials(lambda copy: copy.start())
         sums[...] = jnp.zeros_like(sums)
         stat_ref[...] = before_ref[...]
@@ -127,6 +124,8 @@
         @pl.when((place == wanted) & (units_ref[3, step] == 1))
         def arrived(wanted=wanted):
             gather_pieces(wanted, lambda copy: copy.wait())
+            if wanted + 1 < len(pieces):
+                gather_pieces(wanted + 1, lambda copy: copy.start())
 
     block = stacked[:, pl.ds(pl.multiple_of(place * width, width), width)]
 
@@ -200,7 +199,7 @@
                 pltpu.SemaphoreType.DMA((DEEP,)),
             ],
         ),
-        compiler_params=pltpu.CompilerParams(vmem_limit_bytes=GATE_UP_VMEM),
+        compiler_params=pltpu.CompilerParams(vmem_limit_bytes=VMEM_LIMIT),
         cost_estimate=pl.CostEstimate(
             flops=4 * rows * width * columns * len(units),
             bytes_accessed=2 * width * columns * len(units),
@@ -252,8 +251,6 @@
         gather_pieces(0, lambda copy: copy.start())
         for number in range(min(DEEP - 1, count)):
             fetch(jnp.int32(number))
-        for wanted in range(1, count):
-            gather_pieces(wanted, lambda copy: copy.start())
         sums[...] = jnp.zeros_like(sums)
         stat[...] = before_ref[...]
 
@@ -266,6 +263,8 @@
         @pl.when(step == wanted)
         def arrived(wanted=wanted):
             gather_pieces(wanted, lambda copy: copy.wait())
+            if wanted + 1 < count:
+                gather_pieces(wanted + 1, lambda copy: copy.start())
 
     slot = lax.rem(step, DEEP)
     block = stacked[:, pl.ds(pl.multiple_of(step * width, width), width)]
@@ -319,7 +318,7 @@
                 pltpu.SemaphoreType.DMA((DEEP, 2)),
             ],
         ),
-        compiler_params=pltpu.CompilerParams(vmem_limit_bytes=GATE_UP_VMEM),
+        compiler_params=pltpu.CompilerParams(vmem_limit_bytes=VMEM_LIMIT),
         cost_estimate=pl.CostEstimate(
             flops=8 * rows * count * width * columns,
             bytes_accessed=4 * count * width * columns,
@@ -385,7 +384,7 @@
                 pltpu.SemaphoreType.DMA((DEEP,)),
             ],
         ),
-        compiler_params=pltpu.CompilerParams(vmem_limit_bytes=DOWN_VMEM),
+        compiler_params=pltpu.CompilerParams(vmem_limit_bytes=VMEM_LIMIT),
         cost_estimate=pl.CostEstimate(
             flops=4 * rows * depth * width * (stop - start),
             bytes_accessed=2 * depth * width * (stop - start),

time: 229 us -> 215 us (0.939)
  Pallas kernels: 113 us -> 104 us
  local copies, waits for them, and re-layouts: 10.4 us -> 1.88 us
  waiting for transfers between devices: 46.5 us -> 52.6 us
  other arithmetic: 12.5 us -> 8.61 us
    ppermute x40, waiting for transfers between devices: 46.5 us -> 52.5 us  [ring_shift(): lax.ppermute(value, 'blk', [(ring[i], ring[(i + steps) % count]) for i in...]
    pallas_call x3, Pallas kernels: 44.6 us -> 38.8 us  [gate_up(): pl.pallas_call(functools.partial(gate_up_kernel, fixed), out_shape=(jax.S...]
    unnamed x46 -> x22, local copies, waits for them, and re-layouts: 4.25 us -> 0.05 us
    pallas_call x2, Pallas kernels: 36.5 us -> 33.5 us  [gate_up_columns(): pl.pallas_call(functools.partial(columns_kernel, start, width * count, no...]
    convert_element_type x9, other arithmetic: 4.84 us -> 1.9 us  [joined(): (one.astype(jnp.float32) + two.astype(jnp.float32)).astype(jnp.bfloat16)]
    slice x4, local copies, waits for them, and re-layouts: 2.46 us -> 0.07 us  [gather_step(): before, behind = (before[:cut], behind[cut:])]
  transfers between devices with their start and end apart: 44 -> 44, of which waited for: 16 -> 20; matrix products, arithmetic and copies ran while one was open for 5% -> 3% of each run, Pallas kernels for 50% -> 49%
where the time goes in v12:
time: 215 us
  Pallas kernels  104 us (48%)
  waiting for transfers between devices  52.6 us (24%)
  starting transfers between devices  46.5 us (22%)
  other arithmetic  8.61 us (4%)
    ppermute x40, waiting for transfers between devices, ring_shift(): lax.ppermute(value, 'blk', [(ring[i], ring[(i + steps) % count]) for i in...  52.5 us
    ppermute x40, starting transfers between devices, ring_shift(): lax.ppermute(value, 'blk', [(ring[i], ring[(i + steps) % count]) for i in...  43.5 us
    pallas_call x3, Pallas kernels, gate_up(): pl.pallas_call(functools.partial(gate_up_kernel, fixed), out_shape=(jax.S...  38.8 us
    pallas_call x2, Pallas kernels, gate_up_columns(): pl.pallas_call(functools.partial(columns_kernel, start, width * count, no...  33.5 us
    pallas_call x4, Pallas kernels, down(): pl.pallas_call(functools.partial(down_kernel, start, stop - start), out_s...  32 us
  transfers between devices with their start and end apart: 44, of which 20 were waited for; matrix products, arithmetic and copies ran while one was open for 3% of the time, Pallas kernels for 49%

profile of v12, /device:TPU:0, one launch (start us, length us, event | category | flops | bytes accessed | tf_op | source)
XLA Modules:
  0.0 215.0 jit_solution(12506886754073856681)
XLA Ops:
  0.0 0.8 multiply_add_fusion.2
  0.8 2.4 %collective-permute-start = (f32[3,1024]{1,0:T(4,128)S(1)}, f32[3,1024]{1,0:T(4,128)S(1)}, u32[]{:S(2)}, u32[]{:S(2)}) collective-permute-start(f32[3,1024]{1,0:T(4,128)S(1)} %multiply_add_fusion.2), channel_id=1, source_target_pairs={{0,1},{2,3},{4,5},{6,7},{8,9},{10,11},{12,13},{14,15},{16,17},{18,... | collective-permute-start | bytes 36872 | tf_op jit(solution)/shard_map/ppermute | solution.py:453
  3.1 1.5 multiply_add_fusion
  5.3 0.9 constant_dynamic-slice_fusion.2
  6.3 0.5 multiply_convert_fusion.1.refs_0_
  6.9 0.5 collective-permute-start.10
  7.4 2.4 %collective-permute-start.1 = (bf16[256,1024]{1,0:T(8,128)(2,1)S(1)}, bf16[256,1024]{1,0:T(8,128)(2,1)S(1)}, u32[]{:S(2)}, u32[]{:S(2)}) collective-permute-start(bf16[256,1024]{1,0:T(8,128)(2,1)S(1)} %multiply_convert_fusion.1.refs_0_), channel_id=1, source_target_pairs={{0,4},{4,8},{8,12},{12,14},{14,10},{10,6},{6,2},{2,0},{1,5},{5,9},... | collective-permute-start | bytes 1572872 | tf_op jit(solution)/shard_map/ppermute | solution.py:55
  9.9 0.7 dynamic-slice_bitcast_fusion
  10.6 11.8 %collective-permute-done.1.refs_1_ = bf16[256,1024]{1,0:T(8,128)(2,1)S(1)} collective-permute-done((bf16[256,1024]{1,0:T(8,128)(2,1)S(1)}, bf16[256,1024]{1,0:T(8,128)(2,1)S(1)}, u32[]{:S(2)}, u32[]{:S(2)}) %collective-permute-start.1) | collective-permute-done | bytes 524320 | tf_op jit(solution)/shard_map/ppermute | solution.py:55
  22.3 1.5 collective-permute-done.2.refs_2_
  23.8 1.6 collective-permute-start.3
  25.4 0.4 collective-permute-start.4
  25.9 1.2 multiply_add_fusion.1
  27.1 0.5 multiply_convert_fusion.refs_0_
  27.6 9.4 %collective-permute-done.3.refs_3_ = bf16[256,1024]{1,0:T(8,128)(2,1)S(1)} collective-permute-done((bf16[256,1024]{1,0:T(8,128)(2,1)S(1)}, bf16[256,1024]{1,0:T(8,128)(2,1)S(1)}, u32[]{:S(2)}, u32[]{:S(2)}) %collective-permute-start.3) | collective-permute-done | bytes 524320 | tf_op jit(solution)/shard_map/ppermute | solution.py:55
  37.0 1.3 collective-permute-done.4.refs_4_
  38.3 1.6 collective-permute-start.8
  40.4 12.2 %gate_up.5 = (f32[256,2048]{1,0:T(8,128)}, f32[256,128]{1,0:T(8,128)S(1)}) custom-call(s32[3,8]{1,0:T(4,128)S(1)} %get-tuple-element.229.blocks_ref, s32[5,5]{1,0:T(8,128)S(1)} %copy-done.3, bf16[256,1024]{1,0:T(8,128)(2,1)S(1)} %multiply_convert_fusion.1.refs_0_, bf16[256,1024]{1,0:T(8,128)(2,1)S(1)} %collective-permute-done.1.refs_1_, ...), custom_call_target="tpu_custom_call" | custom-call | flops 10737418240 | bytes 20971520 | tf_op jit(solution)/shard_map/gate_up/pallas_call | solution.py:181
  52.6 0.5 collective-permute-start.12
  53.1 1.6 collective-permute-start.11
  54.7 1.6 collective-permute-start.6
  56.3 2.3 %collective-permute-start.7 = (bf16[256,1024]{1,0:T(8,128)(2,1)S(1)}, bf16[256,1024]{1,0:T(8,128)(2,1)S(1)}, u32[]{:S(2)}, u32[]{:S(2)}) collective-permute-start(bf16[256,1024]{1,0:T(8,128)(2,1)S(1)} %multiply_convert_fusion.refs_0_), channel_id=1, source_target_pairs={{0,2},{4,0},{8,4},{12,8},{14,12},{10,14},{6,10},{2,6},{1,3},{5,1},... | collective-permute-start | bytes 1572872 | tf_op jit(solution)/shard_map/ppermute | solution.py:55
  58.7 15.1 %gate_up.6 = (f32[256,2048]{1,0:T(8,128)}, f32[256,128]{1,0:T(8,128)S(1)}) custom-call(s32[3,8]{1,0:T(4,128)S(1)} %get-tuple-element.229.blocks_ref, s32[5,7]{1,0:T(8,128)S(1)} %copy-done.2, bf16[256,1024]{1,0:T(8,128)(2,1)S(1)} %multiply_convert_fusion.1.refs_0_, bf16[256,1024]{1,0:T(8,128)(2,1)S(1)} %collective-permute-done.1.refs_1_, ...), custom_call_target="tpu_custom_call" | custom-call | flops 15032385536 | bytes 29360128 | tf_op jit(solution)/shard_map/gate_up/pallas_call | solution.py:181
  73.9 1.9 collective-permute-start.14
  75.9 11.5 %gate_up.7 = (bf16[256,2048]{1,0:T(8,128)(2,1)S(1)}, f32[256,128]{1,0:T(8,128)}) custom-call(s32[3,8]{1,0:T(4,128)S(1)} %get-tuple-element.229.blocks_ref, s32[5,4]{1,0:T(8,128)S(1)} %copy-done.1, bf16[256,1024]{1,0:T(8,128)(2,1)S(1)} %collective-permute-done.8.refs_5_.refs_0_, bf16[256,1024]{1,0:T(8,128)(2,1)S(1)} %collective-permute-done.9.refs_6_.refs_1_, ...), custom_call_target="tpu_custom_call" | custom-call | flops 8589934592 | bytes 16777216 | tf_op jit(solution)/shard_map/gate_up/pallas_call | solution.py:181
  87.6 1.7 collective-permute-start.15
  89.7 6.7 %down.4 = bf16[3,256,1024]{2,1,0:T(8,128)(2,1)S(1)} custom-call(s32[3,8]{1,0:T(4,128)S(1)} %get-tuple-element.230.tiles_ref, bf16[256,2048]{1,0:T(8,128)(2,1)S(1)} %get-tuple-element.143.refs_0_, bf16[2048,4096]{1,0:T(8,128)(2,1)} %refs_2_.3, bf16[2048,4096]{1,0:T(8,128)(2,1)} %collective-permute-done.17.refs_2_.refs_3_), custom_call_target="tpu_custom_call" | custom-call | flops 6442450944 | bytes 12582912 | tf_op jit(solution)/shard_map/down/pallas_call | solution.py:373
  96.4 4.2 %collective-permute-done.15.refs_5_ = bf16[256,1024]{1,0:T(8,128)(2,1)S(1)} collective-permute-done((bf16[256,1024]{1,0:T(8,128)(2,1)S(1)}, bf16[256,1024]{1,0:T(8,128)(2,1)S(1)}, u32[]{:S(2)}, u32[]{:S(2)}) %collective-permute-start.15) | collective-permute-done | bytes 524320 | tf_op jit(solution)/shard_map/ppermute | solution.py:55
  100.6 0.9 collective-permute-done.16.refs_6_
  101.6 0.9 collective-permute-start.19
  102.5 1.2 collective-permute-start.18
  103.7 1.6 collective-permute-start.20
  105.7 9.3 %down.5 = bf16[5,256,1024]{2,1,0:T(8,128)(2,1)S(1)} custom-call(s32[3,8]{1,0:T(4,128)S(1)} %get-tuple-element.230.tiles_ref, bf16[256,2048]{1,0:T(8,128)(2,1)S(1)} %get-tuple-element.143.refs_0_, bf16[2048,4096]{1,0:T(8,128)(2,1)} %refs_2_.3, bf16[2048,4096]{1,0:T(8,128)(2,1)} %collective-permute-done.17.refs_2_.refs_3_), custom_call_target="tpu_custom_call" | custom-call | flops 10737418240 | bytes 20971520 | tf_op jit(solution)/shard_map/down/pallas_call | solution.py:373
  115.3 1.6 collective-permute-start.22
  117.0 0.5 collective-permute-start.23
  117.5 16.8 %gate_up.8 = (bf16[256,1024]{1,0:T(8,128)(2,1)S(1)}, f32[256,128]{1,0:T(8,128)S(1)}) custom-call(s32[3,8]{1,0:T(4,128)S(1)} %get-tuple-element.229.blocks_ref, bf16[256,1024]{1,0:T(8,128)(2,1)S(1)} %multiply_convert_fusion.refs_0_, bf16[256,1024]{1,0:T(8,128)(2,1)S(1)} %collective-permute-done.6.refs_1_, ...), custom_call_target="tpu_custom_call" | custom-call | flops 17179869184 | bytes 33554432 | tf_op jit(solution)/shard_map/gate_up/pallas_call | solution.py:302
  134.7 0.9 collective-permute-start.25
  135.6 1.2 collective-permute-start.24
  136.8 16.7 %gate_up.9 = (bf16[256,1024]{1,0:T(8,128)(2,1)S(1)}, f32[256,128]{1,0:T(8,128)}) custom-call(s32[3,8]{1,0:T(4,128)S(1)} %get-tuple-element.229.blocks_ref, bf16[256,1024]{1,0:T(8,128)(2,1)S(1)} %multiply_convert_fusion.refs_0_, bf16[256,1024]{1,0:T(8,128)(2,1)S(1)} %collective-permute-done.6.refs_1_, bf16[256,1024]{1,0:T(8,128)(2,1)S(1)} %collective-permute-done.7.refs_2_, ...), custom_call_target="tpu_custom_call" | custom-call | flops 17179869184 | bytes 33554432 | tf_op jit(solution)/shard_map/gate_up/pallas_call | solution.py:302
  154.0 1.6 collective-permute-start.26
  155.6 0.5 collective-permute-start.27
  156.0 6.7 %down.6 = bf16[3,256,1024]{2,1,0:T(8,128)(2,1)S(1)} custom-call(s32[3,8]{1,0:T(4,128)S(1)} %get-tuple-element.230.tiles_ref, bf16[256,1024]{1,0:T(8,128)(2,1)S(1)} %get-tuple-element.183.refs_0_, bf16[256,1024]{1,0:T(8,128)(2,1)S(1)} %get-tuple-element.184.refs_1_, bf16[2048,4096]{1,0:T(8,128)(2,1)} %refs_2_.3, ...), custom_call_target="tpu_custom_call" | custom-call | flops 6442450944 | bytes 12582912 | tf_op jit(solution)/shard_map/down/pallas_call | solution.py:373
  162.8 2.0 collective-permute-done.26
  164.9 1.8 collective-permute-done.27
  166.7 1.7 collective-permute-start.28
  168.7 1.7 collective-permute-start.30
  170.7 2.3 %collective-permute-done.28 = bf16[64,1024]{1,0:T(8,128)(2,1)S(1)} collective-permute-done((bf16[64,1024]{1,0:T(8,128)(2,1)S(1)}, bf16[64,1024]{1,0:T(8,128)(2,1)S(1)}, u32[]{:S(2)}, u32[]{:S(2)}) %collective-permute-start.28) | collective-permute-done | bytes 131104 | tf_op jit(solution)/shard_map/ppermute | solution.py:55
  173.0 1.6 collective-permute-done.29
  174.8 1.1 collective-permute-done.30
  175.8 1.6 collective-permute-done.31
  177.5 1.9 collective-permute-start.36
  179.7 1.8 collective-permute-start.32
  181.7 9.3 %down.7 = bf16[5,256,1024]{2,1,0:T(8,128)(2,1)S(1)} custom-call(s32[3,8]{1,0:T(4,128)S(1)} %get-tuple-element.230.tiles_ref, bf16[256,1024]{1,0:T(8,128)(2,1)S(1)} %get-tuple-element.183.refs_0_, bf16[256,1024]{1,0:T(8,128)(2,1)S(1)} %get-tuple-element.184.refs_1_, bf16[2048,4096]{1,0:T(8,128)(2,1)} %refs_2_.3, ...), custom_call_target="tpu_custom_call" | custom-call | flops 10737418240 | bytes 20971520 | tf_op jit(solution)/shard_map/down/pallas_call | solution.py:373
  191.0 3.2 %collective-permute-done.33 = bf16[128,1024]{1,0:T(8,128)(2,1)S(1)} collective-permute-done((bf16[128,1024]{1,0:T(8,128)(2,1)S(1)}, bf16[128,1024]{1,0:T(8,128)(2,1)S(1)}, u32[]{:S(2)}, u32[]{:S(2)}) %collective-permute-start.33) | collective-permute-done | bytes 262176 | tf_op jit(solution)/shard_map/ppermute | solution.py:55
  194.7 1.8 collective-permute-start.34
  197.0 1.8 collective-permute-start.40
  198.8 4.8 %collective-permute-done.35 = bf16[128,1024]{1,0:T(8,128)(2,1)S(1)} collective-permute-done((bf16[128,1024]{1,0:T(8,128)(2,1)S(1)}, bf16[128,1024]{1,0:T(8,128)(2,1)S(1)}, u32[]{:S(2)}, u32[]{:S(2)}) %collective-permute-start.35) | collective-permute-done | bytes 262176 | tf_op jit(solution)/shard_map/ppermute | solution.py:55
  204.1 1.8 collective-permute-start.38
  205.9 0.5 collective-permute-done.41
  207.1 1.6 collective-permute-start.43
  208.7 0.5 fusion.15
  209.2 4.1 %collective-permute-done.42 = bf16[128,1024]{1,0:T(8,128)(2,1)S(1)} collective-permute-done((bf16[128,1024]{1,0:T(8,128)(2,1)S(1)}, bf16[128,1024]{1,0:T(8,128)(2,1)S(1)}, u32[]{:S(2)}, u32[]{:S(2)}) %collective-permute-start.42) | collective-permute-done | bytes 262176 | tf_op jit(solution)/shard_map/ppermute | solution.py:55
  213.5 0.5 fusion.33
  214.0 1.0 pad_maximum_fusion.1
  (88 shorter events, 6.7 us)
Async XLA Ops:
  0.0 5.3 %copy-start = (f32[8192]{0:T(1024)S(1)}, f32[8192]{0:T(1024)}, u32[]{:S(2)}) copy-start(f32[8192]{0:T(1024)} %param.18) | copy-start | bytes 98308
  0.8 6.0 %collective-permute-start = (f32[3,1024]{1,0:T(4,128)S(1)}, f32[3,1024]{1,0:T(4,128)S(1)}, u32[]{:S(2)}, u32[]{:S(2)}) collective-permute-start(f32[3,1024]{1,0:T(4,128)S(1)} %multiply_add_fusion.2), channel_id=1, source_target_pairs={{0,1},{2,3},{4,5},{6,7},{8,9},{10,11},{12,13},{14,15},{16,17},{18,... | collective-permute-start | bytes 36872 | tf_op jit(solution)/shard_map/ppermute | solution.py:453
  6.2 19.6 %copy-start.4 = (bf16[512,1024]{1,0:T(8,128)(2,1)S(1)}, bf16[512,1024]{1,0:T(8,128)(2,1)}, u32[]{:S(2)}) copy-start(bf16[512,1024]{1,0:T(8,128)(2,1)} %param.14) | copy-start | bytes 3145732
  6.2 19.6 %copy-start.9 = (f32[1024]{0:T(1024)S(1)}, f32[1024]{0:T(1024)}, u32[]{:S(2)}) copy-start(f32[1024]{0:T(1024)} %param.15) | copy-start | bytes 12292
  6.8 33.6 %copy-start.3 = (s32[5,5]{1,0:T(8,128)S(1)}, s32[5,5]{1,0:T(8,128)}, u32[]{:S(2)}) copy-start(s32[5,5]{1,0:T(8,128)} %constant.34.clone.units_ref) | copy-start | bytes 304
  6.8 33.5 %collective-permute-start.5 = (bf16[4096,2048]{1,0:T(8,128)(2,1)}, bf16[4096,2048]{1,0:T(8,128)(2,1)}, u32[]{:S(2)}, u32[]{:S(2)}) collective-permute-start(bf16[4096,2048]{1,0:T(8,128)(2,1)} %refs_10_.5), channel_id=1, source_target_pairs={{0,1},{1,0},{2,3},{3,2},{4,5},{5,4},{6,7},{7,6},{8,9},{9,8},{10,11... | collective-permute-start | bytes 50331656 | tf_op jit(solution)/shard_map/ppermute | solution.py:59
  6.9 49.5 %collective-permute-start.10 = (bf16[4096,2048]{1,0:T(8,128)(2,1)}, bf16[4096,2048]{1,0:T(8,128)(2,1)}, u32[]{:S(2)}, u32[]{:S(2)}) collective-permute-start(bf16[4096,2048]{1,0:T(8,128)(2,1)} %refs_12_.3), channel_id=1, source_target_pairs={{0,1},{1,0},{2,3},{3,2},{4,5},{5,4},{6,7},{7,6},{8,9},{9,8},{10,11... | collective-permute-start | bytes 50331656 | tf_op jit(solution)/shard_map/ppermute | solution.py:59
  7.4 82.3 %collective-permute-start.17 = (bf16[2048,4096]{1,0:T(8,128)(2,1)}, bf16[2048,4096]{1,0:T(8,128)(2,1)}, u32[]{:S(2)}, u32[]{:S(2)}) collective-permute-start(bf16[2048,4096]{1,0:T(8,128)(2,1)} %refs_2_.3), channel_id=1, source_target_pairs={{0,1},{1,0},{2,3},{3,2},{4,5},{5,4},{6,7},{7,6},{8,9},{9,8},{10,11... | collective-permute-start | bytes 50331656 | tf_op jit(solution)/shard_map/ppermute | solution.py:59
  7.4 14.9 %collective-permute-start.1 = (bf16[256,1024]{1,0:T(8,128)(2,1)S(1)}, bf16[256,1024]{1,0:T(8,128)(2,1)S(1)}, u32[]{:S(2)}, u32[]{:S(2)}) collective-permute-start(bf16[256,1024]{1,0:T(8,128)(2,1)S(1)} %multiply_convert_fusion.1.refs_0_), channel_id=1, source_target_pairs={{0,4},{4,8},{8,12},{12,14},{14,10},{10,6},{6,2},{2,0},{1,5},{5,9},... | collective-permute-start | bytes 1572872 | tf_op jit(solution)/shard_map/ppermute | solution.py:55
  9.9 14.0 %collective-permute-start.2 = (bf16[256,1024]{1,0:T(8,128)(2,1)S(1)}, bf16[256,1024]{1,0:T(8,128)(2,1)S(1)}, u32[]{:S(2)}, u32[]{:S(2)}) collective-permute-start(bf16[256,1024]{1,0:T(8,128)(2,1)S(1)} %multiply_convert_fusion.1.refs_0_), channel_id=1, source_target_pairs={{0,2},{4,0},{8,4},{12,8},{14,12},{10,14},{6,10},{2,6},{1,3},{5,1},... | collective-permute-start | bytes 1572872 | tf_op jit(solution)/shard_map/ppermute | solution.py:55
  23.8 13.2 %collective-permute-start.3 = (bf16[256,1024]{1,0:T(8,128)(2,1)S(1)}, bf16[256,1024]{1,0:T(8,128)(2,1)S(1)}, u32[]{:S(2)}, u32[]{:S(2)}) collective-permute-start(bf16[256,1024]{1,0:T(8,128)(2,1)S(1)} %collective-permute-done.1.refs_1_), channel_id=1, source_target_pairs={{0,4},{4,8},{8,12},{12,14},{14,10},{10,6},{6,2},{2,0},{1,5},{5,9},... | collective-permute-start | bytes 1572872 | tf_op jit(solution)/shard_map/ppermute | solution.py:55
  25.4 12.9 %collective-permute-start.4 = (bf16[256,1024]{1,0:T(8,128)(2,1)S(1)}, bf16[256,1024]{1,0:T(8,128)(2,1)S(1)}, u32[]{:S(2)}, u32[]{:S(2)}) collective-permute-start(bf16[256,1024]{1,0:T(8,128)(2,1)S(1)} %collective-permute-done.2.refs_2_), channel_id=1, source_target_pairs={{0,2},{4,0},{8,4},{12,8},{14,12},{10,14},{6,10},{2,6},{1,3},{5,1},... | collective-permute-start | bytes 1572872 | tf_op jit(solution)/shard_map/ppermute | solution.py:55
  38.3 14.3 %collective-permute-start.8 = (bf16[256,1024]{1,0:T(8,128)(2,1)S(1)}, bf16[256,1024]{1,0:T(8,128)(2,1)S(1)}, u32[]{:S(2)}, u32[]{:S(2)}) collective-permute-start(bf16[256,1024]{1,0:T(8,128)(2,1)S(1)} %collective-permute-done.3.refs_3_), channel_id=1, source_target_pairs={{0,4},{4,8},{8,12},{12,14},{14,10},{10,6},{6,2},{2,0},{1,5},{5,9},... | collective-permute-start | bytes 1572872 | tf_op jit(solution)/shard_map/ppermute | solution.py:55
  39.9 12.7 %collective-permute-start.9 = (bf16[256,1024]{1,0:T(8,128)(2,1)S(1)}, bf16[256,1024]{1,0:T(8,128)(2,1)S(1)}, u32[]{:S(2)}, u32[]{:S(2)}) collective-permute-start(bf16[256,1024]{1,0:T(8,128)(2,1)S(1)} %collective-permute-done.4.refs_4_), channel_id=1, source_target_pairs={{0,2},{4,0},{8,4},{12,8},{14,12},{10,14},{6,10},{2,6},{1,3},{5,1},... | collective-permute-start | bytes 1572872 | tf_op jit(solution)/shard_map/ppermute | solution.py:55
  40.4 18.3 %copy-start.2 = (s32[5,7]{1,0:T(8,128)S(1)}, s32[5,7]{1,0:T(8,128)}, u32[]{:S(2)}) copy-start(s32[5,7]{1,0:T(8,128)} %constant.35.clone.units_ref) | copy-start | bytes 424
  52.6 21.1 %collective-permute-start.12 = (bf16[128,1024]{1,0:T(8,128)(2,1)S(1)}, bf16[128,1024]{1,0:T(8,128)(2,1)S(1)}, u32[]{:S(2)}, u32[]{:S(2)}) collective-permute-start(bf16[128,1024]{1,0:T(8,128)(2,1)S(1)} %slice.332), channel_id=1, source_target_pairs={{0,2},{4,0},{8,4},{12,8},{14,12},{10,14},{6,10},{2,6},{1,3},{5,1},... | collective-permute-start | bytes 786440 | tf_op jit(solution)/shard_map/ppermute | solution.py:55
  53.1 20.6 %collective-permute-start.11 = (bf16[128,1024]{1,0:T(8,128)(2,1)S(1)}, bf16[128,1024]{1,0:T(8,128)(2,1)S(1)}, u32[]{:S(2)}, u32[]{:S(2)}) collective-permute-start(bf16[128,1024]{1,0:T(8,128)(2,1)S(1)} %slice.331), channel_id=1, source_target_pairs={{0,4},{4,8},{8,12},{12,14},{14,10},{10,6},{6,2},{2,0},{1,5},{5,9},... | collective-permute-start | bytes 786440 | tf_op jit(solution)/shard_map/ppermute | solution.py:55
  54.7 19.1 %collective-permute-start.6 = (bf16[256,1024]{1,0:T(8,128)(2,1)S(1)}, bf16[256,1024]{1,0:T(8,128)(2,1)S(1)}, u32[]{:S(2)}, u32[]{:S(2)}) collective-permute-start(bf16[256,1024]{1,0:T(8,128)(2,1)S(1)} %multiply_convert_fusion.refs_0_), channel_id=1, source_target_pairs={{0,4},{4,8},{8,12},{12,14},{14,10},{10,6},{6,2},{2,0},{1,5},{5,9},... | collective-permute-start | bytes 1572872 | tf_op jit(solution)/shard_map/ppermute | solution.py:55
  56.3 17.5 %collective-permute-start.7 = (bf16[256,1024]{1,0:T(8,128)(2,1)S(1)}, bf16[256,1024]{1,0:T(8,128)(2,1)S(1)}, u32[]{:S(2)}, u32[]{:S(2)}) collective-permute-start(bf16[256,1024]{1,0:T(8,128)(2,1)S(1)} %multiply_convert_fusion.refs_0_), channel_id=1, source_target_pairs={{0,2},{4,0},{8,4},{12,8},{14,12},{10,14},{6,10},{2,6},{1,3},{5,1},... | collective-permute-start | bytes 1572872 | tf_op jit(solution)/shard_map/ppermute | solution.py:55
  58.7 17.2 %copy-start.1 = (s32[5,4]{1,0:T(8,128)S(1)}, s32[5,4]{1,0:T(8,128)}, u32[]{:S(2)}) copy-start(s32[5,4]{1,0:T(8,128)} %constant.36.clone.units_ref) | copy-start | bytes 244
  73.8 13.7 %collective-permute-start.13 = (bf16[256,1024]{1,0:T(8,128)(2,1)S(1)}, bf16[256,1024]{1,0:T(8,128)(2,1)S(1)}, u32[]{:S(2)}, u32[]{:S(2)}) collective-permute-start(bf16[256,1024]{1,0:T(8,128)(2,1)S(1)} %collective-permute-done.6.refs_1_), channel_id=1, source_target_pairs={{0,4},{4,8},{8,12},{12,14},{14,10},{10,6},{6,2},{2,0},{1,5},{5,9},... | collective-permute-start | bytes 1572872 | tf_op jit(solution)/shard_map/ppermute | solution.py:55
  73.9 13.7 %collective-permute-start.14 = (bf16[256,1024]{1,0:T(8,128)(2,1)S(1)}, bf16[256,1024]{1,0:T(8,128)(2,1)S(1)}, u32[]{:S(2)}, u32[]{:S(2)}) collective-permute-start(bf16[256,1024]{1,0:T(8,128)(2,1)S(1)} %collective-permute-done.7.refs_2_), channel_id=1, source_target_pairs={{0,2},{4,0},{8,4},{12,8},{14,12},{10,14},{6,10},{2,6},{1,3},{5,1},... | collective-permute-start | bytes 1572872 | tf_op jit(solution)/shard_map/ppermute | solution.py:55
  87.6 13.0 %collective-permute-start.15 = (bf16[256,1024]{1,0:T(8,128)(2,1)S(1)}, bf16[256,1024]{1,0:T(8,128)(2,1)S(1)}, u32[]{:S(2)}, u32[]{:S(2)}) collective-permute-start(bf16[256,1024]{1,0:T(8,128)(2,1)S(1)} %collective-permute-done.13.refs_3_), channel_id=1, source_target_pairs={{0,4},{4,8},{8,12},{12,14},{14,10},{10,6},{6,2},{2,0},{1,5},{5,9},... | collective-permute-start | bytes 1572872 | tf_op jit(solution)/shard_map/ppermute | solution.py:55
  89.4 12.2 %collective-permute-start.16 = (bf16[256,1024]{1,0:T(8,128)(2,1)S(1)}, bf16[256,1024]{1,0:T(8,128)(2,1)S(1)}, u32[]{:S(2)}, u32[]{:S(2)}) collective-permute-start(bf16[256,1024]{1,0:T(8,128)(2,1)S(1)} %collective-permute-done.14.refs_4_), channel_id=1, source_target_pairs={{0,2},{4,0},{8,4},{12,8},{14,12},{10,14},{6,10},{2,6},{1,3},{5,1},... | collective-permute-start | bytes 1572872 | tf_op jit(solution)/shard_map/ppermute | solution.py:55
  100.6 14.4 %copy-start.7 = (bf16[256,1024]{1,0:T(8,128)(2,1)}, bf16[256,1024]{1,0:T(8,128)(2,1)S(1)}, u32[]{:S(2)}) copy-start(bf16[256,1024]{1,0:T(8,128)(2,1)S(1)} %collective-permute-done.15.refs_5_) | copy-start | bytes 1572868
  101.6 13.5 %copy-start.8 = (bf16[256,1024]{1,0:T(8,128)(2,1)}, bf16[256,1024]{1,0:T(8,128)(2,1)S(1)}, u32[]{:S(2)}) copy-start(bf16[256,1024]{1,0:T(8,128)(2,1)S(1)} %collective-permute-done.16.refs_6_) | copy-start | bytes 1572868
  101.6 15.9 %collective-permute-start.19 = (bf16[128,1024]{1,0:T(8,128)(2,1)S(1)}, bf16[128,1024]{1,0:T(8,128)(2,1)S(1)}, u32[]{:S(2)}, u32[]{:S(2)}) collective-permute-start(bf16[128,1024]{1,0:T(8,128)(2,1)S(1)} %slice.334), channel_id=1, source_target_pairs={{0,2},{4,0},{8,4},{12,8},{14,12},{10,14},{6,10},{2,6},{1,3},{5,1},... | collective-permute-start | bytes 786440 | tf_op jit(solution)/shard_map/ppermute | solution.py:55
  102.5 15.0 %collective-permute-start.18 = (bf16[128,1024]{1,0:T(8,128)(2,1)S(1)}, bf16[128,1024]{1,0:T(8,128)(2,1)S(1)}, u32[]{:S(2)}, u32[]{:S(2)}) collective-permute-start(bf16[128,1024]{1,0:T(8,128)(2,1)S(1)} %slice.333), channel_id=1, source_target_pairs={{0,4},{4,8},{8,12},{12,14},{14,10},{10,6},{6,2},{2,0},{1,5},{5,9},... | collective-permute-start | bytes 786440 | tf_op jit(solution)/shard_map/ppermute | solution.py:55
  103.7 11.4 %collective-permute-start.20 = (bf16[128,1024]{1,0:T(8,128)(2,1)S(1)}, bf16[128,1024]{1,0:T(8,128)(2,1)S(1)}, u32[]{:S(2)}, u32[]{:S(2)}) collective-permute-start(bf16[128,1024]{1,0:T(8,128)(2,1)S(1)} %get-tuple-element.144), channel_id=1, source_target_pairs={{0,4},{4,8},{8,12},{12,14},{14,10},{10,6},{6,2},{2,0},{1,5},{5,9},... | collective-permute-start | bytes 786440 | tf_op jit(solution)/shard_map/ppermute | solution.py:55
  105.3 9.8 %collective-permute-start.21 = (bf16[128,1024]{1,0:T(8,128)(2,1)S(1)}, bf16[128,1024]{1,0:T(8,128)(2,1)S(1)}, u32[]{:S(2)}, u32[]{:S(2)}) collective-permute-start(bf16[128,1024]{1,0:T(8,128)(2,1)S(1)} %get-tuple-element.145), channel_id=1, source_target_pairs={{0,2},{4,0},{8,4},{12,8},{14,12},{10,14},{6,10},{2,6},{1,3},{5,1},... | collective-permute-start | bytes 786440 | tf_op jit(solution)/shard_map/ppermute | solution.py:55
  115.3 18.9 %collective-permute-start.22 = (bf16[256,1024]{1,0:T(8,128)(2,1)S(1)}, bf16[256,1024]{1,0:T(8,128)(2,1)S(1)}, u32[]{:S(2)}, u32[]{:S(2)}) collective-permute-start(bf16[256,1024]{1,0:T(8,128)(2,1)S(1)} %pad_maximum_fusion.2), channel_id=1, source_target_pairs={{0,4},{4,8},{8,12},{12,14},{14,10},{10,6},{6,2},{2,0},{1,5},{5,9},... | collective-permute-start | bytes 1572872 | tf_op jit(solution)/shard_map/ppermute | solution.py:55
  117.0 17.3 %collective-permute-start.23 = (bf16[256,1024]{1,0:T(8,128)(2,1)S(1)}, bf16[256,1024]{1,0:T(8,128)(2,1)S(1)}, u32[]{:S(2)}, u32[]{:S(2)}) collective-permute-start(bf16[256,1024]{1,0:T(8,128)(2,1)S(1)} %pad_maximum_fusion.3), channel_id=1, source_target_pairs={{0,2},{4,0},{8,4},{12,8},{14,12},{10,14},{6,10},{2,6},{1,3},{5,1},... | collective-permute-start | bytes 1572872 | tf_op jit(solution)/shard_map/ppermute | solution.py:55
  134.7 18.8 %collective-permute-start.25 = (bf16[256,1024]{1,0:T(8,128)(2,1)S(1)}, bf16[256,1024]{1,0:T(8,128)(2,1)S(1)}, u32[]{:S(2)}, u32[]{:S(2)}) collective-permute-start(bf16[256,1024]{1,0:T(8,128)(2,1)S(1)} %get-tuple-element.205), channel_id=1, source_target_pairs={{0,2},{4,0},{8,4},{12,8},{14,12},{10,14},{6,10},{2,6},{1,3},{5,1},... | collective-permute-start | bytes 1572872 | tf_op jit(solution)/shard_map/ppermute | solution.py:55
  135.6 17.9 %collective-permute-start.24 = (bf16[256,1024]{1,0:T(8,128)(2,1)S(1)}, bf16[256,1024]{1,0:T(8,128)(2,1)S(1)}, u32[]{:S(2)}, u32[]{:S(2)}) collective-permute-start(bf16[256,1024]{1,0:T(8,128)(2,1)S(1)} %get-tuple-element.206), channel_id=1, source_target_pairs={{0,4},{4,8},{8,12},{12,14},{14,10},{10,6},{6,2},{2,0},{1,5},{5,9},... | collective-permute-start | bytes 1572872 | tf_op jit(solution)/shard_map/ppermute | solution.py:55
  154.0 10.9 %collective-permute-start.26 = (bf16[256,1024]{1,0:T(8,128)(2,1)S(1)}, bf16[256,1024]{1,0:T(8,128)(2,1)S(1)}, u32[]{:S(2)}, u32[]{:S(2)}) collective-permute-start(bf16[256,1024]{1,0:T(8,128)(2,1)S(1)} %get-tuple-element.203), channel_id=1, source_target_pairs={{0,4},{4,8},{8,12},{12,14},{14,10},{10,6},{6,2},{2,0},{1,5},{5,9},... | collective-permute-start | bytes 1572872 | tf_op jit(solution)/shard_map/ppermute | solution.py:55
  155.6 11.1 %collective-permute-start.27 = (bf16[256,1024]{1,0:T(8,128)(2,1)S(1)}, bf16[256,1024]{1,0:T(8,128)(2,1)S(1)}, u32[]{:S(2)}, u32[]{:S(2)}) collective-permute-start(bf16[256,1024]{1,0:T(8,128)(2,1)S(1)} %get-tuple-element.204), channel_id=1, source_target_pairs={{0,2},{4,0},{8,4},{12,8},{14,12},{10,14},{6,10},{2,6},{1,3},{5,1},... | collective-permute-start | bytes 1572872 | tf_op jit(solution)/shard_map/ppermute | solution.py:55
  166.7 6.4 %collective-permute-start.28 = (bf16[64,1024]{1,0:T(8,128)(2,1)S(1)}, bf16[64,1024]{1,0:T(8,128)(2,1)S(1)}, u32[]{:S(2)}, u32[]{:S(2)}) collective-permute-start(bf16[64,1024]{1,0:T(8,128)(2,1)S(1)} %get-tuple-element.175), channel_id=1, source_target_pairs={{0,4},{4,8},{8,12},{12,14},{14,10},{10,6},{6,2},{2,0},{1,5},{5,9},... | collective-permute-start | bytes 393224 | tf_op jit(solution)/shard_map/ppermute | solution.py:55
  168.3 6.3 %collective-permute-start.29 = (bf16[64,1024]{1,0:T(8,128)(2,1)S(1)}, bf16[64,1024]{1,0:T(8,128)(2,1)S(1)}, u32[]{:S(2)}, u32[]{:S(2)}) collective-permute-start(bf16[64,1024]{1,0:T(8,128)(2,1)S(1)} %get-tuple-element.176), channel_id=1, source_target_pairs={{0,2},{4,0},{8,4},{12,8},{14,12},{10,14},{6,10},{2,6},{1,3},{5,1},... | collective-permute-start | bytes 393224 | tf_op jit(solution)/shard_map/ppermute | solution.py:55
  168.7 7.1 %collective-permute-start.30 = (bf16[64,1024]{1,0:T(8,128)(2,1)S(1)}, bf16[64,1024]{1,0:T(8,128)(2,1)S(1)}, u32[]{:S(2)}, u32[]{:S(2)}) collective-permute-start(bf16[64,1024]{1,0:T(8,128)(2,1)S(1)} %get-tuple-element.177), channel_id=1, source_target_pairs={{0,4},{4,8},{8,12},{12,14},{14,10},{10,6},{6,2},{2,0},{1,5},{5,9},... | collective-permute-start | bytes 393224 | tf_op jit(solution)/shard_map/ppermute | solution.py:55
  170.4 7.1 %collective-permute-start.31 = (bf16[64,1024]{1,0:T(8,128)(2,1)S(1)}, bf16[64,1024]{1,0:T(8,128)(2,1)S(1)}, u32[]{:S(2)}, u32[]{:S(2)}) collective-permute-start(bf16[64,1024]{1,0:T(8,128)(2,1)S(1)} %get-tuple-element.178), channel_id=1, source_target_pairs={{0,2},{4,0},{8,4},{12,8},{14,12},{10,14},{6,10},{2,6},{1,3},{5,1},... | collective-permute-start | bytes 393224 | tf_op jit(solution)/shard_map/ppermute | solution.py:55
  177.5 19.0 %collective-permute-start.36 = (bf16[128,1024]{1,0:T(8,128)(2,1)S(1)}, bf16[128,1024]{1,0:T(8,128)(2,1)S(1)}, u32[]{:S(2)}, u32[]{:S(2)}) collective-permute-start(bf16[128,1024]{1,0:T(8,128)(2,1)S(1)} %pad_maximum_fusion.6), channel_id=1, source_target_pairs={{0,4},{4,8},{8,12},{12,14},{14,10},{10,6},{6,2},{2,0},{1,5},{5,9},... | collective-permute-start | bytes 786440 | tf_op jit(solution)/shard_map/ppermute | solution.py:55
  179.4 17.1 %collective-permute-start.37 = (bf16[128,1024]{1,0:T(8,128)(2,1)S(1)}, bf16[128,1024]{1,0:T(8,128)(2,1)S(1)}, u32[]{:S(2)}, u32[]{:S(2)}) collective-permute-start(bf16[128,1024]{1,0:T(8,128)(2,1)S(1)} %pad_maximum_fusion.7), channel_id=1, source_target_pairs={{0,2},{4,0},{8,4},{12,8},{14,12},{10,14},{6,10},{2,6},{1,3},{5,1},... | collective-permute-start | bytes 786440 | tf_op jit(solution)/shard_map/ppermute | solution.py:55
  179.7 11.4 %collective-permute-start.32 = (bf16[128,1024]{1,0:T(8,128)(2,1)S(1)}, bf16[128,1024]{1,0:T(8,128)(2,1)S(1)}, u32[]{:S(2)}, u32[]{:S(2)}) collective-permute-start(bf16[128,1024]{1,0:T(8,128)(2,1)S(1)} %pad_maximum_fusion.4), channel_id=1, source_target_pairs={{0,4},{4,8},{8,12},{12,14},{14,10},{10,6},{6,2},{2,0},{1,5},{5,9},... | collective-permute-start | bytes 786440 | tf_op jit(solution)/shard_map/ppermute | solution.py:55
  181.5 12.8 %collective-permute-start.33 = (bf16[128,1024]{1,0:T(8,128)(2,1)S(1)}, bf16[128,1024]{1,0:T(8,128)(2,1)S(1)}, u32[]{:S(2)}, u32[]{:S(2)}) collective-permute-start(bf16[128,1024]{1,0:T(8,128)(2,1)S(1)} %pad_maximum_fusion.5), channel_id=1, source_target_pairs={{0,2},{4,0},{8,4},{12,8},{14,12},{10,14},{6,10},{2,6},{1,3},{5,1},... | collective-permute-start | bytes 786440 | tf_op jit(solution)/shard_map/ppermute | solution.py:55
  194.5 9.1 %collective-permute-start.35 = (bf16[128,1024]{1,0:T(8,128)(2,1)S(1)}, bf16[128,1024]{1,0:T(8,128)(2,1)S(1)}, u32[]{:S(2)}, u32[]{:S(2)}) collective-permute-start(bf16[128,1024]{1,0:T(8,128)(2,1)S(1)} %get-tuple-element.201), channel_id=1, source_target_pairs={{0,2},{4,0},{8,4},{12,8},{14,12},{10,14},{6,10},{2,6},{1,3},{5,1},... | collective-permute-start | bytes 786440 | tf_op jit(solution)/shard_map/ppermute | solution.py:55
  194.7 14.0 %copy-start.5 = (bf16[512,1024]{1,0:T(8,128)(2,1)S(1)}, bf16[512,1024]{1,0:T(8,128)(2,1)}, u32[]{:S(2)}) copy-start(bf16[512,1024]{1,0:T(8,128)(2,1)} %param.14) | copy-start | bytes 3145732
  194.7 14.0 %copy-start.6 = (bf16[512,1024]{1,0:T(8,128)(2,1)S(1)}, bf16[512,1024]{1,0:T(8,128)(2,1)}, u32[]{:S(2)}) copy-start(bf16[512,1024]{1,0:T(8,128)(2,1)} %param.13) | copy-start | bytes 3145732
  194.7 14.0 %copy-start.10 = (f32[1024]{0:T(1024)S(1)}, f32[1024]{0:T(1024)}, u32[]{:S(2)}) copy-start(f32[1024]{0:T(1024)} %param.15) | copy-start | bytes 12292
  194.7 8.9 %collective-permute-start.34 = (bf16[128,1024]{1,0:T(8,128)(2,1)S(1)}, bf16[128,1024]{1,0:T(8,128)(2,1)S(1)}, u32[]{:S(2)}, u32[]{:S(2)}) collective-permute-start(bf16[128,1024]{1,0:T(8,128)(2,1)S(1)} %get-tuple-element.202), channel_id=1, source_target_pairs={{0,4},{4,8},{8,12},{12,14},{14,10},{10,6},{6,2},{2,0},{1,5},{5,9},... | collective-permute-start | bytes 786440 | tf_op jit(solution)/shard_map/ppermute | solution.py:55
  196.8 9.7 %collective-permute-start.41 = (bf16[128,1024]{1,0:T(8,128)(2,1)S(1)}, bf16[128,1024]{1,0:T(8,128)(2,1)S(1)}, u32[]{:S(2)}, u32[]{:S(2)}) collective-permute-start(bf16[128,1024]{1,0:T(8,128)(2,1)S(1)} %get-tuple-element.199), channel_id=1, source_target_pairs={{0,2},{4,0},{8,4},{12,8},{14,12},{10,14},{6,10},{2,6},{1,3},{5,1},... | collective-permute-start | bytes 786440 | tf_op jit(solution)/shard_map/ppermute | solution.py:55
  197.0 9.4 %collective-permute-start.40 = (bf16[128,1024]{1,0:T(8,128)(2,1)S(1)}, bf16[128,1024]{1,0:T(8,128)(2,1)S(1)}, u32[]{:S(2)}, u32[]{:S(2)}) collective-permute-start(bf16[128,1024]{1,0:T(8,128)(2,1)S(1)} %get-tuple-element.200), channel_id=1, source_target_pairs={{0,4},{4,8},{8,12},{12,14},{14,10},{10,6},{6,2},{2,0},{1,5},{5,9},... | collective-permute-start | bytes 786440 | tf_op jit(solution)/shard_map/ppermute | solution.py:55
  203.8 9.6 %collective-permute-start.39 = (bf16[128,1024]{1,0:T(8,128)(2,1)S(1)}, bf16[128,1024]{1,0:T(8,128)(2,1)S(1)}, u32[]{:S(2)}, u32[]{:S(2)}) collective-permute-start(bf16[128,1024]{1,0:T(8,128)(2,1)S(1)} %get-tuple-element.197), channel_id=1, source_target_pairs={{0,2},{4,0},{8,4},{12,8},{14,12},{10,14},{6,10},{2,6},{1,3},{5,1},... | collective-permute-start | bytes 786440 | tf_op jit(solution)/shard_map/ppermute | solution.py:55
  204.1 9.3 %collective-permute-start.38 = (bf16[128,1024]{1,0:T(8,128)(2,1)S(1)}, bf16[128,1024]{1,0:T(8,128)(2,1)S(1)}, u32[]{:S(2)}, u32[]{:S(2)}) collective-permute-start(bf16[128,1024]{1,0:T(8,128)(2,1)S(1)} %get-tuple-element.198), channel_id=1, source_target_pairs={{0,4},{4,8},{8,12},{12,14},{14,10},{10,6},{6,2},{2,0},{1,5},{5,9},... | collective-permute-start | bytes 786440 | tf_op jit(solution)/shard_map/ppermute | solution.py:55
  206.6 6.7 %collective-permute-start.42 = (bf16[128,1024]{1,0:T(8,128)(2,1)S(1)}, bf16[128,1024]{1,0:T(8,128)(2,1)S(1)}, u32[]{:S(2)}, u32[]{:S(2)}) collective-permute-start(bf16[128,1024]{1,0:T(8,128)(2,1)S(1)} %get-tuple-element.195), channel_id=1, source_target_pairs={{0,4},{4,8},{8,12},{12,14},{14,10},{10,6},{6,2},{2,0},{1,5},{5,9},... | collective-permute-start | bytes 786440 | tf_op jit(solution)/shard_map/ppermute | solution.py:55
  207.1 6.4 %collective-permute-start.43 = (bf16[128,1024]{1,0:T(8,128)(2,1)S(1)}, bf16[128,1024]{1,0:T(8,128)(2,1)S(1)}, u32[]{:S(2)}, u32[]{:S(2)}) collective-permute-start(bf16[128,1024]{1,0:T(8,128)(2,1)S(1)} %get-tuple-element.196), channel_id=1, source_target_pairs={{0,2},{4,0},{8,4},{12,8},{14,12},{10,14},{6,10},{2,6},{1,3},{5,1},... | collective-permute-start | bytes 786440 | tf_op jit(solution)/shard_map/ppermute | solution.py:55

commit v13 on v12

--- a/solution.py
+++ b/solution.py
@@ -110,6 +110,8 @@
         gather_pieces(0, lambda copy: copy.start())
         for number in range(min(DEEP - 1, length)):
             fetch(jnp.int32(number))
+        for place in range(1, len(pieces)):
+            gather_pieces(place, lambda copy: copy.start())
         partials(lambda copy: copy.start())
         sums[...] = jnp.zeros_like(sums)
         stat_ref[...] = before_ref[...]
@@ -124,8 +126,6 @@
         @pl.when((place == wanted) & (units_ref[3, step] == 1))
         def arrived(wanted=wanted):
             gather_pieces(wanted, lambda copy: copy.wait())
-            if wanted + 1 < len(pieces):
-                gather_pieces(wanted + 1, lambda copy: copy.start())
 
     block = stacked[:, pl.ds(pl.multiple_of(place * width, width), width)]
 
@@ -251,6 +251,8 @@
         gather_pieces(0, lambda copy: copy.start())
         for number in range(min(DEEP - 1, count)):
             fetch(jnp.int32(number))
+        for wanted in range(1, count):
+            gather_pieces(wanted, lambda copy: copy.start())
         sums[...] = jnp.zeros_like(sums)
         stat[...] = before_ref[...]
 
@@ -263,8 +265,6 @@
         @pl.when(step == wanted)
         def arrived(wanted=wanted):
             gather_pieces(wanted, lambda copy: copy.wait())
-            if wanted + 1 < count:
-                gather_pieces(wanted + 1, lambda copy: copy.start())
 
     slot = lax.rem(step, DEEP)
     block = stacked[:, pl.ds(pl.multiple_of(step * width, width), width)]
@@ -467,7 +467,8 @@
             )
         return (result.astype(jnp.bfloat16).astype(jnp.float32) * own_gain).astype(jnp.bfloat16)
 
-    size = row_count // 2
+    size_b = 3 * row_count // 8
+    size_a = row_count - size_b
     early = min(3, count - 1)
 
     def pieces_of(block, steps):
@@ -496,18 +497,18 @@
 
         return term
 
-    block_a = convolve(noisy_input, self_cond, None, size, size)
+    block_a = convolve(noisy_input, self_cond, None, size_b, size_a)
     later = after((gate_weight, up_weight, down_weight), edges, block_a)
     other_gate, other_up, other_down = (swap(weight) for weight in later)
     weights = (gate_weight, other_gate, up_weight, other_up)
-    nothing = (jnp.zeros((size, LANES), jnp.float32), frozenset())
+    nothing_a, nothing_b = ((jnp.zeros((size, LANES), jnp.float32), frozenset()) for size in (size_a, size_b))
     steps_a = gather_step(block_a, [], half)
     later = after((noisy_input, self_cond, edges), steps_a[0])
-    block_b = convolve(*later, 0, size)
+    block_b = convolve(*later, 0, size_b)
     while len(steps_a) < half - 1:
         if len(steps_a) == half - 2:
             near = 2 * len(steps_a) + 1
-            gate_a, squares_a = matmul(units(0, 0, near), False, {}, nothing, block_a, steps_a)
+            gate_a, squares_a = matmul(units(0, 0, near), False, {}, nothing_a, block_a, steps_a)
         steps_a = gather_step(block_a, steps_a, half)
     steps_b = gather_step(block_b, [], half, gate_a)
     up_a, squares_a = matmul(units(1, 0, count - 1), False, {}, squares_a, block_a, steps_a, gate_a)
@@ -529,7 +530,7 @@
     moved_a = scatter_send(scatter_sums(None, term_a, count, half, third_b))
     sums_a = scatter_sums(moved_a, term_a, count, distances.pop(0))
     columns = gate_weight.shape[1]
-    hidden_b, squares_b = [], nothing
+    hidden_b, squares_b = [], nothing_b
     for first in (0, columns // 2):
         pieces = after(pieces_of(block_b, steps_b), closed_a, sums_a, hidden_b)
         part, squares_b = gate_up_columns(first, first + columns // 2, squares_b, blocks, pieces, gains, weights)
@@ -539,7 +540,7 @@
         sums_a = scatter_sums(scatter_send(sums_a), term_a, count, distance)
     opened_b = open_down(hidden_b, sums_a)
     moved_a = scatter_send(sums_a)
-    spans = [slice(0, size // 2), slice(size // 2, size)]
+    spans = [slice(0, size_b // 2), slice(size_b // 2, size_b)]
     distances = list(range(half, 0, -1))
     parts_b = [None, None]
     closed_b = None
@@ -561,7 +562,7 @@
         return (mix(noisy_input[rows], self_cond[rows]) + ffn).astype(jnp.bfloat16)
 
     outs = [finish(span.start, term, moved) for span, term, moved in zip(spans, terms_b, moved_b)]
-    return jnp.concatenate([*outs, finish(size, term_a, moved_a)], axis=0)
+    return jnp.concatenate([*outs, finish(size_b, term_a, moved_a)], axis=0)
 
 
 def solution(mesh):

time: 215 us -> 210 us (0.977)
  waiting for transfers between devices: 52.6 us -> 44.9 us
  local copies, waits for them, and re-layouts: 1.88 us -> 4.07 us
    ppermute x40, waiting for transfers between devices: 52.5 us -> 44.9 us  [ring_shift(): lax.ppermute(value, 'blk', [(ring[i], ring[(i + steps) % count]) for i in...]
    pallas_call x2, Pallas kernels: 33.5 us -> 27 us  [gate_up_columns(): pl.pallas_call(functools.partial(columns_kernel, start, width * count, no...]
    pallas_call x3, Pallas kernels: 38.8 us -> 43.6 us  [gate_up(): pl.pallas_call(functools.partial(gate_up_kernel, fixed), out_shape=(jax.S...]
    pallas_call x4, Pallas kernels: 32 us -> 34.3 us  [down(): pl.pallas_call(functools.partial(down_kernel, start, stop - start), out_s...]
    unnamed x22 -> x26, local copies, waits for them, and re-layouts: 0.05 us -> 2.23 us
  transfers between devices with their start and end apart: 44 -> 44, of which waited for: 20 -> 13; matrix products, arithmetic and copies ran while one was open for 3% -> 4% of each run, Pallas kernels for 49% -> 50%
where the time goes in v13:
time: 210 us
  Pallas kernels  105 us (50%)
  starting transfers between devices  45.5 us (22%)
  waiting for transfers between devices  44.9 us (21%)
  other arithmetic  8.88 us (4%)
  local copies, waits for them, and re-layouts  4.07 us (2%)
    ppermute x40, waiting for transfers between devices, ring_shift(): lax.ppermute(value, 'blk', [(ring[i], ring[(i + steps) % count]) for i in...  44.9 us
    pallas_call x3, Pallas kernels, gate_up(): pl.pallas_call(functools.partial(gate_up_kernel, fixed), out_shape=(jax.S...  43.6 us
    ppermute x40, starting transfers between devices, ring_shift(): lax.ppermute(value, 'blk', [(ring[i], ring[(i + steps) % count]) for i in...  42.5 us
    pallas_call x4, Pallas kernels, down(): pl.pallas_call(functools.partial(down_kernel, start, stop - start), out_s...  34.3 us
    pallas_call x2, Pallas kernels, gate_up_columns(): pl.pallas_call(functools.partial(columns_kernel, start, width * count, no...  27 us
  transfers between devices with their start and end apart: 44, of which 13 were waited for; matrix products, arithmetic and copies ran while one was open for 4% of the time, Pallas kernels for 50%

profile of v13, /device:TPU:0, one launch (start us, length us, event | category | flops | bytes accessed | tf_op | source)
XLA Modules:
  0.0 209.6 jit_solution(12389935944236250125)
XLA Ops:
  0.0 0.8 multiply_add_fusion.2
  0.8 2.4 %collective-permute-start = (f32[3,1024]{1,0:T(4,128)S(1)}, f32[3,1024]{1,0:T(4,128)S(1)}, u32[]{:S(2)}, u32[]{:S(2)}) collective-permute-start(f32[3,1024]{1,0:T(4,128)S(1)} %multiply_add_fusion.2), channel_id=1, source_target_pairs={{0,1},{2,3},{4,5},{6,7},{8,9},{10,11},{12,13},{14,15},{16,17},{18,... | collective-permute-start | bytes 36872 | tf_op jit(solution)/shard_map/ppermute | solution.py:453
  3.1 1.7 multiply_add_fusion
  5.5 0.9 constant_dynamic-slice_fusion.2
  6.4 0.6 multiply_convert_fusion.refs_0_
  7.1 0.5 collective-permute-start.10
  7.7 2.4 %collective-permute-start.1 = (bf16[320,1024]{1,0:T(8,128)(2,1)S(1)}, bf16[320,1024]{1,0:T(8,128)(2,1)S(1)}, u32[]{:S(2)}, u32[]{:S(2)}) collective-permute-start(bf16[320,1024]{1,0:T(8,128)(2,1)S(1)} %multiply_convert_fusion.refs_0_), channel_id=1, source_target_pairs={{0,4},{4,8},{8,12},{12,14},{14,10},{10,6},{6,2},{2,0},{1,5},{5,9},... | collective-permute-start | bytes 1966088 | tf_op jit(solution)/shard_map/ppermute | solution.py:55
  10.1 15.3 %collective-permute-done.1.refs_1_ = bf16[320,1024]{1,0:T(8,128)(2,1)S(1)} collective-permute-done((bf16[320,1024]{1,0:T(8,128)(2,1)S(1)}, bf16[320,1024]{1,0:T(8,128)(2,1)S(1)}, u32[]{:S(2)}, u32[]{:S(2)}) %collective-permute-start.1) | collective-permute-done | bytes 655392 | tf_op jit(solution)/shard_map/ppermute | solution.py:55
  25.4 1.5 collective-permute-done.2.refs_2_
  26.9 1.6 collective-permute-start.3
  28.9 0.7 dynamic-slice_bitcast_fusion
  29.6 1.3 multiply_add_fusion.1
  31.3 11.6 %collective-permute-done.3.refs_3_ = bf16[320,1024]{1,0:T(8,128)(2,1)S(1)} collective-permute-done((bf16[320,1024]{1,0:T(8,128)(2,1)S(1)}, bf16[320,1024]{1,0:T(8,128)(2,1)S(1)}, u32[]{:S(2)}, u32[]{:S(2)}) %collective-permute-start.3) | collective-permute-done | bytes 655392 | tf_op jit(solution)/shard_map/ppermute | solution.py:55
  42.9 1.3 collective-permute-done.4.refs_4_
  44.2 1.6 collective-permute-start.8
  46.2 13.8 %gate_up.5 = (f32[320,2048]{1,0:T(8,128)}, f32[320,128]{1,0:T(8,128)S(1)}) custom-call(s32[3,8]{1,0:T(4,128)S(1)} %get-tuple-element.229.blocks_ref, s32[5,5]{1,0:T(8,128)S(1)} %copy-done.7, bf16[320,1024]{1,0:T(8,128)(2,1)S(1)} %multiply_convert_fusion.refs_0_, bf16[320,1024]{1,0:T(8,128)(2,1)S(1)} %collective-permute-done.1.refs_1_, ...), custom_call_target="tpu_custom_call" | custom-call | flops 13421772800 | bytes 20971520 | tf_op jit(solution)/shard_map/gate_up/pallas_call | solution.py:181
  60.2 1.5 collective-permute-start.6
  61.8 0.5 collective-permute-start.7
  62.3 1.6 collective-permute-start.11
  63.9 0.5 collective-permute-start.12
  64.5 16.9 %gate_up.6 = (f32[320,2048]{1,0:T(8,128)}, f32[320,128]{1,0:T(8,128)S(1)}) custom-call(s32[3,8]{1,0:T(4,128)S(1)} %get-tuple-element.229.blocks_ref, s32[5,7]{1,0:T(8,128)S(1)} %copy-done.6, bf16[320,1024]{1,0:T(8,128)(2,1)S(1)} %multiply_convert_fusion.refs_0_, bf16[320,1024]{1,0:T(8,128)(2,1)S(1)} %collective-permute-done.1.refs_1_, ...), custom_call_target="tpu_custom_call" | custom-call | flops 18790481920 | bytes 29360128 | tf_op jit(solution)/shard_map/gate_up/pallas_call | solution.py:181
  81.5 1.6 collective-permute-start.13
  83.0 0.5 collective-permute-start.14
  83.6 1.1 copy-done.1
  84.6 1.1 copy-done.3
  85.7 12.8 %gate_up.7 = (bf16[320,2048]{1,0:T(8,128)(2,1)S(1)}, f32[320,128]{1,0:T(8,128)}) custom-call(s32[3,8]{1,0:T(4,128)S(1)} %get-tuple-element.229.blocks_ref, s32[5,4]{1,0:T(8,128)S(1)} %copy-done.5, bf16[320,1024]{1,0:T(8,128)(2,1)S(1)} %copy-done.1, bf16[320,1024]{1,0:T(8,128)(2,1)S(1)} %copy-done.3, bf16[160,1024]{1,0:T(8,128)(2,1)S(1)} %collective-permute-done.11.refs_2_, ...), custom_call_target="tpu_custom_call" | custom-call | flops 10737418240 | bytes 16777216 | tf_op jit(solution)/shard_map/gate_up/pallas_call | solution.py:181
  98.6 1.6 collective-permute-start.15
  100.2 0.5 collective-permute-start.16
  100.7 7.5 %down.4 = bf16[3,320,1024]{2,1,0:T(8,128)(2,1)S(1)} custom-call(s32[3,8]{1,0:T(4,128)S(1)} %get-tuple-element.230.tiles_ref, bf16[320,2048]{1,0:T(8,128)(2,1)S(1)} %get-tuple-element.143.refs_0_, bf16[2048,4096]{1,0:T(8,128)(2,1)} %refs_2_.3, bf16[2048,4096]{1,0:T(8,128)(2,1)} %collective-permute-done.17.refs_2_.refs_3_), custom_call_target="tpu_custom_call" | custom-call | flops 8053063680 | bytes 12582912 | tf_op jit(solution)/shard_map/down/pallas_call | solution.py:373
  108.4 1.6 collective-permute-start.18
  110.0 0.6 collective-permute-start.19
  110.5 1.5 collective-permute-start.20
  112.0 0.5 collective-permute-start.21
  112.5 11.6 %down.5 = bf16[5,320,1024]{2,1,0:T(8,128)(2,1)} custom-call(s32[3,8]{1,0:T(4,128)S(1)} %get-tuple-element.230.tiles_ref, bf16[320,2048]{1,0:T(8,128)(2,1)S(1)} %get-tuple-element.143.refs_0_, bf16[2048,4096]{1,0:T(8,128)(2,1)} %refs_2_.3, bf16[2048,4096]{1,0:T(8,128)(2,1)} %collective-permute-done.17.refs_2_.refs_3_), custom_call_target="tpu_custom_call" | custom-call | flops 13421772800 | bytes 20971520 | tf_op jit(solution)/shard_map/down/pallas_call | solution.py:373
  124.5 0.5 collective-permute-start.23
  125.0 1.6 collective-permute-start.22
  126.7 13.7 %gate_up.8 = (bf16[192,1024]{1,0:T(8,128)(2,1)S(1)}, f32[192,128]{1,0:T(8,128)S(1)}) custom-call(s32[3,8]{1,0:T(4,128)S(1)} %get-tuple-element.229.blocks_ref, bf16[192,1024]{1,0:T(8,128)(2,1)S(1)} %multiply_convert_fusion.1.refs_0_, bf16[192,1024]{1,0:T(8,128)(2,1)S(1)} %collective-permute-done.6.refs_1_, ...), custom_call_target="tpu_custom_call" | custom-call | flops 12884901888 | bytes 33554432 | tf_op jit(solution)/shard_map/gate_up/pallas_call | solution.py:302
  140.4 0.6 fusion.9
  141.0 1.6 collective-permute-start.24
  142.5 0.5 collective-permute-start.25
  143.1 13.4 %gate_up.9 = (bf16[192,1024]{1,0:T(8,128)(2,1)S(1)}, f32[192,128]{1,0:T(8,128)}) custom-call(s32[3,8]{1,0:T(4,128)S(1)} %get-tuple-element.229.blocks_ref, bf16[192,1024]{1,0:T(8,128)(2,1)S(1)} %multiply_convert_fusion.1.refs_0_, bf16[192,1024]{1,0:T(8,128)(2,1)S(1)} %collective-permute-done.6.refs_1_, bf16[192,1024]{1,0:T(8,128)(2,1)S(1)} %collective-permute-done.7.refs_2_, ...), custom_call_target="tpu_custom_call" | custom-call | flops 12884901888 | bytes 33554432 | tf_op jit(solution)/shard_map/gate_up/pallas_call | solution.py:302
  156.5 0.6 fusion.8
  157.1 1.6 collective-permute-start.26
  158.7 0.5 collective-permute-start.27
  159.1 6.3 %down.6 = bf16[3,192,1024]{2,1,0:T(8,128)(2,1)S(1)} custom-call(s32[3,8]{1,0:T(4,128)S(1)} %get-tuple-element.230.tiles_ref, bf16[192,1024]{1,0:T(8,128)(2,1)S(1)} %get-tuple-element.183.refs_0_, bf16[192,1024]{1,0:T(8,128)(2,1)S(1)} %get-tuple-element.184.refs_1_, bf16[2048,4096]{1,0:T(8,128)(2,1)} %refs_2_.3, ...), custom_call_target="tpu_custom_call" | custom-call | flops 4831838208 | bytes 12582912 | tf_op jit(solution)/shard_map/down/pallas_call | solution.py:373
  165.5 4.3 %collective-permute-done.26 = bf16[320,1024]{1,0:T(8,128)(2,1)S(1)} collective-permute-done((bf16[320,1024]{1,0:T(8,128)(2,1)S(1)}, bf16[320,1024]{1,0:T(8,128)(2,1)S(1)}, u32[]{:S(2)}, u32[]{:S(2)}) %collective-permute-start.26) | collective-permute-done | bytes 655392 | tf_op jit(solution)/shard_map/ppermute | solution.py:55
  169.8 2.8 %collective-permute-done.27 = bf16[320,1024]{1,0:T(8,128)(2,1)S(1)} collective-permute-done((bf16[320,1024]{1,0:T(8,128)(2,1)S(1)}, bf16[320,1024]{1,0:T(8,128)(2,1)S(1)}, u32[]{:S(2)}, u32[]{:S(2)}) %collective-permute-start.27) | collective-permute-done | bytes 655392 | tf_op jit(solution)/shard_map/ppermute | solution.py:55
  172.6 2.7 %collective-permute-start.28 = (bf16[48,1024]{1,0:T(8,128)(2,1)S(1)}, bf16[48,1024]{1,0:T(8,128)(2,1)S(1)}, u32[]{:S(2)}, u32[]{:S(2)}) collective-permute-start(bf16[48,1024]{1,0:T(8,128)(2,1)S(1)} %get-tuple-element.175), channel_id=1, source_target_pairs={{0,4},{4,8},{8,12},{12,14},{14,10},{10,6},{6,2},{2,0},{1,5},{5,9},... | collective-permute-start | bytes 294920 | tf_op jit(solution)/shard_map/ppermute | solution.py:55
  175.3 2.0 collective-permute-start.30
  177.5 2.4 %collective-permute-done.29 = bf16[48,1024]{1,0:T(8,128)(2,1)S(1)} collective-permute-done((bf16[48,1024]{1,0:T(8,128)(2,1)S(1)}, bf16[48,1024]{1,0:T(8,128)(2,1)S(1)}, u32[]{:S(2)}, u32[]{:S(2)}) %collective-permute-start.29) | collective-permute-done | bytes 98336 | tf_op jit(solution)/shard_map/ppermute | solution.py:55
  180.1 2.1 collective-permute-start.32
  182.3 2.1 collective-permute-start.36
  184.4 8.9 %down.7 = bf16[5,192,1024]{2,1,0:T(8,128)(2,1)S(1)} custom-call(s32[3,8]{1,0:T(4,128)S(1)} %get-tuple-element.230.tiles_ref, bf16[192,1024]{1,0:T(8,128)(2,1)S(1)} %get-tuple-element.183.refs_0_, bf16[192,1024]{1,0:T(8,128)(2,1)S(1)} %get-tuple-element.184.refs_1_, bf16[2048,4096]{1,0:T(8,128)(2,1)} %refs_2_.3, ...), custom_call_target="tpu_custom_call" | custom-call | flops 8053063680 | bytes 20971520 | tf_op jit(solution)/shard_map/down/pallas_call | solution.py:373
  193.4 0.7 collective-permute-start.34
  194.1 1.4 collective-permute-start.35
  195.7 0.7 collective-permute-start.40
  196.4 1.4 collective-permute-start.41
  197.8 1.4 collective-permute-done.34
  199.1 0.6 collective-permute-done.35
  200.2 1.7 collective-permute-start.39
  202.5 1.7 collective-permute-start.43
  204.3 0.7 fusion.6
  204.9 3.0 %collective-permute-done.42 = bf16[96,1024]{1,0:T(8,128)(2,1)S(1)} collective-permute-done((bf16[96,1024]{1,0:T(8,128)(2,1)S(1)}, bf16[96,1024]{1,0:T(8,128)(2,1)S(1)}, u32[]{:S(2)}, u32[]{:S(2)}) %collective-permute-start.42) | collective-permute-done | bytes 196640 | tf_op jit(solution)/shard_map/ppermute | solution.py:55
  208.5 1.0 pad_maximum_fusion
  (93 shorter events, 4.6 us)
Async XLA Ops:
  0.8 6.3 %collective-permute-start = (f32[3,1024]{1,0:T(4,128)S(1)}, f32[3,1024]{1,0:T(4,128)S(1)}, u32[]{:S(2)}, u32[]{:S(2)}) collective-permute-start(f32[3,1024]{1,0:T(4,128)S(1)} %multiply_add_fusion.2), channel_id=1, source_target_pairs={{0,1},{2,3},{4,5},{6,7},{8,9},{10,11},{12,13},{14,15},{16,17},{18,... | collective-permute-start | bytes 36872 | tf_op jit(solution)/shard_map/ppermute | solution.py:453
  3.1 2.3 %copy-start.4 = (f32[8192]{0:T(1024)S(1)}, f32[8192]{0:T(1024)}, u32[]{:S(2)}) copy-start(f32[8192]{0:T(1024)} %param.18) | copy-start | bytes 98308
  6.4 23.2 %copy-start.11 = (f32[1024]{0:T(1024)S(1)}, f32[1024]{0:T(1024)}, u32[]{:S(2)}) copy-start(f32[1024]{0:T(1024)} %param.15) | copy-start | bytes 12292
  7.0 39.2 %collective-permute-start.5 = (bf16[4096,2048]{1,0:T(8,128)(2,1)}, bf16[4096,2048]{1,0:T(8,128)(2,1)}, u32[]{:S(2)}, u32[]{:S(2)}) collective-permute-start(bf16[4096,2048]{1,0:T(8,128)(2,1)} %refs_10_.5), channel_id=1, source_target_pairs={{0,1},{1,0},{2,3},{3,2},{4,5},{5,4},{6,7},{7,6},{8,9},{9,8},{10,11... | collective-permute-start | bytes 50331656 | tf_op jit(solution)/shard_map/ppermute | solution.py:59
  7.1 56.8 %collective-permute-start.10 = (bf16[4096,2048]{1,0:T(8,128)(2,1)}, bf16[4096,2048]{1,0:T(8,128)(2,1)}, u32[]{:S(2)}, u32[]{:S(2)}) collective-permute-start(bf16[4096,2048]{1,0:T(8,128)(2,1)} %refs_12_.3), channel_id=1, source_target_pairs={{0,1},{1,0},{2,3},{3,2},{4,5},{5,4},{6,7},{7,6},{8,9},{9,8},{10,11... | collective-permute-start | bytes 50331656 | tf_op jit(solution)/shard_map/ppermute | solution.py:59
  7.6 93.0 %collective-permute-start.17 = (bf16[2048,4096]{1,0:T(8,128)(2,1)}, bf16[2048,4096]{1,0:T(8,128)(2,1)}, u32[]{:S(2)}, u32[]{:S(2)}) collective-permute-start(bf16[2048,4096]{1,0:T(8,128)(2,1)} %refs_2_.3), channel_id=1, source_target_pairs={{0,1},{1,0},{2,3},{3,2},{4,5},{5,4},{6,7},{7,6},{8,9},{9,8},{10,11... | collective-permute-start | bytes 50331656 | tf_op jit(solution)/shard_map/ppermute | solution.py:59
  7.7 17.7 %collective-permute-start.1 = (bf16[320,1024]{1,0:T(8,128)(2,1)S(1)}, bf16[320,1024]{1,0:T(8,128)(2,1)S(1)}, u32[]{:S(2)}, u32[]{:S(2)}) collective-permute-start(bf16[320,1024]{1,0:T(8,128)(2,1)S(1)} %multiply_convert_fusion.refs_0_), channel_id=1, source_target_pairs={{0,4},{4,8},{8,12},{12,14},{14,10},{10,6},{6,2},{2,0},{1,5},{5,9},... | collective-permute-start | bytes 1966088 | tf_op jit(solution)/shard_map/ppermute | solution.py:55
  10.1 16.8 %collective-permute-start.2 = (bf16[320,1024]{1,0:T(8,128)(2,1)S(1)}, bf16[320,1024]{1,0:T(8,128)(2,1)S(1)}, u32[]{:S(2)}, u32[]{:S(2)}) collective-permute-start(bf16[320,1024]{1,0:T(8,128)(2,1)S(1)} %multiply_convert_fusion.refs_0_), channel_id=1, source_target_pairs={{0,2},{4,0},{8,4},{12,8},{14,12},{10,14},{6,10},{2,6},{1,3},{5,1},... | collective-permute-start | bytes 1966088 | tf_op jit(solution)/shard_map/ppermute | solution.py:55
  26.9 16.0 %collective-permute-start.3 = (bf16[320,1024]{1,0:T(8,128)(2,1)S(1)}, bf16[320,1024]{1,0:T(8,128)(2,1)S(1)}, u32[]{:S(2)}, u32[]{:S(2)}) collective-permute-start(bf16[320,1024]{1,0:T(8,128)(2,1)S(1)} %collective-permute-done.1.refs_1_), channel_id=1, source_target_pairs={{0,4},{4,8},{8,12},{12,14},{14,10},{10,6},{6,2},{2,0},{1,5},{5,9},... | collective-permute-start | bytes 1966088 | tf_op jit(solution)/shard_map/ppermute | solution.py:55
  28.5 15.7 %collective-permute-start.4 = (bf16[320,1024]{1,0:T(8,128)(2,1)S(1)}, bf16[320,1024]{1,0:T(8,128)(2,1)S(1)}, u32[]{:S(2)}, u32[]{:S(2)}) collective-permute-start(bf16[320,1024]{1,0:T(8,128)(2,1)S(1)} %collective-permute-done.2.refs_2_), channel_id=1, source_target_pairs={{0,2},{4,0},{8,4},{12,8},{14,12},{10,14},{6,10},{2,6},{1,3},{5,1},... | collective-permute-start | bytes 1966088 | tf_op jit(solution)/shard_map/ppermute | solution.py:55
  29.6 16.6 %copy-start.7 = (s32[5,5]{1,0:T(8,128)S(1)}, s32[5,5]{1,0:T(8,128)}, u32[]{:S(2)}) copy-start(s32[5,5]{1,0:T(8,128)} %constant.35.clone.units_ref) | copy-start | bytes 304
  44.2 15.9 %collective-permute-start.8 = (bf16[320,1024]{1,0:T(8,128)(2,1)S(1)}, bf16[320,1024]{1,0:T(8,128)(2,1)S(1)}, u32[]{:S(2)}, u32[]{:S(2)}) collective-permute-start(bf16[320,1024]{1,0:T(8,128)(2,1)S(1)} %collective-permute-done.3.refs_3_), channel_id=1, source_target_pairs={{0,4},{4,8},{8,12},{12,14},{14,10},{10,6},{6,2},{2,0},{1,5},{5,9},... | collective-permute-start | bytes 1966088 | tf_op jit(solution)/shard_map/ppermute | solution.py:55
  45.8 14.5 %collective-permute-start.9 = (bf16[320,1024]{1,0:T(8,128)(2,1)S(1)}, bf16[320,1024]{1,0:T(8,128)(2,1)S(1)}, u32[]{:S(2)}, u32[]{:S(2)}) collective-permute-start(bf16[320,1024]{1,0:T(8,128)(2,1)S(1)} %collective-permute-done.4.refs_4_), channel_id=1, source_target_pairs={{0,2},{4,0},{8,4},{12,8},{14,12},{10,14},{6,10},{2,6},{1,3},{5,1},... | collective-permute-start | bytes 1966088 | tf_op jit(solution)/shard_map/ppermute | solution.py:55
  60.1 4.4 %copy-start.6 = (s32[5,7]{1,0:T(8,128)S(1)}, s32[5,7]{1,0:T(8,128)}, u32[]{:S(2)}) copy-start(s32[5,7]{1,0:T(8,128)} %constant.36.clone.units_ref) | copy-start | bytes 424
  60.1 4.4 %copy-start = (bf16[320,1024]{1,0:T(8,128)(2,1)}, bf16[320,1024]{1,0:T(8,128)(2,1)S(1)}, u32[]{:S(2)}) copy-start(bf16[320,1024]{1,0:T(8,128)(2,1)S(1)} %collective-permute-done.8.refs_5_.refs_0_) | copy-start | bytes 1966084
  60.2 4.2 %copy-start.2 = (bf16[320,1024]{1,0:T(8,128)(2,1)}, bf16[320,1024]{1,0:T(8,128)(2,1)S(1)}, u32[]{:S(2)}) copy-start(bf16[320,1024]{1,0:T(8,128)(2,1)S(1)} %collective-permute-done.9.refs_6_.refs_1_) | copy-start | bytes 1966084
  60.2 21.2 %collective-permute-start.6 = (bf16[192,1024]{1,0:T(8,128)(2,1)S(1)}, bf16[192,1024]{1,0:T(8,128)(2,1)S(1)}, u32[]{:S(2)}, u32[]{:S(2)}) collective-permute-start(bf16[192,1024]{1,0:T(8,128)(2,1)S(1)} %multiply_convert_fusion.1.refs_0_), channel_id=1, source_target_pairs={{0,4},{4,8},{8,12},{12,14},{14,10},{10,6},{6,2},{2,0},{1,5},{5,9},... | collective-permute-start | bytes 1179656 | tf_op jit(solution)/shard_map/ppermute | solution.py:55
  61.8 19.7 %collective-permute-start.7 = (bf16[192,1024]{1,0:T(8,128)(2,1)S(1)}, bf16[192,1024]{1,0:T(8,128)(2,1)S(1)}, u32[]{:S(2)}, u32[]{:S(2)}) collective-permute-start(bf16[192,1024]{1,0:T(8,128)(2,1)S(1)} %multiply_convert_fusion.1.refs_0_), channel_id=1, source_target_pairs={{0,2},{4,0},{8,4},{12,8},{14,12},{10,14},{6,10},{2,6},{1,3},{5,1},... | collective-permute-start | bytes 1179656 | tf_op jit(solution)/shard_map/ppermute | solution.py:55
  62.3 19.1 %collective-permute-start.11 = (bf16[160,1024]{1,0:T(8,128)(2,1)S(1)}, bf16[160,1024]{1,0:T(8,128)(2,1)S(1)}, u32[]{:S(2)}, u32[]{:S(2)}) collective-permute-start(bf16[160,1024]{1,0:T(8,128)(2,1)S(1)} %slice.331), channel_id=1, source_target_pairs={{0,4},{4,8},{8,12},{12,14},{14,10},{10,6},{6,2},{2,0},{1,5},{5,9},... | collective-permute-start | bytes 983048 | tf_op jit(solution)/shard_map/ppermute | solution.py:55
  63.9 17.5 %collective-permute-start.12 = (bf16[160,1024]{1,0:T(8,128)(2,1)S(1)}, bf16[160,1024]{1,0:T(8,128)(2,1)S(1)}, u32[]{:S(2)}, u32[]{:S(2)}) collective-permute-start(bf16[160,1024]{1,0:T(8,128)(2,1)S(1)} %slice.332), channel_id=1, source_target_pairs={{0,2},{4,0},{8,4},{12,8},{14,12},{10,14},{6,10},{2,6},{1,3},{5,1},... | collective-permute-start | bytes 983048 | tf_op jit(solution)/shard_map/ppermute | solution.py:55
  64.5 19.1 %copy-start.5 = (s32[5,4]{1,0:T(8,128)S(1)}, s32[5,4]{1,0:T(8,128)}, u32[]{:S(2)}) copy-start(s32[5,4]{1,0:T(8,128)} %constant.37.clone.units_ref) | copy-start | bytes 244
  81.5 17.1 %collective-permute-start.13 = (bf16[192,1024]{1,0:T(8,128)(2,1)S(1)}, bf16[192,1024]{1,0:T(8,128)(2,1)S(1)}, u32[]{:S(2)}, u32[]{:S(2)}) collective-permute-start(bf16[192,1024]{1,0:T(8,128)(2,1)S(1)} %collective-permute-done.6.refs_1_), channel_id=1, source_target_pairs={{0,4},{4,8},{8,12},{12,14},{14,10},{10,6},{6,2},{2,0},{1,5},{5,9},... | collective-permute-start | bytes 1179656 | tf_op jit(solution)/shard_map/ppermute | solution.py:55
  83.0 15.6 %collective-permute-start.14 = (bf16[192,1024]{1,0:T(8,128)(2,1)S(1)}, bf16[192,1024]{1,0:T(8,128)(2,1)S(1)}, u32[]{:S(2)}, u32[]{:S(2)}) collective-permute-start(bf16[192,1024]{1,0:T(8,128)(2,1)S(1)} %collective-permute-done.7.refs_2_), channel_id=1, source_target_pairs={{0,2},{4,0},{8,4},{12,8},{14,12},{10,14},{6,10},{2,6},{1,3},{5,1},... | collective-permute-start | bytes 1179656 | tf_op jit(solution)/shard_map/ppermute | solution.py:55
  83.5 1.1 copy-start.1
  84.6 1.1 copy-start.3
  98.6 9.7 %collective-permute-start.15 = (bf16[192,1024]{1,0:T(8,128)(2,1)S(1)}, bf16[192,1024]{1,0:T(8,128)(2,1)S(1)}, u32[]{:S(2)}, u32[]{:S(2)}) collective-permute-start(bf16[192,1024]{1,0:T(8,128)(2,1)S(1)} %collective-permute-done.13.refs_3_), channel_id=1, source_target_pairs={{0,4},{4,8},{8,12},{12,14},{14,10},{10,6},{6,2},{2,0},{1,5},{5,9},... | collective-permute-start | bytes 1179656 | tf_op jit(solution)/shard_map/ppermute | solution.py:55
  100.2 8.2 %collective-permute-start.16 = (bf16[192,1024]{1,0:T(8,128)(2,1)S(1)}, bf16[192,1024]{1,0:T(8,128)(2,1)S(1)}, u32[]{:S(2)}, u32[]{:S(2)}) collective-permute-start(bf16[192,1024]{1,0:T(8,128)(2,1)S(1)} %collective-permute-done.14.refs_4_), channel_id=1, source_target_pairs={{0,2},{4,0},{8,4},{12,8},{14,12},{10,14},{6,10},{2,6},{1,3},{5,1},... | collective-permute-start | bytes 1179656 | tf_op jit(solution)/shard_map/ppermute | solution.py:55
  108.4 18.3 %collective-permute-start.18 = (bf16[96,1024]{1,0:T(8,128)(2,1)S(1)}, bf16[96,1024]{1,0:T(8,128)(2,1)S(1)}, u32[]{:S(2)}, u32[]{:S(2)}) collective-permute-start(bf16[96,1024]{1,0:T(8,128)(2,1)S(1)} %slice.333), channel_id=1, source_target_pairs={{0,4},{4,8},{8,12},{12,14},{14,10},{10,6},{6,2},{2,0},{1,5},{5,9},... | collective-permute-start | bytes 589832 | tf_op jit(solution)/shard_map/ppermute | solution.py:55
  110.0 16.7 %collective-permute-start.19 = (bf16[96,1024]{1,0:T(8,128)(2,1)S(1)}, bf16[96,1024]{1,0:T(8,128)(2,1)S(1)}, u32[]{:S(2)}, u32[]{:S(2)}) collective-permute-start(bf16[96,1024]{1,0:T(8,128)(2,1)S(1)} %slice.334), channel_id=1, source_target_pairs={{0,2},{4,0},{8,4},{12,8},{14,12},{10,14},{6,10},{2,6},{1,3},{5,1},... | collective-permute-start | bytes 589832 | tf_op jit(solution)/shard_map/ppermute | solution.py:55
  110.5 13.7 %collective-permute-start.20 = (bf16[160,1024]{1,0:T(8,128)(2,1)S(1)}, bf16[160,1024]{1,0:T(8,128)(2,1)S(1)}, u32[]{:S(2)}, u32[]{:S(2)}) collective-permute-start(bf16[160,1024]{1,0:T(8,128)(2,1)S(1)} %get-tuple-element.144), channel_id=1, source_target_pairs={{0,4},{4,8},{8,12},{12,14},{14,10},{10,6},{6,2},{2,0},{1,5},{5,9},... | collective-permute-start | bytes 983048 | tf_op jit(solution)/shard_map/ppermute | solution.py:55
  112.0 12.2 %collective-permute-start.21 = (bf16[160,1024]{1,0:T(8,128)(2,1)S(1)}, bf16[160,1024]{1,0:T(8,128)(2,1)S(1)}, u32[]{:S(2)}, u32[]{:S(2)}) collective-permute-start(bf16[160,1024]{1,0:T(8,128)(2,1)S(1)} %get-tuple-element.145), channel_id=1, source_target_pairs={{0,2},{4,0},{8,4},{12,8},{14,12},{10,14},{6,10},{2,6},{1,3},{5,1},... | collective-permute-start | bytes 983048 | tf_op jit(solution)/shard_map/ppermute | solution.py:55
  124.5 15.9 %collective-permute-start.23 = (bf16[320,1024]{1,0:T(8,128)(2,1)S(1)}, bf16[320,1024]{1,0:T(8,128)(2,1)S(1)}, u32[]{:S(2)}, u32[]{:S(2)}) collective-permute-start(bf16[320,1024]{1,0:T(8,128)(2,1)S(1)} %pad_maximum_fusion.3), channel_id=1, source_target_pairs={{0,2},{4,0},{8,4},{12,8},{14,12},{10,14},{6,10},{2,6},{1,3},{5,1},... | collective-permute-start | bytes 1966088 | tf_op jit(solution)/shard_map/ppermute | solution.py:55
  125.0 15.3 %collective-permute-start.22 = (bf16[320,1024]{1,0:T(8,128)(2,1)S(1)}, bf16[320,1024]{1,0:T(8,128)(2,1)S(1)}, u32[]{:S(2)}, u32[]{:S(2)}) collective-permute-start(bf16[320,1024]{1,0:T(8,128)(2,1)S(1)} %pad_maximum_fusion.2), channel_id=1, source_target_pairs={{0,4},{4,8},{8,12},{12,14},{14,10},{10,6},{6,2},{2,0},{1,5},{5,9},... | collective-permute-start | bytes 1966088 | tf_op jit(solution)/shard_map/ppermute | solution.py:55
  126.7 13.7 %copy-start.10 = (bf16[5,320,1024]{2,1,0:T(8,128)(2,1)S(1)}, bf16[5,320,1024]{2,1,0:T(8,128)(2,1)}, u32[]{:S(2)}) copy-start(bf16[5,320,1024]{2,1,0:T(8,128)(2,1)} %down.5) | copy-start | bytes 9830404
  141.0 15.5 %collective-permute-start.24 = (bf16[320,1024]{1,0:T(8,128)(2,1)S(1)}, bf16[320,1024]{1,0:T(8,128)(2,1)S(1)}, u32[]{:S(2)}, u32[]{:S(2)}) collective-permute-start(bf16[320,1024]{1,0:T(8,128)(2,1)S(1)} %get-tuple-element.198), channel_id=1, source_target_pairs={{0,4},{4,8},{8,12},{12,14},{14,10},{10,6},{6,2},{2,0},{1,5},{5,9},... | collective-permute-start | bytes 1966088 | tf_op jit(solution)/shard_map/ppermute | solution.py:55
  142.5 13.9 %collective-permute-start.25 = (bf16[320,1024]{1,0:T(8,128)(2,1)S(1)}, bf16[320,1024]{1,0:T(8,128)(2,1)S(1)}, u32[]{:S(2)}, u32[]{:S(2)}) collective-permute-start(bf16[320,1024]{1,0:T(8,128)(2,1)S(1)} %get-tuple-element.197), channel_id=1, source_target_pairs={{0,2},{4,0},{8,4},{12,8},{14,12},{10,14},{6,10},{2,6},{1,3},{5,1},... | collective-permute-start | bytes 1966088 | tf_op jit(solution)/shard_map/ppermute | solution.py:55
  157.1 12.7 %collective-permute-start.26 = (bf16[320,1024]{1,0:T(8,128)(2,1)S(1)}, bf16[320,1024]{1,0:T(8,128)(2,1)S(1)}, u32[]{:S(2)}, u32[]{:S(2)}) collective-permute-start(bf16[320,1024]{1,0:T(8,128)(2,1)S(1)} %get-tuple-element.195), channel_id=1, source_target_pairs={{0,4},{4,8},{8,12},{12,14},{14,10},{10,6},{6,2},{2,0},{1,5},{5,9},... | collective-permute-start | bytes 1966088 | tf_op jit(solution)/shard_map/ppermute | solution.py:55
  158.7 13.9 %collective-permute-start.27 = (bf16[320,1024]{1,0:T(8,128)(2,1)S(1)}, bf16[320,1024]{1,0:T(8,128)(2,1)S(1)}, u32[]{:S(2)}, u32[]{:S(2)}) collective-permute-start(bf16[320,1024]{1,0:T(8,128)(2,1)S(1)} %get-tuple-element.196), channel_id=1, source_target_pairs={{0,2},{4,0},{8,4},{12,8},{14,12},{10,14},{6,10},{2,6},{1,3},{5,1},... | collective-permute-start | bytes 1966088 | tf_op jit(solution)/shard_map/ppermute | solution.py:55
  172.6 4.9 %collective-permute-start.28 = (bf16[48,1024]{1,0:T(8,128)(2,1)S(1)}, bf16[48,1024]{1,0:T(8,128)(2,1)S(1)}, u32[]{:S(2)}, u32[]{:S(2)}) collective-permute-start(bf16[48,1024]{1,0:T(8,128)(2,1)S(1)} %get-tuple-element.175), channel_id=1, source_target_pairs={{0,4},{4,8},{8,12},{12,14},{14,10},{10,6},{6,2},{2,0},{1,5},{5,9},... | collective-permute-start | bytes 294920 | tf_op jit(solution)/shard_map/ppermute | solution.py:55
  175.3 4.6 %collective-permute-start.29 = (bf16[48,1024]{1,0:T(8,128)(2,1)S(1)}, bf16[48,1024]{1,0:T(8,128)(2,1)S(1)}, u32[]{:S(2)}, u32[]{:S(2)}) collective-permute-start(bf16[48,1024]{1,0:T(8,128)(2,1)S(1)} %get-tuple-element.176), channel_id=1, source_target_pairs={{0,2},{4,0},{8,4},{12,8},{14,12},{10,14},{6,10},{2,6},{1,3},{5,1},... | collective-permute-start | bytes 294920 | tf_op jit(solution)/shard_map/ppermute | solution.py:55
  175.3 6.9 %collective-permute-start.30 = (bf16[48,1024]{1,0:T(8,128)(2,1)S(1)}, bf16[48,1024]{1,0:T(8,128)(2,1)S(1)}, u32[]{:S(2)}, u32[]{:S(2)}) collective-permute-start(bf16[48,1024]{1,0:T(8,128)(2,1)S(1)} %get-tuple-element.177), channel_id=1, source_target_pairs={{0,4},{4,8},{8,12},{12,14},{14,10},{10,6},{6,2},{2,0},{1,5},{5,9},... | collective-permute-start | bytes 294920 | tf_op jit(solution)/shard_map/ppermute | solution.py:55
  177.3 4.8 %collective-permute-start.31 = (bf16[48,1024]{1,0:T(8,128)(2,1)S(1)}, bf16[48,1024]{1,0:T(8,128)(2,1)S(1)}, u32[]{:S(2)}, u32[]{:S(2)}) collective-permute-start(bf16[48,1024]{1,0:T(8,128)(2,1)S(1)} %get-tuple-element.178), channel_id=1, source_target_pairs={{0,2},{4,0},{8,4},{12,8},{14,12},{10,14},{6,10},{2,6},{1,3},{5,1},... | collective-permute-start | bytes 294920 | tf_op jit(solution)/shard_map/ppermute | solution.py:55
  180.0 13.3 %collective-permute-start.33 = (bf16[96,1024]{1,0:T(8,128)(2,1)S(1)}, bf16[96,1024]{1,0:T(8,128)(2,1)S(1)}, u32[]{:S(2)}, u32[]{:S(2)}) collective-permute-start(bf16[96,1024]{1,0:T(8,128)(2,1)S(1)} %pad_maximum_fusion.5), channel_id=1, source_target_pairs={{0,2},{4,0},{8,4},{12,8},{14,12},{10,14},{6,10},{2,6},{1,3},{5,1},... | collective-permute-start | bytes 589832 | tf_op jit(solution)/shard_map/ppermute | solution.py:55
  180.1 13.2 %collective-permute-start.32 = (bf16[96,1024]{1,0:T(8,128)(2,1)S(1)}, bf16[96,1024]{1,0:T(8,128)(2,1)S(1)}, u32[]{:S(2)}, u32[]{:S(2)}) collective-permute-start(bf16[96,1024]{1,0:T(8,128)(2,1)S(1)} %pad_maximum_fusion.4), channel_id=1, source_target_pairs={{0,4},{4,8},{8,12},{12,14},{14,10},{10,6},{6,2},{2,0},{1,5},{5,9},... | collective-permute-start | bytes 589832 | tf_op jit(solution)/shard_map/ppermute | solution.py:55
  182.2 13.3 %collective-permute-start.37 = (bf16[96,1024]{1,0:T(8,128)(2,1)S(1)}, bf16[96,1024]{1,0:T(8,128)(2,1)S(1)}, u32[]{:S(2)}, u32[]{:S(2)}) collective-permute-start(bf16[96,1024]{1,0:T(8,128)(2,1)S(1)} %pad_maximum_fusion.7), channel_id=1, source_target_pairs={{0,2},{4,0},{8,4},{12,8},{14,12},{10,14},{6,10},{2,6},{1,3},{5,1},... | collective-permute-start | bytes 589832 | tf_op jit(solution)/shard_map/ppermute | solution.py:55
  182.3 13.2 %collective-permute-start.36 = (bf16[96,1024]{1,0:T(8,128)(2,1)S(1)}, bf16[96,1024]{1,0:T(8,128)(2,1)S(1)}, u32[]{:S(2)}, u32[]{:S(2)}) collective-permute-start(bf16[96,1024]{1,0:T(8,128)(2,1)S(1)} %pad_maximum_fusion.6), channel_id=1, source_target_pairs={{0,4},{4,8},{8,12},{12,14},{14,10},{10,6},{6,2},{2,0},{1,5},{5,9},... | collective-permute-start | bytes 589832 | tf_op jit(solution)/shard_map/ppermute | solution.py:55
  193.4 5.7 %collective-permute-start.34 = (bf16[96,1024]{1,0:T(8,128)(2,1)S(1)}, bf16[96,1024]{1,0:T(8,128)(2,1)S(1)}, u32[]{:S(2)}, u32[]{:S(2)}) collective-permute-start(bf16[96,1024]{1,0:T(8,128)(2,1)S(1)} %get-tuple-element.206), channel_id=1, source_target_pairs={{0,4},{4,8},{8,12},{12,14},{14,10},{10,6},{6,2},{2,0},{1,5},{5,9},... | collective-permute-start | bytes 589832 | tf_op jit(solution)/shard_map/ppermute | solution.py:55
  194.1 5.7 %collective-permute-start.35 = (bf16[96,1024]{1,0:T(8,128)(2,1)S(1)}, bf16[96,1024]{1,0:T(8,128)(2,1)S(1)}, u32[]{:S(2)}, u32[]{:S(2)}) collective-permute-start(bf16[96,1024]{1,0:T(8,128)(2,1)S(1)} %get-tuple-element.205), channel_id=1, source_target_pairs={{0,2},{4,0},{8,4},{12,8},{14,12},{10,14},{6,10},{2,6},{1,3},{5,1},... | collective-permute-start | bytes 589832 | tf_op jit(solution)/shard_map/ppermute | solution.py:55
  195.6 8.6 %copy-start.8 = (bf16[512,1024]{1,0:T(8,128)(2,1)S(1)}, bf16[512,1024]{1,0:T(8,128)(2,1)}, u32[]{:S(2)}) copy-start(bf16[512,1024]{1,0:T(8,128)(2,1)} %param.14) | copy-start | bytes 3145732
  195.6 8.6 %copy-start.9 = (bf16[512,1024]{1,0:T(8,128)(2,1)S(1)}, bf16[512,1024]{1,0:T(8,128)(2,1)}, u32[]{:S(2)}) copy-start(bf16[512,1024]{1,0:T(8,128)(2,1)} %param.13) | copy-start | bytes 3145732
  195.7 8.6 %copy-start.12 = (f32[1024]{0:T(1024)S(1)}, f32[1024]{0:T(1024)}, u32[]{:S(2)}) copy-start(f32[1024]{0:T(1024)} %param.15) | copy-start | bytes 12292
  195.7 6.3 %collective-permute-start.40 = (bf16[96,1024]{1,0:T(8,128)(2,1)S(1)}, bf16[96,1024]{1,0:T(8,128)(2,1)S(1)}, u32[]{:S(2)}, u32[]{:S(2)}) collective-permute-start(bf16[96,1024]{1,0:T(8,128)(2,1)S(1)} %get-tuple-element.204), channel_id=1, source_target_pairs={{0,4},{4,8},{8,12},{12,14},{14,10},{10,6},{6,2},{2,0},{1,5},{5,9},... | collective-permute-start | bytes 589832 | tf_op jit(solution)/shard_map/ppermute | solution.py:55
  196.4 5.7 %collective-permute-start.41 = (bf16[96,1024]{1,0:T(8,128)(2,1)S(1)}, bf16[96,1024]{1,0:T(8,128)(2,1)S(1)}, u32[]{:S(2)}, u32[]{:S(2)}) collective-permute-start(bf16[96,1024]{1,0:T(8,128)(2,1)S(1)} %get-tuple-element.203), channel_id=1, source_target_pairs={{0,2},{4,0},{8,4},{12,8},{14,12},{10,14},{6,10},{2,6},{1,3},{5,1},... | collective-permute-start | bytes 589832 | tf_op jit(solution)/shard_map/ppermute | solution.py:55
  199.9 8.3 %collective-permute-start.38 = (bf16[96,1024]{1,0:T(8,128)(2,1)S(1)}, bf16[96,1024]{1,0:T(8,128)(2,1)S(1)}, u32[]{:S(2)}, u32[]{:S(2)}) collective-permute-start(bf16[96,1024]{1,0:T(8,128)(2,1)S(1)} %get-tuple-element.202), channel_id=1, source_target_pairs={{0,4},{4,8},{8,12},{12,14},{14,10},{10,6},{6,2},{2,0},{1,5},{5,9},... | collective-permute-start | bytes 589832 | tf_op jit(solution)/shard_map/ppermute | solution.py:55
  200.2 7.9 %collective-permute-start.39 = (bf16[96,1024]{1,0:T(8,128)(2,1)S(1)}, bf16[96,1024]{1,0:T(8,128)(2,1)S(1)}, u32[]{:S(2)}, u32[]{:S(2)}) collective-permute-start(bf16[96,1024]{1,0:T(8,128)(2,1)S(1)} %get-tuple-element.201), channel_id=1, source_target_pairs={{0,2},{4,0},{8,4},{12,8},{14,12},{10,14},{6,10},{2,6},{1,3},{5,1},... | collective-permute-start | bytes 589832 | tf_op jit(solution)/shard_map/ppermute | solution.py:55
  202.2 5.7 %collective-permute-start.42 = (bf16[96,1024]{1,0:T(8,128)(2,1)S(1)}, bf16[96,1024]{1,0:T(8,128)(2,1)S(1)}, u32[]{:S(2)}, u32[]{:S(2)}) collective-permute-start(bf16[96,1024]{1,0:T(8,128)(2,1)S(1)} %get-tuple-element.199), channel_id=1, source_target_pairs={{0,4},{4,8},{8,12},{12,14},{14,10},{10,6},{6,2},{2,0},{1,5},{5,9},... | collective-permute-start | bytes 589832 | tf_op jit(solution)/shard_map/ppermute | solution.py:55
  202.5 5.7 %collective-permute-start.43 = (bf16[96,1024]{1,0:T(8,128)(2,1)S(1)}, bf16[96,1024]{1,0:T(8,128)(2,1)S(1)}, u32[]{:S(2)}, u32[]{:S(2)}) collective-permute-start(bf16[96,1024]{1,0:T(8,128)(2,1)S(1)} %get-tuple-element.200), channel_id=1, source_target_pairs={{0,2},{4,0},{8,4},{12,8},{14,12},{10,14},{6,10},{2,6},{1,3},{5,1},... | collective-permute-start | bytes 589832 | tf_op jit(solution)/shard_map/ppermute | solution.py:55

commit v14 on v13

--- a/solution.py
+++ b/solution.py
@@ -8,7 +8,7 @@
 from jax.experimental.pallas import tpu as pltpu
 from jax.sharding import PartitionSpec as P
 
-VMEM_LIMIT = 50 * 1024 * 1024
+VMEM_LIMIT = 49 * 1024 * 1024
 DEEP, PARTS = 3, 4
 LANES = 128
 
@@ -493,7 +493,7 @@
     def term_of(opened, closed, rows=slice(None)):
         def term(distance):
             index = order.index(distance)
-            return (opened[index] if index < early else closed[index - early])[rows]
+            return (opened[index] if index < len(opened) else closed[index - len(opened)])[rows]
 
         return term
 
@@ -538,31 +538,29 @@
         sums_a = scatter_sums(scatter_send(sums_a), term_a, count, distances.pop(0))
     for distance in distances:
         sums_a = scatter_sums(scatter_send(sums_a), term_a, count, distance)
-    opened_b = open_down(hidden_b, sums_a)
+    terms_b = down(0, count, tiles, after(hidden_b, sums_a), down_weight, other_down, width)
     moved_a = scatter_send(sums_a)
     spans = [slice(0, size_b // 2), slice(size_b // 2, size_b)]
-    distances = list(range(half, 0, -1))
     parts_b = [None, None]
-    closed_b = None
-    earlier = []
-    for number, distance in enumerate(distances):
+    earlier = moved_a
+    for distance in range(half, 0, -1):
         for which, span in enumerate(spans):
-            moved = scatter_send(parts_b[which]) if number else None
-            tied = (earlier, moved_a)
-            parts_b[which] = scatter_sums(moved, term_of(opened_b, closed_b, span), count, distance, tied)
+            moved = scatter_send(parts_b[which]) if distance < half else None
+            parts_b[which] = scatter_sums(moved, term_of(terms_b, None, span), count, distance, earlier)
             earlier = parts_b[which]
-        if number == 1:
-            closed_b = close_down(hidden_b, parts_b)
     moved_b = [scatter_send(part) for part in parts_b]
-    terms_b = [term_of(opened_b, closed_b, span) for span in spans]
+    terms_b = [term_of(terms_b, None, span) for span in spans]
 
     def finish(start, term, moved):
         ffn = term(0).astype(jnp.float32) + moved[0].astype(jnp.float32) + moved[1].astype(jnp.float32)
         rows = slice(start, start + ffn.shape[0])
         return (mix(noisy_input[rows], self_cond[rows]) + ffn).astype(jnp.bfloat16)
 
-    outs = [finish(span.start, term, moved) for span, term, moved in zip(spans, terms_b, moved_b)]
-    return jnp.concatenate([*outs, finish(size_b, term_a, moved_a)], axis=0)
+    result = jnp.zeros((row_count, width), noisy_input.dtype)
+    result = lax.dynamic_update_slice(result, finish(size_b, term_a, moved_a), (size_b, 0))
+    for span, term, moved in zip(spans, terms_b, moved_b):
+        result = lax.dynamic_update_slice(result, finish(span.start, term, moved), (span.start, 0))
+    return result
 
 
 def solution(mesh):

time: 210 us -> 202 us (0.962)
  Pallas kernels: 105 us -> 99.9 us
    pallas_call x4 -> x3, Pallas kernels: 34.3 us -> 30.6 us  [down(): pl.pallas_call(functools.partial(down_kernel, start, stop - start), out_s...]
    unnamed x26 -> x16, local copies, waits for them, and re-layouts: 2.23 us -> 0.04 us
  transfers between devices with their start and end apart: 44 -> 44, of which waited for: 13 -> 19; matrix products, arithmetic and copies ran while one was open for 4% -> 4% of each run, Pallas kernels for 50% -> 49%
where the time goes in v14:
time: 202 us
  Pallas kernels  99.9 us (49%)
  waiting for transfers between devices  45.5 us (23%)
  starting transfers between devices  44.9 us (22%)
  other arithmetic  8.5 us (4%)
    ppermute x40, waiting for transfers between devices, ring_shift(): lax.ppermute(value, 'blk', [(ring[i], ring[(i + steps) % count]) for i in...  45.5 us
    pallas_call x3, Pallas kernels, gate_up(): pl.pallas_call(functools.partial(gate_up_kernel, fixed), out_shape=(jax.S...  42.9 us
    ppermute x40, starting transfers between devices, ring_shift(): lax.ppermute(value, 'blk', [(ring[i], ring[(i + steps) % count]) for i in...  41.9 us
    pallas_call x3, Pallas kernels, down(): pl.pallas_call(functools.partial(down_kernel, start, stop - start), out_s...  30.6 us
    pallas_call x2, Pallas kernels, gate_up_columns(): pl.pallas_call(functools.partial(columns_kernel, start, width * count, no...  26.5 us
  transfers between devices with their start and end apart: 44, of which 19 were waited for; matrix products, arithmetic and copies ran while one was open for 4% of the time, Pallas kernels for 49%

profile of v14, /device:TPU:0, one launch (start us, length us, event | category | flops | bytes accessed | tf_op | source)
XLA Modules:
  0.0 202.0 jit_solution(6353308276185032230)
XLA Ops:
  0.0 0.8 multiply_add_fusion.2
  0.8 2.4 %collective-permute-start.6 = (f32[3,1024]{1,0:T(4,128)S(1)}, f32[3,1024]{1,0:T(4,128)S(1)}, u32[]{:S(2)}, u32[]{:S(2)}) collective-permute-start(f32[3,1024]{1,0:T(4,128)S(1)} %multiply_add_fusion.2), channel_id=1, source_target_pairs={{0,1},{2,3},{4,5},{6,7},{8,9},{10,11},{12,13},{14,15},{16,17},{18,... | collective-permute-start | bytes 36872 | tf_op jit(solution)/shard_map/ppermute | solution.py:453
  3.1 1.7 multiply_add_fusion
  5.5 0.9 constant_dynamic-slice_fusion.2
  6.4 0.6 multiply_convert_fusion.refs_0_
  7.7 2.4 %collective-permute-start = (bf16[320,1024]{1,0:T(8,128)(2,1)S(1)}, bf16[320,1024]{1,0:T(8,128)(2,1)S(1)}, u32[]{:S(2)}, u32[]{:S(2)}) collective-permute-start(bf16[320,1024]{1,0:T(8,128)(2,1)S(1)} %multiply_convert_fusion.refs_0_), channel_id=1, source_target_pairs={{0,4},{4,8},{8,12},{12,14},{14,10},{10,6},{6,2},{2,0},{1,5},{5,9},... | collective-permute-start | bytes 1966088 | tf_op jit(solution)/shard_map/ppermute | solution.py:55
  10.1 15.3 %collective-permute-done.refs_1_ = bf16[320,1024]{1,0:T(8,128)(2,1)S(1)} collective-permute-done((bf16[320,1024]{1,0:T(8,128)(2,1)S(1)}, bf16[320,1024]{1,0:T(8,128)(2,1)S(1)}, u32[]{:S(2)}, u32[]{:S(2)}) %collective-permute-start) | collective-permute-done | bytes 655392 | tf_op jit(solution)/shard_map/ppermute | solution.py:55
  25.4 1.5 collective-permute-done.1.refs_2_
  26.9 1.6 collective-permute-start.2
  28.9 0.7 dynamic-slice_bitcast_fusion
  29.6 1.3 multiply_add_fusion.1
  31.3 11.6 %collective-permute-done.2.refs_3_ = bf16[320,1024]{1,0:T(8,128)(2,1)S(1)} collective-permute-done((bf16[320,1024]{1,0:T(8,128)(2,1)S(1)}, bf16[320,1024]{1,0:T(8,128)(2,1)S(1)}, u32[]{:S(2)}, u32[]{:S(2)}) %collective-permute-start.2) | collective-permute-done | bytes 655392 | tf_op jit(solution)/shard_map/ppermute | solution.py:55
  42.9 1.3 collective-permute-done.3.refs_4_
  44.2 1.6 collective-permute-start.4
  46.2 13.6 %gate_up.5 = (f32[320,2048]{1,0:T(8,128)}, f32[320,128]{1,0:T(8,128)S(1)}) custom-call(s32[3,8]{1,0:T(4,128)S(1)} %get-tuple-element.223.blocks_ref, s32[5,5]{1,0:T(8,128)S(1)} %copy-done.3, bf16[320,1024]{1,0:T(8,128)(2,1)S(1)} %multiply_convert_fusion.refs_0_, bf16[320,1024]{1,0:T(8,128)(2,1)S(1)} %collective-permute-done.refs_1_, ...), custom_call_target="tpu_custom_call" | custom-call | flops 13421772800 | bytes 20971520 | tf_op jit(solution)/shard_map/gate_up/pallas_call | solution.py:181
  60.2 1.5 collective-permute-start.10
  62.3 1.6 collective-permute-start.8
  63.9 0.6 collective-permute-start.9
  64.5 16.5 %gate_up.6 = (f32[320,2048]{1,0:T(8,128)}, f32[320,128]{1,0:T(8,128)S(1)}) custom-call(s32[3,8]{1,0:T(4,128)S(1)} %get-tuple-element.223.blocks_ref, s32[5,7]{1,0:T(8,128)S(1)} %copy-done.2, bf16[320,1024]{1,0:T(8,128)(2,1)S(1)} %multiply_convert_fusion.refs_0_, bf16[320,1024]{1,0:T(8,128)(2,1)S(1)} %collective-permute-done.refs_1_, ...), custom_call_target="tpu_custom_call" | custom-call | flops 18790481920 | bytes 29360128 | tf_op jit(solution)/shard_map/gate_up/pallas_call | solution.py:181
  81.1 1.6 collective-permute-start.13
  83.1 12.8 %gate_up.7 = (bf16[320,2048]{1,0:T(8,128)(2,1)S(1)}, f32[320,128]{1,0:T(8,128)}) custom-call(s32[3,8]{1,0:T(4,128)S(1)} %get-tuple-element.223.blocks_ref, s32[5,4]{1,0:T(8,128)S(1)} %copy-done.1, bf16[320,1024]{1,0:T(8,128)(2,1)S(1)} %collective-permute-done.4.refs_5_.refs_0_, bf16[320,1024]{1,0:T(8,128)(2,1)S(1)} %collective-permute-done.5.refs_6_.refs_1_, ...), custom_call_target="tpu_custom_call" | custom-call | flops 10737418240 | bytes 16777216 | tf_op jit(solution)/shard_map/gate_up/pallas_call | solution.py:181
  95.9 1.6 collective-permute-start.16
  98.0 7.4 %down.3 = bf16[3,320,1024]{2,1,0:T(8,128)(2,1)S(1)} custom-call(s32[3,8]{1,0:T(4,128)S(1)} %get-tuple-element.224.tiles_ref, bf16[320,2048]{1,0:T(8,128)(2,1)S(1)} %get-tuple-element.139.refs_0_, bf16[2048,4096]{1,0:T(8,128)(2,1)} %refs_2_.1, bf16[2048,4096]{1,0:T(8,128)(2,1)} %collective-permute-done.15.refs_2_.refs_3_), custom_call_target="tpu_custom_call" | custom-call | flops 8053063680 | bytes 12582912 | tf_op jit(solution)/shard_map/down/pallas_call | solution.py:373
  105.9 1.3 collective-permute-start.26
  107.2 0.8 collective-permute-start.27
  108.0 1.2 collective-permute-start.18
  109.3 0.8 collective-permute-start.19
  110.1 10.6 %down.4 = bf16[5,320,1024]{2,1,0:T(8,128)(2,1)S(1)} custom-call(s32[3,8]{1,0:T(4,128)S(1)} %get-tuple-element.224.tiles_ref, bf16[320,2048]{1,0:T(8,128)(2,1)S(1)} %get-tuple-element.139.refs_0_, bf16[2048,4096]{1,0:T(8,128)(2,1)} %refs_2_.1, bf16[2048,4096]{1,0:T(8,128)(2,1)} %collective-permute-done.15.refs_2_.refs_3_), custom_call_target="tpu_custom_call" | custom-call | flops 13421772800 | bytes 20971520 | tf_op jit(solution)/shard_map/down/pallas_call | solution.py:373
  121.0 0.6 collective-permute-start.21
  121.6 1.5 collective-permute-start.20
  123.1 13.2 %gate_up.8 = (bf16[192,1024]{1,0:T(8,128)(2,1)S(1)}, f32[192,128]{1,0:T(8,128)S(1)}) custom-call(s32[3,8]{1,0:T(4,128)S(1)} %get-tuple-element.223.blocks_ref, bf16[192,1024]{1,0:T(8,128)(2,1)S(1)} %multiply_convert_fusion.1.refs_0_, bf16[192,1024]{1,0:T(8,128)(2,1)S(1)} %collective-permute-done.10.refs_1_, ...), custom_call_target="tpu_custom_call" | custom-call | flops 12884901888 | bytes 33554432 | tf_op jit(solution)/shard_map/gate_up/pallas_call | solution.py:302
  136.4 0.6 fusion.5
  137.0 1.3 collective-permute-start.22
  138.3 0.8 collective-permute-start.23
  139.1 13.3 %gate_up.9 = (bf16[192,1024]{1,0:T(8,128)(2,1)S(1)}, f32[192,128]{1,0:T(8,128)}) custom-call(s32[3,8]{1,0:T(4,128)S(1)} %get-tuple-element.223.blocks_ref, bf16[192,1024]{1,0:T(8,128)(2,1)S(1)} %multiply_convert_fusion.1.refs_0_, bf16[192,1024]{1,0:T(8,128)(2,1)S(1)} %collective-permute-done.10.refs_1_, ...), custom_call_target="tpu_custom_call" | custom-call | flops 12884901888 | bytes 33554432 | tf_op jit(solution)/shard_map/gate_up/pallas_call | solution.py:302
  152.4 0.6 fusion.7
  152.9 1.3 collective-permute-start.24
  154.3 0.8 collective-permute-start.25
  155.0 12.6 %down.5 = bf16[8,192,1024]{2,1,0:T(8,128)(2,1)S(1)} custom-call(s32[3,8]{1,0:T(4,128)S(1)} %get-tuple-element.224.tiles_ref, bf16[192,1024]{1,0:T(8,128)(2,1)S(1)} %get-tuple-element.171.refs_0_, bf16[192,1024]{1,0:T(8,128)(2,1)S(1)} %get-tuple-element.172.refs_1_, bf16[2048,4096]{1,0:T(8,128)(2,1)} %refs_2_.1, ...), custom_call_target="tpu_custom_call" | custom-call | flops 12884901888 | bytes 33554432 | tf_op jit(solution)/shard_map/down/pallas_call | solution.py:373
  167.7 1.3 collective-permute-start.28
  169.0 0.8 collective-permute-start.29
  169.7 1.3 collective-permute-start.32
  171.0 0.8 collective-permute-start.33
  171.8 0.7 fusion.10
  172.6 0.9 collective-permute-done.28
  174.5 1.6 collective-permute-start.30
  176.5 1.1 collective-permute-start.37
  177.6 1.0 collective-permute-start.36
  178.6 1.7 collective-permute-done.31
  180.3 1.9 collective-permute-done.30
  182.4 1.7 collective-permute-start.34
  184.5 1.6 collective-permute-done.36
  186.3 2.0 %collective-permute-start.40 = (bf16[96,1024]{1,0:T(8,128)(2,1)S(1)}, bf16[96,1024]{1,0:T(8,128)(2,1)S(1)}, u32[]{:S(2)}, u32[]{:S(2)}) collective-permute-start(bf16[96,1024]{1,0:T(8,128)(2,1)S(1)} %get-tuple-element.198), channel_id=1, source_target_pairs={{0,4},{4,8},{8,12},{12,14},{14,10},{10,6},{6,2},{2,0},{1,5},{5,9},... | collective-permute-start | bytes 589832 | tf_op jit(solution)/shard_map/ppermute | solution.py:55
  188.3 1.5 collective-permute-done.34
  189.9 1.8 collective-permute-done.35
  191.8 0.7 collective-permute-start.38
  192.4 1.4 collective-permute-start.39
  194.1 1.3 collective-permute-start.42
  195.5 0.7 collective-permute-start.43
  196.2 1.3 collective-permute-done.38
  197.5 0.6 collective-permute-done.39
  198.3 1.6 collective-permute-done.42
  199.8 1.3 collective-permute-done.43
  201.1 0.8 fusion.37
  (83 shorter events, 7.6 us)
Async XLA Ops:
  0.8 6.3 %collective-permute-start.6 = (f32[3,1024]{1,0:T(4,128)S(1)}, f32[3,1024]{1,0:T(4,128)S(1)}, u32[]{:S(2)}, u32[]{:S(2)}) collective-permute-start(f32[3,1024]{1,0:T(4,128)S(1)} %multiply_add_fusion.2), channel_id=1, source_target_pairs={{0,1},{2,3},{4,5},{6,7},{8,9},{10,11},{12,13},{14,15},{16,17},{18,... | collective-permute-start | bytes 36872 | tf_op jit(solution)/shard_map/ppermute | solution.py:453
  3.1 2.3 %copy-start = (f32[8192]{0:T(1024)S(1)}, f32[8192]{0:T(1024)}, u32[]{:S(2)}) copy-start(f32[8192]{0:T(1024)} %param.18) | copy-start | bytes 98308
  6.4 23.2 %copy-start.7 = (f32[1024]{0:T(1024)S(1)}, f32[1024]{0:T(1024)}, u32[]{:S(2)}) copy-start(f32[1024]{0:T(1024)} %param.15) | copy-start | bytes 12292
  7.0 39.2 %collective-permute-start.7 = (bf16[4096,2048]{1,0:T(8,128)(2,1)}, bf16[4096,2048]{1,0:T(8,128)(2,1)}, u32[]{:S(2)}, u32[]{:S(2)}) collective-permute-start(bf16[4096,2048]{1,0:T(8,128)(2,1)} %refs_10_.5), channel_id=1, source_target_pairs={{0,1},{1,0},{2,3},{3,2},{4,5},{5,4},{6,7},{7,6},{8,9},{9,8},{10,11... | collective-permute-start | bytes 50331656 | tf_op jit(solution)/shard_map/ppermute | solution.py:59
  7.1 56.8 %collective-permute-start.12 = (bf16[4096,2048]{1,0:T(8,128)(2,1)}, bf16[4096,2048]{1,0:T(8,128)(2,1)}, u32[]{:S(2)}, u32[]{:S(2)}) collective-permute-start(bf16[4096,2048]{1,0:T(8,128)(2,1)} %refs_12_.3), channel_id=1, source_target_pairs={{0,1},{1,0},{2,3},{3,2},{4,5},{5,4},{6,7},{7,6},{8,9},{9,8},{10,11... | collective-permute-start | bytes 50331656 | tf_op jit(solution)/shard_map/ppermute | solution.py:59
  7.6 90.4 %collective-permute-start.15 = (bf16[2048,4096]{1,0:T(8,128)(2,1)}, bf16[2048,4096]{1,0:T(8,128)(2,1)}, u32[]{:S(2)}, u32[]{:S(2)}) collective-permute-start(bf16[2048,4096]{1,0:T(8,128)(2,1)} %refs_2_.1), channel_id=1, source_target_pairs={{0,1},{1,0},{2,3},{3,2},{4,5},{5,4},{6,7},{7,6},{8,9},{9,8},{10,11... | collective-permute-start | bytes 50331656 | tf_op jit(solution)/shard_map/ppermute | solution.py:59
  7.7 17.7 %collective-permute-start = (bf16[320,1024]{1,0:T(8,128)(2,1)S(1)}, bf16[320,1024]{1,0:T(8,128)(2,1)S(1)}, u32[]{:S(2)}, u32[]{:S(2)}) collective-permute-start(bf16[320,1024]{1,0:T(8,128)(2,1)S(1)} %multiply_convert_fusion.refs_0_), channel_id=1, source_target_pairs={{0,4},{4,8},{8,12},{12,14},{14,10},{10,6},{6,2},{2,0},{1,5},{5,9},... | collective-permute-start | bytes 1966088 | tf_op jit(solution)/shard_map/ppermute | solution.py:55
  10.1 16.8 %collective-permute-start.1 = (bf16[320,1024]{1,0:T(8,128)(2,1)S(1)}, bf16[320,1024]{1,0:T(8,128)(2,1)S(1)}, u32[]{:S(2)}, u32[]{:S(2)}) collective-permute-start(bf16[320,1024]{1,0:T(8,128)(2,1)S(1)} %multiply_convert_fusion.refs_0_), channel_id=1, source_target_pairs={{0,2},{4,0},{8,4},{12,8},{14,12},{10,14},{6,10},{2,6},{1,3},{5,1},... | collective-permute-start | bytes 1966088 | tf_op jit(solution)/shard_map/ppermute | solution.py:55
  26.9 16.0 %collective-permute-start.2 = (bf16[320,1024]{1,0:T(8,128)(2,1)S(1)}, bf16[320,1024]{1,0:T(8,128)(2,1)S(1)}, u32[]{:S(2)}, u32[]{:S(2)}) collective-permute-start(bf16[320,1024]{1,0:T(8,128)(2,1)S(1)} %collective-permute-done.refs_1_), channel_id=1, source_target_pairs={{0,4},{4,8},{8,12},{12,14},{14,10},{10,6},{6,2},{2,0},{1,5},{5,9},... | collective-permute-start | bytes 1966088 | tf_op jit(solution)/shard_map/ppermute | solution.py:55
  28.5 15.7 %collective-permute-start.3 = (bf16[320,1024]{1,0:T(8,128)(2,1)S(1)}, bf16[320,1024]{1,0:T(8,128)(2,1)S(1)}, u32[]{:S(2)}, u32[]{:S(2)}) collective-permute-start(bf16[320,1024]{1,0:T(8,128)(2,1)S(1)} %collective-permute-done.1.refs_2_), channel_id=1, source_target_pairs={{0,2},{4,0},{8,4},{12,8},{14,12},{10,14},{6,10},{2,6},{1,3},{5,1},... | collective-permute-start | bytes 1966088 | tf_op jit(solution)/shard_map/ppermute | solution.py:55
  29.6 16.6 %copy-start.3 = (s32[5,5]{1,0:T(8,128)S(1)}, s32[5,5]{1,0:T(8,128)}, u32[]{:S(2)}) copy-start(s32[5,5]{1,0:T(8,128)} %constant.40.clone.units_ref) | copy-start | bytes 304
  44.2 15.6 %collective-permute-start.4 = (bf16[320,1024]{1,0:T(8,128)(2,1)S(1)}, bf16[320,1024]{1,0:T(8,128)(2,1)S(1)}, u32[]{:S(2)}, u32[]{:S(2)}) collective-permute-start(bf16[320,1024]{1,0:T(8,128)(2,1)S(1)} %collective-permute-done.2.refs_3_), channel_id=1, source_target_pairs={{0,4},{4,8},{8,12},{12,14},{14,10},{10,6},{6,2},{2,0},{1,5},{5,9},... | collective-permute-start | bytes 1966088 | tf_op jit(solution)/shard_map/ppermute | solution.py:55
  45.8 14.5 %collective-permute-start.5 = (bf16[320,1024]{1,0:T(8,128)(2,1)S(1)}, bf16[320,1024]{1,0:T(8,128)(2,1)S(1)}, u32[]{:S(2)}, u32[]{:S(2)}) collective-permute-start(bf16[320,1024]{1,0:T(8,128)(2,1)S(1)} %collective-permute-done.3.refs_4_), channel_id=1, source_target_pairs={{0,2},{4,0},{8,4},{12,8},{14,12},{10,14},{6,10},{2,6},{1,3},{5,1},... | collective-permute-start | bytes 1966088 | tf_op jit(solution)/shard_map/ppermute | solution.py:55
  59.8 4.7 %copy-start.2 = (s32[5,7]{1,0:T(8,128)S(1)}, s32[5,7]{1,0:T(8,128)}, u32[]{:S(2)}) copy-start(s32[5,7]{1,0:T(8,128)} %constant.41.clone.units_ref) | copy-start | bytes 424
  60.2 20.8 %collective-permute-start.10 = (bf16[192,1024]{1,0:T(8,128)(2,1)S(1)}, bf16[192,1024]{1,0:T(8,128)(2,1)S(1)}, u32[]{:S(2)}, u32[]{:S(2)}) collective-permute-start(bf16[192,1024]{1,0:T(8,128)(2,1)S(1)} %multiply_convert_fusion.1.refs_0_), channel_id=1, source_target_pairs={{0,4},{4,8},{8,12},{12,14},{14,10},{10,6},{6,2},{2,0},{1,5},{5,9},... | collective-permute-start | bytes 1179656 | tf_op jit(solution)/shard_map/ppermute | solution.py:55
  61.8 19.3 %collective-permute-start.11 = (bf16[192,1024]{1,0:T(8,128)(2,1)S(1)}, bf16[192,1024]{1,0:T(8,128)(2,1)S(1)}, u32[]{:S(2)}, u32[]{:S(2)}) collective-permute-start(bf16[192,1024]{1,0:T(8,128)(2,1)S(1)} %multiply_convert_fusion.1.refs_0_), channel_id=1, source_target_pairs={{0,2},{4,0},{8,4},{12,8},{14,12},{10,14},{6,10},{2,6},{1,3},{5,1},... | collective-permute-start | bytes 1179656 | tf_op jit(solution)/shard_map/ppermute | solution.py:55
  62.3 18.7 %collective-permute-start.8 = (bf16[160,1024]{1,0:T(8,128)(2,1)S(1)}, bf16[160,1024]{1,0:T(8,128)(2,1)S(1)}, u32[]{:S(2)}, u32[]{:S(2)}) collective-permute-start(bf16[160,1024]{1,0:T(8,128)(2,1)S(1)} %slice.326), channel_id=1, source_target_pairs={{0,4},{4,8},{8,12},{12,14},{14,10},{10,6},{6,2},{2,0},{1,5},{5,9},... | collective-permute-start | bytes 983048 | tf_op jit(solution)/shard_map/ppermute | solution.py:55
  63.9 17.1 %collective-permute-start.9 = (bf16[160,1024]{1,0:T(8,128)(2,1)S(1)}, bf16[160,1024]{1,0:T(8,128)(2,1)S(1)}, u32[]{:S(2)}, u32[]{:S(2)}) collective-permute-start(bf16[160,1024]{1,0:T(8,128)(2,1)S(1)} %slice.327), channel_id=1, source_target_pairs={{0,2},{4,0},{8,4},{12,8},{14,12},{10,14},{6,10},{2,6},{1,3},{5,1},... | collective-permute-start | bytes 983048 | tf_op jit(solution)/shard_map/ppermute | solution.py:55
  64.5 18.7 %copy-start.1 = (s32[5,4]{1,0:T(8,128)S(1)}, s32[5,4]{1,0:T(8,128)}, u32[]{:S(2)}) copy-start(s32[5,4]{1,0:T(8,128)} %constant.42.clone.units_ref) | copy-start | bytes 244
  81.1 14.8 %collective-permute-start.13 = (bf16[192,1024]{1,0:T(8,128)(2,1)S(1)}, bf16[192,1024]{1,0:T(8,128)(2,1)S(1)}, u32[]{:S(2)}, u32[]{:S(2)}) collective-permute-start(bf16[192,1024]{1,0:T(8,128)(2,1)S(1)} %collective-permute-done.10.refs_1_), channel_id=1, source_target_pairs={{0,4},{4,8},{8,12},{12,14},{14,10},{10,6},{6,2},{2,0},{1,5},{5,9},... | collective-permute-start | bytes 1179656 | tf_op jit(solution)/shard_map/ppermute | solution.py:55
  82.6 13.3 %collective-permute-start.14 = (bf16[192,1024]{1,0:T(8,128)(2,1)S(1)}, bf16[192,1024]{1,0:T(8,128)(2,1)S(1)}, u32[]{:S(2)}, u32[]{:S(2)}) collective-permute-start(bf16[192,1024]{1,0:T(8,128)(2,1)S(1)} %collective-permute-done.11.refs_2_), channel_id=1, source_target_pairs={{0,2},{4,0},{8,4},{12,8},{14,12},{10,14},{6,10},{2,6},{1,3},{5,1},... | collective-permute-start | bytes 1179656 | tf_op jit(solution)/shard_map/ppermute | solution.py:55
  95.9 9.6 %collective-permute-start.16 = (bf16[192,1024]{1,0:T(8,128)(2,1)S(1)}, bf16[192,1024]{1,0:T(8,128)(2,1)S(1)}, u32[]{:S(2)}, u32[]{:S(2)}) collective-permute-start(bf16[192,1024]{1,0:T(8,128)(2,1)S(1)} %collective-permute-done.13.refs_3_), channel_id=1, source_target_pairs={{0,4},{4,8},{8,12},{12,14},{14,10},{10,6},{6,2},{2,0},{1,5},{5,9},... | collective-permute-start | bytes 1179656 | tf_op jit(solution)/shard_map/ppermute | solution.py:55
  97.5 8.4 %collective-permute-start.17 = (bf16[192,1024]{1,0:T(8,128)(2,1)S(1)}, bf16[192,1024]{1,0:T(8,128)(2,1)S(1)}, u32[]{:S(2)}, u32[]{:S(2)}) collective-permute-start(bf16[192,1024]{1,0:T(8,128)(2,1)S(1)} %collective-permute-done.14.refs_4_), channel_id=1, source_target_pairs={{0,2},{4,0},{8,4},{12,8},{14,12},{10,14},{6,10},{2,6},{1,3},{5,1},... | collective-permute-start | bytes 1179656 | tf_op jit(solution)/shard_map/ppermute | solution.py:55
  105.9 17.2 %collective-permute-start.26 = (bf16[96,1024]{1,0:T(8,128)(2,1)S(1)}, bf16[96,1024]{1,0:T(8,128)(2,1)S(1)}, u32[]{:S(2)}, u32[]{:S(2)}) collective-permute-start(bf16[96,1024]{1,0:T(8,128)(2,1)S(1)} %slice.350), channel_id=1, source_target_pairs={{0,4},{4,8},{8,12},{12,14},{14,10},{10,6},{6,2},{2,0},{1,5},{5,9},... | collective-permute-start | bytes 589832 | tf_op jit(solution)/shard_map/ppermute | solution.py:55
  107.2 15.9 %collective-permute-start.27 = (bf16[96,1024]{1,0:T(8,128)(2,1)S(1)}, bf16[96,1024]{1,0:T(8,128)(2,1)S(1)}, u32[]{:S(2)}, u32[]{:S(2)}) collective-permute-start(bf16[96,1024]{1,0:T(8,128)(2,1)S(1)} %slice.351), channel_id=1, source_target_pairs={{0,2},{4,0},{8,4},{12,8},{14,12},{10,14},{6,10},{2,6},{1,3},{5,1},... | collective-permute-start | bytes 589832 | tf_op jit(solution)/shard_map/ppermute | solution.py:55
  108.0 12.6 %collective-permute-start.18 = (bf16[160,1024]{1,0:T(8,128)(2,1)S(1)}, bf16[160,1024]{1,0:T(8,128)(2,1)S(1)}, u32[]{:S(2)}, u32[]{:S(2)}) collective-permute-start(bf16[160,1024]{1,0:T(8,128)(2,1)S(1)} %get-tuple-element.140), channel_id=1, source_target_pairs={{0,4},{4,8},{8,12},{12,14},{14,10},{10,6},{6,2},{2,0},{1,5},{5,9},... | collective-permute-start | bytes 983048 | tf_op jit(solution)/shard_map/ppermute | solution.py:55
  109.3 11.4 %collective-permute-start.19 = (bf16[160,1024]{1,0:T(8,128)(2,1)S(1)}, bf16[160,1024]{1,0:T(8,128)(2,1)S(1)}, u32[]{:S(2)}, u32[]{:S(2)}) collective-permute-start(bf16[160,1024]{1,0:T(8,128)(2,1)S(1)} %get-tuple-element.141), channel_id=1, source_target_pairs={{0,2},{4,0},{8,4},{12,8},{14,12},{10,14},{6,10},{2,6},{1,3},{5,1},... | collective-permute-start | bytes 983048 | tf_op jit(solution)/shard_map/ppermute | solution.py:55
  121.0 15.4 %collective-permute-start.21 = (bf16[320,1024]{1,0:T(8,128)(2,1)S(1)}, bf16[320,1024]{1,0:T(8,128)(2,1)S(1)}, u32[]{:S(2)}, u32[]{:S(2)}) collective-permute-start(bf16[320,1024]{1,0:T(8,128)(2,1)S(1)} %pad_maximum_fusion.2), channel_id=1, source_target_pairs={{0,2},{4,0},{8,4},{12,8},{14,12},{10,14},{6,10},{2,6},{1,3},{5,1},... | collective-permute-start | bytes 1966088 | tf_op jit(solution)/shard_map/ppermute | solution.py:55
  121.6 14.8 %collective-permute-start.20 = (bf16[320,1024]{1,0:T(8,128)(2,1)S(1)}, bf16[320,1024]{1,0:T(8,128)(2,1)S(1)}, u32[]{:S(2)}, u32[]{:S(2)}) collective-permute-start(bf16[320,1024]{1,0:T(8,128)(2,1)S(1)} %pad_maximum_fusion.1), channel_id=1, source_target_pairs={{0,4},{4,8},{8,12},{12,14},{14,10},{10,6},{6,2},{2,0},{1,5},{5,9},... | collective-permute-start | bytes 1966088 | tf_op jit(solution)/shard_map/ppermute | solution.py:55
  137.0 15.4 %collective-permute-start.22 = (bf16[320,1024]{1,0:T(8,128)(2,1)S(1)}, bf16[320,1024]{1,0:T(8,128)(2,1)S(1)}, u32[]{:S(2)}, u32[]{:S(2)}) collective-permute-start(bf16[320,1024]{1,0:T(8,128)(2,1)S(1)} %get-tuple-element.192), channel_id=1, source_target_pairs={{0,4},{4,8},{8,12},{12,14},{14,10},{10,6},{6,2},{2,0},{1,5},{5,9},... | collective-permute-start | bytes 1966088 | tf_op jit(solution)/shard_map/ppermute | solution.py:55
  138.3 14.1 %collective-permute-start.23 = (bf16[320,1024]{1,0:T(8,128)(2,1)S(1)}, bf16[320,1024]{1,0:T(8,128)(2,1)S(1)}, u32[]{:S(2)}, u32[]{:S(2)}) collective-permute-start(bf16[320,1024]{1,0:T(8,128)(2,1)S(1)} %get-tuple-element.191), channel_id=1, source_target_pairs={{0,2},{4,0},{8,4},{12,8},{14,12},{10,14},{6,10},{2,6},{1,3},{5,1},... | collective-permute-start | bytes 1966088 | tf_op jit(solution)/shard_map/ppermute | solution.py:55
  152.9 14.7 %collective-permute-start.24 = (bf16[320,1024]{1,0:T(8,128)(2,1)S(1)}, bf16[320,1024]{1,0:T(8,128)(2,1)S(1)}, u32[]{:S(2)}, u32[]{:S(2)}) collective-permute-start(bf16[320,1024]{1,0:T(8,128)(2,1)S(1)} %get-tuple-element.189), channel_id=1, source_target_pairs={{0,4},{4,8},{8,12},{12,14},{14,10},{10,6},{6,2},{2,0},{1,5},{5,9},... | collective-permute-start | bytes 1966088 | tf_op jit(solution)/shard_map/ppermute | solution.py:55
  154.3 13.4 %collective-permute-start.25 = (bf16[320,1024]{1,0:T(8,128)(2,1)S(1)}, bf16[320,1024]{1,0:T(8,128)(2,1)S(1)}, u32[]{:S(2)}, u32[]{:S(2)}) collective-permute-start(bf16[320,1024]{1,0:T(8,128)(2,1)S(1)} %get-tuple-element.190), channel_id=1, source_target_pairs={{0,2},{4,0},{8,4},{12,8},{14,12},{10,14},{6,10},{2,6},{1,3},{5,1},... | collective-permute-start | bytes 1966088 | tf_op jit(solution)/shard_map/ppermute | solution.py:55
  155.0 16.8 %copy-start.5 = (bf16[512,1024]{1,0:T(8,128)(2,1)S(1)}, bf16[512,1024]{1,0:T(8,128)(2,1)}, u32[]{:S(2)}) copy-start(bf16[512,1024]{1,0:T(8,128)(2,1)} %param.13) | copy-start | bytes 3145732
  167.6 4.2 %copy-start.4 = (bf16[512,1024]{1,0:T(8,128)(2,1)S(1)}, bf16[512,1024]{1,0:T(8,128)(2,1)}, u32[]{:S(2)}) copy-start(bf16[512,1024]{1,0:T(8,128)(2,1)} %param.14) | copy-start | bytes 3145732
  167.7 5.8 %collective-permute-start.28 = (bf16[48,1024]{1,0:T(8,128)(2,1)S(1)}, bf16[48,1024]{1,0:T(8,128)(2,1)S(1)}, u32[]{:S(2)}, u32[]{:S(2)}) collective-permute-start(bf16[48,1024]{1,0:T(8,128)(2,1)S(1)} %get-tuple-element.173), channel_id=1, source_target_pairs={{0,4},{4,8},{8,12},{12,14},{14,10},{10,6},{6,2},{2,0},{1,5},{5,9},... | collective-permute-start | bytes 294920 | tf_op jit(solution)/shard_map/ppermute | solution.py:55
  169.0 4.9 %collective-permute-start.29 = (bf16[48,1024]{1,0:T(8,128)(2,1)S(1)}, bf16[48,1024]{1,0:T(8,128)(2,1)S(1)}, u32[]{:S(2)}, u32[]{:S(2)}) collective-permute-start(bf16[48,1024]{1,0:T(8,128)(2,1)S(1)} %get-tuple-element.174), channel_id=1, source_target_pairs={{0,2},{4,0},{8,4},{12,8},{14,12},{10,14},{6,10},{2,6},{1,3},{5,1},... | collective-permute-start | bytes 294920 | tf_op jit(solution)/shard_map/ppermute | solution.py:55
  169.7 6.4 %collective-permute-start.32 = (bf16[48,1024]{1,0:T(8,128)(2,1)S(1)}, bf16[48,1024]{1,0:T(8,128)(2,1)S(1)}, u32[]{:S(2)}, u32[]{:S(2)}) collective-permute-start(bf16[48,1024]{1,0:T(8,128)(2,1)S(1)} %get-tuple-element.175), channel_id=1, source_target_pairs={{0,4},{4,8},{8,12},{12,14},{14,10},{10,6},{6,2},{2,0},{1,5},{5,9},... | collective-permute-start | bytes 294920 | tf_op jit(solution)/shard_map/ppermute | solution.py:55
  171.0 5.4 %collective-permute-start.33 = (bf16[48,1024]{1,0:T(8,128)(2,1)S(1)}, bf16[48,1024]{1,0:T(8,128)(2,1)S(1)}, u32[]{:S(2)}, u32[]{:S(2)}) collective-permute-start(bf16[48,1024]{1,0:T(8,128)(2,1)S(1)} %get-tuple-element.176), channel_id=1, source_target_pairs={{0,2},{4,0},{8,4},{12,8},{14,12},{10,14},{6,10},{2,6},{1,3},{5,1},... | collective-permute-start | bytes 294920 | tf_op jit(solution)/shard_map/ppermute | solution.py:55
  174.0 6.3 %collective-permute-start.31 = (bf16[96,1024]{1,0:T(8,128)(2,1)S(1)}, bf16[96,1024]{1,0:T(8,128)(2,1)S(1)}, u32[]{:S(2)}, u32[]{:S(2)}) collective-permute-start(bf16[96,1024]{1,0:T(8,128)(2,1)S(1)} %pad_maximum_fusion.4), channel_id=1, source_target_pairs={{0,2},{4,0},{8,4},{12,8},{14,12},{10,14},{6,10},{2,6},{1,3},{5,1},... | collective-permute-start | bytes 589832 | tf_op jit(solution)/shard_map/ppermute | solution.py:55
  174.5 7.7 %collective-permute-start.30 = (bf16[96,1024]{1,0:T(8,128)(2,1)S(1)}, bf16[96,1024]{1,0:T(8,128)(2,1)S(1)}, u32[]{:S(2)}, u32[]{:S(2)}) collective-permute-start(bf16[96,1024]{1,0:T(8,128)(2,1)S(1)} %pad_maximum_fusion.3), channel_id=1, source_target_pairs={{0,4},{4,8},{8,12},{12,14},{14,10},{10,6},{6,2},{2,0},{1,5},{5,9},... | collective-permute-start | bytes 589832 | tf_op jit(solution)/shard_map/ppermute | solution.py:55
  176.5 8.1 %collective-permute-start.37 = (bf16[96,1024]{1,0:T(8,128)(2,1)S(1)}, bf16[96,1024]{1,0:T(8,128)(2,1)S(1)}, u32[]{:S(2)}, u32[]{:S(2)}) collective-permute-start(bf16[96,1024]{1,0:T(8,128)(2,1)S(1)} %pad_maximum_fusion.6), channel_id=1, source_target_pairs={{0,2},{4,0},{8,4},{12,8},{14,12},{10,14},{6,10},{2,6},{1,3},{5,1},... | collective-permute-start | bytes 589832 | tf_op jit(solution)/shard_map/ppermute | solution.py:55
  177.6 8.5 %collective-permute-start.36 = (bf16[96,1024]{1,0:T(8,128)(2,1)S(1)}, bf16[96,1024]{1,0:T(8,128)(2,1)S(1)}, u32[]{:S(2)}, u32[]{:S(2)}) collective-permute-start(bf16[96,1024]{1,0:T(8,128)(2,1)S(1)} %pad_maximum_fusion.5), channel_id=1, source_target_pairs={{0,4},{4,8},{8,12},{12,14},{14,10},{10,6},{6,2},{2,0},{1,5},{5,9},... | collective-permute-start | bytes 589832 | tf_op jit(solution)/shard_map/ppermute | solution.py:55
  182.4 7.5 %collective-permute-start.34 = (bf16[96,1024]{1,0:T(8,128)(2,1)S(1)}, bf16[96,1024]{1,0:T(8,128)(2,1)S(1)}, u32[]{:S(2)}, u32[]{:S(2)}) collective-permute-start(bf16[96,1024]{1,0:T(8,128)(2,1)S(1)} %get-tuple-element.200), channel_id=1, source_target_pairs={{0,4},{4,8},{8,12},{12,14},{14,10},{10,6},{6,2},{2,0},{1,5},{5,9},... | collective-permute-start | bytes 589832 | tf_op jit(solution)/shard_map/ppermute | solution.py:55
  184.1 7.6 %collective-permute-start.35 = (bf16[96,1024]{1,0:T(8,128)(2,1)S(1)}, bf16[96,1024]{1,0:T(8,128)(2,1)S(1)}, u32[]{:S(2)}, u32[]{:S(2)}) collective-permute-start(bf16[96,1024]{1,0:T(8,128)(2,1)S(1)} %get-tuple-element.199), channel_id=1, source_target_pairs={{0,2},{4,0},{8,4},{12,8},{14,12},{10,14},{6,10},{2,6},{1,3},{5,1},... | collective-permute-start | bytes 589832 | tf_op jit(solution)/shard_map/ppermute | solution.py:55
  186.3 7.6 %collective-permute-start.40 = (bf16[96,1024]{1,0:T(8,128)(2,1)S(1)}, bf16[96,1024]{1,0:T(8,128)(2,1)S(1)}, u32[]{:S(2)}, u32[]{:S(2)}) collective-permute-start(bf16[96,1024]{1,0:T(8,128)(2,1)S(1)} %get-tuple-element.198), channel_id=1, source_target_pairs={{0,4},{4,8},{8,12},{12,14},{14,10},{10,6},{6,2},{2,0},{1,5},{5,9},... | collective-permute-start | bytes 589832 | tf_op jit(solution)/shard_map/ppermute | solution.py:55
  188.3 5.7 %collective-permute-start.41 = (bf16[96,1024]{1,0:T(8,128)(2,1)S(1)}, bf16[96,1024]{1,0:T(8,128)(2,1)S(1)}, u32[]{:S(2)}, u32[]{:S(2)}) collective-permute-start(bf16[96,1024]{1,0:T(8,128)(2,1)S(1)} %get-tuple-element.197), channel_id=1, source_target_pairs={{0,2},{4,0},{8,4},{12,8},{14,12},{10,14},{6,10},{2,6},{1,3},{5,1},... | collective-permute-start | bytes 589832 | tf_op jit(solution)/shard_map/ppermute | solution.py:55
  191.8 5.7 %collective-permute-start.38 = (bf16[96,1024]{1,0:T(8,128)(2,1)S(1)}, bf16[96,1024]{1,0:T(8,128)(2,1)S(1)}, u32[]{:S(2)}, u32[]{:S(2)}) collective-permute-start(bf16[96,1024]{1,0:T(8,128)(2,1)S(1)} %get-tuple-element.195), channel_id=1, source_target_pairs={{0,4},{4,8},{8,12},{12,14},{14,10},{10,6},{6,2},{2,0},{1,5},{5,9},... | collective-permute-start | bytes 589832 | tf_op jit(solution)/shard_map/ppermute | solution.py:55
  192.4 5.7 %collective-permute-start.39 = (bf16[96,1024]{1,0:T(8,128)(2,1)S(1)}, bf16[96,1024]{1,0:T(8,128)(2,1)S(1)}, u32[]{:S(2)}, u32[]{:S(2)}) collective-permute-start(bf16[96,1024]{1,0:T(8,128)(2,1)S(1)} %get-tuple-element.196), channel_id=1, source_target_pairs={{0,2},{4,0},{8,4},{12,8},{14,12},{10,14},{6,10},{2,6},{1,3},{5,1},... | collective-permute-start | bytes 589832 | tf_op jit(solution)/shard_map/ppermute | solution.py:55
  194.1 5.7 %collective-permute-start.42 = (bf16[96,1024]{1,0:T(8,128)(2,1)S(1)}, bf16[96,1024]{1,0:T(8,128)(2,1)S(1)}, u32[]{:S(2)}, u32[]{:S(2)}) collective-permute-start(bf16[96,1024]{1,0:T(8,128)(2,1)S(1)} %get-tuple-element.193), channel_id=1, source_target_pairs={{0,4},{4,8},{8,12},{12,14},{14,10},{10,6},{6,2},{2,0},{1,5},{5,9},... | collective-permute-start | bytes 589832 | tf_op jit(solution)/shard_map/ppermute | solution.py:55
  195.5 5.7 %collective-permute-start.43 = (bf16[96,1024]{1,0:T(8,128)(2,1)S(1)}, bf16[96,1024]{1,0:T(8,128)(2,1)S(1)}, u32[]{:S(2)}, u32[]{:S(2)}) collective-permute-start(bf16[96,1024]{1,0:T(8,128)(2,1)S(1)} %get-tuple-element.194), channel_id=1, source_target_pairs={{0,2},{4,0},{8,4},{12,8},{14,12},{10,14},{6,10},{2,6},{1,3},{5,1},... | collective-permute-start | bytes 589832 | tf_op jit(solution)/shard_map/ppermute | solution.py:55
  198.3 2.8 %copy-start.6 = (bf16[512,1024]{1,0:T(8,128)(2,1)}, bf16[512,1024]{1,0:T(8,128)(2,1)S(1)}, u32[]{:S(2)}) copy-start(bf16[512,1024]{1,0:T(8,128)(2,1)S(1)} %fusion.36) | copy-start | bytes 3145732

commit v15 on v14

--- a/solution.py
+++ b/solution.py
@@ -9,7 +9,7 @@
 from jax.sharding import PartitionSpec as P
 
 VMEM_LIMIT = 49 * 1024 * 1024
-DEEP, PARTS = 3, 4
+DEEP, DEEPER, PARTS = 3, 4, 4
 LANES = 128
 
 
@@ -223,7 +223,7 @@
     height = width // 2
 
     def fetch(number):
-        slot = lax.rem(number, DEEP)
+        slot = lax.rem(number, DEEPER)
         begin = pl.multiple_of(blocks_ref[1, number] * width, width)
         for other in range(2):
 
@@ -249,16 +249,16 @@
     @pl.when(step == 0)
     def first():
         gather_pieces(0, lambda copy: copy.start())
-        for number in range(min(DEEP - 1, count)):
+        for number in range(min(DEEPER - 1, count)):
             fetch(jnp.int32(number))
         for wanted in range(1, count):
             gather_pieces(wanted, lambda copy: copy.start())
         sums[...] = jnp.zeros_like(sums)
         stat[...] = before_ref[...]
 
-    @pl.when(step + DEEP - 1 < count)
+    @pl.when(step + DEEPER - 1 < count)
     def ahead():
-        fetch(step + DEEP - 1)
+        fetch(step + DEEPER - 1)
 
     for wanted in range(count):
 
@@ -266,7 +266,7 @@
         def arrived(wanted=wanted):
             gather_pieces(wanted, lambda copy: copy.wait())
 
-    slot = lax.rem(step, DEEP)
+    slot = lax.rem(step, DEEPER)
     block = stacked[:, pl.ds(pl.multiple_of(step * width, width), width)]
     if fresh:
         gain = gains_ref[blocks_ref[2, step]]
@@ -313,9 +313,9 @@
             scratch_shapes=[
                 pltpu.VMEM((rows, count * width), jnp.bfloat16),
                 pltpu.VMEM((2, rows, columns), jnp.float32),
-                pltpu.VMEM((DEEP, 2, width, columns), jnp.bfloat16),
+                pltpu.VMEM((DEEPER, 2, width, columns), jnp.bfloat16),
                 pltpu.SemaphoreType.DMA((len(pieces),)),
-                pltpu.SemaphoreType.DMA((DEEP, 2)),
+                pltpu.SemaphoreType.DMA((DEEPER, 2)),
             ],
         ),
         compiler_params=pltpu.CompilerParams(vmem_limit_bytes=VMEM_LIMIT),
@@ -335,7 +335,7 @@
     depth, width = buffer.shape[1:]
 
     def fetch(number):
-        slot = lax.rem(number, DEEP)
+        slot = lax.rem(number, DEEPER)
         for kind, source in ((1, local_ref), (0, other_ref)):
 
             @pl.when(tiles_ref[0, number + start] == kind)
@@ -349,18 +349,18 @@
 
     @pl.when(step == 0)
     def first():
-        for number in range(min(DEEP - 1, steps)):
+        for number in range(min(DEEPER - 1, steps)):
             fetch(jnp.int32(number))
         column = 0
         for part_ref in refs[:-6]:
             hidden[:, column : column + part_ref.shape[1]] = part_ref[...]
             column += part_ref.shape[1]
 
-    @pl.when(step + DEEP - 1 < steps)
+    @pl.when(step + DEEPER - 1 < steps)
     def ahead():
-        fetch(step + DEEP - 1)
-
-    slot = lax.rem(step, DEEP)
+        fetch(step + DEEPER - 1)
+
+    slot = lax.rem(step, DEEPER)
     pltpu.make_async_copy(local_ref.at[:, pl.ds(0, width)], buffer.at[slot], sems.at[slot]).wait()
     weight = buffer[slot]
     out_ref[0] = jnp.dot(hidden[...], weight, preferred_element_type=jnp.float32).astype(jnp.bfloat16)
@@ -380,8 +380,8 @@
             out_specs=pl.BlockSpec((1, rows, width), lambda j, tiles: (j, 0, 0)),
             scratch_shapes=[
                 pltpu.VMEM((rows, depth), jnp.bfloat16),
-                pltpu.VMEM((DEEP, depth, width), jnp.bfloat16),
-                pltpu.SemaphoreType.DMA((DEEP,)),
+                pltpu.VMEM((DEEPER, depth, width), jnp.bfloat16),
+                pltpu.SemaphoreType.DMA((DEEPER,)),
             ],
         ),
         compiler_params=pltpu.CompilerParams(vmem_limit_bytes=VMEM_LIMIT),

time: 202 us -> 202 us (level)
  transfers between devices with their start and end apart: 44 -> 44, of which waited for: 19 -> 20; matrix products, arithmetic and copies ran while one was open for 4% -> 4% of each run, Pallas kernels for 49% -> 49%
where the time goes in v15:
time: 202 us
  Pallas kernels  99.9 us (49%)
  waiting for transfers between devices  45.5 us (23%)
  starting transfers between devices  44.9 us (22%)
  other arithmetic  8.5 us (4%)
    ppermute x40, waiting for transfers between devices, ring_shift(): lax.ppermute(value, 'blk', [(ring[i], ring[(i + steps) % count]) for i in...  45.5 us
    pallas_call x3, Pallas kernels, gate_up(): pl.pallas_call(functools.partial(gate_up_kernel, fixed), out_shape=(jax.S...  42.9 us
    ppermute x40, starting transfers between devices, ring_shift(): lax.ppermute(value, 'blk', [(ring[i], ring[(i + steps) % count]) for i in...  41.9 us
    pallas_call x3, Pallas kernels, down(): pl.pallas_call(functools.partial(down_kernel, start, stop - start), out_s...  30.6 us
    pallas_call x2, Pallas kernels, gate_up_columns(): pl.pallas_call(functools.partial(columns_kernel, start, width * count, no...  26.5 us
  transfers between devices with their start and end apart: 44, of which 20 were waited for; matrix products, arithmetic and copies ran while one was open for 4% of the time, Pallas kernels for 49%

profile of v15, /device:TPU:0, one launch (start us, length us, event | category | flops | bytes accessed | tf_op | source)
XLA Modules:
  0.0 202.0 jit_solution(16730371494727760168)
XLA Ops:
  0.0 0.8 multiply_add_fusion.2
  0.8 2.4 %collective-permute-start.6 = (f32[3,1024]{1,0:T(4,128)S(1)}, f32[3,1024]{1,0:T(4,128)S(1)}, u32[]{:S(2)}, u32[]{:S(2)}) collective-permute-start(f32[3,1024]{1,0:T(4,128)S(1)} %multiply_add_fusion.2), channel_id=1, source_target_pairs={{0,1},{2,3},{4,5},{6,7},{8,9},{10,11},{12,13},{14,15},{16,17},{18,... | collective-permute-start | bytes 36872 | tf_op jit(solution)/shard_map/ppermute | solution.py:453
  3.1 1.7 multiply_add_fusion
  5.5 0.9 constant_dynamic-slice_fusion.2
  6.4 0.6 multiply_convert_fusion.refs_0_
  7.7 2.4 %collective-permute-start = (bf16[320,1024]{1,0:T(8,128)(2,1)S(1)}, bf16[320,1024]{1,0:T(8,128)(2,1)S(1)}, u32[]{:S(2)}, u32[]{:S(2)}) collective-permute-start(bf16[320,1024]{1,0:T(8,128)(2,1)S(1)} %multiply_convert_fusion.refs_0_), channel_id=1, source_target_pairs={{0,4},{4,8},{8,12},{12,14},{14,10},{10,6},{6,2},{2,0},{1,5},{5,9},... | collective-permute-start | bytes 1966088 | tf_op jit(solution)/shard_map/ppermute | solution.py:55
  10.1 15.3 %collective-permute-done.refs_1_ = bf16[320,1024]{1,0:T(8,128)(2,1)S(1)} collective-permute-done((bf16[320,1024]{1,0:T(8,128)(2,1)S(1)}, bf16[320,1024]{1,0:T(8,128)(2,1)S(1)}, u32[]{:S(2)}, u32[]{:S(2)}) %collective-permute-start) | collective-permute-done | bytes 655392 | tf_op jit(solution)/shard_map/ppermute | solution.py:55
  25.4 1.5 collective-permute-done.1.refs_2_
  26.9 1.6 collective-permute-start.2
  28.9 0.7 dynamic-slice_bitcast_fusion
  29.6 1.3 multiply_add_fusion.1
  31.3 11.6 %collective-permute-done.2.refs_3_ = bf16[320,1024]{1,0:T(8,128)(2,1)S(1)} collective-permute-done((bf16[320,1024]{1,0:T(8,128)(2,1)S(1)}, bf16[320,1024]{1,0:T(8,128)(2,1)S(1)}, u32[]{:S(2)}, u32[]{:S(2)}) %collective-permute-start.2) | collective-permute-done | bytes 655392 | tf_op jit(solution)/shard_map/ppermute | solution.py:55
  42.9 1.3 collective-permute-done.3.refs_4_
  44.2 1.6 collective-permute-start.4
  46.2 13.6 %gate_up.5 = (f32[320,2048]{1,0:T(8,128)}, f32[320,128]{1,0:T(8,128)S(1)}) custom-call(s32[3,8]{1,0:T(4,128)S(1)} %get-tuple-element.223.blocks_ref, s32[5,5]{1,0:T(8,128)S(1)} %copy-done.3, bf16[320,1024]{1,0:T(8,128)(2,1)S(1)} %multiply_convert_fusion.refs_0_, bf16[320,1024]{1,0:T(8,128)(2,1)S(1)} %collective-permute-done.refs_1_, ...), custom_call_target="tpu_custom_call" | custom-call | flops 13421772800 | bytes 20971520 | tf_op jit(solution)/shard_map/gate_up/pallas_call | solution.py:181
  60.2 1.5 collective-permute-start.10
  62.3 1.6 collective-permute-start.8
  63.9 0.6 collective-permute-start.9
  64.5 16.5 %gate_up.6 = (f32[320,2048]{1,0:T(8,128)}, f32[320,128]{1,0:T(8,128)S(1)}) custom-call(s32[3,8]{1,0:T(4,128)S(1)} %get-tuple-element.223.blocks_ref, s32[5,7]{1,0:T(8,128)S(1)} %copy-done.2, bf16[320,1024]{1,0:T(8,128)(2,1)S(1)} %multiply_convert_fusion.refs_0_, bf16[320,1024]{1,0:T(8,128)(2,1)S(1)} %collective-permute-done.refs_1_, ...), custom_call_target="tpu_custom_call" | custom-call | flops 18790481920 | bytes 29360128 | tf_op jit(solution)/shard_map/gate_up/pallas_call | solution.py:181
  81.1 1.6 collective-permute-start.13
  83.1 12.8 %gate_up.7 = (bf16[320,2048]{1,0:T(8,128)(2,1)S(1)}, f32[320,128]{1,0:T(8,128)}) custom-call(s32[3,8]{1,0:T(4,128)S(1)} %get-tuple-element.223.blocks_ref, s32[5,4]{1,0:T(8,128)S(1)} %copy-done.1, bf16[320,1024]{1,0:T(8,128)(2,1)S(1)} %collective-permute-done.4.refs_5_.refs_0_, bf16[320,1024]{1,0:T(8,128)(2,1)S(1)} %collective-permute-done.5.refs_6_.refs_1_, ...), custom_call_target="tpu_custom_call" | custom-call | flops 10737418240 | bytes 16777216 | tf_op jit(solution)/shard_map/gate_up/pallas_call | solution.py:181
  95.9 1.6 collective-permute-start.16
  98.0 7.4 %down.3 = bf16[3,320,1024]{2,1,0:T(8,128)(2,1)S(1)} custom-call(s32[3,8]{1,0:T(4,128)S(1)} %get-tuple-element.224.tiles_ref, bf16[320,2048]{1,0:T(8,128)(2,1)S(1)} %get-tuple-element.139.refs_0_, bf16[2048,4096]{1,0:T(8,128)(2,1)} %refs_2_.1, bf16[2048,4096]{1,0:T(8,128)(2,1)} %collective-permute-done.15.refs_2_.refs_3_), custom_call_target="tpu_custom_call" | custom-call | flops 8053063680 | bytes 12582912 | tf_op jit(solution)/shard_map/down/pallas_call | solution.py:373
  105.9 1.3 collective-permute-start.26
  107.2 0.8 collective-permute-start.27
  108.0 1.2 collective-permute-start.18
  109.3 0.8 collective-permute-start.19
  110.1 10.6 %down.4 = bf16[5,320,1024]{2,1,0:T(8,128)(2,1)S(1)} custom-call(s32[3,8]{1,0:T(4,128)S(1)} %get-tuple-element.224.tiles_ref, bf16[320,2048]{1,0:T(8,128)(2,1)S(1)} %get-tuple-element.139.refs_0_, bf16[2048,4096]{1,0:T(8,128)(2,1)} %refs_2_.1, bf16[2048,4096]{1,0:T(8,128)(2,1)} %collective-permute-done.15.refs_2_.refs_3_), custom_call_target="tpu_custom_call" | custom-call | flops 13421772800 | bytes 20971520 | tf_op jit(solution)/shard_map/down/pallas_call | solution.py:373
  121.0 0.6 collective-permute-start.21
  121.6 1.5 collective-permute-start.20
  123.2 13.2 %gate_up.8 = (bf16[192,1024]{1,0:T(8,128)(2,1)S(1)}, f32[192,128]{1,0:T(8,128)S(1)}) custom-call(s32[3,8]{1,0:T(4,128)S(1)} %get-tuple-element.223.blocks_ref, bf16[192,1024]{1,0:T(8,128)(2,1)S(1)} %multiply_convert_fusion.1.refs_0_, bf16[192,1024]{1,0:T(8,128)(2,1)S(1)} %collective-permute-done.10.refs_1_, ...), custom_call_target="tpu_custom_call" | custom-call | flops 12884901888 | bytes 33554432 | tf_op jit(solution)/shard_map/gate_up/pallas_call | solution.py:302
  136.4 0.6 fusion.5
  137.0 1.3 collective-permute-start.22
  138.3 0.8 collective-permute-start.23
  139.1 13.3 %gate_up.9 = (bf16[192,1024]{1,0:T(8,128)(2,1)S(1)}, f32[192,128]{1,0:T(8,128)}) custom-call(s32[3,8]{1,0:T(4,128)S(1)} %get-tuple-element.223.blocks_ref, bf16[192,1024]{1,0:T(8,128)(2,1)S(1)} %multiply_convert_fusion.1.refs_0_, bf16[192,1024]{1,0:T(8,128)(2,1)S(1)} %collective-permute-done.10.refs_1_, ...), custom_call_target="tpu_custom_call" | custom-call | flops 12884901888 | bytes 33554432 | tf_op jit(solution)/shard_map/gate_up/pallas_call | solution.py:302
  152.4 0.6 fusion.7
  152.9 1.3 collective-permute-start.24
  154.3 0.7 collective-permute-start.25
  155.0 12.5 %down.5 = bf16[8,192,1024]{2,1,0:T(8,128)(2,1)S(1)} custom-call(s32[3,8]{1,0:T(4,128)S(1)} %get-tuple-element.224.tiles_ref, bf16[192,1024]{1,0:T(8,128)(2,1)S(1)} %get-tuple-element.171.refs_0_, bf16[192,1024]{1,0:T(8,128)(2,1)S(1)} %get-tuple-element.172.refs_1_, bf16[2048,4096]{1,0:T(8,128)(2,1)} %refs_2_.1, ...), custom_call_target="tpu_custom_call" | custom-call | flops 12884901888 | bytes 33554432 | tf_op jit(solution)/shard_map/down/pallas_call | solution.py:373
  167.7 1.3 collective-permute-start.28
  169.0 0.7 collective-permute-start.29
  169.7 1.3 collective-permute-start.32
  171.0 0.7 collective-permute-start.33
  171.8 0.7 fusion.10
  172.6 0.9 collective-permute-done.28
  174.5 1.6 collective-permute-start.30
  176.5 1.1 collective-permute-start.37
  177.6 1.0 collective-permute-start.36
  178.6 1.7 collective-permute-done.31
  180.3 1.9 collective-permute-done.30
  182.4 1.7 collective-permute-start.34
  184.5 1.6 collective-permute-done.36
  186.3 2.0 collective-permute-start.40
  188.4 1.6 collective-permute-done.34
  190.0 1.7 collective-permute-done.35
  191.8 0.6 collective-permute-start.38
  192.4 1.5 collective-permute-start.39
  194.1 1.4 collective-permute-start.42
  195.5 0.7 collective-permute-start.43
  196.2 1.4 collective-permute-done.38
  197.6 0.6 collective-permute-done.39
  198.3 1.6 collective-permute-done.42
  199.8 1.3 collective-permute-done.43
  201.2 0.8 fusion.37
  (83 shorter events, 7.6 us)
Async XLA Ops:
  0.8 6.3 %collective-permute-start.6 = (f32[3,1024]{1,0:T(4,128)S(1)}, f32[3,1024]{1,0:T(4,128)S(1)}, u32[]{:S(2)}, u32[]{:S(2)}) collective-permute-start(f32[3,1024]{1,0:T(4,128)S(1)} %multiply_add_fusion.2), channel_id=1, source_target_pairs={{0,1},{2,3},{4,5},{6,7},{8,9},{10,11},{12,13},{14,15},{16,17},{18,... | collective-permute-start | bytes 36872 | tf_op jit(solution)/shard_map/ppermute | solution.py:453
  3.1 2.3 %copy-start = (f32[8192]{0:T(1024)S(1)}, f32[8192]{0:T(1024)}, u32[]{:S(2)}) copy-start(f32[8192]{0:T(1024)} %param.18) | copy-start | bytes 98308
  6.4 23.2 %copy-start.7 = (f32[1024]{0:T(1024)S(1)}, f32[1024]{0:T(1024)}, u32[]{:S(2)}) copy-start(f32[1024]{0:T(1024)} %param.15) | copy-start | bytes 12292
  7.0 39.2 %collective-permute-start.7 = (bf16[4096,2048]{1,0:T(8,128)(2,1)}, bf16[4096,2048]{1,0:T(8,128)(2,1)}, u32[]{:S(2)}, u32[]{:S(2)}) collective-permute-start(bf16[4096,2048]{1,0:T(8,128)(2,1)} %refs_10_.5), channel_id=1, source_target_pairs={{0,1},{1,0},{2,3},{3,2},{4,5},{5,4},{6,7},{7,6},{8,9},{9,8},{10,11... | collective-permute-start | bytes 50331656 | tf_op jit(solution)/shard_map/ppermute | solution.py:59
  7.1 56.8 %collective-permute-start.12 = (bf16[4096,2048]{1,0:T(8,128)(2,1)}, bf16[4096,2048]{1,0:T(8,128)(2,1)}, u32[]{:S(2)}, u32[]{:S(2)}) collective-permute-start(bf16[4096,2048]{1,0:T(8,128)(2,1)} %refs_12_.3), channel_id=1, source_target_pairs={{0,1},{1,0},{2,3},{3,2},{4,5},{5,4},{6,7},{7,6},{8,9},{9,8},{10,11... | collective-permute-start | bytes 50331656 | tf_op jit(solution)/shard_map/ppermute | solution.py:59
  7.6 90.4 %collective-permute-start.15 = (bf16[2048,4096]{1,0:T(8,128)(2,1)}, bf16[2048,4096]{1,0:T(8,128)(2,1)}, u32[]{:S(2)}, u32[]{:S(2)}) collective-permute-start(bf16[2048,4096]{1,0:T(8,128)(2,1)} %refs_2_.1), channel_id=1, source_target_pairs={{0,1},{1,0},{2,3},{3,2},{4,5},{5,4},{6,7},{7,6},{8,9},{9,8},{10,11... | collective-permute-start | bytes 50331656 | tf_op jit(solution)/shard_map/ppermute | solution.py:59
  7.7 17.7 %collective-permute-start = (bf16[320,1024]{1,0:T(8,128)(2,1)S(1)}, bf16[320,1024]{1,0:T(8,128)(2,1)S(1)}, u32[]{:S(2)}, u32[]{:S(2)}) collective-permute-start(bf16[320,1024]{1,0:T(8,128)(2,1)S(1)} %multiply_convert_fusion.refs_0_), channel_id=1, source_target_pairs={{0,4},{4,8},{8,12},{12,14},{14,10},{10,6},{6,2},{2,0},{1,5},{5,9},... | collective-permute-start | bytes 1966088 | tf_op jit(solution)/shard_map/ppermute | solution.py:55
  10.1 16.8 %collective-permute-start.1 = (bf16[320,1024]{1,0:T(8,128)(2,1)S(1)}, bf16[320,1024]{1,0:T(8,128)(2,1)S(1)}, u32[]{:S(2)}, u32[]{:S(2)}) collective-permute-start(bf16[320,1024]{1,0:T(8,128)(2,1)S(1)} %multiply_convert_fusion.refs_0_), channel_id=1, source_target_pairs={{0,2},{4,0},{8,4},{12,8},{14,12},{10,14},{6,10},{2,6},{1,3},{5,1},... | collective-permute-start | bytes 1966088 | tf_op jit(solution)/shard_map/ppermute | solution.py:55
  26.9 16.0 %collective-permute-start.2 = (bf16[320,1024]{1,0:T(8,128)(2,1)S(1)}, bf16[320,1024]{1,0:T(8,128)(2,1)S(1)}, u32[]{:S(2)}, u32[]{:S(2)}) collective-permute-start(bf16[320,1024]{1,0:T(8,128)(2,1)S(1)} %collective-permute-done.refs_1_), channel_id=1, source_target_pairs={{0,4},{4,8},{8,12},{12,14},{14,10},{10,6},{6,2},{2,0},{1,5},{5,9},... | collective-permute-start | bytes 1966088 | tf_op jit(solution)/shard_map/ppermute | solution.py:55
  28.5 15.7 %collective-permute-start.3 = (bf16[320,1024]{1,0:T(8,128)(2,1)S(1)}, bf16[320,1024]{1,0:T(8,128)(2,1)S(1)}, u32[]{:S(2)}, u32[]{:S(2)}) collective-permute-start(bf16[320,1024]{1,0:T(8,128)(2,1)S(1)} %collective-permute-done.1.refs_2_), channel_id=1, source_target_pairs={{0,2},{4,0},{8,4},{12,8},{14,12},{10,14},{6,10},{2,6},{1,3},{5,1},... | collective-permute-start | bytes 1966088 | tf_op jit(solution)/shard_map/ppermute | solution.py:55
  29.6 16.6 %copy-start.3 = (s32[5,5]{1,0:T(8,128)S(1)}, s32[5,5]{1,0:T(8,128)}, u32[]{:S(2)}) copy-start(s32[5,5]{1,0:T(8,128)} %constant.40.clone.units_ref) | copy-start | bytes 304
  44.2 15.6 %collective-permute-start.4 = (bf16[320,1024]{1,0:T(8,128)(2,1)S(1)}, bf16[320,1024]{1,0:T(8,128)(2,1)S(1)}, u32[]{:S(2)}, u32[]{:S(2)}) collective-permute-start(bf16[320,1024]{1,0:T(8,128)(2,1)S(1)} %collective-permute-done.2.refs_3_), channel_id=1, source_target_pairs={{0,4},{4,8},{8,12},{12,14},{14,10},{10,6},{6,2},{2,0},{1,5},{5,9},... | collective-permute-start | bytes 1966088 | tf_op jit(solution)/shard_map/ppermute | solution.py:55
  45.8 14.5 %collective-permute-start.5 = (bf16[320,1024]{1,0:T(8,128)(2,1)S(1)}, bf16[320,1024]{1,0:T(8,128)(2,1)S(1)}, u32[]{:S(2)}, u32[]{:S(2)}) collective-permute-start(bf16[320,1024]{1,0:T(8,128)(2,1)S(1)} %collective-permute-done.3.refs_4_), channel_id=1, source_target_pairs={{0,2},{4,0},{8,4},{12,8},{14,12},{10,14},{6,10},{2,6},{1,3},{5,1},... | collective-permute-start | bytes 1966088 | tf_op jit(solution)/shard_map/ppermute | solution.py:55
  59.8 4.7 %copy-start.2 = (s32[5,7]{1,0:T(8,128)S(1)}, s32[5,7]{1,0:T(8,128)}, u32[]{:S(2)}) copy-start(s32[5,7]{1,0:T(8,128)} %constant.41.clone.units_ref) | copy-start | bytes 424
  60.2 20.8 %collective-permute-start.10 = (bf16[192,1024]{1,0:T(8,128)(2,1)S(1)}, bf16[192,1024]{1,0:T(8,128)(2,1)S(1)}, u32[]{:S(2)}, u32[]{:S(2)}) collective-permute-start(bf16[192,1024]{1,0:T(8,128)(2,1)S(1)} %multiply_convert_fusion.1.refs_0_), channel_id=1, source_target_pairs={{0,4},{4,8},{8,12},{12,14},{14,10},{10,6},{6,2},{2,0},{1,5},{5,9},... | collective-permute-start | bytes 1179656 | tf_op jit(solution)/shard_map/ppermute | solution.py:55
  61.8 19.3 %collective-permute-start.11 = (bf16[192,1024]{1,0:T(8,128)(2,1)S(1)}, bf16[192,1024]{1,0:T(8,128)(2,1)S(1)}, u32[]{:S(2)}, u32[]{:S(2)}) collective-permute-start(bf16[192,1024]{1,0:T(8,128)(2,1)S(1)} %multiply_convert_fusion.1.refs_0_), channel_id=1, source_target_pairs={{0,2},{4,0},{8,4},{12,8},{14,12},{10,14},{6,10},{2,6},{1,3},{5,1},... | collective-permute-start | bytes 1179656 | tf_op jit(solution)/shard_map/ppermute | solution.py:55
  62.3 18.7 %collective-permute-start.8 = (bf16[160,1024]{1,0:T(8,128)(2,1)S(1)}, bf16[160,1024]{1,0:T(8,128)(2,1)S(1)}, u32[]{:S(2)}, u32[]{:S(2)}) collective-permute-start(bf16[160,1024]{1,0:T(8,128)(2,1)S(1)} %slice.326), channel_id=1, source_target_pairs={{0,4},{4,8},{8,12},{12,14},{14,10},{10,6},{6,2},{2,0},{1,5},{5,9},... | collective-permute-start | bytes 983048 | tf_op jit(solution)/shard_map/ppermute | solution.py:55
  63.9 17.1 %collective-permute-start.9 = (bf16[160,1024]{1,0:T(8,128)(2,1)S(1)}, bf16[160,1024]{1,0:T(8,128)(2,1)S(1)}, u32[]{:S(2)}, u32[]{:S(2)}) collective-permute-start(bf16[160,1024]{1,0:T(8,128)(2,1)S(1)} %slice.327), channel_id=1, source_target_pairs={{0,2},{4,0},{8,4},{12,8},{14,12},{10,14},{6,10},{2,6},{1,3},{5,1},... | collective-permute-start | bytes 983048 | tf_op jit(solution)/shard_map/ppermute | solution.py:55
  64.5 18.7 %copy-start.1 = (s32[5,4]{1,0:T(8,128)S(1)}, s32[5,4]{1,0:T(8,128)}, u32[]{:S(2)}) copy-start(s32[5,4]{1,0:T(8,128)} %constant.42.clone.units_ref) | copy-start | bytes 244
  81.1 14.8 %collective-permute-start.13 = (bf16[192,1024]{1,0:T(8,128)(2,1)S(1)}, bf16[192,1024]{1,0:T(8,128)(2,1)S(1)}, u32[]{:S(2)}, u32[]{:S(2)}) collective-permute-start(bf16[192,1024]{1,0:T(8,128)(2,1)S(1)} %collective-permute-done.10.refs_1_), channel_id=1, source_target_pairs={{0,4},{4,8},{8,12},{12,14},{14,10},{10,6},{6,2},{2,0},{1,5},{5,9},... | collective-permute-start | bytes 1179656 | tf_op jit(solution)/shard_map/ppermute | solution.py:55
  82.6 13.3 %collective-permute-start.14 = (bf16[192,1024]{1,0:T(8,128)(2,1)S(1)}, bf16[192,1024]{1,0:T(8,128)(2,1)S(1)}, u32[]{:S(2)}, u32[]{:S(2)}) collective-permute-start(bf16[192,1024]{1,0:T(8,128)(2,1)S(1)} %collective-permute-done.11.refs_2_), channel_id=1, source_target_pairs={{0,2},{4,0},{8,4},{12,8},{14,12},{10,14},{6,10},{2,6},{1,3},{5,1},... | collective-permute-start | bytes 1179656 | tf_op jit(solution)/shard_map/ppermute | solution.py:55
  95.9 9.6 %collective-permute-start.16 = (bf16[192,1024]{1,0:T(8,128)(2,1)S(1)}, bf16[192,1024]{1,0:T(8,128)(2,1)S(1)}, u32[]{:S(2)}, u32[]{:S(2)}) collective-permute-start(bf16[192,1024]{1,0:T(8,128)(2,1)S(1)} %collective-permute-done.13.refs_3_), channel_id=1, source_target_pairs={{0,4},{4,8},{8,12},{12,14},{14,10},{10,6},{6,2},{2,0},{1,5},{5,9},... | collective-permute-start | bytes 1179656 | tf_op jit(solution)/shard_map/ppermute | solution.py:55
  97.5 8.4 %collective-permute-start.17 = (bf16[192,1024]{1,0:T(8,128)(2,1)S(1)}, bf16[192,1024]{1,0:T(8,128)(2,1)S(1)}, u32[]{:S(2)}, u32[]{:S(2)}) collective-permute-start(bf16[192,1024]{1,0:T(8,128)(2,1)S(1)} %collective-permute-done.14.refs_4_), channel_id=1, source_target_pairs={{0,2},{4,0},{8,4},{12,8},{14,12},{10,14},{6,10},{2,6},{1,3},{5,1},... | collective-permute-start | bytes 1179656 | tf_op jit(solution)/shard_map/ppermute | solution.py:55
  105.9 17.2 %collective-permute-start.26 = (bf16[96,1024]{1,0:T(8,128)(2,1)S(1)}, bf16[96,1024]{1,0:T(8,128)(2,1)S(1)}, u32[]{:S(2)}, u32[]{:S(2)}) collective-permute-start(bf16[96,1024]{1,0:T(8,128)(2,1)S(1)} %slice.350), channel_id=1, source_target_pairs={{0,4},{4,8},{8,12},{12,14},{14,10},{10,6},{6,2},{2,0},{1,5},{5,9},... | collective-permute-start | bytes 589832 | tf_op jit(solution)/shard_map/ppermute | solution.py:55
  107.2 16.0 %collective-permute-start.27 = (bf16[96,1024]{1,0:T(8,128)(2,1)S(1)}, bf16[96,1024]{1,0:T(8,128)(2,1)S(1)}, u32[]{:S(2)}, u32[]{:S(2)}) collective-permute-start(bf16[96,1024]{1,0:T(8,128)(2,1)S(1)} %slice.351), channel_id=1, source_target_pairs={{0,2},{4,0},{8,4},{12,8},{14,12},{10,14},{6,10},{2,6},{1,3},{5,1},... | collective-permute-start | bytes 589832 | tf_op jit(solution)/shard_map/ppermute | solution.py:55
  108.0 12.6 %collective-permute-start.18 = (bf16[160,1024]{1,0:T(8,128)(2,1)S(1)}, bf16[160,1024]{1,0:T(8,128)(2,1)S(1)}, u32[]{:S(2)}, u32[]{:S(2)}) collective-permute-start(bf16[160,1024]{1,0:T(8,128)(2,1)S(1)} %get-tuple-element.140), channel_id=1, source_target_pairs={{0,4},{4,8},{8,12},{12,14},{14,10},{10,6},{6,2},{2,0},{1,5},{5,9},... | collective-permute-start | bytes 983048 | tf_op jit(solution)/shard_map/ppermute | solution.py:55
  109.3 11.4 %collective-permute-start.19 = (bf16[160,1024]{1,0:T(8,128)(2,1)S(1)}, bf16[160,1024]{1,0:T(8,128)(2,1)S(1)}, u32[]{:S(2)}, u32[]{:S(2)}) collective-permute-start(bf16[160,1024]{1,0:T(8,128)(2,1)S(1)} %get-tuple-element.141), channel_id=1, source_target_pairs={{0,2},{4,0},{8,4},{12,8},{14,12},{10,14},{6,10},{2,6},{1,3},{5,1},... | collective-permute-start | bytes 983048 | tf_op jit(solution)/shard_map/ppermute | solution.py:55
  121.0 15.4 %collective-permute-start.21 = (bf16[320,1024]{1,0:T(8,128)(2,1)S(1)}, bf16[320,1024]{1,0:T(8,128)(2,1)S(1)}, u32[]{:S(2)}, u32[]{:S(2)}) collective-permute-start(bf16[320,1024]{1,0:T(8,128)(2,1)S(1)} %pad_maximum_fusion.2), channel_id=1, source_target_pairs={{0,2},{4,0},{8,4},{12,8},{14,12},{10,14},{6,10},{2,6},{1,3},{5,1},... | collective-permute-start | bytes 1966088 | tf_op jit(solution)/shard_map/ppermute | solution.py:55
  121.6 14.8 %collective-permute-start.20 = (bf16[320,1024]{1,0:T(8,128)(2,1)S(1)}, bf16[320,1024]{1,0:T(8,128)(2,1)S(1)}, u32[]{:S(2)}, u32[]{:S(2)}) collective-permute-start(bf16[320,1024]{1,0:T(8,128)(2,1)S(1)} %pad_maximum_fusion.1), channel_id=1, source_target_pairs={{0,4},{4,8},{8,12},{12,14},{14,10},{10,6},{6,2},{2,0},{1,5},{5,9},... | collective-permute-start | bytes 1966088 | tf_op jit(solution)/shard_map/ppermute | solution.py:55
  137.0 15.4 %collective-permute-start.22 = (bf16[320,1024]{1,0:T(8,128)(2,1)S(1)}, bf16[320,1024]{1,0:T(8,128)(2,1)S(1)}, u32[]{:S(2)}, u32[]{:S(2)}) collective-permute-start(bf16[320,1024]{1,0:T(8,128)(2,1)S(1)} %get-tuple-element.192), channel_id=1, source_target_pairs={{0,4},{4,8},{8,12},{12,14},{14,10},{10,6},{6,2},{2,0},{1,5},{5,9},... | collective-permute-start | bytes 1966088 | tf_op jit(solution)/shard_map/ppermute | solution.py:55
  138.3 14.1 %collective-permute-start.23 = (bf16[320,1024]{1,0:T(8,128)(2,1)S(1)}, bf16[320,1024]{1,0:T(8,128)(2,1)S(1)}, u32[]{:S(2)}, u32[]{:S(2)}) collective-permute-start(bf16[320,1024]{1,0:T(8,128)(2,1)S(1)} %get-tuple-element.191), channel_id=1, source_target_pairs={{0,2},{4,0},{8,4},{12,8},{14,12},{10,14},{6,10},{2,6},{1,3},{5,1},... | collective-permute-start | bytes 1966088 | tf_op jit(solution)/shard_map/ppermute | solution.py:55
  152.9 14.7 %collective-permute-start.24 = (bf16[320,1024]{1,0:T(8,128)(2,1)S(1)}, bf16[320,1024]{1,0:T(8,128)(2,1)S(1)}, u32[]{:S(2)}, u32[]{:S(2)}) collective-permute-start(bf16[320,1024]{1,0:T(8,128)(2,1)S(1)} %get-tuple-element.189), channel_id=1, source_target_pairs={{0,4},{4,8},{8,12},{12,14},{14,10},{10,6},{6,2},{2,0},{1,5},{5,9},... | collective-permute-start | bytes 1966088 | tf_op jit(solution)/shard_map/ppermute | solution.py:55
  154.3 13.4 %collective-permute-start.25 = (bf16[320,1024]{1,0:T(8,128)(2,1)S(1)}, bf16[320,1024]{1,0:T(8,128)(2,1)S(1)}, u32[]{:S(2)}, u32[]{:S(2)}) collective-permute-start(bf16[320,1024]{1,0:T(8,128)(2,1)S(1)} %get-tuple-element.190), channel_id=1, source_target_pairs={{0,2},{4,0},{8,4},{12,8},{14,12},{10,14},{6,10},{2,6},{1,3},{5,1},... | collective-permute-start | bytes 1966088 | tf_op jit(solution)/shard_map/ppermute | solution.py:55
  155.0 16.8 %copy-start.5 = (bf16[512,1024]{1,0:T(8,128)(2,1)S(1)}, bf16[512,1024]{1,0:T(8,128)(2,1)}, u32[]{:S(2)}) copy-start(bf16[512,1024]{1,0:T(8,128)(2,1)} %param.13) | copy-start | bytes 3145732
  167.6 4.2 %copy-start.4 = (bf16[512,1024]{1,0:T(8,128)(2,1)S(1)}, bf16[512,1024]{1,0:T(8,128)(2,1)}, u32[]{:S(2)}) copy-start(bf16[512,1024]{1,0:T(8,128)(2,1)} %param.14) | copy-start | bytes 3145732
  167.7 5.8 %collective-permute-start.28 = (bf16[48,1024]{1,0:T(8,128)(2,1)S(1)}, bf16[48,1024]{1,0:T(8,128)(2,1)S(1)}, u32[]{:S(2)}, u32[]{:S(2)}) collective-permute-start(bf16[48,1024]{1,0:T(8,128)(2,1)S(1)} %get-tuple-element.173), channel_id=1, source_target_pairs={{0,4},{4,8},{8,12},{12,14},{14,10},{10,6},{6,2},{2,0},{1,5},{5,9},... | collective-permute-start | bytes 294920 | tf_op jit(solution)/shard_map/ppermute | solution.py:55
  169.0 4.9 %collective-permute-start.29 = (bf16[48,1024]{1,0:T(8,128)(2,1)S(1)}, bf16[48,1024]{1,0:T(8,128)(2,1)S(1)}, u32[]{:S(2)}, u32[]{:S(2)}) collective-permute-start(bf16[48,1024]{1,0:T(8,128)(2,1)S(1)} %get-tuple-element.174), channel_id=1, source_target_pairs={{0,2},{4,0},{8,4},{12,8},{14,12},{10,14},{6,10},{2,6},{1,3},{5,1},... | collective-permute-start | bytes 294920 | tf_op jit(solution)/shard_map/ppermute | solution.py:55
  169.7 6.4 %collective-permute-start.32 = (bf16[48,1024]{1,0:T(8,128)(2,1)S(1)}, bf16[48,1024]{1,0:T(8,128)(2,1)S(1)}, u32[]{:S(2)}, u32[]{:S(2)}) collective-permute-start(bf16[48,1024]{1,0:T(8,128)(2,1)S(1)} %get-tuple-element.175), channel_id=1, source_target_pairs={{0,4},{4,8},{8,12},{12,14},{14,10},{10,6},{6,2},{2,0},{1,5},{5,9},... | collective-permute-start | bytes 294920 | tf_op jit(solution)/shard_map/ppermute | solution.py:55
  171.0 5.4 %collective-permute-start.33 = (bf16[48,1024]{1,0:T(8,128)(2,1)S(1)}, bf16[48,1024]{1,0:T(8,128)(2,1)S(1)}, u32[]{:S(2)}, u32[]{:S(2)}) collective-permute-start(bf16[48,1024]{1,0:T(8,128)(2,1)S(1)} %get-tuple-element.176), channel_id=1, source_target_pairs={{0,2},{4,0},{8,4},{12,8},{14,12},{10,14},{6,10},{2,6},{1,3},{5,1},... | collective-permute-start | bytes 294920 | tf_op jit(solution)/shard_map/ppermute | solution.py:55
  174.0 6.3 %collective-permute-start.31 = (bf16[96,1024]{1,0:T(8,128)(2,1)S(1)}, bf16[96,1024]{1,0:T(8,128)(2,1)S(1)}, u32[]{:S(2)}, u32[]{:S(2)}) collective-permute-start(bf16[96,1024]{1,0:T(8,128)(2,1)S(1)} %pad_maximum_fusion.4), channel_id=1, source_target_pairs={{0,2},{4,0},{8,4},{12,8},{14,12},{10,14},{6,10},{2,6},{1,3},{5,1},... | collective-permute-start | bytes 589832 | tf_op jit(solution)/shard_map/ppermute | solution.py:55
  174.5 7.7 %collective-permute-start.30 = (bf16[96,1024]{1,0:T(8,128)(2,1)S(1)}, bf16[96,1024]{1,0:T(8,128)(2,1)S(1)}, u32[]{:S(2)}, u32[]{:S(2)}) collective-permute-start(bf16[96,1024]{1,0:T(8,128)(2,1)S(1)} %pad_maximum_fusion.3), channel_id=1, source_target_pairs={{0,4},{4,8},{8,12},{12,14},{14,10},{10,6},{6,2},{2,0},{1,5},{5,9},... | collective-permute-start | bytes 589832 | tf_op jit(solution)/shard_map/ppermute | solution.py:55
  176.5 8.1 %collective-permute-start.37 = (bf16[96,1024]{1,0:T(8,128)(2,1)S(1)}, bf16[96,1024]{1,0:T(8,128)(2,1)S(1)}, u32[]{:S(2)}, u32[]{:S(2)}) collective-permute-start(bf16[96,1024]{1,0:T(8,128)(2,1)S(1)} %pad_maximum_fusion.6), channel_id=1, source_target_pairs={{0,2},{4,0},{8,4},{12,8},{14,12},{10,14},{6,10},{2,6},{1,3},{5,1},... | collective-permute-start | bytes 589832 | tf_op jit(solution)/shard_map/ppermute | solution.py:55
  177.6 8.6 %collective-permute-start.36 = (bf16[96,1024]{1,0:T(8,128)(2,1)S(1)}, bf16[96,1024]{1,0:T(8,128)(2,1)S(1)}, u32[]{:S(2)}, u32[]{:S(2)}) collective-permute-start(bf16[96,1024]{1,0:T(8,128)(2,1)S(1)} %pad_maximum_fusion.5), channel_id=1, source_target_pairs={{0,4},{4,8},{8,12},{12,14},{14,10},{10,6},{6,2},{2,0},{1,5},{5,9},... | collective-permute-start | bytes 589832 | tf_op jit(solution)/shard_map/ppermute | solution.py:55
  182.4 7.6 %collective-permute-start.34 = (bf16[96,1024]{1,0:T(8,128)(2,1)S(1)}, bf16[96,1024]{1,0:T(8,128)(2,1)S(1)}, u32[]{:S(2)}, u32[]{:S(2)}) collective-permute-start(bf16[96,1024]{1,0:T(8,128)(2,1)S(1)} %get-tuple-element.200), channel_id=1, source_target_pairs={{0,4},{4,8},{8,12},{12,14},{14,10},{10,6},{6,2},{2,0},{1,5},{5,9},... | collective-permute-start | bytes 589832 | tf_op jit(solution)/shard_map/ppermute | solution.py:55
  184.1 7.6 %collective-permute-start.35 = (bf16[96,1024]{1,0:T(8,128)(2,1)S(1)}, bf16[96,1024]{1,0:T(8,128)(2,1)S(1)}, u32[]{:S(2)}, u32[]{:S(2)}) collective-permute-start(bf16[96,1024]{1,0:T(8,128)(2,1)S(1)} %get-tuple-element.199), channel_id=1, source_target_pairs={{0,2},{4,0},{8,4},{12,8},{14,12},{10,14},{6,10},{2,6},{1,3},{5,1},... | collective-permute-start | bytes 589832 | tf_op jit(solution)/shard_map/ppermute | solution.py:55
  186.3 7.6 %collective-permute-start.40 = (bf16[96,1024]{1,0:T(8,128)(2,1)S(1)}, bf16[96,1024]{1,0:T(8,128)(2,1)S(1)}, u32[]{:S(2)}, u32[]{:S(2)}) collective-permute-start(bf16[96,1024]{1,0:T(8,128)(2,1)S(1)} %get-tuple-element.198), channel_id=1, source_target_pairs={{0,4},{4,8},{8,12},{12,14},{14,10},{10,6},{6,2},{2,0},{1,5},{5,9},... | collective-permute-start | bytes 589832 | tf_op jit(solution)/shard_map/ppermute | solution.py:55
  188.3 5.7 %collective-permute-start.41 = (bf16[96,1024]{1,0:T(8,128)(2,1)S(1)}, bf16[96,1024]{1,0:T(8,128)(2,1)S(1)}, u32[]{:S(2)}, u32[]{:S(2)}) collective-permute-start(bf16[96,1024]{1,0:T(8,128)(2,1)S(1)} %get-tuple-element.197), channel_id=1, source_target_pairs={{0,2},{4,0},{8,4},{12,8},{14,12},{10,14},{6,10},{2,6},{1,3},{5,1},... | collective-permute-start | bytes 589832 | tf_op jit(solution)/shard_map/ppermute | solution.py:55
  191.8 5.7 %collective-permute-start.38 = (bf16[96,1024]{1,0:T(8,128)(2,1)S(1)}, bf16[96,1024]{1,0:T(8,128)(2,1)S(1)}, u32[]{:S(2)}, u32[]{:S(2)}) collective-permute-start(bf16[96,1024]{1,0:T(8,128)(2,1)S(1)} %get-tuple-element.195), channel_id=1, source_target_pairs={{0,4},{4,8},{8,12},{12,14},{14,10},{10,6},{6,2},{2,0},{1,5},{5,9},... | collective-permute-start | bytes 589832 | tf_op jit(solution)/shard_map/ppermute | solution.py:55
  192.4 5.7 %collective-permute-start.39 = (bf16[96,1024]{1,0:T(8,128)(2,1)S(1)}, bf16[96,1024]{1,0:T(8,128)(2,1)S(1)}, u32[]{:S(2)}, u32[]{:S(2)}) collective-permute-start(bf16[96,1024]{1,0:T(8,128)(2,1)S(1)} %get-tuple-element.196), channel_id=1, source_target_pairs={{0,2},{4,0},{8,4},{12,8},{14,12},{10,14},{6,10},{2,6},{1,3},{5,1},... | collective-permute-start | bytes 589832 | tf_op jit(solution)/shard_map/ppermute | solution.py:55
  194.1 5.7 %collective-permute-start.42 = (bf16[96,1024]{1,0:T(8,128)(2,1)S(1)}, bf16[96,1024]{1,0:T(8,128)(2,1)S(1)}, u32[]{:S(2)}, u32[]{:S(2)}) collective-permute-start(bf16[96,1024]{1,0:T(8,128)(2,1)S(1)} %get-tuple-element.193), channel_id=1, source_target_pairs={{0,4},{4,8},{8,12},{12,14},{14,10},{10,6},{6,2},{2,0},{1,5},{5,9},... | collective-permute-start | bytes 589832 | tf_op jit(solution)/shard_map/ppermute | solution.py:55
  195.5 5.7 %collective-permute-start.43 = (bf16[96,1024]{1,0:T(8,128)(2,1)S(1)}, bf16[96,1024]{1,0:T(8,128)(2,1)S(1)}, u32[]{:S(2)}, u32[]{:S(2)}) collective-permute-start(bf16[96,1024]{1,0:T(8,128)(2,1)S(1)} %get-tuple-element.194), channel_id=1, source_target_pairs={{0,2},{4,0},{8,4},{12,8},{14,12},{10,14},{6,10},{2,6},{1,3},{5,1},... | collective-permute-start | bytes 589832 | tf_op jit(solution)/shard_map/ppermute | solution.py:55
  198.3 2.9 %copy-start.6 = (bf16[512,1024]{1,0:T(8,128)(2,1)}, bf16[512,1024]{1,0:T(8,128)(2,1)S(1)}, u32[]{:S(2)}) copy-start(bf16[512,1024]{1,0:T(8,128)(2,1)S(1)} %fusion.36) | copy-start | bytes 3145732

commit v16 on v15

--- a/solution.py
+++ b/solution.py
@@ -9,7 +9,7 @@
 from jax.sharding import PartitionSpec as P
 
 VMEM_LIMIT = 49 * 1024 * 1024
-DEEP, DEEPER, PARTS = 3, 4, 4
+DEEP, DEEPER, PARTS = 4, 4, 4
 LANES = 128
 
 
@@ -113,7 +113,8 @@
         for place in range(1, len(pieces)):
             gather_pieces(place, lambda copy: copy.start())
         partials(lambda copy: copy.start())
-        sums[...] = jnp.zeros_like(sums)
+        total = sums if final else out_ref
+        total[...] = jnp.zeros_like(total)
         stat_ref[...] = before_ref[...]
 
     @pl.when(step + DEEP - 1 < length)
@@ -142,19 +143,21 @@
     slot = lax.rem(step, DEEP)
     pltpu.make_async_copy(own_and_other[0][0].at[pl.ds(0, width)], weights.at[slot], weight_sems.at[slot]).wait()
     which = units_ref[0, step]
-    place_of_sum = which if final else 0
-    sums[place_of_sum] += jnp.dot(block, weights[slot], preferred_element_type=jnp.float32)
-
-    @pl.when(step == length - 1)
-    def finish():
-        if final:
+    term = jnp.dot(block, weights[slot], preferred_element_type=jnp.float32)
+    if final:
+        sums[which] += term
+    else:
+        out_ref[...] += term
+
+    if final:
+
+        @pl.when(step == length - 1)
+        def finish():
             partials(lambda copy: copy.wait())
             inv = lax.rsqrt(jnp.sum(stat_ref[...], axis=1, keepdims=True) / mean_of + 1e-05)
             gate, up = (sums[kind] + partial[kind] if kind in taken else sums[kind] for kind in range(2))
             gate = gate * inv
             out_ref[...] = (gate / (1.0 + jnp.exp(-gate)) * (up * inv)).astype(jnp.bfloat16)
-        else:
-            out_ref[...] = sums[0]
 
 
 def gate_up(units, final, partial, squares, blocks, pieces, gains, weights):
@@ -177,7 +180,7 @@
     needed = [len(pieces[block]) for block in used]
     fixed = (needed, final, taken, width * count, len(units))
     whole = lambda *shape: pl.BlockSpec(shape, lambda n, blocks, units: (0,) * len(shape))
-    sums_shape = (2 if final else 1, rows, columns)
+    sums_shape = (2, rows, columns) if final else (1, 8, columns)
     out, squares = pl.pallas_call(
         functools.partial(gate_up_kernel, fixed),
         out_shape=(

time: 202 us -> 202 us (level)
  transfers between devices with their start and end apart: 44 -> 44, of which waited for: 20 -> 19; matrix products, arithmetic and copies ran while one was open for 4% -> 4% of each run, Pallas kernels for 49% -> 49%
where the time goes in v16:
time: 202 us; the launch traced here: 201 us
  Pallas kernels  99 us (49%)
  waiting for transfers between devices  45.4 us (22%)
  starting transfers between devices  45.1 us (22%)
  other arithmetic  8.5 us (4%)
    ppermute x40, waiting for transfers between devices, ring_shift(): lax.ppermute(value, 'blk', [(ring[i], ring[(i + steps) % count]) for i in...  45.4 us
    ppermute x40, starting transfers between devices, ring_shift(): lax.ppermute(value, 'blk', [(ring[i], ring[(i + steps) % count]) for i in...  42.1 us
    pallas_call x3, Pallas kernels, gate_up(): pl.pallas_call(functools.partial(gate_up_kernel, fixed), out_shape=(jax.S...  42 us
    pallas_call x3, Pallas kernels, down(): pl.pallas_call(functools.partial(down_kernel, start, stop - start), out_s...  30.5 us
    pallas_call x2, Pallas kernels, gate_up_columns(): pl.pallas_call(functools.partial(columns_kernel, start, width * count, no...  26.5 us
  transfers between devices with their start and end apart: 44, of which 19 were waited for; matrix products, arithmetic and copies ran while one was open for 4% of the time, Pallas kernels for 49%

profile of v16, /device:TPU:0, one launch (start us, length us, event | category | flops | bytes accessed | tf_op | source)
XLA Modules:
  0.0 201.2 jit_solution(2874170662936367269)
XLA Ops:
  0.0 0.8 multiply_add_fusion.2
  0.8 2.4 %collective-permute-start.6 = (f32[3,1024]{1,0:T(4,128)S(1)}, f32[3,1024]{1,0:T(4,128)S(1)}, u32[]{:S(2)}, u32[]{:S(2)}) collective-permute-start(f32[3,1024]{1,0:T(4,128)S(1)} %multiply_add_fusion.2), channel_id=1, source_target_pairs={{0,1},{2,3},{4,5},{6,7},{8,9},{10,11},{12,13},{14,15},{16,17},{18,... | collective-permute-start | bytes 36872 | tf_op jit(solution)/shard_map/ppermute | solution.py:456
  3.1 1.7 multiply_add_fusion
  5.5 0.9 constant_dynamic-slice_fusion.2
  6.4 0.6 multiply_convert_fusion.refs_0_
  7.7 2.4 %collective-permute-start = (bf16[320,1024]{1,0:T(8,128)(2,1)S(1)}, bf16[320,1024]{1,0:T(8,128)(2,1)S(1)}, u32[]{:S(2)}, u32[]{:S(2)}) collective-permute-start(bf16[320,1024]{1,0:T(8,128)(2,1)S(1)} %multiply_convert_fusion.refs_0_), channel_id=1, source_target_pairs={{0,4},{4,8},{8,12},{12,14},{14,10},{10,6},{6,2},{2,0},{1,5},{5,9},... | collective-permute-start | bytes 1966088 | tf_op jit(solution)/shard_map/ppermute | solution.py:55
  10.1 15.3 %collective-permute-done.refs_1_ = bf16[320,1024]{1,0:T(8,128)(2,1)S(1)} collective-permute-done((bf16[320,1024]{1,0:T(8,128)(2,1)S(1)}, bf16[320,1024]{1,0:T(8,128)(2,1)S(1)}, u32[]{:S(2)}, u32[]{:S(2)}) %collective-permute-start) | collective-permute-done | bytes 655392 | tf_op jit(solution)/shard_map/ppermute | solution.py:55
  25.4 1.5 collective-permute-done.1.refs_2_
  26.9 1.6 collective-permute-start.2
  28.9 0.7 dynamic-slice_bitcast_fusion
  29.6 1.3 multiply_add_fusion.1
  31.3 11.6 %collective-permute-done.2.refs_3_ = bf16[320,1024]{1,0:T(8,128)(2,1)S(1)} collective-permute-done((bf16[320,1024]{1,0:T(8,128)(2,1)S(1)}, bf16[320,1024]{1,0:T(8,128)(2,1)S(1)}, u32[]{:S(2)}, u32[]{:S(2)}) %collective-permute-start.2) | collective-permute-done | bytes 655392 | tf_op jit(solution)/shard_map/ppermute | solution.py:55
  42.9 1.3 collective-permute-done.3.refs_4_
  44.2 1.6 collective-permute-start.4
  46.2 13.3 %gate_up.5 = (f32[320,2048]{1,0:T(8,128)}, f32[320,128]{1,0:T(8,128)S(1)}) custom-call(s32[3,8]{1,0:T(4,128)S(1)} %get-tuple-element.223.blocks_ref, s32[5,5]{1,0:T(8,128)S(1)} %copy-done.3, bf16[320,1024]{1,0:T(8,128)(2,1)S(1)} %multiply_convert_fusion.refs_0_, bf16[320,1024]{1,0:T(8,128)(2,1)S(1)} %collective-permute-done.refs_1_, ...), custom_call_target="tpu_custom_call" | custom-call | flops 13421772800 | bytes 20971520 | tf_op jit(solution)/shard_map/gate_up/pallas_call | solution.py:184
  59.6 0.6 collective-permute-done.5.refs_6_.refs_1_
  60.2 1.5 collective-permute-start.10
  62.3 1.6 collective-permute-start.8
  63.9 0.6 collective-permute-start.9
  64.5 16.3 %gate_up.6 = (f32[320,2048]{1,0:T(8,128)}, f32[320,128]{1,0:T(8,128)S(1)}) custom-call(s32[3,8]{1,0:T(4,128)S(1)} %get-tuple-element.223.blocks_ref, s32[5,7]{1,0:T(8,128)S(1)} %copy-done.2, bf16[320,1024]{1,0:T(8,128)(2,1)S(1)} %multiply_convert_fusion.refs_0_, bf16[320,1024]{1,0:T(8,128)(2,1)S(1)} %collective-permute-done.refs_1_, ...), custom_call_target="tpu_custom_call" | custom-call | flops 18790481920 | bytes 29360128 | tf_op jit(solution)/shard_map/gate_up/pallas_call | solution.py:184
  80.8 1.6 collective-permute-start.13
  82.9 12.3 %gate_up.7 = (bf16[320,2048]{1,0:T(8,128)(2,1)S(1)}, f32[320,128]{1,0:T(8,128)}) custom-call(s32[3,8]{1,0:T(4,128)S(1)} %get-tuple-element.223.blocks_ref, s32[5,4]{1,0:T(8,128)S(1)} %copy-done.1, bf16[320,1024]{1,0:T(8,128)(2,1)S(1)} %collective-permute-done.4.refs_5_.refs_0_, bf16[320,1024]{1,0:T(8,128)(2,1)S(1)} %collective-permute-done.5.refs_6_.refs_1_, ...), custom_call_target="tpu_custom_call" | custom-call | flops 10737418240 | bytes 16777216 | tf_op jit(solution)/shard_map/gate_up/pallas_call | solution.py:184
  95.3 1.6 collective-permute-start.16
  97.3 7.4 %down.3 = bf16[3,320,1024]{2,1,0:T(8,128)(2,1)S(1)} custom-call(s32[3,8]{1,0:T(4,128)S(1)} %get-tuple-element.224.tiles_ref, bf16[320,2048]{1,0:T(8,128)(2,1)S(1)} %get-tuple-element.139.refs_0_, bf16[2048,4096]{1,0:T(8,128)(2,1)} %refs_2_.1, bf16[2048,4096]{1,0:T(8,128)(2,1)} %collective-permute-done.15.refs_2_.refs_3_), custom_call_target="tpu_custom_call" | custom-call | flops 8053063680 | bytes 12582912 | tf_op jit(solution)/shard_map/down/pallas_call | solution.py:376
  105.4 1.1 collective-permute-start.26
  106.5 1.1 collective-permute-start.27
  107.6 1.0 collective-permute-start.18
  108.6 1.0 collective-permute-start.19
  109.6 10.6 %down.4 = bf16[5,320,1024]{2,1,0:T(8,128)(2,1)S(1)} custom-call(s32[3,8]{1,0:T(4,128)S(1)} %get-tuple-element.224.tiles_ref, bf16[320,2048]{1,0:T(8,128)(2,1)S(1)} %get-tuple-element.139.refs_0_, bf16[2048,4096]{1,0:T(8,128)(2,1)} %refs_2_.1, bf16[2048,4096]{1,0:T(8,128)(2,1)} %collective-permute-done.15.refs_2_.refs_3_), custom_call_target="tpu_custom_call" | custom-call | flops 13421772800 | bytes 20971520 | tf_op jit(solution)/shard_map/down/pallas_call | solution.py:376
  120.5 0.6 collective-permute-start.21
  121.2 1.5 collective-permute-start.20
  122.7 13.2 %gate_up.8 = (bf16[192,1024]{1,0:T(8,128)(2,1)S(1)}, f32[192,128]{1,0:T(8,128)S(1)}) custom-call(s32[3,8]{1,0:T(4,128)S(1)} %get-tuple-element.223.blocks_ref, bf16[192,1024]{1,0:T(8,128)(2,1)S(1)} %multiply_convert_fusion.1.refs_0_, bf16[192,1024]{1,0:T(8,128)(2,1)S(1)} %collective-permute-done.10.refs_1_, ...), custom_call_target="tpu_custom_call" | custom-call | flops 12884901888 | bytes 33554432 | tf_op jit(solution)/shard_map/gate_up/pallas_call | solution.py:305
  136.5 1.1 collective-permute-start.22
  137.6 1.0 collective-permute-start.23
  138.6 13.3 %gate_up.9 = (bf16[192,1024]{1,0:T(8,128)(2,1)S(1)}, f32[192,128]{1,0:T(8,128)}) custom-call(s32[3,8]{1,0:T(4,128)S(1)} %get-tuple-element.223.blocks_ref, bf16[192,1024]{1,0:T(8,128)(2,1)S(1)} %multiply_convert_fusion.1.refs_0_, bf16[192,1024]{1,0:T(8,128)(2,1)S(1)} %collective-permute-done.10.refs_1_, ...), custom_call_target="tpu_custom_call" | custom-call | flops 12884901888 | bytes 33554432 | tf_op jit(solution)/shard_map/gate_up/pallas_call | solution.py:305
  152.5 1.1 collective-permute-start.24
  153.6 0.9 collective-permute-start.25
  154.6 12.5 %down.5 = bf16[8,192,1024]{2,1,0:T(8,128)(2,1)S(1)} custom-call(s32[3,8]{1,0:T(4,128)S(1)} %get-tuple-element.224.tiles_ref, bf16[192,1024]{1,0:T(8,128)(2,1)S(1)} %get-tuple-element.171.refs_0_, bf16[192,1024]{1,0:T(8,128)(2,1)S(1)} %get-tuple-element.172.refs_1_, bf16[2048,4096]{1,0:T(8,128)(2,1)} %refs_2_.1, ...), custom_call_target="tpu_custom_call" | custom-call | flops 12884901888 | bytes 33554432 | tf_op jit(solution)/shard_map/down/pallas_call | solution.py:376
  167.2 1.1 collective-permute-start.28
  168.3 0.9 collective-permute-start.29
  169.3 1.1 collective-permute-start.32
  170.4 0.9 collective-permute-start.33
  171.3 0.7 fusion.10
  172.1 0.9 collective-permute-done.28
  173.1 0.9 collective-permute-start.31
  174.0 1.2 collective-permute-start.30
  175.3 0.7 collective-permute-done.33
  176.0 1.0 collective-permute-start.37
  177.0 1.1 collective-permute-start.36
  178.2 1.9 collective-permute-done.31
  180.1 0.9 collective-permute-done.30
  181.1 2.2 %collective-permute-start.34 = (bf16[96,1024]{1,0:T(8,128)(2,1)S(1)}, bf16[96,1024]{1,0:T(8,128)(2,1)S(1)}, u32[]{:S(2)}, u32[]{:S(2)}) collective-permute-start(bf16[96,1024]{1,0:T(8,128)(2,1)S(1)} %get-tuple-element.200), channel_id=1, source_target_pairs={{0,4},{4,8},{8,12},{12,14},{14,10},{10,6},{6,2},{2,0},{1,5},{5,9},... | collective-permute-start | bytes 589832 | tf_op jit(solution)/shard_map/ppermute | solution.py:55
  183.2 1.0 collective-permute-done.37
  184.3 0.6 collective-permute-done.36
  185.0 2.2 %collective-permute-start.40 = (bf16[96,1024]{1,0:T(8,128)(2,1)S(1)}, bf16[96,1024]{1,0:T(8,128)(2,1)S(1)}, u32[]{:S(2)}, u32[]{:S(2)}) collective-permute-start(bf16[96,1024]{1,0:T(8,128)(2,1)S(1)} %get-tuple-element.198), channel_id=1, source_target_pairs={{0,4},{4,8},{8,12},{12,14},{14,10},{10,6},{6,2},{2,0},{1,5},{5,9},... | collective-permute-start | bytes 589832 | tf_op jit(solution)/shard_map/ppermute | solution.py:55
  187.2 1.5 collective-permute-done.34
  188.7 2.2 %collective-permute-done.35 = bf16[96,1024]{1,0:T(8,128)(2,1)S(1)} collective-permute-done((bf16[96,1024]{1,0:T(8,128)(2,1)S(1)}, bf16[96,1024]{1,0:T(8,128)(2,1)S(1)}, u32[]{:S(2)}, u32[]{:S(2)}) %collective-permute-start.35) | collective-permute-done | bytes 196640 | tf_op jit(solution)/shard_map/ppermute | solution.py:55
  191.4 1.7 collective-permute-start.39
  193.2 1.4 collective-permute-start.42
  194.6 0.7 collective-permute-start.43
  195.3 1.4 collective-permute-done.38
  197.3 1.7 collective-permute-done.42
  199.0 1.3 collective-permute-done.43
  200.3 0.8 fusion.37
  (83 shorter events, 7.5 us)
Async XLA Ops:
  0.8 6.3 %collective-permute-start.6 = (f32[3,1024]{1,0:T(4,128)S(1)}, f32[3,1024]{1,0:T(4,128)S(1)}, u32[]{:S(2)}, u32[]{:S(2)}) collective-permute-start(f32[3,1024]{1,0:T(4,128)S(1)} %multiply_add_fusion.2), channel_id=1, source_target_pairs={{0,1},{2,3},{4,5},{6,7},{8,9},{10,11},{12,13},{14,15},{16,17},{18,... | collective-permute-start | bytes 36872 | tf_op jit(solution)/shard_map/ppermute | solution.py:456
  3.1 2.3 %copy-start = (f32[8192]{0:T(1024)S(1)}, f32[8192]{0:T(1024)}, u32[]{:S(2)}) copy-start(f32[8192]{0:T(1024)} %param.18) | copy-start | bytes 98308
  6.4 23.2 %copy-start.7 = (f32[1024]{0:T(1024)S(1)}, f32[1024]{0:T(1024)}, u32[]{:S(2)}) copy-start(f32[1024]{0:T(1024)} %param.15) | copy-start | bytes 12292
  7.0 39.2 %collective-permute-start.7 = (bf16[4096,2048]{1,0:T(8,128)(2,1)}, bf16[4096,2048]{1,0:T(8,128)(2,1)}, u32[]{:S(2)}, u32[]{:S(2)}) collective-permute-start(bf16[4096,2048]{1,0:T(8,128)(2,1)} %refs_10_.5), channel_id=1, source_target_pairs={{0,1},{1,0},{2,3},{3,2},{4,5},{5,4},{6,7},{7,6},{8,9},{9,8},{10,11... | collective-permute-start | bytes 50331656 | tf_op jit(solution)/shard_map/ppermute | solution.py:59
  7.1 56.8 %collective-permute-start.12 = (bf16[4096,2048]{1,0:T(8,128)(2,1)}, bf16[4096,2048]{1,0:T(8,128)(2,1)}, u32[]{:S(2)}, u32[]{:S(2)}) collective-permute-start(bf16[4096,2048]{1,0:T(8,128)(2,1)} %refs_12_.3), channel_id=1, source_target_pairs={{0,1},{1,0},{2,3},{3,2},{4,5},{5,4},{6,7},{7,6},{8,9},{9,8},{10,11... | collective-permute-start | bytes 50331656 | tf_op jit(solution)/shard_map/ppermute | solution.py:59
  7.6 89.7 %collective-permute-start.15 = (bf16[2048,4096]{1,0:T(8,128)(2,1)}, bf16[2048,4096]{1,0:T(8,128)(2,1)}, u32[]{:S(2)}, u32[]{:S(2)}) collective-permute-start(bf16[2048,4096]{1,0:T(8,128)(2,1)} %refs_2_.1), channel_id=1, source_target_pairs={{0,1},{1,0},{2,3},{3,2},{4,5},{5,4},{6,7},{7,6},{8,9},{9,8},{10,11... | collective-permute-start | bytes 50331656 | tf_op jit(solution)/shard_map/ppermute | solution.py:59
  7.7 17.7 %collective-permute-start = (bf16[320,1024]{1,0:T(8,128)(2,1)S(1)}, bf16[320,1024]{1,0:T(8,128)(2,1)S(1)}, u32[]{:S(2)}, u32[]{:S(2)}) collective-permute-start(bf16[320,1024]{1,0:T(8,128)(2,1)S(1)} %multiply_convert_fusion.refs_0_), channel_id=1, source_target_pairs={{0,4},{4,8},{8,12},{12,14},{14,10},{10,6},{6,2},{2,0},{1,5},{5,9},... | collective-permute-start | bytes 1966088 | tf_op jit(solution)/shard_map/ppermute | solution.py:55
  10.1 16.8 %collective-permute-start.1 = (bf16[320,1024]{1,0:T(8,128)(2,1)S(1)}, bf16[320,1024]{1,0:T(8,128)(2,1)S(1)}, u32[]{:S(2)}, u32[]{:S(2)}) collective-permute-start(bf16[320,1024]{1,0:T(8,128)(2,1)S(1)} %multiply_convert_fusion.refs_0_), channel_id=1, source_target_pairs={{0,2},{4,0},{8,4},{12,8},{14,12},{10,14},{6,10},{2,6},{1,3},{5,1},... | collective-permute-start | bytes 1966088 | tf_op jit(solution)/shard_map/ppermute | solution.py:55
  26.9 16.0 %collective-permute-start.2 = (bf16[320,1024]{1,0:T(8,128)(2,1)S(1)}, bf16[320,1024]{1,0:T(8,128)(2,1)S(1)}, u32[]{:S(2)}, u32[]{:S(2)}) collective-permute-start(bf16[320,1024]{1,0:T(8,128)(2,1)S(1)} %collective-permute-done.refs_1_), channel_id=1, source_target_pairs={{0,4},{4,8},{8,12},{12,14},{14,10},{10,6},{6,2},{2,0},{1,5},{5,9},... | collective-permute-start | bytes 1966088 | tf_op jit(solution)/shard_map/ppermute | solution.py:55
  28.5 15.7 %collective-permute-start.3 = (bf16[320,1024]{1,0:T(8,128)(2,1)S(1)}, bf16[320,1024]{1,0:T(8,128)(2,1)S(1)}, u32[]{:S(2)}, u32[]{:S(2)}) collective-permute-start(bf16[320,1024]{1,0:T(8,128)(2,1)S(1)} %collective-permute-done.1.refs_2_), channel_id=1, source_target_pairs={{0,2},{4,0},{8,4},{12,8},{14,12},{10,14},{6,10},{2,6},{1,3},{5,1},... | collective-permute-start | bytes 1966088 | tf_op jit(solution)/shard_map/ppermute | solution.py:55
  29.6 16.6 %copy-start.3 = (s32[5,5]{1,0:T(8,128)S(1)}, s32[5,5]{1,0:T(8,128)}, u32[]{:S(2)}) copy-start(s32[5,5]{1,0:T(8,128)} %constant.40.clone.units_ref) | copy-start | bytes 304
  44.2 15.4 %collective-permute-start.4 = (bf16[320,1024]{1,0:T(8,128)(2,1)S(1)}, bf16[320,1024]{1,0:T(8,128)(2,1)S(1)}, u32[]{:S(2)}, u32[]{:S(2)}) collective-permute-start(bf16[320,1024]{1,0:T(8,128)(2,1)S(1)} %collective-permute-done.2.refs_3_), channel_id=1, source_target_pairs={{0,4},{4,8},{8,12},{12,14},{14,10},{10,6},{6,2},{2,0},{1,5},{5,9},... | collective-permute-start | bytes 1966088 | tf_op jit(solution)/shard_map/ppermute | solution.py:55
  45.8 14.5 %collective-permute-start.5 = (bf16[320,1024]{1,0:T(8,128)(2,1)S(1)}, bf16[320,1024]{1,0:T(8,128)(2,1)S(1)}, u32[]{:S(2)}, u32[]{:S(2)}) collective-permute-start(bf16[320,1024]{1,0:T(8,128)(2,1)S(1)} %collective-permute-done.3.refs_4_), channel_id=1, source_target_pairs={{0,2},{4,0},{8,4},{12,8},{14,12},{10,14},{6,10},{2,6},{1,3},{5,1},... | collective-permute-start | bytes 1966088 | tf_op jit(solution)/shard_map/ppermute | solution.py:55
  59.6 4.9 %copy-start.2 = (s32[5,7]{1,0:T(8,128)S(1)}, s32[5,7]{1,0:T(8,128)}, u32[]{:S(2)}) copy-start(s32[5,7]{1,0:T(8,128)} %constant.41.clone.units_ref) | copy-start | bytes 424
  60.2 20.6 %collective-permute-start.10 = (bf16[192,1024]{1,0:T(8,128)(2,1)S(1)}, bf16[192,1024]{1,0:T(8,128)(2,1)S(1)}, u32[]{:S(2)}, u32[]{:S(2)}) collective-permute-start(bf16[192,1024]{1,0:T(8,128)(2,1)S(1)} %multiply_convert_fusion.1.refs_0_), channel_id=1, source_target_pairs={{0,4},{4,8},{8,12},{12,14},{14,10},{10,6},{6,2},{2,0},{1,5},{5,9},... | collective-permute-start | bytes 1179656 | tf_op jit(solution)/shard_map/ppermute | solution.py:55
  61.8 19.0 %collective-permute-start.11 = (bf16[192,1024]{1,0:T(8,128)(2,1)S(1)}, bf16[192,1024]{1,0:T(8,128)(2,1)S(1)}, u32[]{:S(2)}, u32[]{:S(2)}) collective-permute-start(bf16[192,1024]{1,0:T(8,128)(2,1)S(1)} %multiply_convert_fusion.1.refs_0_), channel_id=1, source_target_pairs={{0,2},{4,0},{8,4},{12,8},{14,12},{10,14},{6,10},{2,6},{1,3},{5,1},... | collective-permute-start | bytes 1179656 | tf_op jit(solution)/shard_map/ppermute | solution.py:55
  62.3 18.5 %collective-permute-start.8 = (bf16[160,1024]{1,0:T(8,128)(2,1)S(1)}, bf16[160,1024]{1,0:T(8,128)(2,1)S(1)}, u32[]{:S(2)}, u32[]{:S(2)}) collective-permute-start(bf16[160,1024]{1,0:T(8,128)(2,1)S(1)} %slice.326), channel_id=1, source_target_pairs={{0,4},{4,8},{8,12},{12,14},{14,10},{10,6},{6,2},{2,0},{1,5},{5,9},... | collective-permute-start | bytes 983048 | tf_op jit(solution)/shard_map/ppermute | solution.py:55
  63.9 16.9 %collective-permute-start.9 = (bf16[160,1024]{1,0:T(8,128)(2,1)S(1)}, bf16[160,1024]{1,0:T(8,128)(2,1)S(1)}, u32[]{:S(2)}, u32[]{:S(2)}) collective-permute-start(bf16[160,1024]{1,0:T(8,128)(2,1)S(1)} %slice.327), channel_id=1, source_target_pairs={{0,2},{4,0},{8,4},{12,8},{14,12},{10,14},{6,10},{2,6},{1,3},{5,1},... | collective-permute-start | bytes 983048 | tf_op jit(solution)/shard_map/ppermute | solution.py:55
  64.5 18.4 %copy-start.1 = (s32[5,4]{1,0:T(8,128)S(1)}, s32[5,4]{1,0:T(8,128)}, u32[]{:S(2)}) copy-start(s32[5,4]{1,0:T(8,128)} %constant.42.clone.units_ref) | copy-start | bytes 244
  80.8 14.4 %collective-permute-start.13 = (bf16[192,1024]{1,0:T(8,128)(2,1)S(1)}, bf16[192,1024]{1,0:T(8,128)(2,1)S(1)}, u32[]{:S(2)}, u32[]{:S(2)}) collective-permute-start(bf16[192,1024]{1,0:T(8,128)(2,1)S(1)} %collective-permute-done.10.refs_1_), channel_id=1, source_target_pairs={{0,4},{4,8},{8,12},{12,14},{14,10},{10,6},{6,2},{2,0},{1,5},{5,9},... | collective-permute-start | bytes 1179656 | tf_op jit(solution)/shard_map/ppermute | solution.py:55
  82.4 12.9 %collective-permute-start.14 = (bf16[192,1024]{1,0:T(8,128)(2,1)S(1)}, bf16[192,1024]{1,0:T(8,128)(2,1)S(1)}, u32[]{:S(2)}, u32[]{:S(2)}) collective-permute-start(bf16[192,1024]{1,0:T(8,128)(2,1)S(1)} %collective-permute-done.11.refs_2_), channel_id=1, source_target_pairs={{0,2},{4,0},{8,4},{12,8},{14,12},{10,14},{6,10},{2,6},{1,3},{5,1},... | collective-permute-start | bytes 1179656 | tf_op jit(solution)/shard_map/ppermute | solution.py:55
  95.3 9.6 %collective-permute-start.16 = (bf16[192,1024]{1,0:T(8,128)(2,1)S(1)}, bf16[192,1024]{1,0:T(8,128)(2,1)S(1)}, u32[]{:S(2)}, u32[]{:S(2)}) collective-permute-start(bf16[192,1024]{1,0:T(8,128)(2,1)S(1)} %collective-permute-done.13.refs_3_), channel_id=1, source_target_pairs={{0,4},{4,8},{8,12},{12,14},{14,10},{10,6},{6,2},{2,0},{1,5},{5,9},... | collective-permute-start | bytes 1179656 | tf_op jit(solution)/shard_map/ppermute | solution.py:55
  96.8 8.6 %collective-permute-start.17 = (bf16[192,1024]{1,0:T(8,128)(2,1)S(1)}, bf16[192,1024]{1,0:T(8,128)(2,1)S(1)}, u32[]{:S(2)}, u32[]{:S(2)}) collective-permute-start(bf16[192,1024]{1,0:T(8,128)(2,1)S(1)} %collective-permute-done.14.refs_4_), channel_id=1, source_target_pairs={{0,2},{4,0},{8,4},{12,8},{14,12},{10,14},{6,10},{2,6},{1,3},{5,1},... | collective-permute-start | bytes 1179656 | tf_op jit(solution)/shard_map/ppermute | solution.py:55
  105.4 17.2 %collective-permute-start.26 = (bf16[96,1024]{1,0:T(8,128)(2,1)S(1)}, bf16[96,1024]{1,0:T(8,128)(2,1)S(1)}, u32[]{:S(2)}, u32[]{:S(2)}) collective-permute-start(bf16[96,1024]{1,0:T(8,128)(2,1)S(1)} %slice.350), channel_id=1, source_target_pairs={{0,4},{4,8},{8,12},{12,14},{14,10},{10,6},{6,2},{2,0},{1,5},{5,9},... | collective-permute-start | bytes 589832 | tf_op jit(solution)/shard_map/ppermute | solution.py:55
  106.5 16.2 %collective-permute-start.27 = (bf16[96,1024]{1,0:T(8,128)(2,1)S(1)}, bf16[96,1024]{1,0:T(8,128)(2,1)S(1)}, u32[]{:S(2)}, u32[]{:S(2)}) collective-permute-start(bf16[96,1024]{1,0:T(8,128)(2,1)S(1)} %slice.351), channel_id=1, source_target_pairs={{0,2},{4,0},{8,4},{12,8},{14,12},{10,14},{6,10},{2,6},{1,3},{5,1},... | collective-permute-start | bytes 589832 | tf_op jit(solution)/shard_map/ppermute | solution.py:55
  107.6 12.6 %collective-permute-start.18 = (bf16[160,1024]{1,0:T(8,128)(2,1)S(1)}, bf16[160,1024]{1,0:T(8,128)(2,1)S(1)}, u32[]{:S(2)}, u32[]{:S(2)}) collective-permute-start(bf16[160,1024]{1,0:T(8,128)(2,1)S(1)} %get-tuple-element.140), channel_id=1, source_target_pairs={{0,4},{4,8},{8,12},{12,14},{14,10},{10,6},{6,2},{2,0},{1,5},{5,9},... | collective-permute-start | bytes 983048 | tf_op jit(solution)/shard_map/ppermute | solution.py:55
  108.6 11.6 %collective-permute-start.19 = (bf16[160,1024]{1,0:T(8,128)(2,1)S(1)}, bf16[160,1024]{1,0:T(8,128)(2,1)S(1)}, u32[]{:S(2)}, u32[]{:S(2)}) collective-permute-start(bf16[160,1024]{1,0:T(8,128)(2,1)S(1)} %get-tuple-element.141), channel_id=1, source_target_pairs={{0,2},{4,0},{8,4},{12,8},{14,12},{10,14},{6,10},{2,6},{1,3},{5,1},... | collective-permute-start | bytes 983048 | tf_op jit(solution)/shard_map/ppermute | solution.py:55
  120.5 15.4 %collective-permute-start.21 = (bf16[320,1024]{1,0:T(8,128)(2,1)S(1)}, bf16[320,1024]{1,0:T(8,128)(2,1)S(1)}, u32[]{:S(2)}, u32[]{:S(2)}) collective-permute-start(bf16[320,1024]{1,0:T(8,128)(2,1)S(1)} %pad_maximum_fusion.2), channel_id=1, source_target_pairs={{0,2},{4,0},{8,4},{12,8},{14,12},{10,14},{6,10},{2,6},{1,3},{5,1},... | collective-permute-start | bytes 1966088 | tf_op jit(solution)/shard_map/ppermute | solution.py:55
  121.2 14.8 %collective-permute-start.20 = (bf16[320,1024]{1,0:T(8,128)(2,1)S(1)}, bf16[320,1024]{1,0:T(8,128)(2,1)S(1)}, u32[]{:S(2)}, u32[]{:S(2)}) collective-permute-start(bf16[320,1024]{1,0:T(8,128)(2,1)S(1)} %pad_maximum_fusion.1), channel_id=1, source_target_pairs={{0,4},{4,8},{8,12},{12,14},{14,10},{10,6},{6,2},{2,0},{1,5},{5,9},... | collective-permute-start | bytes 1966088 | tf_op jit(solution)/shard_map/ppermute | solution.py:55
  136.5 15.4 %collective-permute-start.22 = (bf16[320,1024]{1,0:T(8,128)(2,1)S(1)}, bf16[320,1024]{1,0:T(8,128)(2,1)S(1)}, u32[]{:S(2)}, u32[]{:S(2)}) collective-permute-start(bf16[320,1024]{1,0:T(8,128)(2,1)S(1)} %get-tuple-element.192), channel_id=1, source_target_pairs={{0,4},{4,8},{8,12},{12,14},{14,10},{10,6},{6,2},{2,0},{1,5},{5,9},... | collective-permute-start | bytes 1966088 | tf_op jit(solution)/shard_map/ppermute | solution.py:55
  137.6 14.3 %collective-permute-start.23 = (bf16[320,1024]{1,0:T(8,128)(2,1)S(1)}, bf16[320,1024]{1,0:T(8,128)(2,1)S(1)}, u32[]{:S(2)}, u32[]{:S(2)}) collective-permute-start(bf16[320,1024]{1,0:T(8,128)(2,1)S(1)} %get-tuple-element.191), channel_id=1, source_target_pairs={{0,2},{4,0},{8,4},{12,8},{14,12},{10,14},{6,10},{2,6},{1,3},{5,1},... | collective-permute-start | bytes 1966088 | tf_op jit(solution)/shard_map/ppermute | solution.py:55
  152.5 14.7 %collective-permute-start.24 = (bf16[320,1024]{1,0:T(8,128)(2,1)S(1)}, bf16[320,1024]{1,0:T(8,128)(2,1)S(1)}, u32[]{:S(2)}, u32[]{:S(2)}) collective-permute-start(bf16[320,1024]{1,0:T(8,128)(2,1)S(1)} %get-tuple-element.189), channel_id=1, source_target_pairs={{0,4},{4,8},{8,12},{12,14},{14,10},{10,6},{6,2},{2,0},{1,5},{5,9},... | collective-permute-start | bytes 1966088 | tf_op jit(solution)/shard_map/ppermute | solution.py:55
  153.6 13.6 %collective-permute-start.25 = (bf16[320,1024]{1,0:T(8,128)(2,1)S(1)}, bf16[320,1024]{1,0:T(8,128)(2,1)S(1)}, u32[]{:S(2)}, u32[]{:S(2)}) collective-permute-start(bf16[320,1024]{1,0:T(8,128)(2,1)S(1)} %get-tuple-element.190), channel_id=1, source_target_pairs={{0,2},{4,0},{8,4},{12,8},{14,12},{10,14},{6,10},{2,6},{1,3},{5,1},... | collective-permute-start | bytes 1966088 | tf_op jit(solution)/shard_map/ppermute | solution.py:55
  154.6 16.8 %copy-start.5 = (bf16[512,1024]{1,0:T(8,128)(2,1)S(1)}, bf16[512,1024]{1,0:T(8,128)(2,1)}, u32[]{:S(2)}) copy-start(bf16[512,1024]{1,0:T(8,128)(2,1)} %param.13) | copy-start | bytes 3145732
  167.1 4.2 %copy-start.4 = (bf16[512,1024]{1,0:T(8,128)(2,1)S(1)}, bf16[512,1024]{1,0:T(8,128)(2,1)}, u32[]{:S(2)}) copy-start(bf16[512,1024]{1,0:T(8,128)(2,1)} %param.14) | copy-start | bytes 3145732
  167.2 5.8 %collective-permute-start.28 = (bf16[48,1024]{1,0:T(8,128)(2,1)S(1)}, bf16[48,1024]{1,0:T(8,128)(2,1)S(1)}, u32[]{:S(2)}, u32[]{:S(2)}) collective-permute-start(bf16[48,1024]{1,0:T(8,128)(2,1)S(1)} %get-tuple-element.173), channel_id=1, source_target_pairs={{0,4},{4,8},{8,12},{12,14},{14,10},{10,6},{6,2},{2,0},{1,5},{5,9},... | collective-permute-start | bytes 294920 | tf_op jit(solution)/shard_map/ppermute | solution.py:55
  168.3 4.7 %collective-permute-start.29 = (bf16[48,1024]{1,0:T(8,128)(2,1)S(1)}, bf16[48,1024]{1,0:T(8,128)(2,1)S(1)}, u32[]{:S(2)}, u32[]{:S(2)}) collective-permute-start(bf16[48,1024]{1,0:T(8,128)(2,1)S(1)} %get-tuple-element.174), channel_id=1, source_target_pairs={{0,2},{4,0},{8,4},{12,8},{14,12},{10,14},{6,10},{2,6},{1,3},{5,1},... | collective-permute-start | bytes 294920 | tf_op jit(solution)/shard_map/ppermute | solution.py:55
  169.3 6.0 %collective-permute-start.32 = (bf16[48,1024]{1,0:T(8,128)(2,1)S(1)}, bf16[48,1024]{1,0:T(8,128)(2,1)S(1)}, u32[]{:S(2)}, u32[]{:S(2)}) collective-permute-start(bf16[48,1024]{1,0:T(8,128)(2,1)S(1)} %get-tuple-element.175), channel_id=1, source_target_pairs={{0,4},{4,8},{8,12},{12,14},{14,10},{10,6},{6,2},{2,0},{1,5},{5,9},... | collective-permute-start | bytes 294920 | tf_op jit(solution)/shard_map/ppermute | solution.py:55
  170.4 5.6 %collective-permute-start.33 = (bf16[48,1024]{1,0:T(8,128)(2,1)S(1)}, bf16[48,1024]{1,0:T(8,128)(2,1)S(1)}, u32[]{:S(2)}, u32[]{:S(2)}) collective-permute-start(bf16[48,1024]{1,0:T(8,128)(2,1)S(1)} %get-tuple-element.176), channel_id=1, source_target_pairs={{0,2},{4,0},{8,4},{12,8},{14,12},{10,14},{6,10},{2,6},{1,3},{5,1},... | collective-permute-start | bytes 294920 | tf_op jit(solution)/shard_map/ppermute | solution.py:55
  173.1 6.9 %collective-permute-start.31 = (bf16[96,1024]{1,0:T(8,128)(2,1)S(1)}, bf16[96,1024]{1,0:T(8,128)(2,1)S(1)}, u32[]{:S(2)}, u32[]{:S(2)}) collective-permute-start(bf16[96,1024]{1,0:T(8,128)(2,1)S(1)} %pad_maximum_fusion.4), channel_id=1, source_target_pairs={{0,2},{4,0},{8,4},{12,8},{14,12},{10,14},{6,10},{2,6},{1,3},{5,1},... | collective-permute-start | bytes 589832 | tf_op jit(solution)/shard_map/ppermute | solution.py:55
  174.0 6.9 %collective-permute-start.30 = (bf16[96,1024]{1,0:T(8,128)(2,1)S(1)}, bf16[96,1024]{1,0:T(8,128)(2,1)S(1)}, u32[]{:S(2)}, u32[]{:S(2)}) collective-permute-start(bf16[96,1024]{1,0:T(8,128)(2,1)S(1)} %pad_maximum_fusion.3), channel_id=1, source_target_pairs={{0,4},{4,8},{8,12},{12,14},{14,10},{10,6},{6,2},{2,0},{1,5},{5,9},... | collective-permute-start | bytes 589832 | tf_op jit(solution)/shard_map/ppermute | solution.py:55
  176.0 8.3 %collective-permute-start.37 = (bf16[96,1024]{1,0:T(8,128)(2,1)S(1)}, bf16[96,1024]{1,0:T(8,128)(2,1)S(1)}, u32[]{:S(2)}, u32[]{:S(2)}) collective-permute-start(bf16[96,1024]{1,0:T(8,128)(2,1)S(1)} %pad_maximum_fusion.6), channel_id=1, source_target_pairs={{0,2},{4,0},{8,4},{12,8},{14,12},{10,14},{6,10},{2,6},{1,3},{5,1},... | collective-permute-start | bytes 589832 | tf_op jit(solution)/shard_map/ppermute | solution.py:55
  177.0 7.8 %collective-permute-start.36 = (bf16[96,1024]{1,0:T(8,128)(2,1)S(1)}, bf16[96,1024]{1,0:T(8,128)(2,1)S(1)}, u32[]{:S(2)}, u32[]{:S(2)}) collective-permute-start(bf16[96,1024]{1,0:T(8,128)(2,1)S(1)} %pad_maximum_fusion.5), channel_id=1, source_target_pairs={{0,4},{4,8},{8,12},{12,14},{14,10},{10,6},{6,2},{2,0},{1,5},{5,9},... | collective-permute-start | bytes 589832 | tf_op jit(solution)/shard_map/ppermute | solution.py:55
  181.1 7.6 %collective-permute-start.34 = (bf16[96,1024]{1,0:T(8,128)(2,1)S(1)}, bf16[96,1024]{1,0:T(8,128)(2,1)S(1)}, u32[]{:S(2)}, u32[]{:S(2)}) collective-permute-start(bf16[96,1024]{1,0:T(8,128)(2,1)S(1)} %get-tuple-element.200), channel_id=1, source_target_pairs={{0,4},{4,8},{8,12},{12,14},{14,10},{10,6},{6,2},{2,0},{1,5},{5,9},... | collective-permute-start | bytes 589832 | tf_op jit(solution)/shard_map/ppermute | solution.py:55
  183.2 7.6 %collective-permute-start.35 = (bf16[96,1024]{1,0:T(8,128)(2,1)S(1)}, bf16[96,1024]{1,0:T(8,128)(2,1)S(1)}, u32[]{:S(2)}, u32[]{:S(2)}) collective-permute-start(bf16[96,1024]{1,0:T(8,128)(2,1)S(1)} %get-tuple-element.199), channel_id=1, source_target_pairs={{0,2},{4,0},{8,4},{12,8},{14,12},{10,14},{6,10},{2,6},{1,3},{5,1},... | collective-permute-start | bytes 589832 | tf_op jit(solution)/shard_map/ppermute | solution.py:55
  185.0 8.1 %collective-permute-start.40 = (bf16[96,1024]{1,0:T(8,128)(2,1)S(1)}, bf16[96,1024]{1,0:T(8,128)(2,1)S(1)}, u32[]{:S(2)}, u32[]{:S(2)}) collective-permute-start(bf16[96,1024]{1,0:T(8,128)(2,1)S(1)} %get-tuple-element.198), channel_id=1, source_target_pairs={{0,4},{4,8},{8,12},{12,14},{14,10},{10,6},{6,2},{2,0},{1,5},{5,9},... | collective-permute-start | bytes 589832 | tf_op jit(solution)/shard_map/ppermute | solution.py:55
  187.2 5.9 %collective-permute-start.41 = (bf16[96,1024]{1,0:T(8,128)(2,1)S(1)}, bf16[96,1024]{1,0:T(8,128)(2,1)S(1)}, u32[]{:S(2)}, u32[]{:S(2)}) collective-permute-start(bf16[96,1024]{1,0:T(8,128)(2,1)S(1)} %get-tuple-element.197), channel_id=1, source_target_pairs={{0,2},{4,0},{8,4},{12,8},{14,12},{10,14},{6,10},{2,6},{1,3},{5,1},... | collective-permute-start | bytes 589832 | tf_op jit(solution)/shard_map/ppermute | solution.py:55
  191.0 5.7 %collective-permute-start.38 = (bf16[96,1024]{1,0:T(8,128)(2,1)S(1)}, bf16[96,1024]{1,0:T(8,128)(2,1)S(1)}, u32[]{:S(2)}, u32[]{:S(2)}) collective-permute-start(bf16[96,1024]{1,0:T(8,128)(2,1)S(1)} %get-tuple-element.195), channel_id=1, source_target_pairs={{0,4},{4,8},{8,12},{12,14},{14,10},{10,6},{6,2},{2,0},{1,5},{5,9},... | collective-permute-start | bytes 589832 | tf_op jit(solution)/shard_map/ppermute | solution.py:55
  191.4 5.7 %collective-permute-start.39 = (bf16[96,1024]{1,0:T(8,128)(2,1)S(1)}, bf16[96,1024]{1,0:T(8,128)(2,1)S(1)}, u32[]{:S(2)}, u32[]{:S(2)}) collective-permute-start(bf16[96,1024]{1,0:T(8,128)(2,1)S(1)} %get-tuple-element.196), channel_id=1, source_target_pairs={{0,2},{4,0},{8,4},{12,8},{14,12},{10,14},{6,10},{2,6},{1,3},{5,1},... | collective-permute-start | bytes 589832 | tf_op jit(solution)/shard_map/ppermute | solution.py:55
  193.2 5.7 %collective-permute-start.42 = (bf16[96,1024]{1,0:T(8,128)(2,1)S(1)}, bf16[96,1024]{1,0:T(8,128)(2,1)S(1)}, u32[]{:S(2)}, u32[]{:S(2)}) collective-permute-start(bf16[96,1024]{1,0:T(8,128)(2,1)S(1)} %get-tuple-element.193), channel_id=1, source_target_pairs={{0,4},{4,8},{8,12},{12,14},{14,10},{10,6},{6,2},{2,0},{1,5},{5,9},... | collective-permute-start | bytes 589832 | tf_op jit(solution)/shard_map/ppermute | solution.py:55
  194.6 5.7 %collective-permute-start.43 = (bf16[96,1024]{1,0:T(8,128)(2,1)S(1)}, bf16[96,1024]{1,0:T(8,128)(2,1)S(1)}, u32[]{:S(2)}, u32[]{:S(2)}) collective-permute-start(bf16[96,1024]{1,0:T(8,128)(2,1)S(1)} %get-tuple-element.194), channel_id=1, source_target_pairs={{0,2},{4,0},{8,4},{12,8},{14,12},{10,14},{6,10},{2,6},{1,3},{5,1},... | collective-permute-start | bytes 589832 | tf_op jit(solution)/shard_map/ppermute | solution.py:55
  197.2 3.1 %copy-start.6 = (bf16[512,1024]{1,0:T(8,128)(2,1)}, bf16[512,1024]{1,0:T(8,128)(2,1)S(1)}, u32[]{:S(2)}) copy-start(bf16[512,1024]{1,0:T(8,128)(2,1)S(1)} %fusion.36) | copy-start | bytes 3145732
